TPU v7x, 32 devices: a whole 2x2x4 slice. The times are simulated.
32 devices in a mesh: obs: 4 (over x, core), pix: 2 (over y), chan: 4 (over z).
Axes of the slice: x: 2, y: 2, z: 4, core: 2. Of those that a mesh axis runs over, the one named last changes fastest.
Arguments:
- spectra: bfloat16 [16384, 4608], P(('obs', 'pix'), 'chan'), may hold values from -6 to 6
- enc_weight: bfloat16 [4608, 256], P('chan'), may hold values from -0.09375 to 0.09375
- pix_tile: int32 [16384, 1], P(('obs', 'pix')), may hold values from 0 to 1; in each aligned block of 512 rows (0 to 511, 512 to 1023, ...) at most 512 rows name the same one
- pix_local: int32 [16384], P(('obs', 'pix')), may hold values from 0 to 4095
- foot_weight: float32 [16384], P(('obs', 'pix')), may hold values from 0.001 to 0.01
- cotangent: bfloat16 [8192, 256], P('pix'), may hold values from -6 to 6
- adjoint: int32 [8, 8192], P(None, 'pix'), may hold values from 0 to 8191, as said below
- mixing: float32 [8, 256], replicated, may hold values from -2 to 2
Outputs:
- grad_enc: float32 [4608, 256], P('chan')
Inputs may be any that keep to these rules, and one draw needn't show every extreme that they name: `pix_tile`: in each aligned block of 512 rows no tile is named by more than 512 rows, a bound that some block reaches. `adjoint`: every entry is a pixel at most 128 away in index from its column's pixel; in every column the first entry is exactly 128 away.
All inputs are finite; a program needn't handle non-finite values.
Results may differ from a plain program's by a relative error of at most 0.006.
Values may be sent and summed in bfloat16 or wider, within the bound.
No kernel may reach another device: no remote copies, remote signals or barrier semaphores. Data moves between devices by JAX's collectives and lax.ppermute only.
A program may use at most 128 MiB of HBM per device.

v0:
```python
import jax
import jax.numpy as jnp
from jax import lax
from jax.sharding import PartitionSpec as P

NEIGH = 8
HALO = 128


def extended(value, sides, width):
    for axis, dim in sides:
        size, length = (lax.axis_size(axis), value.shape[dim])
        up = [(i, (i + 1) % size) for i in range(size - 1)]
        down = [(j, i) for i, j in up]
        last = lax.slice_in_dim(value, length - width, length, axis=dim)
        first = lax.slice_in_dim(value, 0, width, axis=dim)
        before = lax.ppermute(last, axis, up)
        after = lax.ppermute(first, axis, down)
        value = jnp.concatenate([before, value, after], axis=dim)
    return value


def fetch_rows(pixel_grad, tile_ids, local_ids, capacity):
    tile_count = lax.axis_size("pix")
    feature_count = pixel_grad.shape[1]
    onehot = (tile_ids[:, None] == jnp.arange(tile_count, dtype=jnp.int32)[None, :]).astype(
        jnp.int32
    )
    place_rank = jnp.sum((jnp.cumsum(onehot, axis=0) - 1) * onehot, axis=1)
    slot_index = tile_ids * capacity + place_rank
    outgoing = jnp.full((tile_count * capacity,), -1, jnp.int32).at[slot_index].set(local_ids)
    outgoing = outgoing.reshape(tile_count, capacity)
    requested = lax.all_to_all(outgoing, "pix", split_axis=0, concat_axis=0, tiled=True)
    usable = requested >= 0
    fetched = jnp.take(pixel_grad, jnp.where(usable, requested, 0), axis=0)
    fetched = jnp.where(usable[..., None], fetched, jnp.zeros_like(fetched))
    answers = lax.all_to_all(fetched, "pix", split_axis=0, concat_axis=0, tiled=True)
    return jnp.take(answers.reshape(tile_count * capacity, feature_count), slot_index, axis=0)


def pre_gradient(pre, fetched, weights):
    sigma = jax.nn.sigmoid(pre)
    deriv = sigma * (1.0 + pre * (1.0 - sigma))
    return (weights[:, None] * deriv * fetched.astype(jnp.float32)).astype(jnp.bfloat16)


def shards(spectra, enc_weight, pix_tile, pix_local, foot_weight, cotangent, adjoint, mixing):
    tile_count = lax.axis_size("pix")
    groups = lax.axis_size("chan")
    tile_rows = cotangent.shape[0]
    feature_count = cotangent.shape[1]
    padded = extended(cotangent, (("pix", 0),), HALO)
    block_count = tile_rows // HALO
    stacked = padded.reshape(block_count + 2, HALO, feature_count)
    windows = jnp.concatenate(
        (stacked[:block_count], stacked[1 : block_count + 1], stacked[2 : block_count + 2]), axis=1
    )
    anchor = lax.axis_index("pix") * tile_rows - HALO
    block_start = (jnp.arange(block_count, dtype=jnp.int32) * HALO)[:, None]
    columns = jnp.arange(3 * HALO, dtype=jnp.int32)[None, None, :]
    summed = cotangent.astype(jnp.float32)
    for neighbor in range(NEIGH):
        within = (adjoint[neighbor] - anchor).reshape(block_count, HALO) - block_start
        selector = (within[:, :, None] == columns).astype(jnp.bfloat16)
        picked = jnp.einsum("bij,bje->bie", selector, windows, preferred_element_type=jnp.float32)
        summed = summed + picked.reshape(tile_rows, feature_count) * mixing[neighbor]
    pixel_grad = summed.astype(jnp.bfloat16)
    all_rows = spectra.shape[0]
    quarter = all_rows // groups
    capacity_part = 2 * quarter // tile_count
    pre = lax.psum_scatter(
        jnp.dot(spectra, enc_weight, preferred_element_type=jnp.float32).astype(jnp.bfloat16),
        "chan",
        scatter_dimension=0,
        tiled=True,
    ).astype(jnp.float32)
    first_row = lax.axis_index("chan") * quarter
    tile_ids = lax.dynamic_slice_in_dim(pix_tile[:, 0], first_row, quarter, 0)
    local_ids = lax.dynamic_slice_in_dim(pix_local, first_row, quarter, 0)
    weights = lax.dynamic_slice_in_dim(foot_weight, first_row, quarter, 0)
    fetched = fetch_rows(pixel_grad, tile_ids, local_ids, capacity_part)
    grad_part = pre_gradient(pre, fetched, weights)
    local_grad = lax.dot_general(
        spectra,
        lax.all_gather(grad_part, "chan", axis=0, tiled=True),
        (((0,), (0,)), ((), ())),
        preferred_element_type=jnp.float32,
    )
    return lax.psum(local_grad, ("obs", "pix"))


def solution(mesh):
    return jax.shard_map(
        shards,
        mesh=mesh,
        in_specs=(
            P(("obs", "pix"), "chan"),
            P("chan", None),
            P(("obs", "pix"), None),
            P(("obs", "pix")),
            P(("obs", "pix")),
            P("pix", None),
            P(None, "pix"),
            P(),
        ),
        out_specs=P("chan", None),
        check_vma=False,
    )
```

profile of v0, /device:TPU:0, one launch (start us, length us, event | category | flops | bytes accessed | tf_op | source)
XLA Modules:
  0.0 185.7 jit_solution(8337358434582827373)
XLA Ops:
  6.5 0.9 fusion.37
  7.5 4.9 %collective-permute-start = (bf16[128,256]{1,0:T(8,128)(2,1)S(1)}, bf16[128,256]{1,0:T(8,128)(2,1)S(1)}, u32[]{:S(2)}, u32[]{:S(2)}) collective-permute-start(bf16[128,256]{1,0:T(8,128)(2,1)S(1)} %get-tuple-element.9), channel_id=1, source_target_pairs={{0,4},{1,5},{2,6},{3,7},{8,12},{9,13},{10,14},{11,15},{16,20},{17,... | collective-permute-start | bytes 196616 | tf_op jit(solution)/shard_map/ppermute | solution.py:17
  12.4 1.3 collective-permute-start.1
  13.7 0.7 constant_dynamic-slice_fusion
  14.4 0.6 reduce-window.6
  15.0 0.2 slice_reduce_fusion
  15.5 0.7 and_reduce_fusion
  16.2 0.8 dynamic_slice.11
  16.9 3.0 %scatter_custom_fusion = s32[1024]{0:T(1024)} fusion(s32[512]{0:T(512)S(1)} %bitcast.138, s32[512]{0:T(512)S(1)} %dynamic_slice.11, s32[]{:T(128)} %constant.33.clone.1), kind=kCustom, calls=%fused_computation.93 | custom fusion | bytes 4100 | tf_op jit(solution)/shard_map/scatter | solution.py:31
  20.0 3.9 %all-to-all-start = ((s32[2,1,512]{2,1,0:T(1,128)}), s32[2,1,512]{2,1,0:T(1,128)S(1)}, u32[]{:S(2)}, u32[]{:S(2)}) async-start(s32[2,1,512]{2,1,0:T(1,128)} %bitcast.5), calls=%async_computation.1 | async-start | bytes 8192 | tf_op jit(solution)/shard_map/all_to_all | solution.py:33
  23.9 5.0 %convolution_convert_fusion = bf16[2048,256]{1,0:T(8,128)(2,1)} fusion(bf16[2048,1152]{1,0:T(8,128)(2,1)} %param.8, bf16[1152,256]{1,0:T(8,128)(2,1)S(1)} %copy-done), kind=kOutput, calls=%fused_computation.46 | convolution fusion | flops 1208483840 | bytes 6356992 | tf_op jit(solution)/shard_map/dot_general | solution.py:72
  29.3 0.3 pad_maximum_fusion.2
  29.6 2.9 %fusion = f32[32,128,256]{2,1,0:T(8,128)S(1)} fusion(s32[32,128]{1,0:T(8,128)S(1)} %get-tuple-element.29, bf16[32,128,256]{2,1,0:T(8,128)(2,1)S(1)} %bitcast.118, bf16[32,128,256]{2,1,0:T(8,128)(2,1)S(1)} %bitcast.102, bf16[32,128,256]{2,1,0:T(8,128)(2,1)S(1)} %bitcast.110), kind=kOutput, calls=%fused_computation.12 | convolution fusion | flops 825753600 | bytes 10502144 | tf_op jit(solution)/shard_map/bij,bje->bie/dot_general | solution.py:65
  32.4 2.9 %fusion.1 = f32[32,128,256]{2,1,0:T(8,128)S(1)} fusion(s32[32,128]{1,0:T(8,128)S(1)} %get-tuple-element.30, bf16[32,128,256]{2,1,0:T(8,128)(2,1)S(1)} %bitcast.119, bf16[32,128,256]{2,1,0:T(8,128)(2,1)S(1)} %bitcast.103, bf16[32,128,256]{2,1,0:T(8,128)(2,1)S(1)} %bitcast.111), kind=kOutput, calls=%fused_computation.13 | convolution fusion | flops 825753600 | bytes 10502144 | tf_op jit(solution)/shard_map/bij,bje->bie/dot_general | solution.py:65
  35.3 3.5 %fusion.2 = f32[32,128,256]{2,1,0:T(8,128)} fusion(s32[32,128]{1,0:T(8,128)S(1)} %get-tuple-element.31, bf16[32,128,256]{2,1,0:T(8,128)(2,1)S(1)} %bitcast.120, bf16[32,128,256]{2,1,0:T(8,128)(2,1)S(1)} %bitcast.104, bf16[32,128,256]{2,1,0:T(8,128)(2,1)S(1)} %bitcast.112), kind=kOutput, calls=%fused_computation.14 | convolution fusion | flops 825753600 | bytes 10502144 | tf_op jit(solution)/shard_map/bij,bje->bie/dot_general | solution.py:65
  38.8 3.5 %fusion.3 = f32[32,128,256]{2,1,0:T(8,128)} fusion(s32[32,128]{1,0:T(8,128)S(1)} %get-tuple-element.32, bf16[32,128,256]{2,1,0:T(8,128)(2,1)S(1)} %bitcast.121, bf16[32,128,256]{2,1,0:T(8,128)(2,1)S(1)} %bitcast.105, bf16[32,128,256]{2,1,0:T(8,128)(2,1)S(1)} %bitcast.113), kind=kOutput, calls=%fused_computation.15 | convolution fusion | flops 825753600 | bytes 10502144 | tf_op jit(solution)/shard_map/bij,bje->bie/dot_general | solution.py:65
  42.2 3.5 %fusion.4 = f32[32,128,256]{2,1,0:T(8,128)} fusion(s32[32,128]{1,0:T(8,128)S(1)} %get-tuple-element.33, bf16[32,128,256]{2,1,0:T(8,128)(2,1)S(1)} %bitcast.122, bf16[32,128,256]{2,1,0:T(8,128)(2,1)S(1)} %bitcast.106, bf16[32,128,256]{2,1,0:T(8,128)(2,1)S(1)} %bitcast.114), kind=kOutput, calls=%fused_computation.16 | convolution fusion | flops 825753600 | bytes 10502144 | tf_op jit(solution)/shard_map/bij,bje->bie/dot_general | solution.py:65
  45.7 3.5 %fusion.5 = f32[32,128,256]{2,1,0:T(8,128)} fusion(s32[32,128]{1,0:T(8,128)S(1)} %get-tuple-element.34, bf16[32,128,256]{2,1,0:T(8,128)(2,1)S(1)} %bitcast.123, bf16[32,128,256]{2,1,0:T(8,128)(2,1)S(1)} %bitcast.107, bf16[32,128,256]{2,1,0:T(8,128)(2,1)S(1)} %bitcast.115), kind=kOutput, calls=%fused_computation.17 | convolution fusion | flops 825753600 | bytes 10502144 | tf_op jit(solution)/shard_map/bij,bje->bie/dot_general | solution.py:65
  49.2 3.5 %fusion.6 = f32[32,128,256]{2,1,0:T(8,128)} fusion(s32[32,128]{1,0:T(8,128)S(1)} %get-tuple-element.35, bf16[32,128,256]{2,1,0:T(8,128)(2,1)S(1)} %bitcast.124, bf16[32,128,256]{2,1,0:T(8,128)(2,1)S(1)} %bitcast.108, bf16[32,128,256]{2,1,0:T(8,128)(2,1)S(1)} %bitcast.116), kind=kOutput, calls=%fused_computation.18 | convolution fusion | flops 825753600 | bytes 10502144 | tf_op jit(solution)/shard_map/bij,bje->bie/dot_general | solution.py:65
  52.7 3.5 %fusion.7 = f32[32,128,256]{2,1,0:T(8,128)} fusion(s32[32,128]{1,0:T(8,128)S(1)} %get-tuple-element.36, bf16[32,128,256]{2,1,0:T(8,128)(2,1)S(1)} %bitcast.125, bf16[32,128,256]{2,1,0:T(8,128)(2,1)S(1)} %bitcast.109, bf16[32,128,256]{2,1,0:T(8,128)(2,1)S(1)} %bitcast.117), kind=kOutput, calls=%fused_computation.19 | convolution fusion | flops 825753600 | bytes 10502144 | tf_op jit(solution)/shard_map/bij,bje->bie/dot_general | solution.py:65
  56.1 9.7 %fusion.9 = bf16[4096,256]{1,0:T(8,128)(2,1)S(1)} fusion(f32[32,128,256]{2,1,0:T(8,128)} %fusion.7, f32[32,128,256]{2,1,0:T(8,128)} %fusion.6, f32[32,128,256]{2,1,0:T(8,128)} %fusion.5, f32[32,128,256]{2,1,0:T(8,128)} %fusion.4, f32[32,128,256]{2,1,0:T(8,128)} %fusion.3, f32[32,128,256]{2,1,0:T(8,128)} %fusion.2, f32[32,128,256]{2,1,0:T(8,128)S(1)} %fusion.1, ...), kind=kLoop, calls=%fused_computation.22 | loop fusion | flops 18874368 | bytes 37756928 | tf_op jit(solution)/shard_map/convert_element_type | solution.py:67
  65.8 3.9 %gather_fusion = bf16[1024,256]{1,0:T(8,128)(2,1)S(1)} fusion(bf16[4096,256]{1,0:T(8,128)(2,1)S(1)} %fusion.9, s32[1024]{0:T(1024)S(1)} %broadcast_clamp_fusion), kind=kCustom, calls=%fused_computation | custom fusion | bytes 1052672 | tf_op jit(solution)/shard_map/jit(_take)/gather | solution.py:35
  69.7 1.1 select_select_fusion
  70.9 3.5 %all-to-all-start.1 = ((bf16[2,512,256]{2,1,0:T(8,128)(2,1)}), bf16[2,512,256]{2,1,0:T(8,128)(2,1)S(1)}, u32[]{:S(2)}, u32[]{:S(2)}) async-start(bf16[2,512,256]{2,1,0:T(8,128)(2,1)} %select_select_fusion), calls=%async_computation.2 | async-start | bytes 1048576 | tf_op jit(solution)/shard_map/all_to_all | solution.py:37
  74.4 0.8 dynamic_slice.9
  75.2 7.2 %all-to-all-done.1 = bf16[2,512,256]{2,1,0:T(8,128)(2,1)S(1)} async-done(((bf16[2,512,256]{2,1,0:T(8,128)(2,1)}), bf16[2,512,256]{2,1,0:T(8,128)(2,1)S(1)}, u32[]{:S(2)}, u32[]{:S(2)}) %all-to-all-start.1) | async-done | bytes 524320 | tf_op jit(solution)/shard_map/all_to_all | solution.py:37
  82.3 1.9 %gather_fusion.1 = bf16[512,256]{1,0:T(8,128)(2,1)S(1)} fusion(bf16[1024,256]{1,0:T(8,128)(2,1)S(1)} %bitcast.101, s32[1024]{0:T(1024)S(1)} %pad_clamp_fusion), kind=kCustom, calls=%fused_computation.1 | custom fusion | bytes 526336 | tf_op jit(solution)/shard_map/jit(_take)/gather | solution.py:38
  84.3 1.9 %fusion.32 = bf16[512,256]{1,0:T(8,128)(2,1)} fusion(bf16[512,256]{1,0:T(8,128)(2,1)} %reduce-scatter.2.cloned.1.call-done, bf16[512,256]{1,0:T(8,128)(2,1)S(1)} %gather_fusion.1, f32[512]{0:T(512)S(1)} %dynamic_slice.9, pred[512]{0:T(512)(128)(4,1)S(1)} %get-tuple-element.5), kind=kLoop, calls=%fused_computation.58 | loop fusion | flops 1703936 | bytes 788992 | tf_op jit(solution)/shard_map/convert_element_type | solution.py:44
  86.3 28.2 %all-gather.2.cloned.1.call-done = bf16[2048,256]{1,0:T(8,128)(2,1)} async-done(((bf16[512,256]{1,0:T(8,128)(2,1)}), bf16[2048,256]{1,0:T(8,128)(2,1)}) %all-gather.2.cloned.1.call-update) | async-done | bytes 1048592 | tf_op jit(solution)/shard_map/all_gather | solution.py:85
  114.6 5.2 %convolution_bitcast_fusion = f32[1152,256]{0,1:T(8,128)} fusion(bf16[2048,256]{1,0:T(8,128)(2,1)} %all-gather.2.cloned.1.call-done, bf16[2048,1152]{1,0:T(8,128)(2,1)} %param.8), kind=kOutput, calls=%fused_computation.45 | convolution fusion | flops 1207959552 | bytes 6946816 | tf_op jit(solution)/shard_map/dot_general | solution.py:83
  119.8 56.7 %all-reduce.2.cloned.1.call-done = f32[1152,256]{0,1:T(8,128)} async-done(((f32[1152,256]{0,1:T(8,128)}), f32[1152,256]{0,1:T(8,128)}) %all-reduce.2.cloned.1.call-update) | async-done | bytes 1179664 | tf_op jit(solution)/shard_map/psum | solution.py:89
  176.5 2.7 %copy.11 = f32[1152,256]{1,0:T(8,128)} copy(f32[1152,256]{0,1:T(8,128)} %all-reduce.2.cloned.1.call-done) | data formatting | bytes 2359296 | tf_op jit(solution)/shard_map/psum | solution.py:89
  (32 shorter events, 0.7 us)
Async XLA Ops:
  6.5 17.4 %copy-start = (bf16[1152,256]{1,0:T(8,128)(2,1)S(1)}, bf16[1152,256]{1,0:T(8,128)(2,1)}, u32[]{:S(2)}) copy-start(bf16[1152,256]{1,0:T(8,128)(2,1)} %param.9) | copy-start | bytes 1769476
  7.5 21.8 %collective-permute-start = (bf16[128,256]{1,0:T(8,128)(2,1)S(1)}, bf16[128,256]{1,0:T(8,128)(2,1)S(1)}, u32[]{:S(2)}, u32[]{:S(2)}) collective-permute-start(bf16[128,256]{1,0:T(8,128)(2,1)S(1)} %get-tuple-element.9), channel_id=1, source_target_pairs={{0,4},{1,5},{2,6},{3,7},{8,12},{9,13},{10,14},{11,15},{16,20},{17,... | collective-permute-start | bytes 196616 | tf_op jit(solution)/shard_map/ppermute | solution.py:17
  12.4 16.9 %collective-permute-start.1 = (bf16[128,256]{1,0:T(8,128)(2,1)S(1)}, bf16[128,256]{1,0:T(8,128)(2,1)S(1)}, u32[]{:S(2)}, u32[]{:S(2)}) collective-permute-start(bf16[128,256]{1,0:T(8,128)(2,1)S(1)} %get-tuple-element.10), channel_id=1, source_target_pairs={{4,0},{5,1},{6,2},{7,3},{12,8},{13,9},{14,10},{15,11},{20,16},{21,... | collective-permute-start | bytes 196616 | tf_op jit(solution)/shard_map/ppermute | solution.py:18
  20.0 9.2 %all-to-all-start = ((s32[2,1,512]{2,1,0:T(1,128)}), s32[2,1,512]{2,1,0:T(1,128)S(1)}, u32[]{:S(2)}, u32[]{:S(2)}) async-start(s32[2,1,512]{2,1,0:T(1,128)} %bitcast.5), calls=%async_computation.1 | async-start | bytes 8192 | tf_op jit(solution)/shard_map/all_to_all | solution.py:33
  23.9 5.1 %copy-start.3 = (s32[8,4096]{1,0:T(8,128)S(1)}, s32[8,4096]{1,0:T(8,128)}, u32[]{:S(2)}) copy-start(s32[8,4096]{1,0:T(8,128)} %param.14) | copy-start | bytes 393220
  23.9 5.3 %copy-start.4 = (f32[8,256]{1,0:T(8,128)S(1)}, f32[8,256]{1,0:T(8,128)}, u32[]{:S(2)}) copy-start(f32[8,256]{1,0:T(8,128)} %param.15) | copy-start | bytes 24580
  23.9 5.4 %copy-start.1 = (bf16[4096,256]{1,0:T(8,128)(2,1)S(1)}, bf16[4096,256]{1,0:T(8,128)(2,1)}, u32[]{:S(2)}) copy-start(bf16[4096,256]{1,0:T(8,128)(2,1)} %param.13) | copy-start | bytes 6291460
  23.9 60.4 %reduce-scatter.2.cloned.1.call-start = ((), (), s32[]{:S(2)}) async-start(), calls=%async_computation.3 | async-start | bytes 1310720 | tf_op jit(solution)/shard_map/reduce_scatter | solution.py:71
  52.7 3.5 %copy-start.2 = (bf16[4096,256]{1,0:T(8,128)(2,1)S(1)}, bf16[4096,256]{1,0:T(8,128)(2,1)}, u32[]{:S(2)}) copy-start(bf16[4096,256]{1,0:T(8,128)(2,1)} %param.13) | copy-start | bytes 6291460
  70.9 11.5 %all-to-all-start.1 = ((bf16[2,512,256]{2,1,0:T(8,128)(2,1)}), bf16[2,512,256]{2,1,0:T(8,128)(2,1)S(1)}, u32[]{:S(2)}, u32[]{:S(2)}) async-start(bf16[2,512,256]{2,1,0:T(8,128)(2,1)} %select_select_fusion), calls=%async_computation.2 | async-start | bytes 1048576 | tf_op jit(solution)/shard_map/all_to_all | solution.py:37
  74.4 40.2 %all-gather.2.cloned.1.call-start = ((), (), s32[]{:S(2)}) async-start(), calls=%async_computation.4 | async-start | bytes 1310720 | tf_op jit(solution)/shard_map/all_gather | solution.py:85
  86.3 90.3 %all-reduce.2.cloned.1.call-start = ((), (), s32[]{:S(2)}) async-start(), calls=%async_computation.5 | async-start | bytes 2359296 | tf_op jit(solution)/shard_map/psum | solution.py:89
Sparse Core Ops, SparseCore 0:
  29.1 28.9 reduce-scatter.1
  86.4 28.1 all-gather.1
  119.9 56.5 all-reduce.1
where the time goes:
time: 186 us
  waiting for transfers between devices  92.2 us (50%)
  matrix products  36.7 us (20%)
  local copies, waits for them, and re-layouts  14.9 us (8%)
  other arithmetic  14.8 us (8%)
  starting transfers between devices  13.7 us (7%)
  between operations  13.3 us (7%)
    psum x1, waiting for transfers between devices, shards(): return lax.psum(local_grad, ('obs', 'pix'))  56.7 us
    all_gather x1, waiting for transfers between devices, shards(): lax.all_gather(grad_part, 'chan', axis=0, tiled=True)  28.2 us
    dot_general x8, matrix products, shards(): jnp.einsum('bij,bje->bie', selector, windows, preferred_element_type=jnp....  26.5 us
    convert_element_type x1, other arithmetic, shards(): pixel_grad = summed.astype(jnp.bfloat16)  9.65 us
    all_to_all x1, waiting for transfers between devices, fetch_rows(): lax.all_to_all(fetched, 'pix', split_axis=0, concat_axis=0, tiled=True)  7.16 us
    dot_general x1, matrix products, shards(): lax.dot_general(spectra, lax.all_gather(grad_part, 'chan', axis=0, tiled=...  5.23 us
    dot_general x1, matrix products, shards(): jnp.dot(spectra, enc_weight, preferred_element_type=jnp.float32)  4.99 us
    ppermute x1, starting transfers between devices, extended(): before = lax.ppermute(last, axis, up)  4.87 us
  transfers between devices with their start and end apart: 7, of which 3 were waited for; matrix products, arithmetic and copies ran while one was open for 30% of the time, Pallas kernels for 0%

commit v1 on v0

--- a/solution.py
+++ b/solution.py
@@ -44,6 +44,68 @@
     return (weights[:, None] * deriv * fetched.astype(jnp.float32)).astype(jnp.bfloat16)
 
 
+def swap(value, axis, bit):
+    size = lax.axis_size(axis)
+    return lax.ppermute(value, axis, [(i, i ^ bit) for i in range(size)])
+
+
+def halves(value, which, dim=0):
+    length = value.shape[dim] // 2
+    own = lax.dynamic_slice_in_dim(value, which * length, length, dim)
+    other = lax.dynamic_slice_in_dim(value, (1 - which) * length, length, dim)
+    return own, other
+
+
+def joined(own, other, which):
+    first = jnp.where(which == 0, own, other)
+    second = jnp.where(which == 0, other, own)
+    return jnp.concatenate([first, second], axis=0)
+
+
+def bits_of(axis):
+    size = lax.axis_size(axis)
+    index = lax.axis_index(axis)
+    return [(1 << n, (index >> n) & 1) for n in range(size.bit_length() - 1)]
+
+
+def sum_and_split(parts, axis):
+    total = parts.astype(jnp.float32)
+    for bit, which in bits_of(axis):
+        keep, send = halves(total, which)
+        total = keep + swap(send.astype(jnp.bfloat16), axis, bit).astype(jnp.float32)
+    return total
+
+
+def gather_back(rows, axis):
+    for bit, which in reversed(bits_of(axis)):
+        rows = joined(rows, swap(rows, axis, bit), which)
+    return rows
+
+
+def split_start(rows, axis):
+    start = 0
+    for _, which in bits_of(axis):
+        rows = rows // 2
+        start = start + which * rows
+    return start
+
+
+def add_swapped(value, axis, bit):
+    value = lax.reduce_precision(value, 8, 7)
+    return value + swap(value.astype(jnp.bfloat16), axis, bit).astype(jnp.float32)
+
+
+def sum_over_panels(value):
+    core = lax.axis_index("obs") & 1
+    keep, send = halves(value, core)
+    keep = keep + swap(send.astype(jnp.bfloat16), "obs", 1).astype(jnp.float32)
+    upper, lower = jnp.split(keep, 2, axis=0)
+    upper, lower = add_swapped(upper, "obs", 2), add_swapped(lower, "pix", 1)
+    upper, lower = add_swapped(upper, "pix", 1), add_swapped(lower, "obs", 2)
+    own = jnp.concatenate([upper, lower], axis=0)
+    return joined(own, swap(own, "obs", 1), core)
+
+
 def shards(spectra, enc_weight, pix_tile, pix_local, foot_weight, cotangent, adjoint, mixing):
     tile_count = lax.axis_size("pix")
     groups = lax.axis_size("chan")
@@ -68,13 +130,11 @@
     all_rows = spectra.shape[0]
     quarter = all_rows // groups
     capacity_part = 2 * quarter // tile_count
-    pre = lax.psum_scatter(
+    pre = sum_and_split(
         jnp.dot(spectra, enc_weight, preferred_element_type=jnp.float32).astype(jnp.bfloat16),
         "chan",
-        scatter_dimension=0,
-        tiled=True,
-    ).astype(jnp.float32)
-    first_row = lax.axis_index("chan") * quarter
+    )
+    first_row = split_start(all_rows, "chan")
     tile_ids = lax.dynamic_slice_in_dim(pix_tile[:, 0], first_row, quarter, 0)
     local_ids = lax.dynamic_slice_in_dim(pix_local, first_row, quarter, 0)
     weights = lax.dynamic_slice_in_dim(foot_weight, first_row, quarter, 0)
@@ -82,10 +142,12 @@
     grad_part = pre_gradient(pre, fetched, weights)
     local_grad = lax.dot_general(
         spectra,
-        lax.all_gather(grad_part, "chan", axis=0, tiled=True),
+        gather_back(grad_part, "chan"),
         (((0,), (0,)), ((), ())),
         preferred_element_type=jnp.float32,
     )
+    if lax.axis_size("obs") == 4 and lax.axis_size("pix") == 2:
+        return sum_over_panels(local_grad)
     return lax.psum(local_grad, ("obs", "pix"))
 
 

time: 186 us -> 141 us (0.76)
  waiting for transfers between devices: 92.2 us -> 48.3 us
  between operations: 13.3 us -> 0.4 us
  starting transfers between devices: 13.7 us -> 24.2 us
  matrix products: 36.7 us -> 34.7 us
  other arithmetic: 14.8 us -> 16.8 us
    psum x1 -> x0, waiting for transfers between devices: 56.7 us -> none  [shards(): return lax.psum(local_grad, ('obs', 'pix'))]
    ppermute x0 -> x10, waiting for transfers between devices: none -> 45.6 us  [swap(): return lax.ppermute(value, axis, [(i, i ^ bit) for i in range(size)])]
    all_gather x1 -> x0, waiting for transfers between devices: 28.2 us -> none  [shards(): lax.all_gather(grad_part, 'chan', axis=0, tiled=True)]
    ppermute x0 -> x10, starting transfers between devices: none -> 10.5 us  [swap(): return lax.ppermute(value, axis, [(i, i ^ bit) for i in range(size)])]
    all_to_all x1, waiting for transfers between devices: 7.16 us -> 2.73 us  [fetch_rows(): lax.all_to_all(fetched, 'pix', split_axis=0, concat_axis=0, tiled=True)]
    psum x1 -> x0, local copies, waits for them, and re-layouts: 2.65 us -> none  [shards(): return lax.psum(local_grad, ('obs', 'pix'))]
    add x0 -> x3, other arithmetic: none -> 1.97 us  [the longest x1 1.5 us: sum_and_split(): keep + swap(send.astype(jnp.bfloat16), axis, bit).astype(jnp.float32)]
  transfers between devices with their start and end apart: 7 -> 14, of which waited for: 3 -> 10; matrix products, arithmetic and copies ran while one was open for 30% -> 41% of each run, Pallas kernels for 0% -> 0%
where the time goes in v1:
time: 141 us
  waiting for transfers between devices  48.3 us (34%)
  matrix products  34.7 us (25%)
  starting transfers between devices  24.2 us (17%)
  other arithmetic  16.8 us (12%)
  local copies, waits for them, and re-layouts  16.4 us (12%)
    ppermute x10, waiting for transfers between devices, swap(): return lax.ppermute(value, axis, [(i, i ^ bit) for i in range(size)])  45.6 us
    dot_general x8, matrix products, shards(): jnp.einsum('bij,bje->bie', selector, windows, preferred_element_type=jnp....  26.7 us
    ppermute x10, starting transfers between devices, swap(): return lax.ppermute(value, axis, [(i, i ^ bit) for i in range(size)])  10.5 us
    convert_element_type x1, other arithmetic, shards(): pixel_grad = summed.astype(jnp.bfloat16)  9.61 us
    ppermute x1, starting transfers between devices, extended(): before = lax.ppermute(last, axis, up)  4.86 us
    dot_general x1, matrix products, shards(): jnp.dot(spectra, enc_weight, preferred_element_type=jnp.float32)  4.04 us
    gather x1, local copies, waits for them, and re-layouts, fetch_rows(): fetched = jnp.take(pixel_grad, jnp.where(usable, requested, 0), axis=0)  3.94 us
    all_to_all x1, starting transfers between devices, fetch_rows(): lax.all_to_all(outgoing, 'pix', split_axis=0, concat_axis=0, tiled=True)  3.91 us
  transfers between devices with their start and end apart: 14, of which 10 were waited for; matrix products, arithmetic and copies ran while one was open for 41% of the time, Pallas kernels for 0%

profile of v1, /device:TPU:0, one launch (start us, length us, event | category | flops | bytes accessed | tf_op | source)
XLA Modules:
  0.0 140.7 jit_solution(14261394911917825402)
XLA Ops:
  0.0 1.6 %fusion.40 = (bf16[128,256]{1,0:T(8,128)(2,1)}, bf16[128,256]{1,0:T(8,128)(2,1)S(1)}) fusion(bf16[4096,256]{1,0:T(8,128)(2,1)} %param.13), kind=kLoop, calls=%fused_computation.118 | loop fusion | bytes 262144 | tf_op jit(solution)/shard_map/slice | solution.py:15
  1.6 4.9 %collective-permute-start.2 = (bf16[128,256]{1,0:T(8,128)(2,1)}, bf16[128,256]{1,0:T(8,128)(2,1)S(1)}, u32[]{:S(2)}, u32[]{:S(2)}) collective-permute-start(bf16[128,256]{1,0:T(8,128)(2,1)} %get-tuple-element.9), channel_id=1, source_target_pairs={{0,4},{1,5},{2,6},{3,7},{8,12},{9,13},{10,14},{11,15},{16,20},{17,... | collective-permute-start | bytes 196616 | tf_op jit(solution)/shard_map/ppermute | solution.py:17
  11.6 3.0 %scatter_custom_fusion = s32[1024]{0:T(1024)} fusion(s32[512]{0:T(512)S(1)} %bitcast.139, s32[512]{0:T(512)S(1)} %dynamic_slice.33, s32[]{:T(128)} %constant.37.clone.1), kind=kCustom, calls=%fused_computation.113 | custom fusion | bytes 4100 | tf_op jit(solution)/shard_map/scatter | solution.py:31
  14.6 3.9 %all-to-all-start = ((s32[2,1,512]{2,1,0:T(1,128)}), s32[2,1,512]{2,1,0:T(1,128)S(1)}, u32[]{:S(2)}, u32[]{:S(2)}) async-start(s32[2,1,512]{2,1,0:T(1,128)} %bitcast.5), calls=%async_computation | async-start | bytes 8192 | tf_op jit(solution)/shard_map/all_to_all | solution.py:33
  18.5 4.0 %fusion.25 = f32[2048,256]{1,0:T(8,128)S(1)} fusion(bf16[2048,1152]{1,0:T(8,128)(2,1)} %param.8, bf16[1152,256]{1,0:T(8,128)(2,1)S(1)} %copy-done), kind=kOutput, calls=%fused_computation.46 | convolution fusion | flops 1209008128 | bytes 7405568 | tf_op jit(solution)/shard_map/dot_general | solution.py:134
  24.0 1.6 %collective-permute-start = (bf16[1024,256]{1,0:T(8,128)(2,1)S(1)}, bf16[1024,256]{1,0:T(8,128)(2,1)}, u32[]{:S(2)}, u32[]{:S(2)}) collective-permute-start(bf16[1024,256]{1,0:T(8,128)(2,1)S(1)} %dynamic-slice_convert_fusion), channel_id=1, source_target_pairs={{0,1},{1,0},{2,3},{3,2},{4,5},{5,4},{6,7},{7,6},{8,9},{9,8},{10,11... | collective-permute-start | bytes 1572872 | tf_op jit(solution)/shard_map/ppermute | solution.py:49
  26.3 2.9 %fusion = f32[32,128,256]{2,1,0:T(8,128)S(1)} fusion(s32[32,128]{1,0:T(8,128)S(1)} %get-tuple-element.41, bf16[32,128,256]{2,1,0:T(8,128)(2,1)S(1)} %bitcast.119, bf16[32,128,256]{2,1,0:T(8,128)(2,1)S(1)} %bitcast.103, bf16[32,128,256]{2,1,0:T(8,128)(2,1)S(1)} %bitcast.111), kind=kOutput, calls=%fused_computation.12 | convolution fusion | flops 825753600 | bytes 10502144 | tf_op jit(solution)/shard_map/bij,bje->bie/dot_general | solution.py:127
  29.1 2.9 %fusion.1 = f32[32,128,256]{2,1,0:T(8,128)S(1)} fusion(s32[32,128]{1,0:T(8,128)S(1)} %get-tuple-element.42, bf16[32,128,256]{2,1,0:T(8,128)(2,1)S(1)} %bitcast.120, bf16[32,128,256]{2,1,0:T(8,128)(2,1)S(1)} %bitcast.104, bf16[32,128,256]{2,1,0:T(8,128)(2,1)S(1)} %bitcast.112), kind=kOutput, calls=%fused_computation.13 | convolution fusion | flops 825753600 | bytes 10502144 | tf_op jit(solution)/shard_map/bij,bje->bie/dot_general | solution.py:127
  32.1 3.5 %fusion.2 = f32[32,128,256]{2,1,0:T(8,128)} fusion(s32[32,128]{1,0:T(8,128)S(1)} %get-tuple-element.43, bf16[32,128,256]{2,1,0:T(8,128)(2,1)S(1)} %bitcast.121, bf16[32,128,256]{2,1,0:T(8,128)(2,1)S(1)} %bitcast.105, bf16[32,128,256]{2,1,0:T(8,128)(2,1)S(1)} %bitcast.113), kind=kOutput, calls=%fused_computation.14 | convolution fusion | flops 825753600 | bytes 10502144 | tf_op jit(solution)/shard_map/bij,bje->bie/dot_general | solution.py:127
  35.6 3.4 %fusion.3 = f32[32,128,256]{2,1,0:T(8,128)} fusion(s32[32,128]{1,0:T(8,128)S(1)} %get-tuple-element.44, bf16[32,128,256]{2,1,0:T(8,128)(2,1)S(1)} %bitcast.122, bf16[32,128,256]{2,1,0:T(8,128)(2,1)S(1)} %bitcast.106, bf16[32,128,256]{2,1,0:T(8,128)(2,1)S(1)} %bitcast.114), kind=kOutput, calls=%fused_computation.15 | convolution fusion | flops 825753600 | bytes 10502144 | tf_op jit(solution)/shard_map/bij,bje->bie/dot_general | solution.py:127
  39.0 3.5 %fusion.4 = f32[32,128,256]{2,1,0:T(8,128)} fusion(s32[32,128]{1,0:T(8,128)S(1)} %get-tuple-element.45, bf16[32,128,256]{2,1,0:T(8,128)(2,1)S(1)} %bitcast.123, bf16[32,128,256]{2,1,0:T(8,128)(2,1)S(1)} %bitcast.107, bf16[32,128,256]{2,1,0:T(8,128)(2,1)S(1)} %bitcast.115), kind=kOutput, calls=%fused_computation.16 | convolution fusion | flops 825753600 | bytes 10502144 | tf_op jit(solution)/shard_map/bij,bje->bie/dot_general | solution.py:127
  42.5 3.6 %fusion.5 = f32[32,128,256]{2,1,0:T(8,128)} fusion(s32[32,128]{1,0:T(8,128)S(1)} %get-tuple-element.46, bf16[32,128,256]{2,1,0:T(8,128)(2,1)S(1)} %bitcast.124, bf16[32,128,256]{2,1,0:T(8,128)(2,1)S(1)} %bitcast.108, bf16[32,128,256]{2,1,0:T(8,128)(2,1)S(1)} %bitcast.116), kind=kOutput, calls=%fused_computation.17 | convolution fusion | flops 825753600 | bytes 10502144 | tf_op jit(solution)/shard_map/bij,bje->bie/dot_general | solution.py:127
  46.0 3.5 %fusion.6 = f32[32,128,256]{2,1,0:T(8,128)} fusion(s32[32,128]{1,0:T(8,128)S(1)} %get-tuple-element.47, bf16[32,128,256]{2,1,0:T(8,128)(2,1)S(1)} %bitcast.125, bf16[32,128,256]{2,1,0:T(8,128)(2,1)S(1)} %bitcast.109, bf16[32,128,256]{2,1,0:T(8,128)(2,1)S(1)} %bitcast.117), kind=kOutput, calls=%fused_computation.18 | convolution fusion | flops 825753600 | bytes 10502144 | tf_op jit(solution)/shard_map/bij,bje->bie/dot_general | solution.py:127
  49.6 3.4 %fusion.7 = f32[32,128,256]{2,1,0:T(8,128)} fusion(s32[32,128]{1,0:T(8,128)S(1)} %get-tuple-element.48, bf16[32,128,256]{2,1,0:T(8,128)(2,1)S(1)} %bitcast.126, bf16[32,128,256]{2,1,0:T(8,128)(2,1)S(1)} %bitcast.110, bf16[32,128,256]{2,1,0:T(8,128)(2,1)S(1)} %bitcast.118), kind=kOutput, calls=%fused_computation.19 | convolution fusion | flops 825753600 | bytes 10502144 | tf_op jit(solution)/shard_map/bij,bje->bie/dot_general | solution.py:127
  53.0 9.6 %fusion.9 = bf16[4096,256]{1,0:T(8,128)(2,1)S(1)} fusion(f32[32,128,256]{2,1,0:T(8,128)} %fusion.7, f32[32,128,256]{2,1,0:T(8,128)} %fusion.6, f32[32,128,256]{2,1,0:T(8,128)} %fusion.5, f32[32,128,256]{2,1,0:T(8,128)} %fusion.4, f32[32,128,256]{2,1,0:T(8,128)} %fusion.3, f32[32,128,256]{2,1,0:T(8,128)} %fusion.2, f32[32,128,256]{2,1,0:T(8,128)S(1)} %fusion.1, ...), kind=kLoop, calls=%fused_computation.22 | loop fusion | flops 18874368 | bytes 37756928 | tf_op jit(solution)/shard_map/convert_element_type | solution.py:129
  62.6 3.9 %gather_fusion = bf16[1024,256]{1,0:T(8,128)(2,1)S(1)} fusion(bf16[4096,256]{1,0:T(8,128)(2,1)S(1)} %fusion.9, s32[1024]{0:T(1024)S(1)} %broadcast_clamp_fusion), kind=kCustom, calls=%fused_computation | custom fusion | bytes 1052672 | tf_op jit(solution)/shard_map/jit(_take)/gather | solution.py:35
  67.7 3.7 %all-to-all-start.1 = ((bf16[2,512,256]{2,1,0:T(8,128)(2,1)}), bf16[2,512,256]{2,1,0:T(8,128)(2,1)S(1)}, u32[]{:S(2)}, u32[]{:S(2)}) async-start(bf16[2,512,256]{2,1,0:T(8,128)(2,1)} %select_select_fusion), calls=%async_computation.1 | async-start | bytes 1048576 | tf_op jit(solution)/shard_map/all_to_all | solution.py:37
  71.4 1.5 %convert_add_fusion = f32[1024,256]{1,0:T(8,128)S(1)} fusion(bf16[1024,256]{1,0:T(8,128)(2,1)} %collective-permute-done, f32[2048,256]{1,0:T(8,128)} %copy-done.4, s32[]{:T(128)S(6)} %select_n.114), kind=kLoop, calls=%fused_computation.54 | loop fusion | flops 524288 | bytes 2621444 | tf_op jit(solution)/shard_map/add | solution.py:75
  73.0 2.6 %collective-permute-start.1 = (bf16[512,256]{1,0:T(8,128)(2,1)S(1)}, bf16[512,256]{1,0:T(8,128)(2,1)S(1)}, u32[]{:S(2)}, u32[]{:S(2)}) collective-permute-start(bf16[512,256]{1,0:T(8,128)(2,1)S(1)} %dynamic-slice_convert_fusion.2), channel_id=1, source_target_pairs={{0,2},{1,3},{2,0},{3,1},{4,6},{5,7},{6,4},{7,5},{8,10},{9,11},{10,... | collective-permute-start | bytes 786440 | tf_op jit(solution)/shard_map/ppermute | solution.py:49
  76.3 2.7 %all-to-all-done.1 = bf16[2,512,256]{2,1,0:T(8,128)(2,1)S(1)} async-done(((bf16[2,512,256]{2,1,0:T(8,128)(2,1)}), bf16[2,512,256]{2,1,0:T(8,128)(2,1)S(1)}, u32[]{:S(2)}, u32[]{:S(2)}) %all-to-all-start.1) | async-done | bytes 524320 | tf_op jit(solution)/shard_map/all_to_all | solution.py:37
  79.0 1.9 %gather_fusion.1 = bf16[512,256]{1,0:T(8,128)(2,1)S(1)} fusion(bf16[1024,256]{1,0:T(8,128)(2,1)S(1)} %bitcast.102, s32[1024]{0:T(1024)S(1)} %pad_clamp_fusion), kind=kCustom, calls=%fused_computation.1 | custom fusion | bytes 526336 | tf_op jit(solution)/shard_map/jit(_take)/gather | solution.py:38
  81.0 5.4 %collective-permute-done.1 = bf16[512,256]{1,0:T(8,128)(2,1)S(1)} collective-permute-done((bf16[512,256]{1,0:T(8,128)(2,1)S(1)}, bf16[512,256]{1,0:T(8,128)(2,1)S(1)}, u32[]{:S(2)}, u32[]{:S(2)}) %collective-permute-start.1) | collective-permute-done | bytes 262176 | tf_op jit(solution)/shard_map/ppermute | solution.py:49
  86.7 13.8 %collective-permute-done.4 = bf16[512,256]{1,0:T(8,128)(2,1)S(1)} collective-permute-done((bf16[512,256]{1,0:T(8,128)(2,1)S(1)}, bf16[512,256]{1,0:T(8,128)(2,1)S(1)}, u32[]{:S(2)}, u32[]{:S(2)}) %collective-permute-start.4) | collective-permute-done | bytes 262176 | tf_op jit(solution)/shard_map/ppermute | solution.py:49
  100.7 13.8 %collective-permute-done.5 = bf16[1024,256]{1,0:T(8,128)(2,1)S(1)} collective-permute-done((bf16[1024,256]{1,0:T(8,128)(2,1)S(1)}, bf16[1024,256]{1,0:T(8,128)(2,1)S(1)}, u32[]{:S(2)}, u32[]{:S(2)}) %collective-permute-start.5) | collective-permute-done | bytes 524320 | tf_op jit(solution)/shard_map/ppermute | solution.py:49
  114.7 3.9 %fusion.26 = f32[256,1152]{1,0:T(8,128)S(1)} fusion(bf16[2048,1152]{1,0:T(8,128)(2,1)} %param.8, bf16[1024,256]{1,0:T(8,128)(2,1)S(1)} %get-tuple-element.14, bf16[1024,256]{1,0:T(8,128)(2,1)S(1)} %get-tuple-element.13), kind=kOutput, calls=%fused_computation.50 | convolution fusion | flops 1210056704 | bytes 6946816 | tf_op jit(solution)/shard_map/dot_general | solution.py:143
  118.8 1.6 %collective-permute-done.6 = bf16[576,256]{0,1:T(8,128)(2,1)S(1)} collective-permute-done((bf16[576,256]{0,1:T(8,128)(2,1)S(1)}, bf16[576,256]{0,1:T(8,128)(2,1)S(1)}, u32[]{:S(2)}, u32[]{:S(2)}) %collective-permute-start.6) | collective-permute-done | bytes 294944 | tf_op jit(solution)/shard_map/ppermute | solution.py:49
  122.2 2.3 %collective-permute-start.9 = (bf16[288,256]{0,1:T(8,128)(2,1)S(1)}, bf16[288,256]{0,1:T(8,128)(2,1)S(1)}, u32[]{:S(2)}, u32[]{:S(2)}) collective-permute-start(bf16[288,256]{0,1:T(8,128)(2,1)S(1)} %get-tuple-element.20), channel_id=1, source_target_pairs={{0,4},{4,0},{1,5},{5,1},{2,6},{6,2},{3,7},{7,3},{8,12},{12,8},{9,1... | collective-permute-start | bytes 442376 | tf_op jit(solution)/shard_map/ppermute | solution.py:49
  124.4 3.4 %collective-permute-done.7 = bf16[288,256]{0,1:T(8,128)(2,1)S(1)} collective-permute-done((bf16[288,256]{0,1:T(8,128)(2,1)S(1)}, bf16[288,256]{0,1:T(8,128)(2,1)S(1)}, u32[]{:S(2)}, u32[]{:S(2)}) %collective-permute-start.7) | collective-permute-done | bytes 147488 | tf_op jit(solution)/shard_map/ppermute | solution.py:49
  127.8 1.5 %collective-permute-done.9 = bf16[288,256]{0,1:T(8,128)(2,1)S(1)} collective-permute-done((bf16[288,256]{0,1:T(8,128)(2,1)S(1)}, bf16[288,256]{0,1:T(8,128)(2,1)S(1)}, u32[]{:S(2)}, u32[]{:S(2)}) %collective-permute-start.9) | collective-permute-done | bytes 147488 | tf_op jit(solution)/shard_map/ppermute | solution.py:49
  130.1 1.7 %collective-permute-start.8 = (bf16[288,256]{0,1:T(8,128)(2,1)S(1)}, bf16[288,256]{0,1:T(8,128)(2,1)S(1)}, u32[]{:S(2)}, u32[]{:S(2)}) collective-permute-start(bf16[288,256]{0,1:T(8,128)(2,1)S(1)} %get-tuple-element.17), channel_id=1, source_target_pairs={{0,4},{4,0},{1,5},{5,1},{2,6},{6,2},{3,7},{7,3},{8,12},{12,8},{9,1... | collective-permute-start | bytes 442376 | tf_op jit(solution)/shard_map/ppermute | solution.py:49
  131.9 3.8 %collective-permute-done.10 = bf16[288,256]{0,1:T(8,128)(2,1)S(1)} collective-permute-done((bf16[288,256]{0,1:T(8,128)(2,1)S(1)}, bf16[288,256]{0,1:T(8,128)(2,1)S(1)}, u32[]{:S(2)}, u32[]{:S(2)}) %collective-permute-start.10) | collective-permute-done | bytes 147488 | tf_op jit(solution)/shard_map/ppermute | solution.py:49
  136.7 2.0 %collective-permute-done.11 = f32[576,256]{1,0:T(8,128)S(1)} collective-permute-done((f32[576,256]{1,0:T(8,128)S(1)}, f32[576,256]{1,0:T(8,128)S(1)}, u32[]{:S(2)}, u32[]{:S(2)}) %collective-permute-start.11) | collective-permute-done | bytes 589856 | tf_op jit(solution)/shard_map/ppermute | solution.py:49
  (65 shorter events, 15.4 us)
Async XLA Ops:
  0.0 18.5 %copy-start = (bf16[1152,256]{1,0:T(8,128)(2,1)S(1)}, bf16[1152,256]{1,0:T(8,128)(2,1)}, u32[]{:S(2)}) copy-start(bf16[1152,256]{1,0:T(8,128)(2,1)} %param.9) | copy-start | bytes 1769476
  1.6 24.4 %collective-permute-start.2 = (bf16[128,256]{1,0:T(8,128)(2,1)}, bf16[128,256]{1,0:T(8,128)(2,1)S(1)}, u32[]{:S(2)}, u32[]{:S(2)}) collective-permute-start(bf16[128,256]{1,0:T(8,128)(2,1)} %get-tuple-element.9), channel_id=1, source_target_pairs={{0,4},{1,5},{2,6},{3,7},{8,12},{9,13},{10,14},{11,15},{16,20},{17,... | collective-permute-start | bytes 196616 | tf_op jit(solution)/shard_map/ppermute | solution.py:17
  6.4 19.5 %collective-permute-start.3 = (bf16[128,256]{1,0:T(8,128)(2,1)S(1)}, bf16[128,256]{1,0:T(8,128)(2,1)S(1)}, u32[]{:S(2)}, u32[]{:S(2)}) collective-permute-start(bf16[128,256]{1,0:T(8,128)(2,1)S(1)} %get-tuple-element.10), channel_id=1, source_target_pairs={{4,0},{5,1},{6,2},{7,3},{12,8},{13,9},{14,10},{15,11},{20,16},{21,... | collective-permute-start | bytes 196616 | tf_op jit(solution)/shard_map/ppermute | solution.py:18
  14.6 11.3 %all-to-all-start = ((s32[2,1,512]{2,1,0:T(1,128)}), s32[2,1,512]{2,1,0:T(1,128)S(1)}, u32[]{:S(2)}, u32[]{:S(2)}) async-start(s32[2,1,512]{2,1,0:T(1,128)} %bitcast.5), calls=%async_computation | async-start | bytes 8192 | tf_op jit(solution)/shard_map/all_to_all | solution.py:33
  18.5 7.1 %copy-start.5 = (s32[8,4096]{1,0:T(8,128)S(1)}, s32[8,4096]{1,0:T(8,128)}, u32[]{:S(2)}) copy-start(s32[8,4096]{1,0:T(8,128)} %param.14) | copy-start | bytes 393220
  18.5 7.3 %copy-start.6 = (f32[8,256]{1,0:T(8,128)S(1)}, f32[8,256]{1,0:T(8,128)}, u32[]{:S(2)}) copy-start(f32[8,256]{1,0:T(8,128)} %param.15) | copy-start | bytes 24580
  18.5 7.5 %copy-start.2 = (bf16[4096,256]{1,0:T(8,128)(2,1)S(1)}, bf16[4096,256]{1,0:T(8,128)(2,1)}, u32[]{:S(2)}) copy-start(bf16[4096,256]{1,0:T(8,128)(2,1)} %param.13) | copy-start | bytes 6291460
  22.6 1.4 copy-start.4
  24.0 47.4 %collective-permute-start = (bf16[1024,256]{1,0:T(8,128)(2,1)S(1)}, bf16[1024,256]{1,0:T(8,128)(2,1)}, u32[]{:S(2)}, u32[]{:S(2)}) collective-permute-start(bf16[1024,256]{1,0:T(8,128)(2,1)S(1)} %dynamic-slice_convert_fusion), channel_id=1, source_target_pairs={{0,1},{1,0},{2,3},{3,2},{4,5},{5,4},{6,7},{7,6},{8,9},{9,8},{10,11... | collective-permute-start | bytes 1572872 | tf_op jit(solution)/shard_map/ppermute | solution.py:49
  49.6 3.4 %copy-start.3 = (bf16[4096,256]{1,0:T(8,128)(2,1)S(1)}, bf16[4096,256]{1,0:T(8,128)(2,1)}, u32[]{:S(2)}) copy-start(bf16[4096,256]{1,0:T(8,128)(2,1)} %param.13) | copy-start | bytes 6291460
  66.6 19.8 %copy-start.7 = (pred[512]{0:T(512)(128)(4,1)S(1)}, pred[512]{0:T(512)(128)(4,1)}, u32[]{:S(2)}) copy-start(pred[512]{0:T(512)(128)(4,1)} %get-tuple-element.5) | copy-start | bytes 1540
  67.7 11.3 %all-to-all-start.1 = ((bf16[2,512,256]{2,1,0:T(8,128)(2,1)}), bf16[2,512,256]{2,1,0:T(8,128)(2,1)S(1)}, u32[]{:S(2)}, u32[]{:S(2)}) async-start(bf16[2,512,256]{2,1,0:T(8,128)(2,1)} %select_select_fusion), calls=%async_computation.1 | async-start | bytes 1048576 | tf_op jit(solution)/shard_map/all_to_all | solution.py:37
  73.0 13.4 %collective-permute-start.1 = (bf16[512,256]{1,0:T(8,128)(2,1)S(1)}, bf16[512,256]{1,0:T(8,128)(2,1)S(1)}, u32[]{:S(2)}, u32[]{:S(2)}) collective-permute-start(bf16[512,256]{1,0:T(8,128)(2,1)S(1)} %dynamic-slice_convert_fusion.2), channel_id=1, source_target_pairs={{0,2},{1,3},{2,0},{3,1},{4,6},{5,7},{6,4},{7,5},{8,10},{9,11},{10,... | collective-permute-start | bytes 786440 | tf_op jit(solution)/shard_map/ppermute | solution.py:49
  86.6 13.8 %collective-permute-start.4 = (bf16[512,256]{1,0:T(8,128)(2,1)S(1)}, bf16[512,256]{1,0:T(8,128)(2,1)S(1)}, u32[]{:S(2)}, u32[]{:S(2)}) collective-permute-start(bf16[512,256]{1,0:T(8,128)(2,1)S(1)} %multiply_convert_fusion), channel_id=1, source_target_pairs={{0,2},{1,3},{2,0},{3,1},{4,6},{5,7},{6,4},{7,5},{8,10},{9,11},{10,... | collective-permute-start | bytes 786440 | tf_op jit(solution)/shard_map/ppermute | solution.py:49
  100.6 13.9 %collective-permute-start.5 = (bf16[1024,256]{1,0:T(8,128)(2,1)S(1)}, bf16[1024,256]{1,0:T(8,128)(2,1)S(1)}, u32[]{:S(2)}, u32[]{:S(2)}) collective-permute-start(bf16[1024,256]{1,0:T(8,128)(2,1)S(1)} %pad_maximum_fusion.5), channel_id=1, source_target_pairs={{0,1},{1,0},{2,3},{3,2},{4,5},{5,4},{6,7},{7,6},{8,9},{9,8},{10,11... | collective-permute-start | bytes 1572872 | tf_op jit(solution)/shard_map/ppermute | solution.py:49
  118.7 1.7 %collective-permute-start.6 = (bf16[576,256]{0,1:T(8,128)(2,1)S(1)}, bf16[576,256]{0,1:T(8,128)(2,1)S(1)}, u32[]{:S(2)}, u32[]{:S(2)}) collective-permute-start(bf16[576,256]{0,1:T(8,128)(2,1)S(1)} %fusion.32), channel_id=1, source_target_pairs={{0,8},{8,0},{16,24},{24,16},{1,9},{9,1},{17,25},{25,17},{2,10},{10... | collective-permute-start | bytes 884744 | tf_op jit(solution)/shard_map/ppermute | solution.py:49
  120.8 7.0 %collective-permute-start.7 = (bf16[288,256]{0,1:T(8,128)(2,1)S(1)}, bf16[288,256]{0,1:T(8,128)(2,1)S(1)}, u32[]{:S(2)}, u32[]{:S(2)}) collective-permute-start(bf16[288,256]{0,1:T(8,128)(2,1)S(1)} %get-tuple-element.19), channel_id=1, source_target_pairs={{0,16},{8,24},{16,0},{24,8},{1,17},{9,25},{17,1},{25,9},{2,18},{10... | collective-permute-start | bytes 442376 | tf_op jit(solution)/shard_map/ppermute | solution.py:49
  122.2 7.2 %collective-permute-start.9 = (bf16[288,256]{0,1:T(8,128)(2,1)S(1)}, bf16[288,256]{0,1:T(8,128)(2,1)S(1)}, u32[]{:S(2)}, u32[]{:S(2)}) collective-permute-start(bf16[288,256]{0,1:T(8,128)(2,1)S(1)} %get-tuple-element.20), channel_id=1, source_target_pairs={{0,4},{4,0},{1,5},{5,1},{2,6},{6,2},{3,7},{7,3},{8,12},{12,8},{9,1... | collective-permute-start | bytes 442376 | tf_op jit(solution)/shard_map/ppermute | solution.py:49
  129.5 6.2 %collective-permute-start.10 = (bf16[288,256]{0,1:T(8,128)(2,1)S(1)}, bf16[288,256]{0,1:T(8,128)(2,1)S(1)}, u32[]{:S(2)}, u32[]{:S(2)}) collective-permute-start(bf16[288,256]{0,1:T(8,128)(2,1)S(1)} %get-tuple-element.18), channel_id=1, source_target_pairs={{0,16},{8,24},{16,0},{24,8},{1,17},{9,25},{17,1},{25,9},{2,18},{10... | collective-permute-start | bytes 442376 | tf_op jit(solution)/shard_map/ppermute | solution.py:49
  130.1 5.8 %collective-permute-start.8 = (bf16[288,256]{0,1:T(8,128)(2,1)S(1)}, bf16[288,256]{0,1:T(8,128)(2,1)S(1)}, u32[]{:S(2)}, u32[]{:S(2)}) collective-permute-start(bf16[288,256]{0,1:T(8,128)(2,1)S(1)} %get-tuple-element.17), channel_id=1, source_target_pairs={{0,4},{4,0},{1,5},{5,1},{2,6},{6,2},{3,7},{7,3},{8,12},{12,8},{9,1... | collective-permute-start | bytes 442376 | tf_op jit(solution)/shard_map/ppermute | solution.py:49
  136.6 2.1 %collective-permute-start.11 = (f32[576,256]{1,0:T(8,128)S(1)}, f32[576,256]{1,0:T(8,128)S(1)}, u32[]{:S(2)}, u32[]{:S(2)}) collective-permute-start(f32[576,256]{1,0:T(8,128)S(1)} %copy.11), channel_id=1, source_target_pairs={{0,8},{8,0},{16,24},{24,16},{1,9},{9,1},{17,25},{25,17},{2,10},{10... | collective-permute-start | bytes 1769480 | tf_op jit(solution)/shard_map/ppermute | solution.py:49
  136.7 4.0 %copy-start.1 = (bf16[1152,256]{1,0:T(8,128)(2,1)S(1)}, bf16[1152,256]{1,0:T(8,128)(2,1)}, u32[]{:S(2)}) copy-start(bf16[1152,256]{1,0:T(8,128)(2,1)} %param.9) | copy-start | bytes 1769476

commit v2 on v0

v2 whole, which is shorter than its diff:
```python
import jax
import jax.numpy as jnp
from jax import lax
from jax.experimental import pallas as pl
from jax.experimental.pallas import tpu as pltpu
from jax.sharding import PartitionSpec as P

NEIGH = 8
HALO = 128
BLOCK = 256
VMEM = 40 * 1024 * 1024


def extended(value, axis, width):
    size, length = lax.axis_size(axis), value.shape[0]
    last = lax.slice_in_dim(value, length - width, length, axis=0)
    first = lax.slice_in_dim(value, 0, width, axis=0)
    if size == 2:
        index = lax.axis_index(axis)
        other = lax.ppermute(jnp.where(index == 0, last, first), axis, [(0, 1), (1, 0)])
        return jnp.concatenate([other, value, other], axis=0)
    up = [(i, (i + 1) % size) for i in range(size - 1)]
    down = [(j, i) for i, j in up]
    before = lax.ppermute(last, axis, up)
    after = lax.ppermute(first, axis, down)
    return jnp.concatenate([before, value, after], axis=0)


def requests(tile_ids, local_ids, capacity):
    tile_count = lax.axis_size("pix")
    onehot = (tile_ids[:, None] == jnp.arange(tile_count, dtype=jnp.int32)[None, :]).astype(
        jnp.int32
    )
    place_rank = jnp.sum((jnp.cumsum(onehot, axis=0) - 1) * onehot, axis=1)
    slot_index = tile_ids * capacity + place_rank
    outgoing = jnp.full((tile_count * capacity,), 0, jnp.int32).at[slot_index].set(local_ids)
    outgoing = outgoing.reshape(tile_count, capacity)
    requested = lax.all_to_all(outgoing, "pix", split_axis=0, concat_axis=0, tiled=True)
    return slot_index, requested.reshape(-1)


def swap(value, axis, bit):
    size = lax.axis_size(axis)
    return lax.ppermute(value, axis, [(i, i ^ bit) for i in range(size)])


def halves(value, which, dim=0):
    length = value.shape[dim] // 2
    own = lax.dynamic_slice_in_dim(value, which * length, length, dim)
    other = lax.dynamic_slice_in_dim(value, (1 - which) * length, length, dim)
    return own, other


def joined(own, other, which):
    first = jnp.where(which == 0, own, other)
    second = jnp.where(which == 0, other, own)
    return jnp.concatenate([first, second], axis=0)


def gather_line(rows, axis):
    size, index = lax.axis_size(axis), lax.axis_index(axis)
    right = left = rows
    blocks = [jnp.zeros_like(rows) if size > 1 else rows] * size
    blocks = [jnp.where(index == place, rows, jnp.zeros_like(rows)) for place in range(size)]
    for step in range(size - 1):
        right = lax.ppermute(right, axis, [(i, i + 1) for i in range(step, size - 1)])
        left = lax.ppermute(left, axis, [(i + 1, i) for i in range(size - 1 - step)])
        for place in range(size):
            blocks[place] = jnp.where(index == place + 1 + step, right, blocks[place])
            blocks[place] = jnp.where(index == place - 1 - step, left, blocks[place])
    return jnp.stack(blocks)


def add_swapped(value, axis, bit):
    value = lax.reduce_precision(value, 8, 7)
    return value + swap(value.astype(jnp.bfloat16), axis, bit).astype(jnp.float32)


def sum_over_panels(value):
    core = lax.axis_index("obs") & 1
    keep, send = halves(value, core)
    keep = keep + swap(send.astype(jnp.bfloat16), "obs", 1).astype(jnp.float32)
    upper, lower = jnp.split(keep, 2, axis=0)
    upper, lower = add_swapped(upper, "obs", 2), add_swapped(lower, "pix", 1)
    upper, lower = add_swapped(upper, "pix", 1), add_swapped(lower, "obs", 2)
    own = jnp.concatenate([upper, lower], axis=0)
    return joined(own, swap(own, "obs", 1), core)


def project_kernel(start, spectra, weight, out):
    out[...] = jnp.dot(
        spectra[...], weight[...], preferred_element_type=jnp.float32
    ).astype(out.dtype)


def project(spectra, weight, first_block, rows, block):
    depth, width = weight.shape
    return pl.pallas_call(
        project_kernel,
        out_shape=jax.ShapeDtypeStruct((rows, width), jnp.bfloat16),
        grid_spec=pltpu.PrefetchScalarGridSpec(
            num_scalar_prefetch=1,
            grid=(rows // block,),
            in_specs=[
                pl.BlockSpec((block, depth), lambda i, start: (start[0] + i, 0)),
                pl.BlockSpec((depth, width), lambda i, start: (0, 0)),
            ],
            out_specs=pl.BlockSpec((block, width), lambda i, start: (i, 0)),
        ),
        compiler_params=pltpu.CompilerParams(vmem_limit_bytes=VMEM),
        cost_estimate=pl.CostEstimate(
            flops=2 * rows * depth * width,
            bytes_accessed=2 * (rows * depth + depth * width + rows * width),
            transcendentals=0,
        ),
        name="project",
    )(first_block.reshape(1).astype(jnp.int32), spectra, weight)


def pixel_kernel(anchor, wanted, adjoint, padded, mixing, out, grads, picked):
    step = pl.program_id(0)
    first = pl.multiple_of(step * BLOCK, BLOCK)
    within = (adjoint[...] - (anchor[0] + first)).T
    window = padded[pl.ds(first, BLOCK + 2 * HALO), :]
    total = padded[pl.ds(first + HALO, BLOCK), :].astype(jnp.float32)
    columns = lax.broadcasted_iota(jnp.int32, (BLOCK, BLOCK + 2 * HALO), 1)
    for neighbor in range(NEIGH):
        selector = (within[:, neighbor : neighbor + 1] == columns).astype(jnp.bfloat16)
        rows = jnp.dot(selector, window, preferred_element_type=jnp.float32)
        total = total + rows * mixing[neighbor : neighbor + 1, :]
    grads[pl.ds(first, BLOCK), :] = total.astype(jnp.bfloat16).astype(jnp.float32)

    @pl.when(step == pl.num_programs(0) - 1)
    def _():
        group = 16

        def body(turn, carry):
            base = pl.multiple_of(turn * group, group)
            for n in range(group):
                picked[n : n + 1, :] = grads[pl.ds(wanted[base + n], 1), :]
            out[pl.ds(base, group), :] = picked[...].astype(jnp.bfloat16)
            return carry

        lax.fori_loop(0, out.shape[0] // group, body, 0)


def pixel_rows(padded, adjoint, mixing, anchor, wanted):
    tile_rows = adjoint.shape[1]
    width = padded.shape[1]
    count = wanted.shape[0]
    return pl.pallas_call(
        pixel_kernel,
        out_shape=jax.ShapeDtypeStruct((count, width), jnp.bfloat16),
        grid=(tile_rows // BLOCK,),
        in_specs=[
            pl.BlockSpec(memory_space=pltpu.SMEM),
            pl.BlockSpec(memory_space=pltpu.SMEM),
            pl.BlockSpec((NEIGH, BLOCK), lambda i: (0, i)),
            pl.BlockSpec(padded.shape, lambda i: (0, 0)),
            pl.BlockSpec(mixing.shape, lambda i: (0, 0)),
        ],
        out_specs=pl.BlockSpec((count, width), lambda i: (0, 0)),
        scratch_shapes=[
            pltpu.VMEM((tile_rows, width), jnp.float32),
            pltpu.VMEM((16, width), jnp.float32),
        ],
        compiler_params=pltpu.CompilerParams(vmem_limit_bytes=VMEM),
        cost_estimate=pl.CostEstimate(
            flops=2 * NEIGH * tile_rows * (BLOCK + 2 * HALO) * width,
            bytes_accessed=4 * tile_rows * width,
            transcendentals=0,
        ),
        name="pixel_rows",
    )(anchor.reshape(1).astype(jnp.int32), wanted, adjoint, padded, mixing)


def pre_gradient(pre, fetched, weights):
    sigma = jax.nn.sigmoid(pre)
    deriv = sigma * (1.0 + pre * (1.0 - sigma))
    return (weights[:, None] * deriv * fetched.astype(jnp.float32)).astype(jnp.bfloat16)


def shards(spectra, enc_weight, pix_tile, pix_local, foot_weight, cotangent, adjoint, mixing):
    tile_count = lax.axis_size("pix")
    groups = lax.axis_size("chan")
    tile_rows = cotangent.shape[0]
    all_rows = spectra.shape[0]
    quarter = all_rows // groups
    half = all_rows // 2
    tile = lax.axis_index("pix")
    chan = lax.axis_index("chan")
    low, high = chan & 1, chan >> 1
    first_row = low * half + high * quarter

    send = project(spectra, enc_weight, (1 - low) * 2, half, quarter)
    received = swap(send, "chan", 1)

    padded = extended(cotangent, "pix", HALO)
    anchor = tile * tile_rows - HALO
    tile_ids = lax.dynamic_slice_in_dim(pix_tile[:, 0], first_row, quarter, 0)
    local_ids = lax.dynamic_slice_in_dim(pix_local, first_row, quarter, 0)
    weights = lax.dynamic_slice_in_dim(foot_weight, first_row, quarter, 0)
    capacity = 2 * quarter // tile_count
    if capacity >= quarter and tile_count == 2:
        wanted = jnp.concatenate([local_ids, swap(local_ids, "pix", 1)])
        rows = pixel_rows(padded, adjoint, mixing, anchor, wanted)
        answers = swap(rows[quarter:], "pix", 1)
        fetched = jnp.where((tile_ids == tile)[:, None], rows[:quarter], answers)
    else:
        slot_index, wanted = requests(tile_ids, local_ids, capacity)
        rows = pixel_rows(padded, adjoint, mixing, anchor, wanted)
        answers = lax.all_to_all(
            rows.reshape(tile_count, capacity, -1), "pix", split_axis=0, concat_axis=0, tiled=True
        )
        fetched = jnp.take(answers.reshape(tile_count * capacity, -1), slot_index, axis=0)

    keep = project(spectra, enc_weight, low * 2, half, quarter)
    total = keep.astype(jnp.float32) + received.astype(jnp.float32)
    keep, send = halves(total, high)
    pre = keep + swap(send.astype(jnp.bfloat16), "chan", 2).astype(jnp.float32)

    grad_part = pre_gradient(pre, fetched, weights)
    blocks = gather_line(grad_part, "chan")
    places = [(c & 1) * 2 + (c >> 1) for c in range(groups)]
    order = [places.index(q) for q in range(groups)]
    grads = jnp.concatenate([blocks[c] for c in order], axis=0)
    local_grad = lax.dot_general(
        spectra, grads, (((0,), (0,)), ((), ())), preferred_element_type=jnp.float32
    )
    if lax.axis_size("obs") == 4 and tile_count == 2:
        return sum_over_panels(local_grad)
    return lax.psum(local_grad, ("obs", "pix"))


def solution(mesh):
    return jax.shard_map(
        shards,
        mesh=mesh,
        in_specs=(
            P(("obs", "pix"), "chan"),
            P("chan", None),
            P(("obs", "pix"), None),
            P(("obs", "pix")),
            P(("obs", "pix")),
            P("pix", None),
            P(None, "pix"),
            P(),
        ),
        out_specs=P("chan", None),
        check_vma=False,
    )
```

time: 186 us -> 107 us (0.58)
  waiting for transfers between devices: 92.2 us -> 45.8 us
  matrix products: 36.7 us -> 3.9 us
  Pallas kernels: 0 us -> 21.3 us
  between operations: 13.3 us -> 0.34 us
  other arithmetic: 14.8 us -> 6.31 us
  starting transfers between devices: 13.7 us -> 19.5 us
  local copies, waits for them, and re-layouts: 14.9 us -> 9.31 us
    psum x1 -> x0, waiting for transfers between devices: 56.7 us -> none  [shards(): return lax.psum(local_grad, ('obs', 'pix'))]
    ppermute x2 -> x17, waiting for transfers between devices: 0.01 us -> 45.8 us  [the longest x10 24.3 us: swap(): return lax.ppermute(value, axis, [(i, i ^ bit) for i in range(size)])]
    dot_general x10 -> x1, matrix products: 36.7 us -> 3.9 us  [shards(): lax.dot_general(spectra, grads, (((0,), (0,)), ((), ())), preferred_eleme...]
    all_gather x1 -> x0, waiting for transfers between devices: 28.2 us -> none  [shards(): lax.all_gather(grad_part, 'chan', axis=0, tiled=True)]
    pallas_call x0 -> x3, Pallas kernels: none -> 21.3 us  [the longest x1 19.2 us: pixel_rows(): pl.pallas_call(pixel_kernel, out_shape=jax.ShapeDtypeStruct((count, width...]
    ppermute x2 -> x17, starting transfers between devices: 6.17 us -> 19.5 us  [the longest x10 12.5 us: swap(): return lax.ppermute(value, axis, [(i, i ^ bit) for i in range(size)])]
    convert_element_type x2, other arithmetic: 9.66 us -> 0.28 us  [add_swapped(): value.astype(jnp.bfloat16)]
    all_to_all x2 -> x0, starting transfers between devices: 7.39 us -> none  [the longest x1 3.91 us: fetch_rows(): lax.all_to_all(outgoing, 'pix', split_axis=0, concat_axis=0, tiled=True)]
  transfers between devices with their start and end apart: 7 -> 17, of which waited for: 3 -> 12; matrix products, arithmetic and copies ran while one was open for 30% -> 4% of each run, Pallas kernels for 0% -> 20%
where the time goes in v2:
time: 107 us; the launch traced here: 106 us
  waiting for transfers between devices  45.8 us (43%)
  Pallas kernels  21.3 us (20%)
  starting transfers between devices  19.5 us (18%)
  local copies, waits for them, and re-layouts  9.31 us (9%)
  other arithmetic  6.31 us (6%)
  matrix products  3.9 us (4%)
    ppermute x10, waiting for transfers between devices, swap(): return lax.ppermute(value, axis, [(i, i ^ bit) for i in range(size)])  24.3 us
    pallas_call x1, Pallas kernels, pixel_rows(): pl.pallas_call(pixel_kernel, out_shape=jax.ShapeDtypeStruct((count, width...  19.2 us
    ppermute x3, waiting for transfers between devices, gather_line(): lax.ppermute(left, axis, [(i + 1, i) for i in range(size - 1 - step)])  17.2 us
    ppermute x10, starting transfers between devices, swap(): return lax.ppermute(value, axis, [(i, i ^ bit) for i in range(size)])  12.5 us
    unnamed x12, local copies, waits for them, and re-layouts  5.75 us
    ppermute x3, waiting for transfers between devices, gather_line(): lax.ppermute(right, axis, [(i, i + 1) for i in range(step, size - 1)])  4.31 us
    dot_general x1, matrix products, shards(): lax.dot_general(spectra, grads, (((0,), (0,)), ((), ())), preferred_eleme...  3.9 us
    ppermute x3, starting transfers between devices, gather_line(): lax.ppermute(left, axis, [(i + 1, i) for i in range(size - 1 - step)])  3.85 us
  transfers between devices with their start and end apart: 17, of which 12 were waited for; matrix products, arithmetic and copies ran while one was open for 4% of the time, Pallas kernels for 20%

profile of v2, /device:TPU:0, one launch (start us, length us, event | category | flops | bytes accessed | tf_op | source)
XLA Modules:
  0.0 106.5 jit_solution(4523786055375541445)
XLA Ops:
  0.0 0.8 dynamic_slice.25
  0.8 3.0 %collective-permute-start.2 = (s32[512]{0:T(512)S(1)}, s32[512]{0:T(512)S(1)}, u32[]{:S(2)}, u32[]{:S(2)}) collective-permute-start(s32[512]{0:T(512)S(1)} %dynamic_slice.25), channel_id=1, source_target_pairs={{0,4},{4,0},{1,5},{5,1},{2,6},{6,2},{3,7},{7,3},{8,12},{12,8},{9,1... | collective-permute-start | bytes 6152 | tf_op jit(solution)/shard_map/ppermute | solution.py:44
  3.7 0.9 slice_select_fusion.1
  4.7 2.3 %copy-done = bf16[2048,1152]{1,0:T(8,128)(2,1)S(1)} copy-done((bf16[2048,1152]{1,0:T(8,128)(2,1)S(1)}, bf16[2048,1152]{1,0:T(8,128)(2,1)}, u32[]{:S(2)}) %copy-start) | copy-done | bytes 4718616
  7.0 1.1 copy-done.2
  8.1 1.0 project.3
  9.1 2.1 %collective-permute-start = (bf16[1024,256]{1,0:T(8,128)(2,1)S(1)}, bf16[1024,256]{1,0:T(8,128)(2,1)S(1)}, u32[]{:S(2)}, u32[]{:S(2)}) collective-permute-start(bf16[1024,256]{1,0:T(8,128)(2,1)S(1)} %project.3), channel_id=1, source_target_pairs={{0,1},{1,0},{2,3},{3,2},{4,5},{5,4},{6,7},{7,6},{8,9},{9,8},{10,11... | collective-permute-start | bytes 1572872 | tf_op jit(solution)/shard_map/ppermute | solution.py:44
  11.3 2.3 %copy-done.1 = bf16[2048,1152]{1,0:T(8,128)(2,1)S(1)} copy-done((bf16[2048,1152]{1,0:T(8,128)(2,1)S(1)}, bf16[2048,1152]{1,0:T(8,128)(2,1)}, u32[]{:S(2)}) %copy-start.1) | copy-done | bytes 4718616
  13.6 1.0 project.2
  14.7 1.8 %pad_maximum_fusion.padded = bf16[4352,256]{1,0:T(8,128)(2,1)S(1)} fusion(bf16[128,256]{1,0:T(8,128)(2,1)S(1)} %collective-permute-done.3, bf16[4096,256]{1,0:T(8,128)(2,1)} %param.13), kind=kLoop, calls=%fused_computation | loop fusion | flops 6684672 | bytes 4390912 | tf_op jit(solution)/shard_map/concatenate | solution.py:21
  16.5 19.2 %pixel_rows.1 = bf16[1024,256]{1,0:T(8,128)(2,1)S(1)} custom-call(s32[1]{0:T(128)} %bitcast.2.anchor, s32[1024]{0:T(1024)S(1)} %pad_add_fusion.wanted, s32[8,4096]{1,0:T(8,128)S(1)} %copy-done.4, bf16[4352,256]{1,0:T(8,128)(2,1)S(1)} %pad_maximum_fusion.padded, f32[8,256]{1,0:T(8,128)S(1)} %copy-done.5), custom_call_target="tpu_custom_call" | custom-call | flops 8589934592 | bytes 4194304 | tf_op jit(solution)/shard_map/pixel_rows/pallas_call | solution.py:151
  35.8 1.6 %collective-permute-start.4 = (bf16[512,256]{1,0:T(8,128)(2,1)S(1)}, bf16[512,256]{1,0:T(8,128)(2,1)}, u32[]{:S(2)}, u32[]{:S(2)}) collective-permute-start(bf16[512,256]{1,0:T(8,128)(2,1)S(1)} %slice.17), channel_id=1, source_target_pairs={{0,4},{4,0},{1,5},{5,1},{2,6},{6,2},{3,7},{7,3},{8,12},{12,8},{9,1... | collective-permute-start | bytes 786440 | tf_op jit(solution)/shard_map/ppermute | solution.py:44
  37.5 2.7 %collective-permute-start.1 = (bf16[512,256]{1,0:T(8,128)(2,1)S(1)}, bf16[512,256]{1,0:T(8,128)(2,1)S(1)}, u32[]{:S(2)}, u32[]{:S(2)}) collective-permute-start(bf16[512,256]{1,0:T(8,128)(2,1)S(1)} %dynamic-slice_convert_fusion.1), channel_id=1, source_target_pairs={{0,2},{1,3},{2,0},{3,1},{4,6},{5,7},{6,4},{7,5},{8,10},{9,11},{10,... | collective-permute-start | bytes 786440 | tf_op jit(solution)/shard_map/ppermute | solution.py:44
  41.6 1.5 %collective-permute-done.4 = bf16[512,256]{1,0:T(8,128)(2,1)} collective-permute-done((bf16[512,256]{1,0:T(8,128)(2,1)S(1)}, bf16[512,256]{1,0:T(8,128)(2,1)}, u32[]{:S(2)}, u32[]{:S(2)}) %collective-permute-start.4) | collective-permute-done | bytes 262176 | tf_op jit(solution)/shard_map/ppermute | solution.py:44
  43.1 7.8 %collective-permute-done.1 = bf16[512,256]{1,0:T(8,128)(2,1)S(1)} collective-permute-done((bf16[512,256]{1,0:T(8,128)(2,1)S(1)}, bf16[512,256]{1,0:T(8,128)(2,1)S(1)}, u32[]{:S(2)}, u32[]{:S(2)}) %collective-permute-start.1) | collective-permute-done | bytes 262176 | tf_op jit(solution)/shard_map/ppermute | solution.py:44
  50.9 1.2 %multiply_convert_fusion = bf16[512,256]{1,0:T(8,128)(2,1)S(1)} fusion(bf16[512,256]{1,0:T(8,128)(2,1)S(1)} %collective-permute-done.1, f32[1024,256]{1,0:T(8,128)S(1)} %convert_add_fusion, s32[]{:T(128)S(6)} %select_n.178, bf16[512,256]{1,0:T(8,128)(2,1)} %collective-permute-done.4, bf16[1024,256]{1,0:T(8,128)(2,1)S(1)} %pixel_rows.1, ...), kind=kLoop, calls=%fused_computation.14 | loop fusion | flops 1835008 | bytes 1575428 | tf_op jit(solution)/shard_map/convert_element_type | solution.py:180
  52.2 1.7 %collective-permute-start.8 = (bf16[512,256]{1,0:T(8,128)(2,1)S(1)}, bf16[512,256]{1,0:T(8,128)(2,1)S(1)}, u32[]{:S(2)}, u32[]{:S(2)}) collective-permute-start(bf16[512,256]{1,0:T(8,128)(2,1)S(1)} %multiply_convert_fusion), channel_id=1, source_target_pairs={{0,1},{1,2},{2,3},{4,5},{5,6},{6,7},{8,9},{9,10},{10,11},{12,13},{... | collective-permute-start | bytes 786440 | tf_op jit(solution)/shard_map/ppermute | solution.py:66
  53.9 1.3 %collective-permute-start.5 = (bf16[512,256]{1,0:T(8,128)(2,1)S(1)}, bf16[512,256]{1,0:T(8,128)(2,1)S(1)}, u32[]{:S(2)}, u32[]{:S(2)}) collective-permute-start(bf16[512,256]{1,0:T(8,128)(2,1)S(1)} %multiply_convert_fusion), channel_id=1, source_target_pairs={{1,0},{2,1},{3,2},{5,4},{6,5},{7,6},{9,8},{10,9},{11,10},{13,12},{... | collective-permute-start | bytes 786440 | tf_op jit(solution)/shard_map/ppermute | solution.py:67
  55.2 4.3 %collective-permute-done.8 = bf16[512,256]{1,0:T(8,128)(2,1)S(1)} collective-permute-done((bf16[512,256]{1,0:T(8,128)(2,1)S(1)}, bf16[512,256]{1,0:T(8,128)(2,1)S(1)}, u32[]{:S(2)}, u32[]{:S(2)}) %collective-permute-start.8) | collective-permute-done | bytes 262176 | tf_op jit(solution)/shard_map/ppermute | solution.py:66
  60.1 3.5 %collective-permute-done.5 = bf16[512,256]{1,0:T(8,128)(2,1)S(1)} collective-permute-done((bf16[512,256]{1,0:T(8,128)(2,1)S(1)}, bf16[512,256]{1,0:T(8,128)(2,1)S(1)}, u32[]{:S(2)}, u32[]{:S(2)}) %collective-permute-start.5) | collective-permute-done | bytes 262176 | tf_op jit(solution)/shard_map/ppermute | solution.py:67
  63.6 1.3 %collective-permute-start.6 = (bf16[512,256]{1,0:T(8,128)(2,1)S(1)}, bf16[512,256]{1,0:T(8,128)(2,1)S(1)}, u32[]{:S(2)}, u32[]{:S(2)}) collective-permute-start(bf16[512,256]{1,0:T(8,128)(2,1)S(1)} %collective-permute-done.5), channel_id=1, source_target_pairs={{1,0},{2,1},{5,4},{6,5},{9,8},{10,9},{13,12},{14,13},{17,16},{18,1... | collective-permute-start | bytes 786440 | tf_op jit(solution)/shard_map/ppermute | solution.py:67
  65.6 6.8 %collective-permute-done.6 = bf16[512,256]{1,0:T(8,128)(2,1)S(1)} collective-permute-done((bf16[512,256]{1,0:T(8,128)(2,1)S(1)}, bf16[512,256]{1,0:T(8,128)(2,1)S(1)}, u32[]{:S(2)}, u32[]{:S(2)}) %collective-permute-start.6) | collective-permute-done | bytes 262176 | tf_op jit(solution)/shard_map/ppermute | solution.py:67
  72.4 1.3 %collective-permute-start.7 = (bf16[512,256]{1,0:T(8,128)(2,1)S(1)}, bf16[512,256]{1,0:T(8,128)(2,1)S(1)}, u32[]{:S(2)}, u32[]{:S(2)}) collective-permute-start(bf16[512,256]{1,0:T(8,128)(2,1)S(1)} %collective-permute-done.6), channel_id=1, source_target_pairs={{1,0},{5,4},{9,8},{13,12},{17,16},{21,20},{25,24},{29,28}} | collective-permute-start | bytes 786440 | tf_op jit(solution)/shard_map/ppermute | solution.py:67
  73.8 6.9 %collective-permute-done.7 = bf16[512,256]{1,0:T(8,128)(2,1)S(1)} collective-permute-done((bf16[512,256]{1,0:T(8,128)(2,1)S(1)}, bf16[512,256]{1,0:T(8,128)(2,1)S(1)}, u32[]{:S(2)}, u32[]{:S(2)}) %collective-permute-start.7) | collective-permute-done | bytes 262176 | tf_op jit(solution)/shard_map/ppermute | solution.py:67
  80.9 3.9 %fusion = f32[256,1152]{1,0:T(8,128)S(1)} fusion(bf16[2048,1152]{1,0:T(8,128)(2,1)} %spectra.3, bf16[512,256]{1,0:T(8,128)(2,1)S(1)} %get-tuple-element.6, bf16[512,256]{1,0:T(8,128)(2,1)S(1)} %get-tuple-element.7, bf16[512,256]{1,0:T(8,128)(2,1)S(1)} %get-tuple-element.8, bf16[512,256]{1,0:T(8,128)(2,1)S(1)} %get-tuple-element.5), kind=kOutput, calls=%fused_computation.2 | convolution fusion | flops 1212153856 | bytes 6946816 | tf_op jit(solution)/shard_map/dot_general | solution.py:227
  85.1 1.6 %collective-permute-done.11 = bf16[576,256]{0,1:T(8,128)(2,1)S(1)} collective-permute-done((bf16[576,256]{0,1:T(8,128)(2,1)S(1)}, bf16[576,256]{0,1:T(8,128)(2,1)S(1)}, u32[]{:S(2)}, u32[]{:S(2)}) %collective-permute-start.11) | collective-permute-done | bytes 294944 | tf_op jit(solution)/shard_map/ppermute | solution.py:44
  87.1 1.6 %collective-permute-start.12 = (bf16[288,256]{0,1:T(8,128)(2,1)S(1)}, bf16[288,256]{0,1:T(8,128)(2,1)S(1)}, u32[]{:S(2)}, u32[]{:S(2)}) collective-permute-start(bf16[288,256]{0,1:T(8,128)(2,1)S(1)} %get-tuple-element.15), channel_id=1, source_target_pairs={{0,16},{8,24},{16,0},{24,8},{1,17},{9,25},{17,1},{25,9},{2,18},{10... | collective-permute-start | bytes 442376 | tf_op jit(solution)/shard_map/ppermute | solution.py:44
  89.1 4.9 %collective-permute-done.12 = bf16[288,256]{0,1:T(8,128)(2,1)S(1)} collective-permute-done((bf16[288,256]{0,1:T(8,128)(2,1)S(1)}, bf16[288,256]{0,1:T(8,128)(2,1)S(1)}, u32[]{:S(2)}, u32[]{:S(2)}) %collective-permute-start.12) | collective-permute-done | bytes 147488 | tf_op jit(solution)/shard_map/ppermute | solution.py:44
  94.1 1.2 %collective-permute-done.14 = bf16[288,256]{0,1:T(8,128)(2,1)S(1)} collective-permute-done((bf16[288,256]{0,1:T(8,128)(2,1)S(1)}, bf16[288,256]{0,1:T(8,128)(2,1)S(1)}, u32[]{:S(2)}, u32[]{:S(2)}) %collective-permute-start.14) | collective-permute-done | bytes 147488 | tf_op jit(solution)/shard_map/ppermute | solution.py:44
  96.5 4.9 %collective-permute-done.13 = bf16[288,256]{0,1:T(8,128)(2,1)S(1)} collective-permute-done((bf16[288,256]{0,1:T(8,128)(2,1)S(1)}, bf16[288,256]{0,1:T(8,128)(2,1)S(1)}, u32[]{:S(2)}, u32[]{:S(2)}) %collective-permute-start.13) | collective-permute-done | bytes 147488 | tf_op jit(solution)/shard_map/ppermute | solution.py:44
  102.4 2.0 %collective-permute-done.16 = f32[576,256]{1,0:T(8,128)S(1)} collective-permute-done((f32[576,256]{1,0:T(8,128)S(1)}, f32[576,256]{1,0:T(8,128)S(1)}, u32[]{:S(2)}, u32[]{:S(2)}) %collective-permute-start.16) | collective-permute-done | bytes 589856 | tf_op jit(solution)/shard_map/ppermute | solution.py:44
  105.1 1.4 %copy.13 = f32[1152,256]{1,0:T(8,128)} copy(f32[1152,256]{0,1:T(8,128)S(1)} %pad_maximum_fusion.1) | data formatting | bytes 2359296 | tf_op jit(solution)/shard_map/concatenate | solution.py:57
  (40 shorter events, 7.3 us)
Async XLA Ops:
  0.8 13.9 %collective-permute-start.2 = (s32[512]{0:T(512)S(1)}, s32[512]{0:T(512)S(1)}, u32[]{:S(2)}, u32[]{:S(2)}) collective-permute-start(s32[512]{0:T(512)S(1)} %dynamic_slice.25), channel_id=1, source_target_pairs={{0,4},{4,0},{1,5},{5,1},{2,6},{6,2},{3,7},{7,3},{8,12},{12,8},{9,1... | collective-permute-start | bytes 6152 | tf_op jit(solution)/shard_map/ppermute | solution.py:44
  4.6 10.1 %collective-permute-start.3 = (bf16[128,256]{1,0:T(8,128)(2,1)S(1)}, bf16[128,256]{1,0:T(8,128)(2,1)S(1)}, u32[]{:S(2)}, u32[]{:S(2)}) collective-permute-start(bf16[128,256]{1,0:T(8,128)(2,1)S(1)} %slice_select_fusion.1), channel_id=1, source_target_pairs={{0,4},{4,0},{1,5},{5,1},{2,6},{6,2},{3,7},{7,3},{8,12},{12,8},{9,1... | collective-permute-start | bytes 196616 | tf_op jit(solution)/shard_map/ppermute | solution.py:20
  4.7 2.3 %copy-start = (bf16[2048,1152]{1,0:T(8,128)(2,1)S(1)}, bf16[2048,1152]{1,0:T(8,128)(2,1)}, u32[]{:S(2)}) copy-start(bf16[2048,1152]{1,0:T(8,128)(2,1)} %spectra.3) | copy-start | bytes 14155780
  7.0 1.1 copy-start.2
  8.1 3.2 %copy-start.3 = (bf16[1152,256]{1,0:T(8,128)(2,1)S(1)}, bf16[1152,256]{1,0:T(8,128)(2,1)}, u32[]{:S(2)}) copy-start(bf16[1152,256]{1,0:T(8,128)(2,1)} %weight.3) | copy-start | bytes 1769476
  9.1 28.2 %collective-permute-start = (bf16[1024,256]{1,0:T(8,128)(2,1)S(1)}, bf16[1024,256]{1,0:T(8,128)(2,1)S(1)}, u32[]{:S(2)}, u32[]{:S(2)}) collective-permute-start(bf16[1024,256]{1,0:T(8,128)(2,1)S(1)} %project.3), channel_id=1, source_target_pairs={{0,1},{1,0},{2,3},{3,2},{4,5},{5,4},{6,7},{7,6},{8,9},{9,8},{10,11... | collective-permute-start | bytes 1572872 | tf_op jit(solution)/shard_map/ppermute | solution.py:44
  11.3 2.3 %copy-start.1 = (bf16[2048,1152]{1,0:T(8,128)(2,1)S(1)}, bf16[2048,1152]{1,0:T(8,128)(2,1)}, u32[]{:S(2)}) copy-start(bf16[2048,1152]{1,0:T(8,128)(2,1)} %spectra.3) | copy-start | bytes 14155780
  14.7 1.8 %copy-start.4 = (s32[8,4096]{1,0:T(8,128)S(1)}, s32[8,4096]{1,0:T(8,128)}, u32[]{:S(2)}) copy-start(s32[8,4096]{1,0:T(8,128)} %adjoint.1) | copy-start | bytes 393220
  14.7 1.8 %copy-start.5 = (f32[8,256]{1,0:T(8,128)S(1)}, f32[8,256]{1,0:T(8,128)}, u32[]{:S(2)}) copy-start(f32[8,256]{1,0:T(8,128)} %mixing.1) | copy-start | bytes 24580
  35.8 7.4 %collective-permute-start.4 = (bf16[512,256]{1,0:T(8,128)(2,1)S(1)}, bf16[512,256]{1,0:T(8,128)(2,1)}, u32[]{:S(2)}, u32[]{:S(2)}) collective-permute-start(bf16[512,256]{1,0:T(8,128)(2,1)S(1)} %slice.17), channel_id=1, source_target_pairs={{0,4},{4,0},{1,5},{5,1},{2,6},{6,2},{3,7},{7,3},{8,12},{12,8},{9,1... | collective-permute-start | bytes 786440 | tf_op jit(solution)/shard_map/ppermute | solution.py:44
  37.5 13.4 %collective-permute-start.1 = (bf16[512,256]{1,0:T(8,128)(2,1)S(1)}, bf16[512,256]{1,0:T(8,128)(2,1)S(1)}, u32[]{:S(2)}, u32[]{:S(2)}) collective-permute-start(bf16[512,256]{1,0:T(8,128)(2,1)S(1)} %dynamic-slice_convert_fusion.1), channel_id=1, source_target_pairs={{0,2},{1,3},{2,0},{3,1},{4,6},{5,7},{6,4},{7,5},{8,10},{9,11},{10,... | collective-permute-start | bytes 786440 | tf_op jit(solution)/shard_map/ppermute | solution.py:44
  52.2 7.3 %collective-permute-start.8 = (bf16[512,256]{1,0:T(8,128)(2,1)S(1)}, bf16[512,256]{1,0:T(8,128)(2,1)S(1)}, u32[]{:S(2)}, u32[]{:S(2)}) collective-permute-start(bf16[512,256]{1,0:T(8,128)(2,1)S(1)} %multiply_convert_fusion), channel_id=1, source_target_pairs={{0,1},{1,2},{2,3},{4,5},{5,6},{6,7},{8,9},{9,10},{10,11},{12,13},{... | collective-permute-start | bytes 786440 | tf_op jit(solution)/shard_map/ppermute | solution.py:66
  53.9 9.7 %collective-permute-start.5 = (bf16[512,256]{1,0:T(8,128)(2,1)S(1)}, bf16[512,256]{1,0:T(8,128)(2,1)S(1)}, u32[]{:S(2)}, u32[]{:S(2)}) collective-permute-start(bf16[512,256]{1,0:T(8,128)(2,1)S(1)} %multiply_convert_fusion), channel_id=1, source_target_pairs={{1,0},{2,1},{3,2},{5,4},{6,5},{7,6},{9,8},{10,9},{11,10},{13,12},{... | collective-permute-start | bytes 786440 | tf_op jit(solution)/shard_map/ppermute | solution.py:67
  59.5 5.4 %collective-permute-start.9 = (bf16[512,256]{1,0:T(8,128)(2,1)S(1)}, bf16[512,256]{1,0:T(8,128)(2,1)S(1)}, u32[]{:S(2)}, u32[]{:S(2)}) collective-permute-start(bf16[512,256]{1,0:T(8,128)(2,1)S(1)} %collective-permute-done.8), channel_id=1, source_target_pairs={{1,2},{2,3},{5,6},{6,7},{9,10},{10,11},{13,14},{14,15},{17,18},{18... | collective-permute-start | bytes 786440 | tf_op jit(solution)/shard_map/ppermute | solution.py:66
  63.6 8.8 %collective-permute-start.6 = (bf16[512,256]{1,0:T(8,128)(2,1)S(1)}, bf16[512,256]{1,0:T(8,128)(2,1)S(1)}, u32[]{:S(2)}, u32[]{:S(2)}) collective-permute-start(bf16[512,256]{1,0:T(8,128)(2,1)S(1)} %collective-permute-done.5), channel_id=1, source_target_pairs={{1,0},{2,1},{5,4},{6,5},{9,8},{10,9},{13,12},{14,13},{17,16},{18,1... | collective-permute-start | bytes 786440 | tf_op jit(solution)/shard_map/ppermute | solution.py:67
  64.9 8.8 %collective-permute-start.10 = (bf16[512,256]{1,0:T(8,128)(2,1)S(1)}, bf16[512,256]{1,0:T(8,128)(2,1)S(1)}, u32[]{:S(2)}, u32[]{:S(2)}) collective-permute-start(bf16[512,256]{1,0:T(8,128)(2,1)S(1)} %collective-permute-done.9), channel_id=1, source_target_pairs={{2,3},{6,7},{10,11},{14,15},{18,19},{22,23},{26,27},{30,31}} | collective-permute-start | bytes 786440 | tf_op jit(solution)/shard_map/ppermute | solution.py:66
  72.4 8.3 %collective-permute-start.7 = (bf16[512,256]{1,0:T(8,128)(2,1)S(1)}, bf16[512,256]{1,0:T(8,128)(2,1)S(1)}, u32[]{:S(2)}, u32[]{:S(2)}) collective-permute-start(bf16[512,256]{1,0:T(8,128)(2,1)S(1)} %collective-permute-done.6), channel_id=1, source_target_pairs={{1,0},{5,4},{9,8},{13,12},{17,16},{21,20},{25,24},{29,28}} | collective-permute-start | bytes 786440 | tf_op jit(solution)/shard_map/ppermute | solution.py:67
  85.0 1.7 %collective-permute-start.11 = (bf16[576,256]{0,1:T(8,128)(2,1)S(1)}, bf16[576,256]{0,1:T(8,128)(2,1)S(1)}, u32[]{:S(2)}, u32[]{:S(2)}) collective-permute-start(bf16[576,256]{0,1:T(8,128)(2,1)S(1)} %fusion.10), channel_id=1, source_target_pairs={{0,8},{8,0},{16,24},{24,16},{1,9},{9,1},{17,25},{25,17},{2,10},{10... | collective-permute-start | bytes 884744 | tf_op jit(solution)/shard_map/ppermute | solution.py:44
  87.1 7.0 %collective-permute-start.12 = (bf16[288,256]{0,1:T(8,128)(2,1)S(1)}, bf16[288,256]{0,1:T(8,128)(2,1)S(1)}, u32[]{:S(2)}, u32[]{:S(2)}) collective-permute-start(bf16[288,256]{0,1:T(8,128)(2,1)S(1)} %get-tuple-element.15), channel_id=1, source_target_pairs={{0,16},{8,24},{16,0},{24,8},{1,17},{9,25},{17,1},{25,9},{2,18},{10... | collective-permute-start | bytes 442376 | tf_op jit(solution)/shard_map/ppermute | solution.py:44
  88.6 6.7 %collective-permute-start.14 = (bf16[288,256]{0,1:T(8,128)(2,1)S(1)}, bf16[288,256]{0,1:T(8,128)(2,1)S(1)}, u32[]{:S(2)}, u32[]{:S(2)}) collective-permute-start(bf16[288,256]{0,1:T(8,128)(2,1)S(1)} %get-tuple-element.16), channel_id=1, source_target_pairs={{0,4},{4,0},{1,5},{5,1},{2,6},{6,2},{3,7},{7,3},{8,12},{12,8},{9,1... | collective-permute-start | bytes 442376 | tf_op jit(solution)/shard_map/ppermute | solution.py:44
  95.5 5.9 %collective-permute-start.13 = (bf16[288,256]{0,1:T(8,128)(2,1)S(1)}, bf16[288,256]{0,1:T(8,128)(2,1)S(1)}, u32[]{:S(2)}, u32[]{:S(2)}) collective-permute-start(bf16[288,256]{0,1:T(8,128)(2,1)S(1)} %get-tuple-element.13), channel_id=1, source_target_pairs={{0,4},{4,0},{1,5},{5,1},{2,6},{6,2},{3,7},{7,3},{8,12},{12,8},{9,1... | collective-permute-start | bytes 442376 | tf_op jit(solution)/shard_map/ppermute | solution.py:44
  96.0 5.7 %collective-permute-start.15 = (bf16[288,256]{0,1:T(8,128)(2,1)S(1)}, bf16[288,256]{0,1:T(8,128)(2,1)S(1)}, u32[]{:S(2)}, u32[]{:S(2)}) collective-permute-start(bf16[288,256]{0,1:T(8,128)(2,1)S(1)} %get-tuple-element.14), channel_id=1, source_target_pairs={{0,16},{8,24},{16,0},{24,8},{1,17},{9,25},{17,1},{25,9},{2,18},{10... | collective-permute-start | bytes 442376 | tf_op jit(solution)/shard_map/ppermute | solution.py:44
  102.3 2.1 %collective-permute-start.16 = (f32[576,256]{1,0:T(8,128)S(1)}, f32[576,256]{1,0:T(8,128)S(1)}, u32[]{:S(2)}, u32[]{:S(2)}) collective-permute-start(f32[576,256]{1,0:T(8,128)S(1)} %copy.10), channel_id=1, source_target_pairs={{0,8},{8,0},{16,24},{24,16},{1,9},{9,1},{17,25},{25,17},{2,10},{10... | collective-permute-start | bytes 1769480 | tf_op jit(solution)/shard_map/ppermute | solution.py:44

commit v3 on v2

v3 whole, which is shorter than its diff:
```python
import jax
import jax.numpy as jnp
from jax import lax
from jax.experimental import pallas as pl
from jax.experimental.pallas import tpu as pltpu
from jax.sharding import PartitionSpec as P

NEIGH = 8
HALO = 128
BLOCK = 256
VMEM = 56 * 1024 * 1024


def edges(value, axis, width):
    size, length = lax.axis_size(axis), value.shape[0]
    last = lax.slice_in_dim(value, length - width, length, axis=0)
    first = lax.slice_in_dim(value, 0, width, axis=0)
    if size == 2:
        index = lax.axis_index(axis)
        other = lax.ppermute(jnp.where(index == 0, last, first), axis, [(0, 1), (1, 0)])
        return other, other
    up = [(i, i + 1) for i in range(size - 1)]
    return lax.ppermute(last, axis, up), lax.ppermute(first, axis, [(j, i) for i, j in up])


def requests(tile_ids, local_ids, capacity):
    tile_count = lax.axis_size("pix")
    onehot = (tile_ids[:, None] == jnp.arange(tile_count, dtype=jnp.int32)[None, :]).astype(
        jnp.int32
    )
    place_rank = jnp.sum((jnp.cumsum(onehot, axis=0) - 1) * onehot, axis=1)
    slot_index = tile_ids * capacity + place_rank
    outgoing = jnp.full((tile_count * capacity,), 0, jnp.int32).at[slot_index].set(local_ids)
    outgoing = outgoing.reshape(tile_count, capacity)
    requested = lax.all_to_all(outgoing, "pix", split_axis=0, concat_axis=0, tiled=True)
    return slot_index, requested.reshape(-1)


def swap(value, axis, bit):
    size = 1
    for name in (axis,) if isinstance(axis, str) else axis:
        size *= lax.axis_size(name)
    return lax.ppermute(value, axis, [(i, i ^ bit) for i in range(size)])


def project_kernel(quarters, spectra, weight, first, second):
    result = jnp.dot(
        spectra[...], weight[...], preferred_element_type=jnp.float32
    ).astype(first.dtype)

    @pl.when(pl.program_id(0) == 0)
    def _():
        first[...] = result

    @pl.when(pl.program_id(0) == 1)
    def _():
        second[...] = result


def project(spectra, weight, quarters):
    depth, width = weight.shape
    rows = spectra.shape[0] // 4
    part = jax.ShapeDtypeStruct((rows, width), jnp.bfloat16)
    return pl.pallas_call(
        project_kernel,
        out_shape=(part, part),
        grid_spec=pltpu.PrefetchScalarGridSpec(
            num_scalar_prefetch=1,
            grid=(2,),
            in_specs=[
                pl.BlockSpec((rows, depth), lambda i, quarters: (quarters[i], 0)),
                pl.BlockSpec((depth, width), lambda i, quarters: (0, 0)),
            ],
            out_specs=(
                pl.BlockSpec((rows, width), lambda i, quarters: (0, 0)),
                pl.BlockSpec((rows, width), lambda i, quarters: (0, 0)),
            ),
        ),
        compiler_params=pltpu.CompilerParams(vmem_limit_bytes=VMEM),
        cost_estimate=pl.CostEstimate(
            flops=4 * rows * depth * width,
            bytes_accessed=4 * rows * depth + 2 * depth * width + 4 * rows * width,
            transcendentals=0,
        ),
        name="project",
    )(quarters, spectra, weight)


def backproject_kernel(quarters, spectra, first, second, *rest):
    step = pl.program_id(0)
    before, total = rest if len(rest) == 2 else (None, rest[0])

    def product(rows):
        return lax.dot_general(
            spectra[...], rows[...], (((0,), (0,)), ((), ())), preferred_element_type=jnp.float32
        )

    @pl.when(step == 0)
    def _():
        total[...] = product(first) if before is None else before[...] + product(first)

    @pl.when(step == 1)
    def _():
        total[...] += product(second)


def backproject(spectra, quarters, first, second, before=None):
    depth = spectra.shape[1]
    rows, width = first.shape
    whole = [pl.BlockSpec(x.shape, lambda i, quarters: (0, 0)) for x in (first, second)]
    operands = (first, second)
    if before is not None:
        whole.append(pl.BlockSpec(before.shape, lambda i, quarters: (0, 0)))
        operands += (before,)
    return pl.pallas_call(
        backproject_kernel,
        out_shape=jax.ShapeDtypeStruct((depth, width), jnp.float32),
        grid_spec=pltpu.PrefetchScalarGridSpec(
            num_scalar_prefetch=1,
            grid=(2,),
            in_specs=[
                pl.BlockSpec((rows, depth), lambda i, quarters: (quarters[i], 0)),
                *whole,
            ],
            out_specs=pl.BlockSpec((depth, width), lambda i, quarters: (0, 0)),
        ),
        compiler_params=pltpu.CompilerParams(vmem_limit_bytes=VMEM),
        cost_estimate=pl.CostEstimate(
            flops=4 * rows * depth * width,
            bytes_accessed=4 * rows * depth + 8 * depth * width,
            transcendentals=0,
        ),
        name="backproject",
    )(quarters, spectra, *operands)


def column(row):
    return jnp.broadcast_to(row, (8, row.shape[1])).T[:, :1]


def pixel_kernel(anchor, wanted, adjoint, cotangent, above, below, mixing, out,
                 window, selector, grads):
    step = pl.program_id(0)
    last = pl.num_programs(0) - 1
    first = pl.multiple_of(step * BLOCK, BLOCK)
    wide = BLOCK + 2 * HALO

    window[HALO : HALO + BLOCK, :] = cotangent[pl.ds(first, BLOCK), :]

    @pl.when(step == 0)
    def _():
        window[:HALO, :] = above[...]

    @pl.when(step > 0)
    def _():
        window[:HALO, :] = cotangent[pl.ds(pl.multiple_of(first - HALO, HALO), HALO), :]

    @pl.when(step == last)
    def _():
        window[HALO + BLOCK :, :] = below[...]

    @pl.when(step < last)
    def _():
        window[HALO + BLOCK :, :] = cotangent[pl.ds(pl.multiple_of(first + BLOCK, HALO), HALO), :]

    within = (adjoint[...] - (anchor[0] + first + wide // 2)).T.astype(jnp.float32)
    columns = lax.broadcasted_iota(jnp.int32, (BLOCK, wide), 1) - wide // 2
    columns = columns.astype(jnp.float32).astype(jnp.bfloat16)
    for neighbor in range(1, NEIGH):
        place = within[:, neighbor : neighbor + 1].astype(jnp.bfloat16)
        selector[(neighbor - 1) * BLOCK : neighbor * BLOCK, :] = jnp.where(
            place == columns, jnp.bfloat16(1), jnp.bfloat16(0)
        )
    rows = jnp.dot(selector[...], window[...], preferred_element_type=jnp.float32)
    total = window[HALO : HALO + BLOCK, :].astype(jnp.float32)
    place = lax.broadcasted_iota(jnp.int32, (BLOCK, 1), 0).astype(jnp.float32) - wide // 2
    ahead = jnp.where(
        within[:, :1] == place,
        window[:BLOCK, :].astype(jnp.float32),
        window[2 * HALO :, :].astype(jnp.float32),
    )
    total = total + ahead * mixing[0:1, :]
    for neighbor in range(1, NEIGH):
        part = rows[(neighbor - 1) * BLOCK : neighbor * BLOCK, :]
        total = total + part * mixing[neighbor : neighbor + 1, :]
    grads[pl.ds(first, BLOCK), :] = total.astype(jnp.bfloat16)

    @pl.when(step == last)
    def _():
        group = wanted.shape[1]
        lanes = lax.broadcasted_iota(jnp.int32, (group, BLOCK), 1)
        lanes = lanes.astype(jnp.float32).astype(jnp.bfloat16)
        tile_rows = grads.shape[0]
        for turn in range(wanted.shape[0]):
            names = column(wanted[turn : turn + 1, :])
            found = jnp.zeros((group, grads.shape[1]), jnp.float32)
            picks = []
            for block in range(tile_rows // BLOCK):
                near = names - block * BLOCK
                near = jnp.where((near >= 0) & (near < BLOCK), near, -1)
                near = near.astype(jnp.float32).astype(jnp.bfloat16)
                picks.append(jnp.where(near == lanes, jnp.bfloat16(1), jnp.bfloat16(0)))
            found = jnp.dot(
                jnp.concatenate(picks, axis=1), grads[...], preferred_element_type=jnp.float32
            )
            out[turn * group : (turn + 1) * group, :] = found.astype(jnp.bfloat16)


def pixel_rows(cotangent, above, below, adjoint, mixing, anchor, wanted):
    tile_rows, width = cotangent.shape
    count = wanted.shape[0]
    group = 256
    wide = BLOCK + 2 * HALO
    return pl.pallas_call(
        pixel_kernel,
        out_shape=jax.ShapeDtypeStruct((count, width), jnp.bfloat16),
        grid=(tile_rows // BLOCK,),
        in_specs=[
            pl.BlockSpec(memory_space=pltpu.SMEM),
            pl.BlockSpec((count // group, group), lambda i: (0, 0)),
            pl.BlockSpec((NEIGH, BLOCK), lambda i: (0, i)),
            pl.BlockSpec(cotangent.shape, lambda i: (0, 0)),
            pl.BlockSpec(above.shape, lambda i: (0, 0)),
            pl.BlockSpec(below.shape, lambda i: (0, 0)),
            pl.BlockSpec(mixing.shape, lambda i: (0, 0)),
        ],
        out_specs=pl.BlockSpec((count, width), lambda i: (0, 0)),
        scratch_shapes=[
            pltpu.VMEM((wide, width), jnp.bfloat16),
            pltpu.VMEM(((NEIGH - 1) * BLOCK, wide), jnp.bfloat16),
            pltpu.VMEM((tile_rows, width), jnp.bfloat16),
        ],
        compiler_params=pltpu.CompilerParams(vmem_limit_bytes=VMEM),
        cost_estimate=pl.CostEstimate(
            flops=2 * NEIGH * tile_rows * wide * width,
            bytes_accessed=4 * tile_rows * width,
            transcendentals=0,
        ),
        name="pixel_rows",
    )(anchor.reshape(1), wanted.reshape(-1, group), adjoint, cotangent, above, below, mixing)


def gradient_kernel(own, near, far, tiles, tile, weights, mine, answers, out):
    pre = own[...].astype(jnp.float32) + near[...].astype(jnp.float32)
    pre = pre + far[...].astype(jnp.float32)
    sigma = jax.nn.sigmoid(pre)
    deriv = sigma * (1.0 + pre * (1.0 - sigma))
    fetched = jnp.where(
        tiles[...] == tile[0], mine[...].astype(jnp.float32), answers[...].astype(jnp.float32)
    )
    out[...] = (weights[...] * deriv * fetched).astype(out.dtype)


def pre_gradient(own, near, far, tiles, tile, weights, mine, answers):
    spec = pl.BlockSpec(memory_space=pltpu.VMEM)
    return pl.pallas_call(
        gradient_kernel,
        out_shape=jax.ShapeDtypeStruct(own.shape, jnp.bfloat16),
        in_specs=[spec] * 4 + [pl.BlockSpec(memory_space=pltpu.SMEM)] + [spec] * 3,
        out_specs=spec,
        compiler_params=pltpu.CompilerParams(vmem_limit_bytes=VMEM),
        name="pre_gradient",
    )(own, near, far, tiles, tile.reshape(1), weights, mine, answers)


def deal_kernel(place, keep, received, own, first, second, third):
    rows = own.shape[0]
    for out, bits in ((own, 0), (first, 1), (second, 2), (third, 3)):
        here = pl.ds(pl.multiple_of((place[0] ^ bits) * rows, rows), rows)
        value = keep[here, :] + received[here, :].astype(jnp.float32)
        out[...] = value.astype(out.dtype)


def deal(place, keep, received):
    rows, width = keep.shape[0] // 4, keep.shape[1]
    spec = pl.BlockSpec(memory_space=pltpu.VMEM)
    piece = jax.ShapeDtypeStruct((rows, width), jnp.bfloat16)
    return pl.pallas_call(
        deal_kernel,
        out_shape=(jax.ShapeDtypeStruct((rows, width), jnp.float32), piece, piece, piece),
        in_specs=[pl.BlockSpec(memory_space=pltpu.SMEM), spec, spec],
        out_specs=(spec,) * 4,
        compiler_params=pltpu.CompilerParams(vmem_limit_bytes=VMEM),
        name="deal",
    )(place.reshape(1), keep, received)


def collect_kernel(where, own, received, out):
    half, rows = own.shape[0], own.shape[0] // 4
    for pieces, core in ((own, where[0]), (received, 1 - where[0])):
        for bits in range(4):
            start = pl.multiple_of(core * half + (where[1] ^ bits) * rows, rows)
            out[pl.ds(start, rows), :] = pieces[bits * rows : (bits + 1) * rows, :].astype(
                jnp.float32
            )


def collect(core, place, own, received):
    spec = pl.BlockSpec(memory_space=pltpu.VMEM)
    return pl.pallas_call(
        collect_kernel,
        out_shape=jax.ShapeDtypeStruct((2 * own.shape[0], own.shape[1]), jnp.float32),
        in_specs=[pl.BlockSpec(memory_space=pltpu.SMEM), spec, spec],
        out_specs=spec,
        compiler_params=pltpu.CompilerParams(vmem_limit_bytes=VMEM),
        name="collect",
    )(jnp.stack([core, place]), own, received)


def sum_over_panels(value):
    both = ("obs", "pix")
    core = lax.axis_index("obs") & 1
    place = (lax.axis_index("obs") >> 1) + 2 * lax.axis_index("pix")
    half = value.shape[0] // 2
    keep = lax.dynamic_slice_in_dim(value, core * half, half, 0)
    send = lax.dynamic_slice_in_dim(value, (1 - core) * half, half, 0)
    received = swap(send.astype(jnp.bfloat16), "obs", 1)
    total, *pieces = deal(place, keep, received)
    for piece, bits in zip(pieces, (4, 1, 5)):
        total = total + swap(piece, both, bits).astype(jnp.float32)
    total = total.astype(jnp.bfloat16)
    own = jnp.concatenate([total] + [swap(total, both, bits) for bits in (4, 1, 5)], axis=0)
    return collect(core, place, own, swap(own, "obs", 1))


def shards(spectra, enc_weight, pix_tile, pix_local, foot_weight, cotangent, adjoint, mixing):
    tile_count = lax.axis_size("pix")
    tile_rows = cotangent.shape[0]
    quarter = spectra.shape[0] // lax.axis_size("chan")
    tile = lax.axis_index("pix")
    chan = lax.axis_index("chan")
    first_row = chan * quarter
    inner = (chan == 1) | (chan == 2)
    ahead, behind = [(0, 1), (3, 2)], [(1, 0), (2, 3)]
    middle = [(1, 2), (2, 1)]

    part2, part3 = project(spectra, enc_weight, jnp.stack([chan ^ 2, chan ^ 3]))
    outer2 = lax.ppermute(part2, "chan", ahead)
    inner2 = lax.ppermute(part2, "chan", middle)
    outer3 = lax.ppermute(part3, "chan", [(0, 2), (3, 1)])
    part0, part1 = project(spectra, enc_weight, jnp.stack([chan, chan ^ 1]))
    wide = jnp.float32
    sum1 = part1.astype(wide) + inner2.astype(wide) + outer3.astype(wide)
    sum3 = part3.astype(wide) + outer2.astype(wide)
    near = swap(sum1.astype(jnp.bfloat16), "chan", 1)
    far = lax.ppermute(sum3.astype(jnp.bfloat16), "chan", middle)

    above, below = edges(cotangent, "pix", HALO)
    anchor = tile * tile_rows - HALO
    tile_ids = lax.dynamic_slice_in_dim(pix_tile, first_row, quarter, 0)
    local_ids = lax.dynamic_slice_in_dim(pix_local, first_row, quarter, 0)
    weights = lax.dynamic_slice_in_dim(foot_weight, first_row, quarter, 0)[:, None]
    capacity = 2 * quarter // tile_count
    if capacity >= quarter and tile_count == 2:
        wanted = jnp.concatenate([local_ids, swap(local_ids, "pix", 1)])
        rows = pixel_rows(cotangent, above, below, adjoint, mixing, anchor, wanted)
        mine, answers = rows[:quarter], swap(rows[quarter:], "pix", 1)
    else:
        slot_index, wanted = requests(tile_ids[:, 0], local_ids, capacity)
        rows = pixel_rows(cotangent, above, below, adjoint, mixing, anchor, wanted)
        answers = lax.all_to_all(
            rows.reshape(tile_count, capacity, -1), "pix", split_axis=0, concat_axis=0, tiled=True
        )
        answers = jnp.take(answers.reshape(tile_count * capacity, -1), slot_index, axis=0)
        mine = answers
    grads = pre_gradient(part0, near, far, tile_ids, tile, weights, mine, answers)

    beside = swap(grads, "chan", 1)
    across = lax.ppermute(grads, "chan", middle)
    passed = lax.ppermute(across, "chan", behind)
    crossed = lax.ppermute(beside, "chan", middle)
    skipped = lax.ppermute(beside, "chan", [(2, 0), (1, 3)])
    local_grad = backproject(spectra, jnp.stack([chan, chan ^ 1]), grads, beside)
    local_grad = backproject(
        spectra,
        jnp.stack([chan ^ 2, chan ^ 3]),
        jnp.where(inner, crossed, passed),
        jnp.where(inner, across, skipped),
        local_grad,
    )
    if lax.axis_size("obs") == 4 and tile_count == 2:
        return sum_over_panels(local_grad)
    return lax.psum(local_grad, ("obs", "pix"))


def solution(mesh):
    return jax.shard_map(
        shards,
        mesh=mesh,
        in_specs=(
            P(("obs", "pix"), "chan"),
            P("chan", None),
            P(("obs", "pix"), None),
            P(("obs", "pix")),
            P(("obs", "pix")),
            P("pix", None),
            P(None, "pix"),
            P(),
        ),
        out_specs=P("chan", None),
        check_vma=False,
    )
```

time: 107 us -> 113 us (1.056)
  waiting for transfers between devices: 45.8 us -> 22.2 us
  Pallas kernels: 21.3 us -> 43.7 us
  starting transfers between devices: 19.5 us -> 28.9 us
  matrix products: 3.9 us -> 0 us
  local copies, waits for them, and re-layouts: 9.31 us -> 11 us
    pallas_call x2 -> x7, Pallas kernels: 2.06 us -> 23.2 us  [the longest x2 8.72 us: backproject(): pl.pallas_call(backproject_kernel, out_shape=jax.ShapeDtypeStruct((depth,...]
    ppermute x7 -> x9, waiting for transfers between devices: 21.5 us -> 6.3 us  [the longest x1 4.34 us: shards(): skipped = lax.ppermute(beside, 'chan', [(2, 0), (1, 3)])]
    ppermute x10 -> x12, waiting for transfers between devices: 24.3 us -> 15.9 us  [swap(): return lax.ppermute(value, axis, [(i, i ^ bit) for i in range(size)])]
    ppermute x7 -> x9, starting transfers between devices: 6.96 us -> 14.9 us  [the longest x1 7.75 us: shards(): outer2 = lax.ppermute(part2, 'chan', ahead)]
    dot_general x1 -> x0, matrix products: 3.9 us -> none  [shards(): lax.dot_general(spectra, grads, (((0,), (0,)), ((), ())), preferred_eleme...]
    concatenate x3 -> x1, other arithmetic: 2.18 us -> 0.02 us  [sum_over_panels(): jnp.concatenate([total] + [swap(total, both, bits) for bits in (4, 1, 5)]...]
    unnamed x12 -> x23, local copies, waits for them, and re-layouts: 5.75 us -> 3.69 us
    dynamic_slice x1 -> x3, local copies, waits for them, and re-layouts: 0.76 us -> 2.69 us  [the longest x1 1.92 us: sum_over_panels(): keep = lax.dynamic_slice_in_dim(value, core * half, half, 0)]
  transfers between devices with their start and end apart: 17 -> 21, of which waited for: 12 -> 11; matrix products, arithmetic and copies ran while one was open for 4% -> 10% of each run, Pallas kernels for 20% -> 26%
where the time goes in v3:
time: 113 us; the launch traced here: 112 us
  Pallas kernels  43.7 us (39%)
  starting transfers between devices  28.9 us (26%)
  waiting for transfers between devices  22.2 us (20%)
  local copies, waits for them, and re-layouts  11 us (10%)
  other arithmetic  6.01 us (5%)
    pallas_call x1, Pallas kernels, pixel_rows(): pl.pallas_call(pixel_kernel, out_shape=jax.ShapeDtypeStruct((count, width...  20.5 us
    ppermute x12, waiting for transfers between devices, swap(): return lax.ppermute(value, axis, [(i, i ^ bit) for i in range(size)])  15.9 us
    ppermute x12, starting transfers between devices, swap(): return lax.ppermute(value, axis, [(i, i ^ bit) for i in range(size)])  14 us
    pallas_call x2, Pallas kernels, backproject(): pl.pallas_call(backproject_kernel, out_shape=jax.ShapeDtypeStruct((depth,...  8.72 us
    pallas_call x2, Pallas kernels, project(): pl.pallas_call(project_kernel, out_shape=(part, part), grid_spec=pltpu.Pr...  7.94 us
    ppermute x1, starting transfers between devices, shards(): outer2 = lax.ppermute(part2, 'chan', ahead)  7.75 us
    ppermute x1, waiting for transfers between devices, shards(): skipped = lax.ppermute(beside, 'chan', [(2, 0), (1, 3)])  4.34 us
    unnamed x23, local copies, waits for them, and re-layouts  3.69 us
  transfers between devices with their start and end apart: 21, of which 11 were waited for; matrix products, arithmetic and copies ran while one was open for 10% of the time, Pallas kernels for 26%

profile of v3, /device:TPU:0, one launch (start us, length us, event | category | flops | bytes accessed | tf_op | source)
XLA Modules:
  0.0 112.0 jit_solution(10160052522662335453)
XLA Ops:
  0.7 4.0 %project.3 = (bf16[512,256]{1,0:T(8,128)(2,1)}, bf16[512,256]{1,0:T(8,128)(2,1)}) custom-call(s32[2]{0:T(128)} %pad_add_fusion.2.quarters, bf16[2048,1152]{1,0:T(8,128)(2,1)} %spectra.7, bf16[1152,256]{1,0:T(8,128)(2,1)} %weight.3), custom_call_target="tpu_custom_call" | custom-call | flops 603979776 | bytes 3473408 | tf_op jit(solution)/shard_map/project/pallas_call | solution.py:64
  5.3 7.7 %collective-permute-start.3 = (bf16[512,256]{1,0:T(8,128)(2,1)}, bf16[512,256]{1,0:T(8,128)(2,1)S(1)}, u32[]{:S(2)}, u32[]{:S(2)}) collective-permute-start(bf16[512,256]{1,0:T(8,128)(2,1)} %get-tuple-element.15), channel_id=1, source_target_pairs={{0,1},{3,2},{4,5},{7,6},{8,9},{11,10},{12,13},{15,14},{16,17},{19,... | collective-permute-start | bytes 786440 | tf_op jit(solution)/shard_map/ppermute | solution.py:338
  13.8 1.5 %collective-permute-start.5 = (s32[512]{0:T(512)S(1)}, s32[512]{0:T(512)S(1)}, u32[]{:S(2)}, u32[]{:S(2)}) collective-permute-start(s32[512]{0:T(512)S(1)} %dynamic_slice.17), channel_id=1, source_target_pairs={{0,4},{4,0},{1,5},{5,1},{2,6},{6,2},{3,7},{7,3},{8,12},{12,8},{9,1... | collective-permute-start | bytes 6152 | tf_op jit(solution)/shard_map/ppermute | solution.py:43
  16.8 1.3 %collective-permute-start.1 = (bf16[512,256]{1,0:T(8,128)(2,1)}, bf16[512,256]{1,0:T(8,128)(2,1)S(1)}, u32[]{:S(2)}, u32[]{:S(2)}) collective-permute-start(bf16[512,256]{1,0:T(8,128)(2,1)} %get-tuple-element.16), channel_id=1, source_target_pairs={{0,2},{3,1},{4,6},{7,5},{8,10},{11,9},{12,14},{15,13},{16,18},{19,... | collective-permute-start | bytes 786440 | tf_op jit(solution)/shard_map/ppermute | solution.py:340
  18.7 4.0 %project.2 = (bf16[512,256]{1,0:T(8,128)(2,1)}, bf16[512,256]{1,0:T(8,128)(2,1)}) custom-call(s32[2]{0:T(128)} %pad_add_fusion.3.quarters, bf16[2048,1152]{1,0:T(8,128)(2,1)} %spectra.7, bf16[1152,256]{1,0:T(8,128)(2,1)} %weight.3), custom_call_target="tpu_custom_call" | custom-call | flops 603979776 | bytes 3473408 | tf_op jit(solution)/shard_map/project/pallas_call | solution.py:64
  23.9 20.5 %pixel_rows.1 = bf16[1024,256]{1,0:T(8,128)(2,1)} custom-call(s32[1]{0:T(128)} %bitcast.8.anchor, s32[4,256]{1,0:T(4,128)} %pad_add_fusion.wanted, s32[8,4096]{1,0:T(8,128)} %adjoint.1, bf16[4096,256]{1,0:T(8,128)(2,1)} %cotangent.1, bf16[128,256]{1,0:T(8,128)(2,1)} %copy-done.10, bf16[128,256]{1,0:T(8,128)(2,1)} %copy-done.10, f32[8,256]{1,0:T(8,128)} %mixing.1), custom_call_target="tpu_custom_call" | custom-call | flops 8589934592 | bytes 4194304 | tf_op jit(solution)/shard_map/pixel_rows/pallas_call | solution.py:214
  44.4 1.8 %fusion = (bf16[512,256]{1,0:T(8,128)(2,1)S(1)}, bf16[512,256]{1,0:T(8,128)(2,1)}) fusion(bf16[1024,256]{1,0:T(8,128)(2,1)} %pixel_rows.1), kind=kLoop, calls=%fused_computation.14 | loop fusion | bytes 1048576 | tf_op jit(solution)/shard_map/slice | solution.py:357
  46.3 1.5 %collective-permute-start.7 = (bf16[512,256]{1,0:T(8,128)(2,1)S(1)}, bf16[512,256]{1,0:T(8,128)(2,1)S(1)}, u32[]{:S(2)}, u32[]{:S(2)}) collective-permute-start(bf16[512,256]{1,0:T(8,128)(2,1)S(1)} %get-tuple-element.21), channel_id=1, source_target_pairs={{0,4},{4,0},{1,5},{5,1},{2,6},{6,2},{3,7},{7,3},{8,12},{12,8},{9,1... | collective-permute-start | bytes 786440 | tf_op jit(solution)/shard_map/ppermute | solution.py:43
  51.3 1.9 %collective-permute-done.7.answers = bf16[512,256]{1,0:T(8,128)(2,1)S(1)} collective-permute-done((bf16[512,256]{1,0:T(8,128)(2,1)S(1)}, bf16[512,256]{1,0:T(8,128)(2,1)S(1)}, u32[]{:S(2)}, u32[]{:S(2)}) %collective-permute-start.7) | collective-permute-done | bytes 262176 | tf_op jit(solution)/shard_map/ppermute | solution.py:43
  53.2 1.4 %collective-permute-done.2.near = bf16[512,256]{1,0:T(8,128)(2,1)S(1)} collective-permute-done((bf16[512,256]{1,0:T(8,128)(2,1)S(1)}, bf16[512,256]{1,0:T(8,128)(2,1)S(1)}, u32[]{:S(2)}, u32[]{:S(2)}) %collective-permute-start.2) | collective-permute-done | bytes 262176 | tf_op jit(solution)/shard_map/ppermute | solution.py:43
  55.4 2.5 %pre_gradient.1.first = bf16[512,256]{1,0:T(8,128)(2,1)} custom-call(bf16[512,256]{1,0:T(8,128)(2,1)} %get-tuple-element.13.own, bf16[512,256]{1,0:T(8,128)(2,1)} %copy-done.7, bf16[512,256]{1,0:T(8,128)(2,1)} %copy-done.8, s32[512,1]{1,0:T(8,128)} %copy.12.tiles, s32[1]{0:T(128)} %bitcast.6.tile, f32[512,1]{1,0:T(8,128)} %copy.11.weights, ...), custom_call_target="tpu_custom_call" | custom-call | tf_op jit(solution)/shard_map/pre_gradient/pallas_call | solution.py:256
  57.9 3.7 %collective-permute-start.8 = (bf16[512,256]{1,0:T(8,128)(2,1)}, bf16[512,256]{1,0:T(8,128)(2,1)S(1)}, u32[]{:S(2)}, u32[]{:S(2)}) collective-permute-start(bf16[512,256]{1,0:T(8,128)(2,1)} %pre_gradient.1.first), channel_id=1, source_target_pairs={{0,1},{1,0},{2,3},{3,2},{4,5},{5,4},{6,7},{7,6},{8,9},{9,8},{10,11... | collective-permute-start | bytes 786440 | tf_op jit(solution)/shard_map/ppermute | solution.py:43
  62.2 3.9 %collective-permute-done.8.second = bf16[512,256]{1,0:T(8,128)(2,1)S(1)} collective-permute-done((bf16[512,256]{1,0:T(8,128)(2,1)}, bf16[512,256]{1,0:T(8,128)(2,1)S(1)}, u32[]{:S(2)}, u32[]{:S(2)}) %collective-permute-start.8) | collective-permute-done | bytes 262176 | tf_op jit(solution)/shard_map/ppermute | solution.py:43
  66.1 1.3 %collective-permute-start.12 = (bf16[512,256]{1,0:T(8,128)(2,1)S(1)}, bf16[512,256]{1,0:T(8,128)(2,1)S(1)}, u32[]{:S(2)}, u32[]{:S(2)}) collective-permute-start(bf16[512,256]{1,0:T(8,128)(2,1)S(1)} %collective-permute-done.8.second), channel_id=1, source_target_pairs={{2,0},{1,3},{6,4},{5,7},{10,8},{9,11},{14,12},{13,15},{18,16},{17,... | collective-permute-start | bytes 786440 | tf_op jit(solution)/shard_map/ppermute | solution.py:372
  68.1 1.3 %collective-permute-start.11 = (bf16[512,256]{1,0:T(8,128)(2,1)S(1)}, bf16[512,256]{1,0:T(8,128)(2,1)S(1)}, u32[]{:S(2)}, u32[]{:S(2)}) collective-permute-start(bf16[512,256]{1,0:T(8,128)(2,1)S(1)} %collective-permute-done.10), channel_id=1, source_target_pairs={{1,0},{2,3},{5,4},{6,7},{9,8},{10,11},{13,12},{14,15},{17,16},{18,... | collective-permute-start | bytes 786440 | tf_op jit(solution)/shard_map/ppermute | solution.py:370
  69.4 4.1 %backproject.2.rest_0_ = f32[1152,256]{1,0:T(8,128)} custom-call(s32[2]{0:T(128)} %pad_add_fusion.3.quarters, bf16[2048,1152]{1,0:T(8,128)(2,1)} %spectra.7, bf16[512,256]{1,0:T(8,128)(2,1)} %pre_gradient.1.first, bf16[512,256]{1,0:T(8,128)(2,1)} %copy-done.5), custom_call_target="tpu_custom_call" | custom-call | flops 603979776 | bytes 4718592 | tf_op jit(solution)/shard_map/backproject/pallas_call | solution.py:115
  73.6 4.3 %collective-permute-done.12 = bf16[512,256]{1,0:T(8,128)(2,1)S(1)} collective-permute-done((bf16[512,256]{1,0:T(8,128)(2,1)S(1)}, bf16[512,256]{1,0:T(8,128)(2,1)S(1)}, u32[]{:S(2)}, u32[]{:S(2)}) %collective-permute-start.12) | collective-permute-done | bytes 262176 | tf_op jit(solution)/shard_map/ppermute | solution.py:372
  78.7 1.9 %collective-permute-done.11 = bf16[512,256]{1,0:T(8,128)(2,1)S(1)} collective-permute-done((bf16[512,256]{1,0:T(8,128)(2,1)S(1)}, bf16[512,256]{1,0:T(8,128)(2,1)S(1)}, u32[]{:S(2)}, u32[]{:S(2)}) %collective-permute-start.11) | collective-permute-done | bytes 262176 | tf_op jit(solution)/shard_map/ppermute | solution.py:370
  81.4 4.6 %backproject.3 = f32[1152,256]{1,0:T(8,128)} custom-call(s32[2]{0:T(128)} %pad_add_fusion.2.quarters, bf16[2048,1152]{1,0:T(8,128)(2,1)} %spectra.7, bf16[512,256]{1,0:T(8,128)(2,1)} %broadcast_select_fusion.1.first, bf16[512,256]{1,0:T(8,128)(2,1)} %broadcast_select_fusion.second, f32[1152,256]{1,0:T(8,128)} %backproject.2.rest_0_), custom_call_target="tpu_custom_call" | custom-call | flops 603979776 | bytes 4718592 | tf_op jit(solution)/shard_map/backproject/pallas_call | solution.py:115
  85.9 1.1 dynamic-slice_convert_fusion
  87.1 1.9 %constant_dynamic-slice_fusion.keep = f32[576,256]{1,0:T(8,128)} fusion(f32[1152,256]{1,0:T(8,128)} %backproject.3, s32[]{:T(128)S(6)} %select_n.37), kind=kLoop, calls=%fused_computation.9 | loop fusion | bytes 1179652 | tf_op jit(solution)/shard_map/dynamic_slice | solution.py:315
  89.8 1.9 %deal.1 = (f32[144,256]{1,0:T(8,128)}, bf16[144,256]{1,0:T(8,128)(2,1)}, bf16[144,256]{1,0:T(8,128)(2,1)}, bf16[144,256]{1,0:T(8,128)(2,1)}) custom-call(s32[1]{0:T(128)} %bitcast.1.place, f32[576,256]{1,0:T(8,128)} %constant_dynamic-slice_fusion.keep, bf16[576,256]{1,0:T(8,128)(2,1)} %copy-done.2), custom_call_target="tpu_custom_call" | custom-call | tf_op jit(solution)/shard_map/deal/pallas_call | solution.py:278
  91.7 1.5 %collective-permute-start.14 = (bf16[144,256]{1,0:T(8,128)(2,1)}, bf16[144,256]{1,0:T(8,128)(2,1)S(1)}, u32[]{:S(2)}, u32[]{:S(2)}) collective-permute-start(bf16[144,256]{1,0:T(8,128)(2,1)} %get-tuple-element.18), channel_id=1, source_target_pairs={{0,16},{4,20},{8,24},{12,28},{16,0},{20,4},{24,8},{28,12},{1,17},{... | collective-permute-start | bytes 221192 | tf_op jit(solution)/shard_map/ppermute | solution.py:43
  93.7 1.5 %collective-permute-start.16 = (bf16[144,256]{1,0:T(8,128)(2,1)}, bf16[144,256]{1,0:T(8,128)(2,1)S(1)}, u32[]{:S(2)}, u32[]{:S(2)}) collective-permute-start(bf16[144,256]{1,0:T(8,128)(2,1)} %get-tuple-element.20), channel_id=1, source_target_pairs={{0,20},{4,16},{8,28},{12,24},{16,4},{20,0},{24,12},{28,8},{1,21},{... | collective-permute-start | bytes 221192 | tf_op jit(solution)/shard_map/ppermute | solution.py:43
  95.2 1.4 %collective-permute-done.14 = bf16[144,256]{1,0:T(8,128)(2,1)S(1)} collective-permute-done((bf16[144,256]{1,0:T(8,128)(2,1)}, bf16[144,256]{1,0:T(8,128)(2,1)S(1)}, u32[]{:S(2)}, u32[]{:S(2)}) %collective-permute-start.14) | collective-permute-done | bytes 73760 | tf_op jit(solution)/shard_map/ppermute | solution.py:43
  96.5 2.8 %collective-permute-done.15 = bf16[144,256]{1,0:T(8,128)(2,1)S(1)} collective-permute-done((bf16[144,256]{1,0:T(8,128)(2,1)}, bf16[144,256]{1,0:T(8,128)(2,1)S(1)}, u32[]{:S(2)}, u32[]{:S(2)}) %collective-permute-start.15) | collective-permute-done | bytes 73760 | tf_op jit(solution)/shard_map/ppermute | solution.py:43
  99.4 1.0 add_convert_fusion.2
  100.9 1.3 %collective-permute-start.18 = (bf16[144,256]{1,0:T(8,128)(2,1)S(1)}, bf16[144,256]{1,0:T(8,128)(2,1)S(1)}, u32[]{:S(2)}, u32[]{:S(2)}) collective-permute-start(bf16[144,256]{1,0:T(8,128)(2,1)S(1)} %add_convert_fusion.2), channel_id=1, source_target_pairs={{0,4},{4,0},{8,12},{12,8},{16,20},{20,16},{24,28},{28,24},{1,5},{5... | collective-permute-start | bytes 221192 | tf_op jit(solution)/shard_map/ppermute | solution.py:43
  102.2 1.7 %collective-permute-start.19 = (bf16[144,256]{1,0:T(8,128)(2,1)S(1)}, bf16[144,256]{1,0:T(8,128)(2,1)S(1)}, u32[]{:S(2)}, u32[]{:S(2)}) collective-permute-start(bf16[144,256]{1,0:T(8,128)(2,1)S(1)} %add_convert_fusion.2), channel_id=1, source_target_pairs={{0,20},{4,16},{8,28},{12,24},{16,4},{20,0},{24,12},{28,8},{1,21},{... | collective-permute-start | bytes 221192 | tf_op jit(solution)/shard_map/ppermute | solution.py:43
  105.7 1.8 %collective-permute-done.19 = bf16[144,256]{1,0:T(8,128)(2,1)S(1)} collective-permute-done((bf16[144,256]{1,0:T(8,128)(2,1)S(1)}, bf16[144,256]{1,0:T(8,128)(2,1)S(1)}, u32[]{:S(2)}, u32[]{:S(2)}) %collective-permute-start.19) | collective-permute-done | bytes 73760 | tf_op jit(solution)/shard_map/ppermute | solution.py:43
  108.2 0.9 collective-permute-done.20.received
  109.9 2.2 %collect.1 = f32[1152,256]{1,0:T(8,128)} custom-call(s32[2]{0:T(128)} %pad_add_fusion.1.where, bf16[576,256]{1,0:T(8,128)(2,1)} %copy-done.1, bf16[576,256]{1,0:T(8,128)(2,1)} %copy-done.3), custom_call_target="tpu_custom_call" | custom-call | tf_op jit(solution)/shard_map/collect/pallas_call | solution.py:300
  (61 shorter events, 17.5 us)
Async XLA Ops:
  0.0 50.5 %copy-start = (s32[2048,1]{0,1:T(1,128)S(1)}, s32[2048,1]{0,1:T(1,128)}, u32[]{:S(2)}) copy-start(s32[2048,1]{0,1:T(1,128)} %param.10) | copy-start | bytes 24580
  4.6 43.2 %collective-permute-start = (bf16[512,256]{1,0:T(8,128)(2,1)}, bf16[512,256]{1,0:T(8,128)(2,1)S(1)}, u32[]{:S(2)}, u32[]{:S(2)}) collective-permute-start(bf16[512,256]{1,0:T(8,128)(2,1)} %get-tuple-element.15), channel_id=1, source_target_pairs={{1,2},{2,1},{5,6},{6,5},{9,10},{10,9},{13,14},{14,13},{17,18},{18,... | collective-permute-start | bytes 786440 | tf_op jit(solution)/shard_map/ppermute | solution.py:339
  5.3 42.7 %collective-permute-start.3 = (bf16[512,256]{1,0:T(8,128)(2,1)}, bf16[512,256]{1,0:T(8,128)(2,1)S(1)}, u32[]{:S(2)}, u32[]{:S(2)}) collective-permute-start(bf16[512,256]{1,0:T(8,128)(2,1)} %get-tuple-element.15), channel_id=1, source_target_pairs={{0,1},{3,2},{4,5},{7,6},{8,9},{11,10},{12,13},{15,14},{16,17},{19,... | collective-permute-start | bytes 786440 | tf_op jit(solution)/shard_map/ppermute | solution.py:338
  13.8 8.9 %collective-permute-start.5 = (s32[512]{0:T(512)S(1)}, s32[512]{0:T(512)S(1)}, u32[]{:S(2)}, u32[]{:S(2)}) collective-permute-start(s32[512]{0:T(512)S(1)} %dynamic_slice.17), channel_id=1, source_target_pairs={{0,4},{4,0},{1,5},{5,1},{2,6},{6,2},{3,7},{7,3},{8,12},{12,8},{9,1... | collective-permute-start | bytes 6152 | tf_op jit(solution)/shard_map/ppermute | solution.py:43
  16.2 7.1 %collective-permute-start.6 = (bf16[128,256]{1,0:T(8,128)(2,1)S(1)}, bf16[128,256]{1,0:T(8,128)(2,1)S(1)}, u32[]{:S(2)}, u32[]{:S(2)}) collective-permute-start(bf16[128,256]{1,0:T(8,128)(2,1)S(1)} %slice_select_fusion), channel_id=1, source_target_pairs={{0,4},{4,0},{1,5},{5,1},{2,6},{6,2},{3,7},{7,3},{8,12},{12,8},{9,1... | collective-permute-start | bytes 196616 | tf_op jit(solution)/shard_map/ppermute | solution.py:20
  16.8 31.0 %collective-permute-start.1 = (bf16[512,256]{1,0:T(8,128)(2,1)}, bf16[512,256]{1,0:T(8,128)(2,1)S(1)}, u32[]{:S(2)}, u32[]{:S(2)}) collective-permute-start(bf16[512,256]{1,0:T(8,128)(2,1)} %get-tuple-element.16), channel_id=1, source_target_pairs={{0,2},{3,1},{4,6},{7,5},{8,10},{11,9},{12,14},{15,13},{16,18},{19,... | collective-permute-start | bytes 786440 | tf_op jit(solution)/shard_map/ppermute | solution.py:340
  23.3 0.6 copy-start.10
  44.4 3.4 %copy-start.9 = (bf16[512,256]{1,0:T(8,128)(2,1)S(1)}, bf16[512,256]{1,0:T(8,128)(2,1)}, u32[]{:S(2)}) copy-start(bf16[512,256]{1,0:T(8,128)(2,1)} %get-tuple-element.14) | copy-start | bytes 786436
  44.4 3.6 %copy-start.4 = (bf16[512,256]{1,0:T(8,128)(2,1)S(1)}, bf16[512,256]{1,0:T(8,128)(2,1)}, u32[]{:S(2)}) copy-start(bf16[512,256]{1,0:T(8,128)(2,1)} %get-tuple-element.16) | copy-start | bytes 786436
  46.3 6.9 %collective-permute-start.7 = (bf16[512,256]{1,0:T(8,128)(2,1)S(1)}, bf16[512,256]{1,0:T(8,128)(2,1)S(1)}, u32[]{:S(2)}, u32[]{:S(2)}) collective-permute-start(bf16[512,256]{1,0:T(8,128)(2,1)S(1)} %get-tuple-element.21), channel_id=1, source_target_pairs={{0,4},{4,0},{1,5},{5,1},{2,6},{6,2},{3,7},{7,3},{8,12},{12,8},{9,1... | collective-permute-start | bytes 786440 | tf_op jit(solution)/shard_map/ppermute | solution.py:43
  48.0 6.7 %collective-permute-start.2 = (bf16[512,256]{1,0:T(8,128)(2,1)S(1)}, bf16[512,256]{1,0:T(8,128)(2,1)S(1)}, u32[]{:S(2)}, u32[]{:S(2)}) collective-permute-start(bf16[512,256]{1,0:T(8,128)(2,1)S(1)} %add_convert_fusion.1), channel_id=1, source_target_pairs={{0,1},{1,0},{2,3},{3,2},{4,5},{5,4},{6,7},{7,6},{8,9},{9,8},{10,11... | collective-permute-start | bytes 786440 | tf_op jit(solution)/shard_map/ppermute | solution.py:43
  48.1 6.5 %collective-permute-start.4 = (bf16[512,256]{1,0:T(8,128)(2,1)S(1)}, bf16[512,256]{1,0:T(8,128)(2,1)S(1)}, u32[]{:S(2)}, u32[]{:S(2)}) collective-permute-start(bf16[512,256]{1,0:T(8,128)(2,1)S(1)} %add_convert_fusion), channel_id=1, source_target_pairs={{1,2},{2,1},{5,6},{6,5},{9,10},{10,9},{13,14},{14,13},{17,18},{18,... | collective-permute-start | bytes 786440 | tf_op jit(solution)/shard_map/ppermute | solution.py:346
  53.2 1.4 %copy-start.6 = (bf16[512,256]{1,0:T(8,128)(2,1)}, bf16[512,256]{1,0:T(8,128)(2,1)S(1)}, u32[]{:S(2)}) copy-start(bf16[512,256]{1,0:T(8,128)(2,1)S(1)} %collective-permute-done.7.answers) | copy-start | bytes 786436
  54.6 0.7 copy-start.7
  54.7 0.8 copy-start.8
  57.9 8.2 %collective-permute-start.8 = (bf16[512,256]{1,0:T(8,128)(2,1)}, bf16[512,256]{1,0:T(8,128)(2,1)S(1)}, u32[]{:S(2)}, u32[]{:S(2)}) collective-permute-start(bf16[512,256]{1,0:T(8,128)(2,1)} %pre_gradient.1.first), channel_id=1, source_target_pairs={{0,1},{1,0},{2,3},{3,2},{4,5},{5,4},{6,7},{7,6},{8,9},{9,8},{10,11... | collective-permute-start | bytes 786440 | tf_op jit(solution)/shard_map/ppermute | solution.py:43
  61.6 6.6 %collective-permute-start.10 = (bf16[512,256]{1,0:T(8,128)(2,1)}, bf16[512,256]{1,0:T(8,128)(2,1)S(1)}, u32[]{:S(2)}, u32[]{:S(2)}) collective-permute-start(bf16[512,256]{1,0:T(8,128)(2,1)} %pre_gradient.1.first), channel_id=1, source_target_pairs={{1,2},{2,1},{5,6},{6,5},{9,10},{10,9},{13,14},{14,13},{17,18},{18,... | collective-permute-start | bytes 786440 | tf_op jit(solution)/shard_map/ppermute | solution.py:369
  66.1 3.3 %copy-start.5 = (bf16[512,256]{1,0:T(8,128)(2,1)}, bf16[512,256]{1,0:T(8,128)(2,1)S(1)}, u32[]{:S(2)}) copy-start(bf16[512,256]{1,0:T(8,128)(2,1)S(1)} %collective-permute-done.8.second) | copy-start | bytes 786436
  66.1 11.8 %collective-permute-start.12 = (bf16[512,256]{1,0:T(8,128)(2,1)S(1)}, bf16[512,256]{1,0:T(8,128)(2,1)S(1)}, u32[]{:S(2)}, u32[]{:S(2)}) collective-permute-start(bf16[512,256]{1,0:T(8,128)(2,1)S(1)} %collective-permute-done.8.second), channel_id=1, source_target_pairs={{2,0},{1,3},{6,4},{5,7},{10,8},{9,11},{14,12},{13,15},{18,16},{17,... | collective-permute-start | bytes 786440 | tf_op jit(solution)/shard_map/ppermute | solution.py:372
  67.4 13.2 %collective-permute-start.9 = (bf16[512,256]{1,0:T(8,128)(2,1)S(1)}, bf16[512,256]{1,0:T(8,128)(2,1)S(1)}, u32[]{:S(2)}, u32[]{:S(2)}) collective-permute-start(bf16[512,256]{1,0:T(8,128)(2,1)S(1)} %collective-permute-done.8.second), channel_id=1, source_target_pairs={{1,2},{2,1},{5,6},{6,5},{9,10},{10,9},{13,14},{14,13},{17,18},{18,... | collective-permute-start | bytes 786440 | tf_op jit(solution)/shard_map/ppermute | solution.py:371
  68.1 12.5 %collective-permute-start.11 = (bf16[512,256]{1,0:T(8,128)(2,1)S(1)}, bf16[512,256]{1,0:T(8,128)(2,1)S(1)}, u32[]{:S(2)}, u32[]{:S(2)}) collective-permute-start(bf16[512,256]{1,0:T(8,128)(2,1)S(1)} %collective-permute-done.10), channel_id=1, source_target_pairs={{1,0},{2,3},{5,4},{6,7},{9,8},{10,11},{13,12},{14,15},{17,16},{18,... | collective-permute-start | bytes 786440 | tf_op jit(solution)/shard_map/ppermute | solution.py:370
  87.0 2.0 %collective-permute-start.13 = (bf16[576,256]{1,0:T(8,128)(2,1)S(1)}, bf16[576,256]{1,0:T(8,128)(2,1)S(1)}, u32[]{:S(2)}, u32[]{:S(2)}) collective-permute-start(bf16[576,256]{1,0:T(8,128)(2,1)S(1)} %dynamic-slice_convert_fusion), channel_id=1, source_target_pairs={{0,8},{8,0},{16,24},{24,16},{1,9},{9,1},{17,25},{25,17},{2,10},{10... | collective-permute-start | bytes 884744 | tf_op jit(solution)/shard_map/ppermute | solution.py:43
  89.0 0.7 copy-start.2
  91.7 4.9 %collective-permute-start.14 = (bf16[144,256]{1,0:T(8,128)(2,1)}, bf16[144,256]{1,0:T(8,128)(2,1)S(1)}, u32[]{:S(2)}, u32[]{:S(2)}) collective-permute-start(bf16[144,256]{1,0:T(8,128)(2,1)} %get-tuple-element.18), channel_id=1, source_target_pairs={{0,16},{4,20},{8,24},{12,28},{16,0},{20,4},{24,8},{28,12},{1,17},{... | collective-permute-start | bytes 221192 | tf_op jit(solution)/shard_map/ppermute | solution.py:43
  93.2 6.2 %collective-permute-start.15 = (bf16[144,256]{1,0:T(8,128)(2,1)}, bf16[144,256]{1,0:T(8,128)(2,1)S(1)}, u32[]{:S(2)}, u32[]{:S(2)}) collective-permute-start(bf16[144,256]{1,0:T(8,128)(2,1)} %get-tuple-element.19), channel_id=1, source_target_pairs={{0,4},{4,0},{8,12},{12,8},{16,20},{20,16},{24,28},{28,24},{1,5},{5... | collective-permute-start | bytes 221192 | tf_op jit(solution)/shard_map/ppermute | solution.py:43
  93.7 5.7 %collective-permute-start.16 = (bf16[144,256]{1,0:T(8,128)(2,1)}, bf16[144,256]{1,0:T(8,128)(2,1)S(1)}, u32[]{:S(2)}, u32[]{:S(2)}) collective-permute-start(bf16[144,256]{1,0:T(8,128)(2,1)} %get-tuple-element.20), channel_id=1, source_target_pairs={{0,20},{4,16},{8,28},{12,24},{16,4},{20,0},{24,12},{28,8},{1,21},{... | collective-permute-start | bytes 221192 | tf_op jit(solution)/shard_map/ppermute | solution.py:43
  100.3 4.4 %collective-permute-start.17 = (bf16[144,256]{1,0:T(8,128)(2,1)S(1)}, bf16[144,256]{1,0:T(8,128)(2,1)S(1)}, u32[]{:S(2)}, u32[]{:S(2)}) collective-permute-start(bf16[144,256]{1,0:T(8,128)(2,1)S(1)} %add_convert_fusion.2), channel_id=1, source_target_pairs={{0,16},{4,20},{8,24},{12,28},{16,0},{20,4},{24,8},{28,12},{1,17},{... | collective-permute-start | bytes 221192 | tf_op jit(solution)/shard_map/ppermute | solution.py:43
  100.9 4.8 %collective-permute-start.18 = (bf16[144,256]{1,0:T(8,128)(2,1)S(1)}, bf16[144,256]{1,0:T(8,128)(2,1)S(1)}, u32[]{:S(2)}, u32[]{:S(2)}) collective-permute-start(bf16[144,256]{1,0:T(8,128)(2,1)S(1)} %add_convert_fusion.2), channel_id=1, source_target_pairs={{0,4},{4,0},{8,12},{12,8},{16,20},{20,16},{24,28},{28,24},{1,5},{5... | collective-permute-start | bytes 221192 | tf_op jit(solution)/shard_map/ppermute | solution.py:43
  102.2 5.3 %collective-permute-start.19 = (bf16[144,256]{1,0:T(8,128)(2,1)S(1)}, bf16[144,256]{1,0:T(8,128)(2,1)S(1)}, u32[]{:S(2)}, u32[]{:S(2)}) collective-permute-start(bf16[144,256]{1,0:T(8,128)(2,1)S(1)} %add_convert_fusion.2), channel_id=1, source_target_pairs={{0,20},{4,16},{8,28},{12,24},{16,4},{20,0},{24,12},{28,8},{1,21},{... | collective-permute-start | bytes 221192 | tf_op jit(solution)/shard_map/ppermute | solution.py:43
  107.5 1.7 %copy-start.1 = (bf16[576,256]{1,0:T(8,128)(2,1)}, bf16[576,256]{1,0:T(8,128)(2,1)S(1)}, u32[]{:S(2)}) copy-start(bf16[576,256]{1,0:T(8,128)(2,1)S(1)} %pad_maximum_fusion.own) | copy-start | bytes 884740
  107.5 1.6 %collective-permute-start.20 = (bf16[576,256]{1,0:T(8,128)(2,1)S(1)}, bf16[576,256]{1,0:T(8,128)(2,1)S(1)}, u32[]{:S(2)}, u32[]{:S(2)}) collective-permute-start(bf16[576,256]{1,0:T(8,128)(2,1)S(1)} %pad_maximum_fusion.own), channel_id=1, source_target_pairs={{0,8},{8,0},{16,24},{24,16},{1,9},{9,1},{17,25},{25,17},{2,10},{10... | collective-permute-start | bytes 884744 | tf_op jit(solution)/shard_map/ppermute | solution.py:43
  109.2 0.7 copy-start.3

commit v4 on v0

v4 whole, which is shorter than its diff:
```python
import functools

import jax
import jax.numpy as jnp
from jax import lax
from jax.experimental import pallas as pl
from jax.experimental.pallas import tpu as pltpu
from jax.sharding import PartitionSpec as P

NEIGH = 8
HALO = 128
MIB = 1024 * 1024


def edges(value, axis, width):
    size, length = lax.axis_size(axis), value.shape[0]
    last = lax.slice_in_dim(value, length - width, length, axis=0)
    first = lax.slice_in_dim(value, 0, width, axis=0)
    if size == 2:
        index = lax.axis_index(axis)
        other = lax.ppermute(jnp.where(index == 0, last, first), axis, [(0, 1), (1, 0)])
        return other, other
    up = [(i, i + 1) for i in range(size - 1)]
    return lax.ppermute(last, axis, up), lax.ppermute(first, axis, [(j, i) for i, j in up])


def requests(tile_ids, local_ids, capacity):
    tile_count = lax.axis_size("pix")
    onehot = (tile_ids[:, None] == jnp.arange(tile_count, dtype=jnp.int32)[None, :]).astype(
        jnp.int32
    )
    place_rank = jnp.sum((jnp.cumsum(onehot, axis=0) - 1) * onehot, axis=1)
    slot_index = tile_ids * capacity + place_rank
    outgoing = jnp.full((tile_count * capacity,), 0, jnp.int32).at[slot_index].set(local_ids)
    outgoing = outgoing.reshape(tile_count, capacity)
    requested = lax.all_to_all(outgoing, "pix", split_axis=0, concat_axis=0, tiled=True)
    return slot_index, requested.reshape(-1)


def swap(value, axis, bit):
    size = 1
    for name in (axis,) if isinstance(axis, str) else axis:
        size *= lax.axis_size(name)
    return lax.ppermute(value, axis, [(i, i ^ bit) for i in range(size)])


def memory(mib):
    return pltpu.CompilerParams(vmem_limit_bytes=mib * MIB)


def project_kernel(chan, spectra, weight, *parts):
    step = pl.program_id(0)
    result = jnp.dot(
        spectra[...], weight[...], preferred_element_type=jnp.float32
    ).astype(jnp.bfloat16)
    rows = result.shape[0]
    turns = parts[0].shape[0] // rows
    for index, part in enumerate(parts):
        for turn in range(turns):

            @pl.when(step == index * turns + turn)
            def _(part=part, turn=turn):
                part[turn * rows : (turn + 1) * rows, :] = result


def project(spectra, weight, chan):
    depth, width = weight.shape
    quarter = spectra.shape[0] // 4
    turns = 2
    part = jax.ShapeDtypeStruct((quarter, width), jnp.bfloat16)
    return pl.pallas_call(
        project_kernel,
        out_shape=(part,) * 4,
        grid_spec=pltpu.PrefetchScalarGridSpec(
            num_scalar_prefetch=1,
            grid=(4 * turns,),
            in_specs=[
                pl.BlockSpec(
                    (quarter // turns, depth),
                    lambda i, chan: ((chan[0] ^ (3 - i // turns)) * turns + i % turns, 0),
                ),
                pl.BlockSpec((depth, width), lambda i, chan: (0, 0)),
            ],
            out_specs=(pl.BlockSpec((quarter, width), lambda i, chan: (0, 0)),) * 4,
        ),
        compiler_params=memory(60),
        cost_estimate=pl.CostEstimate(
            flops=8 * quarter * depth * width,
            bytes_accessed=8 * quarter * depth + 2 * depth * width + 8 * quarter * width,
            transcendentals=0,
        ),
        name="project",
    )(chan.reshape(1), spectra, weight)


def turn_kernel(chan, spectra, out):
    out[...] = spectra[...].T


def turned(spectra, chan):
    rows, depth = spectra.shape[0] // 4, spectra.shape[1]
    return pl.pallas_call(
        turn_kernel,
        out_shape=jax.ShapeDtypeStruct((depth, 2 * rows), jnp.bfloat16),
        grid_spec=pltpu.PrefetchScalarGridSpec(
            num_scalar_prefetch=1,
            grid=(2,),
            in_specs=[pl.BlockSpec((rows, depth), lambda i, chan: (chan[0] ^ (2 + i), 0))],
            out_specs=pl.BlockSpec((depth, rows), lambda i, chan: (0, i)),
        ),
        compiler_params=memory(16),
        name="turned",
    )(chan.reshape(1), spectra)


def early_kernel(chan, spectra, first, second, total):
    step = pl.program_id(0)

    def product(rows):
        return lax.dot_general(
            spectra[...], rows[...], (((0,), (0,)), ((), ())), preferred_element_type=jnp.float32
        )

    @pl.when(step == 0)
    def _():
        total[...] = product(first)

    @pl.when(step == 1)
    def _():
        total[...] += product(second)


def early_product(spectra, chan, first, second):
    depth = spectra.shape[1]
    rows, width = first.shape
    whole = pl.BlockSpec((rows, width), lambda i, chan: (0, 0))
    return pl.pallas_call(
        early_kernel,
        out_shape=jax.ShapeDtypeStruct((depth, width), jnp.float32),
        grid_spec=pltpu.PrefetchScalarGridSpec(
            num_scalar_prefetch=1,
            grid=(2,),
            in_specs=[pl.BlockSpec((rows, depth), lambda i, chan: (chan[0] ^ i, 0)), whole, whole],
            out_specs=pl.BlockSpec((depth, width), lambda i, chan: (0, 0)),
        ),
        compiler_params=memory(16),
        cost_estimate=pl.CostEstimate(
            flops=4 * rows * depth * width,
            bytes_accessed=4 * rows * depth + 4 * depth * width,
            transcendentals=0,
        ),
        name="early_product",
    )(chan.reshape(1), spectra, first, second)


def late_kernel(where, flipped, before, crossed, passed, across, skipped, keep, send):
    chan, core = where[0], where[1]
    inner = (chan == 1) | (chan == 2)
    second = jnp.where(inner, crossed[...], passed[...])
    third = jnp.where(inner, across[...], skipped[...])
    rows = jnp.concatenate([second, third], axis=0)
    half = keep.shape[0]
    for out, which in ((send, 1 - core), (keep, core)):
        here = pl.ds(pl.multiple_of(which * half, half), half)
        product = jnp.dot(flipped[here, :], rows, preferred_element_type=jnp.float32)
        out[...] = (before[here, :] + product).astype(out.dtype)


def late_product(chan, core, flipped, before, crossed, passed, across, skipped):
    half, width = before.shape[0] // 2, before.shape[1]
    spec = pl.BlockSpec(memory_space=pltpu.VMEM)
    return pl.pallas_call(
        late_kernel,
        out_shape=(
            jax.ShapeDtypeStruct((half, width), jnp.float32),
            jax.ShapeDtypeStruct((half, width), jnp.bfloat16),
        ),
        in_specs=[pl.BlockSpec(memory_space=pltpu.SMEM)] + [spec] * 6,
        out_specs=(spec, spec),
        compiler_params=memory(16),
        name="late_product",
    )(jnp.stack([chan, core]), flipped, before, crossed, passed, across, skipped)


def pixel_kernel(count, start, places, *refs):
    *lists, cotangent, above, below, mixing, out, table, scale, sums = refs
    tile_rows, half = cotangent.shape[0], table.shape[1]

    def fill(first, values):
        values = values.astype(jnp.float32)
        for side in range(2):
            table[pl.ds(2 * first + side, values.shape[0], stride=2), :] = values[
                :, side * half : (side + 1) * half
            ]

    fill(0, above[...])
    fill(HALO + tile_rows, below[...])
    chunk = 256
    for first in range(0, tile_rows, chunk):
        fill(HALO + first, cotangent[first : first + chunk, :])
    for side in range(2):
        scale[pl.ds(side, NEIGH, stride=2), :] = mixing[:, side * half : (side + 1) * half]
    scales = [scale[2 * k : 2 * k + 2, :] for k in range(NEIGH)]

    group = 8
    for index, wanted in enumerate(lists):

        def body(turn, carry, index=index, wanted=wanted):
            base = turn * group
            for n in range(group):
                pixel = wanted[start[0] + base + n]
                total = table[pl.ds(2 * (pixel + HALO), 2), :]
                for k in range(NEIGH):
                    total = total + table[pl.ds(places[k, pixel], 2), :] * scales[k]
                sums[pl.ds(2 * (index * count + base + n), 2), :] = total
            return carry

        lax.fori_loop(0, count // group, body, 0)
    rows = out.shape[0]
    for side in range(2):
        out[:, side * half : (side + 1) * half] = sums[pl.ds(side, rows, stride=2), :].astype(
            out.dtype
        )


def pixel_rows(cotangent, above, below, adjoint, mixing, anchor, lists, start, count):
    tile_rows, width = cotangent.shape
    rows = count * len(lists)
    smem = pl.BlockSpec(memory_space=pltpu.SMEM)
    vmem = pl.BlockSpec(memory_space=pltpu.VMEM)
    return pl.pallas_call(
        functools.partial(pixel_kernel, count),
        out_shape=jax.ShapeDtypeStruct((rows, width), jnp.bfloat16),
        in_specs=[smem] * (2 + len(lists)) + [vmem] * 4,
        out_specs=vmem,
        scratch_shapes=[
            pltpu.VMEM((2 * (tile_rows + 2 * HALO), width // 2), jnp.float32),
            pltpu.VMEM((2 * NEIGH, width // 2), jnp.float32),
            pltpu.VMEM((2 * rows, width // 2), jnp.float32),
        ],
        compiler_params=memory(24),
        cost_estimate=pl.CostEstimate(
            flops=2 * NEIGH * tile_rows * 256 * width,
            bytes_accessed=4 * tile_rows * width,
            transcendentals=0,
        ),
        name="pixel_rows",
    )(start.reshape(1), (adjoint - anchor) * 2, *lists, cotangent, above, below, mixing)


def gradient_kernel(own, near, far, tiles, tile, weights, mine, answers, out):
    pre = own[...].astype(jnp.float32) + near[...].astype(jnp.float32)
    pre = pre + far[...].astype(jnp.float32)
    sigma = jax.nn.sigmoid(pre)
    deriv = sigma * (1.0 + pre * (1.0 - sigma))
    fetched = jnp.where(
        tiles[...] == tile[0], mine[...].astype(jnp.float32), answers[...].astype(jnp.float32)
    )
    out[...] = (weights[...] * deriv * fetched).astype(out.dtype)


def pre_gradient(own, near, far, tiles, tile, weights, mine, answers):
    spec = pl.BlockSpec(memory_space=pltpu.VMEM)
    return pl.pallas_call(
        gradient_kernel,
        out_shape=jax.ShapeDtypeStruct(own.shape, jnp.bfloat16),
        in_specs=[spec] * 4 + [pl.BlockSpec(memory_space=pltpu.SMEM)] + [spec] * 3,
        out_specs=spec,
        compiler_params=memory(16),
        name="pre_gradient",
    )(own, near, far, tiles, tile.reshape(1), weights, mine, answers)


def collect_kernel(core, own, received, out):
    half = own.shape[0]
    for piece, which in ((own, core[0]), (received, 1 - core[0])):
        out[pl.ds(pl.multiple_of(which * half, half), half), :] = piece[...].astype(jnp.float32)


def collect(core, own, received):
    spec = pl.BlockSpec(memory_space=pltpu.VMEM)
    return pl.pallas_call(
        collect_kernel,
        out_shape=jax.ShapeDtypeStruct((2 * own.shape[0], own.shape[1]), jnp.float32),
        in_specs=[pl.BlockSpec(memory_space=pltpu.SMEM), spec, spec],
        out_specs=spec,
        compiler_params=memory(16),
        name="collect",
    )(core.reshape(1), own, received)


def sum_over_panels(core, keep, send):
    both = ("obs", "pix")
    wide = jnp.float32
    value = keep + swap(send, "obs", 1).astype(wide)
    for order in ((4, 1), (1, 4)):
        value = lax.reduce_precision(value, 8, 7)
        other = lax.ppermute(
            value.astype(jnp.bfloat16), both, [(i, i ^ order[(i >> 1) & 1]) for i in range(8)]
        )
        value = value + other.astype(wide)
    value = lax.reduce_precision(value, 8, 7).astype(jnp.bfloat16)
    return collect(core, value, swap(value, "obs", 1))


def shards(spectra, enc_weight, pix_tile, pix_local, foot_weight, cotangent, adjoint, mixing):
    tile_count = lax.axis_size("pix")
    tile_rows = cotangent.shape[0]
    quarter = spectra.shape[0] // lax.axis_size("chan")
    tile = lax.axis_index("pix")
    chan = lax.axis_index("chan")
    first_row = chan * quarter
    middle = [(1, 2), (2, 1)]

    part3, part2, part1, part0 = project(spectra, enc_weight, chan)
    outer2 = lax.ppermute(part2, "chan", [(0, 1), (3, 2)])
    inner2 = lax.ppermute(part2, "chan", middle)
    outer3 = lax.ppermute(part3, "chan", [(0, 2), (3, 1)])
    wide = jnp.float32
    sum1 = part1.astype(wide) + inner2.astype(wide) + outer3.astype(wide)
    sum3 = part3.astype(wide) + outer2.astype(wide)
    near = swap(sum1.astype(jnp.bfloat16), "chan", 1)
    far = lax.ppermute(sum3.astype(jnp.bfloat16), "chan", middle)

    above, below = edges(cotangent, "pix", HALO)
    anchor = tile * tile_rows - HALO
    tile_ids = lax.dynamic_slice_in_dim(pix_tile, first_row, quarter, 0)
    weights = lax.dynamic_slice_in_dim(foot_weight, first_row, quarter, 0)[:, None]
    capacity = 2 * quarter // tile_count
    if capacity >= quarter and tile_count == 2:
        lists = (pix_local, swap(pix_local, "pix", 1))
        rows = pixel_rows(
            cotangent, above, below, adjoint, mixing, anchor, lists, first_row, quarter
        )
        mine, answers = rows[:quarter], swap(rows[quarter:], "pix", 1)
    else:
        local_ids = lax.dynamic_slice_in_dim(pix_local, first_row, quarter, 0)
        slot_index, wanted = requests(tile_ids[:, 0], local_ids, capacity)
        rows = pixel_rows(
            cotangent, above, below, adjoint, mixing, anchor, (wanted,), 0 * chan, wanted.shape[0]
        )
        answers = lax.all_to_all(
            rows.reshape(tile_count, capacity, -1), "pix", split_axis=0, concat_axis=0, tiled=True
        )
        answers = jnp.take(answers.reshape(tile_count * capacity, -1), slot_index, axis=0)
        mine = answers
    grads = pre_gradient(part0, near, far, tile_ids, tile, weights, mine, answers)

    beside = swap(grads, "chan", 1)
    across = lax.ppermute(grads, "chan", middle)
    passed = lax.ppermute(across, "chan", [(1, 0), (2, 3)])
    crossed = lax.ppermute(beside, "chan", middle)
    skipped = lax.ppermute(beside, "chan", [(2, 0), (1, 3)])
    flipped = turned(spectra, chan)
    core = lax.axis_index("obs") & 1
    early = early_product(spectra, chan, grads, beside)
    keep, send = late_product(chan, core, flipped, early, crossed, passed, across, skipped)
    if lax.axis_size("obs") == 4 and tile_count == 2:
        return sum_over_panels(core, keep, send)
    return lax.psum(collect(core, keep, send), ("obs", "pix"))


def solution(mesh):
    return jax.shard_map(
        shards,
        mesh=mesh,
        in_specs=(
            P(("obs", "pix"), "chan"),
            P("chan", None),
            P(("obs", "pix"), None),
            P(("obs", "pix")),
            P(("obs", "pix")),
            P("pix", None),
            P(None, "pix"),
            P(),
        ),
        out_specs=P("chan", None),
        check_vma=False,
    )
```

time: 186 us -> 92.8 us (0.50)
  the two profiles are of different devices: /device:TPU:0 before, /device:TPU:11 now
where the time goes in v4:
time: 92.8 us; the launch traced here: 92.3 us
  starting transfers between devices  33.6 us (36%)
  Pallas kernels  28.2 us (30%)
  waiting for transfers between devices  22.9 us (25%)
  local copies, waits for them, and re-layouts  5.8 us (6%)
  other arithmetic  1.62 us (2%)
    pallas_call x1, Pallas kernels, pixel_rows(): pl.pallas_call(functools.partial(pixel_kernel, count), out_shape=jax.Shap...  15.2 us
    ppermute x6, starting transfers between devices, swap(): return lax.ppermute(value, axis, [(i, i ^ bit) for i in range(size)])  14 us
    ppermute x2, waiting for transfers between devices, sum_over_panels(): lax.ppermute(value.astype(jnp.bfloat16), both, [(i, i ^ order[i >> 1 & 1]...  10.3 us
    pallas_call x1, Pallas kernels, project(): pl.pallas_call(project_kernel, out_shape=(part,) * 4, grid_spec=pltpu.Pre...  7.72 us
    ppermute x6, waiting for transfers between devices, swap(): return lax.ppermute(value, axis, [(i, i ^ bit) for i in range(size)])  4.91 us
    unnamed x21, local copies, waits for them, and re-layouts  4.85 us
    ppermute x1, waiting for transfers between devices, shards(): across = lax.ppermute(grads, 'chan', middle)  3.83 us
    ppermute x1, starting transfers between devices, shards(): across = lax.ppermute(grads, 'chan', middle)  3.2 us
  transfers between devices with their start and end apart: 17, of which 10 were waited for; matrix products, arithmetic and copies ran while one was open for 3% of the time, Pallas kernels for 19%

profile of v4, /device:TPU:11, one launch (start us, length us, event | category | flops | bytes accessed | tf_op | source)
XLA Modules:
  0.0 92.3 jit_solution(10803410942655149494)
XLA Ops:
  0.0 7.7 %project.1 = (bf16[512,256]{1,0:T(8,128)(2,1)}, bf16[512,256]{1,0:T(8,128)(2,1)}, bf16[512,256]{1,0:T(8,128)(2,1)}, bf16[512,256]{1,0:T(8,128)(2,1)}) custom-call(s32[1]{0:T(128)} %bitcast.1.chan, bf16[2048,1152]{1,0:T(8,128)(2,1)} %spectra.5, bf16[1152,256]{1,0:T(8,128)(2,1)} %weight.1), custom_call_target="tpu_custom_call" | custom-call | flops 1207959552 | bytes 6356992 | tf_op jit(solution)/shard_map/project/pallas_call | solution.py:71
  7.8 1.3 %collective-permute-start.3 = (bf16[512,256]{1,0:T(8,128)(2,1)}, bf16[512,256]{1,0:T(8,128)(2,1)S(1)}, u32[]{:S(2)}, u32[]{:S(2)}) collective-permute-start(bf16[512,256]{1,0:T(8,128)(2,1)} %get-tuple-element.13), channel_id=1, source_target_pairs={{0,1},{3,2},{4,5},{7,6},{8,9},{11,10},{12,13},{15,14},{16,17},{19,... | collective-permute-start | bytes 786440 | tf_op jit(solution)/shard_map/ppermute | solution.py:316
  9.0 3.2 %collective-permute-start = (bf16[512,256]{1,0:T(8,128)(2,1)}, bf16[512,256]{1,0:T(8,128)(2,1)S(1)}, u32[]{:S(2)}, u32[]{:S(2)}) collective-permute-start(bf16[512,256]{1,0:T(8,128)(2,1)} %get-tuple-element.13), channel_id=1, source_target_pairs={{1,2},{2,1},{5,6},{6,5},{9,10},{10,9},{13,14},{14,13},{17,18},{18,... | collective-permute-start | bytes 786440 | tf_op jit(solution)/shard_map/ppermute | solution.py:317
  12.3 1.3 %collective-permute-start.5 = (s32[2048]{0:T(1024)S(1)}, s32[2048]{0:T(1024)S(1)}, u32[]{:S(2)}, u32[]{:S(2)}) collective-permute-start(s32[2048]{0:T(1024)S(1)} %copy-done.5), channel_id=1, source_target_pairs={{0,4},{4,0},{1,5},{5,1},{2,6},{6,2},{3,7},{7,3},{8,12},{12,8},{9,1... | collective-permute-start | bytes 24584 | tf_op jit(solution)/shard_map/ppermute | solution.py:44
  13.9 1.3 %collective-permute-start.1 = (bf16[512,256]{1,0:T(8,128)(2,1)}, bf16[512,256]{1,0:T(8,128)(2,1)}, u32[]{:S(2)}, u32[]{:S(2)}) collective-permute-start(bf16[512,256]{1,0:T(8,128)(2,1)} %get-tuple-element.14), channel_id=1, source_target_pairs={{0,2},{3,1},{4,6},{7,5},{8,10},{11,9},{12,14},{15,13},{16,18},{19,... | collective-permute-start | bytes 786440 | tf_op jit(solution)/shard_map/ppermute | solution.py:318
  15.2 1.9 %collective-permute-done.6.refs_3_.refs_4_ = bf16[128,256]{1,0:T(8,128)(2,1)S(1)} collective-permute-done((bf16[128,256]{1,0:T(8,128)(2,1)S(1)}, bf16[128,256]{1,0:T(8,128)(2,1)S(1)}, u32[]{:S(2)}, u32[]{:S(2)}) %collective-permute-start.6) | collective-permute-done | bytes 65568 | tf_op jit(solution)/shard_map/ppermute | solution.py:21
  17.2 15.2 %pixel_rows.1 = bf16[1024,256]{1,0:T(8,128)(2,1)S(1)} custom-call(s32[1]{0:T(128)} %bitcast.4.start, s32[8,4096]{1,0:T(8,128)S(1)} %subtract_multiply_fusion.places, s32[2048]{0:T(1024)S(1)} %copy-done.5, s32[2048]{0:T(1024)S(1)} %collective-permute-done.5.refs_1_, bf16[4096,256]{1,0:T(8,128)(2,1)S(1)} %copy-done.4, ...), custom_call_target="tpu_custom_call" | custom-call | flops 4294967296 | bytes 4194304 | tf_op jit(solution)/shard_map/pixel_rows/pallas_call | solution.py:231
  32.7 2.1 %collective-permute-start.4 = (bf16[512,256]{1,0:T(8,128)(2,1)S(1)}, bf16[512,256]{1,0:T(8,128)(2,1)S(1)}, u32[]{:S(2)}, u32[]{:S(2)}) collective-permute-start(bf16[512,256]{1,0:T(8,128)(2,1)S(1)} %add_convert_fusion), channel_id=1, source_target_pairs={{1,2},{2,1},{5,6},{6,5},{9,10},{10,9},{13,14},{14,13},{17,18},{18,... | collective-permute-start | bytes 786440 | tf_op jit(solution)/shard_map/ppermute | solution.py:323
  34.8 1.1 %add_convert_fusion.1 = bf16[512,256]{1,0:T(8,128)(2,1)S(1)} fusion(bf16[512,256]{1,0:T(8,128)(2,1)} %collective-permute-done.1, bf16[512,256]{1,0:T(8,128)(2,1)S(1)} %collective-permute-done, bf16[512,256]{1,0:T(8,128)(2,1)S(1)} %copy-done.8), kind=kLoop, calls=%fused_computation.4 | loop fusion | flops 786432 | bytes 1048576 | tf_op jit(solution)/shard_map/convert_element_type | solution.py:322
  35.9 0.5 collective-permute-start.2
  36.4 0.8 dynamic_slice.7
  37.5 0.8 collective-permute-done.7.answers
  38.3 1.8 %collective-permute-done.4.far = bf16[512,256]{1,0:T(8,128)(2,1)S(1)} collective-permute-done((bf16[512,256]{1,0:T(8,128)(2,1)S(1)}, bf16[512,256]{1,0:T(8,128)(2,1)S(1)}, u32[]{:S(2)}, u32[]{:S(2)}) %collective-permute-start.4) | collective-permute-done | bytes 262176 | tf_op jit(solution)/shard_map/ppermute | solution.py:323
  40.1 1.4 %collective-permute-done.2.near = bf16[512,256]{1,0:T(8,128)(2,1)S(1)} collective-permute-done((bf16[512,256]{1,0:T(8,128)(2,1)S(1)}, bf16[512,256]{1,0:T(8,128)(2,1)S(1)}, u32[]{:S(2)}, u32[]{:S(2)}) %collective-permute-start.2) | collective-permute-done | bytes 262176 | tf_op jit(solution)/shard_map/ppermute | solution.py:44
  41.8 3.2 %collective-permute-start.10 = (bf16[512,256]{1,0:T(8,128)(2,1)S(1)}, bf16[512,256]{1,0:T(8,128)(2,1)S(1)}, u32[]{:S(2)}, u32[]{:S(2)}) collective-permute-start(bf16[512,256]{1,0:T(8,128)(2,1)S(1)} %pre_gradient.1.first), channel_id=1, source_target_pairs={{1,2},{2,1},{5,6},{6,5},{9,10},{10,9},{13,14},{14,13},{17,18},{18,... | collective-permute-start | bytes 786440 | tf_op jit(solution)/shard_map/ppermute | solution.py:350
  45.1 3.8 %collective-permute-done.10.across = bf16[512,256]{1,0:T(8,128)(2,1)S(1)} collective-permute-done((bf16[512,256]{1,0:T(8,128)(2,1)S(1)}, bf16[512,256]{1,0:T(8,128)(2,1)S(1)}, u32[]{:S(2)}, u32[]{:S(2)}) %collective-permute-start.10) | collective-permute-done | bytes 262176 | tf_op jit(solution)/shard_map/ppermute | solution.py:350
  48.9 1.3 %collective-permute-start.11 = (bf16[512,256]{1,0:T(8,128)(2,1)S(1)}, bf16[512,256]{1,0:T(8,128)(2,1)S(1)}, u32[]{:S(2)}, u32[]{:S(2)}) collective-permute-start(bf16[512,256]{1,0:T(8,128)(2,1)S(1)} %collective-permute-done.10.across), channel_id=1, source_target_pairs={{1,0},{2,3},{5,4},{6,7},{9,8},{10,11},{13,12},{14,15},{17,16},{18,... | collective-permute-start | bytes 786440 | tf_op jit(solution)/shard_map/ppermute | solution.py:351
  50.6 2.2 %collective-permute-start.12 = (bf16[512,256]{1,0:T(8,128)(2,1)S(1)}, bf16[512,256]{1,0:T(8,128)(2,1)}, u32[]{:S(2)}, u32[]{:S(2)}) collective-permute-start(bf16[512,256]{1,0:T(8,128)(2,1)S(1)} %collective-permute-done.8.second), channel_id=1, source_target_pairs={{2,0},{1,3},{6,4},{5,7},{10,8},{9,11},{14,12},{13,15},{18,16},{17,... | collective-permute-start | bytes 786440 | tf_op jit(solution)/shard_map/ppermute | solution.py:353
  52.8 3.2 %collective-permute-start.9 = (bf16[512,256]{1,0:T(8,128)(2,1)S(1)}, bf16[512,256]{1,0:T(8,128)(2,1)}, u32[]{:S(2)}, u32[]{:S(2)}) collective-permute-start(bf16[512,256]{1,0:T(8,128)(2,1)S(1)} %collective-permute-done.8.second), channel_id=1, source_target_pairs={{1,2},{2,1},{5,6},{6,5},{9,10},{10,9},{13,14},{14,13},{17,18},{18,... | collective-permute-start | bytes 786440 | tf_op jit(solution)/shard_map/ppermute | solution.py:352
  56.0 2.3 %copy-done.1 = bf16[2048,1152]{1,0:T(8,128)(2,1)S(1)} copy-done((bf16[2048,1152]{1,0:T(8,128)(2,1)S(1)}, bf16[2048,1152]{1,0:T(8,128)(2,1)}, u32[]{:S(2)}) %copy-start.1) | copy-done | bytes 4718616
  58.4 0.9 turned.1.flipped
  59.4 2.3 %copy-done.2 = bf16[2048,1152]{1,0:T(8,128)(2,1)S(1)} copy-done((bf16[2048,1152]{1,0:T(8,128)(2,1)S(1)}, bf16[2048,1152]{1,0:T(8,128)(2,1)}, u32[]{:S(2)}) %copy-start.2) | copy-done | bytes 4718616
  61.7 1.1 %early_product.1.before = f32[1152,256]{1,0:T(8,128)S(1)} custom-call(s32[1]{0:T(128)} %bitcast.1.chan, bf16[2048,1152]{1,0:T(8,128)(2,1)S(1)} %copy-done.2, bf16[512,256]{1,0:T(8,128)(2,1)S(1)} %pre_gradient.1.first, bf16[512,256]{1,0:T(8,128)(2,1)S(1)} %collective-permute-done.8.second), custom_call_target="tpu_custom_call" | custom-call | flops 603979776 | bytes 3538944 | tf_op jit(solution)/shard_map/early_product/pallas_call | solution.py:137
  62.8 1.8 %late_product.1 = (f32[576,256]{1,0:T(8,128)S(1)}, bf16[576,256]{1,0:T(8,128)(2,1)S(1)}) custom-call(s32[2]{0:T(128)S(1)} %pad_add_fusion.where, bf16[1152,1024]{1,0:T(8,128)(2,1)S(1)} %turned.1.flipped, f32[1152,256]{1,0:T(8,128)S(1)} %early_product.1.before, bf16[512,256]{1,0:T(8,128)(2,1)} %collective-permute-done.9.crossed, ...), custom_call_target="tpu_custom_call" | custom-call | tf_op jit(solution)/shard_map/late_product/pallas_call | solution.py:172
  64.7 9.7 %collective-permute-start.13 = (bf16[576,256]{1,0:T(8,128)(2,1)S(1)}, bf16[576,256]{1,0:T(8,128)(2,1)S(1)}, u32[]{:S(2)}, u32[]{:S(2)}) collective-permute-start(bf16[576,256]{1,0:T(8,128)(2,1)S(1)} %get-tuple-element.16), channel_id=1, source_target_pairs={{0,8},{8,0},{16,24},{24,16},{1,9},{9,1},{17,25},{25,17},{2,10},{10... | collective-permute-start | bytes 884744 | tf_op jit(solution)/shard_map/ppermute | solution.py:44
  74.4 1.2 %collective-permute-done.13 = bf16[576,256]{1,0:T(8,128)(2,1)S(1)} collective-permute-done((bf16[576,256]{1,0:T(8,128)(2,1)S(1)}, bf16[576,256]{1,0:T(8,128)(2,1)S(1)}, u32[]{:S(2)}, u32[]{:S(2)}) %collective-permute-start.13) | collective-permute-done | bytes 294944 | tf_op jit(solution)/shard_map/ppermute | solution.py:44
  75.7 1.2 %collective-permute-start.14 = (bf16[576,256]{1,0:T(8,128)(2,1)S(1)}, bf16[576,256]{1,0:T(8,128)(2,1)S(1)}, u32[]{:S(2)}, u32[]{:S(2)}) collective-permute-start(bf16[576,256]{1,0:T(8,128)(2,1)S(1)} %fusion), channel_id=1, source_target_pairs={{0,16},{4,20},{8,12},{12,8},{16,0},{20,4},{24,28},{28,24},{1,17},{... | collective-permute-start | bytes 884744 | tf_op jit(solution)/shard_map/ppermute | solution.py:298
  76.9 4.7 %collective-permute-done.14 = bf16[576,256]{1,0:T(8,128)(2,1)S(1)} collective-permute-done((bf16[576,256]{1,0:T(8,128)(2,1)S(1)}, bf16[576,256]{1,0:T(8,128)(2,1)S(1)}, u32[]{:S(2)}, u32[]{:S(2)}) %collective-permute-start.14) | collective-permute-done | bytes 294944 | tf_op jit(solution)/shard_map/ppermute | solution.py:298
  82.1 5.6 %collective-permute-done.15 = bf16[576,256]{1,0:T(8,128)(2,1)S(1)} collective-permute-done((bf16[576,256]{1,0:T(8,128)(2,1)S(1)}, bf16[576,256]{1,0:T(8,128)(2,1)S(1)}, u32[]{:S(2)}, u32[]{:S(2)}) %collective-permute-start.15) | collective-permute-done | bytes 294944 | tf_op jit(solution)/shard_map/ppermute | solution.py:298
  87.9 2.1 %collective-permute-start.16 = (bf16[576,256]{1,0:T(8,128)(2,1)S(1)}, bf16[576,256]{1,0:T(8,128)(2,1)S(1)}, u32[]{:S(2)}, u32[]{:S(2)}) collective-permute-start(bf16[576,256]{1,0:T(8,128)(2,1)S(1)} %reduce-precision_convert_fusion.own), channel_id=1, source_target_pairs={{0,8},{8,0},{16,24},{24,16},{1,9},{9,1},{17,25},{25,17},{2,10},{10... | collective-permute-start | bytes 884744 | tf_op jit(solution)/shard_map/ppermute | solution.py:44
  90.0 1.2 %collective-permute-done.16.received = bf16[576,256]{1,0:T(8,128)(2,1)S(1)} collective-permute-done((bf16[576,256]{1,0:T(8,128)(2,1)S(1)}, bf16[576,256]{1,0:T(8,128)(2,1)S(1)}, u32[]{:S(2)}, u32[]{:S(2)}) %collective-permute-start.16) | collective-permute-done | bytes 294944 | tf_op jit(solution)/shard_map/ppermute | solution.py:44
  91.3 1.1 %collect.1 = f32[1152,256]{1,0:T(8,128)} custom-call(s32[1]{0:T(128)} %bitcast.core, bf16[576,256]{1,0:T(8,128)(2,1)S(1)} %reduce-precision_convert_fusion.own, bf16[576,256]{1,0:T(8,128)(2,1)S(1)} %collective-permute-done.16.received), custom_call_target="tpu_custom_call" | custom-call | tf_op jit(solution)/shard_map/collect/pallas_call | solution.py:282
  (42 shorter events, 2.6 us)
Async XLA Ops:
  0.0 37.3 %copy-start = (s32[2048,1]{0,1:T(1,128)S(1)}, s32[2048,1]{0,1:T(1,128)}, u32[]{:S(2)}) copy-start(s32[2048,1]{0,1:T(1,128)} %param.10) | copy-start | bytes 24580
  0.0 12.3 %copy-start.5 = (s32[2048]{0:T(1024)S(1)}, s32[2048]{0:T(1024)}, u32[]{:S(2)}) copy-start(s32[2048]{0:T(1024)} %refs_0_.1) | copy-start | bytes 24580
  0.0 13.6 %copy-start.4 = (bf16[4096,256]{1,0:T(8,128)(2,1)S(1)}, bf16[4096,256]{1,0:T(8,128)(2,1)}, u32[]{:S(2)}) copy-start(bf16[4096,256]{1,0:T(8,128)(2,1)} %refs_2_.1) | copy-start | bytes 6291460
  0.0 15.2 %copy-start.9 = (s32[8,4096]{1,0:T(8,128)S(1)}, s32[8,4096]{1,0:T(8,128)}, u32[]{:S(2)}) copy-start(s32[8,4096]{1,0:T(8,128)} %param.14) | copy-start | bytes 393220
  0.0 17.1 %copy-start.6 = (f32[8,256]{1,0:T(8,128)S(1)}, f32[8,256]{1,0:T(8,128)}, u32[]{:S(2)}) copy-start(f32[8,256]{1,0:T(8,128)} %refs_5_.1) | copy-start | bytes 24580
  7.8 24.9 %collective-permute-start.3 = (bf16[512,256]{1,0:T(8,128)(2,1)}, bf16[512,256]{1,0:T(8,128)(2,1)S(1)}, u32[]{:S(2)}, u32[]{:S(2)}) collective-permute-start(bf16[512,256]{1,0:T(8,128)(2,1)} %get-tuple-element.13), channel_id=1, source_target_pairs={{0,1},{3,2},{4,5},{7,6},{8,9},{11,10},{12,13},{15,14},{16,17},{19,... | collective-permute-start | bytes 786440 | tf_op jit(solution)/shard_map/ppermute | solution.py:316
  9.0 25.7 %collective-permute-start = (bf16[512,256]{1,0:T(8,128)(2,1)}, bf16[512,256]{1,0:T(8,128)(2,1)S(1)}, u32[]{:S(2)}, u32[]{:S(2)}) collective-permute-start(bf16[512,256]{1,0:T(8,128)(2,1)} %get-tuple-element.13), channel_id=1, source_target_pairs={{1,2},{2,1},{5,6},{6,5},{9,10},{10,9},{13,14},{14,13},{17,18},{18,... | collective-permute-start | bytes 786440 | tf_op jit(solution)/shard_map/ppermute | solution.py:317
  12.3 2.9 %collective-permute-start.5 = (s32[2048]{0:T(1024)S(1)}, s32[2048]{0:T(1024)S(1)}, u32[]{:S(2)}, u32[]{:S(2)}) collective-permute-start(s32[2048]{0:T(1024)S(1)} %copy-done.5), channel_id=1, source_target_pairs={{0,4},{4,0},{1,5},{5,1},{2,6},{6,2},{3,7},{7,3},{8,12},{12,8},{9,1... | collective-permute-start | bytes 24584 | tf_op jit(solution)/shard_map/ppermute | solution.py:44
  13.6 3.6 %collective-permute-start.6 = (bf16[128,256]{1,0:T(8,128)(2,1)S(1)}, bf16[128,256]{1,0:T(8,128)(2,1)S(1)}, u32[]{:S(2)}, u32[]{:S(2)}) collective-permute-start(bf16[128,256]{1,0:T(8,128)(2,1)S(1)} %slice_select_fusion), channel_id=1, source_target_pairs={{0,4},{4,0},{1,5},{5,1},{2,6},{6,2},{3,7},{7,3},{8,12},{12,8},{9,1... | collective-permute-start | bytes 196616 | tf_op jit(solution)/shard_map/ppermute | solution.py:21
  13.9 20.9 %collective-permute-start.1 = (bf16[512,256]{1,0:T(8,128)(2,1)}, bf16[512,256]{1,0:T(8,128)(2,1)}, u32[]{:S(2)}, u32[]{:S(2)}) collective-permute-start(bf16[512,256]{1,0:T(8,128)(2,1)} %get-tuple-element.14), channel_id=1, source_target_pairs={{0,2},{3,1},{4,6},{7,5},{8,10},{11,9},{12,14},{15,13},{16,18},{19,... | collective-permute-start | bytes 786440 | tf_op jit(solution)/shard_map/ppermute | solution.py:318
  17.2 15.5 %copy-start.7 = (bf16[512,256]{1,0:T(8,128)(2,1)S(1)}, bf16[512,256]{1,0:T(8,128)(2,1)}, u32[]{:S(2)}) copy-start(bf16[512,256]{1,0:T(8,128)(2,1)} %get-tuple-element.14) | copy-start | bytes 786436
  17.2 17.6 %copy-start.8 = (bf16[512,256]{1,0:T(8,128)(2,1)S(1)}, bf16[512,256]{1,0:T(8,128)(2,1)}, u32[]{:S(2)}) copy-start(bf16[512,256]{1,0:T(8,128)(2,1)} %get-tuple-element.12) | copy-start | bytes 786436
  32.4 9.1 %copy-start.3 = (bf16[512,256]{1,0:T(8,128)(2,1)S(1)}, bf16[512,256]{1,0:T(8,128)(2,1)}, u32[]{:S(2)}) copy-start(bf16[512,256]{1,0:T(8,128)(2,1)} %get-tuple-element.11.own) | copy-start | bytes 786436
  32.4 5.9 %collective-permute-start.7 = (bf16[512,256]{1,0:T(8,128)(2,1)S(1)}, bf16[512,256]{1,0:T(8,128)(2,1)S(1)}, u32[]{:S(2)}, u32[]{:S(2)}) collective-permute-start(bf16[512,256]{1,0:T(8,128)(2,1)S(1)} %get-tuple-element.17), channel_id=1, source_target_pairs={{0,4},{4,0},{1,5},{5,1},{2,6},{6,2},{3,7},{7,3},{8,12},{12,8},{9,1... | collective-permute-start | bytes 786440 | tf_op jit(solution)/shard_map/ppermute | solution.py:44
  32.7 7.4 %collective-permute-start.4 = (bf16[512,256]{1,0:T(8,128)(2,1)S(1)}, bf16[512,256]{1,0:T(8,128)(2,1)S(1)}, u32[]{:S(2)}, u32[]{:S(2)}) collective-permute-start(bf16[512,256]{1,0:T(8,128)(2,1)S(1)} %add_convert_fusion), channel_id=1, source_target_pairs={{1,2},{2,1},{5,6},{6,5},{9,10},{10,9},{13,14},{14,13},{17,18},{18,... | collective-permute-start | bytes 786440 | tf_op jit(solution)/shard_map/ppermute | solution.py:323
  35.9 5.6 %collective-permute-start.2 = (bf16[512,256]{1,0:T(8,128)(2,1)S(1)}, bf16[512,256]{1,0:T(8,128)(2,1)S(1)}, u32[]{:S(2)}, u32[]{:S(2)}) collective-permute-start(bf16[512,256]{1,0:T(8,128)(2,1)S(1)} %add_convert_fusion.1), channel_id=1, source_target_pairs={{0,1},{1,0},{2,3},{3,2},{4,5},{5,4},{6,7},{7,6},{8,9},{9,8},{10,11... | collective-permute-start | bytes 786440 | tf_op jit(solution)/shard_map/ppermute | solution.py:44
  41.8 7.1 %collective-permute-start.10 = (bf16[512,256]{1,0:T(8,128)(2,1)S(1)}, bf16[512,256]{1,0:T(8,128)(2,1)S(1)}, u32[]{:S(2)}, u32[]{:S(2)}) collective-permute-start(bf16[512,256]{1,0:T(8,128)(2,1)S(1)} %pre_gradient.1.first), channel_id=1, source_target_pairs={{1,2},{2,1},{5,6},{6,5},{9,10},{10,9},{13,14},{14,13},{17,18},{18,... | collective-permute-start | bytes 786440 | tf_op jit(solution)/shard_map/ppermute | solution.py:350
  45.0 5.6 %collective-permute-start.8 = (bf16[512,256]{1,0:T(8,128)(2,1)S(1)}, bf16[512,256]{1,0:T(8,128)(2,1)S(1)}, u32[]{:S(2)}, u32[]{:S(2)}) collective-permute-start(bf16[512,256]{1,0:T(8,128)(2,1)S(1)} %pre_gradient.1.first), channel_id=1, source_target_pairs={{0,1},{1,0},{2,3},{3,2},{4,5},{5,4},{6,7},{7,6},{8,9},{9,8},{10,11... | collective-permute-start | bytes 786440 | tf_op jit(solution)/shard_map/ppermute | solution.py:44
  48.9 13.8 %collective-permute-start.11 = (bf16[512,256]{1,0:T(8,128)(2,1)S(1)}, bf16[512,256]{1,0:T(8,128)(2,1)S(1)}, u32[]{:S(2)}, u32[]{:S(2)}) collective-permute-start(bf16[512,256]{1,0:T(8,128)(2,1)S(1)} %collective-permute-done.10.across), channel_id=1, source_target_pairs={{1,0},{2,3},{5,4},{6,7},{9,8},{10,11},{13,12},{14,15},{17,16},{18,... | collective-permute-start | bytes 786440 | tf_op jit(solution)/shard_map/ppermute | solution.py:351
  50.6 12.2 %collective-permute-start.12 = (bf16[512,256]{1,0:T(8,128)(2,1)S(1)}, bf16[512,256]{1,0:T(8,128)(2,1)}, u32[]{:S(2)}, u32[]{:S(2)}) collective-permute-start(bf16[512,256]{1,0:T(8,128)(2,1)S(1)} %collective-permute-done.8.second), channel_id=1, source_target_pairs={{2,0},{1,3},{6,4},{5,7},{10,8},{9,11},{14,12},{13,15},{18,16},{17,... | collective-permute-start | bytes 786440 | tf_op jit(solution)/shard_map/ppermute | solution.py:353
  52.8 10.0 %collective-permute-start.9 = (bf16[512,256]{1,0:T(8,128)(2,1)S(1)}, bf16[512,256]{1,0:T(8,128)(2,1)}, u32[]{:S(2)}, u32[]{:S(2)}) collective-permute-start(bf16[512,256]{1,0:T(8,128)(2,1)S(1)} %collective-permute-done.8.second), channel_id=1, source_target_pairs={{1,2},{2,1},{5,6},{6,5},{9,10},{10,9},{13,14},{14,13},{17,18},{18,... | collective-permute-start | bytes 786440 | tf_op jit(solution)/shard_map/ppermute | solution.py:352
  56.0 2.3 %copy-start.1 = (bf16[2048,1152]{1,0:T(8,128)(2,1)S(1)}, bf16[2048,1152]{1,0:T(8,128)(2,1)}, u32[]{:S(2)}) copy-start(bf16[2048,1152]{1,0:T(8,128)(2,1)} %spectra.5) | copy-start | bytes 14155780
  59.4 2.3 %copy-start.2 = (bf16[2048,1152]{1,0:T(8,128)(2,1)S(1)}, bf16[2048,1152]{1,0:T(8,128)(2,1)}, u32[]{:S(2)}) copy-start(bf16[2048,1152]{1,0:T(8,128)(2,1)} %spectra.5) | copy-start | bytes 14155780
  64.7 11.0 %collective-permute-start.13 = (bf16[576,256]{1,0:T(8,128)(2,1)S(1)}, bf16[576,256]{1,0:T(8,128)(2,1)S(1)}, u32[]{:S(2)}, u32[]{:S(2)}) collective-permute-start(bf16[576,256]{1,0:T(8,128)(2,1)S(1)} %get-tuple-element.16), channel_id=1, source_target_pairs={{0,8},{8,0},{16,24},{24,16},{1,9},{9,1},{17,25},{25,17},{2,10},{10... | collective-permute-start | bytes 884744 | tf_op jit(solution)/shard_map/ppermute | solution.py:44
  75.7 5.9 %collective-permute-start.14 = (bf16[576,256]{1,0:T(8,128)(2,1)S(1)}, bf16[576,256]{1,0:T(8,128)(2,1)S(1)}, u32[]{:S(2)}, u32[]{:S(2)}) collective-permute-start(bf16[576,256]{1,0:T(8,128)(2,1)S(1)} %fusion), channel_id=1, source_target_pairs={{0,16},{4,20},{8,12},{12,8},{16,0},{20,4},{24,28},{28,24},{1,17},{... | collective-permute-start | bytes 884744 | tf_op jit(solution)/shard_map/ppermute | solution.py:298
  81.8 5.9 %collective-permute-start.15 = (bf16[576,256]{1,0:T(8,128)(2,1)S(1)}, bf16[576,256]{1,0:T(8,128)(2,1)S(1)}, u32[]{:S(2)}, u32[]{:S(2)}) collective-permute-start(bf16[576,256]{1,0:T(8,128)(2,1)S(1)} %fusion.1), channel_id=1, source_target_pairs={{0,4},{4,0},{8,24},{12,28},{16,20},{20,16},{24,8},{28,12},{1,5},{5... | collective-permute-start | bytes 884744 | tf_op jit(solution)/shard_map/ppermute | solution.py:298
  87.9 3.4 %collective-permute-start.16 = (bf16[576,256]{1,0:T(8,128)(2,1)S(1)}, bf16[576,256]{1,0:T(8,128)(2,1)S(1)}, u32[]{:S(2)}, u32[]{:S(2)}) collective-permute-start(bf16[576,256]{1,0:T(8,128)(2,1)S(1)} %reduce-precision_convert_fusion.own), channel_id=1, source_target_pairs={{0,8},{8,0},{16,24},{24,16},{1,9},{9,1},{17,25},{25,17},{2,10},{10... | collective-permute-start | bytes 884744 | tf_op jit(solution)/shard_map/ppermute | solution.py:44

commit v5 on v4

--- a/solution.py
+++ b/solution.py
@@ -48,42 +48,45 @@
     return pltpu.CompilerParams(vmem_limit_bytes=mib * MIB)
 
 
-def project_kernel(chan, spectra, weight, *parts):
-    step = pl.program_id(0)
-    result = jnp.dot(
-        spectra[...], weight[...], preferred_element_type=jnp.float32
-    ).astype(jnp.bfloat16)
-    rows = result.shape[0]
-    turns = parts[0].shape[0] // rows
-    for index, part in enumerate(parts):
-        for turn in range(turns):
-
-            @pl.when(step == index * turns + turn)
-            def _(part=part, turn=turn):
-                part[turn * rows : (turn + 1) * rows, :] = result
+def project_kernel(chan, spectra, weight, part3, part2, part1, part0, held, near, sems):
+    parts = (part3, part2, part1, part0)
+    quarter = part0.shape[0]
+    chunk = quarter // 2
+    copies = [pltpu.make_async_copy(weight, near, sems.at[8])]
+    places = []
+    for turn in range(8):
+        first = (chan[0] ^ (3 - turn // 2)) * quarter + (turn % 2) * chunk
+        places.append(pl.ds(pl.multiple_of(first, chunk), chunk))
+        copies.append(
+            pltpu.make_async_copy(spectra.at[places[-1]], held.at[places[-1]], sems.at[turn])
+        )
+    for copy in copies:
+        copy.start()
+    copies[0].wait()
+    for turn in range(8):
+        copies[turn + 1].wait()
+        result = jnp.dot(held[places[turn], :], near[...], preferred_element_type=jnp.float32)
+        first = (turn % 2) * chunk
+        parts[turn // 2][first : first + chunk, :] = result.astype(jnp.bfloat16)
 
 
 def project(spectra, weight, chan):
     depth, width = weight.shape
     quarter = spectra.shape[0] // 4
-    turns = 2
     part = jax.ShapeDtypeStruct((quarter, width), jnp.bfloat16)
+    vmem = pl.BlockSpec(memory_space=pltpu.VMEM)
+    hbm = pl.BlockSpec(memory_space=pltpu.HBM)
     return pl.pallas_call(
         project_kernel,
         out_shape=(part,) * 4,
-        grid_spec=pltpu.PrefetchScalarGridSpec(
-            num_scalar_prefetch=1,
-            grid=(4 * turns,),
-            in_specs=[
-                pl.BlockSpec(
-                    (quarter // turns, depth),
-                    lambda i, chan: ((chan[0] ^ (3 - i // turns)) * turns + i % turns, 0),
-                ),
-                pl.BlockSpec((depth, width), lambda i, chan: (0, 0)),
-            ],
-            out_specs=(pl.BlockSpec((quarter, width), lambda i, chan: (0, 0)),) * 4,
-        ),
-        compiler_params=memory(60),
+        in_specs=[pl.BlockSpec(memory_space=pltpu.SMEM), hbm, hbm],
+        out_specs=(vmem,) * 4,
+        scratch_shapes=[
+            pltpu.VMEM(spectra.shape, jnp.bfloat16),
+            pltpu.VMEM((depth, width), jnp.bfloat16),
+            pltpu.SemaphoreType.DMA((9,)),
+        ],
+        compiler_params=memory(52),
         cost_estimate=pl.CostEstimate(
             flops=8 * quarter * depth * width,
             bytes_accessed=8 * quarter * depth + 2 * depth * width + 8 * quarter * width,
@@ -93,64 +96,48 @@
     )(chan.reshape(1), spectra, weight)
 
 
-def turn_kernel(chan, spectra, out):
-    out[...] = spectra[...].T
+def turn_kernel(chan, spectra, *outs):
+    rows = spectra.shape[0] // 4
+    for turn in range(4):
+        first = pl.multiple_of((chan[0] ^ turn) * rows, rows)
+        side = turn % 2
+        outs[turn // 2][:, side * rows : (side + 1) * rows] = spectra[pl.ds(first, rows), :].T
 
 
 def turned(spectra, chan):
     rows, depth = spectra.shape[0] // 4, spectra.shape[1]
+    vmem = pl.BlockSpec(memory_space=pltpu.VMEM)
     return pl.pallas_call(
         turn_kernel,
-        out_shape=jax.ShapeDtypeStruct((depth, 2 * rows), jnp.bfloat16),
-        grid_spec=pltpu.PrefetchScalarGridSpec(
-            num_scalar_prefetch=1,
-            grid=(2,),
-            in_specs=[pl.BlockSpec((rows, depth), lambda i, chan: (chan[0] ^ (2 + i), 0))],
-            out_specs=pl.BlockSpec((depth, rows), lambda i, chan: (0, i)),
-        ),
+        out_shape=(jax.ShapeDtypeStruct((depth, 2 * rows), jnp.bfloat16),) * 2,
+        in_specs=[pl.BlockSpec(memory_space=pltpu.SMEM), vmem],
+        out_specs=(vmem,) * 2,
         compiler_params=memory(16),
         name="turned",
     )(chan.reshape(1), spectra)
 
 
-def early_kernel(chan, spectra, first, second, total):
-    step = pl.program_id(0)
-
-    def product(rows):
-        return lax.dot_general(
-            spectra[...], rows[...], (((0,), (0,)), ((), ())), preferred_element_type=jnp.float32
-        )
-
-    @pl.when(step == 0)
-    def _():
-        total[...] = product(first)
-
-    @pl.when(step == 1)
-    def _():
-        total[...] += product(second)
-
-
-def early_product(spectra, chan, first, second):
-    depth = spectra.shape[1]
-    rows, width = first.shape
-    whole = pl.BlockSpec((rows, width), lambda i, chan: (0, 0))
+def early_kernel(flipped, first, second, total):
+    rows = jnp.concatenate([first[...], second[...]], axis=0)
+    total[...] = jnp.dot(flipped[...], rows, preferred_element_type=jnp.float32)
+
+
+def early_product(flipped, first, second):
+    depth, width = flipped.shape[0], first.shape[1]
+    vmem = pl.BlockSpec(memory_space=pltpu.VMEM)
     return pl.pallas_call(
         early_kernel,
         out_shape=jax.ShapeDtypeStruct((depth, width), jnp.float32),
-        grid_spec=pltpu.PrefetchScalarGridSpec(
-            num_scalar_prefetch=1,
-            grid=(2,),
-            in_specs=[pl.BlockSpec((rows, depth), lambda i, chan: (chan[0] ^ i, 0)), whole, whole],
-            out_specs=pl.BlockSpec((depth, width), lambda i, chan: (0, 0)),
-        ),
+        in_specs=[vmem] * 3,
+        out_specs=vmem,
         compiler_params=memory(16),
         cost_estimate=pl.CostEstimate(
-            flops=4 * rows * depth * width,
-            bytes_accessed=4 * rows * depth + 4 * depth * width,
+            flops=2 * flipped.shape[0] * flipped.shape[1] * width,
+            bytes_accessed=2 * flipped.shape[0] * flipped.shape[1] + 4 * depth * width,
             transcendentals=0,
         ),
         name="early_product",
-    )(chan.reshape(1), spectra, first, second)
+    )(flipped, first, second)
 
 
 def late_kernel(where, flipped, before, crossed, passed, across, skipped, keep, send):
@@ -183,8 +170,10 @@
 
 
 def pixel_kernel(count, start, places, *refs):
-    *lists, cotangent, above, below, mixing, out, table, scale, sums = refs
+    *lists, cotangent, above, below, mixing, out, table, scale, sums, near, sem = refs
     tile_rows, half = cotangent.shape[0], table.shape[1]
+    copy = pltpu.make_async_copy(places, near, sem)
+    copy.start()
 
     def fill(first, values):
         values = values.astype(jnp.float32)
@@ -201,18 +190,22 @@
     for side in range(2):
         scale[pl.ds(side, NEIGH, stride=2), :] = mixing[:, side * half : (side + 1) * half]
     scales = [scale[2 * k : 2 * k + 2, :] for k in range(NEIGH)]
-
-    group = 8
+    copy.wait()
+
+    group = 16
     for index, wanted in enumerate(lists):
 
         def body(turn, carry, index=index, wanted=wanted):
             base = turn * group
             for n in range(group):
                 pixel = wanted[start[0] + base + n]
-                total = table[pl.ds(2 * (pixel + HALO), 2), :]
+                terms = [table[pl.ds(2 * (pixel + HALO), 2), :]]
                 for k in range(NEIGH):
-                    total = total + table[pl.ds(places[k, pixel], 2), :] * scales[k]
-                sums[pl.ds(2 * (index * count + base + n), 2), :] = total
+                    terms.append(table[pl.ds(near[k, pixel], 2), :] * scales[k])
+                while len(terms) > 1:
+                    pairs = [x + y for x, y in zip(terms[::2], terms[1::2])]
+                    terms = pairs + terms[len(terms) // 2 * 2 :]
+                sums[pl.ds(2 * (index * count + base + n), 2), :] = terms[0]
             return carry
 
         lax.fori_loop(0, count // group, body, 0)
@@ -231,12 +224,14 @@
     return pl.pallas_call(
         functools.partial(pixel_kernel, count),
         out_shape=jax.ShapeDtypeStruct((rows, width), jnp.bfloat16),
-        in_specs=[smem] * (2 + len(lists)) + [vmem] * 4,
+        in_specs=[smem, pl.BlockSpec(memory_space=pl.ANY)] + [smem] * len(lists) + [vmem] * 4,
         out_specs=vmem,
         scratch_shapes=[
             pltpu.VMEM((2 * (tile_rows + 2 * HALO), width // 2), jnp.float32),
             pltpu.VMEM((2 * NEIGH, width // 2), jnp.float32),
             pltpu.VMEM((2 * rows, width // 2), jnp.float32),
+            pltpu.SMEM(adjoint.shape, jnp.int32),
+            pltpu.SemaphoreType.DMA,
         ],
         compiler_params=memory(24),
         cost_estimate=pl.CostEstimate(
@@ -344,6 +339,7 @@
         )
         answers = jnp.take(answers.reshape(tile_count * capacity, -1), slot_index, axis=0)
         mine = answers
+    part0, flipped = lax.optimization_barrier((part0, turned(spectra, chan)))
     grads = pre_gradient(part0, near, far, tile_ids, tile, weights, mine, answers)
 
     beside = swap(grads, "chan", 1)
@@ -351,10 +347,9 @@
     passed = lax.ppermute(across, "chan", [(1, 0), (2, 3)])
     crossed = lax.ppermute(beside, "chan", middle)
     skipped = lax.ppermute(beside, "chan", [(2, 0), (1, 3)])
-    flipped = turned(spectra, chan)
     core = lax.axis_index("obs") & 1
-    early = early_product(spectra, chan, grads, beside)
-    keep, send = late_product(chan, core, flipped, early, crossed, passed, across, skipped)
+    early = early_product(flipped[0], grads, beside)
+    keep, send = late_product(chan, core, flipped[1], early, crossed, passed, across, skipped)
     if lax.axis_size("obs") == 4 and tile_count == 2:
         return sum_over_panels(core, keep, send)
     return lax.psum(collect(core, keep, send), ("obs", "pix"))

time: 92.8 us -> 93.9 us (1.012)
  the two profiles are of different devices: /device:TPU:11 before, /device:TPU:0 now
where the time goes in v5:
time: 93.9 us; the launch traced here: 92.9 us
  starting transfers between devices  27.3 us (29%)
  Pallas kernels  26.4 us (28%)
  waiting for transfers between devices  22.9 us (24%)
  local copies, waits for them, and re-layouts  13.2 us (14%)
  other arithmetic  2.93 us (3%)
    pallas_call x1, Pallas kernels, pixel_rows(): pl.pallas_call(functools.partial(pixel_kernel, count), out_shape=jax.Shap...  14.7 us
    unnamed x27, local copies, waits for them, and re-layouts  11.5 us
    ppermute x2, waiting for transfers between devices, sum_over_panels(): lax.ppermute(value.astype(jnp.bfloat16), both, [(i, i ^ order[i >> 1 & 1]...  10.6 us
    ppermute x6, starting transfers between devices, swap(): return lax.ppermute(value, axis, [(i, i ^ bit) for i in range(size)])  8.15 us
    ppermute x6, waiting for transfers between devices, swap(): return lax.ppermute(value, axis, [(i, i ^ bit) for i in range(size)])  6.66 us
    ppermute x1, waiting for transfers between devices, shards(): passed = lax.ppermute(across, 'chan', [(1, 0), (2, 3)])  5.57 us
    pallas_call x1, Pallas kernels, project(): pl.pallas_call(project_kernel, out_shape=(part,) * 4, in_specs=[pl.BlockS...  5.16 us
    ppermute x1, starting transfers between devices, shards(): outer2 = lax.ppermute(part2, 'chan', [(0, 1), (3, 2)])  4.93 us
  transfers between devices with their start and end apart: 17, of which 6 were waited for; matrix products, arithmetic and copies ran while one was open for 5% of the time, Pallas kernels for 18%

profile of v5, /device:TPU:0, one launch (start us, length us, event | category | flops | bytes accessed | tf_op | source)
XLA Modules:
  0.0 92.9 jit_solution(258952143887492929)
XLA Ops:
  0.0 1.1 %copy-done.4 = bf16[1152,256]{1,0:T(8,128)(2,1)S(1)} copy-done((bf16[1152,256]{1,0:T(8,128)(2,1)S(1)}, bf16[1152,256]{1,0:T(8,128)(2,1)}, u32[]{:S(2)}) %copy-start.4) | copy-done | bytes 589848
  1.1 5.2 %project.1 = (bf16[512,256]{1,0:T(8,128)(2,1)S(1)}, bf16[512,256]{1,0:T(8,128)(2,1)S(1)}, bf16[512,256]{1,0:T(8,128)(2,1)S(1)}, bf16[512,256]{1,0:T(8,128)(2,1)S(1)}) custom-call(s32[1]{0:T(128)} %bitcast.1.chan, bf16[2048,1152]{1,0:T(8,128)(2,1)} %spectra.3, bf16[1152,256]{1,0:T(8,128)(2,1)S(1)} %copy-done.4), custom_call_target="tpu_custom_call" | custom-call | flops 1207959552 | bytes 6356992 | tf_op jit(solution)/shard_map/project/pallas_call | solution.py:79
  7.0 4.9 %collective-permute-start.3 = (bf16[512,256]{1,0:T(8,128)(2,1)S(1)}, bf16[512,256]{1,0:T(8,128)(2,1)S(1)}, u32[]{:S(2)}, u32[]{:S(2)}) collective-permute-start(bf16[512,256]{1,0:T(8,128)(2,1)S(1)} %get-tuple-element.23), channel_id=1, source_target_pairs={{0,1},{3,2},{4,5},{7,6},{8,9},{11,10},{12,13},{15,14},{16,17},{19,... | collective-permute-start | bytes 786440 | tf_op jit(solution)/shard_map/ppermute | solution.py:311
  12.6 1.6 %collective-permute-start.5 = (s32[2048]{0:T(1024)S(1)}, s32[2048]{0:T(1024)S(1)}, u32[]{:S(2)}, u32[]{:S(2)}) collective-permute-start(s32[2048]{0:T(1024)S(1)} %copy-done.10), channel_id=1, source_target_pairs={{0,4},{4,0},{1,5},{5,1},{2,6},{6,2},{3,7},{7,3},{8,12},{12,8},{9,1... | collective-permute-start | bytes 24584 | tf_op jit(solution)/shard_map/ppermute | solution.py:44
  14.2 0.9 slice_select_fusion
  15.6 4.0 %collective-permute-start.1 = (bf16[512,256]{1,0:T(8,128)(2,1)S(1)}, bf16[512,256]{1,0:T(8,128)(2,1)S(1)}, u32[]{:S(2)}, u32[]{:S(2)}) collective-permute-start(bf16[512,256]{1,0:T(8,128)(2,1)S(1)} %get-tuple-element.24), channel_id=1, source_target_pairs={{0,2},{3,1},{4,6},{7,5},{8,10},{11,9},{12,14},{15,13},{16,18},{19,... | collective-permute-start | bytes 786440 | tf_op jit(solution)/shard_map/ppermute | solution.py:313
  19.7 1.6 %copy-done.9 = bf16[4096,256]{1,0:T(8,128)(2,1)S(1)} copy-done((bf16[4096,256]{1,0:T(8,128)(2,1)S(1)}, bf16[4096,256]{1,0:T(8,128)(2,1)}, u32[]{:S(2)}) %copy-start.9) | copy-done | bytes 2097176
  21.3 14.7 %pixel_rows.1 = bf16[1024,256]{1,0:T(8,128)(2,1)S(1)} custom-call(s32[1]{0:T(128)} %bitcast.4.start, s32[8,4096]{1,0:T(8,128)S(1)} %subtract_multiply_fusion.places, s32[2048]{0:T(1024)S(1)} %copy-done.10, s32[2048]{0:T(1024)S(1)} %collective-permute-done.5.refs_1_, bf16[4096,256]{1,0:T(8,128)(2,1)S(1)} %copy-done.9, ...), custom_call_target="tpu_custom_call" | custom-call | flops 4294967296 | bytes 4194304 | tf_op jit(solution)/shard_map/pixel_rows/pallas_call | solution.py:224
  36.8 1.5 %collective-permute-start.7 = (bf16[512,256]{1,0:T(8,128)(2,1)}, bf16[512,256]{1,0:T(8,128)(2,1)S(1)}, u32[]{:S(2)}, u32[]{:S(2)}) collective-permute-start(bf16[512,256]{1,0:T(8,128)(2,1)} %get-tuple-element.27), channel_id=1, source_target_pairs={{0,4},{4,0},{1,5},{5,1},{2,6},{6,2},{3,7},{7,3},{8,12},{12,8},{9,1... | collective-permute-start | bytes 786440 | tf_op jit(solution)/shard_map/ppermute | solution.py:44
  39.1 1.4 %collective-permute-start.4 = (bf16[512,256]{1,0:T(8,128)(2,1)}, bf16[512,256]{1,0:T(8,128)(2,1)}, u32[]{:S(2)}, u32[]{:S(2)}) collective-permute-start(bf16[512,256]{1,0:T(8,128)(2,1)} %add_convert_fusion), channel_id=1, source_target_pairs={{1,2},{2,1},{5,6},{6,5},{9,10},{10,9},{13,14},{14,13},{17,18},{18,... | collective-permute-start | bytes 786440 | tf_op jit(solution)/shard_map/ppermute | solution.py:318
  41.3 1.9 %collective-permute-start.2 = (bf16[512,256]{1,0:T(8,128)(2,1)}, bf16[512,256]{1,0:T(8,128)(2,1)}, u32[]{:S(2)}, u32[]{:S(2)}) collective-permute-start(bf16[512,256]{1,0:T(8,128)(2,1)} %add_convert_fusion.1), channel_id=1, source_target_pairs={{0,1},{1,0},{2,3},{3,2},{4,5},{5,4},{6,7},{7,6},{8,9},{9,8},{10,11... | collective-permute-start | bytes 786440 | tf_op jit(solution)/shard_map/ppermute | solution.py:44
  43.1 2.3 %copy-done.1 = bf16[2048,1152]{1,0:T(8,128)(2,1)S(1)} copy-done((bf16[2048,1152]{1,0:T(8,128)(2,1)S(1)}, bf16[2048,1152]{1,0:T(8,128)(2,1)}, u32[]{:S(2)}) %copy-start.1) | copy-done | bytes 4718616
  45.5 1.4 %turned.1 = (bf16[1152,1024]{1,0:T(8,128)(2,1)S(1)}, bf16[1152,1024]{1,0:T(8,128)(2,1)S(1)}) custom-call(s32[1]{0:T(128)} %bitcast.1.chan, bf16[2048,1152]{1,0:T(8,128)(2,1)S(1)} %copy-done.1), custom_call_target="tpu_custom_call" | custom-call | tf_op jit(solution)/shard_map/turned/pallas_call | solution.py:110
  46.8 1.4 %copy-done.2 = bf16[1152,1024]{1,0:T(8,128)(2,1)} copy-done((bf16[1152,1024]{1,0:T(8,128)(2,1)}, bf16[1152,1024]{1,0:T(8,128)(2,1)S(1)}, u32[]{:S(2)}) %copy-start.2) | copy-done | bytes 2359320
  50.1 0.9 %copy-done.6 = bf16[512,256]{1,0:T(8,128)(2,1)S(1)} copy-done((bf16[512,256]{1,0:T(8,128)(2,1)S(1)}, bf16[512,256]{1,0:T(8,128)(2,1)}, u32[]{:S(2)}) %copy-start.6) | copy-done | bytes 262168
  51.0 0.9 %copy-done.8 = bf16[512,256]{1,0:T(8,128)(2,1)S(1)} copy-done((bf16[512,256]{1,0:T(8,128)(2,1)S(1)}, bf16[512,256]{1,0:T(8,128)(2,1)}, u32[]{:S(2)}) %copy-start.8) | copy-done | bytes 262168
  52.0 1.4 %pre_gradient.1.first = bf16[512,256]{1,0:T(8,128)(2,1)S(1)} custom-call(bf16[512,256]{1,0:T(8,128)(2,1)S(1)} %copy-done.6, bf16[512,256]{1,0:T(8,128)(2,1)} %collective-permute-done.2.near, bf16[512,256]{1,0:T(8,128)(2,1)} %collective-permute-done.4.far, s32[512,1]{1,0:T(8,128)S(1)} %copy.12.tiles, s32[1]{0:T(128)} %bitcast.2.tile, ...), custom_call_target="tpu_custom_call" | custom-call | tf_op jit(solution)/shard_map/pre_gradient/pallas_call | solution.py:259
  54.0 3.0 %collective-permute-start.8 = (bf16[512,256]{1,0:T(8,128)(2,1)S(1)}, bf16[512,256]{1,0:T(8,128)(2,1)S(1)}, u32[]{:S(2)}, u32[]{:S(2)}) collective-permute-start(bf16[512,256]{1,0:T(8,128)(2,1)S(1)} %pre_gradient.1.first), channel_id=1, source_target_pairs={{0,1},{1,0},{2,3},{3,2},{4,5},{5,4},{6,7},{7,6},{8,9},{9,8},{10,11... | collective-permute-start | bytes 786440 | tf_op jit(solution)/shard_map/ppermute | solution.py:44
  57.1 1.3 %collective-permute-start.11 = (bf16[512,256]{1,0:T(8,128)(2,1)S(1)}, bf16[512,256]{1,0:T(8,128)(2,1)S(1)}, u32[]{:S(2)}, u32[]{:S(2)}) collective-permute-start(bf16[512,256]{1,0:T(8,128)(2,1)S(1)} %collective-permute-done.10.across), channel_id=1, source_target_pairs={{1,0},{2,3},{5,4},{6,7},{9,8},{10,11},{13,12},{14,15},{17,16},{18,... | collective-permute-start | bytes 786440 | tf_op jit(solution)/shard_map/ppermute | solution.py:347
  58.4 3.5 %collective-permute-done.8.second = bf16[512,256]{1,0:T(8,128)(2,1)S(1)} collective-permute-done((bf16[512,256]{1,0:T(8,128)(2,1)S(1)}, bf16[512,256]{1,0:T(8,128)(2,1)S(1)}, u32[]{:S(2)}, u32[]{:S(2)}) %collective-permute-start.8) | collective-permute-done | bytes 262176 | tf_op jit(solution)/shard_map/ppermute | solution.py:44
  61.9 1.3 %collective-permute-start.12 = (bf16[512,256]{1,0:T(8,128)(2,1)S(1)}, bf16[512,256]{1,0:T(8,128)(2,1)}, u32[]{:S(2)}, u32[]{:S(2)}) collective-permute-start(bf16[512,256]{1,0:T(8,128)(2,1)S(1)} %collective-permute-done.8.second), channel_id=1, source_target_pairs={{2,0},{1,3},{6,4},{5,7},{10,8},{9,11},{14,12},{13,15},{18,16},{17,... | collective-permute-start | bytes 786440 | tf_op jit(solution)/shard_map/ppermute | solution.py:349
  63.2 1.4 %collective-permute-start.9 = (bf16[512,256]{1,0:T(8,128)(2,1)S(1)}, bf16[512,256]{1,0:T(8,128)(2,1)}, u32[]{:S(2)}, u32[]{:S(2)}) collective-permute-start(bf16[512,256]{1,0:T(8,128)(2,1)S(1)} %collective-permute-done.8.second), channel_id=1, source_target_pairs={{1,2},{2,1},{5,6},{6,5},{9,10},{10,9},{13,14},{14,13},{17,18},{18,... | collective-permute-start | bytes 786440 | tf_op jit(solution)/shard_map/ppermute | solution.py:348
  64.7 1.7 %copy-done.3 = bf16[1152,1024]{1,0:T(8,128)(2,1)S(1)} copy-done((bf16[1152,1024]{1,0:T(8,128)(2,1)S(1)}, bf16[1152,1024]{1,0:T(8,128)(2,1)}, u32[]{:S(2)}) %copy-start.3) | copy-done | bytes 2359320
  67.1 5.6 %collective-permute-done.11.passed = bf16[512,256]{1,0:T(8,128)(2,1)S(1)} collective-permute-done((bf16[512,256]{1,0:T(8,128)(2,1)S(1)}, bf16[512,256]{1,0:T(8,128)(2,1)S(1)}, u32[]{:S(2)}, u32[]{:S(2)}) %collective-permute-start.11) | collective-permute-done | bytes 262176 | tf_op jit(solution)/shard_map/ppermute | solution.py:347
  72.7 1.8 %late_product.1 = (f32[576,256]{1,0:T(8,128)S(1)}, bf16[576,256]{1,0:T(8,128)(2,1)S(1)}) custom-call(s32[2]{0:T(128)S(1)} %pad_add_fusion.where, bf16[1152,1024]{1,0:T(8,128)(2,1)S(1)} %get-tuple-element.19.flipped, f32[1152,256]{1,0:T(8,128)S(1)} %early_product.1.before, bf16[512,256]{1,0:T(8,128)(2,1)} %collective-permute-done.9.crossed, ...), custom_call_target="tpu_custom_call" | custom-call | tf_op jit(solution)/shard_map/late_product/pallas_call | solution.py:159
  74.6 1.6 %collective-permute-done.13 = bf16[576,256]{1,0:T(8,128)(2,1)S(1)} collective-permute-done((bf16[576,256]{1,0:T(8,128)(2,1)S(1)}, bf16[576,256]{1,0:T(8,128)(2,1)S(1)}, u32[]{:S(2)}, u32[]{:S(2)}) %collective-permute-start.13) | collective-permute-done | bytes 294944 | tf_op jit(solution)/shard_map/ppermute | solution.py:44
  76.3 1.5 %collective-permute-start.14 = (bf16[576,256]{1,0:T(8,128)(2,1)S(1)}, bf16[576,256]{1,0:T(8,128)(2,1)S(1)}, u32[]{:S(2)}, u32[]{:S(2)}) collective-permute-start(bf16[576,256]{1,0:T(8,128)(2,1)S(1)} %fusion), channel_id=1, source_target_pairs={{0,16},{4,20},{8,12},{12,8},{16,0},{20,4},{24,28},{28,24},{1,17},{... | collective-permute-start | bytes 884744 | tf_op jit(solution)/shard_map/ppermute | solution.py:293
  77.8 5.2 %collective-permute-done.14 = bf16[576,256]{1,0:T(8,128)(2,1)S(1)} collective-permute-done((bf16[576,256]{1,0:T(8,128)(2,1)S(1)}, bf16[576,256]{1,0:T(8,128)(2,1)S(1)}, u32[]{:S(2)}, u32[]{:S(2)}) %collective-permute-start.14) | collective-permute-done | bytes 294944 | tf_op jit(solution)/shard_map/ppermute | solution.py:293
  83.2 1.4 %collective-permute-start.15 = (bf16[576,256]{1,0:T(8,128)(2,1)S(1)}, bf16[576,256]{1,0:T(8,128)(2,1)S(1)}, u32[]{:S(2)}, u32[]{:S(2)}) collective-permute-start(bf16[576,256]{1,0:T(8,128)(2,1)S(1)} %fusion.1), channel_id=1, source_target_pairs={{0,4},{4,0},{8,24},{12,28},{16,20},{20,16},{24,8},{28,12},{1,5},{5... | collective-permute-start | bytes 884744 | tf_op jit(solution)/shard_map/ppermute | solution.py:293
  84.6 5.4 %collective-permute-done.15 = bf16[576,256]{1,0:T(8,128)(2,1)S(1)} collective-permute-done((bf16[576,256]{1,0:T(8,128)(2,1)S(1)}, bf16[576,256]{1,0:T(8,128)(2,1)S(1)}, u32[]{:S(2)}, u32[]{:S(2)}) %collective-permute-start.15) | collective-permute-done | bytes 294944 | tf_op jit(solution)/shard_map/ppermute | solution.py:293
  90.2 1.6 %collective-permute-done.16.received = bf16[576,256]{1,0:T(8,128)(2,1)S(1)} collective-permute-done((bf16[576,256]{1,0:T(8,128)(2,1)S(1)}, bf16[576,256]{1,0:T(8,128)(2,1)S(1)}, u32[]{:S(2)}, u32[]{:S(2)}) %collective-permute-start.16) | collective-permute-done | bytes 294944 | tf_op jit(solution)/shard_map/ppermute | solution.py:44
  91.8 1.1 %collect.1 = f32[1152,256]{1,0:T(8,128)} custom-call(s32[1]{0:T(128)} %bitcast.core, bf16[576,256]{1,0:T(8,128)(2,1)S(1)} %reduce-precision_convert_fusion.own, bf16[576,256]{1,0:T(8,128)(2,1)S(1)} %collective-permute-done.16.received), custom_call_target="tpu_custom_call" | custom-call | tf_op jit(solution)/shard_map/collect/pallas_call | solution.py:277
  (48 shorter events, 8.1 us)
Async XLA Ops:
  0.0 49.2 %copy-start = (s32[2048,1]{0,1:T(1,128)S(1)}, s32[2048,1]{0,1:T(1,128)}, u32[]{:S(2)}) copy-start(s32[2048,1]{0,1:T(1,128)} %param.10) | copy-start | bytes 24580
  0.0 1.1 %copy-start.4 = (bf16[1152,256]{1,0:T(8,128)(2,1)S(1)}, bf16[1152,256]{1,0:T(8,128)(2,1)}, u32[]{:S(2)}) copy-start(bf16[1152,256]{1,0:T(8,128)(2,1)} %weight.1) | copy-start | bytes 1769476
  1.1 11.5 %copy-start.10 = (s32[2048]{0:T(1024)S(1)}, s32[2048]{0:T(1024)}, u32[]{:S(2)}) copy-start(s32[2048]{0:T(1024)} %refs_0_.1) | copy-start | bytes 24580
  1.1 18.5 %copy-start.12 = (s32[8,4096]{1,0:T(8,128)S(1)}, s32[8,4096]{1,0:T(8,128)}, u32[]{:S(2)}) copy-start(s32[8,4096]{1,0:T(8,128)} %param.14) | copy-start | bytes 393220
  1.1 18.6 %copy-start.11 = (f32[8,256]{1,0:T(8,128)S(1)}, f32[8,256]{1,0:T(8,128)}, u32[]{:S(2)}) copy-start(f32[8,256]{1,0:T(8,128)} %refs_5_.1) | copy-start | bytes 24580
  6.3 0.7 copy-start.5
  7.0 31.3 %collective-permute-start.3 = (bf16[512,256]{1,0:T(8,128)(2,1)S(1)}, bf16[512,256]{1,0:T(8,128)(2,1)S(1)}, u32[]{:S(2)}, u32[]{:S(2)}) collective-permute-start(bf16[512,256]{1,0:T(8,128)(2,1)S(1)} %get-tuple-element.23), channel_id=1, source_target_pairs={{0,1},{3,2},{4,5},{7,6},{8,9},{11,10},{12,13},{15,14},{16,17},{19,... | collective-permute-start | bytes 786440 | tf_op jit(solution)/shard_map/ppermute | solution.py:311
  11.9 28.6 %collective-permute-start = (bf16[512,256]{1,0:T(8,128)(2,1)S(1)}, bf16[512,256]{1,0:T(8,128)(2,1)S(1)}, u32[]{:S(2)}, u32[]{:S(2)}) collective-permute-start(bf16[512,256]{1,0:T(8,128)(2,1)S(1)} %get-tuple-element.23), channel_id=1, source_target_pairs={{1,2},{2,1},{5,6},{6,5},{9,10},{10,9},{13,14},{14,13},{17,18},{18,... | collective-permute-start | bytes 786440 | tf_op jit(solution)/shard_map/ppermute | solution.py:312
  12.6 7.1 %collective-permute-start.5 = (s32[2048]{0:T(1024)S(1)}, s32[2048]{0:T(1024)S(1)}, u32[]{:S(2)}, u32[]{:S(2)}) collective-permute-start(s32[2048]{0:T(1024)S(1)} %copy-done.10), channel_id=1, source_target_pairs={{0,4},{4,0},{1,5},{5,1},{2,6},{6,2},{3,7},{7,3},{8,12},{12,8},{9,1... | collective-permute-start | bytes 24584 | tf_op jit(solution)/shard_map/ppermute | solution.py:44
  15.1 4.6 %collective-permute-start.6 = (bf16[128,256]{1,0:T(8,128)(2,1)S(1)}, bf16[128,256]{1,0:T(8,128)(2,1)S(1)}, u32[]{:S(2)}, u32[]{:S(2)}) collective-permute-start(bf16[128,256]{1,0:T(8,128)(2,1)S(1)} %slice_select_fusion), channel_id=1, source_target_pairs={{0,4},{4,0},{1,5},{5,1},{2,6},{6,2},{3,7},{7,3},{8,12},{12,8},{9,1... | collective-permute-start | bytes 196616 | tf_op jit(solution)/shard_map/ppermute | solution.py:21
  15.6 24.8 %collective-permute-start.1 = (bf16[512,256]{1,0:T(8,128)(2,1)S(1)}, bf16[512,256]{1,0:T(8,128)(2,1)S(1)}, u32[]{:S(2)}, u32[]{:S(2)}) collective-permute-start(bf16[512,256]{1,0:T(8,128)(2,1)S(1)} %get-tuple-element.24), channel_id=1, source_target_pairs={{0,2},{3,1},{4,6},{7,5},{8,10},{11,9},{12,14},{15,13},{16,18},{19,... | collective-permute-start | bytes 786440 | tf_op jit(solution)/shard_map/ppermute | solution.py:313
  19.7 1.6 %copy-start.9 = (bf16[4096,256]{1,0:T(8,128)(2,1)S(1)}, bf16[4096,256]{1,0:T(8,128)(2,1)}, u32[]{:S(2)}) copy-start(bf16[4096,256]{1,0:T(8,128)(2,1)} %refs_2_.1) | copy-start | bytes 6291460
  36.8 12.6 %collective-permute-start.7 = (bf16[512,256]{1,0:T(8,128)(2,1)}, bf16[512,256]{1,0:T(8,128)(2,1)S(1)}, u32[]{:S(2)}, u32[]{:S(2)}) collective-permute-start(bf16[512,256]{1,0:T(8,128)(2,1)} %get-tuple-element.27), channel_id=1, source_target_pairs={{0,4},{4,0},{1,5},{5,1},{2,6},{6,2},{3,7},{7,3},{8,12},{12,8},{9,1... | collective-permute-start | bytes 786440 | tf_op jit(solution)/shard_map/ppermute | solution.py:44
  39.1 11.0 %collective-permute-start.4 = (bf16[512,256]{1,0:T(8,128)(2,1)}, bf16[512,256]{1,0:T(8,128)(2,1)}, u32[]{:S(2)}, u32[]{:S(2)}) collective-permute-start(bf16[512,256]{1,0:T(8,128)(2,1)} %add_convert_fusion), channel_id=1, source_target_pairs={{1,2},{2,1},{5,6},{6,5},{9,10},{10,9},{13,14},{14,13},{17,18},{18,... | collective-permute-start | bytes 786440 | tf_op jit(solution)/shard_map/ppermute | solution.py:318
  41.3 8.8 %collective-permute-start.2 = (bf16[512,256]{1,0:T(8,128)(2,1)}, bf16[512,256]{1,0:T(8,128)(2,1)}, u32[]{:S(2)}, u32[]{:S(2)}) collective-permute-start(bf16[512,256]{1,0:T(8,128)(2,1)} %add_convert_fusion.1), channel_id=1, source_target_pairs={{0,1},{1,0},{2,3},{3,2},{4,5},{5,4},{6,7},{7,6},{8,9},{9,8},{10,11... | collective-permute-start | bytes 786440 | tf_op jit(solution)/shard_map/ppermute | solution.py:44
  43.1 2.3 %copy-start.1 = (bf16[2048,1152]{1,0:T(8,128)(2,1)S(1)}, bf16[2048,1152]{1,0:T(8,128)(2,1)}, u32[]{:S(2)}) copy-start(bf16[2048,1152]{1,0:T(8,128)(2,1)} %spectra.3) | copy-start | bytes 14155780
  46.8 1.4 %copy-start.2 = (bf16[1152,1024]{1,0:T(8,128)(2,1)}, bf16[1152,1024]{1,0:T(8,128)(2,1)S(1)}, u32[]{:S(2)}) copy-start(bf16[1152,1024]{1,0:T(8,128)(2,1)S(1)} %get-tuple-element.20.flipped) | copy-start | bytes 7077892
  49.4 0.7 copy-start.7
  50.1 1.0 %copy-start.6 = (bf16[512,256]{1,0:T(8,128)(2,1)S(1)}, bf16[512,256]{1,0:T(8,128)(2,1)}, u32[]{:S(2)}) copy-start(bf16[512,256]{1,0:T(8,128)(2,1)} %copy-done.5) | copy-start | bytes 786436
  51.0 0.9 %copy-start.8 = (bf16[512,256]{1,0:T(8,128)(2,1)S(1)}, bf16[512,256]{1,0:T(8,128)(2,1)}, u32[]{:S(2)}) copy-start(bf16[512,256]{1,0:T(8,128)(2,1)} %copy-done.7) | copy-start | bytes 786436
  53.4 3.7 %collective-permute-start.10 = (bf16[512,256]{1,0:T(8,128)(2,1)S(1)}, bf16[512,256]{1,0:T(8,128)(2,1)S(1)}, u32[]{:S(2)}, u32[]{:S(2)}) collective-permute-start(bf16[512,256]{1,0:T(8,128)(2,1)S(1)} %pre_gradient.1.first), channel_id=1, source_target_pairs={{1,2},{2,1},{5,6},{6,5},{9,10},{10,9},{13,14},{14,13},{17,18},{18,... | collective-permute-start | bytes 786440 | tf_op jit(solution)/shard_map/ppermute | solution.py:346
  54.0 7.8 %collective-permute-start.8 = (bf16[512,256]{1,0:T(8,128)(2,1)S(1)}, bf16[512,256]{1,0:T(8,128)(2,1)S(1)}, u32[]{:S(2)}, u32[]{:S(2)}) collective-permute-start(bf16[512,256]{1,0:T(8,128)(2,1)S(1)} %pre_gradient.1.first), channel_id=1, source_target_pairs={{0,1},{1,0},{2,3},{3,2},{4,5},{5,4},{6,7},{7,6},{8,9},{9,8},{10,11... | collective-permute-start | bytes 786440 | tf_op jit(solution)/shard_map/ppermute | solution.py:44
  57.1 15.6 %collective-permute-start.11 = (bf16[512,256]{1,0:T(8,128)(2,1)S(1)}, bf16[512,256]{1,0:T(8,128)(2,1)S(1)}, u32[]{:S(2)}, u32[]{:S(2)}) collective-permute-start(bf16[512,256]{1,0:T(8,128)(2,1)S(1)} %collective-permute-done.10.across), channel_id=1, source_target_pairs={{1,0},{2,3},{5,4},{6,7},{9,8},{10,11},{13,12},{14,15},{17,16},{18,... | collective-permute-start | bytes 786440 | tf_op jit(solution)/shard_map/ppermute | solution.py:347
  61.9 10.8 %collective-permute-start.12 = (bf16[512,256]{1,0:T(8,128)(2,1)S(1)}, bf16[512,256]{1,0:T(8,128)(2,1)}, u32[]{:S(2)}, u32[]{:S(2)}) collective-permute-start(bf16[512,256]{1,0:T(8,128)(2,1)S(1)} %collective-permute-done.8.second), channel_id=1, source_target_pairs={{2,0},{1,3},{6,4},{5,7},{10,8},{9,11},{14,12},{13,15},{18,16},{17,... | collective-permute-start | bytes 786440 | tf_op jit(solution)/shard_map/ppermute | solution.py:349
  63.2 9.5 %collective-permute-start.9 = (bf16[512,256]{1,0:T(8,128)(2,1)S(1)}, bf16[512,256]{1,0:T(8,128)(2,1)}, u32[]{:S(2)}, u32[]{:S(2)}) collective-permute-start(bf16[512,256]{1,0:T(8,128)(2,1)S(1)} %collective-permute-done.8.second), channel_id=1, source_target_pairs={{1,2},{2,1},{5,6},{6,5},{9,10},{10,9},{13,14},{14,13},{17,18},{18,... | collective-permute-start | bytes 786440 | tf_op jit(solution)/shard_map/ppermute | solution.py:348
  64.6 1.7 %copy-start.3 = (bf16[1152,1024]{1,0:T(8,128)(2,1)S(1)}, bf16[1152,1024]{1,0:T(8,128)(2,1)}, u32[]{:S(2)}) copy-start(bf16[1152,1024]{1,0:T(8,128)(2,1)} %copy-done.2) | copy-start | bytes 7077892
  74.5 1.6 %collective-permute-start.13 = (bf16[576,256]{1,0:T(8,128)(2,1)S(1)}, bf16[576,256]{1,0:T(8,128)(2,1)S(1)}, u32[]{:S(2)}, u32[]{:S(2)}) collective-permute-start(bf16[576,256]{1,0:T(8,128)(2,1)S(1)} %get-tuple-element.26), channel_id=1, source_target_pairs={{0,8},{8,0},{16,24},{24,16},{1,9},{9,1},{17,25},{25,17},{2,10},{10... | collective-permute-start | bytes 884744 | tf_op jit(solution)/shard_map/ppermute | solution.py:44
  76.3 6.8 %collective-permute-start.14 = (bf16[576,256]{1,0:T(8,128)(2,1)S(1)}, bf16[576,256]{1,0:T(8,128)(2,1)S(1)}, u32[]{:S(2)}, u32[]{:S(2)}) collective-permute-start(bf16[576,256]{1,0:T(8,128)(2,1)S(1)} %fusion), channel_id=1, source_target_pairs={{0,16},{4,20},{8,12},{12,8},{16,0},{20,4},{24,28},{28,24},{1,17},{... | collective-permute-start | bytes 884744 | tf_op jit(solution)/shard_map/ppermute | solution.py:293
  83.2 6.8 %collective-permute-start.15 = (bf16[576,256]{1,0:T(8,128)(2,1)S(1)}, bf16[576,256]{1,0:T(8,128)(2,1)S(1)}, u32[]{:S(2)}, u32[]{:S(2)}) collective-permute-start(bf16[576,256]{1,0:T(8,128)(2,1)S(1)} %fusion.1), channel_id=1, source_target_pairs={{0,4},{4,0},{8,24},{12,28},{16,20},{20,16},{24,8},{28,12},{1,5},{5... | collective-permute-start | bytes 884744 | tf_op jit(solution)/shard_map/ppermute | solution.py:293
  90.2 1.6 %collective-permute-start.16 = (bf16[576,256]{1,0:T(8,128)(2,1)S(1)}, bf16[576,256]{1,0:T(8,128)(2,1)S(1)}, u32[]{:S(2)}, u32[]{:S(2)}) collective-permute-start(bf16[576,256]{1,0:T(8,128)(2,1)S(1)} %reduce-precision_convert_fusion.own), channel_id=1, source_target_pairs={{0,8},{8,0},{16,24},{24,16},{1,9},{9,1},{17,25},{25,17},{2,10},{10... | collective-permute-start | bytes 884744 | tf_op jit(solution)/shard_map/ppermute | solution.py:44

commit v6 on v5

v6 whole, which is shorter than its diff:
```python
import functools

import jax
import jax.numpy as jnp
from jax import lax
from jax.experimental import pallas as pl
from jax.experimental.pallas import tpu as pltpu
from jax.sharding import PartitionSpec as P

NEIGH = 8
HALO = 128
MIB = 1024 * 1024


def edges(value, axis, width):
    size, length = lax.axis_size(axis), value.shape[0]
    last = lax.slice_in_dim(value, length - width, length, axis=0)
    first = lax.slice_in_dim(value, 0, width, axis=0)
    if size == 2:
        index = lax.axis_index(axis)
        other = lax.ppermute(jnp.where(index == 0, last, first), axis, [(0, 1), (1, 0)])
        return other, other
    up = [(i, i + 1) for i in range(size - 1)]
    return lax.ppermute(last, axis, up), lax.ppermute(first, axis, [(j, i) for i, j in up])


def requests(tile_ids, local_ids, capacity):
    tile_count = lax.axis_size("pix")
    onehot = (tile_ids[:, None] == jnp.arange(tile_count, dtype=jnp.int32)[None, :]).astype(
        jnp.int32
    )
    place_rank = jnp.sum((jnp.cumsum(onehot, axis=0) - 1) * onehot, axis=1)
    slot_index = tile_ids * capacity + place_rank
    outgoing = jnp.full((tile_count * capacity,), 0, jnp.int32).at[slot_index].set(local_ids)
    outgoing = outgoing.reshape(tile_count, capacity)
    requested = lax.all_to_all(outgoing, "pix", split_axis=0, concat_axis=0, tiled=True)
    return slot_index, requested.reshape(-1)


def swap(value, axis, bit):
    size = 1
    for name in (axis,) if isinstance(axis, str) else axis:
        size *= lax.axis_size(name)
    return lax.ppermute(value, axis, [(i, i ^ bit) for i in range(size)])


def memory(mib):
    return pltpu.CompilerParams(vmem_limit_bytes=mib * MIB)


def project_kernel(quarters, spectra, weight, out):
    rows = out.shape[0] // 2
    for turn in range(2):
        first = pl.multiple_of(quarters[turn] * rows, rows)
        result = jnp.dot(
            spectra[pl.ds(first, rows), :], weight[...], preferred_element_type=jnp.float32
        )
        out[turn * rows : (turn + 1) * rows, :] = result.astype(out.dtype)


def project(spectra, weight, chan, bits):
    depth, width = weight.shape
    rows = spectra.shape[0] // 2
    vmem = pl.BlockSpec(memory_space=pltpu.VMEM)

    def kernel(chan, spectra, weight, out):
        project_kernel((chan[0] ^ bits, chan[0] ^ 2 ^ bits), spectra, weight, out)

    return pl.pallas_call(
        kernel,
        out_shape=jax.ShapeDtypeStruct((rows, width), jnp.bfloat16),
        in_specs=[pl.BlockSpec(memory_space=pltpu.SMEM), vmem, vmem],
        out_specs=vmem,
        compiler_params=memory(16),
        cost_estimate=pl.CostEstimate(
            flops=2 * rows * depth * width,
            bytes_accessed=2 * rows * depth + 2 * depth * width + 2 * rows * width,
            transcendentals=0,
        ),
        name="project",
    )(chan.reshape(1), spectra, weight)


def turn_kernel(chan, spectra, *outs):
    rows = spectra.shape[0] // 4
    for turn in range(4):
        first = pl.multiple_of((chan[0] ^ turn) * rows, rows)
        side = turn % 2
        outs[turn // 2][:, side * rows : (side + 1) * rows] = spectra[pl.ds(first, rows), :].T


def turned(spectra, chan):
    rows, depth = spectra.shape[0] // 4, spectra.shape[1]
    vmem = pl.BlockSpec(memory_space=pltpu.VMEM)
    return pl.pallas_call(
        turn_kernel,
        out_shape=(jax.ShapeDtypeStruct((depth, 2 * rows), jnp.bfloat16),) * 2,
        in_specs=[pl.BlockSpec(memory_space=pltpu.SMEM), vmem],
        out_specs=(vmem,) * 2,
        compiler_params=memory(16),
        name="turned",
    )(chan.reshape(1), spectra)


def early_kernel(flipped, first, second, total):
    rows = jnp.concatenate([first[...], second[...]], axis=0)
    total[...] = jnp.dot(flipped[...], rows, preferred_element_type=jnp.float32)


def early_product(flipped, first, second):
    depth, width = flipped.shape[0], first.shape[1]
    vmem = pl.BlockSpec(memory_space=pltpu.VMEM)
    return pl.pallas_call(
        early_kernel,
        out_shape=jax.ShapeDtypeStruct((depth, width), jnp.float32),
        in_specs=[vmem] * 3,
        out_specs=vmem,
        compiler_params=memory(16),
        cost_estimate=pl.CostEstimate(
            flops=2 * flipped.shape[0] * flipped.shape[1] * width,
            bytes_accessed=2 * flipped.shape[0] * flipped.shape[1] + 4 * depth * width,
            transcendentals=0,
        ),
        name="early_product",
    )(flipped, first, second)


def late_kernel(other, where, flipped, before, crossed, passed, across, skipped, *outs):
    chan, core = where[0], where[1]
    inner = (chan == 1) | (chan == 2)
    second = jnp.where(inner, crossed[...], passed[...])
    third = jnp.where(inner, across[...], skipped[...])
    rows = jnp.concatenate([second, third], axis=0)
    size = outs[0].shape[0]
    for index, out in enumerate(outs):
        first = (core ^ other) * size * len(outs) + index * size
        here = pl.ds(pl.multiple_of(first, size), size)
        product = jnp.dot(flipped[here, :], rows, preferred_element_type=jnp.float32)
        out[...] = (before[here, :] + product).astype(out.dtype)


def late_product(other, where, flipped, before, crossed, passed, across, skipped):
    size, width = before.shape[0] // 4, before.shape[1]
    spec = pl.BlockSpec(memory_space=pltpu.VMEM)
    part = jax.ShapeDtypeStruct((size, width), jnp.bfloat16 if other else jnp.float32)
    return pl.pallas_call(
        functools.partial(late_kernel, other),
        out_shape=(part, part),
        in_specs=[pl.BlockSpec(memory_space=pltpu.SMEM)] + [spec] * 6,
        out_specs=(spec, spec),
        compiler_params=memory(16),
        cost_estimate=pl.CostEstimate(
            flops=4 * size * flipped.shape[1] * width,
            bytes_accessed=4 * size * flipped.shape[1] + 16 * size * width,
            transcendentals=0,
        ),
        name="late_product",
    )(where, flipped, before, crossed, passed, across, skipped)


def pixel_kernel(count, start, places, *refs):
    *lists, cotangent, above, below, mixing, out = refs[:-6]
    left, right, left_sums, right_sums, near, sem = refs[-6:]
    sides = ((left, left_sums), (right, right_sums))
    tile_rows, half = cotangent.shape[0], left.shape[1]
    copy = pltpu.make_async_copy(places, near, sem)
    copy.start()

    def fill(first, values):
        values = values.astype(jnp.float32)
        for side, (table, _) in enumerate(sides):
            table[first : first + values.shape[0], :] = values[:, side * half : (side + 1) * half]

    fill(0, above[...])
    fill(HALO + tile_rows, below[...])
    chunk = 256
    for first in range(0, tile_rows, chunk):
        fill(HALO + first, cotangent[first : first + chunk, :])
    scales = [
        [mixing[k : k + 1, side * half : (side + 1) * half] for k in range(NEIGH)]
        for side in range(2)
    ]
    copy.wait()

    group = 16
    for index, wanted in enumerate(lists):

        def body(turn, carry, index=index, wanted=wanted):
            base = turn * group
            for n in range(group):
                pixel = wanted[start[0] + base + n]
                spots = [near[k, pixel] for k in range(NEIGH)]
                for (table, sums), scale in zip(sides, scales):
                    terms = [table[pl.ds(pixel + HALO, 1), :]]
                    terms += [table[pl.ds(s, 1), :] * x for s, x in zip(spots, scale)]
                    while len(terms) > 1:
                        pairs = [x + y for x, y in zip(terms[::2], terms[1::2])]
                        terms = pairs + terms[len(terms) // 2 * 2 :]
                    sums[pl.ds(index * count + base + n, 1), :] = terms[0]
            return carry

        lax.fori_loop(0, count // group, body, 0)
    for side, (_, sums) in enumerate(sides):
        out[:, side * half : (side + 1) * half] = sums[...].astype(out.dtype)


def pixel_rows(cotangent, above, below, adjoint, mixing, anchor, lists, start, count):
    tile_rows, width = cotangent.shape
    rows = count * len(lists)
    smem = pl.BlockSpec(memory_space=pltpu.SMEM)
    vmem = pl.BlockSpec(memory_space=pltpu.VMEM)
    return pl.pallas_call(
        functools.partial(pixel_kernel, count),
        out_shape=jax.ShapeDtypeStruct((rows, width), jnp.bfloat16),
        in_specs=[smem, pl.BlockSpec(memory_space=pl.ANY)] + [smem] * len(lists) + [vmem] * 4,
        out_specs=vmem,
        scratch_shapes=[
            pltpu.VMEM((tile_rows + 2 * HALO, width // 2), jnp.float32),
            pltpu.VMEM((tile_rows + 2 * HALO, width // 2), jnp.float32),
            pltpu.VMEM((rows, width // 2), jnp.float32),
            pltpu.VMEM((rows, width // 2), jnp.float32),
            pltpu.SMEM(adjoint.shape, jnp.int32),
            pltpu.SemaphoreType.DMA,
        ],
        compiler_params=memory(16),
        cost_estimate=pl.CostEstimate(
            flops=6 * NEIGH * tile_rows * 256 * width,
            bytes_accessed=4 * tile_rows * width,
            transcendentals=0,
        ),
        name="pixel_rows",
    )(start.reshape(1), adjoint - anchor, *lists, cotangent, above, below, mixing)


def gradient_kernel(keep, near, far, tiles, tile, weights, mine, answers, out):
    rows = out.shape[0]
    pre = keep[:rows, :].astype(jnp.float32) + near[:rows, :].astype(jnp.float32)
    pre = pre + far[...].astype(jnp.float32)
    sigma = jax.nn.sigmoid(pre)
    deriv = sigma * (1.0 + pre * (1.0 - sigma))
    fetched = jnp.where(
        tiles[...] == tile[0], mine[:rows, :].astype(jnp.float32), answers[...].astype(jnp.float32)
    )
    out[...] = (weights[...] * deriv * fetched).astype(out.dtype)


def pre_gradient(keep, near, far, tiles, tile, weights, mine, answers):
    spec = pl.BlockSpec(memory_space=pltpu.VMEM)
    return pl.pallas_call(
        gradient_kernel,
        out_shape=jax.ShapeDtypeStruct(far.shape, jnp.bfloat16),
        in_specs=[spec] * 4 + [pl.BlockSpec(memory_space=pltpu.SMEM)] + [spec] * 3,
        out_specs=spec,
        compiler_params=memory(16),
        name="pre_gradient",
    )(keep, near, far, tiles, tile.reshape(1), weights, mine, answers)


def collect_kernel(core, *refs):
    *pieces, out = refs
    half, rows = out.shape[0] // 2, pieces[0].shape[0]
    count = len(pieces) // 2
    for index, piece in enumerate(pieces):
        which = core[0] if index < count else 1 - core[0]
        first = which * half + (index % count) * rows
        out[pl.ds(pl.multiple_of(first, rows), rows), :] = piece[...].astype(jnp.float32)


def collect(core, own, received):
    spec = pl.BlockSpec(memory_space=pltpu.VMEM)
    pieces = [*own, *received]
    rows, width = sum(piece.shape[0] for piece in pieces), own[0].shape[1]
    return pl.pallas_call(
        collect_kernel,
        out_shape=jax.ShapeDtypeStruct((rows, width), jnp.float32),
        in_specs=[pl.BlockSpec(memory_space=pltpu.SMEM)] + [spec] * len(pieces),
        out_specs=spec,
        compiler_params=memory(16),
        name="collect",
    )(core.reshape(1), *pieces)


def add_kernel(first, second, out):
    out[...] = (first[...].astype(jnp.float32) + second[...].astype(jnp.float32)).astype(out.dtype)


def added(first, second):
    spec = pl.BlockSpec(memory_space=pltpu.VMEM)
    return pl.pallas_call(
        add_kernel,
        out_shape=jax.ShapeDtypeStruct(first.shape, jnp.bfloat16),
        in_specs=[spec, spec],
        out_specs=spec,
        compiler_params=memory(16),
        name="added",
    )(first, second)


def sum_over_panels(core, parts, received):
    both = ("obs", "pix")
    parts = [added(part, other) for part, other in zip(parts, received)]
    for order in ((4, 1), (1, 4)):
        perm = [(i, i ^ order[(i >> 1) & 1]) for i in range(8)]
        parts = [added(part, lax.ppermute(part, both, perm)) for part in parts]
    return collect(core, parts, [swap(part, "obs", 1) for part in parts])


def shards(spectra, enc_weight, pix_tile, pix_local, foot_weight, cotangent, adjoint, mixing):
    tile_count = lax.axis_size("pix")
    tile_rows = cotangent.shape[0]
    quarter = spectra.shape[0] // lax.axis_size("chan")
    tile = lax.axis_index("pix")
    chan = lax.axis_index("chan")
    first_row = chan * quarter
    middle = [(1, 2), (2, 1)]

    send = project(spectra, enc_weight, chan, 1)
    near = swap(send, "chan", 1)
    keep = project(spectra, enc_weight, chan, 0)
    above, below = edges(cotangent, "pix", HALO)
    anchor = tile * tile_rows - HALO
    tile_ids = lax.dynamic_slice_in_dim(pix_tile, first_row, quarter, 0)
    weights = lax.dynamic_slice_in_dim(foot_weight, first_row, quarter, 0)[:, None]
    capacity = 2 * quarter // tile_count
    if capacity >= quarter and tile_count == 2:
        lists = (pix_local, swap(pix_local, "pix", 1))
        rows = pixel_rows(
            cotangent, above, below, adjoint, mixing, anchor, lists, first_row, quarter
        )
        answers = swap(rows[quarter:], "pix", 1)
    else:
        local_ids = lax.dynamic_slice_in_dim(pix_local, first_row, quarter, 0)
        slot_index, wanted = requests(tile_ids[:, 0], local_ids, capacity)
        rows = pixel_rows(
            cotangent, above, below, adjoint, mixing, anchor, (wanted,), 0 * chan, wanted.shape[0]
        )
        answers = lax.all_to_all(
            rows.reshape(tile_count, capacity, -1), "pix", split_axis=0, concat_axis=0, tiled=True
        )
        answers = jnp.take(answers.reshape(tile_count * capacity, -1), slot_index, axis=0)
        rows = answers
    near, rows = lax.optimization_barrier((near, rows))
    passed_on = keep[quarter:].astype(jnp.float32) + near[quarter:].astype(jnp.float32)
    far = swap(passed_on.astype(jnp.bfloat16), "chan", 2)
    far, flipped = lax.optimization_barrier((far, turned(spectra, chan)))
    grads = pre_gradient(keep, near, far, tile_ids, tile, weights, rows, answers)

    beside = swap(grads, "chan", 1)
    across = lax.ppermute(grads, "chan", middle)
    passed = lax.ppermute(across, "chan", [(1, 0), (2, 3)])
    crossed = lax.ppermute(beside, "chan", middle)
    skipped = lax.ppermute(beside, "chan", [(2, 0), (1, 3)])
    core = lax.axis_index("obs") & 1
    early = early_product(flipped[0], grads, beside)
    rest = (jnp.stack([chan, core]), flipped[1], early, crossed, passed, across, skipped)
    send = late_product(1, *rest)
    if lax.axis_size("obs") == 4 and tile_count == 2:
        received = [swap(part, "obs", 1) for part in send]
        return sum_over_panels(core, late_product(0, *rest), received)
    return lax.psum(collect(core, late_product(0, *rest), send), ("obs", "pix"))


def solution(mesh):
    return jax.shard_map(
        shards,
        mesh=mesh,
        in_specs=(
            P(("obs", "pix"), "chan"),
            P("chan", None),
            P(("obs", "pix"), None),
            P(("obs", "pix")),
            P(("obs", "pix")),
            P("pix", None),
            P(None, "pix"),
            P(),
        ),
        out_specs=P("chan", None),
        check_vma=False,
    )
```

time: 93.9 us -> 92.6 us (0.986)
  the two profiles are of different devices: /device:TPU:0 before, /device:TPU:11 now
where the time goes in v6:
time: 92.6 us; the launch traced here: 91.9 us
  Pallas kernels  26.7 us (29%)
  starting transfers between devices  25 us (27%)
  local copies, waits for them, and re-layouts  20.6 us (22%)
  waiting for transfers between devices  17.4 us (19%)
  other arithmetic  1.84 us (2%)
    unnamed x37, local copies, waits for them, and re-layouts  18.2 us
    pallas_call x1, Pallas kernels, pixel_rows(): pl.pallas_call(functools.partial(pixel_kernel, count), out_shape=jax.Shap...  17.2 us
    ppermute x9, starting transfers between devices, swap(): return lax.ppermute(value, axis, [(i, i ^ bit) for i in range(size)])  12.2 us
    ppermute x4, waiting for transfers between devices, sum_over_panels(): parts = [added(part, lax.ppermute(part, both, perm)) for part in parts]  6.12 us
    ppermute x1, waiting for transfers between devices, shards(): crossed = lax.ppermute(beside, 'chan', middle)  4.51 us
    ppermute x1, starting transfers between devices, shards(): crossed = lax.ppermute(beside, 'chan', middle)  4.16 us
    ppermute x1, waiting for transfers between devices, shards(): across = lax.ppermute(grads, 'chan', middle)  3.76 us
    ppermute x9, waiting for transfers between devices, swap(): return lax.ppermute(value, axis, [(i, i ^ bit) for i in range(size)])  3.05 us
  transfers between devices with their start and end apart: 18, of which 8 were waited for; matrix products, arithmetic and copies ran while one was open for 5% of the time, Pallas kernels for 25%

profile of v6, /device:TPU:11, one launch (start us, length us, event | category | flops | bytes accessed | tf_op | source)
XLA Modules:
  0.0 91.9 jit_solution(2517731667572537630)
XLA Ops:
  0.0 1.2 %collective-permute-start.1 = (s32[2048]{0:T(1024)}, s32[2048]{0:T(1024)S(1)}, u32[]{:S(2)}, u32[]{:S(2)}) collective-permute-start(s32[2048]{0:T(1024)} %refs_0_.1), channel_id=1, source_target_pairs={{0,4},{4,0},{1,5},{5,1},{2,6},{6,2},{3,7},{7,3},{8,12},{12,8},{9,1... | collective-permute-start | bytes 24584 | tf_op jit(solution)/shard_map/ppermute | solution.py:44
  2.4 2.3 %copy-done.1 = bf16[2048,1152]{1,0:T(8,128)(2,1)S(1)} copy-done((bf16[2048,1152]{1,0:T(8,128)(2,1)S(1)}, bf16[2048,1152]{1,0:T(8,128)(2,1)}, u32[]{:S(2)}) %copy-start.1) | copy-done | bytes 4718616
  4.8 1.1 %copy-done.4 = bf16[1152,256]{1,0:T(8,128)(2,1)S(1)} copy-done((bf16[1152,256]{1,0:T(8,128)(2,1)S(1)}, bf16[1152,256]{1,0:T(8,128)(2,1)}, u32[]{:S(2)}) %copy-start.4) | copy-done | bytes 589848
  7.0 2.3 %copy-done.2 = bf16[2048,1152]{1,0:T(8,128)(2,1)S(1)} copy-done((bf16[2048,1152]{1,0:T(8,128)(2,1)S(1)}, bf16[2048,1152]{1,0:T(8,128)(2,1)}, u32[]{:S(2)}) %copy-start.2) | copy-done | bytes 4718616
  10.2 1.6 %copy-done.14 = bf16[4096,256]{1,0:T(8,128)(2,1)S(1)} copy-done((bf16[4096,256]{1,0:T(8,128)(2,1)S(1)}, bf16[4096,256]{1,0:T(8,128)(2,1)}, u32[]{:S(2)}) %copy-start.14) | copy-done | bytes 2097176
  11.8 17.2 %pixel_rows.1.mine = bf16[1024,256]{1,0:T(8,128)(2,1)S(1)} custom-call(s32[1]{0:T(128)} %bitcast.2.start, s32[8,4096]{1,0:T(8,128)S(1)} %broadcast_subtract_fusion.places, s32[2048]{0:T(1024)S(1)} %copy-done.15, s32[2048]{0:T(1024)S(1)} %collective-permute-done.1.refs_1_, bf16[4096,256]{1,0:T(8,128)(2,1)S(1)} %copy-done.14, ...), custom_call_target="tpu_custom_call" | custom-call | flops 12884901888 | bytes 4194304 | tf_op jit(solution)/shard_map/pixel_rows/pallas_call | solution.py:212
  29.9 2.3 %collective-permute-start.3 = (bf16[512,256]{1,0:T(8,128)(2,1)}, bf16[512,256]{1,0:T(8,128)(2,1)}, u32[]{:S(2)}, u32[]{:S(2)}) collective-permute-start(bf16[512,256]{1,0:T(8,128)(2,1)} %add_convert_fusion), channel_id=1, source_target_pairs={{0,2},{1,3},{2,0},{3,1},{4,6},{5,7},{6,4},{7,5},{8,10},{9,11},{10,... | collective-permute-start | bytes 786440 | tf_op jit(solution)/shard_map/ppermute | solution.py:44
  32.9 1.2 %collective-permute-start.4 = (bf16[512,256]{1,0:T(8,128)(2,1)}, bf16[512,256]{1,0:T(8,128)(2,1)}, u32[]{:S(2)}, u32[]{:S(2)}) collective-permute-start(bf16[512,256]{1,0:T(8,128)(2,1)} %slice.21), channel_id=1, source_target_pairs={{0,4},{4,0},{1,5},{5,1},{2,6},{6,2},{3,7},{7,3},{8,12},{12,8},{9,1... | collective-permute-start | bytes 786440 | tf_op jit(solution)/shard_map/ppermute | solution.py:44
  34.2 2.3 %copy-done.3 = bf16[2048,1152]{1,0:T(8,128)(2,1)S(1)} copy-done((bf16[2048,1152]{1,0:T(8,128)(2,1)S(1)}, bf16[2048,1152]{1,0:T(8,128)(2,1)}, u32[]{:S(2)}) %copy-start.3) | copy-done | bytes 4718616
  36.5 1.4 %turned.1 = (bf16[1152,1024]{1,0:T(8,128)(2,1)S(1)}, bf16[1152,1024]{1,0:T(8,128)(2,1)S(1)}) custom-call(s32[1]{0:T(128)} %bitcast.1.chan, bf16[2048,1152]{1,0:T(8,128)(2,1)S(1)} %copy-done.3), custom_call_target="tpu_custom_call" | custom-call | tf_op jit(solution)/shard_map/turned/pallas_call | solution.py:95
  37.9 1.4 %copy-done.6 = bf16[1152,1024]{1,0:T(8,128)(2,1)} copy-done((bf16[1152,1024]{1,0:T(8,128)(2,1)}, bf16[1152,1024]{1,0:T(8,128)(2,1)S(1)}, u32[]{:S(2)}) %copy-start.6) | copy-done | bytes 2359320
  41.8 1.3 %collective-permute-done.3.far = bf16[512,256]{1,0:T(8,128)(2,1)} collective-permute-done((bf16[512,256]{1,0:T(8,128)(2,1)}, bf16[512,256]{1,0:T(8,128)(2,1)}, u32[]{:S(2)}, u32[]{:S(2)}) %collective-permute-start.3) | collective-permute-done | bytes 262176 | tf_op jit(solution)/shard_map/ppermute | solution.py:44
  43.1 1.0 %copy-done.9 = bf16[1024,256]{1,0:T(8,128)(2,1)S(1)} copy-done((bf16[1024,256]{1,0:T(8,128)(2,1)S(1)}, bf16[1024,256]{1,0:T(8,128)(2,1)}, u32[]{:S(2)}) %copy-start.9) | copy-done | bytes 524312
  46.1 1.4 %pre_gradient.1.first = bf16[512,256]{1,0:T(8,128)(2,1)S(1)} custom-call(bf16[1024,256]{1,0:T(8,128)(2,1)S(1)} %project.2.keep, bf16[1024,256]{1,0:T(8,128)(2,1)S(1)} %collective-permute-done.near, bf16[512,256]{1,0:T(8,128)(2,1)} %collective-permute-done.3.far, s32[512,1]{1,0:T(8,128)S(1)} %copy-done.13, s32[1]{0:T(128)} %bitcast.3.tile, ...), custom_call_target="tpu_custom_call" | custom-call | tf_op jit(solution)/shard_map/pre_gradient/pallas_call | solution.py:249
  47.5 3.0 %collective-permute-start.7 = (bf16[512,256]{1,0:T(8,128)(2,1)S(1)}, bf16[512,256]{1,0:T(8,128)(2,1)S(1)}, u32[]{:S(2)}, u32[]{:S(2)}) collective-permute-start(bf16[512,256]{1,0:T(8,128)(2,1)S(1)} %pre_gradient.1.first), channel_id=1, source_target_pairs={{1,2},{2,1},{5,6},{6,5},{9,10},{10,9},{13,14},{14,13},{17,18},{18,... | collective-permute-start | bytes 786440 | tf_op jit(solution)/shard_map/ppermute | solution.py:349
  51.9 3.8 %collective-permute-done.7.across = bf16[512,256]{1,0:T(8,128)(2,1)S(1)} collective-permute-done((bf16[512,256]{1,0:T(8,128)(2,1)S(1)}, bf16[512,256]{1,0:T(8,128)(2,1)S(1)}, u32[]{:S(2)}, u32[]{:S(2)}) %collective-permute-start.7) | collective-permute-done | bytes 262176 | tf_op jit(solution)/shard_map/ppermute | solution.py:349
  55.7 1.3 %collective-permute-start.8 = (bf16[512,256]{1,0:T(8,128)(2,1)S(1)}, bf16[512,256]{1,0:T(8,128)(2,1)S(1)}, u32[]{:S(2)}, u32[]{:S(2)}) collective-permute-start(bf16[512,256]{1,0:T(8,128)(2,1)S(1)} %collective-permute-done.7.across), channel_id=1, source_target_pairs={{1,0},{2,3},{5,4},{6,7},{9,8},{10,11},{13,12},{14,15},{17,16},{18,... | collective-permute-start | bytes 786440 | tf_op jit(solution)/shard_map/ppermute | solution.py:350
  57.7 1.9 %collective-permute-start.9 = (bf16[512,256]{1,0:T(8,128)(2,1)}, bf16[512,256]{1,0:T(8,128)(2,1)S(1)}, u32[]{:S(2)}, u32[]{:S(2)}) collective-permute-start(bf16[512,256]{1,0:T(8,128)(2,1)} %collective-permute-done.5.second), channel_id=1, source_target_pairs={{2,0},{1,3},{6,4},{5,7},{10,8},{9,11},{14,12},{13,15},{18,16},{17,... | collective-permute-start | bytes 786440 | tf_op jit(solution)/shard_map/ppermute | solution.py:352
  59.6 4.2 %collective-permute-start.6 = (bf16[512,256]{1,0:T(8,128)(2,1)}, bf16[512,256]{1,0:T(8,128)(2,1)S(1)}, u32[]{:S(2)}, u32[]{:S(2)}) collective-permute-start(bf16[512,256]{1,0:T(8,128)(2,1)} %collective-permute-done.5.second), channel_id=1, source_target_pairs={{1,2},{2,1},{5,6},{6,5},{9,10},{10,9},{13,14},{14,13},{17,18},{18,... | collective-permute-start | bytes 786440 | tf_op jit(solution)/shard_map/ppermute | solution.py:351
  63.8 1.7 %copy-done.7 = bf16[1152,1024]{1,0:T(8,128)(2,1)S(1)} copy-done((bf16[1152,1024]{1,0:T(8,128)(2,1)S(1)}, bf16[1152,1024]{1,0:T(8,128)(2,1)}, u32[]{:S(2)}) %copy-start.7) | copy-done | bytes 2359320
  66.4 1.7 %early_product.1.before = f32[1152,256]{1,0:T(8,128)S(1)} custom-call(bf16[1152,1024]{1,0:T(8,128)(2,1)S(1)} %copy-done.7, bf16[512,256]{1,0:T(8,128)(2,1)S(1)} %copy-done.11, bf16[512,256]{1,0:T(8,128)(2,1)} %collective-permute-done.5.second), custom_call_target="tpu_custom_call" | custom-call | flops 603979776 | bytes 3538944 | tf_op jit(solution)/shard_map/early_product/pallas_call | solution.py:113
  68.2 4.5 %collective-permute-done.6.crossed = bf16[512,256]{1,0:T(8,128)(2,1)S(1)} collective-permute-done((bf16[512,256]{1,0:T(8,128)(2,1)}, bf16[512,256]{1,0:T(8,128)(2,1)S(1)}, u32[]{:S(2)}, u32[]{:S(2)}) %collective-permute-start.6) | collective-permute-done | bytes 262176 | tf_op jit(solution)/shard_map/ppermute | solution.py:351
  72.7 1.0 %late_product.3 = (bf16[288,256]{1,0:T(8,128)(2,1)S(1)}, bf16[288,256]{1,0:T(8,128)(2,1)S(1)}) custom-call(s32[2]{0:T(128)S(1)} %pad_add_fusion.where, bf16[1152,1024]{1,0:T(8,128)(2,1)S(1)} %get-tuple-element.19.flipped, f32[1152,256]{1,0:T(8,128)S(1)} %early_product.1.before, bf16[512,256]{1,0:T(8,128)(2,1)S(1)} %collective-permute-done.6.crossed, ...), custom_call_target="tpu_custom_call" | custom-call | flops 301989888 | bytes 2359296 | tf_op jit(solution)/shard_map/late_product/pallas_call | solution.py:146
  73.7 2.3 %collective-permute-start.10 = (bf16[288,256]{1,0:T(8,128)(2,1)S(1)}, bf16[288,256]{1,0:T(8,128)(2,1)S(1)}, u32[]{:S(2)}, u32[]{:S(2)}) collective-permute-start(bf16[288,256]{1,0:T(8,128)(2,1)S(1)} %get-tuple-element.24), channel_id=1, source_target_pairs={{0,8},{8,0},{16,24},{24,16},{1,9},{9,1},{17,25},{25,17},{2,10},{10... | collective-permute-start | bytes 442376 | tf_op jit(solution)/shard_map/ppermute | solution.py:44
  76.1 1.0 %late_product.2 = (f32[288,256]{1,0:T(8,128)S(1)}, f32[288,256]{1,0:T(8,128)S(1)}) custom-call(s32[2]{0:T(128)S(1)} %pad_add_fusion.where, bf16[1152,1024]{1,0:T(8,128)(2,1)S(1)} %get-tuple-element.19.flipped, f32[1152,256]{1,0:T(8,128)S(1)} %early_product.1.before, bf16[512,256]{1,0:T(8,128)(2,1)S(1)} %collective-permute-done.6.crossed, ...), custom_call_target="tpu_custom_call" | custom-call | flops 301989888 | bytes 2359296 | tf_op jit(solution)/shard_map/late_product/pallas_call | solution.py:146
  77.2 1.3 %collective-permute-start.11 = (bf16[288,256]{1,0:T(8,128)(2,1)S(1)}, bf16[288,256]{1,0:T(8,128)(2,1)S(1)}, u32[]{:S(2)}, u32[]{:S(2)}) collective-permute-start(bf16[288,256]{1,0:T(8,128)(2,1)S(1)} %added.6.first), channel_id=1, source_target_pairs={{0,16},{4,20},{8,12},{12,8},{16,0},{20,4},{24,28},{28,24},{1,17},{... | collective-permute-start | bytes 442376 | tf_op jit(solution)/shard_map/ppermute | solution.py:304
  78.8 2.7 %collective-permute-done.11.second = bf16[288,256]{1,0:T(8,128)(2,1)S(1)} collective-permute-done((bf16[288,256]{1,0:T(8,128)(2,1)S(1)}, bf16[288,256]{1,0:T(8,128)(2,1)S(1)}, u32[]{:S(2)}, u32[]{:S(2)}) %collective-permute-start.11) | collective-permute-done | bytes 147488 | tf_op jit(solution)/shard_map/ppermute | solution.py:304
  81.9 1.2 %collective-permute-done.14.second = bf16[288,256]{1,0:T(8,128)(2,1)S(1)} collective-permute-done((bf16[288,256]{1,0:T(8,128)(2,1)S(1)}, bf16[288,256]{1,0:T(8,128)(2,1)S(1)}, u32[]{:S(2)}, u32[]{:S(2)}) %collective-permute-start.14) | collective-permute-done | bytes 147488 | tf_op jit(solution)/shard_map/ppermute | solution.py:304
  83.5 2.2 %collective-permute-done.12.second = bf16[288,256]{1,0:T(8,128)(2,1)S(1)} collective-permute-done((bf16[288,256]{1,0:T(8,128)(2,1)S(1)}, bf16[288,256]{1,0:T(8,128)(2,1)S(1)}, u32[]{:S(2)}, u32[]{:S(2)}) %collective-permute-start.12) | collective-permute-done | bytes 147488 | tf_op jit(solution)/shard_map/ppermute | solution.py:304
  85.7 2.5 %collective-permute-start.16 = (bf16[288,256]{1,0:T(8,128)(2,1)S(1)}, bf16[288,256]{1,0:T(8,128)(2,1)S(1)}, u32[]{:S(2)}, u32[]{:S(2)}) collective-permute-start(bf16[288,256]{1,0:T(8,128)(2,1)S(1)} %added.8.refs_0_), channel_id=1, source_target_pairs={{0,8},{8,0},{16,24},{24,16},{1,9},{9,1},{17,25},{25,17},{2,10},{10... | collective-permute-start | bytes 442376 | tf_op jit(solution)/shard_map/ppermute | solution.py:44
  88.2 1.6 %collective-permute-start.17 = (bf16[288,256]{1,0:T(8,128)(2,1)S(1)}, bf16[288,256]{1,0:T(8,128)(2,1)S(1)}, u32[]{:S(2)}, u32[]{:S(2)}) collective-permute-start(bf16[288,256]{1,0:T(8,128)(2,1)S(1)} %added.11.refs_1_), channel_id=1, source_target_pairs={{0,8},{8,0},{16,24},{24,16},{1,9},{9,1},{17,25},{25,17},{2,10},{10... | collective-permute-start | bytes 442376 | tf_op jit(solution)/shard_map/ppermute | solution.py:44
  90.8 1.1 %collect.1 = f32[1152,256]{1,0:T(8,128)} custom-call(s32[1]{0:T(128)} %bitcast.core, bf16[288,256]{1,0:T(8,128)(2,1)S(1)} %added.8.refs_0_, bf16[288,256]{1,0:T(8,128)(2,1)S(1)} %added.11.refs_1_, bf16[288,256]{1,0:T(8,128)(2,1)S(1)} %collective-permute-done.16.refs_2_, bf16[288,256]{1,0:T(8,128)(2,1)S(1)} %collective-permute-done.17.refs_3_), custom_call_target="tpu_custom_call" | custom-call | tf_op jit(solution)/shard_map/collect/pallas_call | solution.py:273
  (64 shorter events, 14.6 us)
Async XLA Ops:
  0.0 40.9 %copy-start = (s32[2048,1]{0,1:T(1,128)S(1)}, s32[2048,1]{0,1:T(1,128)}, u32[]{:S(2)}) copy-start(s32[2048,1]{0,1:T(1,128)} %param.10) | copy-start | bytes 24580
  0.0 10.2 %collective-permute-start.1 = (s32[2048]{0:T(1024)}, s32[2048]{0:T(1024)S(1)}, u32[]{:S(2)}, u32[]{:S(2)}) collective-permute-start(s32[2048]{0:T(1024)} %refs_0_.1), channel_id=1, source_target_pairs={{0,4},{4,0},{1,5},{5,1},{2,6},{6,2},{3,7},{7,3},{8,12},{12,8},{9,1... | collective-permute-start | bytes 24584 | tf_op jit(solution)/shard_map/ppermute | solution.py:44
  2.1 8.0 %collective-permute-start.2 = (bf16[128,256]{1,0:T(8,128)(2,1)S(1)}, bf16[128,256]{1,0:T(8,128)(2,1)S(1)}, u32[]{:S(2)}, u32[]{:S(2)}) collective-permute-start(bf16[128,256]{1,0:T(8,128)(2,1)S(1)} %slice_select_fusion), channel_id=1, source_target_pairs={{0,4},{4,0},{1,5},{5,1},{2,6},{6,2},{3,7},{7,3},{8,12},{12,8},{9,1... | collective-permute-start | bytes 196616 | tf_op jit(solution)/shard_map/ppermute | solution.py:21
  2.4 2.3 %copy-start.1 = (bf16[2048,1152]{1,0:T(8,128)(2,1)S(1)}, bf16[2048,1152]{1,0:T(8,128)(2,1)}, u32[]{:S(2)}) copy-start(bf16[2048,1152]{1,0:T(8,128)(2,1)} %spectra.5) | copy-start | bytes 14155780
  4.8 1.1 %copy-start.4 = (bf16[1152,256]{1,0:T(8,128)(2,1)S(1)}, bf16[1152,256]{1,0:T(8,128)(2,1)}, u32[]{:S(2)}) copy-start(bf16[1152,256]{1,0:T(8,128)(2,1)} %weight.3) | copy-start | bytes 1769476
  5.8 1.1 %copy-start.17 = (s32[8,4096]{1,0:T(8,128)S(1)}, s32[8,4096]{1,0:T(8,128)}, u32[]{:S(2)}) copy-start(s32[8,4096]{1,0:T(8,128)} %param.14) | copy-start | bytes 393220
  5.8 1.1 %copy-start.5 = (bf16[1152,256]{1,0:T(8,128)(2,1)S(1)}, bf16[1152,256]{1,0:T(8,128)(2,1)}, u32[]{:S(2)}) copy-start(bf16[1152,256]{1,0:T(8,128)(2,1)} %weight.3) | copy-start | bytes 1769476
  6.7 22.3 %collective-permute-start = (bf16[1024,256]{1,0:T(8,128)(2,1)S(1)}, bf16[1024,256]{1,0:T(8,128)(2,1)S(1)}, u32[]{:S(2)}, u32[]{:S(2)}) collective-permute-start(bf16[1024,256]{1,0:T(8,128)(2,1)S(1)} %project.3), channel_id=1, source_target_pairs={{0,1},{1,0},{2,3},{3,2},{4,5},{5,4},{6,7},{7,6},{8,9},{9,8},{10,11... | collective-permute-start | bytes 1572872 | tf_op jit(solution)/shard_map/ppermute | solution.py:44
  7.0 2.3 %copy-start.2 = (bf16[2048,1152]{1,0:T(8,128)(2,1)S(1)}, bf16[2048,1152]{1,0:T(8,128)(2,1)}, u32[]{:S(2)}) copy-start(bf16[2048,1152]{1,0:T(8,128)(2,1)} %spectra.5) | copy-start | bytes 14155780
  10.2 1.6 %copy-start.14 = (bf16[4096,256]{1,0:T(8,128)(2,1)S(1)}, bf16[4096,256]{1,0:T(8,128)(2,1)}, u32[]{:S(2)}) copy-start(bf16[4096,256]{1,0:T(8,128)(2,1)} %refs_2_.1) | copy-start | bytes 6291460
  29.0 5.2 %copy-start.8 = (bf16[1024,256]{1,0:T(8,128)(2,1)}, bf16[1024,256]{1,0:T(8,128)(2,1)S(1)}, u32[]{:S(2)}) copy-start(bf16[1024,256]{1,0:T(8,128)(2,1)S(1)} %pixel_rows.1.mine) | copy-start | bytes 1572868
  29.9 13.2 %collective-permute-start.3 = (bf16[512,256]{1,0:T(8,128)(2,1)}, bf16[512,256]{1,0:T(8,128)(2,1)}, u32[]{:S(2)}, u32[]{:S(2)}) collective-permute-start(bf16[512,256]{1,0:T(8,128)(2,1)} %add_convert_fusion), channel_id=1, source_target_pairs={{0,2},{1,3},{2,0},{3,1},{4,6},{5,7},{6,4},{7,5},{8,10},{9,11},{10,... | collective-permute-start | bytes 786440 | tf_op jit(solution)/shard_map/ppermute | solution.py:44
  32.9 10.2 %collective-permute-start.4 = (bf16[512,256]{1,0:T(8,128)(2,1)}, bf16[512,256]{1,0:T(8,128)(2,1)}, u32[]{:S(2)}, u32[]{:S(2)}) collective-permute-start(bf16[512,256]{1,0:T(8,128)(2,1)} %slice.21), channel_id=1, source_target_pairs={{0,4},{4,0},{1,5},{5,1},{2,6},{6,2},{3,7},{7,3},{8,12},{12,8},{9,1... | collective-permute-start | bytes 786440 | tf_op jit(solution)/shard_map/ppermute | solution.py:44
  34.2 2.3 %copy-start.3 = (bf16[2048,1152]{1,0:T(8,128)(2,1)S(1)}, bf16[2048,1152]{1,0:T(8,128)(2,1)}, u32[]{:S(2)}) copy-start(bf16[2048,1152]{1,0:T(8,128)(2,1)} %spectra.5) | copy-start | bytes 14155780
  37.9 1.4 %copy-start.6 = (bf16[1152,1024]{1,0:T(8,128)(2,1)}, bf16[1152,1024]{1,0:T(8,128)(2,1)S(1)}, u32[]{:S(2)}) copy-start(bf16[1152,1024]{1,0:T(8,128)(2,1)S(1)} %get-tuple-element.20.flipped) | copy-start | bytes 7077892
  43.1 1.0 %copy-start.9 = (bf16[1024,256]{1,0:T(8,128)(2,1)S(1)}, bf16[1024,256]{1,0:T(8,128)(2,1)}, u32[]{:S(2)}) copy-start(bf16[1024,256]{1,0:T(8,128)(2,1)} %copy-done.8) | copy-start | bytes 1572868
  44.2 0.9 %copy-start.12 = (f32[512,1]{1,0:T(8,128)S(1)}, f32[512,1]{1,0:T(8,128)}, u32[]{:S(2)}) copy-start(f32[512,1]{1,0:T(8,128)} %copy.11.weights) | copy-start | bytes 6148
  45.1 0.9 %copy-start.13 = (s32[512,1]{1,0:T(8,128)S(1)}, s32[512,1]{1,0:T(8,128)}, u32[]{:S(2)}) copy-start(s32[512,1]{1,0:T(8,128)} %copy.12.tiles) | copy-start | bytes 6148
  47.5 8.2 %collective-permute-start.7 = (bf16[512,256]{1,0:T(8,128)(2,1)S(1)}, bf16[512,256]{1,0:T(8,128)(2,1)S(1)}, u32[]{:S(2)}, u32[]{:S(2)}) collective-permute-start(bf16[512,256]{1,0:T(8,128)(2,1)S(1)} %pre_gradient.1.first), channel_id=1, source_target_pairs={{1,2},{2,1},{5,6},{6,5},{9,10},{10,9},{13,14},{14,13},{17,18},{18,... | collective-permute-start | bytes 786440 | tf_op jit(solution)/shard_map/ppermute | solution.py:349
  50.5 7.2 %collective-permute-start.5 = (bf16[512,256]{1,0:T(8,128)(2,1)S(1)}, bf16[512,256]{1,0:T(8,128)(2,1)}, u32[]{:S(2)}, u32[]{:S(2)}) collective-permute-start(bf16[512,256]{1,0:T(8,128)(2,1)S(1)} %pre_gradient.1.first), channel_id=1, source_target_pairs={{0,1},{1,0},{2,3},{3,2},{4,5},{5,4},{6,7},{7,6},{8,9},{9,8},{10,11... | collective-permute-start | bytes 786440 | tf_op jit(solution)/shard_map/ppermute | solution.py:44
  55.7 12.5 %collective-permute-start.8 = (bf16[512,256]{1,0:T(8,128)(2,1)S(1)}, bf16[512,256]{1,0:T(8,128)(2,1)S(1)}, u32[]{:S(2)}, u32[]{:S(2)}) collective-permute-start(bf16[512,256]{1,0:T(8,128)(2,1)S(1)} %collective-permute-done.7.across), channel_id=1, source_target_pairs={{1,0},{2,3},{5,4},{6,7},{9,8},{10,11},{13,12},{14,15},{17,16},{18,... | collective-permute-start | bytes 786440 | tf_op jit(solution)/shard_map/ppermute | solution.py:350
  57.7 10.5 %collective-permute-start.9 = (bf16[512,256]{1,0:T(8,128)(2,1)}, bf16[512,256]{1,0:T(8,128)(2,1)S(1)}, u32[]{:S(2)}, u32[]{:S(2)}) collective-permute-start(bf16[512,256]{1,0:T(8,128)(2,1)} %collective-permute-done.5.second), channel_id=1, source_target_pairs={{2,0},{1,3},{6,4},{5,7},{10,8},{9,11},{14,12},{13,15},{18,16},{17,... | collective-permute-start | bytes 786440 | tf_op jit(solution)/shard_map/ppermute | solution.py:352
  59.6 13.1 %collective-permute-start.6 = (bf16[512,256]{1,0:T(8,128)(2,1)}, bf16[512,256]{1,0:T(8,128)(2,1)S(1)}, u32[]{:S(2)}, u32[]{:S(2)}) collective-permute-start(bf16[512,256]{1,0:T(8,128)(2,1)} %collective-permute-done.5.second), channel_id=1, source_target_pairs={{1,2},{2,1},{5,6},{6,5},{9,10},{10,9},{13,14},{14,13},{17,18},{18,... | collective-permute-start | bytes 786440 | tf_op jit(solution)/shard_map/ppermute | solution.py:351
  63.8 1.7 %copy-start.7 = (bf16[1152,1024]{1,0:T(8,128)(2,1)S(1)}, bf16[1152,1024]{1,0:T(8,128)(2,1)}, u32[]{:S(2)}) copy-start(bf16[1152,1024]{1,0:T(8,128)(2,1)} %copy-done.6) | copy-start | bytes 7077892
  73.7 3.4 %collective-permute-start.10 = (bf16[288,256]{1,0:T(8,128)(2,1)S(1)}, bf16[288,256]{1,0:T(8,128)(2,1)S(1)}, u32[]{:S(2)}, u32[]{:S(2)}) collective-permute-start(bf16[288,256]{1,0:T(8,128)(2,1)S(1)} %get-tuple-element.24), channel_id=1, source_target_pairs={{0,8},{8,0},{16,24},{24,16},{1,9},{9,1},{17,25},{25,17},{2,10},{10... | collective-permute-start | bytes 442376 | tf_op jit(solution)/shard_map/ppermute | solution.py:44
  76.0 2.5 %collective-permute-start.13 = (bf16[288,256]{1,0:T(8,128)(2,1)S(1)}, bf16[288,256]{1,0:T(8,128)(2,1)S(1)}, u32[]{:S(2)}, u32[]{:S(2)}) collective-permute-start(bf16[288,256]{1,0:T(8,128)(2,1)S(1)} %get-tuple-element.26), channel_id=1, source_target_pairs={{0,8},{8,0},{16,24},{24,16},{1,9},{9,1},{17,25},{25,17},{2,10},{10... | collective-permute-start | bytes 442376 | tf_op jit(solution)/shard_map/ppermute | solution.py:44
  77.2 4.4 %collective-permute-start.11 = (bf16[288,256]{1,0:T(8,128)(2,1)S(1)}, bf16[288,256]{1,0:T(8,128)(2,1)S(1)}, u32[]{:S(2)}, u32[]{:S(2)}) collective-permute-start(bf16[288,256]{1,0:T(8,128)(2,1)S(1)} %added.6.first), channel_id=1, source_target_pairs={{0,16},{4,20},{8,12},{12,8},{16,0},{20,4},{24,28},{28,24},{1,17},{... | collective-permute-start | bytes 442376 | tf_op jit(solution)/shard_map/ppermute | solution.py:304
  78.5 4.6 %collective-permute-start.14 = (bf16[288,256]{1,0:T(8,128)(2,1)S(1)}, bf16[288,256]{1,0:T(8,128)(2,1)S(1)}, u32[]{:S(2)}, u32[]{:S(2)}) collective-permute-start(bf16[288,256]{1,0:T(8,128)(2,1)S(1)} %added.9.first), channel_id=1, source_target_pairs={{0,16},{4,20},{8,12},{12,8},{16,0},{20,4},{24,28},{28,24},{1,17},{... | collective-permute-start | bytes 442376 | tf_op jit(solution)/shard_map/ppermute | solution.py:304
  81.6 4.1 %collective-permute-start.12 = (bf16[288,256]{1,0:T(8,128)(2,1)S(1)}, bf16[288,256]{1,0:T(8,128)(2,1)S(1)}, u32[]{:S(2)}, u32[]{:S(2)}) collective-permute-start(bf16[288,256]{1,0:T(8,128)(2,1)S(1)} %added.7.first), channel_id=1, source_target_pairs={{0,4},{4,0},{8,24},{12,28},{16,20},{20,16},{24,8},{28,12},{1,5},{5... | collective-permute-start | bytes 442376 | tf_op jit(solution)/shard_map/ppermute | solution.py:304
  83.1 5.0 %collective-permute-start.15 = (bf16[288,256]{1,0:T(8,128)(2,1)S(1)}, bf16[288,256]{1,0:T(8,128)(2,1)S(1)}, u32[]{:S(2)}, u32[]{:S(2)}) collective-permute-start(bf16[288,256]{1,0:T(8,128)(2,1)S(1)} %added.10.first), channel_id=1, source_target_pairs={{0,4},{4,0},{8,24},{12,28},{16,20},{20,16},{24,8},{28,12},{1,5},{5... | collective-permute-start | bytes 442376 | tf_op jit(solution)/shard_map/ppermute | solution.py:304
  85.7 4.1 %collective-permute-start.16 = (bf16[288,256]{1,0:T(8,128)(2,1)S(1)}, bf16[288,256]{1,0:T(8,128)(2,1)S(1)}, u32[]{:S(2)}, u32[]{:S(2)}) collective-permute-start(bf16[288,256]{1,0:T(8,128)(2,1)S(1)} %added.8.refs_0_), channel_id=1, source_target_pairs={{0,8},{8,0},{16,24},{24,16},{1,9},{9,1},{17,25},{25,17},{2,10},{10... | collective-permute-start | bytes 442376 | tf_op jit(solution)/shard_map/ppermute | solution.py:44
  88.2 2.6 %collective-permute-start.17 = (bf16[288,256]{1,0:T(8,128)(2,1)S(1)}, bf16[288,256]{1,0:T(8,128)(2,1)S(1)}, u32[]{:S(2)}, u32[]{:S(2)}) collective-permute-start(bf16[288,256]{1,0:T(8,128)(2,1)S(1)} %added.11.refs_1_), channel_id=1, source_target_pairs={{0,8},{8,0},{16,24},{24,16},{1,9},{9,1},{17,25},{25,17},{2,10},{10... | collective-permute-start | bytes 442376 | tf_op jit(solution)/shard_map/ppermute | solution.py:44
  (4 other events, 3.4 us)

commit v7 on v6

v7 whole, which is shorter than its diff:
```python
import functools

import jax
import jax.numpy as jnp
from jax import lax
from jax.experimental import pallas as pl
from jax.experimental.pallas import tpu as pltpu
from jax.sharding import PartitionSpec as P

NEIGH = 8
HALO = 128
MIB = 1024 * 1024
LARGE = 48


def edges(value, axis, width):
    size, length = lax.axis_size(axis), value.shape[0]
    last = lax.slice_in_dim(value, length - width, length, axis=0)
    first = lax.slice_in_dim(value, 0, width, axis=0)
    if size == 2:
        index = lax.axis_index(axis)
        other = lax.ppermute(jnp.where(index == 0, last, first), axis, [(0, 1), (1, 0)])
        return other, other
    up = [(i, i + 1) for i in range(size - 1)]
    return lax.ppermute(last, axis, up), lax.ppermute(first, axis, [(j, i) for i, j in up])


def requests(tile_ids, local_ids, capacity):
    tile_count = lax.axis_size("pix")
    onehot = (tile_ids[:, None] == jnp.arange(tile_count, dtype=jnp.int32)[None, :]).astype(
        jnp.int32
    )
    place_rank = jnp.sum((jnp.cumsum(onehot, axis=0) - 1) * onehot, axis=1)
    slot_index = tile_ids * capacity + place_rank
    outgoing = jnp.full((tile_count * capacity,), 0, jnp.int32).at[slot_index].set(local_ids)
    outgoing = outgoing.reshape(tile_count, capacity)
    requested = lax.all_to_all(outgoing, "pix", split_axis=0, concat_axis=0, tiled=True)
    return slot_index, requested.reshape(-1)


def swap(value, axis, bit):
    size = 1
    for name in (axis,) if isinstance(axis, str) else axis:
        size *= lax.axis_size(name)
    return lax.ppermute(value, axis, [(i, i ^ bit) for i in range(size)])


def memory(mib):
    return pltpu.CompilerParams(vmem_limit_bytes=mib * MIB)


def project_kernel(bits, chan, spectra, weight, out, held, near, sems):
    chunk = out.shape[0] // 4
    copies = [pltpu.make_async_copy(weight, near, sems.at[4])]
    for turn in range(4):
        first = ((chan[0] ^ bits ^ (turn // 2 * 2)) * 2 + turn % 2) * chunk
        copies.append(
            pltpu.make_async_copy(
                spectra.at[pl.ds(pl.multiple_of(first, chunk), chunk)],
                held.at[pl.ds(turn * chunk, chunk)],
                sems.at[turn],
            )
        )
    for copy in copies:
        copy.start()
    copies[0].wait()
    for turn in range(4):
        copies[turn + 1].wait()
        rows = pl.ds(turn * chunk, chunk)
        result = jnp.dot(held[rows, :], near[...], preferred_element_type=jnp.float32)
        out[rows, :] = result.astype(out.dtype)


def project(spectra, weight, chan, bits):
    depth, width = weight.shape
    rows = spectra.shape[0] // 2
    hbm = pl.BlockSpec(memory_space=pltpu.HBM)
    return pl.pallas_call(
        functools.partial(project_kernel, bits),
        out_shape=jax.ShapeDtypeStruct((rows, width), jnp.bfloat16),
        in_specs=[pl.BlockSpec(memory_space=pltpu.SMEM), hbm, hbm],
        out_specs=pl.BlockSpec(memory_space=pltpu.VMEM),
        scratch_shapes=[
            pltpu.VMEM((rows, depth), jnp.bfloat16),
            pltpu.VMEM((depth, width), jnp.bfloat16),
            pltpu.SemaphoreType.DMA((5,)),
        ],
        compiler_params=memory(LARGE),
        cost_estimate=pl.CostEstimate(
            flops=2 * rows * depth * width,
            bytes_accessed=2 * rows * depth + 2 * depth * width + 2 * rows * width,
            transcendentals=0,
        ),
        name="project",
    )(chan.reshape(1), spectra, weight)


def turned_product(left, right):
    return lax.dot_general(
        left, right, (((0,), (0,)), ((), ())), preferred_element_type=jnp.float32
    )


def early_kernel(chan, spectra, first, second, total, late, held, sems):
    rows = first.shape[0]
    copies = []
    for turn in range(4):
        start = pl.multiple_of((chan[0] ^ turn) * rows, rows)
        target = (held, late)[turn // 2].at[pl.ds(turn % 2 * rows, rows)]
        copies.append(pltpu.make_async_copy(spectra.at[pl.ds(start, rows)], target, sems.at[turn]))
    for copy in copies:
        copy.start()
    copies[0].wait()
    product = turned_product(held[:rows, :], first[...])
    copies[1].wait()
    total[...] = product + turned_product(held[rows:, :], second[...])
    copies[2].wait()
    copies[3].wait()


def early_product(spectra, chan, first, second):
    depth = spectra.shape[1]
    rows, width = first.shape
    vmem = pl.BlockSpec(memory_space=pltpu.VMEM)
    return pl.pallas_call(
        early_kernel,
        out_shape=(
            jax.ShapeDtypeStruct((depth, width), jnp.float32),
            jax.ShapeDtypeStruct((2 * rows, depth), jnp.bfloat16),
        ),
        in_specs=[
            pl.BlockSpec(memory_space=pltpu.SMEM),
            pl.BlockSpec(memory_space=pltpu.HBM),
            vmem,
            vmem,
        ],
        out_specs=(vmem, vmem),
        scratch_shapes=[
            pltpu.VMEM((2 * rows, depth), jnp.bfloat16),
            pltpu.SemaphoreType.DMA((4,)),
        ],
        compiler_params=memory(LARGE),
        cost_estimate=pl.CostEstimate(
            flops=4 * rows * depth * width,
            bytes_accessed=8 * rows * depth + 4 * depth * width,
            transcendentals=0,
        ),
        name="early_product",
    )(chan.reshape(1), spectra, first, second)


def late_kernel(where, held, before, crossed, passed, across, skipped, *outs):
    *outs, total = outs
    chan, core = where[0], where[1]
    inner = (chan == 1) | (chan == 2)
    second = jnp.where(inner, crossed[...], passed[...])
    third = jnp.where(inner, across[...], skipped[...])
    rows = jnp.concatenate([second, third], axis=0)
    total[...] = before[...] + turned_product(held[...], rows)
    size = outs[0].shape[0]
    for index, out in enumerate(outs):
        first = (core ^ (1 - index // 2)) * 2 * size + index % 2 * size
        here = pl.ds(pl.multiple_of(first, size), size)
        out[...] = total[here, :].astype(out.dtype)


def late_product(where, held, before, crossed, passed, across, skipped):
    size, width = before.shape[0] // 4, before.shape[1]
    spec = pl.BlockSpec(memory_space=pltpu.VMEM)
    send = jax.ShapeDtypeStruct((size, width), jnp.bfloat16)
    keep = jax.ShapeDtypeStruct((size, width), jnp.float32)
    outs = pl.pallas_call(
        late_kernel,
        out_shape=(send, send, keep, keep),
        in_specs=[pl.BlockSpec(memory_space=pltpu.SMEM)] + [spec] * 6,
        out_specs=(spec,) * 4,
        scratch_shapes=[pltpu.VMEM(before.shape, jnp.float32)],
        compiler_params=memory(16),
        cost_estimate=pl.CostEstimate(
            flops=2 * held.shape[0] * held.shape[1] * width,
            bytes_accessed=2 * held.shape[0] * held.shape[1] + 16 * size * width,
            transcendentals=0,
        ),
        name="late_product",
    )(where, held, before, crossed, passed, across, skipped)
    return outs[:2], outs[2:]


def pixel_kernel(count, start, places, *refs):
    lists = refs[: len(refs) // 2 - 5]
    cotangent, above, below, mixing = refs[len(lists) : len(lists) + 4]
    outs = refs[len(lists) + 4 : 2 * len(lists) + 4]
    table, scale, sums, held, near, sems = refs[2 * len(lists) + 4 :]
    tile_rows, half = held.shape[0], table.shape[1]
    chunk = tile_rows // 4
    copies = [
        pltpu.make_async_copy(
            cotangent.at[pl.ds(n * chunk, chunk)], held.at[pl.ds(n * chunk, chunk)], sems.at[n]
        )
        for n in range(4)
    ]
    copies.append(pltpu.make_async_copy(places, near, sems.at[4]))
    for copy in copies:
        copy.start()

    def fill(first, values):
        values = values.astype(jnp.float32)
        for side in range(2):
            table[pl.ds(2 * first + side, values.shape[0], stride=2), :] = values[
                :, side * half : (side + 1) * half
            ]

    for side in range(2):
        scale[pl.ds(side, NEIGH, stride=2), :] = mixing[:, side * half : (side + 1) * half]
    scales = [scale[2 * k : 2 * k + 2, :] for k in range(NEIGH)]
    fill(0, above[...])
    fill(HALO + tile_rows, below[...])
    for n in range(4):
        copies[n].wait()
        for first in range(n * chunk, (n + 1) * chunk, 256):
            fill(HALO + first, held[first : first + 256, :])
    copies[4].wait()

    group = 16
    for index, wanted in enumerate(lists):

        def body(turn, carry, index=index, wanted=wanted):
            base = turn * group
            totals = []
            for n in range(group):
                pixel = wanted[start[0] + base + n]
                terms = [table[pl.ds(2 * (pixel + HALO), 2), :]]
                for k in range(NEIGH):
                    terms.append(table[pl.ds(near[k, pixel], 2), :] * scales[k])
                while len(terms) > 1:
                    pairs = [x + y for x, y in zip(terms[::2], terms[1::2])]
                    terms = pairs + terms[len(terms) // 2 * 2 :]
                totals += terms
            for n, total in enumerate(totals):
                sums[pl.ds(2 * (index * count + base + n), 2), :] = total
            return carry

        lax.fori_loop(0, count // group, body, 0)
    for index, out in enumerate(outs):
        for side in range(2):
            out[:, side * half : (side + 1) * half] = sums[
                pl.ds(2 * index * count + side, count, stride=2), :
            ].astype(out.dtype)


def pixel_rows(cotangent, above, below, adjoint, mixing, anchor, lists, start, count):
    tile_rows, width = cotangent.shape
    smem = pl.BlockSpec(memory_space=pltpu.SMEM)
    vmem = pl.BlockSpec(memory_space=pltpu.VMEM)
    return pl.pallas_call(
        functools.partial(pixel_kernel, count),
        out_shape=(jax.ShapeDtypeStruct((count, width), jnp.bfloat16),) * len(lists),
        in_specs=[
            smem,
            pl.BlockSpec(memory_space=pl.ANY),
            *[smem] * len(lists),
            pl.BlockSpec(memory_space=pltpu.HBM),
            *[vmem] * 3,
        ],
        out_specs=(vmem,) * len(lists),
        scratch_shapes=[
            pltpu.VMEM((2 * (tile_rows + 2 * HALO), width // 2), jnp.float32),
            pltpu.VMEM((2 * NEIGH, width // 2), jnp.float32),
            pltpu.VMEM((2 * count * len(lists), width // 2), jnp.float32),
            pltpu.VMEM(cotangent.shape, cotangent.dtype),
            pltpu.SMEM(adjoint.shape, jnp.int32),
            pltpu.SemaphoreType.DMA((5,)),
        ],
        compiler_params=memory(LARGE),
        cost_estimate=pl.CostEstimate(
            flops=6 * NEIGH * tile_rows * 256 * width,
            bytes_accessed=4 * tile_rows * width,
            transcendentals=0,
        ),
        name="pixel_rows",
    )(start.reshape(1), (adjoint - anchor) * 2, *lists, cotangent, above, below, mixing)


def gradient_kernel(where, keep, near, far, tiles, weights, mine, answers, out):
    tile, chan = where[0], where[1]
    rows = out.shape[0]
    size = tiles.shape[1]
    count = rows // size
    group = 8 // count
    wide = jnp.float32
    first = pl.multiple_of(chan // group * 8, 8)

    def columns(values):
        turned = values[pl.ds(first, 8), :].T
        places = [turned[:, n * count : (n + 1) * count] for n in range(group)]
        picked = places[0]
        for n in range(1, group):
            picked = jnp.where(chan % group == n, places[n], picked)
        return picked

    own = columns(tiles).astype(wide)
    factors = columns(weights)
    for n in range(count):
        here = slice(n * size, (n + 1) * size)
        pre = keep[here, :].astype(wide) + near[here, :].astype(wide) + far[here, :].astype(wide)
        sigma = jax.nn.sigmoid(pre)
        deriv = sigma * (1.0 + pre * (1.0 - sigma))
        fetched = jnp.where(
            own[:, n : n + 1] == tile.astype(wide),
            mine[here, :].astype(wide),
            answers[here, :].astype(wide),
        )
        out[here, :] = (factors[:, n : n + 1] * deriv * fetched).astype(out.dtype)


def pre_gradient(tile, chan, keep, near, far, tiles, weights, mine, answers):
    spec = pl.BlockSpec(memory_space=pltpu.VMEM)
    tiles, weights = tiles.reshape(-1, 128), weights.reshape(-1, 128)
    return pl.pallas_call(
        gradient_kernel,
        out_shape=jax.ShapeDtypeStruct(far.shape, jnp.bfloat16),
        in_specs=[pl.BlockSpec(memory_space=pltpu.SMEM)] + [spec] * 7,
        out_specs=spec,
        compiler_params=memory(16),
        name="pre_gradient",
    )(jnp.stack([tile, chan]), keep, near, far, tiles, weights, mine, answers)


def collect_kernel(core, *refs):
    *pieces, out = refs
    half, rows = out.shape[0] // 2, pieces[0].shape[0]
    count = len(pieces) // 2
    for index, piece in enumerate(pieces):
        which = core[0] if index < count else 1 - core[0]
        first = which * half + (index % count) * rows
        out[pl.ds(pl.multiple_of(first, rows), rows), :] = piece[...].astype(jnp.float32)


def collect(core, own, received):
    spec = pl.BlockSpec(memory_space=pltpu.VMEM)
    pieces = [*own, *received]
    rows, width = sum(piece.shape[0] for piece in pieces), own[0].shape[1]
    return pl.pallas_call(
        collect_kernel,
        out_shape=jax.ShapeDtypeStruct((rows, width), jnp.float32),
        in_specs=[pl.BlockSpec(memory_space=pltpu.SMEM)] + [spec] * len(pieces),
        out_specs=spec,
        compiler_params=memory(16),
        name="collect",
    )(core.reshape(1), *pieces)


def add_kernel(first, second, out):
    out[...] = (first[...].astype(jnp.float32) + second[...].astype(jnp.float32)).astype(out.dtype)


def added(first, second):
    spec = pl.BlockSpec(memory_space=pltpu.VMEM)
    return pl.pallas_call(
        add_kernel,
        out_shape=jax.ShapeDtypeStruct(first.shape, jnp.bfloat16),
        in_specs=[spec, spec],
        out_specs=spec,
        compiler_params=memory(16),
        name="added",
    )(first, second)


def sum_over_panels(core, parts, received):
    both = ("obs", "pix")
    parts = [added(part, other) for part, other in zip(parts, received)]
    for order in ((4, 1), (1, 4)):
        perm = [(i, i ^ order[(i >> 1) & 1]) for i in range(8)]
        parts = [added(part, lax.ppermute(part, both, perm)) for part in parts]
    return collect(core, parts, [swap(part, "obs", 1) for part in parts])


def shards(spectra, enc_weight, pix_tile, pix_local, foot_weight, cotangent, adjoint, mixing):
    tile_count = lax.axis_size("pix")
    tile_rows = cotangent.shape[0]
    quarter = spectra.shape[0] // lax.axis_size("chan")
    tile = lax.axis_index("pix")
    chan = lax.axis_index("chan")
    first_row = chan * quarter
    middle = [(1, 2), (2, 1)]

    send = project(spectra, enc_weight, chan, 1)
    near = swap(send, "chan", 1)
    keep = project(spectra, enc_weight, chan, 0)
    above, below = edges(cotangent, "pix", HALO)
    anchor = tile * tile_rows - HALO
    capacity = 2 * quarter // tile_count
    if capacity >= quarter and tile_count == 2:
        lists = (pix_local, swap(pix_local, "pix", 1))
        mine, theirs = pixel_rows(
            cotangent, above, below, adjoint, mixing, anchor, lists, first_row, quarter
        )
        answers = swap(theirs, "pix", 1)
    else:
        tile_ids = lax.dynamic_slice_in_dim(pix_tile[:, 0], first_row, quarter, 0)
        local_ids = lax.dynamic_slice_in_dim(pix_local, first_row, quarter, 0)
        slot_index, wanted = requests(tile_ids, local_ids, capacity)
        (rows,) = pixel_rows(
            cotangent, above, below, adjoint, mixing, anchor, (wanted,), 0 * chan, wanted.shape[0]
        )
        answers = lax.all_to_all(
            rows.reshape(tile_count, capacity, -1), "pix", split_axis=0, concat_axis=0, tiled=True
        )
        mine = answers = jnp.take(answers.reshape(tile_count * capacity, -1), slot_index, axis=0)
    near, mine = lax.optimization_barrier((near, mine))
    passed_on = keep[quarter:].astype(jnp.float32) + near[quarter:].astype(jnp.float32)
    far = swap(passed_on.astype(jnp.bfloat16), "chan", 2)
    grads = pre_gradient(tile, chan, keep, near, far, pix_tile, foot_weight, mine, answers)

    beside = swap(grads, "chan", 1)
    across = lax.ppermute(grads, "chan", middle)
    passed = lax.ppermute(across, "chan", [(1, 0), (2, 3)])
    crossed = lax.ppermute(beside, "chan", middle)
    skipped = lax.ppermute(beside, "chan", [(2, 0), (1, 3)])
    core = lax.axis_index("obs") & 1
    early, held = early_product(spectra, chan, grads, beside)
    where = jnp.stack([chan, core])
    send, keep = late_product(where, held, early, crossed, passed, across, skipped)
    if lax.axis_size("obs") == 4 and tile_count == 2:
        return sum_over_panels(core, keep, [swap(part, "obs", 1) for part in send])
    return lax.psum(collect(core, keep, send), ("obs", "pix"))


def solution(mesh):
    return jax.shard_map(
        shards,
        mesh=mesh,
        in_specs=(
            P(("obs", "pix"), "chan"),
            P("chan", None),
            P(("obs", "pix"), None),
            P(("obs", "pix")),
            P(("obs", "pix")),
            P("pix", None),
            P(None, "pix"),
            P(),
        ),
        out_specs=P("chan", None),
        check_vma=False,
    )
```

time: 92.6 us -> 90.1 us (0.973)
  the two profiles are of different devices: /device:TPU:11 before, /device:TPU:9 now
where the time goes in v7:
time: 90.1 us; the launch traced here: 89.8 us
  waiting for transfers between devices  27.9 us (31%)
  starting transfers between devices  26.9 us (30%)
  Pallas kernels  26.2 us (29%)
  local copies, waits for them, and re-layouts  7.34 us (8%)
  other arithmetic  1.11 us (1%)
    pallas_call x1, Pallas kernels, pixel_rows(): pl.pallas_call(functools.partial(pixel_kernel, count), out_shape=(jax.Sha...  14.8 us
    ppermute x9, waiting for transfers between devices, swap(): return lax.ppermute(value, axis, [(i, i ^ bit) for i in range(size)])  13.2 us
    ppermute x9, starting transfers between devices, swap(): return lax.ppermute(value, axis, [(i, i ^ bit) for i in range(size)])  12.2 us
    unnamed x20, local copies, waits for them, and re-layouts  7.34 us
    ppermute x1, waiting for transfers between devices, shards(): crossed = lax.ppermute(beside, 'chan', middle)  6.14 us
    pallas_call x2, Pallas kernels, project(): pl.pallas_call(functools.partial(project_kernel, bits), out_shape=jax.Sha...  5.2 us
    ppermute x1, waiting for transfers between devices, shards(): across = lax.ppermute(grads, 'chan', middle)  4.41 us
    ppermute x1, starting transfers between devices, shards(): crossed = lax.ppermute(beside, 'chan', middle)  4.2 us
  transfers between devices with their start and end apart: 18, of which 11 were waited for; matrix products, arithmetic and copies ran while one was open for 1% of the time, Pallas kernels for 25%

profile of v7, /device:TPU:9, one launch (start us, length us, event | category | flops | bytes accessed | tf_op | source)
XLA Modules:
  0.0 89.8 jit_solution(9550693628345212984)
XLA Ops:
  0.0 1.2 %collective-permute-start.1 = (s32[2048]{0:T(1024)}, s32[2048]{0:T(1024)S(1)}, u32[]{:S(2)}, u32[]{:S(2)}) collective-permute-start(s32[2048]{0:T(1024)} %refs_0_.1), channel_id=1, source_target_pairs={{0,4},{4,0},{1,5},{5,1},{2,6},{6,2},{3,7},{7,3},{8,12},{12,8},{9,1... | collective-permute-start | bytes 24584 | tf_op jit(solution)/shard_map/ppermute | solution.py:45
  2.4 2.3 %copy-done = bf16[2048,1152]{1,0:T(8,128)(2,1)S(1)} copy-done((bf16[2048,1152]{1,0:T(8,128)(2,1)S(1)}, bf16[2048,1152]{1,0:T(8,128)(2,1)}, u32[]{:S(2)}) %copy-start) | copy-done | bytes 4718616
  4.8 1.1 %copy-done.2 = bf16[1152,256]{1,0:T(8,128)(2,1)S(1)} copy-done((bf16[1152,256]{1,0:T(8,128)(2,1)S(1)}, bf16[1152,256]{1,0:T(8,128)(2,1)}, u32[]{:S(2)}) %copy-start.2) | copy-done | bytes 589848
  5.8 2.6 %project.3 = bf16[1024,256]{1,0:T(8,128)(2,1)S(1)} custom-call(s32[1]{0:T(128)} %bitcast.1.chan, bf16[2048,1152]{1,0:T(8,128)(2,1)S(1)} %copy-done, bf16[1152,256]{1,0:T(8,128)(2,1)S(1)} %copy-done.2), custom_call_target="tpu_custom_call" | custom-call | flops 603979776 | bytes 3473408 | tf_op jit(solution)/shard_map/project/pallas_call | solution.py:78
  8.6 2.3 %copy-done.1 = bf16[2048,1152]{1,0:T(8,128)(2,1)S(1)} copy-done((bf16[2048,1152]{1,0:T(8,128)(2,1)S(1)}, bf16[2048,1152]{1,0:T(8,128)(2,1)}, u32[]{:S(2)}) %copy-start.1) | copy-done | bytes 4718616
  10.9 2.6 %project.2.keep = bf16[1024,256]{1,0:T(8,128)(2,1)S(1)} custom-call(s32[1]{0:T(128)} %bitcast.1.chan, bf16[2048,1152]{1,0:T(8,128)(2,1)S(1)} %copy-done.1, bf16[1152,256]{1,0:T(8,128)(2,1)S(1)} %copy-done.3), custom_call_target="tpu_custom_call" | custom-call | flops 603979776 | bytes 3473408 | tf_op jit(solution)/shard_map/project/pallas_call | solution.py:78
  13.6 1.6 %copy-done.6 = bf16[4096,256]{1,0:T(8,128)(2,1)S(1)} copy-done((bf16[4096,256]{1,0:T(8,128)(2,1)S(1)}, bf16[4096,256]{1,0:T(8,128)(2,1)}, u32[]{:S(2)}) %copy-start.6) | copy-done | bytes 2097176
  15.1 14.8 %pixel_rows.1 = (bf16[512,256]{1,0:T(8,128)(2,1)S(1)}, bf16[512,256]{1,0:T(8,128)(2,1)S(1)}) custom-call(s32[1]{0:T(128)} %bitcast.3.start, s32[8,4096]{1,0:T(8,128)S(1)} %subtract_multiply_fusion.places, s32[2048]{0:T(1024)S(1)} %copy-done.7, s32[2048]{0:T(1024)S(1)} %collective-permute-done.1.refs_1_, bf16[4096,256]{1,0:T(8,128)(2,1)S(1)} %copy-done.6, ...), custom_call_target="tpu_custom_call" | custom-call | flops 12884901888 | bytes 4194304 | tf_op jit(solution)/shard_map/pixel_rows/pallas_call | solution.py:255
  29.9 1.4 %collective-permute-start.4 = (bf16[512,256]{1,0:T(8,128)(2,1)S(1)}, bf16[512,256]{1,0:T(8,128)(2,1)S(1)}, u32[]{:S(2)}, u32[]{:S(2)}) collective-permute-start(bf16[512,256]{1,0:T(8,128)(2,1)S(1)} %get-tuple-element.18), channel_id=1, source_target_pairs={{0,4},{4,0},{1,5},{5,1},{2,6},{6,2},{3,7},{7,3},{8,12},{12,8},{9,1... | collective-permute-start | bytes 786440 | tf_op jit(solution)/shard_map/ppermute | solution.py:45
  31.4 2.4 %collective-permute-start.3 = (bf16[512,256]{1,0:T(8,128)(2,1)S(1)}, bf16[512,256]{1,0:T(8,128)(2,1)S(1)}, u32[]{:S(2)}, u32[]{:S(2)}) collective-permute-start(bf16[512,256]{1,0:T(8,128)(2,1)S(1)} %add_convert_fusion), channel_id=1, source_target_pairs={{0,2},{1,3},{2,0},{3,1},{4,6},{5,7},{6,4},{7,5},{8,10},{9,11},{10,... | collective-permute-start | bytes 786440 | tf_op jit(solution)/shard_map/ppermute | solution.py:45
  33.9 2.7 %collective-permute-done.4.answers = bf16[512,256]{1,0:T(8,128)(2,1)S(1)} collective-permute-done((bf16[512,256]{1,0:T(8,128)(2,1)S(1)}, bf16[512,256]{1,0:T(8,128)(2,1)S(1)}, u32[]{:S(2)}, u32[]{:S(2)}) %collective-permute-start.4) | collective-permute-done | bytes 262176 | tf_op jit(solution)/shard_map/ppermute | solution.py:45
  36.6 7.8 %collective-permute-done.3.far = bf16[512,256]{1,0:T(8,128)(2,1)S(1)} collective-permute-done((bf16[512,256]{1,0:T(8,128)(2,1)S(1)}, bf16[512,256]{1,0:T(8,128)(2,1)S(1)}, u32[]{:S(2)}, u32[]{:S(2)}) %collective-permute-start.3) | collective-permute-done | bytes 262176 | tf_op jit(solution)/shard_map/ppermute | solution.py:45
  44.4 1.0 %pre_gradient.1.first = bf16[512,256]{1,0:T(8,128)(2,1)S(1)} custom-call(s32[2]{0:T(128)S(1)} %pad_add_fusion.1.where, bf16[1024,256]{1,0:T(8,128)(2,1)S(1)} %project.2.keep, bf16[1024,256]{1,0:T(8,128)(2,1)S(1)} %collective-permute-done.near, bf16[512,256]{1,0:T(8,128)(2,1)S(1)} %collective-permute-done.3.far, s32[16,128]{1,0:T(8,128)S(1)} %bitcast.6, ...), custom_call_target="tpu_custom_call" | custom-call | tf_op jit(solution)/shard_map/pre_gradient/pallas_call | solution.py:319
  45.4 3.0 %collective-permute-start.7 = (bf16[512,256]{1,0:T(8,128)(2,1)S(1)}, bf16[512,256]{1,0:T(8,128)(2,1)S(1)}, u32[]{:S(2)}, u32[]{:S(2)}) collective-permute-start(bf16[512,256]{1,0:T(8,128)(2,1)S(1)} %pre_gradient.1.first), channel_id=1, source_target_pairs={{1,2},{2,1},{5,6},{6,5},{9,10},{10,9},{13,14},{14,13},{17,18},{18,... | collective-permute-start | bytes 786440 | tf_op jit(solution)/shard_map/ppermute | solution.py:416
  49.2 4.4 %collective-permute-done.7.across = bf16[512,256]{1,0:T(8,128)(2,1)S(1)} collective-permute-done((bf16[512,256]{1,0:T(8,128)(2,1)S(1)}, bf16[512,256]{1,0:T(8,128)(2,1)S(1)}, u32[]{:S(2)}, u32[]{:S(2)}) %collective-permute-start.7) | collective-permute-done | bytes 262176 | tf_op jit(solution)/shard_map/ppermute | solution.py:416
  53.6 1.3 %collective-permute-start.8 = (bf16[512,256]{1,0:T(8,128)(2,1)S(1)}, bf16[512,256]{1,0:T(8,128)(2,1)S(1)}, u32[]{:S(2)}, u32[]{:S(2)}) collective-permute-start(bf16[512,256]{1,0:T(8,128)(2,1)S(1)} %collective-permute-done.7.across), channel_id=1, source_target_pairs={{1,0},{2,3},{5,4},{6,7},{9,8},{10,11},{13,12},{14,15},{17,16},{18,... | collective-permute-start | bytes 786440 | tf_op jit(solution)/shard_map/ppermute | solution.py:417
  55.6 1.8 %collective-permute-start.9 = (bf16[512,256]{1,0:T(8,128)(2,1)S(1)}, bf16[512,256]{1,0:T(8,128)(2,1)S(1)}, u32[]{:S(2)}, u32[]{:S(2)}) collective-permute-start(bf16[512,256]{1,0:T(8,128)(2,1)S(1)} %collective-permute-done.5.second), channel_id=1, source_target_pairs={{2,0},{1,3},{6,4},{5,7},{10,8},{9,11},{14,12},{13,15},{18,16},{17,... | collective-permute-start | bytes 786440 | tf_op jit(solution)/shard_map/ppermute | solution.py:419
  57.4 4.2 %collective-permute-start.6 = (bf16[512,256]{1,0:T(8,128)(2,1)S(1)}, bf16[512,256]{1,0:T(8,128)(2,1)S(1)}, u32[]{:S(2)}, u32[]{:S(2)}) collective-permute-start(bf16[512,256]{1,0:T(8,128)(2,1)S(1)} %collective-permute-done.5.second), channel_id=1, source_target_pairs={{1,2},{2,1},{5,6},{6,5},{9,10},{10,9},{13,14},{14,13},{17,18},{18,... | collective-permute-start | bytes 786440 | tf_op jit(solution)/shard_map/ppermute | solution.py:418
  61.7 2.5 %early_product.1 = (f32[1152,256]{1,0:T(8,128)S(1)}, bf16[1024,1152]{1,0:T(8,128)(2,1)S(1)}) custom-call(s32[1]{0:T(128)} %bitcast.1.chan, bf16[2048,1152]{1,0:T(8,128)(2,1)} %spectra.5, bf16[512,256]{1,0:T(8,128)(2,1)S(1)} %pre_gradient.1.first, bf16[512,256]{1,0:T(8,128)(2,1)S(1)} %collective-permute-done.5.second), custom_call_target="tpu_custom_call" | custom-call | flops 603979776 | bytes 5898240 | tf_op jit(solution)/shard_map/early_product/pallas_call | solution.py:125
  64.2 6.1 %collective-permute-done.6.crossed = bf16[512,256]{1,0:T(8,128)(2,1)S(1)} collective-permute-done((bf16[512,256]{1,0:T(8,128)(2,1)S(1)}, bf16[512,256]{1,0:T(8,128)(2,1)S(1)}, u32[]{:S(2)}, u32[]{:S(2)}) %collective-permute-start.6) | collective-permute-done | bytes 262176 | tf_op jit(solution)/shard_map/ppermute | solution.py:418
  70.4 1.4 %late_product.1 = (bf16[288,256]{1,0:T(8,128)(2,1)S(1)}, bf16[288,256]{1,0:T(8,128)(2,1)S(1)}, f32[288,256]{1,0:T(8,128)S(1)}, f32[288,256]{1,0:T(8,128)S(1)}) custom-call(s32[2]{0:T(128)S(1)} %pad_add_fusion.where, bf16[1024,1152]{1,0:T(8,128)(2,1)S(1)} %get-tuple-element.19.held, f32[1152,256]{1,0:T(8,128)S(1)} %get-tuple-element.20.before, ...), custom_call_target="tpu_custom_call" | custom-call | flops 603979776 | bytes 3538944 | tf_op jit(solution)/shard_map/late_product/pallas_call | solution.py:172
  71.8 2.3 %collective-permute-start.10 = (bf16[288,256]{1,0:T(8,128)(2,1)S(1)}, bf16[288,256]{1,0:T(8,128)(2,1)S(1)}, u32[]{:S(2)}, u32[]{:S(2)}) collective-permute-start(bf16[288,256]{1,0:T(8,128)(2,1)S(1)} %get-tuple-element.22), channel_id=1, source_target_pairs={{0,8},{8,0},{16,24},{24,16},{1,9},{9,1},{17,25},{25,17},{2,10},{10... | collective-permute-start | bytes 442376 | tf_op jit(solution)/shard_map/ppermute | solution.py:45
  74.2 0.9 %collective-permute-done.10.second = bf16[288,256]{1,0:T(8,128)(2,1)S(1)} collective-permute-done((bf16[288,256]{1,0:T(8,128)(2,1)S(1)}, bf16[288,256]{1,0:T(8,128)(2,1)S(1)}, u32[]{:S(2)}, u32[]{:S(2)}) %collective-permute-start.10) | collective-permute-done | bytes 147488 | tf_op jit(solution)/shard_map/ppermute | solution.py:45
  75.5 1.3 %collective-permute-start.14 = (bf16[288,256]{1,0:T(8,128)(2,1)S(1)}, bf16[288,256]{1,0:T(8,128)(2,1)S(1)}, u32[]{:S(2)}, u32[]{:S(2)}) collective-permute-start(bf16[288,256]{1,0:T(8,128)(2,1)S(1)} %added.9.first), channel_id=1, source_target_pairs={{0,16},{4,20},{8,12},{12,8},{16,0},{20,4},{24,28},{28,24},{1,17},{... | collective-permute-start | bytes 442376 | tf_op jit(solution)/shard_map/ppermute | solution.py:374
  76.8 2.7 %collective-permute-done.11.second = bf16[288,256]{1,0:T(8,128)(2,1)S(1)} collective-permute-done((bf16[288,256]{1,0:T(8,128)(2,1)S(1)}, bf16[288,256]{1,0:T(8,128)(2,1)S(1)}, u32[]{:S(2)}, u32[]{:S(2)}) %collective-permute-start.11) | collective-permute-done | bytes 147488 | tf_op jit(solution)/shard_map/ppermute | solution.py:374
  79.6 1.3 %collective-permute-start.12 = (bf16[288,256]{1,0:T(8,128)(2,1)S(1)}, bf16[288,256]{1,0:T(8,128)(2,1)S(1)}, u32[]{:S(2)}, u32[]{:S(2)}) collective-permute-start(bf16[288,256]{1,0:T(8,128)(2,1)S(1)} %added.7.first), channel_id=1, source_target_pairs={{0,4},{4,0},{8,24},{12,28},{16,20},{20,16},{24,8},{28,12},{1,5},{5... | collective-permute-start | bytes 442376 | tf_op jit(solution)/shard_map/ppermute | solution.py:374
  81.1 1.3 %collective-permute-start.15 = (bf16[288,256]{1,0:T(8,128)(2,1)S(1)}, bf16[288,256]{1,0:T(8,128)(2,1)S(1)}, u32[]{:S(2)}, u32[]{:S(2)}) collective-permute-start(bf16[288,256]{1,0:T(8,128)(2,1)S(1)} %added.10.first), channel_id=1, source_target_pairs={{0,4},{4,0},{8,24},{12,28},{16,20},{20,16},{24,8},{28,12},{1,5},{5... | collective-permute-start | bytes 442376 | tf_op jit(solution)/shard_map/ppermute | solution.py:374
  82.4 1.2 %collective-permute-done.12.second = bf16[288,256]{1,0:T(8,128)(2,1)S(1)} collective-permute-done((bf16[288,256]{1,0:T(8,128)(2,1)S(1)}, bf16[288,256]{1,0:T(8,128)(2,1)S(1)}, u32[]{:S(2)}, u32[]{:S(2)}) %collective-permute-start.12) | collective-permute-done | bytes 147488 | tf_op jit(solution)/shard_map/ppermute | solution.py:374
  83.7 2.4 %collective-permute-start.16 = (bf16[288,256]{1,0:T(8,128)(2,1)S(1)}, bf16[288,256]{1,0:T(8,128)(2,1)S(1)}, u32[]{:S(2)}, u32[]{:S(2)}) collective-permute-start(bf16[288,256]{1,0:T(8,128)(2,1)S(1)} %added.8.refs_0_), channel_id=1, source_target_pairs={{0,8},{8,0},{16,24},{24,16},{1,9},{9,1},{17,25},{25,17},{2,10},{10... | collective-permute-start | bytes 442376 | tf_op jit(solution)/shard_map/ppermute | solution.py:45
  86.1 1.6 %collective-permute-start.17 = (bf16[288,256]{1,0:T(8,128)(2,1)S(1)}, bf16[288,256]{1,0:T(8,128)(2,1)S(1)}, u32[]{:S(2)}, u32[]{:S(2)}) collective-permute-start(bf16[288,256]{1,0:T(8,128)(2,1)S(1)} %added.11.refs_1_), channel_id=1, source_target_pairs={{0,8},{8,0},{16,24},{24,16},{1,9},{9,1},{17,25},{25,17},{2,10},{10... | collective-permute-start | bytes 442376 | tf_op jit(solution)/shard_map/ppermute | solution.py:45
  87.7 1.0 %collective-permute-done.17.refs_3_ = bf16[288,256]{1,0:T(8,128)(2,1)S(1)} collective-permute-done((bf16[288,256]{1,0:T(8,128)(2,1)S(1)}, bf16[288,256]{1,0:T(8,128)(2,1)S(1)}, u32[]{:S(2)}, u32[]{:S(2)}) %collective-permute-start.17) | collective-permute-done | bytes 147488 | tf_op jit(solution)/shard_map/ppermute | solution.py:45
  88.7 1.1 %collect.1 = f32[1152,256]{1,0:T(8,128)} custom-call(s32[1]{0:T(128)} %bitcast.core, bf16[288,256]{1,0:T(8,128)(2,1)S(1)} %added.8.refs_0_, bf16[288,256]{1,0:T(8,128)(2,1)S(1)} %added.11.refs_1_, bf16[288,256]{1,0:T(8,128)(2,1)S(1)} %collective-permute-done.16.refs_2_, bf16[288,256]{1,0:T(8,128)(2,1)S(1)} %collective-permute-done.17.refs_3_), custom_call_target="tpu_custom_call" | custom-call | tf_op jit(solution)/shard_map/collect/pallas_call | solution.py:343
  (42 shorter events, 3.8 us)
Async XLA Ops:
  0.0 13.5 %collective-permute-start.1 = (s32[2048]{0:T(1024)}, s32[2048]{0:T(1024)S(1)}, u32[]{:S(2)}, u32[]{:S(2)}) collective-permute-start(s32[2048]{0:T(1024)} %refs_0_.1), channel_id=1, source_target_pairs={{0,4},{4,0},{1,5},{5,1},{2,6},{6,2},{3,7},{7,3},{8,12},{12,8},{9,1... | collective-permute-start | bytes 24584 | tf_op jit(solution)/shard_map/ppermute | solution.py:45
  2.1 11.4 %collective-permute-start.2 = (bf16[128,256]{1,0:T(8,128)(2,1)S(1)}, bf16[128,256]{1,0:T(8,128)(2,1)S(1)}, u32[]{:S(2)}, u32[]{:S(2)}) collective-permute-start(bf16[128,256]{1,0:T(8,128)(2,1)S(1)} %slice_select_fusion), channel_id=1, source_target_pairs={{0,4},{4,0},{1,5},{5,1},{2,6},{6,2},{3,7},{7,3},{8,12},{12,8},{9,1... | collective-permute-start | bytes 196616 | tf_op jit(solution)/shard_map/ppermute | solution.py:22
  2.4 2.3 %copy-start = (bf16[2048,1152]{1,0:T(8,128)(2,1)S(1)}, bf16[2048,1152]{1,0:T(8,128)(2,1)}, u32[]{:S(2)}) copy-start(bf16[2048,1152]{1,0:T(8,128)(2,1)} %spectra.5) | copy-start | bytes 14155780
  4.8 1.1 %copy-start.2 = (bf16[1152,256]{1,0:T(8,128)(2,1)S(1)}, bf16[1152,256]{1,0:T(8,128)(2,1)}, u32[]{:S(2)}) copy-start(bf16[1152,256]{1,0:T(8,128)(2,1)} %weight.3) | copy-start | bytes 1769476
  5.8 2.7 %copy-start.9 = (s32[8,4096]{1,0:T(8,128)S(1)}, s32[8,4096]{1,0:T(8,128)}, u32[]{:S(2)}) copy-start(s32[8,4096]{1,0:T(8,128)} %param.14) | copy-start | bytes 393220
  5.8 2.7 %copy-start.3 = (bf16[1152,256]{1,0:T(8,128)(2,1)S(1)}, bf16[1152,256]{1,0:T(8,128)(2,1)}, u32[]{:S(2)}) copy-start(bf16[1152,256]{1,0:T(8,128)(2,1)} %weight.3) | copy-start | bytes 1769476
  8.4 22.9 %collective-permute-start = (bf16[1024,256]{1,0:T(8,128)(2,1)S(1)}, bf16[1024,256]{1,0:T(8,128)(2,1)S(1)}, u32[]{:S(2)}, u32[]{:S(2)}) collective-permute-start(bf16[1024,256]{1,0:T(8,128)(2,1)S(1)} %project.3), channel_id=1, source_target_pairs={{0,1},{1,0},{2,3},{3,2},{4,5},{5,4},{6,7},{7,6},{8,9},{9,8},{10,11... | collective-permute-start | bytes 1572872 | tf_op jit(solution)/shard_map/ppermute | solution.py:45
  8.6 2.3 %copy-start.1 = (bf16[2048,1152]{1,0:T(8,128)(2,1)S(1)}, bf16[2048,1152]{1,0:T(8,128)(2,1)}, u32[]{:S(2)}) copy-start(bf16[2048,1152]{1,0:T(8,128)(2,1)} %spectra.5) | copy-start | bytes 14155780
  10.9 2.6 %copy-start.7 = (s32[2048]{0:T(1024)S(1)}, s32[2048]{0:T(1024)}, u32[]{:S(2)}) copy-start(s32[2048]{0:T(1024)} %refs_0_.1) | copy-start | bytes 24580
  10.9 2.6 %copy-start.8 = (f32[8,256]{1,0:T(8,128)S(1)}, f32[8,256]{1,0:T(8,128)}, u32[]{:S(2)}) copy-start(f32[8,256]{1,0:T(8,128)} %refs_5_.1) | copy-start | bytes 24580
  13.5 1.6 %copy-start.6 = (bf16[4096,256]{1,0:T(8,128)(2,1)S(1)}, bf16[4096,256]{1,0:T(8,128)(2,1)}, u32[]{:S(2)}) copy-start(bf16[4096,256]{1,0:T(8,128)(2,1)} %refs_2_.1) | copy-start | bytes 6291460
  15.1 29.2 %copy-start.4 = (s32[2048,1]{0,1:T(1,128)S(1)}, s32[2048,1]{0,1:T(1,128)}, u32[]{:S(2)}) copy-start(s32[2048,1]{0,1:T(1,128)} %param.10) | copy-start | bytes 24580
  15.1 29.2 %copy-start.5 = (f32[2048]{0:T(1024)S(1)}, f32[2048]{0:T(1024)}, u32[]{:S(2)}) copy-start(f32[2048]{0:T(1024)} %param.12) | copy-start | bytes 24580
  29.9 6.6 %collective-permute-start.4 = (bf16[512,256]{1,0:T(8,128)(2,1)S(1)}, bf16[512,256]{1,0:T(8,128)(2,1)S(1)}, u32[]{:S(2)}, u32[]{:S(2)}) collective-permute-start(bf16[512,256]{1,0:T(8,128)(2,1)S(1)} %get-tuple-element.18), channel_id=1, source_target_pairs={{0,4},{4,0},{1,5},{5,1},{2,6},{6,2},{3,7},{7,3},{8,12},{12,8},{9,1... | collective-permute-start | bytes 786440 | tf_op jit(solution)/shard_map/ppermute | solution.py:45
  31.4 12.9 %collective-permute-start.3 = (bf16[512,256]{1,0:T(8,128)(2,1)S(1)}, bf16[512,256]{1,0:T(8,128)(2,1)S(1)}, u32[]{:S(2)}, u32[]{:S(2)}) collective-permute-start(bf16[512,256]{1,0:T(8,128)(2,1)S(1)} %add_convert_fusion), channel_id=1, source_target_pairs={{0,2},{1,3},{2,0},{3,1},{4,6},{5,7},{6,4},{7,5},{8,10},{9,11},{10,... | collective-permute-start | bytes 786440 | tf_op jit(solution)/shard_map/ppermute | solution.py:45
  45.4 8.2 %collective-permute-start.7 = (bf16[512,256]{1,0:T(8,128)(2,1)S(1)}, bf16[512,256]{1,0:T(8,128)(2,1)S(1)}, u32[]{:S(2)}, u32[]{:S(2)}) collective-permute-start(bf16[512,256]{1,0:T(8,128)(2,1)S(1)} %pre_gradient.1.first), channel_id=1, source_target_pairs={{1,2},{2,1},{5,6},{6,5},{9,10},{10,9},{13,14},{14,13},{17,18},{18,... | collective-permute-start | bytes 786440 | tf_op jit(solution)/shard_map/ppermute | solution.py:416
  48.5 7.1 %collective-permute-start.5 = (bf16[512,256]{1,0:T(8,128)(2,1)S(1)}, bf16[512,256]{1,0:T(8,128)(2,1)S(1)}, u32[]{:S(2)}, u32[]{:S(2)}) collective-permute-start(bf16[512,256]{1,0:T(8,128)(2,1)S(1)} %pre_gradient.1.first), channel_id=1, source_target_pairs={{0,1},{1,0},{2,3},{3,2},{4,5},{5,4},{6,7},{7,6},{8,9},{9,8},{10,11... | collective-permute-start | bytes 786440 | tf_op jit(solution)/shard_map/ppermute | solution.py:45
  53.6 10.6 %collective-permute-start.8 = (bf16[512,256]{1,0:T(8,128)(2,1)S(1)}, bf16[512,256]{1,0:T(8,128)(2,1)S(1)}, u32[]{:S(2)}, u32[]{:S(2)}) collective-permute-start(bf16[512,256]{1,0:T(8,128)(2,1)S(1)} %collective-permute-done.7.across), channel_id=1, source_target_pairs={{1,0},{2,3},{5,4},{6,7},{9,8},{10,11},{13,12},{14,15},{17,16},{18,... | collective-permute-start | bytes 786440 | tf_op jit(solution)/shard_map/ppermute | solution.py:417
  55.6 8.6 %collective-permute-start.9 = (bf16[512,256]{1,0:T(8,128)(2,1)S(1)}, bf16[512,256]{1,0:T(8,128)(2,1)S(1)}, u32[]{:S(2)}, u32[]{:S(2)}) collective-permute-start(bf16[512,256]{1,0:T(8,128)(2,1)S(1)} %collective-permute-done.5.second), channel_id=1, source_target_pairs={{2,0},{1,3},{6,4},{5,7},{10,8},{9,11},{14,12},{13,15},{18,16},{17,... | collective-permute-start | bytes 786440 | tf_op jit(solution)/shard_map/ppermute | solution.py:419
  57.4 13.0 %collective-permute-start.6 = (bf16[512,256]{1,0:T(8,128)(2,1)S(1)}, bf16[512,256]{1,0:T(8,128)(2,1)S(1)}, u32[]{:S(2)}, u32[]{:S(2)}) collective-permute-start(bf16[512,256]{1,0:T(8,128)(2,1)S(1)} %collective-permute-done.5.second), channel_id=1, source_target_pairs={{1,2},{2,1},{5,6},{6,5},{9,10},{10,9},{13,14},{14,13},{17,18},{18,... | collective-permute-start | bytes 786440 | tf_op jit(solution)/shard_map/ppermute | solution.py:418
  71.8 3.3 %collective-permute-start.10 = (bf16[288,256]{1,0:T(8,128)(2,1)S(1)}, bf16[288,256]{1,0:T(8,128)(2,1)S(1)}, u32[]{:S(2)}, u32[]{:S(2)}) collective-permute-start(bf16[288,256]{1,0:T(8,128)(2,1)S(1)} %get-tuple-element.22), channel_id=1, source_target_pairs={{0,8},{8,0},{16,24},{24,16},{1,9},{9,1},{17,25},{25,17},{2,10},{10... | collective-permute-start | bytes 442376 | tf_op jit(solution)/shard_map/ppermute | solution.py:45
  74.1 1.4 %collective-permute-start.13 = (bf16[288,256]{1,0:T(8,128)(2,1)S(1)}, bf16[288,256]{1,0:T(8,128)(2,1)S(1)}, u32[]{:S(2)}, u32[]{:S(2)}) collective-permute-start(bf16[288,256]{1,0:T(8,128)(2,1)S(1)} %get-tuple-element.24), channel_id=1, source_target_pairs={{0,8},{8,0},{16,24},{24,16},{1,9},{9,1},{17,25},{25,17},{2,10},{10... | collective-permute-start | bytes 442376 | tf_op jit(solution)/shard_map/ppermute | solution.py:45
  75.2 4.4 %collective-permute-start.11 = (bf16[288,256]{1,0:T(8,128)(2,1)S(1)}, bf16[288,256]{1,0:T(8,128)(2,1)S(1)}, u32[]{:S(2)}, u32[]{:S(2)}) collective-permute-start(bf16[288,256]{1,0:T(8,128)(2,1)S(1)} %added.6.first), channel_id=1, source_target_pairs={{0,16},{4,20},{8,12},{12,8},{16,0},{20,4},{24,28},{28,24},{1,17},{... | collective-permute-start | bytes 442376 | tf_op jit(solution)/shard_map/ppermute | solution.py:374
  75.5 5.6 %collective-permute-start.14 = (bf16[288,256]{1,0:T(8,128)(2,1)S(1)}, bf16[288,256]{1,0:T(8,128)(2,1)S(1)}, u32[]{:S(2)}, u32[]{:S(2)}) collective-permute-start(bf16[288,256]{1,0:T(8,128)(2,1)S(1)} %added.9.first), channel_id=1, source_target_pairs={{0,16},{4,20},{8,12},{12,8},{16,0},{20,4},{24,28},{28,24},{1,17},{... | collective-permute-start | bytes 442376 | tf_op jit(solution)/shard_map/ppermute | solution.py:374
  79.6 4.1 %collective-permute-start.12 = (bf16[288,256]{1,0:T(8,128)(2,1)S(1)}, bf16[288,256]{1,0:T(8,128)(2,1)S(1)}, u32[]{:S(2)}, u32[]{:S(2)}) collective-permute-start(bf16[288,256]{1,0:T(8,128)(2,1)S(1)} %added.7.first), channel_id=1, source_target_pairs={{0,4},{4,0},{8,24},{12,28},{16,20},{20,16},{24,8},{28,12},{1,5},{5... | collective-permute-start | bytes 442376 | tf_op jit(solution)/shard_map/ppermute | solution.py:374
  81.1 5.0 %collective-permute-start.15 = (bf16[288,256]{1,0:T(8,128)(2,1)S(1)}, bf16[288,256]{1,0:T(8,128)(2,1)S(1)}, u32[]{:S(2)}, u32[]{:S(2)}) collective-permute-start(bf16[288,256]{1,0:T(8,128)(2,1)S(1)} %added.10.first), channel_id=1, source_target_pairs={{0,4},{4,0},{8,24},{12,28},{16,20},{20,16},{24,8},{28,12},{1,5},{5... | collective-permute-start | bytes 442376 | tf_op jit(solution)/shard_map/ppermute | solution.py:374
  83.7 4.0 %collective-permute-start.16 = (bf16[288,256]{1,0:T(8,128)(2,1)S(1)}, bf16[288,256]{1,0:T(8,128)(2,1)S(1)}, u32[]{:S(2)}, u32[]{:S(2)}) collective-permute-start(bf16[288,256]{1,0:T(8,128)(2,1)S(1)} %added.8.refs_0_), channel_id=1, source_target_pairs={{0,8},{8,0},{16,24},{24,16},{1,9},{9,1},{17,25},{25,17},{2,10},{10... | collective-permute-start | bytes 442376 | tf_op jit(solution)/shard_map/ppermute | solution.py:45
  86.1 2.6 %collective-permute-start.17 = (bf16[288,256]{1,0:T(8,128)(2,1)S(1)}, bf16[288,256]{1,0:T(8,128)(2,1)S(1)}, u32[]{:S(2)}, u32[]{:S(2)}) collective-permute-start(bf16[288,256]{1,0:T(8,128)(2,1)S(1)} %added.11.refs_1_), channel_id=1, source_target_pairs={{0,8},{8,0},{16,24},{24,16},{1,9},{9,1},{17,25},{25,17},{2,10},{10... | collective-permute-start | bytes 442376 | tf_op jit(solution)/shard_map/ppermute | solution.py:45

commit v8 on v7

--- a/solution.py
+++ b/solution.py
@@ -10,7 +10,7 @@
 NEIGH = 8
 HALO = 128
 MIB = 1024 * 1024
-LARGE = 48
+LARGE = 52
 
 
 def edges(value, axis, width):
@@ -49,11 +49,11 @@
     return pltpu.CompilerParams(vmem_limit_bytes=mib * MIB)
 
 
-def project_kernel(bits, chan, spectra, weight, out, held, near, sems):
-    chunk = out.shape[0] // 4
+def quarter_copies(spectra, weight, held, near, sems, chan, bits):
+    chunk = held.shape[0] // 4
     copies = [pltpu.make_async_copy(weight, near, sems.at[4])]
     for turn in range(4):
-        first = ((chan[0] ^ bits ^ (turn // 2 * 2)) * 2 + turn % 2) * chunk
+        first = ((chan ^ bits ^ (turn // 2 * 2)) * 2 + turn % 2) * chunk
         copies.append(
             pltpu.make_async_copy(
                 spectra.at[pl.ds(pl.multiple_of(first, chunk), chunk)],
@@ -61,8 +61,11 @@
                 sems.at[turn],
             )
         )
-    for copy in copies:
-        copy.start()
+    return copies
+
+
+def project_rows(copies, held, near, out):
+    chunk = held.shape[0] // 4
     copies[0].wait()
     for turn in range(4):
         copies[turn + 1].wait()
@@ -71,12 +74,19 @@
         out[rows, :] = result.astype(out.dtype)
 
 
-def project(spectra, weight, chan, bits):
+def project_kernel(chan, spectra, weight, out, held, near, sems):
+    copies = quarter_copies(spectra, weight, held, near, sems, chan[0], 1)
+    for copy in copies:
+        copy.start()
+    project_rows(copies, held, near, out)
+
+
+def project(spectra, weight, chan):
     depth, width = weight.shape
     rows = spectra.shape[0] // 2
     hbm = pl.BlockSpec(memory_space=pltpu.HBM)
     return pl.pallas_call(
-        functools.partial(project_kernel, bits),
+        project_kernel,
         out_shape=jax.ShapeDtypeStruct((rows, width), jnp.bfloat16),
         in_specs=[pl.BlockSpec(memory_space=pltpu.SMEM), hbm, hbm],
         out_specs=pl.BlockSpec(memory_space=pltpu.VMEM),
@@ -139,7 +149,7 @@
             pltpu.VMEM((2 * rows, depth), jnp.bfloat16),
             pltpu.SemaphoreType.DMA((4,)),
         ],
-        compiler_params=memory(LARGE),
+        compiler_params=memory(48),
         cost_estimate=pl.CostEstimate(
             flops=4 * rows * depth * width,
             bytes_accessed=8 * rows * depth + 4 * depth * width,
@@ -186,22 +196,31 @@
     return outs[:2], outs[2:]
 
 
-def pixel_kernel(count, start, places, *refs):
-    lists = refs[: len(refs) // 2 - 5]
-    cotangent, above, below, mixing = refs[len(lists) : len(lists) + 4]
-    outs = refs[len(lists) + 4 : 2 * len(lists) + 4]
-    table, scale, sums, held, near, sems = refs[2 * len(lists) + 4 :]
+def pixel_kernel(count, where, places, *refs):
+    lists = refs[: (len(refs) - 16) // 3]
+    names = refs[-len(lists) :]
+    refs = refs[len(lists) : -len(lists)]
+    cotangent, above, below, mixing, spectra, weight, keep = refs[:7]
+    outs = refs[7 : 7 + len(lists)]
+    table, scale, sums, held, near, block, factor, sems, more = refs[7 + len(lists) :]
+    start, chan = where[0], where[1]
     tile_rows, half = held.shape[0], table.shape[1]
     chunk = tile_rows // 4
-    copies = [
+    copies = [pltpu.make_async_copy(places, near, sems.at[4])]
+    copies += [
+        pltpu.make_async_copy(wanted, name, sems.at[5 + n])
+        for n, (wanted, name) in enumerate(zip(lists, names))
+    ]
+    parts = quarter_copies(spectra, weight, block, factor, more, chan, 0)
+    rows = [
         pltpu.make_async_copy(
             cotangent.at[pl.ds(n * chunk, chunk)], held.at[pl.ds(n * chunk, chunk)], sems.at[n]
         )
         for n in range(4)
     ]
-    copies.append(pltpu.make_async_copy(places, near, sems.at[4]))
-    for copy in copies:
+    for copy in copies + parts + rows:
         copy.start()
+    project_rows(parts, block, factor, keep)
 
     def fill(first, values):
         values = values.astype(jnp.float32)
@@ -216,22 +235,25 @@
     fill(0, above[...])
     fill(HALO + tile_rows, below[...])
     for n in range(4):
-        copies[n].wait()
+        rows[n].wait()
         for first in range(n * chunk, (n + 1) * chunk, 256):
             fill(HALO + first, held[first : first + 256, :])
-    copies[4].wait()
+    for copy in copies:
+        copy.wait()
 
     group = 16
-    for index, wanted in enumerate(lists):
+    for index, wanted in enumerate(names):
 
         def body(turn, carry, index=index, wanted=wanted):
             base = turn * group
             totals = []
             for n in range(group):
-                pixel = wanted[start[0] + base + n]
+                pixel = wanted[start + base + n]
                 terms = [table[pl.ds(2 * (pixel + HALO), 2), :]]
-                for k in range(NEIGH):
-                    terms.append(table[pl.ds(near[k, pixel], 2), :] * scales[k])
+                for k in range(NEIGH // 2):
+                    pair = near[k * tile_rows + pixel]
+                    for place, scale in ((pair & 0xFFFF, k), (pair >> 16, k + NEIGH // 2)):
+                        terms.append(table[pl.ds(place, 2), :] * scales[scale])
                 while len(terms) > 1:
                     pairs = [x + y for x, y in zip(terms[::2], terms[1::2])]
                     terms = pairs + terms[len(terms) // 2 * 2 :]
@@ -248,28 +270,43 @@
             ].astype(out.dtype)
 
 
-def pixel_rows(cotangent, above, below, adjoint, mixing, anchor, lists, start, count):
+def pixel_rows(
+    cotangent, above, below, adjoint, mixing, anchor, lists, start, count, spectra, weight, chan
+):
     tile_rows, width = cotangent.shape
-    smem = pl.BlockSpec(memory_space=pltpu.SMEM)
+    depth, rows = spectra.shape[1], spectra.shape[0] // 2
+    places = (adjoint - anchor) * 2
+    places = (places[: NEIGH // 2] | (places[NEIGH // 2 :] << 16)).reshape(-1)
+    anywhere = pl.BlockSpec(memory_space=pl.ANY)
+    hbm = pl.BlockSpec(memory_space=pltpu.HBM)
     vmem = pl.BlockSpec(memory_space=pltpu.VMEM)
     return pl.pallas_call(
         functools.partial(pixel_kernel, count),
-        out_shape=(jax.ShapeDtypeStruct((count, width), jnp.bfloat16),) * len(lists),
+        out_shape=(
+            jax.ShapeDtypeStruct((rows, width), jnp.bfloat16),
+            *[jax.ShapeDtypeStruct((count, width), jnp.bfloat16)] * len(lists),
+        ),
         in_specs=[
-            smem,
-            pl.BlockSpec(memory_space=pl.ANY),
-            *[smem] * len(lists),
-            pl.BlockSpec(memory_space=pltpu.HBM),
+            pl.BlockSpec(memory_space=pltpu.SMEM),
+            anywhere,
+            *[anywhere] * len(lists),
+            hbm,
             *[vmem] * 3,
+            hbm,
+            hbm,
         ],
-        out_specs=(vmem,) * len(lists),
+        out_specs=(vmem,) * (1 + len(lists)),
         scratch_shapes=[
             pltpu.VMEM((2 * (tile_rows + 2 * HALO), width // 2), jnp.float32),
             pltpu.VMEM((2 * NEIGH, width // 2), jnp.float32),
             pltpu.VMEM((2 * count * len(lists), width // 2), jnp.float32),
             pltpu.VMEM(cotangent.shape, cotangent.dtype),
-            pltpu.SMEM(adjoint.shape, jnp.int32),
+            pltpu.SMEM(places.shape, jnp.int32),
+            pltpu.VMEM((rows, depth), jnp.bfloat16),
+            pltpu.VMEM((depth, width), jnp.bfloat16),
+            pltpu.SemaphoreType.DMA((5 + len(lists),)),
             pltpu.SemaphoreType.DMA((5,)),
+            *[pltpu.SMEM(names.shape, jnp.int32) for names in lists],
         ],
         compiler_params=memory(LARGE),
         cost_estimate=pl.CostEstimate(
@@ -278,7 +315,9 @@
             transcendentals=0,
         ),
         name="pixel_rows",
-    )(start.reshape(1), (adjoint - anchor) * 2, *lists, cotangent, above, below, mixing)
+    )(
+        jnp.stack([start, chan]), places, *lists, cotangent, above, below, mixing, spectra, weight
+    )
 
 
 def gradient_kernel(where, keep, near, far, tiles, weights, mine, answers, out):
@@ -384,25 +423,24 @@
     first_row = chan * quarter
     middle = [(1, 2), (2, 1)]
 
-    send = project(spectra, enc_weight, chan, 1)
+    send = project(spectra, enc_weight, chan)
+    send, pix_local, edge_rows = lax.optimization_barrier((send, pix_local, cotangent))
     near = swap(send, "chan", 1)
-    keep = project(spectra, enc_weight, chan, 0)
-    above, below = edges(cotangent, "pix", HALO)
+
+    above, below = edges(edge_rows, "pix", HALO)
     anchor = tile * tile_rows - HALO
     capacity = 2 * quarter // tile_count
+    pixels = (cotangent, above, below, adjoint, mixing, anchor)
+    rest = (spectra, enc_weight, chan)
     if capacity >= quarter and tile_count == 2:
         lists = (pix_local, swap(pix_local, "pix", 1))
-        mine, theirs = pixel_rows(
-            cotangent, above, below, adjoint, mixing, anchor, lists, first_row, quarter
-        )
+        keep, mine, theirs = pixel_rows(*pixels, lists, first_row, quarter, *rest)
         answers = swap(theirs, "pix", 1)
     else:
         tile_ids = lax.dynamic_slice_in_dim(pix_tile[:, 0], first_row, quarter, 0)
         local_ids = lax.dynamic_slice_in_dim(pix_local, first_row, quarter, 0)
         slot_index, wanted = requests(tile_ids, local_ids, capacity)
-        (rows,) = pixel_rows(
-            cotangent, above, below, adjoint, mixing, anchor, (wanted,), 0 * chan, wanted.shape[0]
-        )
+        keep, rows = pixel_rows(*pixels, (wanted,), 0 * chan, wanted.shape[0], *rest)
         answers = lax.all_to_all(
             rows.reshape(tile_count, capacity, -1), "pix", split_axis=0, concat_axis=0, tiled=True
         )

time: 90.1 us -> 80.8 us (0.90)
  the two profiles are of different devices: /device:TPU:9 before, /device:TPU:0 now
where the time goes in v8:
time: 80.8 us; the launch traced here: 80.2 us
  waiting for transfers between devices  35.8 us (44%)
  Pallas kernels  21.6 us (27%)
  starting transfers between devices  20.3 us (25%)
  other arithmetic  1.21 us (1%)
  local copies, waits for them, and re-layouts  1.09 us (1%)
    ppermute x9, waiting for transfers between devices, swap(): return lax.ppermute(value, axis, [(i, i ^ bit) for i in range(size)])  17.6 us
    pallas_call x1, Pallas kernels, pixel_rows(): pl.pallas_call(functools.partial(pixel_kernel, count), out_shape=(jax.Sha...  12 us
    ppermute x9, starting transfers between devices, swap(): return lax.ppermute(value, axis, [(i, i ^ bit) for i in range(size)])  11.1 us
    ppermute x1, waiting for transfers between devices, shards(): passed = lax.ppermute(across, 'chan', [(1, 0), (2, 3)])  9.61 us
    ppermute x4, waiting for transfers between devices, sum_over_panels(): parts = [added(part, lax.ppermute(part, both, perm)) for part in parts]  6.58 us
    ppermute x4, starting transfers between devices, sum_over_panels(): parts = [added(part, lax.ppermute(part, both, perm)) for part in parts]  5.23 us
    pallas_call x1, Pallas kernels, project(): pl.pallas_call(project_kernel, out_shape=jax.ShapeDtypeStruct((rows, widt...  3.29 us
    pallas_call x1, Pallas kernels, early_product(): pl.pallas_call(early_kernel, out_shape=(jax.ShapeDtypeStruct((depth, widt...  2.49 us
  transfers between devices with their start and end apart: 18, of which 10 were waited for; matrix products, arithmetic and copies ran while one was open for 2% of the time, Pallas kernels for 18%

profile of v8, /device:TPU:0, one launch (start us, length us, event | category | flops | bytes accessed | tf_op | source)
XLA Modules:
  0.0 80.2 jit_solution(8397845220473673965)
XLA Ops:
  0.0 1.1 %copy-done = bf16[1152,256]{1,0:T(8,128)(2,1)S(1)} copy-done((bf16[1152,256]{1,0:T(8,128)(2,1)S(1)}, bf16[1152,256]{1,0:T(8,128)(2,1)}, u32[]{:S(2)}) %copy-start) | copy-done | bytes 589848
  1.1 3.3 %project.1 = bf16[1024,256]{1,0:T(8,128)(2,1)S(1)} custom-call(s32[1]{0:T(128)} %bitcast.1.chan, bf16[2048,1152]{1,0:T(8,128)(2,1)} %spectra.3, bf16[1152,256]{1,0:T(8,128)(2,1)S(1)} %copy-done), custom_call_target="tpu_custom_call" | custom-call | flops 603979776 | bytes 3473408 | tf_op jit(solution)/shard_map/project/pallas_call | solution.py:88
  4.4 3.0 %collective-permute-start = (s32[2048]{0:T(1024)S(1)}, s32[2048]{0:T(1024)S(1)}, u32[]{:S(2)}, u32[]{:S(2)}) collective-permute-start(s32[2048]{0:T(1024)S(1)} %copy-done.4), channel_id=1, source_target_pairs={{0,4},{4,0},{1,5},{5,1},{2,6},{6,2},{3,7},{7,3},{8,12},{12,8},{9,1... | collective-permute-start | bytes 24584 | tf_op jit(solution)/shard_map/ppermute | solution.py:45
  7.4 0.9 %slice_select_fusion = bf16[128,256]{1,0:T(8,128)(2,1)S(1)} fusion(bf16[4096,256]{1,0:T(8,128)(2,1)} %refs_2_.1, pred[]{:T(512)S(6)} %eq.3), kind=kLoop, calls=%fused_computation.5 | loop fusion | flops 32768 | bytes 196609 | tf_op jit(solution)/shard_map/jit(_where)/select_n | solution.py:22
  8.3 0.1 collective-permute-start.1
  8.4 2.1 %collective-permute-start.2 = (bf16[1024,256]{1,0:T(8,128)(2,1)S(1)}, bf16[1024,256]{1,0:T(8,128)(2,1)S(1)}, u32[]{:S(2)}, u32[]{:S(2)}) collective-permute-start(bf16[1024,256]{1,0:T(8,128)(2,1)S(1)} %project.1), channel_id=1, source_target_pairs={{0,1},{1,0},{2,3},{3,2},{4,5},{5,4},{6,7},{7,6},{8,9},{9,8},{10,11... | collective-permute-start | bytes 1572872 | tf_op jit(solution)/shard_map/ppermute | solution.py:45
  10.6 2.0 %collective-permute-done.1.refs_3_.refs_4_ = bf16[128,256]{1,0:T(8,128)(2,1)S(1)} collective-permute-done((bf16[128,256]{1,0:T(8,128)(2,1)S(1)}, bf16[128,256]{1,0:T(8,128)(2,1)S(1)}, u32[]{:S(2)}, u32[]{:S(2)}) %collective-permute-start.1) | collective-permute-done | bytes 65568 | tf_op jit(solution)/shard_map/ppermute | solution.py:22
  12.6 12.0 %pixel_rows.1 = (bf16[1024,256]{1,0:T(8,128)(2,1)S(1)}, bf16[512,256]{1,0:T(8,128)(2,1)S(1)}, bf16[512,256]{1,0:T(8,128)(2,1)S(1)}) custom-call(s32[2]{0:T(128)S(1)} %pad_add_fusion.2.where, s32[16384]{0:T(1024)S(1)} %bitcast.9, s32[2048]{0:T(1024)S(1)} %copy-done.4, s32[2048]{0:T(1024)S(1)} %collective-permute-done.refs_1_, bf16[4096,256]{1,0:T(8,128)(2,1)} %refs_2_.1, ...), custom_call_target="tpu_custom_call" | custom-call | flops 12884901888 | bytes 4194304 | tf_op jit(solution)/shard_map/pixel_rows/pallas_call | solution.py:283
  24.8 3.1 %collective-permute-start.3 = (bf16[512,256]{1,0:T(8,128)(2,1)S(1)}, bf16[512,256]{1,0:T(8,128)(2,1)S(1)}, u32[]{:S(2)}, u32[]{:S(2)}) collective-permute-start(bf16[512,256]{1,0:T(8,128)(2,1)S(1)} %add_convert_fusion), channel_id=1, source_target_pairs={{0,2},{1,3},{2,0},{3,1},{4,6},{5,7},{6,4},{7,5},{8,10},{9,11},{10,... | collective-permute-start | bytes 786440 | tf_op jit(solution)/shard_map/ppermute | solution.py:45
  28.0 3.3 %collective-permute-done.4.answers = bf16[512,256]{1,0:T(8,128)(2,1)S(1)} collective-permute-done((bf16[512,256]{1,0:T(8,128)(2,1)S(1)}, bf16[512,256]{1,0:T(8,128)(2,1)S(1)}, u32[]{:S(2)}, u32[]{:S(2)}) %collective-permute-start.4) | collective-permute-done | bytes 262176 | tf_op jit(solution)/shard_map/ppermute | solution.py:45
  31.4 6.9 %collective-permute-done.3.far = bf16[512,256]{1,0:T(8,128)(2,1)S(1)} collective-permute-done((bf16[512,256]{1,0:T(8,128)(2,1)S(1)}, bf16[512,256]{1,0:T(8,128)(2,1)S(1)}, u32[]{:S(2)}, u32[]{:S(2)}) %collective-permute-start.3) | collective-permute-done | bytes 262176 | tf_op jit(solution)/shard_map/ppermute | solution.py:45
  38.2 1.0 %pre_gradient.1.first = bf16[512,256]{1,0:T(8,128)(2,1)S(1)} custom-call(s32[2]{0:T(128)S(1)} %pad_add_fusion.1.where, bf16[1024,256]{1,0:T(8,128)(2,1)S(1)} %get-tuple-element.21.keep, bf16[1024,256]{1,0:T(8,128)(2,1)S(1)} %collective-permute-done.2.near, bf16[512,256]{1,0:T(8,128)(2,1)S(1)} %collective-permute-done.3.far, s32[16,128]{1,0:T(8,128)S(1)} %bitcast.10, ...), custom_call_target="tpu_custom_call" | custom-call | tf_op jit(solution)/shard_map/pre_gradient/pallas_call | solution.py:358
  39.3 0.7 collective-permute-start.7
  39.9 2.0 %collective-permute-start.5 = (bf16[512,256]{1,0:T(8,128)(2,1)S(1)}, bf16[512,256]{1,0:T(8,128)(2,1)S(1)}, u32[]{:S(2)}, u32[]{:S(2)}) collective-permute-start(bf16[512,256]{1,0:T(8,128)(2,1)S(1)} %pre_gradient.1.first), channel_id=1, source_target_pairs={{0,1},{1,0},{2,3},{3,2},{4,5},{5,4},{6,7},{7,6},{8,9},{9,8},{10,11... | collective-permute-start | bytes 786440 | tf_op jit(solution)/shard_map/ppermute | solution.py:45
  42.0 1.3 %collective-permute-start.8 = (bf16[512,256]{1,0:T(8,128)(2,1)S(1)}, bf16[512,256]{1,0:T(8,128)(2,1)S(1)}, u32[]{:S(2)}, u32[]{:S(2)}) collective-permute-start(bf16[512,256]{1,0:T(8,128)(2,1)S(1)} %collective-permute-done.7.across), channel_id=1, source_target_pairs={{1,0},{2,3},{5,4},{6,7},{9,8},{10,11},{13,12},{14,15},{17,16},{18,... | collective-permute-start | bytes 786440 | tf_op jit(solution)/shard_map/ppermute | solution.py:455
  43.3 5.2 %collective-permute-done.5.second = bf16[512,256]{1,0:T(8,128)(2,1)S(1)} collective-permute-done((bf16[512,256]{1,0:T(8,128)(2,1)S(1)}, bf16[512,256]{1,0:T(8,128)(2,1)S(1)}, u32[]{:S(2)}, u32[]{:S(2)}) %collective-permute-start.5) | collective-permute-done | bytes 262176 | tf_op jit(solution)/shard_map/ppermute | solution.py:45
  48.5 1.3 %collective-permute-start.9 = (bf16[512,256]{1,0:T(8,128)(2,1)S(1)}, bf16[512,256]{1,0:T(8,128)(2,1)S(1)}, u32[]{:S(2)}, u32[]{:S(2)}) collective-permute-start(bf16[512,256]{1,0:T(8,128)(2,1)S(1)} %collective-permute-done.5.second), channel_id=1, source_target_pairs={{2,0},{1,3},{6,4},{5,7},{10,8},{9,11},{14,12},{13,15},{18,16},{17,... | collective-permute-start | bytes 786440 | tf_op jit(solution)/shard_map/ppermute | solution.py:457
  49.8 0.7 collective-permute-start.6
  50.5 2.5 %early_product.1 = (f32[1152,256]{1,0:T(8,128)S(1)}, bf16[1024,1152]{1,0:T(8,128)(2,1)S(1)}) custom-call(s32[1]{0:T(128)} %bitcast.1.chan, bf16[2048,1152]{1,0:T(8,128)(2,1)} %spectra.3, bf16[512,256]{1,0:T(8,128)(2,1)S(1)} %pre_gradient.1.first, bf16[512,256]{1,0:T(8,128)(2,1)S(1)} %collective-permute-done.5.second), custom_call_target="tpu_custom_call" | custom-call | flops 603979776 | bytes 5898240 | tf_op jit(solution)/shard_map/early_product/pallas_call | solution.py:135
  53.0 9.6 %collective-permute-done.8.passed = bf16[512,256]{1,0:T(8,128)(2,1)S(1)} collective-permute-done((bf16[512,256]{1,0:T(8,128)(2,1)S(1)}, bf16[512,256]{1,0:T(8,128)(2,1)S(1)}, u32[]{:S(2)}, u32[]{:S(2)}) %collective-permute-start.8) | collective-permute-done | bytes 262176 | tf_op jit(solution)/shard_map/ppermute | solution.py:455
  62.6 1.5 %late_product.1 = (bf16[288,256]{1,0:T(8,128)(2,1)S(1)}, bf16[288,256]{1,0:T(8,128)(2,1)S(1)}, f32[288,256]{1,0:T(8,128)S(1)}, f32[288,256]{1,0:T(8,128)S(1)}) custom-call(s32[2]{0:T(128)S(1)} %pad_add_fusion.where, bf16[1024,1152]{1,0:T(8,128)(2,1)S(1)} %get-tuple-element.27.held, f32[1152,256]{1,0:T(8,128)S(1)} %get-tuple-element.28.before, ...), custom_call_target="tpu_custom_call" | custom-call | flops 603979776 | bytes 3538944 | tf_op jit(solution)/shard_map/late_product/pallas_call | solution.py:182
  64.2 0.5 collective-permute-start.13
  64.7 0.9 %collective-permute-done.10.second = bf16[288,256]{1,0:T(8,128)(2,1)S(1)} collective-permute-done((bf16[288,256]{1,0:T(8,128)(2,1)S(1)}, bf16[288,256]{1,0:T(8,128)(2,1)S(1)}, u32[]{:S(2)}, u32[]{:S(2)}) %collective-permute-start.10) | collective-permute-done | bytes 147488 | tf_op jit(solution)/shard_map/ppermute | solution.py:45
  65.6 1.6 %collective-permute-start.11 = (bf16[288,256]{1,0:T(8,128)(2,1)S(1)}, bf16[288,256]{1,0:T(8,128)(2,1)S(1)}, u32[]{:S(2)}, u32[]{:S(2)}) collective-permute-start(bf16[288,256]{1,0:T(8,128)(2,1)S(1)} %added.6.first), channel_id=1, source_target_pairs={{0,16},{4,20},{8,12},{12,8},{16,0},{20,4},{24,28},{28,24},{1,17},{... | collective-permute-start | bytes 442376 | tf_op jit(solution)/shard_map/ppermute | solution.py:413
  67.2 0.6 collective-permute-start.14
  67.8 3.0 %collective-permute-done.11.second = bf16[288,256]{1,0:T(8,128)(2,1)S(1)} collective-permute-done((bf16[288,256]{1,0:T(8,128)(2,1)S(1)}, bf16[288,256]{1,0:T(8,128)(2,1)S(1)}, u32[]{:S(2)}, u32[]{:S(2)}) %collective-permute-start.11) | collective-permute-done | bytes 147488 | tf_op jit(solution)/shard_map/ppermute | solution.py:413
  70.8 1.5 %collective-permute-start.12 = (bf16[288,256]{1,0:T(8,128)(2,1)S(1)}, bf16[288,256]{1,0:T(8,128)(2,1)S(1)}, u32[]{:S(2)}, u32[]{:S(2)}) collective-permute-start(bf16[288,256]{1,0:T(8,128)(2,1)S(1)} %added.7.first), channel_id=1, source_target_pairs={{0,4},{4,0},{8,24},{12,28},{16,20},{20,16},{24,8},{28,12},{1,5},{5... | collective-permute-start | bytes 442376 | tf_op jit(solution)/shard_map/ppermute | solution.py:413
  72.4 1.5 %collective-permute-start.15 = (bf16[288,256]{1,0:T(8,128)(2,1)S(1)}, bf16[288,256]{1,0:T(8,128)(2,1)S(1)}, u32[]{:S(2)}, u32[]{:S(2)}) collective-permute-start(bf16[288,256]{1,0:T(8,128)(2,1)S(1)} %added.10.first), channel_id=1, source_target_pairs={{0,4},{4,0},{8,24},{12,28},{16,20},{20,16},{24,8},{28,12},{1,5},{5... | collective-permute-start | bytes 442376 | tf_op jit(solution)/shard_map/ppermute | solution.py:413
  73.9 2.1 %collective-permute-done.12.second = bf16[288,256]{1,0:T(8,128)(2,1)S(1)} collective-permute-done((bf16[288,256]{1,0:T(8,128)(2,1)S(1)}, bf16[288,256]{1,0:T(8,128)(2,1)S(1)}, u32[]{:S(2)}, u32[]{:S(2)}) %collective-permute-start.12) | collective-permute-done | bytes 147488 | tf_op jit(solution)/shard_map/ppermute | solution.py:413
  76.1 1.5 %collective-permute-done.15.second = bf16[288,256]{1,0:T(8,128)(2,1)S(1)} collective-permute-done((bf16[288,256]{1,0:T(8,128)(2,1)S(1)}, bf16[288,256]{1,0:T(8,128)(2,1)S(1)}, u32[]{:S(2)}, u32[]{:S(2)}) %collective-permute-start.15) | collective-permute-done | bytes 147488 | tf_op jit(solution)/shard_map/ppermute | solution.py:413
  77.7 1.3 %collective-permute-done.17.refs_3_ = bf16[288,256]{1,0:T(8,128)(2,1)S(1)} collective-permute-done((bf16[288,256]{1,0:T(8,128)(2,1)S(1)}, bf16[288,256]{1,0:T(8,128)(2,1)S(1)}, u32[]{:S(2)}, u32[]{:S(2)}) %collective-permute-start.17) | collective-permute-done | bytes 147488 | tf_op jit(solution)/shard_map/ppermute | solution.py:45
  79.1 1.1 %collect.1 = f32[1152,256]{1,0:T(8,128)} custom-call(s32[1]{0:T(128)} %bitcast.core, bf16[288,256]{1,0:T(8,128)(2,1)S(1)} %added.8.refs_0_, bf16[288,256]{1,0:T(8,128)(2,1)S(1)} %added.11.refs_1_, bf16[288,256]{1,0:T(8,128)(2,1)S(1)} %collective-permute-done.16.refs_2_, bf16[288,256]{1,0:T(8,128)(2,1)S(1)} %collective-permute-done.17.refs_3_), custom_call_target="tpu_custom_call" | custom-call | tf_op jit(solution)/shard_map/collect/pallas_call | solution.py:382
  (38 shorter events, 0.9 us)
Async XLA Ops:
  0.0 1.1 %copy-start = (bf16[1152,256]{1,0:T(8,128)(2,1)S(1)}, bf16[1152,256]{1,0:T(8,128)(2,1)}, u32[]{:S(2)}) copy-start(bf16[1152,256]{1,0:T(8,128)(2,1)} %refs_7_.1) | copy-start | bytes 1769476
  1.1 3.3 %copy-start.4 = (s32[2048]{0:T(1024)S(1)}, s32[2048]{0:T(1024)}, u32[]{:S(2)}) copy-start(s32[2048]{0:T(1024)} %refs_0_) | copy-start | bytes 24580
  1.1 9.4 %copy-start.6 = (s32[8,4096]{1,0:T(8,128)S(1)}, s32[8,4096]{1,0:T(8,128)}, u32[]{:S(2)}) copy-start(s32[8,4096]{1,0:T(8,128)} %param.14) | copy-start | bytes 393220
  1.1 11.6 %copy-start.1 = (bf16[1152,256]{1,0:T(8,128)(2,1)S(1)}, bf16[1152,256]{1,0:T(8,128)(2,1)}, u32[]{:S(2)}) copy-start(bf16[1152,256]{1,0:T(8,128)(2,1)} %refs_7_.1) | copy-start | bytes 1769476
  1.1 11.6 %copy-start.5 = (f32[8,256]{1,0:T(8,128)S(1)}, f32[8,256]{1,0:T(8,128)}, u32[]{:S(2)}) copy-start(f32[8,256]{1,0:T(8,128)} %refs_5_.1) | copy-start | bytes 24580
  4.4 6.2 %collective-permute-start = (s32[2048]{0:T(1024)S(1)}, s32[2048]{0:T(1024)S(1)}, u32[]{:S(2)}, u32[]{:S(2)}) collective-permute-start(s32[2048]{0:T(1024)S(1)} %copy-done.4), channel_id=1, source_target_pairs={{0,4},{4,0},{1,5},{5,1},{2,6},{6,2},{3,7},{7,3},{8,12},{12,8},{9,1... | collective-permute-start | bytes 24584 | tf_op jit(solution)/shard_map/ppermute | solution.py:45
  8.3 4.3 %collective-permute-start.1 = (bf16[128,256]{1,0:T(8,128)(2,1)S(1)}, bf16[128,256]{1,0:T(8,128)(2,1)S(1)}, u32[]{:S(2)}, u32[]{:S(2)}) collective-permute-start(bf16[128,256]{1,0:T(8,128)(2,1)S(1)} %slice_select_fusion), channel_id=1, source_target_pairs={{0,4},{4,0},{1,5},{5,1},{2,6},{6,2},{3,7},{7,3},{8,12},{12,8},{9,1... | collective-permute-start | bytes 196616 | tf_op jit(solution)/shard_map/ppermute | solution.py:22
  8.4 16.4 %collective-permute-start.2 = (bf16[1024,256]{1,0:T(8,128)(2,1)S(1)}, bf16[1024,256]{1,0:T(8,128)(2,1)S(1)}, u32[]{:S(2)}, u32[]{:S(2)}) collective-permute-start(bf16[1024,256]{1,0:T(8,128)(2,1)S(1)} %project.1), channel_id=1, source_target_pairs={{0,1},{1,0},{2,3},{3,2},{4,5},{5,4},{6,7},{7,6},{8,9},{9,8},{10,11... | collective-permute-start | bytes 1572872 | tf_op jit(solution)/shard_map/ppermute | solution.py:45
  12.6 25.6 %copy-start.2 = (s32[2048,1]{0,1:T(1,128)S(1)}, s32[2048,1]{0,1:T(1,128)}, u32[]{:S(2)}) copy-start(s32[2048,1]{0,1:T(1,128)} %param.10) | copy-start | bytes 24580
  12.6 25.6 %copy-start.3 = (f32[2048]{0:T(1024)S(1)}, f32[2048]{0:T(1024)}, u32[]{:S(2)}) copy-start(f32[2048]{0:T(1024)} %param.12) | copy-start | bytes 24580
  24.7 6.7 %collective-permute-start.4 = (bf16[512,256]{1,0:T(8,128)(2,1)S(1)}, bf16[512,256]{1,0:T(8,128)(2,1)S(1)}, u32[]{:S(2)}, u32[]{:S(2)}) collective-permute-start(bf16[512,256]{1,0:T(8,128)(2,1)S(1)} %get-tuple-element.26), channel_id=1, source_target_pairs={{0,4},{4,0},{1,5},{5,1},{2,6},{6,2},{3,7},{7,3},{8,12},{12,8},{9,1... | collective-permute-start | bytes 786440 | tf_op jit(solution)/shard_map/ppermute | solution.py:45
  24.8 13.4 %collective-permute-start.3 = (bf16[512,256]{1,0:T(8,128)(2,1)S(1)}, bf16[512,256]{1,0:T(8,128)(2,1)S(1)}, u32[]{:S(2)}, u32[]{:S(2)}) collective-permute-start(bf16[512,256]{1,0:T(8,128)(2,1)S(1)} %add_convert_fusion), channel_id=1, source_target_pairs={{0,2},{1,3},{2,0},{3,1},{4,6},{5,7},{6,4},{7,5},{8,10},{9,11},{10,... | collective-permute-start | bytes 786440 | tf_op jit(solution)/shard_map/ppermute | solution.py:45
  39.3 2.7 %collective-permute-start.7 = (bf16[512,256]{1,0:T(8,128)(2,1)S(1)}, bf16[512,256]{1,0:T(8,128)(2,1)S(1)}, u32[]{:S(2)}, u32[]{:S(2)}) collective-permute-start(bf16[512,256]{1,0:T(8,128)(2,1)S(1)} %pre_gradient.1.first), channel_id=1, source_target_pairs={{1,2},{2,1},{5,6},{6,5},{9,10},{10,9},{13,14},{14,13},{17,18},{18,... | collective-permute-start | bytes 786440 | tf_op jit(solution)/shard_map/ppermute | solution.py:454
  39.9 8.5 %collective-permute-start.5 = (bf16[512,256]{1,0:T(8,128)(2,1)S(1)}, bf16[512,256]{1,0:T(8,128)(2,1)S(1)}, u32[]{:S(2)}, u32[]{:S(2)}) collective-permute-start(bf16[512,256]{1,0:T(8,128)(2,1)S(1)} %pre_gradient.1.first), channel_id=1, source_target_pairs={{0,1},{1,0},{2,3},{3,2},{4,5},{5,4},{6,7},{7,6},{8,9},{9,8},{10,11... | collective-permute-start | bytes 786440 | tf_op jit(solution)/shard_map/ppermute | solution.py:45
  42.0 20.6 %collective-permute-start.8 = (bf16[512,256]{1,0:T(8,128)(2,1)S(1)}, bf16[512,256]{1,0:T(8,128)(2,1)S(1)}, u32[]{:S(2)}, u32[]{:S(2)}) collective-permute-start(bf16[512,256]{1,0:T(8,128)(2,1)S(1)} %collective-permute-done.7.across), channel_id=1, source_target_pairs={{1,0},{2,3},{5,4},{6,7},{9,8},{10,11},{13,12},{14,15},{17,16},{18,... | collective-permute-start | bytes 786440 | tf_op jit(solution)/shard_map/ppermute | solution.py:455
  48.5 14.2 %collective-permute-start.9 = (bf16[512,256]{1,0:T(8,128)(2,1)S(1)}, bf16[512,256]{1,0:T(8,128)(2,1)S(1)}, u32[]{:S(2)}, u32[]{:S(2)}) collective-permute-start(bf16[512,256]{1,0:T(8,128)(2,1)S(1)} %collective-permute-done.5.second), channel_id=1, source_target_pairs={{2,0},{1,3},{6,4},{5,7},{10,8},{9,11},{14,12},{13,15},{18,16},{17,... | collective-permute-start | bytes 786440 | tf_op jit(solution)/shard_map/ppermute | solution.py:457
  49.8 12.9 %collective-permute-start.6 = (bf16[512,256]{1,0:T(8,128)(2,1)S(1)}, bf16[512,256]{1,0:T(8,128)(2,1)S(1)}, u32[]{:S(2)}, u32[]{:S(2)}) collective-permute-start(bf16[512,256]{1,0:T(8,128)(2,1)S(1)} %collective-permute-done.5.second), channel_id=1, source_target_pairs={{1,2},{2,1},{5,6},{6,5},{9,10},{10,9},{13,14},{14,13},{17,18},{18,... | collective-permute-start | bytes 786440 | tf_op jit(solution)/shard_map/ppermute | solution.py:456
  64.1 1.4 %collective-permute-start.10 = (bf16[288,256]{1,0:T(8,128)(2,1)S(1)}, bf16[288,256]{1,0:T(8,128)(2,1)S(1)}, u32[]{:S(2)}, u32[]{:S(2)}) collective-permute-start(bf16[288,256]{1,0:T(8,128)(2,1)S(1)} %get-tuple-element.30), channel_id=1, source_target_pairs={{0,8},{8,0},{16,24},{24,16},{1,9},{9,1},{17,25},{25,17},{2,10},{10... | collective-permute-start | bytes 442376 | tf_op jit(solution)/shard_map/ppermute | solution.py:45
  64.2 2.9 %collective-permute-start.13 = (bf16[288,256]{1,0:T(8,128)(2,1)S(1)}, bf16[288,256]{1,0:T(8,128)(2,1)S(1)}, u32[]{:S(2)}, u32[]{:S(2)}) collective-permute-start(bf16[288,256]{1,0:T(8,128)(2,1)S(1)} %get-tuple-element.32), channel_id=1, source_target_pairs={{0,8},{8,0},{16,24},{24,16},{1,9},{9,1},{17,25},{25,17},{2,10},{10... | collective-permute-start | bytes 442376 | tf_op jit(solution)/shard_map/ppermute | solution.py:45
  65.6 5.2 %collective-permute-start.11 = (bf16[288,256]{1,0:T(8,128)(2,1)S(1)}, bf16[288,256]{1,0:T(8,128)(2,1)S(1)}, u32[]{:S(2)}, u32[]{:S(2)}) collective-permute-start(bf16[288,256]{1,0:T(8,128)(2,1)S(1)} %added.6.first), channel_id=1, source_target_pairs={{0,16},{4,20},{8,12},{12,8},{16,0},{20,4},{24,28},{28,24},{1,17},{... | collective-permute-start | bytes 442376 | tf_op jit(solution)/shard_map/ppermute | solution.py:413
  67.2 5.2 %collective-permute-start.14 = (bf16[288,256]{1,0:T(8,128)(2,1)S(1)}, bf16[288,256]{1,0:T(8,128)(2,1)S(1)}, u32[]{:S(2)}, u32[]{:S(2)}) collective-permute-start(bf16[288,256]{1,0:T(8,128)(2,1)S(1)} %added.9.first), channel_id=1, source_target_pairs={{0,16},{4,20},{8,12},{12,8},{16,0},{20,4},{24,28},{28,24},{1,17},{... | collective-permute-start | bytes 442376 | tf_op jit(solution)/shard_map/ppermute | solution.py:413
  70.8 5.2 %collective-permute-start.12 = (bf16[288,256]{1,0:T(8,128)(2,1)S(1)}, bf16[288,256]{1,0:T(8,128)(2,1)S(1)}, u32[]{:S(2)}, u32[]{:S(2)}) collective-permute-start(bf16[288,256]{1,0:T(8,128)(2,1)S(1)} %added.7.first), channel_id=1, source_target_pairs={{0,4},{4,0},{8,24},{12,28},{16,20},{20,16},{24,8},{28,12},{1,5},{5... | collective-permute-start | bytes 442376 | tf_op jit(solution)/shard_map/ppermute | solution.py:413
  72.4 5.2 %collective-permute-start.15 = (bf16[288,256]{1,0:T(8,128)(2,1)S(1)}, bf16[288,256]{1,0:T(8,128)(2,1)S(1)}, u32[]{:S(2)}, u32[]{:S(2)}) collective-permute-start(bf16[288,256]{1,0:T(8,128)(2,1)S(1)} %added.10.first), channel_id=1, source_target_pairs={{0,4},{4,0},{8,24},{12,28},{16,20},{20,16},{24,8},{28,12},{1,5},{5... | collective-permute-start | bytes 442376 | tf_op jit(solution)/shard_map/ppermute | solution.py:413
  76.1 1.7 %collective-permute-start.16 = (bf16[288,256]{1,0:T(8,128)(2,1)S(1)}, bf16[288,256]{1,0:T(8,128)(2,1)S(1)}, u32[]{:S(2)}, u32[]{:S(2)}) collective-permute-start(bf16[288,256]{1,0:T(8,128)(2,1)S(1)} %added.8.refs_0_), channel_id=1, source_target_pairs={{0,8},{8,0},{16,24},{24,16},{1,9},{9,1},{17,25},{25,17},{2,10},{10... | collective-permute-start | bytes 442376 | tf_op jit(solution)/shard_map/ppermute | solution.py:45
  77.6 1.4 %collective-permute-start.17 = (bf16[288,256]{1,0:T(8,128)(2,1)S(1)}, bf16[288,256]{1,0:T(8,128)(2,1)S(1)}, u32[]{:S(2)}, u32[]{:S(2)}) collective-permute-start(bf16[288,256]{1,0:T(8,128)(2,1)S(1)} %added.11.refs_1_), channel_id=1, source_target_pairs={{0,8},{8,0},{16,24},{24,16},{1,9},{9,1},{17,25},{25,17},{2,10},{10... | collective-permute-start | bytes 442376 | tf_op jit(solution)/shard_map/ppermute | solution.py:45

commit v9 on v8

--- a/solution.py
+++ b/solution.py
@@ -11,6 +11,7 @@
 HALO = 128
 MIB = 1024 * 1024
 LARGE = 52
+PIECES = 8
 
 
 def edges(value, axis, width):
@@ -50,10 +51,10 @@
 
 
 def quarter_copies(spectra, weight, held, near, sems, chan, bits):
-    chunk = held.shape[0] // 4
-    copies = [pltpu.make_async_copy(weight, near, sems.at[4])]
-    for turn in range(4):
-        first = ((chan ^ bits ^ (turn // 2 * 2)) * 2 + turn % 2) * chunk
+    chunk = held.shape[0] // len(bits) // 2
+    copies = [pltpu.make_async_copy(weight, near, sems.at[2 * len(bits)])]
+    for turn in range(2 * len(bits)):
+        first = ((chan ^ bits[turn // 2]) * 2 + turn % 2) * chunk
         copies.append(
             pltpu.make_async_copy(
                 spectra.at[pl.ds(pl.multiple_of(first, chunk), chunk)],
@@ -64,26 +65,27 @@
     return copies
 
 
-def project_rows(copies, held, near, out):
-    chunk = held.shape[0] // 4
+def project_rows(copies, held, near, outs):
+    chunk = outs[0].shape[0] // 2
     copies[0].wait()
-    for turn in range(4):
+    for turn in range(2 * len(outs)):
         copies[turn + 1].wait()
-        rows = pl.ds(turn * chunk, chunk)
-        result = jnp.dot(held[rows, :], near[...], preferred_element_type=jnp.float32)
-        out[rows, :] = result.astype(out.dtype)
+        rows = held[turn * chunk : (turn + 1) * chunk, :]
+        result = jnp.dot(rows, near[...], preferred_element_type=jnp.float32)
+        first = turn % 2 * chunk
+        outs[turn // 2][first : first + chunk, :] = result.astype(outs[0].dtype)
 
 
 def project_kernel(chan, spectra, weight, out, held, near, sems):
-    copies = quarter_copies(spectra, weight, held, near, sems, chan[0], 1)
+    copies = quarter_copies(spectra, weight, held, near, sems, chan[0], (3,))
     for copy in copies:
         copy.start()
-    project_rows(copies, held, near, out)
+    project_rows(copies, held, near, (out,))
 
 
 def project(spectra, weight, chan):
     depth, width = weight.shape
-    rows = spectra.shape[0] // 2
+    rows = spectra.shape[0] // 4
     hbm = pl.BlockSpec(memory_space=pltpu.HBM)
     return pl.pallas_call(
         project_kernel,
@@ -93,7 +95,7 @@
         scratch_shapes=[
             pltpu.VMEM((rows, depth), jnp.bfloat16),
             pltpu.VMEM((depth, width), jnp.bfloat16),
-            pltpu.SemaphoreType.DMA((5,)),
+            pltpu.SemaphoreType.DMA((3,)),
         ],
         compiler_params=memory(LARGE),
         cost_estimate=pl.CostEstimate(
@@ -197,21 +199,27 @@
 
 
 def pixel_kernel(count, where, places, *refs):
-    lists = refs[: (len(refs) - 16) // 3]
+    lists = refs[: (len(refs) - 18) // 3]
     names = refs[-len(lists) :]
     refs = refs[len(lists) : -len(lists)]
-    cotangent, above, below, mixing, spectra, weight, keep = refs[:7]
-    outs = refs[7 : 7 + len(lists)]
-    table, scale, sums, held, near, block, factor, sems, more = refs[7 + len(lists) :]
+    cotangent, above, below, mixing, spectra, weight = refs[:6]
+    quarters, outs = refs[6:9], refs[9 : 9 + len(lists)]
+    table, scale, sums, held, near, block, factor, sems, more = refs[9 + len(lists) :]
     start, chan = where[0], where[1]
     tile_rows, half = held.shape[0], table.shape[1]
     chunk = tile_rows // 4
-    copies = [pltpu.make_async_copy(places, near, sems.at[4])]
+    piece = near.shape[0] // PIECES
+    copies = [
+        pltpu.make_async_copy(
+            places.at[pl.ds(n * piece, piece)], near.at[pl.ds(n * piece, piece)], sems.at[4 + n]
+        )
+        for n in range(PIECES)
+    ]
     copies += [
-        pltpu.make_async_copy(wanted, name, sems.at[5 + n])
+        pltpu.make_async_copy(wanted, name, sems.at[4 + PIECES + n])
         for n, (wanted, name) in enumerate(zip(lists, names))
     ]
-    parts = quarter_copies(spectra, weight, block, factor, more, chan, 0)
+    parts = quarter_copies(spectra, weight, block, factor, more, chan, (2, 1, 0))
     rows = [
         pltpu.make_async_copy(
             cotangent.at[pl.ds(n * chunk, chunk)], held.at[pl.ds(n * chunk, chunk)], sems.at[n]
@@ -220,7 +228,7 @@
     ]
     for copy in copies + parts + rows:
         copy.start()
-    project_rows(parts, block, factor, keep)
+    project_rows(parts, block, factor, quarters)
 
     def fill(first, values):
         values = values.astype(jnp.float32)
@@ -271,19 +279,17 @@
 
 
 def pixel_rows(
-    cotangent, above, below, adjoint, mixing, anchor, lists, start, count, spectra, weight, chan
+    cotangent, above, below, places, mixing, lists, start, count, spectra, weight, chan
 ):
     tile_rows, width = cotangent.shape
-    depth, rows = spectra.shape[1], spectra.shape[0] // 2
-    places = (adjoint - anchor) * 2
-    places = (places[: NEIGH // 2] | (places[NEIGH // 2 :] << 16)).reshape(-1)
+    depth, rows = spectra.shape[1], spectra.shape[0] // 4
     anywhere = pl.BlockSpec(memory_space=pl.ANY)
     hbm = pl.BlockSpec(memory_space=pltpu.HBM)
     vmem = pl.BlockSpec(memory_space=pltpu.VMEM)
     return pl.pallas_call(
         functools.partial(pixel_kernel, count),
         out_shape=(
-            jax.ShapeDtypeStruct((rows, width), jnp.bfloat16),
+            *[jax.ShapeDtypeStruct((rows, width), jnp.bfloat16)] * 3,
             *[jax.ShapeDtypeStruct((count, width), jnp.bfloat16)] * len(lists),
         ),
         in_specs=[
@@ -295,17 +301,17 @@
             hbm,
             hbm,
         ],
-        out_specs=(vmem,) * (1 + len(lists)),
+        out_specs=(vmem,) * (3 + len(lists)),
         scratch_shapes=[
             pltpu.VMEM((2 * (tile_rows + 2 * HALO), width // 2), jnp.float32),
             pltpu.VMEM((2 * NEIGH, width // 2), jnp.float32),
             pltpu.VMEM((2 * count * len(lists), width // 2), jnp.float32),
             pltpu.VMEM(cotangent.shape, cotangent.dtype),
             pltpu.SMEM(places.shape, jnp.int32),
-            pltpu.VMEM((rows, depth), jnp.bfloat16),
+            pltpu.VMEM((3 * rows, depth), jnp.bfloat16),
             pltpu.VMEM((depth, width), jnp.bfloat16),
-            pltpu.SemaphoreType.DMA((5 + len(lists),)),
-            pltpu.SemaphoreType.DMA((5,)),
+            pltpu.SemaphoreType.DMA((4 + PIECES + len(lists),)),
+            pltpu.SemaphoreType.DMA((7,)),
             *[pltpu.SMEM(names.shape, jnp.int32) for names in lists],
         ],
         compiler_params=memory(LARGE),
@@ -423,31 +429,34 @@
     first_row = chan * quarter
     middle = [(1, 2), (2, 1)]
 
-    send = project(spectra, enc_weight, chan)
-    send, pix_local, edge_rows = lax.optimization_barrier((send, pix_local, cotangent))
-    near = swap(send, "chan", 1)
-
-    above, below = edges(edge_rows, "pix", HALO)
-    anchor = tile * tile_rows - HALO
+    near_first = swap(project(spectra, enc_weight, chan), "chan", 1)
+    places = (adjoint - (tile * tile_rows - HALO)) * 2
+    places = (places[: NEIGH // 2] | (places[NEIGH // 2 :] << 16)).reshape(-1)
+
+    above, below = edges(cotangent, "pix", HALO)
     capacity = 2 * quarter // tile_count
-    pixels = (cotangent, above, below, adjoint, mixing, anchor)
+    pixels = (cotangent, above, below, places, mixing)
     rest = (spectra, enc_weight, chan)
     if capacity >= quarter and tile_count == 2:
         lists = (pix_local, swap(pix_local, "pix", 1))
-        keep, mine, theirs = pixel_rows(*pixels, lists, first_row, quarter, *rest)
-        answers = swap(theirs, "pix", 1)
+        shared, send, keep, mine, rows = pixel_rows(*pixels, lists, first_row, quarter, *rest)
     else:
         tile_ids = lax.dynamic_slice_in_dim(pix_tile[:, 0], first_row, quarter, 0)
         local_ids = lax.dynamic_slice_in_dim(pix_local, first_row, quarter, 0)
         slot_index, wanted = requests(tile_ids, local_ids, capacity)
-        keep, rows = pixel_rows(*pixels, (wanted,), 0 * chan, wanted.shape[0], *rest)
+        shared, send, keep, rows = pixel_rows(*pixels, (wanted,), 0 * chan, wanted.shape[0], *rest)
+    near_first, rows = lax.optimization_barrier((near_first, rows))
+    passed_on = (shared.astype(jnp.float32) + near_first.astype(jnp.float32)).astype(jnp.bfloat16)
+    passed_on, rows, send = lax.optimization_barrier((passed_on, rows, send))
+    far = swap(passed_on, "chan", 2)
+    near = swap(send, "chan", 1)
+    if capacity >= quarter and tile_count == 2:
+        answers = swap(rows, "pix", 1)
+    else:
         answers = lax.all_to_all(
             rows.reshape(tile_count, capacity, -1), "pix", split_axis=0, concat_axis=0, tiled=True
         )
         mine = answers = jnp.take(answers.reshape(tile_count * capacity, -1), slot_index, axis=0)
-    near, mine = lax.optimization_barrier((near, mine))
-    passed_on = keep[quarter:].astype(jnp.float32) + near[quarter:].astype(jnp.float32)
-    far = swap(passed_on.astype(jnp.bfloat16), "chan", 2)
     grads = pre_gradient(tile, chan, keep, near, far, pix_tile, foot_weight, mine, answers)
 
     beside = swap(grads, "chan", 1)

time: 80.8 us -> 76.4 us (0.946)
  waiting for transfers between devices: 35.8 us -> 27.7 us
  starting transfers between devices: 20.3 us -> 23.6 us
    ppermute x9 -> x10, waiting for transfers between devices: 17.6 us -> 13.7 us  [swap(): return lax.ppermute(value, axis, [(i, i ^ bit) for i in range(size)])]
    ppermute x9 -> x10, starting transfers between devices: 11.1 us -> 14.3 us  [swap(): return lax.ppermute(value, axis, [(i, i ^ bit) for i in range(size)])]
    ppermute x1, waiting for transfers between devices: 9.61 us -> 7.45 us  [shards(): passed = lax.ppermute(across, 'chan', [(1, 0), (2, 3)])]
    ppermute x1, waiting for transfers between devices: 2.04 us -> 0.01 us  [edges(): lax.ppermute(jnp.where(index == 0, last, first), axis, [(0, 1), (1, 0)])]
    pallas_call x1, Pallas kernels: 12 us -> 13.2 us  [pixel_rows(): pl.pallas_call(functools.partial(pixel_kernel, count), out_shape=(*[jax.S...]
    pallas_call x1, Pallas kernels: 3.29 us -> 2.18 us  [project(): pl.pallas_call(project_kernel, out_shape=jax.ShapeDtypeStruct((rows, widt...]
  transfers between devices with their start and end apart: 18 -> 19, of which waited for: 10 -> 8; matrix products, arithmetic and copies ran while one was open for 2% -> 2% of each run, Pallas kernels for 18% -> 24%
where the time goes in v9:
time: 76.4 us; the launch traced here: 75.5 us
  waiting for transfers between devices  27.7 us (36%)
  starting transfers between devices  23.6 us (31%)
  Pallas kernels  21.7 us (28%)
  other arithmetic  1.22 us (2%)
  local copies, waits for them, and re-layouts  1.09 us (1%)
    ppermute x10, starting transfers between devices, swap(): return lax.ppermute(value, axis, [(i, i ^ bit) for i in range(size)])  14.3 us
    ppermute x10, waiting for transfers between devices, swap(): return lax.ppermute(value, axis, [(i, i ^ bit) for i in range(size)])  13.7 us
    pallas_call x1, Pallas kernels, pixel_rows(): pl.pallas_call(functools.partial(pixel_kernel, count), out_shape=(*[jax.S...  13.2 us
    ppermute x1, waiting for transfers between devices, shards(): passed = lax.ppermute(across, 'chan', [(1, 0), (2, 3)])  7.45 us
    ppermute x4, waiting for transfers between devices, sum_over_panels(): parts = [added(part, lax.ppermute(part, both, perm)) for part in parts]  6.56 us
    ppermute x4, starting transfers between devices, sum_over_panels(): parts = [added(part, lax.ppermute(part, both, perm)) for part in parts]  5.29 us
    pallas_call x1, Pallas kernels, early_product(): pl.pallas_call(early_kernel, out_shape=(jax.ShapeDtypeStruct((depth, widt...  2.49 us
    pallas_call x1, Pallas kernels, project(): pl.pallas_call(project_kernel, out_shape=jax.ShapeDtypeStruct((rows, widt...  2.18 us
  transfers between devices with their start and end apart: 19, of which 8 were waited for; matrix products, arithmetic and copies ran while one was open for 2% of the time, Pallas kernels for 24%

profile of v9, /device:TPU:0, one launch (start us, length us, event | category | flops | bytes accessed | tf_op | source)
XLA Modules:
  0.0 75.5 jit_solution(16337400394411437056)
XLA Ops:
  0.0 3.0 %collective-permute-start = (s32[2048]{0:T(1024)}, s32[2048]{0:T(1024)S(1)}, u32[]{:S(2)}, u32[]{:S(2)}) collective-permute-start(s32[2048]{0:T(1024)} %refs_0_.1), channel_id=1, source_target_pairs={{0,4},{4,0},{1,5},{5,1},{2,6},{6,2},{3,7},{7,3},{8,12},{12,8},{9,1... | collective-permute-start | bytes 24584 | tf_op jit(solution)/shard_map/ppermute | solution.py:46
  3.0 0.9 %slice_select_fusion = bf16[128,256]{1,0:T(8,128)(2,1)S(1)} fusion(bf16[4096,256]{1,0:T(8,128)(2,1)} %refs_2_.1, pred[]{:T(512)S(6)} %eq.3), kind=kLoop, calls=%fused_computation.5 | loop fusion | flops 32768 | bytes 196609 | tf_op jit(solution)/shard_map/jit(_where)/select_n | solution.py:23
  3.9 1.1 %copy-done = bf16[1152,256]{1,0:T(8,128)(2,1)S(1)} copy-done((bf16[1152,256]{1,0:T(8,128)(2,1)S(1)}, bf16[1152,256]{1,0:T(8,128)(2,1)}, u32[]{:S(2)}) %copy-start) | copy-done | bytes 589848
  5.0 2.2 %project.1 = bf16[512,256]{1,0:T(8,128)(2,1)S(1)} custom-call(s32[1]{0:T(128)} %bitcast.1.chan, bf16[2048,1152]{1,0:T(8,128)(2,1)} %spectra.3, bf16[1152,256]{1,0:T(8,128)(2,1)S(1)} %copy-done), custom_call_target="tpu_custom_call" | custom-call | flops 301989888 | bytes 2031616 | tf_op jit(solution)/shard_map/project/pallas_call | solution.py:90
  7.2 2.1 %collective-permute-start.2 = (bf16[512,256]{1,0:T(8,128)(2,1)S(1)}, bf16[512,256]{1,0:T(8,128)(2,1)S(1)}, u32[]{:S(2)}, u32[]{:S(2)}) collective-permute-start(bf16[512,256]{1,0:T(8,128)(2,1)S(1)} %project.1), channel_id=1, source_target_pairs={{0,1},{1,0},{2,3},{3,2},{4,5},{5,4},{6,7},{7,6},{8,9},{9,8},{10,11... | collective-permute-start | bytes 786440 | tf_op jit(solution)/shard_map/ppermute | solution.py:46
  9.4 0.1 pad_add_fusion.2.where
  9.5 13.2 %pixel_rows.1 = (bf16[512,256]{1,0:T(8,128)(2,1)S(1)}, bf16[512,256]{1,0:T(8,128)(2,1)S(1)}, bf16[512,256]{1,0:T(8,128)(2,1)S(1)}, bf16[512,256]{1,0:T(8,128)(2,1)S(1)}, bf16[512,256]{1,0:T(8,128)(2,1)S(1)}) custom-call(s32[2]{0:T(128)S(1)} %pad_add_fusion.2.where, s32[16384]{0:T(1024)S(1)} %bitcast.9, s32[2048]{0:T(1024)S(1)} %copy-done.3, ...), custom_call_target="tpu_custom_call" | custom-call | flops 12884901888 | bytes 4194304 | tf_op jit(solution)/shard_map/pixel_rows/pallas_call | solution.py:289
  22.8 0.3 collective-permute-start.3
  23.2 2.8 %collective-permute-start.4 = (bf16[512,256]{1,0:T(8,128)(2,1)S(1)}, bf16[512,256]{1,0:T(8,128)(2,1)S(1)}, u32[]{:S(2)}, u32[]{:S(2)}) collective-permute-start(bf16[512,256]{1,0:T(8,128)(2,1)S(1)} %add_convert_fusion), channel_id=1, source_target_pairs={{0,2},{1,3},{2,0},{3,1},{4,6},{5,7},{6,4},{7,5},{8,10},{9,11},{10,... | collective-permute-start | bytes 786440 | tf_op jit(solution)/shard_map/ppermute | solution.py:46
  25.9 1.5 %collective-permute-start.5 = (bf16[512,256]{1,0:T(8,128)(2,1)S(1)}, bf16[512,256]{1,0:T(8,128)(2,1)S(1)}, u32[]{:S(2)}, u32[]{:S(2)}) collective-permute-start(bf16[512,256]{1,0:T(8,128)(2,1)S(1)} %get-tuple-element.30), channel_id=1, source_target_pairs={{0,4},{4,0},{1,5},{5,1},{2,6},{6,2},{3,7},{7,3},{8,12},{12,8},{9,1... | collective-permute-start | bytes 786440 | tf_op jit(solution)/shard_map/ppermute | solution.py:46
  27.5 8.2 %collective-permute-done.3.near = bf16[512,256]{1,0:T(8,128)(2,1)S(1)} collective-permute-done((bf16[512,256]{1,0:T(8,128)(2,1)S(1)}, bf16[512,256]{1,0:T(8,128)(2,1)S(1)}, u32[]{:S(2)}, u32[]{:S(2)}) %collective-permute-start.3) | collective-permute-done | bytes 262176 | tf_op jit(solution)/shard_map/ppermute | solution.py:46
  35.8 1.0 %pre_gradient.1.first = bf16[512,256]{1,0:T(8,128)(2,1)S(1)} custom-call(s32[2]{0:T(128)S(1)} %pad_add_fusion.1.where, bf16[512,256]{1,0:T(8,128)(2,1)S(1)} %get-tuple-element.21.keep, bf16[512,256]{1,0:T(8,128)(2,1)S(1)} %collective-permute-done.3.near, bf16[512,256]{1,0:T(8,128)(2,1)S(1)} %collective-permute-done.4.far, s32[16,128]{1,0:T(8,128)S(1)} %bitcast.10, ...), custom_call_target="tpu_custom_call" | custom-call | tf_op jit(solution)/shard_map/pre_gradient/pallas_call | solution.py:364
  36.8 0.7 collective-permute-start.8
  37.5 3.9 %collective-permute-start.6 = (bf16[512,256]{1,0:T(8,128)(2,1)S(1)}, bf16[512,256]{1,0:T(8,128)(2,1)S(1)}, u32[]{:S(2)}, u32[]{:S(2)}) collective-permute-start(bf16[512,256]{1,0:T(8,128)(2,1)S(1)} %pre_gradient.1.first), channel_id=1, source_target_pairs={{0,1},{1,0},{2,3},{3,2},{4,5},{5,4},{6,7},{7,6},{8,9},{9,8},{10,11... | collective-permute-start | bytes 786440 | tf_op jit(solution)/shard_map/ppermute | solution.py:46
  41.4 1.3 %collective-permute-start.9 = (bf16[512,256]{1,0:T(8,128)(2,1)S(1)}, bf16[512,256]{1,0:T(8,128)(2,1)S(1)}, u32[]{:S(2)}, u32[]{:S(2)}) collective-permute-start(bf16[512,256]{1,0:T(8,128)(2,1)S(1)} %collective-permute-done.8.across), channel_id=1, source_target_pairs={{1,0},{2,3},{5,4},{6,7},{9,8},{10,11},{13,12},{14,15},{17,16},{18,... | collective-permute-start | bytes 786440 | tf_op jit(solution)/shard_map/ppermute | solution.py:464
  42.7 3.2 %collective-permute-done.6.second = bf16[512,256]{1,0:T(8,128)(2,1)S(1)} collective-permute-done((bf16[512,256]{1,0:T(8,128)(2,1)S(1)}, bf16[512,256]{1,0:T(8,128)(2,1)S(1)}, u32[]{:S(2)}, u32[]{:S(2)}) %collective-permute-start.6) | collective-permute-done | bytes 262176 | tf_op jit(solution)/shard_map/ppermute | solution.py:46
  45.9 1.3 %collective-permute-start.10 = (bf16[512,256]{1,0:T(8,128)(2,1)S(1)}, bf16[512,256]{1,0:T(8,128)(2,1)S(1)}, u32[]{:S(2)}, u32[]{:S(2)}) collective-permute-start(bf16[512,256]{1,0:T(8,128)(2,1)S(1)} %collective-permute-done.6.second), channel_id=1, source_target_pairs={{2,0},{1,3},{6,4},{5,7},{10,8},{9,11},{14,12},{13,15},{18,16},{17,... | collective-permute-start | bytes 786440 | tf_op jit(solution)/shard_map/ppermute | solution.py:466
  47.2 0.7 collective-permute-start.7
  48.0 2.5 %early_product.1 = (f32[1152,256]{1,0:T(8,128)S(1)}, bf16[1024,1152]{1,0:T(8,128)(2,1)S(1)}) custom-call(s32[1]{0:T(128)} %bitcast.1.chan, bf16[2048,1152]{1,0:T(8,128)(2,1)} %spectra.3, bf16[512,256]{1,0:T(8,128)(2,1)S(1)} %pre_gradient.1.first, bf16[512,256]{1,0:T(8,128)(2,1)S(1)} %collective-permute-done.6.second), custom_call_target="tpu_custom_call" | custom-call | flops 603979776 | bytes 5898240 | tf_op jit(solution)/shard_map/early_product/pallas_call | solution.py:137
  50.5 7.4 %collective-permute-done.9.passed = bf16[512,256]{1,0:T(8,128)(2,1)S(1)} collective-permute-done((bf16[512,256]{1,0:T(8,128)(2,1)S(1)}, bf16[512,256]{1,0:T(8,128)(2,1)S(1)}, u32[]{:S(2)}, u32[]{:S(2)}) %collective-permute-start.9) | collective-permute-done | bytes 262176 | tf_op jit(solution)/shard_map/ppermute | solution.py:464
  57.9 1.4 %late_product.1 = (bf16[288,256]{1,0:T(8,128)(2,1)S(1)}, bf16[288,256]{1,0:T(8,128)(2,1)S(1)}, f32[288,256]{1,0:T(8,128)S(1)}, f32[288,256]{1,0:T(8,128)S(1)}) custom-call(s32[2]{0:T(128)S(1)} %pad_add_fusion.where, bf16[1024,1152]{1,0:T(8,128)(2,1)S(1)} %get-tuple-element.31.held, f32[1152,256]{1,0:T(8,128)S(1)} %get-tuple-element.32.before, ...), custom_call_target="tpu_custom_call" | custom-call | flops 603979776 | bytes 3538944 | tf_op jit(solution)/shard_map/late_product/pallas_call | solution.py:184
  59.5 0.5 collective-permute-start.14
  60.0 0.9 %collective-permute-done.11.second = bf16[288,256]{1,0:T(8,128)(2,1)S(1)} collective-permute-done((bf16[288,256]{1,0:T(8,128)(2,1)S(1)}, bf16[288,256]{1,0:T(8,128)(2,1)S(1)}, u32[]{:S(2)}, u32[]{:S(2)}) %collective-permute-start.11) | collective-permute-done | bytes 147488 | tf_op jit(solution)/shard_map/ppermute | solution.py:46
  60.8 1.6 %collective-permute-start.12 = (bf16[288,256]{1,0:T(8,128)(2,1)S(1)}, bf16[288,256]{1,0:T(8,128)(2,1)S(1)}, u32[]{:S(2)}, u32[]{:S(2)}) collective-permute-start(bf16[288,256]{1,0:T(8,128)(2,1)S(1)} %added.6.first), channel_id=1, source_target_pairs={{0,16},{4,20},{8,12},{12,8},{16,0},{20,4},{24,28},{28,24},{1,17},{... | collective-permute-start | bytes 442376 | tf_op jit(solution)/shard_map/ppermute | solution.py:419
  62.4 0.6 collective-permute-start.15
  63.0 3.0 %collective-permute-done.12.second = bf16[288,256]{1,0:T(8,128)(2,1)S(1)} collective-permute-done((bf16[288,256]{1,0:T(8,128)(2,1)S(1)}, bf16[288,256]{1,0:T(8,128)(2,1)S(1)}, u32[]{:S(2)}, u32[]{:S(2)}) %collective-permute-start.12) | collective-permute-done | bytes 147488 | tf_op jit(solution)/shard_map/ppermute | solution.py:419
  66.1 1.6 %collective-permute-start.13 = (bf16[288,256]{1,0:T(8,128)(2,1)S(1)}, bf16[288,256]{1,0:T(8,128)(2,1)S(1)}, u32[]{:S(2)}, u32[]{:S(2)}) collective-permute-start(bf16[288,256]{1,0:T(8,128)(2,1)S(1)} %added.7.first), channel_id=1, source_target_pairs={{0,4},{4,0},{8,24},{12,28},{16,20},{20,16},{24,8},{28,12},{1,5},{5... | collective-permute-start | bytes 442376 | tf_op jit(solution)/shard_map/ppermute | solution.py:419
  67.7 1.5 %collective-permute-start.16 = (bf16[288,256]{1,0:T(8,128)(2,1)S(1)}, bf16[288,256]{1,0:T(8,128)(2,1)S(1)}, u32[]{:S(2)}, u32[]{:S(2)}) collective-permute-start(bf16[288,256]{1,0:T(8,128)(2,1)S(1)} %added.10.first), channel_id=1, source_target_pairs={{0,4},{4,0},{8,24},{12,28},{16,20},{20,16},{24,8},{28,12},{1,5},{5... | collective-permute-start | bytes 442376 | tf_op jit(solution)/shard_map/ppermute | solution.py:419
  69.3 2.0 %collective-permute-done.13.second = bf16[288,256]{1,0:T(8,128)(2,1)S(1)} collective-permute-done((bf16[288,256]{1,0:T(8,128)(2,1)S(1)}, bf16[288,256]{1,0:T(8,128)(2,1)S(1)}, u32[]{:S(2)}, u32[]{:S(2)}) %collective-permute-start.13) | collective-permute-done | bytes 147488 | tf_op jit(solution)/shard_map/ppermute | solution.py:419
  71.4 1.5 %collective-permute-done.16.second = bf16[288,256]{1,0:T(8,128)(2,1)S(1)} collective-permute-done((bf16[288,256]{1,0:T(8,128)(2,1)S(1)}, bf16[288,256]{1,0:T(8,128)(2,1)S(1)}, u32[]{:S(2)}, u32[]{:S(2)}) %collective-permute-start.16) | collective-permute-done | bytes 147488 | tf_op jit(solution)/shard_map/ppermute | solution.py:419
  73.1 1.3 %collective-permute-done.18.refs_3_ = bf16[288,256]{1,0:T(8,128)(2,1)S(1)} collective-permute-done((bf16[288,256]{1,0:T(8,128)(2,1)S(1)}, bf16[288,256]{1,0:T(8,128)(2,1)S(1)}, u32[]{:S(2)}, u32[]{:S(2)}) %collective-permute-start.18) | collective-permute-done | bytes 147488 | tf_op jit(solution)/shard_map/ppermute | solution.py:46
  74.4 1.1 %collect.1 = f32[1152,256]{1,0:T(8,128)} custom-call(s32[1]{0:T(128)} %bitcast.core, bf16[288,256]{1,0:T(8,128)(2,1)S(1)} %added.8.refs_0_, bf16[288,256]{1,0:T(8,128)(2,1)S(1)} %added.11.refs_1_, bf16[288,256]{1,0:T(8,128)(2,1)S(1)} %collective-permute-done.17.refs_2_, bf16[288,256]{1,0:T(8,128)(2,1)S(1)} %collective-permute-done.18.refs_3_), custom_call_target="tpu_custom_call" | custom-call | tf_op jit(solution)/shard_map/collect/pallas_call | solution.py:388
  (38 shorter events, 0.8 us)
Async XLA Ops:
  0.0 9.5 %collective-permute-start = (s32[2048]{0:T(1024)}, s32[2048]{0:T(1024)S(1)}, u32[]{:S(2)}, u32[]{:S(2)}) collective-permute-start(s32[2048]{0:T(1024)} %refs_0_.1), channel_id=1, source_target_pairs={{0,4},{4,0},{1,5},{5,1},{2,6},{6,2},{3,7},{7,3},{8,12},{12,8},{9,1... | collective-permute-start | bytes 24584 | tf_op jit(solution)/shard_map/ppermute | solution.py:46
  3.9 5.6 %collective-permute-start.1 = (bf16[128,256]{1,0:T(8,128)(2,1)S(1)}, bf16[128,256]{1,0:T(8,128)(2,1)S(1)}, u32[]{:S(2)}, u32[]{:S(2)}) collective-permute-start(bf16[128,256]{1,0:T(8,128)(2,1)S(1)} %slice_select_fusion), channel_id=1, source_target_pairs={{0,4},{4,0},{1,5},{5,1},{2,6},{6,2},{3,7},{7,3},{8,12},{12,8},{9,1... | collective-permute-start | bytes 196616 | tf_op jit(solution)/shard_map/ppermute | solution.py:23
  3.9 1.1 %copy-start = (bf16[1152,256]{1,0:T(8,128)(2,1)S(1)}, bf16[1152,256]{1,0:T(8,128)(2,1)}, u32[]{:S(2)}) copy-start(bf16[1152,256]{1,0:T(8,128)(2,1)} %weight.1) | copy-start | bytes 1769476
  5.0 4.3 %copy-start.5 = (s32[8,4096]{1,0:T(8,128)S(1)}, s32[8,4096]{1,0:T(8,128)}, u32[]{:S(2)}) copy-start(s32[8,4096]{1,0:T(8,128)} %param.14) | copy-start | bytes 393220
  5.0 4.5 %copy-start.3 = (s32[2048]{0:T(1024)S(1)}, s32[2048]{0:T(1024)}, u32[]{:S(2)}) copy-start(s32[2048]{0:T(1024)} %refs_0_.1) | copy-start | bytes 24580
  5.0 4.5 %copy-start.4 = (f32[8,256]{1,0:T(8,128)S(1)}, f32[8,256]{1,0:T(8,128)}, u32[]{:S(2)}) copy-start(f32[8,256]{1,0:T(8,128)} %refs_5_.1) | copy-start | bytes 24580
  7.2 15.6 %collective-permute-start.2 = (bf16[512,256]{1,0:T(8,128)(2,1)S(1)}, bf16[512,256]{1,0:T(8,128)(2,1)S(1)}, u32[]{:S(2)}, u32[]{:S(2)}) collective-permute-start(bf16[512,256]{1,0:T(8,128)(2,1)S(1)} %project.1), channel_id=1, source_target_pairs={{0,1},{1,0},{2,3},{3,2},{4,5},{5,4},{6,7},{7,6},{8,9},{9,8},{10,11... | collective-permute-start | bytes 786440 | tf_op jit(solution)/shard_map/ppermute | solution.py:46
  9.5 26.2 %copy-start.1 = (s32[2048,1]{0,1:T(1,128)S(1)}, s32[2048,1]{0,1:T(1,128)}, u32[]{:S(2)}) copy-start(s32[2048,1]{0,1:T(1,128)} %param.10) | copy-start | bytes 24580
  9.5 26.2 %copy-start.2 = (f32[2048]{0:T(1024)S(1)}, f32[2048]{0:T(1024)}, u32[]{:S(2)}) copy-start(f32[2048]{0:T(1024)} %param.12) | copy-start | bytes 24580
  22.8 12.9 %collective-permute-start.3 = (bf16[512,256]{1,0:T(8,128)(2,1)S(1)}, bf16[512,256]{1,0:T(8,128)(2,1)S(1)}, u32[]{:S(2)}, u32[]{:S(2)}) collective-permute-start(bf16[512,256]{1,0:T(8,128)(2,1)S(1)} %get-tuple-element.27), channel_id=1, source_target_pairs={{0,1},{1,0},{2,3},{3,2},{4,5},{5,4},{6,7},{7,6},{8,9},{9,8},{10,11... | collective-permute-start | bytes 786440 | tf_op jit(solution)/shard_map/ppermute | solution.py:46
  23.2 12.6 %collective-permute-start.4 = (bf16[512,256]{1,0:T(8,128)(2,1)S(1)}, bf16[512,256]{1,0:T(8,128)(2,1)S(1)}, u32[]{:S(2)}, u32[]{:S(2)}) collective-permute-start(bf16[512,256]{1,0:T(8,128)(2,1)S(1)} %add_convert_fusion), channel_id=1, source_target_pairs={{0,2},{1,3},{2,0},{3,1},{4,6},{5,7},{6,4},{7,5},{8,10},{9,11},{10,... | collective-permute-start | bytes 786440 | tf_op jit(solution)/shard_map/ppermute | solution.py:46
  25.9 9.8 %collective-permute-start.5 = (bf16[512,256]{1,0:T(8,128)(2,1)S(1)}, bf16[512,256]{1,0:T(8,128)(2,1)S(1)}, u32[]{:S(2)}, u32[]{:S(2)}) collective-permute-start(bf16[512,256]{1,0:T(8,128)(2,1)S(1)} %get-tuple-element.30), channel_id=1, source_target_pairs={{0,4},{4,0},{1,5},{5,1},{2,6},{6,2},{3,7},{7,3},{8,12},{12,8},{9,1... | collective-permute-start | bytes 786440 | tf_op jit(solution)/shard_map/ppermute | solution.py:46
  36.8 4.6 %collective-permute-start.8 = (bf16[512,256]{1,0:T(8,128)(2,1)S(1)}, bf16[512,256]{1,0:T(8,128)(2,1)S(1)}, u32[]{:S(2)}, u32[]{:S(2)}) collective-permute-start(bf16[512,256]{1,0:T(8,128)(2,1)S(1)} %pre_gradient.1.first), channel_id=1, source_target_pairs={{1,2},{2,1},{5,6},{6,5},{9,10},{10,9},{13,14},{14,13},{17,18},{18,... | collective-permute-start | bytes 786440 | tf_op jit(solution)/shard_map/ppermute | solution.py:463
  37.5 8.4 %collective-permute-start.6 = (bf16[512,256]{1,0:T(8,128)(2,1)S(1)}, bf16[512,256]{1,0:T(8,128)(2,1)S(1)}, u32[]{:S(2)}, u32[]{:S(2)}) collective-permute-start(bf16[512,256]{1,0:T(8,128)(2,1)S(1)} %pre_gradient.1.first), channel_id=1, source_target_pairs={{0,1},{1,0},{2,3},{3,2},{4,5},{5,4},{6,7},{7,6},{8,9},{9,8},{10,11... | collective-permute-start | bytes 786440 | tf_op jit(solution)/shard_map/ppermute | solution.py:46
  41.4 16.5 %collective-permute-start.9 = (bf16[512,256]{1,0:T(8,128)(2,1)S(1)}, bf16[512,256]{1,0:T(8,128)(2,1)S(1)}, u32[]{:S(2)}, u32[]{:S(2)}) collective-permute-start(bf16[512,256]{1,0:T(8,128)(2,1)S(1)} %collective-permute-done.8.across), channel_id=1, source_target_pairs={{1,0},{2,3},{5,4},{6,7},{9,8},{10,11},{13,12},{14,15},{17,16},{18,... | collective-permute-start | bytes 786440 | tf_op jit(solution)/shard_map/ppermute | solution.py:464
  45.9 12.0 %collective-permute-start.10 = (bf16[512,256]{1,0:T(8,128)(2,1)S(1)}, bf16[512,256]{1,0:T(8,128)(2,1)S(1)}, u32[]{:S(2)}, u32[]{:S(2)}) collective-permute-start(bf16[512,256]{1,0:T(8,128)(2,1)S(1)} %collective-permute-done.6.second), channel_id=1, source_target_pairs={{2,0},{1,3},{6,4},{5,7},{10,8},{9,11},{14,12},{13,15},{18,16},{17,... | collective-permute-start | bytes 786440 | tf_op jit(solution)/shard_map/ppermute | solution.py:466
  47.2 10.7 %collective-permute-start.7 = (bf16[512,256]{1,0:T(8,128)(2,1)S(1)}, bf16[512,256]{1,0:T(8,128)(2,1)S(1)}, u32[]{:S(2)}, u32[]{:S(2)}) collective-permute-start(bf16[512,256]{1,0:T(8,128)(2,1)S(1)} %collective-permute-done.6.second), channel_id=1, source_target_pairs={{1,2},{2,1},{5,6},{6,5},{9,10},{10,9},{13,14},{14,13},{17,18},{18,... | collective-permute-start | bytes 786440 | tf_op jit(solution)/shard_map/ppermute | solution.py:465
  59.4 1.4 %collective-permute-start.11 = (bf16[288,256]{1,0:T(8,128)(2,1)S(1)}, bf16[288,256]{1,0:T(8,128)(2,1)S(1)}, u32[]{:S(2)}, u32[]{:S(2)}) collective-permute-start(bf16[288,256]{1,0:T(8,128)(2,1)S(1)} %get-tuple-element.34), channel_id=1, source_target_pairs={{0,8},{8,0},{16,24},{24,16},{1,9},{9,1},{17,25},{25,17},{2,10},{10... | collective-permute-start | bytes 442376 | tf_op jit(solution)/shard_map/ppermute | solution.py:46
  59.5 2.9 %collective-permute-start.14 = (bf16[288,256]{1,0:T(8,128)(2,1)S(1)}, bf16[288,256]{1,0:T(8,128)(2,1)S(1)}, u32[]{:S(2)}, u32[]{:S(2)}) collective-permute-start(bf16[288,256]{1,0:T(8,128)(2,1)S(1)} %get-tuple-element.36), channel_id=1, source_target_pairs={{0,8},{8,0},{16,24},{24,16},{1,9},{9,1},{17,25},{25,17},{2,10},{10... | collective-permute-start | bytes 442376 | tf_op jit(solution)/shard_map/ppermute | solution.py:46
  60.8 5.2 %collective-permute-start.12 = (bf16[288,256]{1,0:T(8,128)(2,1)S(1)}, bf16[288,256]{1,0:T(8,128)(2,1)S(1)}, u32[]{:S(2)}, u32[]{:S(2)}) collective-permute-start(bf16[288,256]{1,0:T(8,128)(2,1)S(1)} %added.6.first), channel_id=1, source_target_pairs={{0,16},{4,20},{8,12},{12,8},{16,0},{20,4},{24,28},{28,24},{1,17},{... | collective-permute-start | bytes 442376 | tf_op jit(solution)/shard_map/ppermute | solution.py:419
  62.4 5.2 %collective-permute-start.15 = (bf16[288,256]{1,0:T(8,128)(2,1)S(1)}, bf16[288,256]{1,0:T(8,128)(2,1)S(1)}, u32[]{:S(2)}, u32[]{:S(2)}) collective-permute-start(bf16[288,256]{1,0:T(8,128)(2,1)S(1)} %added.9.first), channel_id=1, source_target_pairs={{0,16},{4,20},{8,12},{12,8},{16,0},{20,4},{24,28},{28,24},{1,17},{... | collective-permute-start | bytes 442376 | tf_op jit(solution)/shard_map/ppermute | solution.py:419
  66.1 5.2 %collective-permute-start.13 = (bf16[288,256]{1,0:T(8,128)(2,1)S(1)}, bf16[288,256]{1,0:T(8,128)(2,1)S(1)}, u32[]{:S(2)}, u32[]{:S(2)}) collective-permute-start(bf16[288,256]{1,0:T(8,128)(2,1)S(1)} %added.7.first), channel_id=1, source_target_pairs={{0,4},{4,0},{8,24},{12,28},{16,20},{20,16},{24,8},{28,12},{1,5},{5... | collective-permute-start | bytes 442376 | tf_op jit(solution)/shard_map/ppermute | solution.py:419
  67.7 5.2 %collective-permute-start.16 = (bf16[288,256]{1,0:T(8,128)(2,1)S(1)}, bf16[288,256]{1,0:T(8,128)(2,1)S(1)}, u32[]{:S(2)}, u32[]{:S(2)}) collective-permute-start(bf16[288,256]{1,0:T(8,128)(2,1)S(1)} %added.10.first), channel_id=1, source_target_pairs={{0,4},{4,0},{8,24},{12,28},{16,20},{20,16},{24,8},{28,12},{1,5},{5... | collective-permute-start | bytes 442376 | tf_op jit(solution)/shard_map/ppermute | solution.py:419
  71.3 1.7 %collective-permute-start.17 = (bf16[288,256]{1,0:T(8,128)(2,1)S(1)}, bf16[288,256]{1,0:T(8,128)(2,1)S(1)}, u32[]{:S(2)}, u32[]{:S(2)}) collective-permute-start(bf16[288,256]{1,0:T(8,128)(2,1)S(1)} %added.8.refs_0_), channel_id=1, source_target_pairs={{0,8},{8,0},{16,24},{24,16},{1,9},{9,1},{17,25},{25,17},{2,10},{10... | collective-permute-start | bytes 442376 | tf_op jit(solution)/shard_map/ppermute | solution.py:46
  73.0 1.4 %collective-permute-start.18 = (bf16[288,256]{1,0:T(8,128)(2,1)S(1)}, bf16[288,256]{1,0:T(8,128)(2,1)S(1)}, u32[]{:S(2)}, u32[]{:S(2)}) collective-permute-start(bf16[288,256]{1,0:T(8,128)(2,1)S(1)} %added.11.refs_1_), channel_id=1, source_target_pairs={{0,8},{8,0},{16,24},{24,16},{1,9},{9,1},{17,25},{25,17},{2,10},{10... | collective-permute-start | bytes 442376 | tf_op jit(solution)/shard_map/ppermute | solution.py:46

commit v10 on v9

--- a/solution.py
+++ b/solution.py
@@ -11,7 +11,6 @@
 HALO = 128
 MIB = 1024 * 1024
 LARGE = 52
-PIECES = 8
 
 
 def edges(value, axis, width):
@@ -76,31 +75,32 @@
         outs[turn // 2][first : first + chunk, :] = result.astype(outs[0].dtype)
 
 
-def project_kernel(chan, spectra, weight, out, held, near, sems):
-    copies = quarter_copies(spectra, weight, held, near, sems, chan[0], (3,))
+def project_kernel(bits, chan, spectra, weight, *refs):
+    *outs, held, near, sems = refs
+    copies = quarter_copies(spectra, weight, held, near, sems, chan[0], bits)
     for copy in copies:
         copy.start()
-    project_rows(copies, held, near, (out,))
-
-
-def project(spectra, weight, chan):
+    project_rows(copies, held, near, outs)
+
+
+def project(spectra, weight, chan, bits):
     depth, width = weight.shape
     rows = spectra.shape[0] // 4
     hbm = pl.BlockSpec(memory_space=pltpu.HBM)
     return pl.pallas_call(
-        project_kernel,
-        out_shape=jax.ShapeDtypeStruct((rows, width), jnp.bfloat16),
+        functools.partial(project_kernel, bits),
+        out_shape=(jax.ShapeDtypeStruct((rows, width), jnp.bfloat16),) * len(bits),
         in_specs=[pl.BlockSpec(memory_space=pltpu.SMEM), hbm, hbm],
-        out_specs=pl.BlockSpec(memory_space=pltpu.VMEM),
+        out_specs=(pl.BlockSpec(memory_space=pltpu.VMEM),) * len(bits),
         scratch_shapes=[
-            pltpu.VMEM((rows, depth), jnp.bfloat16),
+            pltpu.VMEM((len(bits) * rows, depth), jnp.bfloat16),
             pltpu.VMEM((depth, width), jnp.bfloat16),
-            pltpu.SemaphoreType.DMA((3,)),
+            pltpu.SemaphoreType.DMA((2 * len(bits) + 1,)),
         ],
         compiler_params=memory(LARGE),
         cost_estimate=pl.CostEstimate(
-            flops=2 * rows * depth * width,
-            bytes_accessed=2 * rows * depth + 2 * depth * width + 2 * rows * width,
+            flops=2 * len(bits) * rows * depth * width,
+            bytes_accessed=2 * len(bits) * rows * (depth + width) + 2 * depth * width,
             transcendentals=0,
         ),
         name="project",
@@ -198,37 +198,28 @@
     return outs[:2], outs[2:]
 
 
-def pixel_kernel(count, where, places, *refs):
-    lists = refs[: (len(refs) - 18) // 3]
-    names = refs[-len(lists) :]
-    refs = refs[len(lists) : -len(lists)]
-    cotangent, above, below, mixing, spectra, weight = refs[:6]
-    quarters, outs = refs[6:9], refs[9 : 9 + len(lists)]
-    table, scale, sums, held, near, block, factor, sems, more = refs[9 + len(lists) :]
+def pixel_kernel(count, bits, where, places, wanted, cotangent, above, below, mixing, spectra,
+                 weight, out, *refs):
+    quarters, refs = refs[: len(bits)], refs[len(bits) :]
+    table, scale, sums, held, near, names, block, factor, sems, more = refs
     start, chan = where[0], where[1]
     tile_rows, half = held.shape[0], table.shape[1]
+    listed = names.shape[0]
+    first_name = pl.multiple_of(start // listed * listed, listed)
+    copies = [
+        pltpu.make_async_copy(places, near, sems.at[4]),
+        pltpu.make_async_copy(wanted.at[pl.ds(first_name, listed)], names, sems.at[5]),
+    ]
     chunk = tile_rows // 4
-    piece = near.shape[0] // PIECES
-    copies = [
-        pltpu.make_async_copy(
-            places.at[pl.ds(n * piece, piece)], near.at[pl.ds(n * piece, piece)], sems.at[4 + n]
-        )
-        for n in range(PIECES)
-    ]
-    copies += [
-        pltpu.make_async_copy(wanted, name, sems.at[4 + PIECES + n])
-        for n, (wanted, name) in enumerate(zip(lists, names))
-    ]
-    parts = quarter_copies(spectra, weight, block, factor, more, chan, (2, 1, 0))
     rows = [
         pltpu.make_async_copy(
             cotangent.at[pl.ds(n * chunk, chunk)], held.at[pl.ds(n * chunk, chunk)], sems.at[n]
         )
         for n in range(4)
     ]
-    for copy in copies + parts + rows:
+    parts = quarter_copies(spectra, weight, block, factor, more, chan, bits) if bits else []
+    for copy in copies + rows + parts:
         copy.start()
-    project_rows(parts, block, factor, quarters)
 
     def fill(first, values):
         values = values.astype(jnp.float32)
@@ -246,83 +237,85 @@
         rows[n].wait()
         for first in range(n * chunk, (n + 1) * chunk, 256):
             fill(HALO + first, held[first : first + 256, :])
+    if bits:
+        project_rows(parts, block, factor, quarters)
     for copy in copies:
         copy.wait()
 
-    group = 16
-    for index, wanted in enumerate(names):
-
-        def body(turn, carry, index=index, wanted=wanted):
-            base = turn * group
-            totals = []
-            for n in range(group):
-                pixel = wanted[start + base + n]
-                terms = [table[pl.ds(2 * (pixel + HALO), 2), :]]
-                for k in range(NEIGH // 2):
-                    pair = near[k * tile_rows + pixel]
-                    for place, scale in ((pair & 0xFFFF, k), (pair >> 16, k + NEIGH // 2)):
-                        terms.append(table[pl.ds(place, 2), :] * scales[scale])
-                while len(terms) > 1:
-                    pairs = [x + y for x, y in zip(terms[::2], terms[1::2])]
-                    terms = pairs + terms[len(terms) // 2 * 2 :]
-                totals += terms
-            for n, total in enumerate(totals):
-                sums[pl.ds(2 * (index * count + base + n), 2), :] = total
-            return carry
-
-        lax.fori_loop(0, count // group, body, 0)
-    for index, out in enumerate(outs):
-        for side in range(2):
-            out[:, side * half : (side + 1) * half] = sums[
-                pl.ds(2 * index * count + side, count, stride=2), :
-            ].astype(out.dtype)
+    group = 32
+    offset = start - first_name
+
+    def body(turn, carry):
+        base = turn * group
+        totals = []
+        for n in range(group):
+            pixel = names[offset + base + n]
+            terms = [table[pl.ds(2 * (pixel + HALO), 2), :]]
+            for k in range(NEIGH // 2):
+                pair = near[k * tile_rows + pixel]
+                for place, scale in ((pair & 0xFFFF, k), (pair >> 16, k + NEIGH // 2)):
+                    terms.append(table[pl.ds(place, 2), :] * scales[scale])
+            while len(terms) > 1:
+                pairs = [x + y for x, y in zip(terms[::2], terms[1::2])]
+                terms = pairs + terms[len(terms) // 2 * 2 :]
+            totals += terms
+        for n, total in enumerate(totals):
+            sums[pl.ds(2 * (base + n), 2), :] = total
+        return carry
+
+    lax.fori_loop(0, count // group, body, 0)
+    for side in range(2):
+        out[:, side * half : (side + 1) * half] = sums[pl.ds(side, count, stride=2), :].astype(
+            out.dtype
+        )
 
 
 def pixel_rows(
-    cotangent, above, below, places, mixing, lists, start, count, spectra, weight, chan
+    cotangent, above, below, places, mixing, wanted, start, count, spectra, weight, chan, bits
 ):
     tile_rows, width = cotangent.shape
     depth, rows = spectra.shape[1], spectra.shape[0] // 4
+    listed = min(wanted.shape[0], 1024)
     anywhere = pl.BlockSpec(memory_space=pl.ANY)
     hbm = pl.BlockSpec(memory_space=pltpu.HBM)
     vmem = pl.BlockSpec(memory_space=pltpu.VMEM)
     return pl.pallas_call(
-        functools.partial(pixel_kernel, count),
+        functools.partial(pixel_kernel, count, bits),
         out_shape=(
-            *[jax.ShapeDtypeStruct((rows, width), jnp.bfloat16)] * 3,
-            *[jax.ShapeDtypeStruct((count, width), jnp.bfloat16)] * len(lists),
+            jax.ShapeDtypeStruct((count, width), jnp.bfloat16),
+            *[jax.ShapeDtypeStruct((rows, width), jnp.bfloat16)] * len(bits),
         ),
         in_specs=[
             pl.BlockSpec(memory_space=pltpu.SMEM),
             anywhere,
-            *[anywhere] * len(lists),
+            anywhere,
             hbm,
             *[vmem] * 3,
             hbm,
             hbm,
         ],
-        out_specs=(vmem,) * (3 + len(lists)),
+        out_specs=(vmem,) * (1 + len(bits)),
         scratch_shapes=[
             pltpu.VMEM((2 * (tile_rows + 2 * HALO), width // 2), jnp.float32),
             pltpu.VMEM((2 * NEIGH, width // 2), jnp.float32),
-            pltpu.VMEM((2 * count * len(lists), width // 2), jnp.float32),
+            pltpu.VMEM((2 * count, width // 2), jnp.float32),
             pltpu.VMEM(cotangent.shape, cotangent.dtype),
             pltpu.SMEM(places.shape, jnp.int32),
-            pltpu.VMEM((3 * rows, depth), jnp.bfloat16),
+            pltpu.SMEM((listed,), jnp.int32),
+            pltpu.VMEM((max(len(bits), 1) * rows, depth), jnp.bfloat16),
             pltpu.VMEM((depth, width), jnp.bfloat16),
-            pltpu.SemaphoreType.DMA((4 + PIECES + len(lists),)),
-            pltpu.SemaphoreType.DMA((7,)),
-            *[pltpu.SMEM(names.shape, jnp.int32) for names in lists],
+            pltpu.SemaphoreType.DMA((6,)),
+            pltpu.SemaphoreType.DMA((2 * len(bits) + 1,)),
         ],
         compiler_params=memory(LARGE),
         cost_estimate=pl.CostEstimate(
-            flops=6 * NEIGH * tile_rows * 256 * width,
+            flops=8 * NEIGH * count * 2048 * width,
             bytes_accessed=4 * tile_rows * width,
             transcendentals=0,
         ),
         name="pixel_rows",
     )(
-        jnp.stack([start, chan]), places, *lists, cotangent, above, below, mixing, spectra, weight
+        jnp.stack([start, chan]), places, wanted, cotangent, above, below, mixing, spectra, weight
     )
 
 
@@ -429,29 +422,33 @@
     first_row = chan * quarter
     middle = [(1, 2), (2, 1)]
 
-    near_first = swap(project(spectra, enc_weight, chan), "chan", 1)
+    near_first = swap(project(spectra, enc_weight, chan, (3,))[0], "chan", 1)
     places = (adjoint - (tile * tile_rows - HALO)) * 2
     places = (places[: NEIGH // 2] | (places[NEIGH // 2 :] << 16)).reshape(-1)
 
     above, below = edges(cotangent, "pix", HALO)
     capacity = 2 * quarter // tile_count
     pixels = (cotangent, above, below, places, mixing)
-    rest = (spectra, enc_weight, chan)
-    if capacity >= quarter and tile_count == 2:
-        lists = (pix_local, swap(pix_local, "pix", 1))
-        shared, send, keep, mine, rows = pixel_rows(*pixels, lists, first_row, quarter, *rest)
+    rest = (spectra, enc_weight)
+    paired = capacity >= quarter and tile_count == 2
+    if paired:
+        wanted, start, count = swap(pix_local, "pix", 1), first_row, quarter
     else:
         tile_ids = lax.dynamic_slice_in_dim(pix_tile[:, 0], first_row, quarter, 0)
         local_ids = lax.dynamic_slice_in_dim(pix_local, first_row, quarter, 0)
         slot_index, wanted = requests(tile_ids, local_ids, capacity)
-        shared, send, keep, rows = pixel_rows(*pixels, (wanted,), 0 * chan, wanted.shape[0], *rest)
+        start, count = 0 * chan, wanted.shape[0]
+    rows, shared = pixel_rows(*pixels, wanted, start, count, *rest, chan, (2,))
     near_first, rows = lax.optimization_barrier((near_first, rows))
     passed_on = (shared.astype(jnp.float32) + near_first.astype(jnp.float32)).astype(jnp.bfloat16)
-    passed_on, rows, send = lax.optimization_barrier((passed_on, rows, send))
+    passed_on, rows, later = lax.optimization_barrier((passed_on, rows, chan))
     far = swap(passed_on, "chan", 2)
+    send, keep = project(*rest, later, (1, 0))
+    send, keep, later = lax.optimization_barrier((send, keep, later))
     near = swap(send, "chan", 1)
-    if capacity >= quarter and tile_count == 2:
+    if paired:
         answers = swap(rows, "pix", 1)
+        (mine,) = pixel_rows(*pixels, pix_local, later * quarter, count, *rest, later, ())
     else:
         answers = lax.all_to_all(
             rows.reshape(tile_count, capacity, -1), "pix", split_axis=0, concat_axis=0, tiled=True

time: 76.4 us -> 77.8 us (1.018)
  starting transfers between devices: 23.6 us -> 18.1 us
  waiting for transfers between devices: 27.7 us -> 31.3 us
  Pallas kernels: 21.7 us -> 25 us
    pallas_call x2 -> x4, Pallas kernels: 15.4 us -> 18.7 us  [the longest x2 13.3 us: pixel_rows(): pl.pallas_call(functools.partial(pixel_kernel, count, bits), out_shape=(j...]
    ppermute x10, starting transfers between devices: 14.3 us -> 11.3 us  [swap(): return lax.ppermute(value, axis, [(i, i ^ bit) for i in range(size)])]
    ppermute x4, waiting for transfers between devices: 6.56 us -> 9.07 us  [sum_over_panels(): parts = [added(part, lax.ppermute(part, both, perm)) for part in parts]]
    ppermute x4, starting transfers between devices: 5.29 us -> 2.79 us  [sum_over_panels(): parts = [added(part, lax.ppermute(part, both, perm)) for part in parts]]
    ppermute x1, waiting for transfers between devices: 7.45 us -> 8.66 us  [shards(): passed = lax.ppermute(across, 'chan', [(1, 0), (2, 3)])]
  transfers between devices with their start and end apart: 19 -> 19, of which waited for: 8 -> 9; matrix products, arithmetic and copies ran while one was open for 2% -> 2% of each run, Pallas kernels for 24% -> 28%
where the time goes in v10:
time: 77.8 us; the launch traced here: 77 us
  waiting for transfers between devices  31.3 us (40%)
  Pallas kernels  25 us (32%)
  starting transfers between devices  18.1 us (23%)
  other arithmetic  1.29 us (2%)
  local copies, waits for them, and re-layouts  1.09 us (1%)
    ppermute x10, waiting for transfers between devices, swap(): return lax.ppermute(value, axis, [(i, i ^ bit) for i in range(size)])  13.5 us
    pallas_call x2, Pallas kernels, pixel_rows(): pl.pallas_call(functools.partial(pixel_kernel, count, bits), out_shape=(j...  13.3 us
    ppermute x10, starting transfers between devices, swap(): return lax.ppermute(value, axis, [(i, i ^ bit) for i in range(size)])  11.3 us
    ppermute x4, waiting for transfers between devices, sum_over_panels(): parts = [added(part, lax.ppermute(part, both, perm)) for part in parts]  9.07 us
    ppermute x1, waiting for transfers between devices, shards(): passed = lax.ppermute(across, 'chan', [(1, 0), (2, 3)])  8.66 us
    pallas_call x2, Pallas kernels, project(): pl.pallas_call(functools.partial(project_kernel, bits), out_shape=(jax.Sh...  5.43 us
    ppermute x4, starting transfers between devices, sum_over_panels(): parts = [added(part, lax.ppermute(part, both, perm)) for part in parts]  2.79 us
    pallas_call x1, Pallas kernels, early_product(): pl.pallas_call(early_kernel, out_shape=(jax.ShapeDtypeStruct((depth, widt...  2.49 us
  transfers between devices with their start and end apart: 19, of which 9 were waited for; matrix products, arithmetic and copies ran while one was open for 2% of the time, Pallas kernels for 28%

profile of v10, /device:TPU:0, one launch (start us, length us, event | category | flops | bytes accessed | tf_op | source)
XLA Modules:
  0.0 77.0 jit_solution(5394669510631759918)
XLA Ops:
  0.0 3.0 %collective-permute-start = (s32[2048]{0:T(1024)}, s32[2048]{0:T(1024)S(1)}, u32[]{:S(2)}, u32[]{:S(2)}) collective-permute-start(s32[2048]{0:T(1024)} %wanted.1), channel_id=1, source_target_pairs={{0,4},{4,0},{1,5},{5,1},{2,6},{6,2},{3,7},{7,3},{8,12},{12,8},{9,1... | collective-permute-start | bytes 24584 | tf_op jit(solution)/shard_map/ppermute | solution.py:45
  3.0 0.9 %slice_select_fusion = bf16[128,256]{1,0:T(8,128)(2,1)S(1)} fusion(bf16[4096,256]{1,0:T(8,128)(2,1)} %cotangent.3, pred[]{:T(512)S(6)} %eq.3), kind=kLoop, calls=%fused_computation.5 | loop fusion | flops 32768 | bytes 196609 | tf_op jit(solution)/shard_map/jit(_where)/select_n | solution.py:22
  3.9 1.1 %copy-done = bf16[1152,256]{1,0:T(8,128)(2,1)S(1)} copy-done((bf16[1152,256]{1,0:T(8,128)(2,1)S(1)}, bf16[1152,256]{1,0:T(8,128)(2,1)}, u32[]{:S(2)}) %copy-start) | copy-done | bytes 589848
  5.0 2.3 %project.2 = bf16[512,256]{1,0:T(8,128)(2,1)S(1)} custom-call(s32[1]{0:T(128)} %bitcast.1.chan, bf16[2048,1152]{1,0:T(8,128)(2,1)} %spectra.9, bf16[1152,256]{1,0:T(8,128)(2,1)S(1)} %copy-done), custom_call_target="tpu_custom_call" | custom-call | flops 301989888 | bytes 2031616 | tf_op jit(solution)/shard_map/project/pallas_call | solution.py:90
  7.3 2.1 %collective-permute-start.2 = (bf16[512,256]{1,0:T(8,128)(2,1)S(1)}, bf16[512,256]{1,0:T(8,128)(2,1)S(1)}, u32[]{:S(2)}, u32[]{:S(2)}) collective-permute-start(bf16[512,256]{1,0:T(8,128)(2,1)S(1)} %project.2), channel_id=1, source_target_pairs={{0,1},{1,0},{2,3},{3,2},{4,5},{5,4},{6,7},{7,6},{8,9},{9,8},{10,11... | collective-permute-start | bytes 786440 | tf_op jit(solution)/shard_map/ppermute | solution.py:45
  9.7 7.2 %pixel_rows.2 = (bf16[512,256]{1,0:T(8,128)(2,1)S(1)}, bf16[512,256]{1,0:T(8,128)(2,1)S(1)}) custom-call(s32[2]{0:T(128)S(1)} %pad_add_fusion.2.where, s32[16384]{0:T(1024)S(1)} %bitcast.12, s32[2048]{0:T(1024)S(1)} %collective-permute-done.wanted, bf16[4096,256]{1,0:T(8,128)(2,1)} %cotangent.3, bf16[128,256]{1,0:T(8,128)(2,1)S(1)} %collective-permute-done.1.above.below, ...), custom_call_target="tpu_custom_call" | custom-call | flops 17179869184 | bytes 4194304 | tf_op jit(solution)/shard_map/pixel_rows/pallas_call | solution.py:282
  16.9 2.7 %collective-permute-start.4 = (bf16[512,256]{1,0:T(8,128)(2,1)S(1)}, bf16[512,256]{1,0:T(8,128)(2,1)S(1)}, u32[]{:S(2)}, u32[]{:S(2)}) collective-permute-start(bf16[512,256]{1,0:T(8,128)(2,1)S(1)} %add_convert_fusion), channel_id=1, source_target_pairs={{0,2},{1,3},{2,0},{3,1},{4,6},{5,7},{6,4},{7,5},{8,10},{9,11},{10,... | collective-permute-start | bytes 786440 | tf_op jit(solution)/shard_map/ppermute | solution.py:45
  19.6 1.5 %collective-permute-start.5 = (bf16[512,256]{1,0:T(8,128)(2,1)S(1)}, bf16[512,256]{1,0:T(8,128)(2,1)S(1)}, u32[]{:S(2)}, u32[]{:S(2)}) collective-permute-start(bf16[512,256]{1,0:T(8,128)(2,1)S(1)} %get-tuple-element.34), channel_id=1, source_target_pairs={{0,4},{4,0},{1,5},{5,1},{2,6},{6,2},{3,7},{7,3},{8,12},{12,8},{9,1... | collective-permute-start | bytes 786440 | tf_op jit(solution)/shard_map/ppermute | solution.py:45
  21.1 3.2 %project.3 = (bf16[512,256]{1,0:T(8,128)(2,1)S(1)}, bf16[512,256]{1,0:T(8,128)(2,1)S(1)}) custom-call(s32[1]{0:T(128)} %bitcast.4.chan, bf16[2048,1152]{1,0:T(8,128)(2,1)} %spectra.9, bf16[1152,256]{1,0:T(8,128)(2,1)S(1)} %copy-done.1), custom_call_target="tpu_custom_call" | custom-call | flops 603979776 | bytes 3473408 | tf_op jit(solution)/shard_map/project/pallas_call | solution.py:90
  24.3 0.5 collective-permute-start.3
  24.9 6.1 %pixel_rows.3.mine = bf16[512,256]{1,0:T(8,128)(2,1)S(1)} custom-call(s32[2]{0:T(128)S(1)} %pad_add_fusion.3.where, s32[16384]{0:T(1024)S(1)} %bitcast.13, s32[2048]{0:T(1024)S(1)} %copy-done.4, bf16[4096,256]{1,0:T(8,128)(2,1)} %cotangent.3, bf16[128,256]{1,0:T(8,128)(2,1)S(1)} %collective-permute-done.1.above.below, ...), custom_call_target="tpu_custom_call" | custom-call | flops 17179869184 | bytes 4194304 | tf_op jit(solution)/shard_map/pixel_rows/pallas_call | solution.py:282
  31.0 5.2 %collective-permute-done.3.near = bf16[512,256]{1,0:T(8,128)(2,1)S(1)} collective-permute-done((bf16[512,256]{1,0:T(8,128)(2,1)S(1)}, bf16[512,256]{1,0:T(8,128)(2,1)S(1)}, u32[]{:S(2)}, u32[]{:S(2)}) %collective-permute-start.3) | collective-permute-done | bytes 262176 | tf_op jit(solution)/shard_map/ppermute | solution.py:45
  36.2 1.0 %pre_gradient.1.first = bf16[512,256]{1,0:T(8,128)(2,1)S(1)} custom-call(s32[2]{0:T(128)S(1)} %pad_add_fusion.1.where, bf16[512,256]{1,0:T(8,128)(2,1)S(1)} %get-tuple-element.30.keep, bf16[512,256]{1,0:T(8,128)(2,1)S(1)} %collective-permute-done.3.near, bf16[512,256]{1,0:T(8,128)(2,1)S(1)} %collective-permute-done.4.far, s32[16,128]{1,0:T(8,128)S(1)} %bitcast.14, ...), custom_call_target="tpu_custom_call" | custom-call | tf_op jit(solution)/shard_map/pre_gradient/pallas_call | solution.py:357
  37.2 0.7 collective-permute-start.8
  37.9 0.9 %collective-permute-start.6 = (bf16[512,256]{1,0:T(8,128)(2,1)S(1)}, bf16[512,256]{1,0:T(8,128)(2,1)S(1)}, u32[]{:S(2)}, u32[]{:S(2)}) collective-permute-start(bf16[512,256]{1,0:T(8,128)(2,1)S(1)} %pre_gradient.1.first), channel_id=1, source_target_pairs={{0,1},{1,0},{2,3},{3,2},{4,5},{5,4},{6,7},{7,6},{8,9},{9,8},{10,11... | collective-permute-start | bytes 786440 | tf_op jit(solution)/shard_map/ppermute | solution.py:45
  38.8 1.3 %collective-permute-start.9 = (bf16[512,256]{1,0:T(8,128)(2,1)S(1)}, bf16[512,256]{1,0:T(8,128)(2,1)S(1)}, u32[]{:S(2)}, u32[]{:S(2)}) collective-permute-start(bf16[512,256]{1,0:T(8,128)(2,1)S(1)} %collective-permute-done.8.across), channel_id=1, source_target_pairs={{1,0},{2,3},{5,4},{6,7},{9,8},{10,11},{13,12},{14,15},{17,16},{18,... | collective-permute-start | bytes 786440 | tf_op jit(solution)/shard_map/ppermute | solution.py:461
  40.0 6.1 %collective-permute-done.6.second = bf16[512,256]{1,0:T(8,128)(2,1)S(1)} collective-permute-done((bf16[512,256]{1,0:T(8,128)(2,1)S(1)}, bf16[512,256]{1,0:T(8,128)(2,1)S(1)}, u32[]{:S(2)}, u32[]{:S(2)}) %collective-permute-start.6) | collective-permute-done | bytes 262176 | tf_op jit(solution)/shard_map/ppermute | solution.py:45
  46.2 1.3 %collective-permute-start.10 = (bf16[512,256]{1,0:T(8,128)(2,1)S(1)}, bf16[512,256]{1,0:T(8,128)(2,1)S(1)}, u32[]{:S(2)}, u32[]{:S(2)}) collective-permute-start(bf16[512,256]{1,0:T(8,128)(2,1)S(1)} %collective-permute-done.6.second), channel_id=1, source_target_pairs={{2,0},{1,3},{6,4},{5,7},{10,8},{9,11},{14,12},{13,15},{18,16},{17,... | collective-permute-start | bytes 786440 | tf_op jit(solution)/shard_map/ppermute | solution.py:463
  47.5 0.7 collective-permute-start.7
  48.2 2.5 %early_product.1 = (f32[1152,256]{1,0:T(8,128)S(1)}, bf16[1024,1152]{1,0:T(8,128)(2,1)S(1)}) custom-call(s32[1]{0:T(128)} %bitcast.1.chan, bf16[2048,1152]{1,0:T(8,128)(2,1)} %spectra.9, bf16[512,256]{1,0:T(8,128)(2,1)S(1)} %pre_gradient.1.first, bf16[512,256]{1,0:T(8,128)(2,1)S(1)} %collective-permute-done.6.second), custom_call_target="tpu_custom_call" | custom-call | flops 603979776 | bytes 5898240 | tf_op jit(solution)/shard_map/early_product/pallas_call | solution.py:137
  50.7 8.7 %collective-permute-done.9.passed = bf16[512,256]{1,0:T(8,128)(2,1)S(1)} collective-permute-done((bf16[512,256]{1,0:T(8,128)(2,1)S(1)}, bf16[512,256]{1,0:T(8,128)(2,1)S(1)}, u32[]{:S(2)}, u32[]{:S(2)}) %collective-permute-start.9) | collective-permute-done | bytes 262176 | tf_op jit(solution)/shard_map/ppermute | solution.py:461
  59.4 1.4 %late_product.1 = (bf16[288,256]{1,0:T(8,128)(2,1)S(1)}, bf16[288,256]{1,0:T(8,128)(2,1)S(1)}, f32[288,256]{1,0:T(8,128)S(1)}, f32[288,256]{1,0:T(8,128)S(1)}) custom-call(s32[2]{0:T(128)S(1)} %pad_add_fusion.where, bf16[1024,1152]{1,0:T(8,128)(2,1)S(1)} %get-tuple-element.35.held, f32[1152,256]{1,0:T(8,128)S(1)} %get-tuple-element.36.before, ...), custom_call_target="tpu_custom_call" | custom-call | flops 603979776 | bytes 3538944 | tf_op jit(solution)/shard_map/late_product/pallas_call | solution.py:184
  61.4 0.9 %collective-permute-done.11.second = bf16[288,256]{1,0:T(8,128)(2,1)S(1)} collective-permute-done((bf16[288,256]{1,0:T(8,128)(2,1)S(1)}, bf16[288,256]{1,0:T(8,128)(2,1)S(1)}, u32[]{:S(2)}, u32[]{:S(2)}) %collective-permute-start.11) | collective-permute-done | bytes 147488 | tf_op jit(solution)/shard_map/ppermute | solution.py:45
  62.3 1.6 %collective-permute-start.12 = (bf16[288,256]{1,0:T(8,128)(2,1)S(1)}, bf16[288,256]{1,0:T(8,128)(2,1)S(1)}, u32[]{:S(2)}, u32[]{:S(2)}) collective-permute-start(bf16[288,256]{1,0:T(8,128)(2,1)S(1)} %added.6.first), channel_id=1, source_target_pairs={{0,16},{4,20},{8,12},{12,8},{16,0},{20,4},{24,28},{28,24},{1,17},{... | collective-permute-start | bytes 442376 | tf_op jit(solution)/shard_map/ppermute | solution.py:412
  64.0 0.6 collective-permute-start.15
  64.5 3.0 %collective-permute-done.12.second = bf16[288,256]{1,0:T(8,128)(2,1)S(1)} collective-permute-done((bf16[288,256]{1,0:T(8,128)(2,1)S(1)}, bf16[288,256]{1,0:T(8,128)(2,1)S(1)}, u32[]{:S(2)}, u32[]{:S(2)}) %collective-permute-start.12) | collective-permute-done | bytes 147488 | tf_op jit(solution)/shard_map/ppermute | solution.py:412
  67.6 1.5 %collective-permute-done.15.second = bf16[288,256]{1,0:T(8,128)(2,1)S(1)} collective-permute-done((bf16[288,256]{1,0:T(8,128)(2,1)S(1)}, bf16[288,256]{1,0:T(8,128)(2,1)S(1)}, u32[]{:S(2)}, u32[]{:S(2)}) %collective-permute-start.15) | collective-permute-done | bytes 147488 | tf_op jit(solution)/shard_map/ppermute | solution.py:412
  69.2 0.6 collective-permute-start.16
  69.8 3.0 %collective-permute-done.13.second = bf16[288,256]{1,0:T(8,128)(2,1)S(1)} collective-permute-done((bf16[288,256]{1,0:T(8,128)(2,1)S(1)}, bf16[288,256]{1,0:T(8,128)(2,1)S(1)}, u32[]{:S(2)}, u32[]{:S(2)}) %collective-permute-start.13) | collective-permute-done | bytes 147488 | tf_op jit(solution)/shard_map/ppermute | solution.py:412
  72.9 1.5 %collective-permute-done.16.second = bf16[288,256]{1,0:T(8,128)(2,1)S(1)} collective-permute-done((bf16[288,256]{1,0:T(8,128)(2,1)S(1)}, bf16[288,256]{1,0:T(8,128)(2,1)S(1)}, u32[]{:S(2)}, u32[]{:S(2)}) %collective-permute-start.16) | collective-permute-done | bytes 147488 | tf_op jit(solution)/shard_map/ppermute | solution.py:412
  74.5 1.3 %collective-permute-done.18.refs_3_ = bf16[288,256]{1,0:T(8,128)(2,1)S(1)} collective-permute-done((bf16[288,256]{1,0:T(8,128)(2,1)S(1)}, bf16[288,256]{1,0:T(8,128)(2,1)S(1)}, u32[]{:S(2)}, u32[]{:S(2)}) %collective-permute-start.18) | collective-permute-done | bytes 147488 | tf_op jit(solution)/shard_map/ppermute | solution.py:45
  75.9 1.1 %collect.1 = f32[1152,256]{1,0:T(8,128)} custom-call(s32[1]{0:T(128)} %bitcast.core, bf16[288,256]{1,0:T(8,128)(2,1)S(1)} %added.8.refs_0_, bf16[288,256]{1,0:T(8,128)(2,1)S(1)} %added.11.refs_1_, bf16[288,256]{1,0:T(8,128)(2,1)S(1)} %collective-permute-done.17.refs_2_, bf16[288,256]{1,0:T(8,128)(2,1)S(1)} %collective-permute-done.18.refs_3_), custom_call_target="tpu_custom_call" | custom-call | tf_op jit(solution)/shard_map/collect/pallas_call | solution.py:381
  (43 shorter events, 1.5 us)
Async XLA Ops:
  0.0 9.6 %collective-permute-start = (s32[2048]{0:T(1024)}, s32[2048]{0:T(1024)S(1)}, u32[]{:S(2)}, u32[]{:S(2)}) collective-permute-start(s32[2048]{0:T(1024)} %wanted.1), channel_id=1, source_target_pairs={{0,4},{4,0},{1,5},{5,1},{2,6},{6,2},{3,7},{7,3},{8,12},{12,8},{9,1... | collective-permute-start | bytes 24584 | tf_op jit(solution)/shard_map/ppermute | solution.py:45
  3.9 5.8 %collective-permute-start.1 = (bf16[128,256]{1,0:T(8,128)(2,1)S(1)}, bf16[128,256]{1,0:T(8,128)(2,1)S(1)}, u32[]{:S(2)}, u32[]{:S(2)}) collective-permute-start(bf16[128,256]{1,0:T(8,128)(2,1)S(1)} %slice_select_fusion), channel_id=1, source_target_pairs={{0,4},{4,0},{1,5},{5,1},{2,6},{6,2},{3,7},{7,3},{8,12},{12,8},{9,1... | collective-permute-start | bytes 196616 | tf_op jit(solution)/shard_map/ppermute | solution.py:22
  3.9 1.1 %copy-start = (bf16[1152,256]{1,0:T(8,128)(2,1)S(1)}, bf16[1152,256]{1,0:T(8,128)(2,1)}, u32[]{:S(2)}) copy-start(bf16[1152,256]{1,0:T(8,128)(2,1)} %weight.7) | copy-start | bytes 1769476
  5.0 4.5 %copy-start.6 = (s32[8,4096]{1,0:T(8,128)S(1)}, s32[8,4096]{1,0:T(8,128)}, u32[]{:S(2)}) copy-start(s32[8,4096]{1,0:T(8,128)} %param.14) | copy-start | bytes 393220
  5.0 4.6 %copy-start.1 = (bf16[1152,256]{1,0:T(8,128)(2,1)S(1)}, bf16[1152,256]{1,0:T(8,128)(2,1)}, u32[]{:S(2)}) copy-start(bf16[1152,256]{1,0:T(8,128)(2,1)} %weight.7) | copy-start | bytes 1769476
  5.0 4.6 %copy-start.5 = (f32[8,256]{1,0:T(8,128)S(1)}, f32[8,256]{1,0:T(8,128)}, u32[]{:S(2)}) copy-start(f32[8,256]{1,0:T(8,128)} %mixing.3) | copy-start | bytes 24580
  7.3 9.6 %collective-permute-start.2 = (bf16[512,256]{1,0:T(8,128)(2,1)S(1)}, bf16[512,256]{1,0:T(8,128)(2,1)S(1)}, u32[]{:S(2)}, u32[]{:S(2)}) collective-permute-start(bf16[512,256]{1,0:T(8,128)(2,1)S(1)} %project.2), channel_id=1, source_target_pairs={{0,1},{1,0},{2,3},{3,2},{4,5},{5,4},{6,7},{7,6},{8,9},{9,8},{10,11... | collective-permute-start | bytes 786440 | tf_op jit(solution)/shard_map/ppermute | solution.py:45
  16.9 14.1 %collective-permute-start.4 = (bf16[512,256]{1,0:T(8,128)(2,1)S(1)}, bf16[512,256]{1,0:T(8,128)(2,1)S(1)}, u32[]{:S(2)}, u32[]{:S(2)}) collective-permute-start(bf16[512,256]{1,0:T(8,128)(2,1)S(1)} %add_convert_fusion), channel_id=1, source_target_pairs={{0,2},{1,3},{2,0},{3,1},{4,6},{5,7},{6,4},{7,5},{8,10},{9,11},{10,... | collective-permute-start | bytes 786440 | tf_op jit(solution)/shard_map/ppermute | solution.py:45
  19.6 11.4 %collective-permute-start.5 = (bf16[512,256]{1,0:T(8,128)(2,1)S(1)}, bf16[512,256]{1,0:T(8,128)(2,1)S(1)}, u32[]{:S(2)}, u32[]{:S(2)}) collective-permute-start(bf16[512,256]{1,0:T(8,128)(2,1)S(1)} %get-tuple-element.34), channel_id=1, source_target_pairs={{0,4},{4,0},{1,5},{5,1},{2,6},{6,2},{3,7},{7,3},{8,12},{12,8},{9,1... | collective-permute-start | bytes 786440 | tf_op jit(solution)/shard_map/ppermute | solution.py:45
  21.1 3.8 %copy-start.4 = (s32[2048]{0:T(1024)S(1)}, s32[2048]{0:T(1024)}, u32[]{:S(2)}) copy-start(s32[2048]{0:T(1024)} %wanted.1) | copy-start | bytes 24580
  24.3 11.9 %collective-permute-start.3 = (bf16[512,256]{1,0:T(8,128)(2,1)S(1)}, bf16[512,256]{1,0:T(8,128)(2,1)S(1)}, u32[]{:S(2)}, u32[]{:S(2)}) collective-permute-start(bf16[512,256]{1,0:T(8,128)(2,1)S(1)} %get-tuple-element.31), channel_id=1, source_target_pairs={{0,1},{1,0},{2,3},{3,2},{4,5},{5,4},{6,7},{7,6},{8,9},{9,8},{10,11... | collective-permute-start | bytes 786440 | tf_op jit(solution)/shard_map/ppermute | solution.py:45
  24.9 11.3 %copy-start.2 = (s32[2048,1]{0,1:T(1,128)S(1)}, s32[2048,1]{0,1:T(1,128)}, u32[]{:S(2)}) copy-start(s32[2048,1]{0,1:T(1,128)} %param.10) | copy-start | bytes 24580
  24.9 11.3 %copy-start.3 = (f32[2048]{0:T(1024)S(1)}, f32[2048]{0:T(1024)}, u32[]{:S(2)}) copy-start(f32[2048]{0:T(1024)} %param.12) | copy-start | bytes 24580
  37.2 1.5 %collective-permute-start.8 = (bf16[512,256]{1,0:T(8,128)(2,1)S(1)}, bf16[512,256]{1,0:T(8,128)(2,1)S(1)}, u32[]{:S(2)}, u32[]{:S(2)}) collective-permute-start(bf16[512,256]{1,0:T(8,128)(2,1)S(1)} %pre_gradient.1.first), channel_id=1, source_target_pairs={{1,2},{2,1},{5,6},{6,5},{9,10},{10,9},{13,14},{14,13},{17,18},{18,... | collective-permute-start | bytes 786440 | tf_op jit(solution)/shard_map/ppermute | solution.py:460
  37.9 8.3 %collective-permute-start.6 = (bf16[512,256]{1,0:T(8,128)(2,1)S(1)}, bf16[512,256]{1,0:T(8,128)(2,1)S(1)}, u32[]{:S(2)}, u32[]{:S(2)}) collective-permute-start(bf16[512,256]{1,0:T(8,128)(2,1)S(1)} %pre_gradient.1.first), channel_id=1, source_target_pairs={{0,1},{1,0},{2,3},{3,2},{4,5},{5,4},{6,7},{7,6},{8,9},{9,8},{10,11... | collective-permute-start | bytes 786440 | tf_op jit(solution)/shard_map/ppermute | solution.py:45
  38.8 20.6 %collective-permute-start.9 = (bf16[512,256]{1,0:T(8,128)(2,1)S(1)}, bf16[512,256]{1,0:T(8,128)(2,1)S(1)}, u32[]{:S(2)}, u32[]{:S(2)}) collective-permute-start(bf16[512,256]{1,0:T(8,128)(2,1)S(1)} %collective-permute-done.8.across), channel_id=1, source_target_pairs={{1,0},{2,3},{5,4},{6,7},{9,8},{10,11},{13,12},{14,15},{17,16},{18,... | collective-permute-start | bytes 786440 | tf_op jit(solution)/shard_map/ppermute | solution.py:461
  46.2 13.2 %collective-permute-start.10 = (bf16[512,256]{1,0:T(8,128)(2,1)S(1)}, bf16[512,256]{1,0:T(8,128)(2,1)S(1)}, u32[]{:S(2)}, u32[]{:S(2)}) collective-permute-start(bf16[512,256]{1,0:T(8,128)(2,1)S(1)} %collective-permute-done.6.second), channel_id=1, source_target_pairs={{2,0},{1,3},{6,4},{5,7},{10,8},{9,11},{14,12},{13,15},{18,16},{17,... | collective-permute-start | bytes 786440 | tf_op jit(solution)/shard_map/ppermute | solution.py:463
  47.5 11.9 %collective-permute-start.7 = (bf16[512,256]{1,0:T(8,128)(2,1)S(1)}, bf16[512,256]{1,0:T(8,128)(2,1)S(1)}, u32[]{:S(2)}, u32[]{:S(2)}) collective-permute-start(bf16[512,256]{1,0:T(8,128)(2,1)S(1)} %collective-permute-done.6.second), channel_id=1, source_target_pairs={{1,2},{2,1},{5,6},{6,5},{9,10},{10,9},{13,14},{14,13},{17,18},{18,... | collective-permute-start | bytes 786440 | tf_op jit(solution)/shard_map/ppermute | solution.py:462
  60.8 1.4 %collective-permute-start.11 = (bf16[288,256]{1,0:T(8,128)(2,1)S(1)}, bf16[288,256]{1,0:T(8,128)(2,1)S(1)}, u32[]{:S(2)}, u32[]{:S(2)}) collective-permute-start(bf16[288,256]{1,0:T(8,128)(2,1)S(1)} %get-tuple-element.38), channel_id=1, source_target_pairs={{0,8},{8,0},{16,24},{24,16},{1,9},{9,1},{17,25},{25,17},{2,10},{10... | collective-permute-start | bytes 442376 | tf_op jit(solution)/shard_map/ppermute | solution.py:45
  60.9 3.0 %collective-permute-start.14 = (bf16[288,256]{1,0:T(8,128)(2,1)S(1)}, bf16[288,256]{1,0:T(8,128)(2,1)S(1)}, u32[]{:S(2)}, u32[]{:S(2)}) collective-permute-start(bf16[288,256]{1,0:T(8,128)(2,1)S(1)} %get-tuple-element.40), channel_id=1, source_target_pairs={{0,8},{8,0},{16,24},{24,16},{1,9},{9,1},{17,25},{25,17},{2,10},{10... | collective-permute-start | bytes 442376 | tf_op jit(solution)/shard_map/ppermute | solution.py:45
  62.3 5.2 %collective-permute-start.12 = (bf16[288,256]{1,0:T(8,128)(2,1)S(1)}, bf16[288,256]{1,0:T(8,128)(2,1)S(1)}, u32[]{:S(2)}, u32[]{:S(2)}) collective-permute-start(bf16[288,256]{1,0:T(8,128)(2,1)S(1)} %added.6.first), channel_id=1, source_target_pairs={{0,16},{4,20},{8,12},{12,8},{16,0},{20,4},{24,28},{28,24},{1,17},{... | collective-permute-start | bytes 442376 | tf_op jit(solution)/shard_map/ppermute | solution.py:412
  64.0 5.2 %collective-permute-start.15 = (bf16[288,256]{1,0:T(8,128)(2,1)S(1)}, bf16[288,256]{1,0:T(8,128)(2,1)S(1)}, u32[]{:S(2)}, u32[]{:S(2)}) collective-permute-start(bf16[288,256]{1,0:T(8,128)(2,1)S(1)} %added.9.first), channel_id=1, source_target_pairs={{0,16},{4,20},{8,12},{12,8},{16,0},{20,4},{24,28},{28,24},{1,17},{... | collective-permute-start | bytes 442376 | tf_op jit(solution)/shard_map/ppermute | solution.py:412
  67.6 5.2 %collective-permute-start.13 = (bf16[288,256]{1,0:T(8,128)(2,1)S(1)}, bf16[288,256]{1,0:T(8,128)(2,1)S(1)}, u32[]{:S(2)}, u32[]{:S(2)}) collective-permute-start(bf16[288,256]{1,0:T(8,128)(2,1)S(1)} %added.7.first), channel_id=1, source_target_pairs={{0,4},{4,0},{8,24},{12,28},{16,20},{20,16},{24,8},{28,12},{1,5},{5... | collective-permute-start | bytes 442376 | tf_op jit(solution)/shard_map/ppermute | solution.py:412
  69.2 5.2 %collective-permute-start.16 = (bf16[288,256]{1,0:T(8,128)(2,1)S(1)}, bf16[288,256]{1,0:T(8,128)(2,1)S(1)}, u32[]{:S(2)}, u32[]{:S(2)}) collective-permute-start(bf16[288,256]{1,0:T(8,128)(2,1)S(1)} %added.10.first), channel_id=1, source_target_pairs={{0,4},{4,0},{8,24},{12,28},{16,20},{20,16},{24,8},{28,12},{1,5},{5... | collective-permute-start | bytes 442376 | tf_op jit(solution)/shard_map/ppermute | solution.py:412
  72.8 1.7 %collective-permute-start.17 = (bf16[288,256]{1,0:T(8,128)(2,1)S(1)}, bf16[288,256]{1,0:T(8,128)(2,1)S(1)}, u32[]{:S(2)}, u32[]{:S(2)}) collective-permute-start(bf16[288,256]{1,0:T(8,128)(2,1)S(1)} %added.8.refs_0_), channel_id=1, source_target_pairs={{0,8},{8,0},{16,24},{24,16},{1,9},{9,1},{17,25},{25,17},{2,10},{10... | collective-permute-start | bytes 442376 | tf_op jit(solution)/shard_map/ppermute | solution.py:45
  74.5 1.4 %collective-permute-start.18 = (bf16[288,256]{1,0:T(8,128)(2,1)S(1)}, bf16[288,256]{1,0:T(8,128)(2,1)S(1)}, u32[]{:S(2)}, u32[]{:S(2)}) collective-permute-start(bf16[288,256]{1,0:T(8,128)(2,1)S(1)} %added.11.refs_1_), channel_id=1, source_target_pairs={{0,8},{8,0},{16,24},{24,16},{1,9},{9,1},{17,25},{25,17},{2,10},{10... | collective-permute-start | bytes 442376 | tf_op jit(solution)/shard_map/ppermute | solution.py:45

commit v11 on v10

--- a/solution.py
+++ b/solution.py
@@ -113,24 +113,25 @@
     )
 
 
-def early_kernel(chan, spectra, first, second, total, late, held, sems):
+def early_kernel(chan, spectra, first, second, third, total, late, held, sems):
     rows = first.shape[0]
     copies = []
-    for turn in range(4):
-        start = pl.multiple_of((chan[0] ^ turn) * rows, rows)
-        target = (held, late)[turn // 2].at[pl.ds(turn % 2 * rows, rows)]
+    for turn, bits in enumerate((0, 1, 3, 2)):
+        start = pl.multiple_of((chan[0] ^ bits) * rows, rows)
+        target = held.at[pl.ds(turn * rows, rows)] if turn < 3 else late
         copies.append(pltpu.make_async_copy(spectra.at[pl.ds(start, rows)], target, sems.at[turn]))
     for copy in copies:
         copy.start()
     copies[0].wait()
     product = turned_product(held[:rows, :], first[...])
     copies[1].wait()
-    total[...] = product + turned_product(held[rows:, :], second[...])
+    product += turned_product(held[rows : 2 * rows, :], second[...])
     copies[2].wait()
+    total[...] = product + turned_product(held[2 * rows :, :], third[...])
     copies[3].wait()
 
 
-def early_product(spectra, chan, first, second):
+def early_product(spectra, chan, first, second, third):
     depth = spectra.shape[1]
     rows, width = first.shape
     vmem = pl.BlockSpec(memory_space=pltpu.VMEM)
@@ -138,45 +139,39 @@
         early_kernel,
         out_shape=(
             jax.ShapeDtypeStruct((depth, width), jnp.float32),
-            jax.ShapeDtypeStruct((2 * rows, depth), jnp.bfloat16),
+            jax.ShapeDtypeStruct((rows, depth), jnp.bfloat16),
         ),
         in_specs=[
             pl.BlockSpec(memory_space=pltpu.SMEM),
             pl.BlockSpec(memory_space=pltpu.HBM),
-            vmem,
-            vmem,
+            *[vmem] * 3,
         ],
         out_specs=(vmem, vmem),
         scratch_shapes=[
-            pltpu.VMEM((2 * rows, depth), jnp.bfloat16),
+            pltpu.VMEM((3 * rows, depth), jnp.bfloat16),
             pltpu.SemaphoreType.DMA((4,)),
         ],
         compiler_params=memory(48),
         cost_estimate=pl.CostEstimate(
-            flops=4 * rows * depth * width,
+            flops=6 * rows * depth * width,
             bytes_accessed=8 * rows * depth + 4 * depth * width,
             transcendentals=0,
         ),
         name="early_product",
-    )(chan.reshape(1), spectra, first, second)
-
-
-def late_kernel(where, held, before, crossed, passed, across, skipped, *outs):
+    )(chan.reshape(1), spectra, first, second, third)
+
+
+def late_kernel(core, held, before, rows, *outs):
     *outs, total = outs
-    chan, core = where[0], where[1]
-    inner = (chan == 1) | (chan == 2)
-    second = jnp.where(inner, crossed[...], passed[...])
-    third = jnp.where(inner, across[...], skipped[...])
-    rows = jnp.concatenate([second, third], axis=0)
-    total[...] = before[...] + turned_product(held[...], rows)
+    total[...] = before[...] + turned_product(held[...], rows[...])
     size = outs[0].shape[0]
     for index, out in enumerate(outs):
-        first = (core ^ (1 - index // 2)) * 2 * size + index % 2 * size
+        first = (core[0] ^ (1 - index // 2)) * 2 * size + index % 2 * size
         here = pl.ds(pl.multiple_of(first, size), size)
         out[...] = total[here, :].astype(out.dtype)
 
 
-def late_product(where, held, before, crossed, passed, across, skipped):
+def late_product(core, held, before, rows):
     size, width = before.shape[0] // 4, before.shape[1]
     spec = pl.BlockSpec(memory_space=pltpu.VMEM)
     send = jax.ShapeDtypeStruct((size, width), jnp.bfloat16)
@@ -184,7 +179,7 @@
     outs = pl.pallas_call(
         late_kernel,
         out_shape=(send, send, keep, keep),
-        in_specs=[pl.BlockSpec(memory_space=pltpu.SMEM)] + [spec] * 6,
+        in_specs=[pl.BlockSpec(memory_space=pltpu.SMEM)] + [spec] * 3,
         out_specs=(spec,) * 4,
         scratch_shapes=[pltpu.VMEM(before.shape, jnp.float32)],
         compiler_params=memory(16),
@@ -194,7 +189,7 @@
             transcendentals=0,
         ),
         name="late_product",
-    )(where, held, before, crossed, passed, across, skipped)
+    )(core.reshape(1), held, before, rows)
     return outs[:2], outs[2:]
 
 
@@ -420,7 +415,6 @@
     tile = lax.axis_index("pix")
     chan = lax.axis_index("chan")
     first_row = chan * quarter
-    middle = [(1, 2), (2, 1)]
 
     near_first = swap(project(spectra, enc_weight, chan, (3,))[0], "chan", 1)
     places = (adjoint - (tile * tile_rows - HALO)) * 2
@@ -438,14 +432,13 @@
         local_ids = lax.dynamic_slice_in_dim(pix_local, first_row, quarter, 0)
         slot_index, wanted = requests(tile_ids, local_ids, capacity)
         start, count = 0 * chan, wanted.shape[0]
-    rows, shared = pixel_rows(*pixels, wanted, start, count, *rest, chan, (2,))
+    rows, shared, send = pixel_rows(*pixels, wanted, start, count, *rest, chan, (2, 1))
     near_first, rows = lax.optimization_barrier((near_first, rows))
     passed_on = (shared.astype(jnp.float32) + near_first.astype(jnp.float32)).astype(jnp.bfloat16)
-    passed_on, rows, later = lax.optimization_barrier((passed_on, rows, chan))
+    passed_on, send, rows, later = lax.optimization_barrier((passed_on, send, rows, chan))
     far = swap(passed_on, "chan", 2)
-    send, keep = project(*rest, later, (1, 0))
-    send, keep, later = lax.optimization_barrier((send, keep, later))
     near = swap(send, "chan", 1)
+    (keep,) = project(*rest, later, (0,))
     if paired:
         answers = swap(rows, "pix", 1)
         (mine,) = pixel_rows(*pixels, pix_local, later * quarter, count, *rest, later, ())
@@ -456,15 +449,12 @@
         mine = answers = jnp.take(answers.reshape(tile_count * capacity, -1), slot_index, axis=0)
     grads = pre_gradient(tile, chan, keep, near, far, pix_tile, foot_weight, mine, answers)
 
+    across = swap(grads, "chan", 3)
     beside = swap(grads, "chan", 1)
-    across = lax.ppermute(grads, "chan", middle)
-    passed = lax.ppermute(across, "chan", [(1, 0), (2, 3)])
-    crossed = lax.ppermute(beside, "chan", middle)
-    skipped = lax.ppermute(beside, "chan", [(2, 0), (1, 3)])
+    last = swap(across, "chan", 1)
+    early, held = early_product(spectra, chan, grads, beside, across)
     core = lax.axis_index("obs") & 1
-    early, held = early_product(spectra, chan, grads, beside)
-    where = jnp.stack([chan, core])
-    send, keep = late_product(where, held, early, crossed, passed, across, skipped)
+    send, keep = late_product(core, held, early, last)
     if lax.axis_size("obs") == 4 and tile_count == 2:
         return sum_over_panels(core, keep, [swap(part, "obs", 1) for part in send])
     return lax.psum(collect(core, keep, send), ("obs", "pix"))

time: 77.8 us -> 69.9 us (0.90)
  waiting for transfers between devices: 31.3 us -> 18.9 us
  starting transfers between devices: 18.1 us -> 23 us
    ppermute x4 -> x0, waiting for transfers between devices: 8.67 us -> none  [the longest x1 8.66 us: shards(): passed = lax.ppermute(across, 'chan', [(1, 0), (2, 3)])]
    ppermute x10 -> x12, starting transfers between devices: 11.3 us -> 17.6 us  [swap(): return lax.ppermute(value, axis, [(i, i ^ bit) for i in range(size)])]
    ppermute x4 -> x0, starting transfers between devices: 3.92 us -> none  [the longest x1 1.28 us: shards(): passed = lax.ppermute(across, 'chan', [(1, 0), (2, 3)])]
    ppermute x4, starting transfers between devices: 2.79 us -> 5.32 us  [sum_over_panels(): parts = [added(part, lax.ppermute(part, both, perm)) for part in parts]]
    ppermute x4, waiting for transfers between devices: 9.07 us -> 6.56 us  [sum_over_panels(): parts = [added(part, lax.ppermute(part, both, perm)) for part in parts]]
    ppermute x10 -> x12, waiting for transfers between devices: 13.5 us -> 12.3 us  [swap(): return lax.ppermute(value, axis, [(i, i ^ bit) for i in range(size)])]
    pallas_call x1, Pallas kernels: 2.49 us -> 3.53 us  [early_product(): pl.pallas_call(early_kernel, out_shape=(jax.ShapeDtypeStruct((depth, widt...]
    pallas_call x2, Pallas kernels: 13.3 us -> 14.3 us  [pixel_rows(): pl.pallas_call(functools.partial(pixel_kernel, count, bits), out_shape=(j...]
  transfers between devices with their start and end apart: 19 -> 17, of which waited for: 9 -> 8; matrix products, arithmetic and copies ran while one was open for 2% -> 2% of each run, Pallas kernels for 28% -> 32%
where the time goes in v11:
time: 69.9 us; the launch traced here: 69.6 us
  Pallas kernels  25.2 us (36%)
  starting transfers between devices  23 us (33%)
  waiting for transfers between devices  18.9 us (27%)
  other arithmetic  1.21 us (2%)
  local copies, waits for them, and re-layouts  1.09 us (2%)
    ppermute x12, starting transfers between devices, swap(): return lax.ppermute(value, axis, [(i, i ^ bit) for i in range(size)])  17.6 us
    pallas_call x2, Pallas kernels, pixel_rows(): pl.pallas_call(functools.partial(pixel_kernel, count, bits), out_shape=(j...  14.3 us
    ppermute x12, waiting for transfers between devices, swap(): return lax.ppermute(value, axis, [(i, i ^ bit) for i in range(size)])  12.3 us
    ppermute x4, waiting for transfers between devices, sum_over_panels(): parts = [added(part, lax.ppermute(part, both, perm)) for part in parts]  6.56 us
    ppermute x4, starting transfers between devices, sum_over_panels(): parts = [added(part, lax.ppermute(part, both, perm)) for part in parts]  5.32 us
    pallas_call x2, Pallas kernels, project(): pl.pallas_call(functools.partial(project_kernel, bits), out_shape=(jax.Sh...  4.45 us
    pallas_call x1, Pallas kernels, early_product(): pl.pallas_call(early_kernel, out_shape=(jax.ShapeDtypeStruct((depth, widt...  3.53 us
  transfers between devices with their start and end apart: 17, of which 8 were waited for; matrix products, arithmetic and copies ran while one was open for 2% of the time, Pallas kernels for 32%

profile of v11, /device:TPU:0, one launch (start us, length us, event | category | flops | bytes accessed | tf_op | source)
XLA Modules:
  0.0 69.6 jit_solution(268953571918366897)
XLA Ops:
  0.0 3.0 %collective-permute-start = (s32[2048]{0:T(1024)}, s32[2048]{0:T(1024)S(1)}, u32[]{:S(2)}, u32[]{:S(2)}) collective-permute-start(s32[2048]{0:T(1024)} %wanted.1), channel_id=1, source_target_pairs={{0,4},{4,0},{1,5},{5,1},{2,6},{6,2},{3,7},{7,3},{8,12},{12,8},{9,1... | collective-permute-start | bytes 24584 | tf_op jit(solution)/shard_map/ppermute | solution.py:45
  3.0 0.9 %slice_select_fusion = bf16[128,256]{1,0:T(8,128)(2,1)S(1)} fusion(bf16[4096,256]{1,0:T(8,128)(2,1)} %cotangent.3, pred[]{:T(512)S(6)} %eq.3), kind=kLoop, calls=%fused_computation.5 | loop fusion | flops 32768 | bytes 196609 | tf_op jit(solution)/shard_map/jit(_where)/select_n | solution.py:22
  3.9 1.1 %copy-done = bf16[1152,256]{1,0:T(8,128)(2,1)S(1)} copy-done((bf16[1152,256]{1,0:T(8,128)(2,1)S(1)}, bf16[1152,256]{1,0:T(8,128)(2,1)}, u32[]{:S(2)}) %copy-start) | copy-done | bytes 589848
  5.0 2.3 %project.2 = bf16[512,256]{1,0:T(8,128)(2,1)S(1)} custom-call(s32[1]{0:T(128)} %bitcast.1.chan, bf16[2048,1152]{1,0:T(8,128)(2,1)} %spectra.9, bf16[1152,256]{1,0:T(8,128)(2,1)S(1)} %copy-done), custom_call_target="tpu_custom_call" | custom-call | flops 301989888 | bytes 2031616 | tf_op jit(solution)/shard_map/project/pallas_call | solution.py:90
  7.3 2.1 %collective-permute-start.2 = (bf16[512,256]{1,0:T(8,128)(2,1)S(1)}, bf16[512,256]{1,0:T(8,128)(2,1)S(1)}, u32[]{:S(2)}, u32[]{:S(2)}) collective-permute-start(bf16[512,256]{1,0:T(8,128)(2,1)S(1)} %project.2), channel_id=1, source_target_pairs={{0,1},{1,0},{2,3},{3,2},{4,5},{5,4},{6,7},{7,6},{8,9},{9,8},{10,11... | collective-permute-start | bytes 786440 | tf_op jit(solution)/shard_map/ppermute | solution.py:45
  9.4 0.1 pad_add_fusion.1.where
  9.5 0.1 pad_add_fusion.where
  9.7 8.2 %pixel_rows.2 = (bf16[512,256]{1,0:T(8,128)(2,1)S(1)}, bf16[512,256]{1,0:T(8,128)(2,1)S(1)}, bf16[512,256]{1,0:T(8,128)(2,1)S(1)}) custom-call(s32[2]{0:T(128)S(1)} %pad_add_fusion.1.where, s32[16384]{0:T(1024)S(1)} %bitcast.11, s32[2048]{0:T(1024)S(1)} %collective-permute-done.wanted, bf16[4096,256]{1,0:T(8,128)(2,1)} %cotangent.3, ...), custom_call_target="tpu_custom_call" | custom-call | flops 17179869184 | bytes 4194304 | tf_op jit(solution)/shard_map/pixel_rows/pallas_call | solution.py:277
  17.9 0.2 collective-permute-start.3
  18.1 2.9 %collective-permute-start.4 = (bf16[512,256]{1,0:T(8,128)(2,1)S(1)}, bf16[512,256]{1,0:T(8,128)(2,1)S(1)}, u32[]{:S(2)}, u32[]{:S(2)}) collective-permute-start(bf16[512,256]{1,0:T(8,128)(2,1)S(1)} %add_convert_fusion), channel_id=1, source_target_pairs={{0,2},{1,3},{2,0},{3,1},{4,6},{5,7},{6,4},{7,5},{8,10},{9,11},{10,... | collective-permute-start | bytes 786440 | tf_op jit(solution)/shard_map/ppermute | solution.py:45
  21.0 1.5 %collective-permute-start.5 = (bf16[512,256]{1,0:T(8,128)(2,1)S(1)}, bf16[512,256]{1,0:T(8,128)(2,1)S(1)}, u32[]{:S(2)}, u32[]{:S(2)}) collective-permute-start(bf16[512,256]{1,0:T(8,128)(2,1)S(1)} %get-tuple-element.28), channel_id=1, source_target_pairs={{0,4},{4,0},{1,5},{5,1},{2,6},{6,2},{3,7},{7,3},{8,12},{12,8},{9,1... | collective-permute-start | bytes 786440 | tf_op jit(solution)/shard_map/ppermute | solution.py:45
  22.6 6.1 %pixel_rows.3.mine = bf16[512,256]{1,0:T(8,128)(2,1)S(1)} custom-call(s32[2]{0:T(128)S(1)} %pad_add_fusion.2.where, s32[16384]{0:T(1024)S(1)} %bitcast.12, s32[2048]{0:T(1024)S(1)} %copy-done.4, bf16[4096,256]{1,0:T(8,128)(2,1)} %cotangent.3, bf16[128,256]{1,0:T(8,128)(2,1)S(1)} %collective-permute-done.1.above.below, ...), custom_call_target="tpu_custom_call" | custom-call | flops 17179869184 | bytes 4194304 | tf_op jit(solution)/shard_map/pixel_rows/pallas_call | solution.py:277
  28.8 2.2 %project.3.keep = bf16[512,256]{1,0:T(8,128)(2,1)S(1)} custom-call(s32[1]{0:T(128)} %bitcast.4.chan, bf16[2048,1152]{1,0:T(8,128)(2,1)} %spectra.9, bf16[1152,256]{1,0:T(8,128)(2,1)S(1)} %copy-done.1), custom_call_target="tpu_custom_call" | custom-call | flops 301989888 | bytes 2031616 | tf_op jit(solution)/shard_map/project/pallas_call | solution.py:90
  31.0 1.0 %pre_gradient.1.first = bf16[512,256]{1,0:T(8,128)(2,1)S(1)} custom-call(s32[2]{0:T(128)S(1)} %pad_add_fusion.where, bf16[512,256]{1,0:T(8,128)(2,1)S(1)} %project.3.keep, bf16[512,256]{1,0:T(8,128)(2,1)S(1)} %collective-permute-done.3.near, bf16[512,256]{1,0:T(8,128)(2,1)S(1)} %collective-permute-done.4.far, s32[16,128]{1,0:T(8,128)S(1)} %bitcast.13, ...), custom_call_target="tpu_custom_call" | custom-call | tf_op jit(solution)/shard_map/pre_gradient/pallas_call | solution.py:352
  32.1 4.6 %collective-permute-start.7 = (bf16[512,256]{1,0:T(8,128)(2,1)S(1)}, bf16[512,256]{1,0:T(8,128)(2,1)S(1)}, u32[]{:S(2)}, u32[]{:S(2)}) collective-permute-start(bf16[512,256]{1,0:T(8,128)(2,1)S(1)} %pre_gradient.1.first), channel_id=1, source_target_pairs={{0,3},{1,2},{2,1},{3,0},{4,7},{5,6},{6,5},{7,4},{8,11},{9,10},{10,... | collective-permute-start | bytes 786440 | tf_op jit(solution)/shard_map/ppermute | solution.py:45
  36.7 7.2 %collective-permute-done.7.third = bf16[512,256]{1,0:T(8,128)(2,1)S(1)} collective-permute-done((bf16[512,256]{1,0:T(8,128)(2,1)S(1)}, bf16[512,256]{1,0:T(8,128)(2,1)S(1)}, u32[]{:S(2)}, u32[]{:S(2)}) %collective-permute-start.7) | collective-permute-done | bytes 262176 | tf_op jit(solution)/shard_map/ppermute | solution.py:45
  43.9 2.5 %collective-permute-start.8 = (bf16[512,256]{1,0:T(8,128)(2,1)S(1)}, bf16[512,256]{1,0:T(8,128)(2,1)S(1)}, u32[]{:S(2)}, u32[]{:S(2)}) collective-permute-start(bf16[512,256]{1,0:T(8,128)(2,1)S(1)} %collective-permute-done.7.third), channel_id=1, source_target_pairs={{0,1},{1,0},{2,3},{3,2},{4,5},{5,4},{6,7},{7,6},{8,9},{9,8},{10,11... | collective-permute-start | bytes 786440 | tf_op jit(solution)/shard_map/ppermute | solution.py:45
  46.4 1.3 %collective-permute-done.6.second = bf16[512,256]{1,0:T(8,128)(2,1)S(1)} collective-permute-done((bf16[512,256]{1,0:T(8,128)(2,1)S(1)}, bf16[512,256]{1,0:T(8,128)(2,1)S(1)}, u32[]{:S(2)}, u32[]{:S(2)}) %collective-permute-start.6) | collective-permute-done | bytes 262176 | tf_op jit(solution)/shard_map/ppermute | solution.py:45
  47.7 3.5 %early_product.1 = (f32[1152,256]{1,0:T(8,128)S(1)}, bf16[512,1152]{1,0:T(8,128)(2,1)S(1)}) custom-call(s32[1]{0:T(128)} %bitcast.1.chan, bf16[2048,1152]{1,0:T(8,128)(2,1)} %spectra.9, bf16[512,256]{1,0:T(8,128)(2,1)S(1)} %pre_gradient.1.first, bf16[512,256]{1,0:T(8,128)(2,1)S(1)} %collective-permute-done.6.second, ...), custom_call_target="tpu_custom_call" | custom-call | flops 905969664 | bytes 5898240 | tf_op jit(solution)/shard_map/early_product/pallas_call | solution.py:138
  51.3 1.6 %collective-permute-done.8.rows = bf16[512,256]{1,0:T(8,128)(2,1)S(1)} collective-permute-done((bf16[512,256]{1,0:T(8,128)(2,1)S(1)}, bf16[512,256]{1,0:T(8,128)(2,1)S(1)}, u32[]{:S(2)}, u32[]{:S(2)}) %collective-permute-start.8) | collective-permute-done | bytes 262176 | tf_op jit(solution)/shard_map/ppermute | solution.py:45
  52.8 0.6 late_product.1
  53.5 0.5 collective-permute-start.12
  54.0 0.9 %collective-permute-done.9.second = bf16[288,256]{1,0:T(8,128)(2,1)S(1)} collective-permute-done((bf16[288,256]{1,0:T(8,128)(2,1)S(1)}, bf16[288,256]{1,0:T(8,128)(2,1)S(1)}, u32[]{:S(2)}, u32[]{:S(2)}) %collective-permute-start.9) | collective-permute-done | bytes 147488 | tf_op jit(solution)/shard_map/ppermute | solution.py:45
  54.9 1.6 %collective-permute-start.10 = (bf16[288,256]{1,0:T(8,128)(2,1)S(1)}, bf16[288,256]{1,0:T(8,128)(2,1)S(1)}, u32[]{:S(2)}, u32[]{:S(2)}) collective-permute-start(bf16[288,256]{1,0:T(8,128)(2,1)S(1)} %added.6.first), channel_id=1, source_target_pairs={{0,16},{4,20},{8,12},{12,8},{16,0},{20,4},{24,28},{28,24},{1,17},{... | collective-permute-start | bytes 442376 | tf_op jit(solution)/shard_map/ppermute | solution.py:407
  56.5 0.6 collective-permute-start.13
  57.1 3.0 %collective-permute-done.10.second = bf16[288,256]{1,0:T(8,128)(2,1)S(1)} collective-permute-done((bf16[288,256]{1,0:T(8,128)(2,1)S(1)}, bf16[288,256]{1,0:T(8,128)(2,1)S(1)}, u32[]{:S(2)}, u32[]{:S(2)}) %collective-permute-start.10) | collective-permute-done | bytes 147488 | tf_op jit(solution)/shard_map/ppermute | solution.py:407
  60.1 1.6 %collective-permute-start.11 = (bf16[288,256]{1,0:T(8,128)(2,1)S(1)}, bf16[288,256]{1,0:T(8,128)(2,1)S(1)}, u32[]{:S(2)}, u32[]{:S(2)}) collective-permute-start(bf16[288,256]{1,0:T(8,128)(2,1)S(1)} %added.7.first), channel_id=1, source_target_pairs={{0,4},{4,0},{8,24},{12,28},{16,20},{20,16},{24,8},{28,12},{1,5},{5... | collective-permute-start | bytes 442376 | tf_op jit(solution)/shard_map/ppermute | solution.py:407
  61.8 1.5 %collective-permute-start.14 = (bf16[288,256]{1,0:T(8,128)(2,1)S(1)}, bf16[288,256]{1,0:T(8,128)(2,1)S(1)}, u32[]{:S(2)}, u32[]{:S(2)}) collective-permute-start(bf16[288,256]{1,0:T(8,128)(2,1)S(1)} %added.10.first), channel_id=1, source_target_pairs={{0,4},{4,0},{8,24},{12,28},{16,20},{20,16},{24,8},{28,12},{1,5},{5... | collective-permute-start | bytes 442376 | tf_op jit(solution)/shard_map/ppermute | solution.py:407
  63.3 2.0 %collective-permute-done.11.second = bf16[288,256]{1,0:T(8,128)(2,1)S(1)} collective-permute-done((bf16[288,256]{1,0:T(8,128)(2,1)S(1)}, bf16[288,256]{1,0:T(8,128)(2,1)S(1)}, u32[]{:S(2)}, u32[]{:S(2)}) %collective-permute-start.11) | collective-permute-done | bytes 147488 | tf_op jit(solution)/shard_map/ppermute | solution.py:407
  65.5 1.5 %collective-permute-done.14.second = bf16[288,256]{1,0:T(8,128)(2,1)S(1)} collective-permute-done((bf16[288,256]{1,0:T(8,128)(2,1)S(1)}, bf16[288,256]{1,0:T(8,128)(2,1)S(1)}, u32[]{:S(2)}, u32[]{:S(2)}) %collective-permute-start.14) | collective-permute-done | bytes 147488 | tf_op jit(solution)/shard_map/ppermute | solution.py:407
  67.1 1.3 %collective-permute-done.16.refs_3_ = bf16[288,256]{1,0:T(8,128)(2,1)S(1)} collective-permute-done((bf16[288,256]{1,0:T(8,128)(2,1)S(1)}, bf16[288,256]{1,0:T(8,128)(2,1)S(1)}, u32[]{:S(2)}, u32[]{:S(2)}) %collective-permute-start.16) | collective-permute-done | bytes 147488 | tf_op jit(solution)/shard_map/ppermute | solution.py:45
  68.5 1.1 %collect.1 = f32[1152,256]{1,0:T(8,128)} custom-call(s32[1]{0:T(128)} %bitcast.core, bf16[288,256]{1,0:T(8,128)(2,1)S(1)} %added.8.refs_0_, bf16[288,256]{1,0:T(8,128)(2,1)S(1)} %added.11.refs_1_, bf16[288,256]{1,0:T(8,128)(2,1)S(1)} %collective-permute-done.15.refs_2_, bf16[288,256]{1,0:T(8,128)(2,1)S(1)} %collective-permute-done.16.refs_3_), custom_call_target="tpu_custom_call" | custom-call | tf_op jit(solution)/shard_map/collect/pallas_call | solution.py:376
  (38 shorter events, 0.7 us)
Async XLA Ops:
  0.0 9.6 %collective-permute-start = (s32[2048]{0:T(1024)}, s32[2048]{0:T(1024)S(1)}, u32[]{:S(2)}, u32[]{:S(2)}) collective-permute-start(s32[2048]{0:T(1024)} %wanted.1), channel_id=1, source_target_pairs={{0,4},{4,0},{1,5},{5,1},{2,6},{6,2},{3,7},{7,3},{8,12},{12,8},{9,1... | collective-permute-start | bytes 24584 | tf_op jit(solution)/shard_map/ppermute | solution.py:45
  3.9 5.8 %collective-permute-start.1 = (bf16[128,256]{1,0:T(8,128)(2,1)S(1)}, bf16[128,256]{1,0:T(8,128)(2,1)S(1)}, u32[]{:S(2)}, u32[]{:S(2)}) collective-permute-start(bf16[128,256]{1,0:T(8,128)(2,1)S(1)} %slice_select_fusion), channel_id=1, source_target_pairs={{0,4},{4,0},{1,5},{5,1},{2,6},{6,2},{3,7},{7,3},{8,12},{12,8},{9,1... | collective-permute-start | bytes 196616 | tf_op jit(solution)/shard_map/ppermute | solution.py:22
  3.9 1.1 %copy-start = (bf16[1152,256]{1,0:T(8,128)(2,1)S(1)}, bf16[1152,256]{1,0:T(8,128)(2,1)}, u32[]{:S(2)}) copy-start(bf16[1152,256]{1,0:T(8,128)(2,1)} %weight.7) | copy-start | bytes 1769476
  5.0 4.5 %copy-start.6 = (s32[8,4096]{1,0:T(8,128)S(1)}, s32[8,4096]{1,0:T(8,128)}, u32[]{:S(2)}) copy-start(s32[8,4096]{1,0:T(8,128)} %param.14) | copy-start | bytes 393220
  5.0 4.6 %copy-start.1 = (bf16[1152,256]{1,0:T(8,128)(2,1)S(1)}, bf16[1152,256]{1,0:T(8,128)(2,1)}, u32[]{:S(2)}) copy-start(bf16[1152,256]{1,0:T(8,128)(2,1)} %weight.7) | copy-start | bytes 1769476
  5.0 4.6 %copy-start.5 = (f32[8,256]{1,0:T(8,128)S(1)}, f32[8,256]{1,0:T(8,128)}, u32[]{:S(2)}) copy-start(f32[8,256]{1,0:T(8,128)} %mixing.3) | copy-start | bytes 24580
  7.3 10.6 %collective-permute-start.2 = (bf16[512,256]{1,0:T(8,128)(2,1)S(1)}, bf16[512,256]{1,0:T(8,128)(2,1)S(1)}, u32[]{:S(2)}, u32[]{:S(2)}) collective-permute-start(bf16[512,256]{1,0:T(8,128)(2,1)S(1)} %project.2), channel_id=1, source_target_pairs={{0,1},{1,0},{2,3},{3,2},{4,5},{5,4},{6,7},{7,6},{8,9},{9,8},{10,11... | collective-permute-start | bytes 786440 | tf_op jit(solution)/shard_map/ppermute | solution.py:45
  9.7 13.0 %copy-start.4 = (s32[2048]{0:T(1024)S(1)}, s32[2048]{0:T(1024)}, u32[]{:S(2)}) copy-start(s32[2048]{0:T(1024)} %wanted.1) | copy-start | bytes 24580
  17.9 13.0 %collective-permute-start.3 = (bf16[512,256]{1,0:T(8,128)(2,1)S(1)}, bf16[512,256]{1,0:T(8,128)(2,1)S(1)}, u32[]{:S(2)}, u32[]{:S(2)}) collective-permute-start(bf16[512,256]{1,0:T(8,128)(2,1)S(1)} %get-tuple-element.26), channel_id=1, source_target_pairs={{0,1},{1,0},{2,3},{3,2},{4,5},{5,4},{6,7},{7,6},{8,9},{9,8},{10,11... | collective-permute-start | bytes 786440 | tf_op jit(solution)/shard_map/ppermute | solution.py:45
  18.1 12.9 %collective-permute-start.4 = (bf16[512,256]{1,0:T(8,128)(2,1)S(1)}, bf16[512,256]{1,0:T(8,128)(2,1)S(1)}, u32[]{:S(2)}, u32[]{:S(2)}) collective-permute-start(bf16[512,256]{1,0:T(8,128)(2,1)S(1)} %add_convert_fusion), channel_id=1, source_target_pairs={{0,2},{1,3},{2,0},{3,1},{4,6},{5,7},{6,4},{7,5},{8,10},{9,11},{10,... | collective-permute-start | bytes 786440 | tf_op jit(solution)/shard_map/ppermute | solution.py:45
  21.0 10.0 %collective-permute-start.5 = (bf16[512,256]{1,0:T(8,128)(2,1)S(1)}, bf16[512,256]{1,0:T(8,128)(2,1)S(1)}, u32[]{:S(2)}, u32[]{:S(2)}) collective-permute-start(bf16[512,256]{1,0:T(8,128)(2,1)S(1)} %get-tuple-element.28), channel_id=1, source_target_pairs={{0,4},{4,0},{1,5},{5,1},{2,6},{6,2},{3,7},{7,3},{8,12},{12,8},{9,1... | collective-permute-start | bytes 786440 | tf_op jit(solution)/shard_map/ppermute | solution.py:45
  28.7 2.3 %copy-start.2 = (s32[2048,1]{0,1:T(1,128)S(1)}, s32[2048,1]{0,1:T(1,128)}, u32[]{:S(2)}) copy-start(s32[2048,1]{0,1:T(1,128)} %param.10) | copy-start | bytes 24580
  28.8 2.3 %copy-start.3 = (f32[2048]{0:T(1024)S(1)}, f32[2048]{0:T(1024)}, u32[]{:S(2)}) copy-start(f32[2048]{0:T(1024)} %param.12) | copy-start | bytes 24580
  32.1 11.8 %collective-permute-start.7 = (bf16[512,256]{1,0:T(8,128)(2,1)S(1)}, bf16[512,256]{1,0:T(8,128)(2,1)S(1)}, u32[]{:S(2)}, u32[]{:S(2)}) collective-permute-start(bf16[512,256]{1,0:T(8,128)(2,1)S(1)} %pre_gradient.1.first), channel_id=1, source_target_pairs={{0,3},{1,2},{2,1},{3,0},{4,7},{5,6},{6,5},{7,4},{8,11},{9,10},{10,... | collective-permute-start | bytes 786440 | tf_op jit(solution)/shard_map/ppermute | solution.py:45
  36.7 11.1 %collective-permute-start.6 = (bf16[512,256]{1,0:T(8,128)(2,1)S(1)}, bf16[512,256]{1,0:T(8,128)(2,1)S(1)}, u32[]{:S(2)}, u32[]{:S(2)}) collective-permute-start(bf16[512,256]{1,0:T(8,128)(2,1)S(1)} %pre_gradient.1.first), channel_id=1, source_target_pairs={{0,1},{1,0},{2,3},{3,2},{4,5},{5,4},{6,7},{7,6},{8,9},{9,8},{10,11... | collective-permute-start | bytes 786440 | tf_op jit(solution)/shard_map/ppermute | solution.py:45
  43.9 8.9 %collective-permute-start.8 = (bf16[512,256]{1,0:T(8,128)(2,1)S(1)}, bf16[512,256]{1,0:T(8,128)(2,1)S(1)}, u32[]{:S(2)}, u32[]{:S(2)}) collective-permute-start(bf16[512,256]{1,0:T(8,128)(2,1)S(1)} %collective-permute-done.7.third), channel_id=1, source_target_pairs={{0,1},{1,0},{2,3},{3,2},{4,5},{5,4},{6,7},{7,6},{8,9},{9,8},{10,11... | collective-permute-start | bytes 786440 | tf_op jit(solution)/shard_map/ppermute | solution.py:45
  53.4 1.4 %collective-permute-start.9 = (bf16[288,256]{1,0:T(8,128)(2,1)S(1)}, bf16[288,256]{1,0:T(8,128)(2,1)S(1)}, u32[]{:S(2)}, u32[]{:S(2)}) collective-permute-start(bf16[288,256]{1,0:T(8,128)(2,1)S(1)} %get-tuple-element.32), channel_id=1, source_target_pairs={{0,8},{8,0},{16,24},{24,16},{1,9},{9,1},{17,25},{25,17},{2,10},{10... | collective-permute-start | bytes 442376 | tf_op jit(solution)/shard_map/ppermute | solution.py:45
  53.5 3.0 %collective-permute-start.12 = (bf16[288,256]{1,0:T(8,128)(2,1)S(1)}, bf16[288,256]{1,0:T(8,128)(2,1)S(1)}, u32[]{:S(2)}, u32[]{:S(2)}) collective-permute-start(bf16[288,256]{1,0:T(8,128)(2,1)S(1)} %get-tuple-element.34), channel_id=1, source_target_pairs={{0,8},{8,0},{16,24},{24,16},{1,9},{9,1},{17,25},{25,17},{2,10},{10... | collective-permute-start | bytes 442376 | tf_op jit(solution)/shard_map/ppermute | solution.py:45
  54.9 5.2 %collective-permute-start.10 = (bf16[288,256]{1,0:T(8,128)(2,1)S(1)}, bf16[288,256]{1,0:T(8,128)(2,1)S(1)}, u32[]{:S(2)}, u32[]{:S(2)}) collective-permute-start(bf16[288,256]{1,0:T(8,128)(2,1)S(1)} %added.6.first), channel_id=1, source_target_pairs={{0,16},{4,20},{8,12},{12,8},{16,0},{20,4},{24,28},{28,24},{1,17},{... | collective-permute-start | bytes 442376 | tf_op jit(solution)/shard_map/ppermute | solution.py:407
  56.5 5.2 %collective-permute-start.13 = (bf16[288,256]{1,0:T(8,128)(2,1)S(1)}, bf16[288,256]{1,0:T(8,128)(2,1)S(1)}, u32[]{:S(2)}, u32[]{:S(2)}) collective-permute-start(bf16[288,256]{1,0:T(8,128)(2,1)S(1)} %added.9.first), channel_id=1, source_target_pairs={{0,16},{4,20},{8,12},{12,8},{16,0},{20,4},{24,28},{28,24},{1,17},{... | collective-permute-start | bytes 442376 | tf_op jit(solution)/shard_map/ppermute | solution.py:407
  60.1 5.2 %collective-permute-start.11 = (bf16[288,256]{1,0:T(8,128)(2,1)S(1)}, bf16[288,256]{1,0:T(8,128)(2,1)S(1)}, u32[]{:S(2)}, u32[]{:S(2)}) collective-permute-start(bf16[288,256]{1,0:T(8,128)(2,1)S(1)} %added.7.first), channel_id=1, source_target_pairs={{0,4},{4,0},{8,24},{12,28},{16,20},{20,16},{24,8},{28,12},{1,5},{5... | collective-permute-start | bytes 442376 | tf_op jit(solution)/shard_map/ppermute | solution.py:407
  61.8 5.2 %collective-permute-start.14 = (bf16[288,256]{1,0:T(8,128)(2,1)S(1)}, bf16[288,256]{1,0:T(8,128)(2,1)S(1)}, u32[]{:S(2)}, u32[]{:S(2)}) collective-permute-start(bf16[288,256]{1,0:T(8,128)(2,1)S(1)} %added.10.first), channel_id=1, source_target_pairs={{0,4},{4,0},{8,24},{12,28},{16,20},{20,16},{24,8},{28,12},{1,5},{5... | collective-permute-start | bytes 442376 | tf_op jit(solution)/shard_map/ppermute | solution.py:407
  65.4 1.7 %collective-permute-start.15 = (bf16[288,256]{1,0:T(8,128)(2,1)S(1)}, bf16[288,256]{1,0:T(8,128)(2,1)S(1)}, u32[]{:S(2)}, u32[]{:S(2)}) collective-permute-start(bf16[288,256]{1,0:T(8,128)(2,1)S(1)} %added.8.refs_0_), channel_id=1, source_target_pairs={{0,8},{8,0},{16,24},{24,16},{1,9},{9,1},{17,25},{25,17},{2,10},{10... | collective-permute-start | bytes 442376 | tf_op jit(solution)/shard_map/ppermute | solution.py:45
  67.0 1.4 %collective-permute-start.16 = (bf16[288,256]{1,0:T(8,128)(2,1)S(1)}, bf16[288,256]{1,0:T(8,128)(2,1)S(1)}, u32[]{:S(2)}, u32[]{:S(2)}) collective-permute-start(bf16[288,256]{1,0:T(8,128)(2,1)S(1)} %added.11.refs_1_), channel_id=1, source_target_pairs={{0,8},{8,0},{16,24},{24,16},{1,9},{9,1},{17,25},{25,17},{2,10},{10... | collective-permute-start | bytes 442376 | tf_op jit(solution)/shard_map/ppermute | solution.py:45

commit v12 on v11

--- a/solution.py
+++ b/solution.py
@@ -83,7 +83,7 @@
     project_rows(copies, held, near, outs)
 
 
-def project(spectra, weight, chan, bits):
+def project(spectra, weight, chan, bits, grant):
     depth, width = weight.shape
     rows = spectra.shape[0] // 4
     hbm = pl.BlockSpec(memory_space=pltpu.HBM)
@@ -97,7 +97,7 @@
             pltpu.VMEM((depth, width), jnp.bfloat16),
             pltpu.SemaphoreType.DMA((2 * len(bits) + 1,)),
         ],
-        compiler_params=memory(LARGE),
+        compiler_params=memory(grant),
         cost_estimate=pl.CostEstimate(
             flops=2 * len(bits) * rows * depth * width,
             bytes_accessed=2 * len(bits) * rows * (depth + width) + 2 * depth * width,
@@ -359,17 +359,19 @@
     )(jnp.stack([tile, chan]), keep, near, far, tiles, weights, mine, answers)
 
 
-def collect_kernel(core, *refs):
+def collect_kernel(where, *refs):
     *pieces, out = refs
-    half, rows = out.shape[0] // 2, pieces[0].shape[0]
-    count = len(pieces) // 2
+    core, bits = where[0], (where[1], where[2])
+    rows = pieces[0].shape[0]
+    count = len(pieces) // 4
     for index, piece in enumerate(pieces):
-        which = core[0] if index < count else 1 - core[0]
-        first = which * half + (index % count) * rows
-        out[pl.ds(pl.multiple_of(first, rows), rows), :] = piece[...].astype(jnp.float32)
-
-
-def collect(core, own, received):
+        other, index = divmod(index, 2 * count)
+        chunk, handed = divmod(index, 2)
+        place = (core ^ other) * 2 * count + 2 * chunk + (bits[other] ^ handed)
+        out[pl.ds(pl.multiple_of(place * rows, rows), rows), :] = piece[...].astype(jnp.float32)
+
+
+def collect(where, own, received):
     spec = pl.BlockSpec(memory_space=pltpu.VMEM)
     pieces = [*own, *received]
     rows, width = sum(piece.shape[0] for piece in pieces), own[0].shape[1]
@@ -380,7 +382,7 @@
         out_specs=spec,
         compiler_params=memory(16),
         name="collect",
-    )(core.reshape(1), *pieces)
+    )(where, *pieces)
 
 
 def add_kernel(first, second, out):
@@ -399,13 +401,45 @@
     )(first, second)
 
 
+def halve_kernel(where, first, second, send, keep):
+    rows = keep.shape[0]
+    for out, which in ((send, 1 - where[1]), (keep, where[1])):
+        here = pl.ds(pl.multiple_of(which * rows, rows), rows)
+        out[...] = (first[here, :] + second[here, :].astype(jnp.float32)).astype(out.dtype)
+
+
+def halved(where, first, second):
+    rows, width = first.shape[0] // 2, first.shape[1]
+    spec = pl.BlockSpec(memory_space=pltpu.VMEM)
+    return pl.pallas_call(
+        halve_kernel,
+        out_shape=(
+            jax.ShapeDtypeStruct((rows, width), jnp.bfloat16),
+            jax.ShapeDtypeStruct((rows, width), jnp.float32),
+        ),
+        in_specs=[pl.BlockSpec(memory_space=pltpu.SMEM), spec, spec],
+        out_specs=(spec, spec),
+        compiler_params=memory(16),
+        name="halved",
+    )(where, first, second)
+
+
 def sum_over_panels(core, parts, received):
     both = ("obs", "pix")
-    parts = [added(part, other) for part, other in zip(parts, received)]
-    for order in ((4, 1), (1, 4)):
-        perm = [(i, i ^ order[(i >> 1) & 1]) for i in range(8)]
-        parts = [added(part, lax.ppermute(part, both, perm)) for part in parts]
-    return collect(core, parts, [swap(part, "obs", 1) for part in parts])
+    x, y = lax.axis_index("obs") >> 1, lax.axis_index("pix")
+    where = jnp.stack([core, jnp.where(core == 0, x, y), jnp.where(core == 0, y, x)])
+
+    def along(value, step):
+        axis = ((4, 1), (1, 4))
+        return lax.ppermute(value, both, [(i, i ^ axis[(i >> 1) & 1][step]) for i in range(8)])
+
+    halves = [halved(where, part, other) for part, other in zip(parts, received)]
+    sums = [added(keep, along(send, 0)) for send, keep in halves]
+    sums = [added(value, along(value, 1)) for value in sums]
+    pieces = []
+    for value in sums:
+        pieces += [value, along(value, 0)]
+    return collect(where, pieces, [swap(piece, "obs", 1) for piece in pieces])
 
 
 def shards(spectra, enc_weight, pix_tile, pix_local, foot_weight, cotangent, adjoint, mixing):
@@ -416,7 +450,7 @@
     chan = lax.axis_index("chan")
     first_row = chan * quarter
 
-    near_first = swap(project(spectra, enc_weight, chan, (3,))[0], "chan", 1)
+    near_first = swap(project(spectra, enc_weight, chan, (3,), LARGE + 4)[0], "chan", 1)
     places = (adjoint - (tile * tile_rows - HALO)) * 2
     places = (places[: NEIGH // 2] | (places[NEIGH // 2 :] << 16)).reshape(-1)
 
@@ -438,7 +472,7 @@
     passed_on, send, rows, later = lax.optimization_barrier((passed_on, send, rows, chan))
     far = swap(passed_on, "chan", 2)
     near = swap(send, "chan", 1)
-    (keep,) = project(*rest, later, (0,))
+    (keep,) = project(*rest, later, (0,), LARGE)
     if paired:
         answers = swap(rows, "pix", 1)
         (mine,) = pixel_rows(*pixels, pix_local, later * quarter, count, *rest, later, ())
@@ -457,7 +491,9 @@
     send, keep = late_product(core, held, early, last)
     if lax.axis_size("obs") == 4 and tile_count == 2:
         return sum_over_panels(core, keep, [swap(part, "obs", 1) for part in send])
-    return lax.psum(collect(core, keep, send), ("obs", "pix"))
+    first, second = jnp.concatenate(keep), jnp.concatenate(send).astype(jnp.float32)
+    first, second = jnp.where(core == 0, first, second), jnp.where(core == 0, second, first)
+    return lax.psum(jnp.concatenate([first, second]), ("obs", "pix"))
 
 
 def solution(mesh):

time: 69.9 us -> 74.2 us (1.062)
  starting transfers between devices: 23 us -> 25.7 us
  Pallas kernels: 25.2 us -> 27.5 us
  local copies, waits for them, and re-layouts: 1.09 us -> 0.04 us
    ppermute x4 -> x6, starting transfers between devices: 5.32 us -> 7.75 us  [along(): lax.ppermute(value, both, [(i, i ^ axis[i >> 1 & 1][step]) for i in range...]
    pallas_call x0 -> x2, Pallas kernels: none -> 1.15 us  [halved(): pl.pallas_call(halve_kernel, out_shape=(jax.ShapeDtypeStruct((rows, width...]
    unnamed x15 -> x13, local copies, waits for them, and re-layouts: 1.09 us -> 0.04 us
    pallas_call x2, Pallas kernels: 4.45 us -> 5.2 us  [project(): pl.pallas_call(functools.partial(project_kernel, bits), out_shape=(jax.Sh...]
    ppermute x4 -> x6, waiting for transfers between devices: 6.56 us -> 6.97 us  [along(): lax.ppermute(value, both, [(i, i ^ axis[i >> 1 & 1][step]) for i in range...]
    ppermute x12 -> x14, starting transfers between devices: 17.6 us -> 17.9 us  [swap(): return lax.ppermute(value, axis, [(i, i ^ bit) for i in range(size)])]
    ppermute x12 -> x14, waiting for transfers between devices: 12.3 us -> 12.2 us  [swap(): return lax.ppermute(value, axis, [(i, i ^ bit) for i in range(size)])]
  transfers between devices with their start and end apart: 17 -> 21, of which waited for: 8 -> 11; matrix products, arithmetic and copies ran while one was open for 2% -> 2% of each run, Pallas kernels for 32% -> 33%
where the time goes in v12:
time: 74.2 us; the launch traced here: 74 us
  Pallas kernels  27.5 us (37%)
  starting transfers between devices  25.7 us (35%)
  waiting for transfers between devices  19.2 us (26%)
  other arithmetic  1.29 us (2%)
    ppermute x14, starting transfers between devices, swap(): return lax.ppermute(value, axis, [(i, i ^ bit) for i in range(size)])  17.9 us
    pallas_call x2, Pallas kernels, pixel_rows(): pl.pallas_call(functools.partial(pixel_kernel, count, bits), out_shape=(j...  14.3 us
    ppermute x14, waiting for transfers between devices, swap(): return lax.ppermute(value, axis, [(i, i ^ bit) for i in range(size)])  12.2 us
    ppermute x6, starting transfers between devices, along(): lax.ppermute(value, both, [(i, i ^ axis[i >> 1 & 1][step]) for i in range...  7.75 us
    ppermute x6, waiting for transfers between devices, along(): lax.ppermute(value, both, [(i, i ^ axis[i >> 1 & 1][step]) for i in range...  6.97 us
    pallas_call x2, Pallas kernels, project(): pl.pallas_call(functools.partial(project_kernel, bits), out_shape=(jax.Sh...  5.2 us
    pallas_call x1, Pallas kernels, early_product(): pl.pallas_call(early_kernel, out_shape=(jax.ShapeDtypeStruct((depth, widt...  3.53 us
    pallas_call x1, Pallas kernels, collect(): pl.pallas_call(collect_kernel, out_shape=jax.ShapeDtypeStruct((rows, widt...  1.64 us
  transfers between devices with their start and end apart: 21, of which 11 were waited for; matrix products, arithmetic and copies ran while one was open for 2% of the time, Pallas kernels for 33%

profile of v12, /device:TPU:0, one launch (start us, length us, event | category | flops | bytes accessed | tf_op | source)
XLA Modules:
  0.0 74.0 jit_solution(602123010018609360)
XLA Ops:
  0.0 3.0 %collective-permute-start = (s32[2048]{0:T(1024)}, s32[2048]{0:T(1024)S(1)}, u32[]{:S(2)}, u32[]{:S(2)}) collective-permute-start(s32[2048]{0:T(1024)} %wanted.1), channel_id=1, source_target_pairs={{0,4},{4,0},{1,5},{5,1},{2,6},{6,2},{3,7},{7,3},{8,12},{12,8},{9,1... | collective-permute-start | bytes 24584 | tf_op jit(solution)/shard_map/ppermute | solution.py:45
  3.0 0.9 %slice_select_fusion = bf16[128,256]{1,0:T(8,128)(2,1)S(1)} fusion(bf16[4096,256]{1,0:T(8,128)(2,1)} %cotangent.3, pred[]{:T(512)S(6)} %eq.8), kind=kLoop, calls=%fused_computation.5 | loop fusion | flops 32768 | bytes 196609 | tf_op jit(solution)/shard_map/jit(_where)/select_n | solution.py:22
  4.0 3.0 %project.2 = bf16[512,256]{1,0:T(8,128)(2,1)} custom-call(s32[1]{0:T(128)} %bitcast.3.chan, bf16[2048,1152]{1,0:T(8,128)(2,1)} %spectra.9, bf16[1152,256]{1,0:T(8,128)(2,1)} %weight.7), custom_call_target="tpu_custom_call" | custom-call | flops 301989888 | bytes 2031616 | tf_op jit(solution)/shard_map/project/pallas_call | solution.py:90
  7.0 2.1 %collective-permute-start.2 = (bf16[512,256]{1,0:T(8,128)(2,1)}, bf16[512,256]{1,0:T(8,128)(2,1)S(1)}, u32[]{:S(2)}, u32[]{:S(2)}) collective-permute-start(bf16[512,256]{1,0:T(8,128)(2,1)} %project.2), channel_id=1, source_target_pairs={{0,1},{1,0},{2,3},{3,2},{4,5},{5,4},{6,7},{7,6},{8,9},{9,8},{10,11... | collective-permute-start | bytes 786440 | tf_op jit(solution)/shard_map/ppermute | solution.py:45
  9.3 8.2 %pixel_rows.2 = (bf16[512,256]{1,0:T(8,128)(2,1)S(1)}, bf16[512,256]{1,0:T(8,128)(2,1)S(1)}, bf16[512,256]{1,0:T(8,128)(2,1)S(1)}) custom-call(s32[2]{0:T(128)S(1)} %pad_add_fusion.2.where, s32[16384]{0:T(1024)S(1)} %bitcast.13, s32[2048]{0:T(1024)S(1)} %collective-permute-done.wanted, bf16[4096,256]{1,0:T(8,128)(2,1)} %cotangent.3, ...), custom_call_target="tpu_custom_call" | custom-call | flops 17179869184 | bytes 4194304 | tf_op jit(solution)/shard_map/pixel_rows/pallas_call | solution.py:277
  18.1 2.6 %collective-permute-start.4 = (bf16[512,256]{1,0:T(8,128)(2,1)S(1)}, bf16[512,256]{1,0:T(8,128)(2,1)S(1)}, u32[]{:S(2)}, u32[]{:S(2)}) collective-permute-start(bf16[512,256]{1,0:T(8,128)(2,1)S(1)} %add_convert_fusion), channel_id=1, source_target_pairs={{0,2},{1,3},{2,0},{3,1},{4,6},{5,7},{6,4},{7,5},{8,10},{9,11},{10,... | collective-permute-start | bytes 786440 | tf_op jit(solution)/shard_map/ppermute | solution.py:45
  20.7 1.5 %collective-permute-start.5 = (bf16[512,256]{1,0:T(8,128)(2,1)S(1)}, bf16[512,256]{1,0:T(8,128)(2,1)S(1)}, u32[]{:S(2)}, u32[]{:S(2)}) collective-permute-start(bf16[512,256]{1,0:T(8,128)(2,1)S(1)} %get-tuple-element.32), channel_id=1, source_target_pairs={{0,4},{4,0},{1,5},{5,1},{2,6},{6,2},{3,7},{7,3},{8,12},{12,8},{9,1... | collective-permute-start | bytes 786440 | tf_op jit(solution)/shard_map/ppermute | solution.py:45
  22.3 6.1 %pixel_rows.3.mine = bf16[512,256]{1,0:T(8,128)(2,1)S(1)} custom-call(s32[2]{0:T(128)S(1)} %pad_add_fusion.3.where, s32[16384]{0:T(1024)S(1)} %bitcast.14, s32[2048]{0:T(1024)S(1)} %copy-done.3, bf16[4096,256]{1,0:T(8,128)(2,1)} %cotangent.3, bf16[128,256]{1,0:T(8,128)(2,1)S(1)} %collective-permute-done.1.above.below, ...), custom_call_target="tpu_custom_call" | custom-call | flops 17179869184 | bytes 4194304 | tf_op jit(solution)/shard_map/pixel_rows/pallas_call | solution.py:277
  28.4 2.2 %project.3.keep = bf16[512,256]{1,0:T(8,128)(2,1)S(1)} custom-call(s32[1]{0:T(128)} %bitcast.6.chan, bf16[2048,1152]{1,0:T(8,128)(2,1)} %spectra.9, bf16[1152,256]{1,0:T(8,128)(2,1)S(1)} %copy-done), custom_call_target="tpu_custom_call" | custom-call | flops 301989888 | bytes 2031616 | tf_op jit(solution)/shard_map/project/pallas_call | solution.py:90
  30.7 1.0 %pre_gradient.1.first = bf16[512,256]{1,0:T(8,128)(2,1)S(1)} custom-call(s32[2]{0:T(128)S(1)} %pad_add_fusion.1.where, bf16[512,256]{1,0:T(8,128)(2,1)S(1)} %project.3.keep, bf16[512,256]{1,0:T(8,128)(2,1)S(1)} %collective-permute-done.3.near, bf16[512,256]{1,0:T(8,128)(2,1)S(1)} %collective-permute-done.4.far, s32[16,128]{1,0:T(8,128)S(1)} %bitcast.15, ...), custom_call_target="tpu_custom_call" | custom-call | tf_op jit(solution)/shard_map/pre_gradient/pallas_call | solution.py:352
  31.7 4.6 %collective-permute-start.7 = (bf16[512,256]{1,0:T(8,128)(2,1)S(1)}, bf16[512,256]{1,0:T(8,128)(2,1)S(1)}, u32[]{:S(2)}, u32[]{:S(2)}) collective-permute-start(bf16[512,256]{1,0:T(8,128)(2,1)S(1)} %pre_gradient.1.first), channel_id=1, source_target_pairs={{0,3},{1,2},{2,1},{3,0},{4,7},{5,6},{6,5},{7,4},{8,11},{9,10},{10,... | collective-permute-start | bytes 786440 | tf_op jit(solution)/shard_map/ppermute | solution.py:45
  36.3 7.2 %collective-permute-done.7.third = bf16[512,256]{1,0:T(8,128)(2,1)S(1)} collective-permute-done((bf16[512,256]{1,0:T(8,128)(2,1)S(1)}, bf16[512,256]{1,0:T(8,128)(2,1)S(1)}, u32[]{:S(2)}, u32[]{:S(2)}) %collective-permute-start.7) | collective-permute-done | bytes 262176 | tf_op jit(solution)/shard_map/ppermute | solution.py:45
  43.5 2.6 %collective-permute-start.8 = (bf16[512,256]{1,0:T(8,128)(2,1)S(1)}, bf16[512,256]{1,0:T(8,128)(2,1)S(1)}, u32[]{:S(2)}, u32[]{:S(2)}) collective-permute-start(bf16[512,256]{1,0:T(8,128)(2,1)S(1)} %collective-permute-done.7.third), channel_id=1, source_target_pairs={{0,1},{1,0},{2,3},{3,2},{4,5},{5,4},{6,7},{7,6},{8,9},{9,8},{10,11... | collective-permute-start | bytes 786440 | tf_op jit(solution)/shard_map/ppermute | solution.py:45
  46.1 1.3 %collective-permute-done.6.second = bf16[512,256]{1,0:T(8,128)(2,1)S(1)} collective-permute-done((bf16[512,256]{1,0:T(8,128)(2,1)S(1)}, bf16[512,256]{1,0:T(8,128)(2,1)S(1)}, u32[]{:S(2)}, u32[]{:S(2)}) %collective-permute-start.6) | collective-permute-done | bytes 262176 | tf_op jit(solution)/shard_map/ppermute | solution.py:45
  47.4 3.5 %early_product.1 = (f32[1152,256]{1,0:T(8,128)S(1)}, bf16[512,1152]{1,0:T(8,128)(2,1)S(1)}) custom-call(s32[1]{0:T(128)} %bitcast.3.chan, bf16[2048,1152]{1,0:T(8,128)(2,1)} %spectra.9, bf16[512,256]{1,0:T(8,128)(2,1)S(1)} %pre_gradient.1.first, bf16[512,256]{1,0:T(8,128)(2,1)S(1)} %collective-permute-done.6.second, ...), custom_call_target="tpu_custom_call" | custom-call | flops 905969664 | bytes 5898240 | tf_op jit(solution)/shard_map/early_product/pallas_call | solution.py:138
  50.9 1.6 %collective-permute-done.8.rows = bf16[512,256]{1,0:T(8,128)(2,1)S(1)} collective-permute-done((bf16[512,256]{1,0:T(8,128)(2,1)S(1)}, bf16[512,256]{1,0:T(8,128)(2,1)S(1)}, u32[]{:S(2)}, u32[]{:S(2)}) %collective-permute-start.8) | collective-permute-done | bytes 262176 | tf_op jit(solution)/shard_map/ppermute | solution.py:45
  52.6 0.6 late_product.1
  53.8 0.8 %collective-permute-done.9.second = bf16[288,256]{1,0:T(8,128)(2,1)S(1)} collective-permute-done((bf16[288,256]{1,0:T(8,128)(2,1)S(1)}, bf16[288,256]{1,0:T(8,128)(2,1)S(1)}, u32[]{:S(2)}, u32[]{:S(2)}) %collective-permute-start.9) | collective-permute-done | bytes 147488 | tf_op jit(solution)/shard_map/ppermute | solution.py:45
  54.6 0.6 halved.2
  55.2 1.5 %collective-permute-start.10 = (bf16[144,256]{1,0:T(8,128)(2,1)S(1)}, bf16[144,256]{1,0:T(8,128)(2,1)S(1)}, u32[]{:S(2)}, u32[]{:S(2)}) collective-permute-start(bf16[144,256]{1,0:T(8,128)(2,1)S(1)} %get-tuple-element.38), channel_id=1, source_target_pairs={{0,16},{4,20},{8,12},{12,8},{16,0},{20,4},{24,28},{28,24},{1,17},{... | collective-permute-start | bytes 221192 | tf_op jit(solution)/shard_map/ppermute | solution.py:434
  56.7 0.6 halved.3
  57.3 0.6 collective-permute-start.14
  57.9 1.7 %collective-permute-done.10.second = bf16[144,256]{1,0:T(8,128)(2,1)S(1)} collective-permute-done((bf16[144,256]{1,0:T(8,128)(2,1)S(1)}, bf16[144,256]{1,0:T(8,128)(2,1)S(1)}, u32[]{:S(2)}, u32[]{:S(2)}) %collective-permute-start.10) | collective-permute-done | bytes 73760 | tf_op jit(solution)/shard_map/ppermute | solution.py:434
  59.6 1.5 %collective-permute-start.11 = (bf16[144,256]{1,0:T(8,128)(2,1)S(1)}, bf16[144,256]{1,0:T(8,128)(2,1)S(1)}, u32[]{:S(2)}, u32[]{:S(2)}) collective-permute-start(bf16[144,256]{1,0:T(8,128)(2,1)S(1)} %added.4.first), channel_id=1, source_target_pairs={{0,4},{4,0},{8,24},{12,28},{16,20},{20,16},{24,8},{28,12},{1,5},{5... | collective-permute-start | bytes 221192 | tf_op jit(solution)/shard_map/ppermute | solution.py:434
  61.2 1.0 %collective-permute-done.14.second = bf16[144,256]{1,0:T(8,128)(2,1)S(1)} collective-permute-done((bf16[144,256]{1,0:T(8,128)(2,1)S(1)}, bf16[144,256]{1,0:T(8,128)(2,1)S(1)}, u32[]{:S(2)}, u32[]{:S(2)}) %collective-permute-start.14) | collective-permute-done | bytes 73760 | tf_op jit(solution)/shard_map/ppermute | solution.py:434
  62.2 1.5 %collective-permute-start.15 = (bf16[144,256]{1,0:T(8,128)(2,1)S(1)}, bf16[144,256]{1,0:T(8,128)(2,1)S(1)}, u32[]{:S(2)}, u32[]{:S(2)}) collective-permute-start(bf16[144,256]{1,0:T(8,128)(2,1)S(1)} %added.6.first), channel_id=1, source_target_pairs={{0,4},{4,0},{8,24},{12,28},{16,20},{20,16},{24,8},{28,12},{1,5},{5... | collective-permute-start | bytes 221192 | tf_op jit(solution)/shard_map/ppermute | solution.py:434
  64.1 1.5 %collective-permute-start.12 = (bf16[144,256]{1,0:T(8,128)(2,1)S(1)}, bf16[144,256]{1,0:T(8,128)(2,1)S(1)}, u32[]{:S(2)}, u32[]{:S(2)}) collective-permute-start(bf16[144,256]{1,0:T(8,128)(2,1)S(1)} %added.5.refs_0_), channel_id=1, source_target_pairs={{0,16},{4,20},{8,12},{12,8},{16,0},{20,4},{24,28},{28,24},{1,17},{... | collective-permute-start | bytes 221192 | tf_op jit(solution)/shard_map/ppermute | solution.py:434
  65.6 1.1 %collective-permute-done.15.second = bf16[144,256]{1,0:T(8,128)(2,1)S(1)} collective-permute-done((bf16[144,256]{1,0:T(8,128)(2,1)S(1)}, bf16[144,256]{1,0:T(8,128)(2,1)S(1)}, u32[]{:S(2)}, u32[]{:S(2)}) %collective-permute-start.15) | collective-permute-done | bytes 73760 | tf_op jit(solution)/shard_map/ppermute | solution.py:434
  66.7 1.0 %collective-permute-start.16 = (bf16[144,256]{1,0:T(8,128)(2,1)S(1)}, bf16[144,256]{1,0:T(8,128)(2,1)S(1)}, u32[]{:S(2)}, u32[]{:S(2)}) collective-permute-start(bf16[144,256]{1,0:T(8,128)(2,1)S(1)} %added.7.refs_2_), channel_id=1, source_target_pairs={{0,16},{4,20},{8,12},{12,8},{16,0},{20,4},{24,28},{28,24},{1,17},{... | collective-permute-start | bytes 221192 | tf_op jit(solution)/shard_map/ppermute | solution.py:434
  68.5 2.6 %collective-permute-done.16.refs_3_ = bf16[144,256]{1,0:T(8,128)(2,1)S(1)} collective-permute-done((bf16[144,256]{1,0:T(8,128)(2,1)S(1)}, bf16[144,256]{1,0:T(8,128)(2,1)S(1)}, u32[]{:S(2)}, u32[]{:S(2)}) %collective-permute-start.16) | collective-permute-done | bytes 73760 | tf_op jit(solution)/shard_map/ppermute | solution.py:434
  71.1 1.2 %collective-permute-done.20.refs_7_ = bf16[144,256]{1,0:T(8,128)(2,1)S(1)} collective-permute-done((bf16[144,256]{1,0:T(8,128)(2,1)S(1)}, bf16[144,256]{1,0:T(8,128)(2,1)S(1)}, u32[]{:S(2)}, u32[]{:S(2)}) %collective-permute-start.20) | collective-permute-done | bytes 73760 | tf_op jit(solution)/shard_map/ppermute | solution.py:45
  72.4 1.6 %collect.1 = f32[1152,256]{1,0:T(8,128)} custom-call(s32[3]{0:T(128)S(1)} %pad_add_fusion.where, bf16[144,256]{1,0:T(8,128)(2,1)S(1)} %added.5.refs_0_, bf16[144,256]{1,0:T(8,128)(2,1)S(1)} %collective-permute-done.12.refs_1_, bf16[144,256]{1,0:T(8,128)(2,1)S(1)} %added.7.refs_2_, bf16[144,256]{1,0:T(8,128)(2,1)S(1)} %collective-permute-done.16.refs_3_, ...), custom_call_target="tpu_custom_call" | custom-call | tf_op jit(solution)/shard_map/collect/pallas_call | solution.py:378
  (45 shorter events, 2.7 us)
Async XLA Ops:
  0.0 9.3 %collective-permute-start = (s32[2048]{0:T(1024)}, s32[2048]{0:T(1024)S(1)}, u32[]{:S(2)}, u32[]{:S(2)}) collective-permute-start(s32[2048]{0:T(1024)} %wanted.1), channel_id=1, source_target_pairs={{0,4},{4,0},{1,5},{5,1},{2,6},{6,2},{3,7},{7,3},{8,12},{12,8},{9,1... | collective-permute-start | bytes 24584 | tf_op jit(solution)/shard_map/ppermute | solution.py:45
  3.9 5.5 %collective-permute-start.1 = (bf16[128,256]{1,0:T(8,128)(2,1)S(1)}, bf16[128,256]{1,0:T(8,128)(2,1)S(1)}, u32[]{:S(2)}, u32[]{:S(2)}) collective-permute-start(bf16[128,256]{1,0:T(8,128)(2,1)S(1)} %slice_select_fusion), channel_id=1, source_target_pairs={{0,4},{4,0},{1,5},{5,1},{2,6},{6,2},{3,7},{7,3},{8,12},{12,8},{9,1... | collective-permute-start | bytes 196616 | tf_op jit(solution)/shard_map/ppermute | solution.py:22
  3.9 5.2 %copy-start.5 = (s32[8,4096]{1,0:T(8,128)S(1)}, s32[8,4096]{1,0:T(8,128)}, u32[]{:S(2)}) copy-start(s32[8,4096]{1,0:T(8,128)} %param.14) | copy-start | bytes 393220
  3.9 5.4 %copy-start = (bf16[1152,256]{1,0:T(8,128)(2,1)S(1)}, bf16[1152,256]{1,0:T(8,128)(2,1)}, u32[]{:S(2)}) copy-start(bf16[1152,256]{1,0:T(8,128)(2,1)} %weight.7) | copy-start | bytes 1769476
  4.0 5.4 %copy-start.4 = (f32[8,256]{1,0:T(8,128)S(1)}, f32[8,256]{1,0:T(8,128)}, u32[]{:S(2)}) copy-start(f32[8,256]{1,0:T(8,128)} %mixing.3) | copy-start | bytes 24580
  7.0 10.5 %collective-permute-start.2 = (bf16[512,256]{1,0:T(8,128)(2,1)}, bf16[512,256]{1,0:T(8,128)(2,1)S(1)}, u32[]{:S(2)}, u32[]{:S(2)}) collective-permute-start(bf16[512,256]{1,0:T(8,128)(2,1)} %project.2), channel_id=1, source_target_pairs={{0,1},{1,0},{2,3},{3,2},{4,5},{5,4},{6,7},{7,6},{8,9},{9,8},{10,11... | collective-permute-start | bytes 786440 | tf_op jit(solution)/shard_map/ppermute | solution.py:45
  9.3 13.0 %copy-start.3 = (s32[2048]{0:T(1024)S(1)}, s32[2048]{0:T(1024)}, u32[]{:S(2)}) copy-start(s32[2048]{0:T(1024)} %wanted.1) | copy-start | bytes 24580
  17.6 13.0 %collective-permute-start.3 = (bf16[512,256]{1,0:T(8,128)(2,1)S(1)}, bf16[512,256]{1,0:T(8,128)(2,1)S(1)}, u32[]{:S(2)}, u32[]{:S(2)}) collective-permute-start(bf16[512,256]{1,0:T(8,128)(2,1)S(1)} %get-tuple-element.30), channel_id=1, source_target_pairs={{0,1},{1,0},{2,3},{3,2},{4,5},{5,4},{6,7},{7,6},{8,9},{9,8},{10,11... | collective-permute-start | bytes 786440 | tf_op jit(solution)/shard_map/ppermute | solution.py:45
  18.1 12.6 %collective-permute-start.4 = (bf16[512,256]{1,0:T(8,128)(2,1)S(1)}, bf16[512,256]{1,0:T(8,128)(2,1)S(1)}, u32[]{:S(2)}, u32[]{:S(2)}) collective-permute-start(bf16[512,256]{1,0:T(8,128)(2,1)S(1)} %add_convert_fusion), channel_id=1, source_target_pairs={{0,2},{1,3},{2,0},{3,1},{4,6},{5,7},{6,4},{7,5},{8,10},{9,11},{10,... | collective-permute-start | bytes 786440 | tf_op jit(solution)/shard_map/ppermute | solution.py:45
  20.7 10.0 %collective-permute-start.5 = (bf16[512,256]{1,0:T(8,128)(2,1)S(1)}, bf16[512,256]{1,0:T(8,128)(2,1)S(1)}, u32[]{:S(2)}, u32[]{:S(2)}) collective-permute-start(bf16[512,256]{1,0:T(8,128)(2,1)S(1)} %get-tuple-element.32), channel_id=1, source_target_pairs={{0,4},{4,0},{1,5},{5,1},{2,6},{6,2},{3,7},{7,3},{8,12},{12,8},{9,1... | collective-permute-start | bytes 786440 | tf_op jit(solution)/shard_map/ppermute | solution.py:45
  28.4 2.3 %copy-start.1 = (s32[2048,1]{0,1:T(1,128)S(1)}, s32[2048,1]{0,1:T(1,128)}, u32[]{:S(2)}) copy-start(s32[2048,1]{0,1:T(1,128)} %param.10) | copy-start | bytes 24580
  28.4 2.3 %copy-start.2 = (f32[2048]{0:T(1024)S(1)}, f32[2048]{0:T(1024)}, u32[]{:S(2)}) copy-start(f32[2048]{0:T(1024)} %param.12) | copy-start | bytes 24580
  31.7 11.8 %collective-permute-start.7 = (bf16[512,256]{1,0:T(8,128)(2,1)S(1)}, bf16[512,256]{1,0:T(8,128)(2,1)S(1)}, u32[]{:S(2)}, u32[]{:S(2)}) collective-permute-start(bf16[512,256]{1,0:T(8,128)(2,1)S(1)} %pre_gradient.1.first), channel_id=1, source_target_pairs={{0,3},{1,2},{2,1},{3,0},{4,7},{5,6},{6,5},{7,4},{8,11},{9,10},{10,... | collective-permute-start | bytes 786440 | tf_op jit(solution)/shard_map/ppermute | solution.py:45
  36.3 11.1 %collective-permute-start.6 = (bf16[512,256]{1,0:T(8,128)(2,1)S(1)}, bf16[512,256]{1,0:T(8,128)(2,1)S(1)}, u32[]{:S(2)}, u32[]{:S(2)}) collective-permute-start(bf16[512,256]{1,0:T(8,128)(2,1)S(1)} %pre_gradient.1.first), channel_id=1, source_target_pairs={{0,1},{1,0},{2,3},{3,2},{4,5},{5,4},{6,7},{7,6},{8,9},{9,8},{10,11... | collective-permute-start | bytes 786440 | tf_op jit(solution)/shard_map/ppermute | solution.py:45
  43.5 9.1 %collective-permute-start.8 = (bf16[512,256]{1,0:T(8,128)(2,1)S(1)}, bf16[512,256]{1,0:T(8,128)(2,1)S(1)}, u32[]{:S(2)}, u32[]{:S(2)}) collective-permute-start(bf16[512,256]{1,0:T(8,128)(2,1)S(1)} %collective-permute-done.7.third), channel_id=1, source_target_pairs={{0,1},{1,0},{2,3},{3,2},{4,5},{5,4},{6,7},{7,6},{8,9},{9,8},{10,11... | collective-permute-start | bytes 786440 | tf_op jit(solution)/shard_map/ppermute | solution.py:45
  53.2 1.4 %collective-permute-start.9 = (bf16[288,256]{1,0:T(8,128)(2,1)S(1)}, bf16[288,256]{1,0:T(8,128)(2,1)S(1)}, u32[]{:S(2)}, u32[]{:S(2)}) collective-permute-start(bf16[288,256]{1,0:T(8,128)(2,1)S(1)} %get-tuple-element.36), channel_id=1, source_target_pairs={{0,8},{8,0},{16,24},{24,16},{1,9},{9,1},{17,25},{25,17},{2,10},{10... | collective-permute-start | bytes 442376 | tf_op jit(solution)/shard_map/ppermute | solution.py:45
  53.2 3.5 %collective-permute-start.13 = (bf16[288,256]{1,0:T(8,128)(2,1)S(1)}, bf16[288,256]{1,0:T(8,128)(2,1)S(1)}, u32[]{:S(2)}, u32[]{:S(2)}) collective-permute-start(bf16[288,256]{1,0:T(8,128)(2,1)S(1)} %get-tuple-element.40), channel_id=1, source_target_pairs={{0,8},{8,0},{16,24},{24,16},{1,9},{9,1},{17,25},{25,17},{2,10},{10... | collective-permute-start | bytes 442376 | tf_op jit(solution)/shard_map/ppermute | solution.py:45
  55.2 4.4 %collective-permute-start.10 = (bf16[144,256]{1,0:T(8,128)(2,1)S(1)}, bf16[144,256]{1,0:T(8,128)(2,1)S(1)}, u32[]{:S(2)}, u32[]{:S(2)}) collective-permute-start(bf16[144,256]{1,0:T(8,128)(2,1)S(1)} %get-tuple-element.38), channel_id=1, source_target_pairs={{0,16},{4,20},{8,12},{12,8},{16,0},{20,4},{24,28},{28,24},{1,17},{... | collective-permute-start | bytes 221192 | tf_op jit(solution)/shard_map/ppermute | solution.py:434
  57.3 4.9 %collective-permute-start.14 = (bf16[144,256]{1,0:T(8,128)(2,1)S(1)}, bf16[144,256]{1,0:T(8,128)(2,1)S(1)}, u32[]{:S(2)}, u32[]{:S(2)}) collective-permute-start(bf16[144,256]{1,0:T(8,128)(2,1)S(1)} %get-tuple-element.42), channel_id=1, source_target_pairs={{0,16},{4,20},{8,12},{12,8},{16,0},{20,4},{24,28},{28,24},{1,17},{... | collective-permute-start | bytes 221192 | tf_op jit(solution)/shard_map/ppermute | solution.py:434
  59.6 4.4 %collective-permute-start.11 = (bf16[144,256]{1,0:T(8,128)(2,1)S(1)}, bf16[144,256]{1,0:T(8,128)(2,1)S(1)}, u32[]{:S(2)}, u32[]{:S(2)}) collective-permute-start(bf16[144,256]{1,0:T(8,128)(2,1)S(1)} %added.4.first), channel_id=1, source_target_pairs={{0,4},{4,0},{8,24},{12,28},{16,20},{20,16},{24,8},{28,12},{1,5},{5... | collective-permute-start | bytes 221192 | tf_op jit(solution)/shard_map/ppermute | solution.py:434
  62.2 4.4 %collective-permute-start.15 = (bf16[144,256]{1,0:T(8,128)(2,1)S(1)}, bf16[144,256]{1,0:T(8,128)(2,1)S(1)}, u32[]{:S(2)}, u32[]{:S(2)}) collective-permute-start(bf16[144,256]{1,0:T(8,128)(2,1)S(1)} %added.6.first), channel_id=1, source_target_pairs={{0,4},{4,0},{8,24},{12,28},{16,20},{20,16},{24,8},{28,12},{1,5},{5... | collective-permute-start | bytes 221192 | tf_op jit(solution)/shard_map/ppermute | solution.py:434
  64.1 4.4 %collective-permute-start.12 = (bf16[144,256]{1,0:T(8,128)(2,1)S(1)}, bf16[144,256]{1,0:T(8,128)(2,1)S(1)}, u32[]{:S(2)}, u32[]{:S(2)}) collective-permute-start(bf16[144,256]{1,0:T(8,128)(2,1)S(1)} %added.5.refs_0_), channel_id=1, source_target_pairs={{0,16},{4,20},{8,12},{12,8},{16,0},{20,4},{24,28},{28,24},{1,17},{... | collective-permute-start | bytes 221192 | tf_op jit(solution)/shard_map/ppermute | solution.py:434
  66.7 4.4 %collective-permute-start.16 = (bf16[144,256]{1,0:T(8,128)(2,1)S(1)}, bf16[144,256]{1,0:T(8,128)(2,1)S(1)}, u32[]{:S(2)}, u32[]{:S(2)}) collective-permute-start(bf16[144,256]{1,0:T(8,128)(2,1)S(1)} %added.7.refs_2_), channel_id=1, source_target_pairs={{0,16},{4,20},{8,12},{12,8},{16,0},{20,4},{24,28},{28,24},{1,17},{... | collective-permute-start | bytes 221192 | tf_op jit(solution)/shard_map/ppermute | solution.py:434
  67.7 3.4 %collective-permute-start.17 = (bf16[144,256]{1,0:T(8,128)(2,1)S(1)}, bf16[144,256]{1,0:T(8,128)(2,1)S(1)}, u32[]{:S(2)}, u32[]{:S(2)}) collective-permute-start(bf16[144,256]{1,0:T(8,128)(2,1)S(1)} %added.5.refs_0_), channel_id=1, source_target_pairs={{0,8},{8,0},{16,24},{24,16},{1,9},{9,1},{17,25},{25,17},{2,10},{10... | collective-permute-start | bytes 221192 | tf_op jit(solution)/shard_map/ppermute | solution.py:45
  67.7 3.4 %collective-permute-start.19 = (bf16[144,256]{1,0:T(8,128)(2,1)S(1)}, bf16[144,256]{1,0:T(8,128)(2,1)S(1)}, u32[]{:S(2)}, u32[]{:S(2)}) collective-permute-start(bf16[144,256]{1,0:T(8,128)(2,1)S(1)} %added.7.refs_2_), channel_id=1, source_target_pairs={{0,8},{8,0},{16,24},{24,16},{1,9},{9,1},{17,25},{25,17},{2,10},{10... | collective-permute-start | bytes 221192 | tf_op jit(solution)/shard_map/ppermute | solution.py:45
  68.5 2.6 %collective-permute-start.18 = (bf16[144,256]{1,0:T(8,128)(2,1)S(1)}, bf16[144,256]{1,0:T(8,128)(2,1)S(1)}, u32[]{:S(2)}, u32[]{:S(2)}) collective-permute-start(bf16[144,256]{1,0:T(8,128)(2,1)S(1)} %collective-permute-done.12.refs_1_), channel_id=1, source_target_pairs={{0,8},{8,0},{16,24},{24,16},{1,9},{9,1},{17,25},{25,17},{2,10},{10... | collective-permute-start | bytes 221192 | tf_op jit(solution)/shard_map/ppermute | solution.py:45
  71.1 1.3 %collective-permute-start.20 = (bf16[144,256]{1,0:T(8,128)(2,1)S(1)}, bf16[144,256]{1,0:T(8,128)(2,1)S(1)}, u32[]{:S(2)}, u32[]{:S(2)}) collective-permute-start(bf16[144,256]{1,0:T(8,128)(2,1)S(1)} %collective-permute-done.16.refs_3_), channel_id=1, source_target_pairs={{0,8},{8,0},{16,24},{24,16},{1,9},{9,1},{17,25},{25,17},{2,10},{10... | collective-permute-start | bytes 221192 | tf_op jit(solution)/shard_map/ppermute | solution.py:45

commit v13 on v11

--- a/solution.py
+++ b/solution.py
@@ -83,7 +83,7 @@
     project_rows(copies, held, near, outs)
 
 
-def project(spectra, weight, chan, bits):
+def project(spectra, weight, chan, bits, grant):
     depth, width = weight.shape
     rows = spectra.shape[0] // 4
     hbm = pl.BlockSpec(memory_space=pltpu.HBM)
@@ -97,7 +97,7 @@
             pltpu.VMEM((depth, width), jnp.bfloat16),
             pltpu.SemaphoreType.DMA((2 * len(bits) + 1,)),
         ],
-        compiler_params=memory(LARGE),
+        compiler_params=memory(grant),
         cost_estimate=pl.CostEstimate(
             flops=2 * len(bits) * rows * depth * width,
             bytes_accessed=2 * len(bits) * rows * (depth + width) + 2 * depth * width,
@@ -416,7 +416,7 @@
     chan = lax.axis_index("chan")
     first_row = chan * quarter
 
-    near_first = swap(project(spectra, enc_weight, chan, (3,))[0], "chan", 1)
+    near_first = swap(project(spectra, enc_weight, chan, (2,), LARGE + 4)[0], "chan", 1)
     places = (adjoint - (tile * tile_rows - HALO)) * 2
     places = (places[: NEIGH // 2] | (places[NEIGH // 2 :] << 16)).reshape(-1)
 
@@ -432,13 +432,13 @@
         local_ids = lax.dynamic_slice_in_dim(pix_local, first_row, quarter, 0)
         slot_index, wanted = requests(tile_ids, local_ids, capacity)
         start, count = 0 * chan, wanted.shape[0]
-    rows, shared, send = pixel_rows(*pixels, wanted, start, count, *rest, chan, (2, 1))
+    rows, shared, send = pixel_rows(*pixels, wanted, start, count, *rest, chan, (3, 1))
     near_first, rows = lax.optimization_barrier((near_first, rows))
     passed_on = (shared.astype(jnp.float32) + near_first.astype(jnp.float32)).astype(jnp.bfloat16)
     passed_on, send, rows, later = lax.optimization_barrier((passed_on, send, rows, chan))
-    far = swap(passed_on, "chan", 2)
+    far = swap(passed_on, "chan", 3)
     near = swap(send, "chan", 1)
-    (keep,) = project(*rest, later, (0,))
+    (keep,) = project(*rest, later, (0,), LARGE)
     if paired:
         answers = swap(rows, "pix", 1)
         (mine,) = pixel_rows(*pixels, pix_local, later * quarter, count, *rest, later, ())

time: 69.9 us -> 68.2 us (0.976)
  starting transfers between devices: 23 us -> 18.6 us
  waiting for transfers between devices: 18.9 us -> 22 us
  local copies, waits for them, and re-layouts: 1.09 us -> 0.04 us
  Pallas kernels: 25.2 us -> 25.9 us
    ppermute x12, starting transfers between devices: 17.6 us -> 13.2 us  [swap(): return lax.ppermute(value, axis, [(i, i ^ bit) for i in range(size)])]
    ppermute x12, waiting for transfers between devices: 12.3 us -> 15.4 us  [swap(): return lax.ppermute(value, axis, [(i, i ^ bit) for i in range(size)])]
    unnamed x15 -> x13, local copies, waits for them, and re-layouts: 1.09 us -> 0.04 us
    pallas_call x2, Pallas kernels: 4.45 us -> 5.2 us  [project(): pl.pallas_call(functools.partial(project_kernel, bits), out_shape=(jax.Sh...]
  transfers between devices with their start and end apart: 17 -> 17, of which waited for: 8 -> 9; matrix products, arithmetic and copies ran while one was open for 2% -> 2% of each run, Pallas kernels for 32% -> 34%
where the time goes in v13:
time: 68.2 us; the launch traced here: 68 us
  Pallas kernels  25.9 us (38%)
  waiting for transfers between devices  22 us (32%)
  starting transfers between devices  18.6 us (27%)
  other arithmetic  1.21 us (2%)
    ppermute x12, waiting for transfers between devices, swap(): return lax.ppermute(value, axis, [(i, i ^ bit) for i in range(size)])  15.4 us
    pallas_call x2, Pallas kernels, pixel_rows(): pl.pallas_call(functools.partial(pixel_kernel, count, bits), out_shape=(j...  14.3 us
    ppermute x12, starting transfers between devices, swap(): return lax.ppermute(value, axis, [(i, i ^ bit) for i in range(size)])  13.2 us
    ppermute x4, waiting for transfers between devices, sum_over_panels(): parts = [added(part, lax.ppermute(part, both, perm)) for part in parts]  6.56 us
    ppermute x4, starting transfers between devices, sum_over_panels(): parts = [added(part, lax.ppermute(part, both, perm)) for part in parts]  5.29 us
    pallas_call x2, Pallas kernels, project(): pl.pallas_call(functools.partial(project_kernel, bits), out_shape=(jax.Sh...  5.2 us
    pallas_call x1, Pallas kernels, early_product(): pl.pallas_call(early_kernel, out_shape=(jax.ShapeDtypeStruct((depth, widt...  3.53 us
  transfers between devices with their start and end apart: 17, of which 9 were waited for; matrix products, arithmetic and copies ran while one was open for 2% of the time, Pallas kernels for 34%

profile of v13, /device:TPU:0, one launch (start us, length us, event | category | flops | bytes accessed | tf_op | source)
XLA Modules:
  0.0 68.0 jit_solution(5324199585321214231)
XLA Ops:
  0.0 3.0 %collective-permute-start = (s32[2048]{0:T(1024)}, s32[2048]{0:T(1024)S(1)}, u32[]{:S(2)}, u32[]{:S(2)}) collective-permute-start(s32[2048]{0:T(1024)} %wanted.1), channel_id=1, source_target_pairs={{0,4},{4,0},{1,5},{5,1},{2,6},{6,2},{3,7},{7,3},{8,12},{12,8},{9,1... | collective-permute-start | bytes 24584 | tf_op jit(solution)/shard_map/ppermute | solution.py:45
  3.0 0.9 %slice_select_fusion = bf16[128,256]{1,0:T(8,128)(2,1)S(1)} fusion(bf16[4096,256]{1,0:T(8,128)(2,1)} %cotangent.3, pred[]{:T(512)S(6)} %eq.3), kind=kLoop, calls=%fused_computation.5 | loop fusion | flops 32768 | bytes 196609 | tf_op jit(solution)/shard_map/jit(_where)/select_n | solution.py:22
  4.0 3.0 %project.2 = bf16[512,256]{1,0:T(8,128)(2,1)} custom-call(s32[1]{0:T(128)} %bitcast.1.chan, bf16[2048,1152]{1,0:T(8,128)(2,1)} %spectra.9, bf16[1152,256]{1,0:T(8,128)(2,1)} %weight.7), custom_call_target="tpu_custom_call" | custom-call | flops 301989888 | bytes 2031616 | tf_op jit(solution)/shard_map/project/pallas_call | solution.py:90
  7.0 2.1 %collective-permute-start.2 = (bf16[512,256]{1,0:T(8,128)(2,1)}, bf16[512,256]{1,0:T(8,128)(2,1)S(1)}, u32[]{:S(2)}, u32[]{:S(2)}) collective-permute-start(bf16[512,256]{1,0:T(8,128)(2,1)} %project.2), channel_id=1, source_target_pairs={{0,1},{1,0},{2,3},{3,2},{4,5},{5,4},{6,7},{7,6},{8,9},{9,8},{10,11... | collective-permute-start | bytes 786440 | tf_op jit(solution)/shard_map/ppermute | solution.py:45
  9.2 0.1 pad_add_fusion.where
  9.3 8.2 %pixel_rows.2 = (bf16[512,256]{1,0:T(8,128)(2,1)S(1)}, bf16[512,256]{1,0:T(8,128)(2,1)S(1)}, bf16[512,256]{1,0:T(8,128)(2,1)S(1)}) custom-call(s32[2]{0:T(128)S(1)} %pad_add_fusion.1.where, s32[16384]{0:T(1024)S(1)} %bitcast.11, s32[2048]{0:T(1024)S(1)} %collective-permute-done.wanted, bf16[4096,256]{1,0:T(8,128)(2,1)} %cotangent.3, ...), custom_call_target="tpu_custom_call" | custom-call | flops 17179869184 | bytes 4194304 | tf_op jit(solution)/shard_map/pixel_rows/pallas_call | solution.py:277
  17.6 0.5 collective-permute-start.3
  18.1 3.6 %collective-permute-start.4 = (bf16[512,256]{1,0:T(8,128)(2,1)S(1)}, bf16[512,256]{1,0:T(8,128)(2,1)S(1)}, u32[]{:S(2)}, u32[]{:S(2)}) collective-permute-start(bf16[512,256]{1,0:T(8,128)(2,1)S(1)} %add_convert_fusion), channel_id=1, source_target_pairs={{0,3},{1,2},{2,1},{3,0},{4,7},{5,6},{6,5},{7,4},{8,11},{9,10},{10,... | collective-permute-start | bytes 786440 | tf_op jit(solution)/shard_map/ppermute | solution.py:45
  21.7 1.5 %collective-permute-start.5 = (bf16[512,256]{1,0:T(8,128)(2,1)S(1)}, bf16[512,256]{1,0:T(8,128)(2,1)S(1)}, u32[]{:S(2)}, u32[]{:S(2)}) collective-permute-start(bf16[512,256]{1,0:T(8,128)(2,1)S(1)} %get-tuple-element.28), channel_id=1, source_target_pairs={{0,4},{4,0},{1,5},{5,1},{2,6},{6,2},{3,7},{7,3},{8,12},{12,8},{9,1... | collective-permute-start | bytes 786440 | tf_op jit(solution)/shard_map/ppermute | solution.py:45
  23.3 6.1 %pixel_rows.3.mine = bf16[512,256]{1,0:T(8,128)(2,1)S(1)} custom-call(s32[2]{0:T(128)S(1)} %pad_add_fusion.2.where, s32[16384]{0:T(1024)S(1)} %bitcast.12, s32[2048]{0:T(1024)S(1)} %copy-done.3, bf16[4096,256]{1,0:T(8,128)(2,1)} %cotangent.3, bf16[128,256]{1,0:T(8,128)(2,1)S(1)} %collective-permute-done.1.above.below, ...), custom_call_target="tpu_custom_call" | custom-call | flops 17179869184 | bytes 4194304 | tf_op jit(solution)/shard_map/pixel_rows/pallas_call | solution.py:277
  29.5 2.2 %project.3.keep = bf16[512,256]{1,0:T(8,128)(2,1)S(1)} custom-call(s32[1]{0:T(128)} %bitcast.4.chan, bf16[2048,1152]{1,0:T(8,128)(2,1)} %spectra.9, bf16[1152,256]{1,0:T(8,128)(2,1)S(1)} %copy-done), custom_call_target="tpu_custom_call" | custom-call | flops 301989888 | bytes 2031616 | tf_op jit(solution)/shard_map/project/pallas_call | solution.py:90
  31.7 0.9 %collective-permute-done.4.far = bf16[512,256]{1,0:T(8,128)(2,1)S(1)} collective-permute-done((bf16[512,256]{1,0:T(8,128)(2,1)S(1)}, bf16[512,256]{1,0:T(8,128)(2,1)S(1)}, u32[]{:S(2)}, u32[]{:S(2)}) %collective-permute-start.4) | collective-permute-done | bytes 262176 | tf_op jit(solution)/shard_map/ppermute | solution.py:45
  32.5 1.0 %pre_gradient.1.first = bf16[512,256]{1,0:T(8,128)(2,1)S(1)} custom-call(s32[2]{0:T(128)S(1)} %pad_add_fusion.where, bf16[512,256]{1,0:T(8,128)(2,1)S(1)} %project.3.keep, bf16[512,256]{1,0:T(8,128)(2,1)S(1)} %collective-permute-done.3.near, bf16[512,256]{1,0:T(8,128)(2,1)S(1)} %collective-permute-done.4.far, s32[16,128]{1,0:T(8,128)S(1)} %bitcast.13, ...), custom_call_target="tpu_custom_call" | custom-call | tf_op jit(solution)/shard_map/pre_gradient/pallas_call | solution.py:352
  33.6 0.5 collective-permute-start.7
  34.1 1.0 %collective-permute-start.6 = (bf16[512,256]{1,0:T(8,128)(2,1)S(1)}, bf16[512,256]{1,0:T(8,128)(2,1)S(1)}, u32[]{:S(2)}, u32[]{:S(2)}) collective-permute-start(bf16[512,256]{1,0:T(8,128)(2,1)S(1)} %pre_gradient.1.first), channel_id=1, source_target_pairs={{0,1},{1,0},{2,3},{3,2},{4,5},{5,4},{6,7},{7,6},{8,9},{9,8},{10,11... | collective-permute-start | bytes 786440 | tf_op jit(solution)/shard_map/ppermute | solution.py:45
  35.1 9.5 %collective-permute-done.7.third = bf16[512,256]{1,0:T(8,128)(2,1)S(1)} collective-permute-done((bf16[512,256]{1,0:T(8,128)(2,1)S(1)}, bf16[512,256]{1,0:T(8,128)(2,1)S(1)}, u32[]{:S(2)}, u32[]{:S(2)}) %collective-permute-start.7) | collective-permute-done | bytes 262176 | tf_op jit(solution)/shard_map/ppermute | solution.py:45
  44.7 0.2 collective-permute-start.8
  44.9 2.6 %collective-permute-done.6.second = bf16[512,256]{1,0:T(8,128)(2,1)S(1)} collective-permute-done((bf16[512,256]{1,0:T(8,128)(2,1)S(1)}, bf16[512,256]{1,0:T(8,128)(2,1)S(1)}, u32[]{:S(2)}, u32[]{:S(2)}) %collective-permute-start.6) | collective-permute-done | bytes 262176 | tf_op jit(solution)/shard_map/ppermute | solution.py:45
  47.6 3.5 %early_product.1 = (f32[1152,256]{1,0:T(8,128)S(1)}, bf16[512,1152]{1,0:T(8,128)(2,1)S(1)}) custom-call(s32[1]{0:T(128)} %bitcast.1.chan, bf16[2048,1152]{1,0:T(8,128)(2,1)} %spectra.9, bf16[512,256]{1,0:T(8,128)(2,1)S(1)} %pre_gradient.1.first, bf16[512,256]{1,0:T(8,128)(2,1)S(1)} %collective-permute-done.6.second, ...), custom_call_target="tpu_custom_call" | custom-call | flops 905969664 | bytes 5898240 | tf_op jit(solution)/shard_map/early_product/pallas_call | solution.py:138
  51.1 0.1 collective-permute-done.8.rows
  51.2 0.6 late_product.1
  51.9 0.5 collective-permute-start.12
  52.4 0.9 %collective-permute-done.9.second = bf16[288,256]{1,0:T(8,128)(2,1)S(1)} collective-permute-done((bf16[288,256]{1,0:T(8,128)(2,1)S(1)}, bf16[288,256]{1,0:T(8,128)(2,1)S(1)}, u32[]{:S(2)}, u32[]{:S(2)}) %collective-permute-start.9) | collective-permute-done | bytes 147488 | tf_op jit(solution)/shard_map/ppermute | solution.py:45
  53.3 1.6 %collective-permute-start.10 = (bf16[288,256]{1,0:T(8,128)(2,1)S(1)}, bf16[288,256]{1,0:T(8,128)(2,1)S(1)}, u32[]{:S(2)}, u32[]{:S(2)}) collective-permute-start(bf16[288,256]{1,0:T(8,128)(2,1)S(1)} %added.6.first), channel_id=1, source_target_pairs={{0,16},{4,20},{8,12},{12,8},{16,0},{20,4},{24,28},{28,24},{1,17},{... | collective-permute-start | bytes 442376 | tf_op jit(solution)/shard_map/ppermute | solution.py:407
  54.9 0.6 collective-permute-start.13
  55.5 3.0 %collective-permute-done.10.second = bf16[288,256]{1,0:T(8,128)(2,1)S(1)} collective-permute-done((bf16[288,256]{1,0:T(8,128)(2,1)S(1)}, bf16[288,256]{1,0:T(8,128)(2,1)S(1)}, u32[]{:S(2)}, u32[]{:S(2)}) %collective-permute-start.10) | collective-permute-done | bytes 147488 | tf_op jit(solution)/shard_map/ppermute | solution.py:407
  58.5 1.6 %collective-permute-start.11 = (bf16[288,256]{1,0:T(8,128)(2,1)S(1)}, bf16[288,256]{1,0:T(8,128)(2,1)S(1)}, u32[]{:S(2)}, u32[]{:S(2)}) collective-permute-start(bf16[288,256]{1,0:T(8,128)(2,1)S(1)} %added.7.first), channel_id=1, source_target_pairs={{0,4},{4,0},{8,24},{12,28},{16,20},{20,16},{24,8},{28,12},{1,5},{5... | collective-permute-start | bytes 442376 | tf_op jit(solution)/shard_map/ppermute | solution.py:407
  60.2 1.5 %collective-permute-start.14 = (bf16[288,256]{1,0:T(8,128)(2,1)S(1)}, bf16[288,256]{1,0:T(8,128)(2,1)S(1)}, u32[]{:S(2)}, u32[]{:S(2)}) collective-permute-start(bf16[288,256]{1,0:T(8,128)(2,1)S(1)} %added.10.first), channel_id=1, source_target_pairs={{0,4},{4,0},{8,24},{12,28},{16,20},{20,16},{24,8},{28,12},{1,5},{5... | collective-permute-start | bytes 442376 | tf_op jit(solution)/shard_map/ppermute | solution.py:407
  61.7 2.0 %collective-permute-done.11.second = bf16[288,256]{1,0:T(8,128)(2,1)S(1)} collective-permute-done((bf16[288,256]{1,0:T(8,128)(2,1)S(1)}, bf16[288,256]{1,0:T(8,128)(2,1)S(1)}, u32[]{:S(2)}, u32[]{:S(2)}) %collective-permute-start.11) | collective-permute-done | bytes 147488 | tf_op jit(solution)/shard_map/ppermute | solution.py:407
  63.9 1.5 %collective-permute-done.14.second = bf16[288,256]{1,0:T(8,128)(2,1)S(1)} collective-permute-done((bf16[288,256]{1,0:T(8,128)(2,1)S(1)}, bf16[288,256]{1,0:T(8,128)(2,1)S(1)}, u32[]{:S(2)}, u32[]{:S(2)}) %collective-permute-start.14) | collective-permute-done | bytes 147488 | tf_op jit(solution)/shard_map/ppermute | solution.py:407
  65.5 1.3 %collective-permute-done.16.refs_3_ = bf16[288,256]{1,0:T(8,128)(2,1)S(1)} collective-permute-done((bf16[288,256]{1,0:T(8,128)(2,1)S(1)}, bf16[288,256]{1,0:T(8,128)(2,1)S(1)}, u32[]{:S(2)}, u32[]{:S(2)}) %collective-permute-start.16) | collective-permute-done | bytes 147488 | tf_op jit(solution)/shard_map/ppermute | solution.py:45
  66.9 1.1 %collect.1 = f32[1152,256]{1,0:T(8,128)} custom-call(s32[1]{0:T(128)} %bitcast.core, bf16[288,256]{1,0:T(8,128)(2,1)S(1)} %added.8.refs_0_, bf16[288,256]{1,0:T(8,128)(2,1)S(1)} %added.11.refs_1_, bf16[288,256]{1,0:T(8,128)(2,1)S(1)} %collective-permute-done.15.refs_2_, bf16[288,256]{1,0:T(8,128)(2,1)S(1)} %collective-permute-done.16.refs_3_), custom_call_target="tpu_custom_call" | custom-call | tf_op jit(solution)/shard_map/collect/pallas_call | solution.py:376
  (36 shorter events, 0.8 us)
Async XLA Ops:
  0.0 9.3 %collective-permute-start = (s32[2048]{0:T(1024)}, s32[2048]{0:T(1024)S(1)}, u32[]{:S(2)}, u32[]{:S(2)}) collective-permute-start(s32[2048]{0:T(1024)} %wanted.1), channel_id=1, source_target_pairs={{0,4},{4,0},{1,5},{5,1},{2,6},{6,2},{3,7},{7,3},{8,12},{12,8},{9,1... | collective-permute-start | bytes 24584 | tf_op jit(solution)/shard_map/ppermute | solution.py:45
  3.9 5.5 %collective-permute-start.1 = (bf16[128,256]{1,0:T(8,128)(2,1)S(1)}, bf16[128,256]{1,0:T(8,128)(2,1)S(1)}, u32[]{:S(2)}, u32[]{:S(2)}) collective-permute-start(bf16[128,256]{1,0:T(8,128)(2,1)S(1)} %slice_select_fusion), channel_id=1, source_target_pairs={{0,4},{4,0},{1,5},{5,1},{2,6},{6,2},{3,7},{7,3},{8,12},{12,8},{9,1... | collective-permute-start | bytes 196616 | tf_op jit(solution)/shard_map/ppermute | solution.py:22
  3.9 5.2 %copy-start.5 = (s32[8,4096]{1,0:T(8,128)S(1)}, s32[8,4096]{1,0:T(8,128)}, u32[]{:S(2)}) copy-start(s32[8,4096]{1,0:T(8,128)} %param.14) | copy-start | bytes 393220
  3.9 5.4 %copy-start = (bf16[1152,256]{1,0:T(8,128)(2,1)S(1)}, bf16[1152,256]{1,0:T(8,128)(2,1)}, u32[]{:S(2)}) copy-start(bf16[1152,256]{1,0:T(8,128)(2,1)} %weight.7) | copy-start | bytes 1769476
  4.0 5.4 %copy-start.4 = (f32[8,256]{1,0:T(8,128)S(1)}, f32[8,256]{1,0:T(8,128)}, u32[]{:S(2)}) copy-start(f32[8,256]{1,0:T(8,128)} %mixing.3) | copy-start | bytes 24580
  7.0 10.5 %collective-permute-start.2 = (bf16[512,256]{1,0:T(8,128)(2,1)}, bf16[512,256]{1,0:T(8,128)(2,1)S(1)}, u32[]{:S(2)}, u32[]{:S(2)}) collective-permute-start(bf16[512,256]{1,0:T(8,128)(2,1)} %project.2), channel_id=1, source_target_pairs={{0,1},{1,0},{2,3},{3,2},{4,5},{5,4},{6,7},{7,6},{8,9},{9,8},{10,11... | collective-permute-start | bytes 786440 | tf_op jit(solution)/shard_map/ppermute | solution.py:45
  9.3 14.0 %copy-start.3 = (s32[2048]{0:T(1024)S(1)}, s32[2048]{0:T(1024)}, u32[]{:S(2)}) copy-start(s32[2048]{0:T(1024)} %wanted.1) | copy-start | bytes 24580
  17.6 14.0 %collective-permute-start.3 = (bf16[512,256]{1,0:T(8,128)(2,1)S(1)}, bf16[512,256]{1,0:T(8,128)(2,1)S(1)}, u32[]{:S(2)}, u32[]{:S(2)}) collective-permute-start(bf16[512,256]{1,0:T(8,128)(2,1)S(1)} %get-tuple-element.26), channel_id=1, source_target_pairs={{0,1},{1,0},{2,3},{3,2},{4,5},{5,4},{6,7},{7,6},{8,9},{9,8},{10,11... | collective-permute-start | bytes 786440 | tf_op jit(solution)/shard_map/ppermute | solution.py:45
  18.1 14.4 %collective-permute-start.4 = (bf16[512,256]{1,0:T(8,128)(2,1)S(1)}, bf16[512,256]{1,0:T(8,128)(2,1)S(1)}, u32[]{:S(2)}, u32[]{:S(2)}) collective-permute-start(bf16[512,256]{1,0:T(8,128)(2,1)S(1)} %add_convert_fusion), channel_id=1, source_target_pairs={{0,3},{1,2},{2,1},{3,0},{4,7},{5,6},{6,5},{7,4},{8,11},{9,10},{10,... | collective-permute-start | bytes 786440 | tf_op jit(solution)/shard_map/ppermute | solution.py:45
  21.7 10.8 %collective-permute-start.5 = (bf16[512,256]{1,0:T(8,128)(2,1)S(1)}, bf16[512,256]{1,0:T(8,128)(2,1)S(1)}, u32[]{:S(2)}, u32[]{:S(2)}) collective-permute-start(bf16[512,256]{1,0:T(8,128)(2,1)S(1)} %get-tuple-element.28), channel_id=1, source_target_pairs={{0,4},{4,0},{1,5},{5,1},{2,6},{6,2},{3,7},{7,3},{8,12},{12,8},{9,1... | collective-permute-start | bytes 786440 | tf_op jit(solution)/shard_map/ppermute | solution.py:45
  29.4 3.1 %copy-start.1 = (s32[2048,1]{0,1:T(1,128)S(1)}, s32[2048,1]{0,1:T(1,128)}, u32[]{:S(2)}) copy-start(s32[2048,1]{0,1:T(1,128)} %param.10) | copy-start | bytes 24580
  29.5 3.1 %copy-start.2 = (f32[2048]{0:T(1024)S(1)}, f32[2048]{0:T(1024)}, u32[]{:S(2)}) copy-start(f32[2048]{0:T(1024)} %param.12) | copy-start | bytes 24580
  33.6 11.1 %collective-permute-start.7 = (bf16[512,256]{1,0:T(8,128)(2,1)S(1)}, bf16[512,256]{1,0:T(8,128)(2,1)S(1)}, u32[]{:S(2)}, u32[]{:S(2)}) collective-permute-start(bf16[512,256]{1,0:T(8,128)(2,1)S(1)} %pre_gradient.1.first), channel_id=1, source_target_pairs={{0,3},{1,2},{2,1},{3,0},{4,7},{5,6},{6,5},{7,4},{8,11},{9,10},{10,... | collective-permute-start | bytes 786440 | tf_op jit(solution)/shard_map/ppermute | solution.py:45
  34.1 13.4 %collective-permute-start.6 = (bf16[512,256]{1,0:T(8,128)(2,1)S(1)}, bf16[512,256]{1,0:T(8,128)(2,1)S(1)}, u32[]{:S(2)}, u32[]{:S(2)}) collective-permute-start(bf16[512,256]{1,0:T(8,128)(2,1)S(1)} %pre_gradient.1.first), channel_id=1, source_target_pairs={{0,1},{1,0},{2,3},{3,2},{4,5},{5,4},{6,7},{7,6},{8,9},{9,8},{10,11... | collective-permute-start | bytes 786440 | tf_op jit(solution)/shard_map/ppermute | solution.py:45
  44.7 6.5 %collective-permute-start.8 = (bf16[512,256]{1,0:T(8,128)(2,1)S(1)}, bf16[512,256]{1,0:T(8,128)(2,1)S(1)}, u32[]{:S(2)}, u32[]{:S(2)}) collective-permute-start(bf16[512,256]{1,0:T(8,128)(2,1)S(1)} %collective-permute-done.7.third), channel_id=1, source_target_pairs={{0,1},{1,0},{2,3},{3,2},{4,5},{5,4},{6,7},{7,6},{8,9},{9,8},{10,11... | collective-permute-start | bytes 786440 | tf_op jit(solution)/shard_map/ppermute | solution.py:45
  51.8 1.4 %collective-permute-start.9 = (bf16[288,256]{1,0:T(8,128)(2,1)S(1)}, bf16[288,256]{1,0:T(8,128)(2,1)S(1)}, u32[]{:S(2)}, u32[]{:S(2)}) collective-permute-start(bf16[288,256]{1,0:T(8,128)(2,1)S(1)} %get-tuple-element.32), channel_id=1, source_target_pairs={{0,8},{8,0},{16,24},{24,16},{1,9},{9,1},{17,25},{25,17},{2,10},{10... | collective-permute-start | bytes 442376 | tf_op jit(solution)/shard_map/ppermute | solution.py:45
  51.9 2.9 %collective-permute-start.12 = (bf16[288,256]{1,0:T(8,128)(2,1)S(1)}, bf16[288,256]{1,0:T(8,128)(2,1)S(1)}, u32[]{:S(2)}, u32[]{:S(2)}) collective-permute-start(bf16[288,256]{1,0:T(8,128)(2,1)S(1)} %get-tuple-element.34), channel_id=1, source_target_pairs={{0,8},{8,0},{16,24},{24,16},{1,9},{9,1},{17,25},{25,17},{2,10},{10... | collective-permute-start | bytes 442376 | tf_op jit(solution)/shard_map/ppermute | solution.py:45
  53.3 5.2 %collective-permute-start.10 = (bf16[288,256]{1,0:T(8,128)(2,1)S(1)}, bf16[288,256]{1,0:T(8,128)(2,1)S(1)}, u32[]{:S(2)}, u32[]{:S(2)}) collective-permute-start(bf16[288,256]{1,0:T(8,128)(2,1)S(1)} %added.6.first), channel_id=1, source_target_pairs={{0,16},{4,20},{8,12},{12,8},{16,0},{20,4},{24,28},{28,24},{1,17},{... | collective-permute-start | bytes 442376 | tf_op jit(solution)/shard_map/ppermute | solution.py:407
  54.9 5.2 %collective-permute-start.13 = (bf16[288,256]{1,0:T(8,128)(2,1)S(1)}, bf16[288,256]{1,0:T(8,128)(2,1)S(1)}, u32[]{:S(2)}, u32[]{:S(2)}) collective-permute-start(bf16[288,256]{1,0:T(8,128)(2,1)S(1)} %added.9.first), channel_id=1, source_target_pairs={{0,16},{4,20},{8,12},{12,8},{16,0},{20,4},{24,28},{28,24},{1,17},{... | collective-permute-start | bytes 442376 | tf_op jit(solution)/shard_map/ppermute | solution.py:407
  58.5 5.2 %collective-permute-start.11 = (bf16[288,256]{1,0:T(8,128)(2,1)S(1)}, bf16[288,256]{1,0:T(8,128)(2,1)S(1)}, u32[]{:S(2)}, u32[]{:S(2)}) collective-permute-start(bf16[288,256]{1,0:T(8,128)(2,1)S(1)} %added.7.first), channel_id=1, source_target_pairs={{0,4},{4,0},{8,24},{12,28},{16,20},{20,16},{24,8},{28,12},{1,5},{5... | collective-permute-start | bytes 442376 | tf_op jit(solution)/shard_map/ppermute | solution.py:407
  60.2 5.2 %collective-permute-start.14 = (bf16[288,256]{1,0:T(8,128)(2,1)S(1)}, bf16[288,256]{1,0:T(8,128)(2,1)S(1)}, u32[]{:S(2)}, u32[]{:S(2)}) collective-permute-start(bf16[288,256]{1,0:T(8,128)(2,1)S(1)} %added.10.first), channel_id=1, source_target_pairs={{0,4},{4,0},{8,24},{12,28},{16,20},{20,16},{24,8},{28,12},{1,5},{5... | collective-permute-start | bytes 442376 | tf_op jit(solution)/shard_map/ppermute | solution.py:407
  63.8 1.7 %collective-permute-start.15 = (bf16[288,256]{1,0:T(8,128)(2,1)S(1)}, bf16[288,256]{1,0:T(8,128)(2,1)S(1)}, u32[]{:S(2)}, u32[]{:S(2)}) collective-permute-start(bf16[288,256]{1,0:T(8,128)(2,1)S(1)} %added.8.refs_0_), channel_id=1, source_target_pairs={{0,8},{8,0},{16,24},{24,16},{1,9},{9,1},{17,25},{25,17},{2,10},{10... | collective-permute-start | bytes 442376 | tf_op jit(solution)/shard_map/ppermute | solution.py:45
  65.4 1.4 %collective-permute-start.16 = (bf16[288,256]{1,0:T(8,128)(2,1)S(1)}, bf16[288,256]{1,0:T(8,128)(2,1)S(1)}, u32[]{:S(2)}, u32[]{:S(2)}) collective-permute-start(bf16[288,256]{1,0:T(8,128)(2,1)S(1)} %added.11.refs_1_), channel_id=1, source_target_pairs={{0,8},{8,0},{16,24},{24,16},{1,9},{9,1},{17,25},{25,17},{2,10},{10... | collective-permute-start | bytes 442376 | tf_op jit(solution)/shard_map/ppermute | solution.py:45

commit v14 on v13

--- a/solution.py
+++ b/solution.py
@@ -49,38 +49,38 @@
     return pltpu.CompilerParams(vmem_limit_bytes=mib * MIB)
 
 
-def quarter_copies(spectra, weight, held, near, sems, chan, bits):
-    chunk = held.shape[0] // len(bits) // 2
-    copies = [pltpu.make_async_copy(weight, near, sems.at[2 * len(bits)])]
-    for turn in range(2 * len(bits)):
-        first = ((chan ^ bits[turn // 2]) * 2 + turn % 2) * chunk
-        copies.append(
-            pltpu.make_async_copy(
-                spectra.at[pl.ds(pl.multiple_of(first, chunk), chunk)],
-                held.at[pl.ds(turn * chunk, chunk)],
-                sems.at[turn],
-            )
+def quarter_copies(spectra, held, sems, chan, bits):
+    rows = spectra.shape[0] // 4
+    return [
+        pltpu.make_async_copy(
+            spectra.at[pl.ds(pl.multiple_of((chan ^ bit) * rows, rows), rows)],
+            held.at[pl.ds(turn * rows, rows)],
+            sems.at[turn],
         )
-    return copies
-
-
-def project_rows(copies, held, near, outs):
-    chunk = outs[0].shape[0] // 2
-    copies[0].wait()
-    for turn in range(2 * len(outs)):
-        copies[turn + 1].wait()
-        rows = held[turn * chunk : (turn + 1) * chunk, :]
-        result = jnp.dot(rows, near[...], preferred_element_type=jnp.float32)
-        first = turn % 2 * chunk
-        outs[turn // 2][first : first + chunk, :] = result.astype(outs[0].dtype)
+        for turn, bit in enumerate(bits)
+    ]
+
+
+def project_rows(copies, held, weight, outs):
+    rows = outs[0].shape[0] if outs else 0
+    for turn, (copy, out) in enumerate(zip(copies, outs)):
+        copy.wait()
+        result = jnp.dot(
+            held[turn * rows : (turn + 1) * rows, :],
+            weight[...],
+            preferred_element_type=jnp.float32,
+        )
+        out[...] = result.astype(out.dtype)
 
 
 def project_kernel(bits, chan, spectra, weight, *refs):
     *outs, held, near, sems = refs
-    copies = quarter_copies(spectra, weight, held, near, sems, chan[0], bits)
+    copies = [pltpu.make_async_copy(weight, near, sems.at[len(bits)])]
+    copies += quarter_copies(spectra, held, sems, chan[0], bits)
     for copy in copies:
         copy.start()
-    project_rows(copies, held, near, outs)
+    copies[0].wait()
+    project_rows(copies[1:], held, near, outs)
 
 
 def project(spectra, weight, chan, bits, grant):
@@ -95,7 +95,7 @@
         scratch_shapes=[
             pltpu.VMEM((len(bits) * rows, depth), jnp.bfloat16),
             pltpu.VMEM((depth, width), jnp.bfloat16),
-            pltpu.SemaphoreType.DMA((2 * len(bits) + 1,)),
+            pltpu.SemaphoreType.DMA((len(bits) + 1,)),
         ],
         compiler_params=memory(grant),
         cost_estimate=pl.CostEstimate(
@@ -113,25 +113,24 @@
     )
 
 
-def early_kernel(chan, spectra, first, second, third, total, late, held, sems):
+def early_kernel(chan, spectra, first, second, total, third, fourth, held, sems):
     rows = first.shape[0]
+    targets = (held.at[pl.ds(0, rows)], held.at[pl.ds(rows, rows)], third, fourth)
     copies = []
-    for turn, bits in enumerate((0, 1, 3, 2)):
+    for turn, (bits, target) in enumerate(zip((0, 3, 1, 2), targets)):
         start = pl.multiple_of((chan[0] ^ bits) * rows, rows)
-        target = held.at[pl.ds(turn * rows, rows)] if turn < 3 else late
         copies.append(pltpu.make_async_copy(spectra.at[pl.ds(start, rows)], target, sems.at[turn]))
     for copy in copies:
         copy.start()
     copies[0].wait()
     product = turned_product(held[:rows, :], first[...])
     copies[1].wait()
-    product += turned_product(held[rows : 2 * rows, :], second[...])
+    total[...] = product + turned_product(held[rows:, :], second[...])
     copies[2].wait()
-    total[...] = product + turned_product(held[2 * rows :, :], third[...])
     copies[3].wait()
 
 
-def early_product(spectra, chan, first, second, third):
+def early_product(spectra, chan, first, second):
     depth = spectra.shape[1]
     rows, width = first.shape
     vmem = pl.BlockSpec(memory_space=pltpu.VMEM)
@@ -140,25 +139,48 @@
         out_shape=(
             jax.ShapeDtypeStruct((depth, width), jnp.float32),
             jax.ShapeDtypeStruct((rows, depth), jnp.bfloat16),
+            jax.ShapeDtypeStruct((rows, depth), jnp.bfloat16),
         ),
         in_specs=[
             pl.BlockSpec(memory_space=pltpu.SMEM),
             pl.BlockSpec(memory_space=pltpu.HBM),
-            *[vmem] * 3,
+            vmem,
+            vmem,
         ],
-        out_specs=(vmem, vmem),
+        out_specs=(vmem,) * 3,
         scratch_shapes=[
-            pltpu.VMEM((3 * rows, depth), jnp.bfloat16),
+            pltpu.VMEM((2 * rows, depth), jnp.bfloat16),
             pltpu.SemaphoreType.DMA((4,)),
         ],
         compiler_params=memory(48),
         cost_estimate=pl.CostEstimate(
-            flops=6 * rows * depth * width,
+            flops=4 * rows * depth * width,
             bytes_accessed=8 * rows * depth + 4 * depth * width,
             transcendentals=0,
         ),
         name="early_product",
-    )(chan.reshape(1), spectra, first, second, third)
+    )(chan.reshape(1), spectra, first, second)
+
+
+def more_kernel(held, before, rows, total):
+    total[...] = before[...] + turned_product(held[...], rows[...])
+
+
+def more_product(held, before, rows):
+    vmem = pl.BlockSpec(memory_space=pltpu.VMEM)
+    return pl.pallas_call(
+        more_kernel,
+        out_shape=jax.ShapeDtypeStruct(before.shape, jnp.float32),
+        in_specs=[vmem] * 3,
+        out_specs=vmem,
+        compiler_params=memory(16),
+        cost_estimate=pl.CostEstimate(
+            flops=2 * held.shape[0] * held.shape[1] * rows.shape[1],
+            bytes_accessed=2 * held.shape[0] * held.shape[1] + 8 * before.size,
+            transcendentals=0,
+        ),
+        name="more_product",
+    )(held, before, rows)
 
 
 def late_kernel(core, held, before, rows, *outs):
@@ -193,27 +215,20 @@
     return outs[:2], outs[2:]
 
 
-def pixel_kernel(count, bits, where, places, wanted, cotangent, above, below, mixing, spectra,
-                 weight, out, *refs):
+def pixel_kernel(count, bits, where, places, wanted, cotangent, above, below, mixing, weight,
+                 spectra, out, *refs):
     quarters, refs = refs[: len(bits)], refs[len(bits) :]
-    table, scale, sums, held, near, names, block, factor, sems, more = refs
+    table, scale, sums, near, names, held, sems = refs
     start, chan = where[0], where[1]
-    tile_rows, half = held.shape[0], table.shape[1]
+    tile_rows, half = cotangent.shape[0], table.shape[1]
     listed = names.shape[0]
     first_name = pl.multiple_of(start // listed * listed, listed)
     copies = [
-        pltpu.make_async_copy(places, near, sems.at[4]),
-        pltpu.make_async_copy(wanted.at[pl.ds(first_name, listed)], names, sems.at[5]),
+        pltpu.make_async_copy(places, near, sems.at[len(bits)]),
+        pltpu.make_async_copy(wanted.at[pl.ds(first_name, listed)], names, sems.at[len(bits) + 1]),
     ]
-    chunk = tile_rows // 4
-    rows = [
-        pltpu.make_async_copy(
-            cotangent.at[pl.ds(n * chunk, chunk)], held.at[pl.ds(n * chunk, chunk)], sems.at[n]
-        )
-        for n in range(4)
-    ]
-    parts = quarter_copies(spectra, weight, block, factor, more, chan, bits) if bits else []
-    for copy in copies + rows + parts:
+    parts = quarter_copies(spectra, held, sems, chan, bits)
+    for copy in copies + parts:
         copy.start()
 
     def fill(first, values):
@@ -228,12 +243,9 @@
     scales = [scale[2 * k : 2 * k + 2, :] for k in range(NEIGH)]
     fill(0, above[...])
     fill(HALO + tile_rows, below[...])
-    for n in range(4):
-        rows[n].wait()
-        for first in range(n * chunk, (n + 1) * chunk, 256):
-            fill(HALO + first, held[first : first + 256, :])
-    if bits:
-        project_rows(parts, block, factor, quarters)
+    for first in range(0, tile_rows, 256):
+        fill(HALO + first, cotangent[first : first + 256, :])
+    project_rows(parts, held, weight, quarters)
     for copy in copies:
         copy.wait()
 
@@ -272,7 +284,6 @@
     depth, rows = spectra.shape[1], spectra.shape[0] // 4
     listed = min(wanted.shape[0], 1024)
     anywhere = pl.BlockSpec(memory_space=pl.ANY)
-    hbm = pl.BlockSpec(memory_space=pltpu.HBM)
     vmem = pl.BlockSpec(memory_space=pltpu.VMEM)
     return pl.pallas_call(
         functools.partial(pixel_kernel, count, bits),
@@ -284,25 +295,20 @@
             pl.BlockSpec(memory_space=pltpu.SMEM),
             anywhere,
             anywhere,
-            hbm,
-            *[vmem] * 3,
-            hbm,
-            hbm,
+            *[vmem] * 5,
+            pl.BlockSpec(memory_space=pltpu.HBM),
         ],
         out_specs=(vmem,) * (1 + len(bits)),
         scratch_shapes=[
             pltpu.VMEM((2 * (tile_rows + 2 * HALO), width // 2), jnp.float32),
             pltpu.VMEM((2 * NEIGH, width // 2), jnp.float32),
             pltpu.VMEM((2 * count, width // 2), jnp.float32),
-            pltpu.VMEM(cotangent.shape, cotangent.dtype),
             pltpu.SMEM(places.shape, jnp.int32),
             pltpu.SMEM((listed,), jnp.int32),
             pltpu.VMEM((max(len(bits), 1) * rows, depth), jnp.bfloat16),
-            pltpu.VMEM((depth, width), jnp.bfloat16),
-            pltpu.SemaphoreType.DMA((6,)),
-            pltpu.SemaphoreType.DMA((2 * len(bits) + 1,)),
+            pltpu.SemaphoreType.DMA((len(bits) + 2,)),
         ],
-        compiler_params=memory(LARGE),
+        compiler_params=memory(48),
         cost_estimate=pl.CostEstimate(
             flops=8 * NEIGH * count * 2048 * width,
             bytes_accessed=4 * tile_rows * width,
@@ -310,7 +316,7 @@
         ),
         name="pixel_rows",
     )(
-        jnp.stack([start, chan]), places, wanted, cotangent, above, below, mixing, spectra, weight
+        jnp.stack([start, chan]), places, wanted, cotangent, above, below, mixing, weight, spectra
     )
 
 
@@ -452,9 +458,10 @@
     across = swap(grads, "chan", 3)
     beside = swap(grads, "chan", 1)
     last = swap(across, "chan", 1)
-    early, held = early_product(spectra, chan, grads, beside, across)
+    early, held, held_last = early_product(spectra, chan, grads, across)
+    early = more_product(held, early, beside)
     core = lax.axis_index("obs") & 1
-    send, keep = late_product(core, held, early, last)
+    send, keep = late_product(core, held_last, early, last)
     if lax.axis_size("obs") == 4 and tile_count == 2:
         return sum_over_panels(core, keep, [swap(part, "obs", 1) for part in send])
     return lax.psum(collect(core, keep, send), ("obs", "pix"))

time: 68.2 us -> 68.8 us (level)
  Pallas kernels: 25.9 us -> 24.1 us
  other arithmetic: 1.21 us -> 2.86 us
    convert_element_type x1, other arithmetic: 0.07 us -> 1.72 us  [shards(): (shared.astype(jnp.float32) + near_first.astype(jnp.float32)).astype(jnp....]
    pallas_call x1, Pallas kernels: 3.53 us -> 2.49 us  [early_product(): pl.pallas_call(early_kernel, out_shape=(jax.ShapeDtypeStruct((depth, widt...]
    pallas_call x2, Pallas kernels: 14.3 us -> 13.4 us  [pixel_rows(): pl.pallas_call(functools.partial(pixel_kernel, count, bits), out_shape=(j...]
  transfers between devices with their start and end apart: 17 -> 17, of which waited for: 9 -> 9; matrix products, arithmetic and copies ran while one was open for 2% -> 2% of each run, Pallas kernels for 34% -> 31%
where the time goes in v14:
time: 68.8 us; the launch traced here: 68.5 us
  Pallas kernels  24.1 us (35%)
  waiting for transfers between devices  22.1 us (32%)
  starting transfers between devices  19.2 us (28%)
  other arithmetic  2.86 us (4%)
    ppermute x12, waiting for transfers between devices, swap(): return lax.ppermute(value, axis, [(i, i ^ bit) for i in range(size)])  15.6 us
    ppermute x12, starting transfers between devices, swap(): return lax.ppermute(value, axis, [(i, i ^ bit) for i in range(size)])  13.8 us
    pallas_call x2, Pallas kernels, pixel_rows(): pl.pallas_call(functools.partial(pixel_kernel, count, bits), out_shape=(j...  13.4 us
    ppermute x4, waiting for transfers between devices, sum_over_panels(): parts = [added(part, lax.ppermute(part, both, perm)) for part in parts]  6.55 us
    ppermute x4, starting transfers between devices, sum_over_panels(): parts = [added(part, lax.ppermute(part, both, perm)) for part in parts]  5.3 us
    pallas_call x2, Pallas kernels, project(): pl.pallas_call(functools.partial(project_kernel, bits), out_shape=(jax.Sh...  4.75 us
    pallas_call x1, Pallas kernels, early_product(): pl.pallas_call(early_kernel, out_shape=(jax.ShapeDtypeStruct((depth, widt...  2.49 us
    convert_element_type x1, other arithmetic, shards(): (shared.astype(jnp.float32) + near_first.astype(jnp.float32)).astype(jnp....  1.72 us
  transfers between devices with their start and end apart: 17, of which 9 were waited for; matrix products, arithmetic and copies ran while one was open for 2% of the time, Pallas kernels for 31%

profile of v14, /device:TPU:0, one launch (start us, length us, event | category | flops | bytes accessed | tf_op | source)
XLA Modules:
  0.0 68.5 jit_solution(15962171039817898631)
XLA Ops:
  0.0 3.0 %collective-permute-start = (s32[2048]{0:T(1024)}, s32[2048]{0:T(1024)S(1)}, u32[]{:S(2)}, u32[]{:S(2)}) collective-permute-start(s32[2048]{0:T(1024)} %wanted.1), channel_id=1, source_target_pairs={{0,4},{4,0},{1,5},{5,1},{2,6},{6,2},{3,7},{7,3},{8,12},{12,8},{9,1... | collective-permute-start | bytes 24584 | tf_op jit(solution)/shard_map/ppermute | solution.py:45
  3.0 0.9 %slice_select_fusion = bf16[128,256]{1,0:T(8,128)(2,1)S(1)} fusion(bf16[4096,256]{1,0:T(8,128)(2,1)} %cotangent.3, pred[]{:T(512)S(6)} %eq.3), kind=kLoop, calls=%fused_computation.5 | loop fusion | flops 32768 | bytes 196609 | tf_op jit(solution)/shard_map/jit(_where)/select_n | solution.py:22
  4.0 2.8 %project.2 = bf16[512,256]{1,0:T(8,128)(2,1)} custom-call(s32[1]{0:T(128)} %bitcast.1.chan, bf16[2048,1152]{1,0:T(8,128)(2,1)} %spectra.9, bf16[1152,256]{1,0:T(8,128)(2,1)} %weight.7), custom_call_target="tpu_custom_call" | custom-call | flops 301989888 | bytes 2031616 | tf_op jit(solution)/shard_map/project/pallas_call | solution.py:90
  6.8 2.1 %collective-permute-start.2 = (bf16[512,256]{1,0:T(8,128)(2,1)}, bf16[512,256]{1,0:T(8,128)(2,1)}, u32[]{:S(2)}, u32[]{:S(2)}) collective-permute-start(bf16[512,256]{1,0:T(8,128)(2,1)} %project.2), channel_id=1, source_target_pairs={{0,1},{1,0},{2,3},{3,2},{4,5},{5,4},{6,7},{7,6},{8,9},{9,8},{10,11... | collective-permute-start | bytes 786440 | tf_op jit(solution)/shard_map/ppermute | solution.py:45
  9.2 7.4 %pixel_rows.2 = (bf16[512,256]{1,0:T(8,128)(2,1)S(1)}, bf16[512,256]{1,0:T(8,128)(2,1)S(1)}, bf16[512,256]{1,0:T(8,128)(2,1)S(1)}) custom-call(s32[2]{0:T(128)S(1)} %pad_add_fusion.1.where, s32[16384]{0:T(1024)S(1)} %bitcast.11, s32[2048]{0:T(1024)S(1)} %collective-permute-done.wanted, bf16[4096,256]{1,0:T(8,128)(2,1)S(1)} %copy-done.3, ...), custom_call_target="tpu_custom_call" | custom-call | flops 17179869184 | bytes 4194304 | tf_op jit(solution)/shard_map/pixel_rows/pallas_call | solution.py:288
  16.6 1.7 %add_convert_fusion = bf16[512,256]{1,0:T(8,128)(2,1)} fusion(bf16[512,256]{1,0:T(8,128)(2,1)} %collective-permute-done.2, bf16[512,256]{1,0:T(8,128)(2,1)S(1)} %get-tuple-element.21), kind=kLoop, calls=%fused_computation | loop fusion | flops 524288 | bytes 786432 | tf_op jit(solution)/shard_map/convert_element_type | solution.py:443
  18.3 0.6 collective-permute-start.3
  18.9 3.4 %collective-permute-start.4 = (bf16[512,256]{1,0:T(8,128)(2,1)}, bf16[512,256]{1,0:T(8,128)(2,1)S(1)}, u32[]{:S(2)}, u32[]{:S(2)}) collective-permute-start(bf16[512,256]{1,0:T(8,128)(2,1)} %add_convert_fusion), channel_id=1, source_target_pairs={{0,3},{1,2},{2,1},{3,0},{4,7},{5,6},{6,5},{7,4},{8,11},{9,10},{10,... | collective-permute-start | bytes 786440 | tf_op jit(solution)/shard_map/ppermute | solution.py:45
  22.3 1.5 %collective-permute-start.5 = (bf16[512,256]{1,0:T(8,128)(2,1)S(1)}, bf16[512,256]{1,0:T(8,128)(2,1)S(1)}, u32[]{:S(2)}, u32[]{:S(2)}) collective-permute-start(bf16[512,256]{1,0:T(8,128)(2,1)S(1)} %get-tuple-element.29), channel_id=1, source_target_pairs={{0,4},{4,0},{1,5},{5,1},{2,6},{6,2},{3,7},{7,3},{8,12},{12,8},{9,1... | collective-permute-start | bytes 786440 | tf_op jit(solution)/shard_map/ppermute | solution.py:45
  23.9 6.1 %pixel_rows.3.mine = bf16[512,256]{1,0:T(8,128)(2,1)S(1)} custom-call(s32[2]{0:T(128)S(1)} %pad_add_fusion.2.where, s32[16384]{0:T(1024)S(1)} %bitcast.12, s32[2048]{0:T(1024)S(1)} %copy-done.4, bf16[4096,256]{1,0:T(8,128)(2,1)S(1)} %copy-done.3, bf16[128,256]{1,0:T(8,128)(2,1)S(1)} %collective-permute-done.1.above.below, ...), custom_call_target="tpu_custom_call" | custom-call | flops 17179869184 | bytes 4194304 | tf_op jit(solution)/shard_map/pixel_rows/pallas_call | solution.py:288
  30.0 1.9 %project.3.keep = bf16[512,256]{1,0:T(8,128)(2,1)S(1)} custom-call(s32[1]{0:T(128)} %bitcast.4.chan, bf16[2048,1152]{1,0:T(8,128)(2,1)} %spectra.9, bf16[1152,256]{1,0:T(8,128)(2,1)S(1)} %copy-done), custom_call_target="tpu_custom_call" | custom-call | flops 301989888 | bytes 2031616 | tf_op jit(solution)/shard_map/project/pallas_call | solution.py:90
  32.0 1.2 %collective-permute-done.4.far = bf16[512,256]{1,0:T(8,128)(2,1)S(1)} collective-permute-done((bf16[512,256]{1,0:T(8,128)(2,1)}, bf16[512,256]{1,0:T(8,128)(2,1)S(1)}, u32[]{:S(2)}, u32[]{:S(2)}) %collective-permute-start.4) | collective-permute-done | bytes 262176 | tf_op jit(solution)/shard_map/ppermute | solution.py:45
  33.2 1.0 %pre_gradient.1.first = bf16[512,256]{1,0:T(8,128)(2,1)S(1)} custom-call(s32[2]{0:T(128)S(1)} %pad_add_fusion.where, bf16[512,256]{1,0:T(8,128)(2,1)S(1)} %project.3.keep, bf16[512,256]{1,0:T(8,128)(2,1)S(1)} %collective-permute-done.3.near, bf16[512,256]{1,0:T(8,128)(2,1)S(1)} %collective-permute-done.4.far, s32[16,128]{1,0:T(8,128)S(1)} %bitcast.13, ...), custom_call_target="tpu_custom_call" | custom-call | tf_op jit(solution)/shard_map/pre_gradient/pallas_call | solution.py:358
  34.2 0.5 collective-permute-start.6
  34.7 1.8 %collective-permute-start.7 = (bf16[512,256]{1,0:T(8,128)(2,1)S(1)}, bf16[512,256]{1,0:T(8,128)(2,1)S(1)}, u32[]{:S(2)}, u32[]{:S(2)}) collective-permute-start(bf16[512,256]{1,0:T(8,128)(2,1)S(1)} %pre_gradient.1.first), channel_id=1, source_target_pairs={{0,1},{1,0},{2,3},{3,2},{4,5},{5,4},{6,7},{7,6},{8,9},{9,8},{10,11... | collective-permute-start | bytes 786440 | tf_op jit(solution)/shard_map/ppermute | solution.py:45
  36.5 8.8 %collective-permute-done.6.second = bf16[512,256]{1,0:T(8,128)(2,1)S(1)} collective-permute-done((bf16[512,256]{1,0:T(8,128)(2,1)S(1)}, bf16[512,256]{1,0:T(8,128)(2,1)S(1)}, u32[]{:S(2)}, u32[]{:S(2)}) %collective-permute-start.6) | collective-permute-done | bytes 262176 | tf_op jit(solution)/shard_map/ppermute | solution.py:45
  45.3 0.2 collective-permute-start.8
  45.5 2.5 %early_product.1 = (f32[1152,256]{1,0:T(8,128)S(1)}, bf16[512,1152]{1,0:T(8,128)(2,1)S(1)}, bf16[512,1152]{1,0:T(8,128)(2,1)S(1)}) custom-call(s32[1]{0:T(128)} %bitcast.1.chan, bf16[2048,1152]{1,0:T(8,128)(2,1)} %spectra.9, bf16[512,256]{1,0:T(8,128)(2,1)S(1)} %pre_gradient.1.first, bf16[512,256]{1,0:T(8,128)(2,1)S(1)} %collective-permute-done.6.second), custom_call_target="tpu_custom_call" | custom-call | flops 603979776 | bytes 5898240 | tf_op jit(solution)/shard_map/early_product/pallas_call | solution.py:137
  48.1 0.5 more_product.1.before
  48.7 3.2 %collective-permute-done.8.rows = bf16[512,256]{1,0:T(8,128)(2,1)S(1)} collective-permute-done((bf16[512,256]{1,0:T(8,128)(2,1)S(1)}, bf16[512,256]{1,0:T(8,128)(2,1)S(1)}, u32[]{:S(2)}, u32[]{:S(2)}) %collective-permute-start.8) | collective-permute-done | bytes 262176 | tf_op jit(solution)/shard_map/ppermute | solution.py:45
  51.8 0.6 late_product.1
  52.5 0.5 collective-permute-start.12
  53.0 0.9 %collective-permute-done.9.second = bf16[288,256]{1,0:T(8,128)(2,1)S(1)} collective-permute-done((bf16[288,256]{1,0:T(8,128)(2,1)S(1)}, bf16[288,256]{1,0:T(8,128)(2,1)S(1)}, u32[]{:S(2)}, u32[]{:S(2)}) %collective-permute-start.9) | collective-permute-done | bytes 147488 | tf_op jit(solution)/shard_map/ppermute | solution.py:45
  53.9 1.6 %collective-permute-start.10 = (bf16[288,256]{1,0:T(8,128)(2,1)S(1)}, bf16[288,256]{1,0:T(8,128)(2,1)S(1)}, u32[]{:S(2)}, u32[]{:S(2)}) collective-permute-start(bf16[288,256]{1,0:T(8,128)(2,1)S(1)} %added.6.first), channel_id=1, source_target_pairs={{0,16},{4,20},{8,12},{12,8},{16,0},{20,4},{24,28},{28,24},{1,17},{... | collective-permute-start | bytes 442376 | tf_op jit(solution)/shard_map/ppermute | solution.py:413
  55.5 0.6 collective-permute-start.13
  56.1 3.0 %collective-permute-done.10.second = bf16[288,256]{1,0:T(8,128)(2,1)S(1)} collective-permute-done((bf16[288,256]{1,0:T(8,128)(2,1)S(1)}, bf16[288,256]{1,0:T(8,128)(2,1)S(1)}, u32[]{:S(2)}, u32[]{:S(2)}) %collective-permute-start.10) | collective-permute-done | bytes 147488 | tf_op jit(solution)/shard_map/ppermute | solution.py:413
  59.1 1.6 %collective-permute-start.11 = (bf16[288,256]{1,0:T(8,128)(2,1)S(1)}, bf16[288,256]{1,0:T(8,128)(2,1)S(1)}, u32[]{:S(2)}, u32[]{:S(2)}) collective-permute-start(bf16[288,256]{1,0:T(8,128)(2,1)S(1)} %added.7.first), channel_id=1, source_target_pairs={{0,4},{4,0},{8,24},{12,28},{16,20},{20,16},{24,8},{28,12},{1,5},{5... | collective-permute-start | bytes 442376 | tf_op jit(solution)/shard_map/ppermute | solution.py:413
  60.8 1.6 %collective-permute-start.14 = (bf16[288,256]{1,0:T(8,128)(2,1)S(1)}, bf16[288,256]{1,0:T(8,128)(2,1)S(1)}, u32[]{:S(2)}, u32[]{:S(2)}) collective-permute-start(bf16[288,256]{1,0:T(8,128)(2,1)S(1)} %added.10.first), channel_id=1, source_target_pairs={{0,4},{4,0},{8,24},{12,28},{16,20},{20,16},{24,8},{28,12},{1,5},{5... | collective-permute-start | bytes 442376 | tf_op jit(solution)/shard_map/ppermute | solution.py:413
  62.3 2.0 %collective-permute-done.11.second = bf16[288,256]{1,0:T(8,128)(2,1)S(1)} collective-permute-done((bf16[288,256]{1,0:T(8,128)(2,1)S(1)}, bf16[288,256]{1,0:T(8,128)(2,1)S(1)}, u32[]{:S(2)}, u32[]{:S(2)}) %collective-permute-start.11) | collective-permute-done | bytes 147488 | tf_op jit(solution)/shard_map/ppermute | solution.py:413
  64.5 1.5 %collective-permute-done.14.second = bf16[288,256]{1,0:T(8,128)(2,1)S(1)} collective-permute-done((bf16[288,256]{1,0:T(8,128)(2,1)S(1)}, bf16[288,256]{1,0:T(8,128)(2,1)S(1)}, u32[]{:S(2)}, u32[]{:S(2)}) %collective-permute-start.14) | collective-permute-done | bytes 147488 | tf_op jit(solution)/shard_map/ppermute | solution.py:413
  66.1 1.3 %collective-permute-done.16.refs_3_ = bf16[288,256]{1,0:T(8,128)(2,1)S(1)} collective-permute-done((bf16[288,256]{1,0:T(8,128)(2,1)S(1)}, bf16[288,256]{1,0:T(8,128)(2,1)S(1)}, u32[]{:S(2)}, u32[]{:S(2)}) %collective-permute-start.16) | collective-permute-done | bytes 147488 | tf_op jit(solution)/shard_map/ppermute | solution.py:45
  67.5 1.1 %collect.1 = f32[1152,256]{1,0:T(8,128)} custom-call(s32[1]{0:T(128)} %bitcast.core, bf16[288,256]{1,0:T(8,128)(2,1)S(1)} %added.8.refs_0_, bf16[288,256]{1,0:T(8,128)(2,1)S(1)} %added.11.refs_1_, bf16[288,256]{1,0:T(8,128)(2,1)S(1)} %collective-permute-done.15.refs_2_, bf16[288,256]{1,0:T(8,128)(2,1)S(1)} %collective-permute-done.16.refs_3_), custom_call_target="tpu_custom_call" | custom-call | tf_op jit(solution)/shard_map/collect/pallas_call | solution.py:382
  (39 shorter events, 1.0 us)
Async XLA Ops:
  0.0 9.1 %collective-permute-start = (s32[2048]{0:T(1024)}, s32[2048]{0:T(1024)S(1)}, u32[]{:S(2)}, u32[]{:S(2)}) collective-permute-start(s32[2048]{0:T(1024)} %wanted.1), channel_id=1, source_target_pairs={{0,4},{4,0},{1,5},{5,1},{2,6},{6,2},{3,7},{7,3},{8,12},{12,8},{9,1... | collective-permute-start | bytes 24584 | tf_op jit(solution)/shard_map/ppermute | solution.py:45
  3.9 5.3 %collective-permute-start.1 = (bf16[128,256]{1,0:T(8,128)(2,1)S(1)}, bf16[128,256]{1,0:T(8,128)(2,1)S(1)}, u32[]{:S(2)}, u32[]{:S(2)}) collective-permute-start(bf16[128,256]{1,0:T(8,128)(2,1)S(1)} %slice_select_fusion), channel_id=1, source_target_pairs={{0,4},{4,0},{1,5},{5,1},{2,6},{6,2},{3,7},{7,3},{8,12},{12,8},{9,1... | collective-permute-start | bytes 196616 | tf_op jit(solution)/shard_map/ppermute | solution.py:22
  3.9 5.1 %copy-start.6 = (s32[8,4096]{1,0:T(8,128)S(1)}, s32[8,4096]{1,0:T(8,128)}, u32[]{:S(2)}) copy-start(s32[8,4096]{1,0:T(8,128)} %param.14) | copy-start | bytes 393220
  3.9 5.2 %copy-start = (bf16[1152,256]{1,0:T(8,128)(2,1)S(1)}, bf16[1152,256]{1,0:T(8,128)(2,1)}, u32[]{:S(2)}) copy-start(bf16[1152,256]{1,0:T(8,128)(2,1)} %weight.7) | copy-start | bytes 1769476
  4.0 5.2 %copy-start.3 = (bf16[4096,256]{1,0:T(8,128)(2,1)S(1)}, bf16[4096,256]{1,0:T(8,128)(2,1)}, u32[]{:S(2)}) copy-start(bf16[4096,256]{1,0:T(8,128)(2,1)} %cotangent.3) | copy-start | bytes 6291460
  4.0 5.2 %copy-start.5 = (f32[8,256]{1,0:T(8,128)S(1)}, f32[8,256]{1,0:T(8,128)}, u32[]{:S(2)}) copy-start(f32[8,256]{1,0:T(8,128)} %mixing.3) | copy-start | bytes 24580
  6.8 9.7 %collective-permute-start.2 = (bf16[512,256]{1,0:T(8,128)(2,1)}, bf16[512,256]{1,0:T(8,128)(2,1)}, u32[]{:S(2)}, u32[]{:S(2)}) collective-permute-start(bf16[512,256]{1,0:T(8,128)(2,1)} %project.2), channel_id=1, source_target_pairs={{0,1},{1,0},{2,3},{3,2},{4,5},{5,4},{6,7},{7,6},{8,9},{9,8},{10,11... | collective-permute-start | bytes 786440 | tf_op jit(solution)/shard_map/ppermute | solution.py:45
  9.2 14.8 %copy-start.4 = (s32[2048]{0:T(1024)S(1)}, s32[2048]{0:T(1024)}, u32[]{:S(2)}) copy-start(s32[2048]{0:T(1024)} %wanted.1) | copy-start | bytes 24580
  18.3 13.7 %collective-permute-start.3 = (bf16[512,256]{1,0:T(8,128)(2,1)S(1)}, bf16[512,256]{1,0:T(8,128)(2,1)S(1)}, u32[]{:S(2)}, u32[]{:S(2)}) collective-permute-start(bf16[512,256]{1,0:T(8,128)(2,1)S(1)} %get-tuple-element.27), channel_id=1, source_target_pairs={{0,1},{1,0},{2,3},{3,2},{4,5},{5,4},{6,7},{7,6},{8,9},{9,8},{10,11... | collective-permute-start | bytes 786440 | tf_op jit(solution)/shard_map/ppermute | solution.py:45
  18.9 14.3 %collective-permute-start.4 = (bf16[512,256]{1,0:T(8,128)(2,1)}, bf16[512,256]{1,0:T(8,128)(2,1)S(1)}, u32[]{:S(2)}, u32[]{:S(2)}) collective-permute-start(bf16[512,256]{1,0:T(8,128)(2,1)} %add_convert_fusion), channel_id=1, source_target_pairs={{0,3},{1,2},{2,1},{3,0},{4,7},{5,6},{6,5},{7,4},{8,11},{9,10},{10,... | collective-permute-start | bytes 786440 | tf_op jit(solution)/shard_map/ppermute | solution.py:45
  22.3 10.8 %collective-permute-start.5 = (bf16[512,256]{1,0:T(8,128)(2,1)S(1)}, bf16[512,256]{1,0:T(8,128)(2,1)S(1)}, u32[]{:S(2)}, u32[]{:S(2)}) collective-permute-start(bf16[512,256]{1,0:T(8,128)(2,1)S(1)} %get-tuple-element.29), channel_id=1, source_target_pairs={{0,4},{4,0},{1,5},{5,1},{2,6},{6,2},{3,7},{7,3},{8,12},{12,8},{9,1... | collective-permute-start | bytes 786440 | tf_op jit(solution)/shard_map/ppermute | solution.py:45
  30.0 3.2 %copy-start.1 = (s32[2048,1]{0,1:T(1,128)S(1)}, s32[2048,1]{0,1:T(1,128)}, u32[]{:S(2)}) copy-start(s32[2048,1]{0,1:T(1,128)} %param.10) | copy-start | bytes 24580
  30.0 3.2 %copy-start.2 = (f32[2048]{0:T(1024)S(1)}, f32[2048]{0:T(1024)}, u32[]{:S(2)}) copy-start(f32[2048]{0:T(1024)} %param.12) | copy-start | bytes 24580
  34.2 11.1 %collective-permute-start.6 = (bf16[512,256]{1,0:T(8,128)(2,1)S(1)}, bf16[512,256]{1,0:T(8,128)(2,1)S(1)}, u32[]{:S(2)}, u32[]{:S(2)}) collective-permute-start(bf16[512,256]{1,0:T(8,128)(2,1)S(1)} %pre_gradient.1.first), channel_id=1, source_target_pairs={{0,3},{1,2},{2,1},{3,0},{4,7},{5,6},{6,5},{7,4},{8,11},{9,10},{10,... | collective-permute-start | bytes 786440 | tf_op jit(solution)/shard_map/ppermute | solution.py:45
  34.7 13.4 %collective-permute-start.7 = (bf16[512,256]{1,0:T(8,128)(2,1)S(1)}, bf16[512,256]{1,0:T(8,128)(2,1)S(1)}, u32[]{:S(2)}, u32[]{:S(2)}) collective-permute-start(bf16[512,256]{1,0:T(8,128)(2,1)S(1)} %pre_gradient.1.first), channel_id=1, source_target_pairs={{0,1},{1,0},{2,3},{3,2},{4,5},{5,4},{6,7},{7,6},{8,9},{9,8},{10,11... | collective-permute-start | bytes 786440 | tf_op jit(solution)/shard_map/ppermute | solution.py:45
  45.3 6.5 %collective-permute-start.8 = (bf16[512,256]{1,0:T(8,128)(2,1)S(1)}, bf16[512,256]{1,0:T(8,128)(2,1)S(1)}, u32[]{:S(2)}, u32[]{:S(2)}) collective-permute-start(bf16[512,256]{1,0:T(8,128)(2,1)S(1)} %collective-permute-done.6.second), channel_id=1, source_target_pairs={{0,1},{1,0},{2,3},{3,2},{4,5},{5,4},{6,7},{7,6},{8,9},{9,8},{10,11... | collective-permute-start | bytes 786440 | tf_op jit(solution)/shard_map/ppermute | solution.py:45
  52.4 1.4 %collective-permute-start.9 = (bf16[288,256]{1,0:T(8,128)(2,1)S(1)}, bf16[288,256]{1,0:T(8,128)(2,1)S(1)}, u32[]{:S(2)}, u32[]{:S(2)}) collective-permute-start(bf16[288,256]{1,0:T(8,128)(2,1)S(1)} %get-tuple-element.34), channel_id=1, source_target_pairs={{0,8},{8,0},{16,24},{24,16},{1,9},{9,1},{17,25},{25,17},{2,10},{10... | collective-permute-start | bytes 442376 | tf_op jit(solution)/shard_map/ppermute | solution.py:45
  52.5 3.0 %collective-permute-start.12 = (bf16[288,256]{1,0:T(8,128)(2,1)S(1)}, bf16[288,256]{1,0:T(8,128)(2,1)S(1)}, u32[]{:S(2)}, u32[]{:S(2)}) collective-permute-start(bf16[288,256]{1,0:T(8,128)(2,1)S(1)} %get-tuple-element.36), channel_id=1, source_target_pairs={{0,8},{8,0},{16,24},{24,16},{1,9},{9,1},{17,25},{25,17},{2,10},{10... | collective-permute-start | bytes 442376 | tf_op jit(solution)/shard_map/ppermute | solution.py:45
  53.9 5.2 %collective-permute-start.10 = (bf16[288,256]{1,0:T(8,128)(2,1)S(1)}, bf16[288,256]{1,0:T(8,128)(2,1)S(1)}, u32[]{:S(2)}, u32[]{:S(2)}) collective-permute-start(bf16[288,256]{1,0:T(8,128)(2,1)S(1)} %added.6.first), channel_id=1, source_target_pairs={{0,16},{4,20},{8,12},{12,8},{16,0},{20,4},{24,28},{28,24},{1,17},{... | collective-permute-start | bytes 442376 | tf_op jit(solution)/shard_map/ppermute | solution.py:413
  55.5 5.2 %collective-permute-start.13 = (bf16[288,256]{1,0:T(8,128)(2,1)S(1)}, bf16[288,256]{1,0:T(8,128)(2,1)S(1)}, u32[]{:S(2)}, u32[]{:S(2)}) collective-permute-start(bf16[288,256]{1,0:T(8,128)(2,1)S(1)} %added.9.first), channel_id=1, source_target_pairs={{0,16},{4,20},{8,12},{12,8},{16,0},{20,4},{24,28},{28,24},{1,17},{... | collective-permute-start | bytes 442376 | tf_op jit(solution)/shard_map/ppermute | solution.py:413
  59.1 5.2 %collective-permute-start.11 = (bf16[288,256]{1,0:T(8,128)(2,1)S(1)}, bf16[288,256]{1,0:T(8,128)(2,1)S(1)}, u32[]{:S(2)}, u32[]{:S(2)}) collective-permute-start(bf16[288,256]{1,0:T(8,128)(2,1)S(1)} %added.7.first), channel_id=1, source_target_pairs={{0,4},{4,0},{8,24},{12,28},{16,20},{20,16},{24,8},{28,12},{1,5},{5... | collective-permute-start | bytes 442376 | tf_op jit(solution)/shard_map/ppermute | solution.py:413
  60.8 5.2 %collective-permute-start.14 = (bf16[288,256]{1,0:T(8,128)(2,1)S(1)}, bf16[288,256]{1,0:T(8,128)(2,1)S(1)}, u32[]{:S(2)}, u32[]{:S(2)}) collective-permute-start(bf16[288,256]{1,0:T(8,128)(2,1)S(1)} %added.10.first), channel_id=1, source_target_pairs={{0,4},{4,0},{8,24},{12,28},{16,20},{20,16},{24,8},{28,12},{1,5},{5... | collective-permute-start | bytes 442376 | tf_op jit(solution)/shard_map/ppermute | solution.py:413
  64.4 1.7 %collective-permute-start.15 = (bf16[288,256]{1,0:T(8,128)(2,1)S(1)}, bf16[288,256]{1,0:T(8,128)(2,1)S(1)}, u32[]{:S(2)}, u32[]{:S(2)}) collective-permute-start(bf16[288,256]{1,0:T(8,128)(2,1)S(1)} %added.8.refs_0_), channel_id=1, source_target_pairs={{0,8},{8,0},{16,24},{24,16},{1,9},{9,1},{17,25},{25,17},{2,10},{10... | collective-permute-start | bytes 442376 | tf_op jit(solution)/shard_map/ppermute | solution.py:45
  66.0 1.4 %collective-permute-start.16 = (bf16[288,256]{1,0:T(8,128)(2,1)S(1)}, bf16[288,256]{1,0:T(8,128)(2,1)S(1)}, u32[]{:S(2)}, u32[]{:S(2)}) collective-permute-start(bf16[288,256]{1,0:T(8,128)(2,1)S(1)} %added.11.refs_1_), channel_id=1, source_target_pairs={{0,8},{8,0},{16,24},{24,16},{1,9},{9,1},{17,25},{25,17},{2,10},{10... | collective-permute-start | bytes 442376 | tf_op jit(solution)/shard_map/ppermute | solution.py:45

commit v15 on v14

--- a/solution.py
+++ b/solution.py
@@ -308,7 +308,7 @@
             pltpu.VMEM((max(len(bits), 1) * rows, depth), jnp.bfloat16),
             pltpu.SemaphoreType.DMA((len(bits) + 2,)),
         ],
-        compiler_params=memory(48),
+        compiler_params=memory(47),
         cost_estimate=pl.CostEstimate(
             flops=8 * NEIGH * count * 2048 * width,
             bytes_accessed=4 * tile_rows * width,
@@ -422,7 +422,7 @@
     chan = lax.axis_index("chan")
     first_row = chan * quarter
 
-    near_first = swap(project(spectra, enc_weight, chan, (2,), LARGE + 4)[0], "chan", 1)
+    near_first = swap(project(spectra, enc_weight, chan, (2,), LARGE + 2)[0], "chan", 1)
     places = (adjoint - (tile * tile_rows - HALO)) * 2
     places = (places[: NEIGH // 2] | (places[NEIGH // 2 :] << 16)).reshape(-1)
 

time: 68.8 us -> 68.8 us (level)
  no operation moved by 1% of the time
where the time goes in v15:
time: 68.8 us; the launch traced here: 68.5 us
  Pallas kernels  24.1 us (35%)
  waiting for transfers between devices  22.1 us (32%)
  starting transfers between devices  19.2 us (28%)
  other arithmetic  2.86 us (4%)
    ppermute x12, waiting for transfers between devices, swap(): return lax.ppermute(value, axis, [(i, i ^ bit) for i in range(size)])  15.6 us
    ppermute x12, starting transfers between devices, swap(): return lax.ppermute(value, axis, [(i, i ^ bit) for i in range(size)])  13.8 us
    pallas_call x2, Pallas kernels, pixel_rows(): pl.pallas_call(functools.partial(pixel_kernel, count, bits), out_shape=(j...  13.4 us
    ppermute x4, waiting for transfers between devices, sum_over_panels(): parts = [added(part, lax.ppermute(part, both, perm)) for part in parts]  6.55 us
    ppermute x4, starting transfers between devices, sum_over_panels(): parts = [added(part, lax.ppermute(part, both, perm)) for part in parts]  5.3 us
    pallas_call x2, Pallas kernels, project(): pl.pallas_call(functools.partial(project_kernel, bits), out_shape=(jax.Sh...  4.75 us
    pallas_call x1, Pallas kernels, early_product(): pl.pallas_call(early_kernel, out_shape=(jax.ShapeDtypeStruct((depth, widt...  2.49 us
    convert_element_type x1, other arithmetic, shards(): (shared.astype(jnp.float32) + near_first.astype(jnp.float32)).astype(jnp....  1.72 us
  transfers between devices with their start and end apart: 17, of which 9 were waited for; matrix products, arithmetic and copies ran while one was open for 2% of the time, Pallas kernels for 31%

profile of v15, /device:TPU:0, one launch (start us, length us, event | category | flops | bytes accessed | tf_op | source)
XLA Modules:
  0.0 68.5 jit_solution(4679149374831541407)
XLA Ops:
  0.0 3.0 %collective-permute-start = (s32[2048]{0:T(1024)}, s32[2048]{0:T(1024)S(1)}, u32[]{:S(2)}, u32[]{:S(2)}) collective-permute-start(s32[2048]{0:T(1024)} %wanted.1), channel_id=1, source_target_pairs={{0,4},{4,0},{1,5},{5,1},{2,6},{6,2},{3,7},{7,3},{8,12},{12,8},{9,1... | collective-permute-start | bytes 24584 | tf_op jit(solution)/shard_map/ppermute | solution.py:45
  3.0 0.9 %slice_select_fusion = bf16[128,256]{1,0:T(8,128)(2,1)S(1)} fusion(bf16[4096,256]{1,0:T(8,128)(2,1)} %cotangent.3, pred[]{:T(512)S(6)} %eq.3), kind=kLoop, calls=%fused_computation.5 | loop fusion | flops 32768 | bytes 196609 | tf_op jit(solution)/shard_map/jit(_where)/select_n | solution.py:22
  4.0 2.8 %project.2 = bf16[512,256]{1,0:T(8,128)(2,1)} custom-call(s32[1]{0:T(128)} %bitcast.1.chan, bf16[2048,1152]{1,0:T(8,128)(2,1)} %spectra.9, bf16[1152,256]{1,0:T(8,128)(2,1)} %weight.7), custom_call_target="tpu_custom_call" | custom-call | flops 301989888 | bytes 2031616 | tf_op jit(solution)/shard_map/project/pallas_call | solution.py:90
  6.8 2.1 %collective-permute-start.2 = (bf16[512,256]{1,0:T(8,128)(2,1)}, bf16[512,256]{1,0:T(8,128)(2,1)}, u32[]{:S(2)}, u32[]{:S(2)}) collective-permute-start(bf16[512,256]{1,0:T(8,128)(2,1)} %project.2), channel_id=1, source_target_pairs={{0,1},{1,0},{2,3},{3,2},{4,5},{5,4},{6,7},{7,6},{8,9},{9,8},{10,11... | collective-permute-start | bytes 786440 | tf_op jit(solution)/shard_map/ppermute | solution.py:45
  9.2 7.4 %pixel_rows.2 = (bf16[512,256]{1,0:T(8,128)(2,1)S(1)}, bf16[512,256]{1,0:T(8,128)(2,1)S(1)}, bf16[512,256]{1,0:T(8,128)(2,1)S(1)}) custom-call(s32[2]{0:T(128)S(1)} %pad_add_fusion.1.where, s32[16384]{0:T(1024)S(1)} %bitcast.11, s32[2048]{0:T(1024)S(1)} %collective-permute-done.wanted, bf16[4096,256]{1,0:T(8,128)(2,1)S(1)} %copy-done.3, ...), custom_call_target="tpu_custom_call" | custom-call | flops 17179869184 | bytes 4194304 | tf_op jit(solution)/shard_map/pixel_rows/pallas_call | solution.py:288
  16.6 1.7 %add_convert_fusion = bf16[512,256]{1,0:T(8,128)(2,1)} fusion(bf16[512,256]{1,0:T(8,128)(2,1)} %collective-permute-done.2, bf16[512,256]{1,0:T(8,128)(2,1)S(1)} %get-tuple-element.21), kind=kLoop, calls=%fused_computation | loop fusion | flops 524288 | bytes 786432 | tf_op jit(solution)/shard_map/convert_element_type | solution.py:443
  18.3 0.6 collective-permute-start.3
  18.9 3.4 %collective-permute-start.4 = (bf16[512,256]{1,0:T(8,128)(2,1)}, bf16[512,256]{1,0:T(8,128)(2,1)S(1)}, u32[]{:S(2)}, u32[]{:S(2)}) collective-permute-start(bf16[512,256]{1,0:T(8,128)(2,1)} %add_convert_fusion), channel_id=1, source_target_pairs={{0,3},{1,2},{2,1},{3,0},{4,7},{5,6},{6,5},{7,4},{8,11},{9,10},{10,... | collective-permute-start | bytes 786440 | tf_op jit(solution)/shard_map/ppermute | solution.py:45
  22.3 1.5 %collective-permute-start.5 = (bf16[512,256]{1,0:T(8,128)(2,1)S(1)}, bf16[512,256]{1,0:T(8,128)(2,1)S(1)}, u32[]{:S(2)}, u32[]{:S(2)}) collective-permute-start(bf16[512,256]{1,0:T(8,128)(2,1)S(1)} %get-tuple-element.29), channel_id=1, source_target_pairs={{0,4},{4,0},{1,5},{5,1},{2,6},{6,2},{3,7},{7,3},{8,12},{12,8},{9,1... | collective-permute-start | bytes 786440 | tf_op jit(solution)/shard_map/ppermute | solution.py:45
  23.9 6.1 %pixel_rows.3.mine = bf16[512,256]{1,0:T(8,128)(2,1)S(1)} custom-call(s32[2]{0:T(128)S(1)} %pad_add_fusion.2.where, s32[16384]{0:T(1024)S(1)} %bitcast.12, s32[2048]{0:T(1024)S(1)} %copy-done.4, bf16[4096,256]{1,0:T(8,128)(2,1)S(1)} %copy-done.3, bf16[128,256]{1,0:T(8,128)(2,1)S(1)} %collective-permute-done.1.above.below, ...), custom_call_target="tpu_custom_call" | custom-call | flops 17179869184 | bytes 4194304 | tf_op jit(solution)/shard_map/pixel_rows/pallas_call | solution.py:288
  30.0 1.9 %project.3.keep = bf16[512,256]{1,0:T(8,128)(2,1)S(1)} custom-call(s32[1]{0:T(128)} %bitcast.4.chan, bf16[2048,1152]{1,0:T(8,128)(2,1)} %spectra.9, bf16[1152,256]{1,0:T(8,128)(2,1)S(1)} %copy-done), custom_call_target="tpu_custom_call" | custom-call | flops 301989888 | bytes 2031616 | tf_op jit(solution)/shard_map/project/pallas_call | solution.py:90
  32.0 1.2 %collective-permute-done.4.far = bf16[512,256]{1,0:T(8,128)(2,1)S(1)} collective-permute-done((bf16[512,256]{1,0:T(8,128)(2,1)}, bf16[512,256]{1,0:T(8,128)(2,1)S(1)}, u32[]{:S(2)}, u32[]{:S(2)}) %collective-permute-start.4) | collective-permute-done | bytes 262176 | tf_op jit(solution)/shard_map/ppermute | solution.py:45
  33.2 1.0 %pre_gradient.1.first = bf16[512,256]{1,0:T(8,128)(2,1)S(1)} custom-call(s32[2]{0:T(128)S(1)} %pad_add_fusion.where, bf16[512,256]{1,0:T(8,128)(2,1)S(1)} %project.3.keep, bf16[512,256]{1,0:T(8,128)(2,1)S(1)} %collective-permute-done.3.near, bf16[512,256]{1,0:T(8,128)(2,1)S(1)} %collective-permute-done.4.far, s32[16,128]{1,0:T(8,128)S(1)} %bitcast.13, ...), custom_call_target="tpu_custom_call" | custom-call | tf_op jit(solution)/shard_map/pre_gradient/pallas_call | solution.py:358
  34.2 0.5 collective-permute-start.6
  34.7 1.8 %collective-permute-start.7 = (bf16[512,256]{1,0:T(8,128)(2,1)S(1)}, bf16[512,256]{1,0:T(8,128)(2,1)S(1)}, u32[]{:S(2)}, u32[]{:S(2)}) collective-permute-start(bf16[512,256]{1,0:T(8,128)(2,1)S(1)} %pre_gradient.1.first), channel_id=1, source_target_pairs={{0,1},{1,0},{2,3},{3,2},{4,5},{5,4},{6,7},{7,6},{8,9},{9,8},{10,11... | collective-permute-start | bytes 786440 | tf_op jit(solution)/shard_map/ppermute | solution.py:45
  36.5 8.8 %collective-permute-done.6.second = bf16[512,256]{1,0:T(8,128)(2,1)S(1)} collective-permute-done((bf16[512,256]{1,0:T(8,128)(2,1)S(1)}, bf16[512,256]{1,0:T(8,128)(2,1)S(1)}, u32[]{:S(2)}, u32[]{:S(2)}) %collective-permute-start.6) | collective-permute-done | bytes 262176 | tf_op jit(solution)/shard_map/ppermute | solution.py:45
  45.3 0.2 collective-permute-start.8
  45.5 2.5 %early_product.1 = (f32[1152,256]{1,0:T(8,128)S(1)}, bf16[512,1152]{1,0:T(8,128)(2,1)S(1)}, bf16[512,1152]{1,0:T(8,128)(2,1)S(1)}) custom-call(s32[1]{0:T(128)} %bitcast.1.chan, bf16[2048,1152]{1,0:T(8,128)(2,1)} %spectra.9, bf16[512,256]{1,0:T(8,128)(2,1)S(1)} %pre_gradient.1.first, bf16[512,256]{1,0:T(8,128)(2,1)S(1)} %collective-permute-done.6.second), custom_call_target="tpu_custom_call" | custom-call | flops 603979776 | bytes 5898240 | tf_op jit(solution)/shard_map/early_product/pallas_call | solution.py:137
  48.1 0.5 more_product.1.before
  48.7 3.2 %collective-permute-done.8.rows = bf16[512,256]{1,0:T(8,128)(2,1)S(1)} collective-permute-done((bf16[512,256]{1,0:T(8,128)(2,1)S(1)}, bf16[512,256]{1,0:T(8,128)(2,1)S(1)}, u32[]{:S(2)}, u32[]{:S(2)}) %collective-permute-start.8) | collective-permute-done | bytes 262176 | tf_op jit(solution)/shard_map/ppermute | solution.py:45
  51.8 0.6 late_product.1
  52.5 0.5 collective-permute-start.12
  53.0 0.9 %collective-permute-done.9.second = bf16[288,256]{1,0:T(8,128)(2,1)S(1)} collective-permute-done((bf16[288,256]{1,0:T(8,128)(2,1)S(1)}, bf16[288,256]{1,0:T(8,128)(2,1)S(1)}, u32[]{:S(2)}, u32[]{:S(2)}) %collective-permute-start.9) | collective-permute-done | bytes 147488 | tf_op jit(solution)/shard_map/ppermute | solution.py:45
  53.9 1.6 %collective-permute-start.10 = (bf16[288,256]{1,0:T(8,128)(2,1)S(1)}, bf16[288,256]{1,0:T(8,128)(2,1)S(1)}, u32[]{:S(2)}, u32[]{:S(2)}) collective-permute-start(bf16[288,256]{1,0:T(8,128)(2,1)S(1)} %added.6.first), channel_id=1, source_target_pairs={{0,16},{4,20},{8,12},{12,8},{16,0},{20,4},{24,28},{28,24},{1,17},{... | collective-permute-start | bytes 442376 | tf_op jit(solution)/shard_map/ppermute | solution.py:413
  55.5 0.6 collective-permute-start.13
  56.1 3.0 %collective-permute-done.10.second = bf16[288,256]{1,0:T(8,128)(2,1)S(1)} collective-permute-done((bf16[288,256]{1,0:T(8,128)(2,1)S(1)}, bf16[288,256]{1,0:T(8,128)(2,1)S(1)}, u32[]{:S(2)}, u32[]{:S(2)}) %collective-permute-start.10) | collective-permute-done | bytes 147488 | tf_op jit(solution)/shard_map/ppermute | solution.py:413
  59.1 1.6 %collective-permute-start.11 = (bf16[288,256]{1,0:T(8,128)(2,1)S(1)}, bf16[288,256]{1,0:T(8,128)(2,1)S(1)}, u32[]{:S(2)}, u32[]{:S(2)}) collective-permute-start(bf16[288,256]{1,0:T(8,128)(2,1)S(1)} %added.7.first), channel_id=1, source_target_pairs={{0,4},{4,0},{8,24},{12,28},{16,20},{20,16},{24,8},{28,12},{1,5},{5... | collective-permute-start | bytes 442376 | tf_op jit(solution)/shard_map/ppermute | solution.py:413
  60.8 1.6 %collective-permute-start.14 = (bf16[288,256]{1,0:T(8,128)(2,1)S(1)}, bf16[288,256]{1,0:T(8,128)(2,1)S(1)}, u32[]{:S(2)}, u32[]{:S(2)}) collective-permute-start(bf16[288,256]{1,0:T(8,128)(2,1)S(1)} %added.10.first), channel_id=1, source_target_pairs={{0,4},{4,0},{8,24},{12,28},{16,20},{20,16},{24,8},{28,12},{1,5},{5... | collective-permute-start | bytes 442376 | tf_op jit(solution)/shard_map/ppermute | solution.py:413
  62.3 2.0 %collective-permute-done.11.second = bf16[288,256]{1,0:T(8,128)(2,1)S(1)} collective-permute-done((bf16[288,256]{1,0:T(8,128)(2,1)S(1)}, bf16[288,256]{1,0:T(8,128)(2,1)S(1)}, u32[]{:S(2)}, u32[]{:S(2)}) %collective-permute-start.11) | collective-permute-done | bytes 147488 | tf_op jit(solution)/shard_map/ppermute | solution.py:413
  64.5 1.5 %collective-permute-done.14.second = bf16[288,256]{1,0:T(8,128)(2,1)S(1)} collective-permute-done((bf16[288,256]{1,0:T(8,128)(2,1)S(1)}, bf16[288,256]{1,0:T(8,128)(2,1)S(1)}, u32[]{:S(2)}, u32[]{:S(2)}) %collective-permute-start.14) | collective-permute-done | bytes 147488 | tf_op jit(solution)/shard_map/ppermute | solution.py:413
  66.1 1.3 %collective-permute-done.16.refs_3_ = bf16[288,256]{1,0:T(8,128)(2,1)S(1)} collective-permute-done((bf16[288,256]{1,0:T(8,128)(2,1)S(1)}, bf16[288,256]{1,0:T(8,128)(2,1)S(1)}, u32[]{:S(2)}, u32[]{:S(2)}) %collective-permute-start.16) | collective-permute-done | bytes 147488 | tf_op jit(solution)/shard_map/ppermute | solution.py:45
  67.5 1.1 %collect.1 = f32[1152,256]{1,0:T(8,128)} custom-call(s32[1]{0:T(128)} %bitcast.core, bf16[288,256]{1,0:T(8,128)(2,1)S(1)} %added.8.refs_0_, bf16[288,256]{1,0:T(8,128)(2,1)S(1)} %added.11.refs_1_, bf16[288,256]{1,0:T(8,128)(2,1)S(1)} %collective-permute-done.15.refs_2_, bf16[288,256]{1,0:T(8,128)(2,1)S(1)} %collective-permute-done.16.refs_3_), custom_call_target="tpu_custom_call" | custom-call | tf_op jit(solution)/shard_map/collect/pallas_call | solution.py:382
  (39 shorter events, 1.0 us)
Async XLA Ops:
  0.0 9.1 %collective-permute-start = (s32[2048]{0:T(1024)}, s32[2048]{0:T(1024)S(1)}, u32[]{:S(2)}, u32[]{:S(2)}) collective-permute-start(s32[2048]{0:T(1024)} %wanted.1), channel_id=1, source_target_pairs={{0,4},{4,0},{1,5},{5,1},{2,6},{6,2},{3,7},{7,3},{8,12},{12,8},{9,1... | collective-permute-start | bytes 24584 | tf_op jit(solution)/shard_map/ppermute | solution.py:45
  3.9 5.3 %collective-permute-start.1 = (bf16[128,256]{1,0:T(8,128)(2,1)S(1)}, bf16[128,256]{1,0:T(8,128)(2,1)S(1)}, u32[]{:S(2)}, u32[]{:S(2)}) collective-permute-start(bf16[128,256]{1,0:T(8,128)(2,1)S(1)} %slice_select_fusion), channel_id=1, source_target_pairs={{0,4},{4,0},{1,5},{5,1},{2,6},{6,2},{3,7},{7,3},{8,12},{12,8},{9,1... | collective-permute-start | bytes 196616 | tf_op jit(solution)/shard_map/ppermute | solution.py:22
  3.9 5.1 %copy-start.6 = (s32[8,4096]{1,0:T(8,128)S(1)}, s32[8,4096]{1,0:T(8,128)}, u32[]{:S(2)}) copy-start(s32[8,4096]{1,0:T(8,128)} %param.14) | copy-start | bytes 393220
  3.9 5.2 %copy-start = (bf16[1152,256]{1,0:T(8,128)(2,1)S(1)}, bf16[1152,256]{1,0:T(8,128)(2,1)}, u32[]{:S(2)}) copy-start(bf16[1152,256]{1,0:T(8,128)(2,1)} %weight.7) | copy-start | bytes 1769476
  4.0 5.2 %copy-start.3 = (bf16[4096,256]{1,0:T(8,128)(2,1)S(1)}, bf16[4096,256]{1,0:T(8,128)(2,1)}, u32[]{:S(2)}) copy-start(bf16[4096,256]{1,0:T(8,128)(2,1)} %cotangent.3) | copy-start | bytes 6291460
  4.0 5.2 %copy-start.5 = (f32[8,256]{1,0:T(8,128)S(1)}, f32[8,256]{1,0:T(8,128)}, u32[]{:S(2)}) copy-start(f32[8,256]{1,0:T(8,128)} %mixing.3) | copy-start | bytes 24580
  6.8 9.7 %collective-permute-start.2 = (bf16[512,256]{1,0:T(8,128)(2,1)}, bf16[512,256]{1,0:T(8,128)(2,1)}, u32[]{:S(2)}, u32[]{:S(2)}) collective-permute-start(bf16[512,256]{1,0:T(8,128)(2,1)} %project.2), channel_id=1, source_target_pairs={{0,1},{1,0},{2,3},{3,2},{4,5},{5,4},{6,7},{7,6},{8,9},{9,8},{10,11... | collective-permute-start | bytes 786440 | tf_op jit(solution)/shard_map/ppermute | solution.py:45
  9.2 14.8 %copy-start.4 = (s32[2048]{0:T(1024)S(1)}, s32[2048]{0:T(1024)}, u32[]{:S(2)}) copy-start(s32[2048]{0:T(1024)} %wanted.1) | copy-start | bytes 24580
  18.3 13.7 %collective-permute-start.3 = (bf16[512,256]{1,0:T(8,128)(2,1)S(1)}, bf16[512,256]{1,0:T(8,128)(2,1)S(1)}, u32[]{:S(2)}, u32[]{:S(2)}) collective-permute-start(bf16[512,256]{1,0:T(8,128)(2,1)S(1)} %get-tuple-element.27), channel_id=1, source_target_pairs={{0,1},{1,0},{2,3},{3,2},{4,5},{5,4},{6,7},{7,6},{8,9},{9,8},{10,11... | collective-permute-start | bytes 786440 | tf_op jit(solution)/shard_map/ppermute | solution.py:45
  18.9 14.3 %collective-permute-start.4 = (bf16[512,256]{1,0:T(8,128)(2,1)}, bf16[512,256]{1,0:T(8,128)(2,1)S(1)}, u32[]{:S(2)}, u32[]{:S(2)}) collective-permute-start(bf16[512,256]{1,0:T(8,128)(2,1)} %add_convert_fusion), channel_id=1, source_target_pairs={{0,3},{1,2},{2,1},{3,0},{4,7},{5,6},{6,5},{7,4},{8,11},{9,10},{10,... | collective-permute-start | bytes 786440 | tf_op jit(solution)/shard_map/ppermute | solution.py:45
  22.3 10.8 %collective-permute-start.5 = (bf16[512,256]{1,0:T(8,128)(2,1)S(1)}, bf16[512,256]{1,0:T(8,128)(2,1)S(1)}, u32[]{:S(2)}, u32[]{:S(2)}) collective-permute-start(bf16[512,256]{1,0:T(8,128)(2,1)S(1)} %get-tuple-element.29), channel_id=1, source_target_pairs={{0,4},{4,0},{1,5},{5,1},{2,6},{6,2},{3,7},{7,3},{8,12},{12,8},{9,1... | collective-permute-start | bytes 786440 | tf_op jit(solution)/shard_map/ppermute | solution.py:45
  30.0 3.2 %copy-start.1 = (s32[2048,1]{0,1:T(1,128)S(1)}, s32[2048,1]{0,1:T(1,128)}, u32[]{:S(2)}) copy-start(s32[2048,1]{0,1:T(1,128)} %param.10) | copy-start | bytes 24580
  30.0 3.2 %copy-start.2 = (f32[2048]{0:T(1024)S(1)}, f32[2048]{0:T(1024)}, u32[]{:S(2)}) copy-start(f32[2048]{0:T(1024)} %param.12) | copy-start | bytes 24580
  34.2 11.1 %collective-permute-start.6 = (bf16[512,256]{1,0:T(8,128)(2,1)S(1)}, bf16[512,256]{1,0:T(8,128)(2,1)S(1)}, u32[]{:S(2)}, u32[]{:S(2)}) collective-permute-start(bf16[512,256]{1,0:T(8,128)(2,1)S(1)} %pre_gradient.1.first), channel_id=1, source_target_pairs={{0,3},{1,2},{2,1},{3,0},{4,7},{5,6},{6,5},{7,4},{8,11},{9,10},{10,... | collective-permute-start | bytes 786440 | tf_op jit(solution)/shard_map/ppermute | solution.py:45
  34.7 13.4 %collective-permute-start.7 = (bf16[512,256]{1,0:T(8,128)(2,1)S(1)}, bf16[512,256]{1,0:T(8,128)(2,1)S(1)}, u32[]{:S(2)}, u32[]{:S(2)}) collective-permute-start(bf16[512,256]{1,0:T(8,128)(2,1)S(1)} %pre_gradient.1.first), channel_id=1, source_target_pairs={{0,1},{1,0},{2,3},{3,2},{4,5},{5,4},{6,7},{7,6},{8,9},{9,8},{10,11... | collective-permute-start | bytes 786440 | tf_op jit(solution)/shard_map/ppermute | solution.py:45
  45.3 6.5 %collective-permute-start.8 = (bf16[512,256]{1,0:T(8,128)(2,1)S(1)}, bf16[512,256]{1,0:T(8,128)(2,1)S(1)}, u32[]{:S(2)}, u32[]{:S(2)}) collective-permute-start(bf16[512,256]{1,0:T(8,128)(2,1)S(1)} %collective-permute-done.6.second), channel_id=1, source_target_pairs={{0,1},{1,0},{2,3},{3,2},{4,5},{5,4},{6,7},{7,6},{8,9},{9,8},{10,11... | collective-permute-start | bytes 786440 | tf_op jit(solution)/shard_map/ppermute | solution.py:45
  52.4 1.4 %collective-permute-start.9 = (bf16[288,256]{1,0:T(8,128)(2,1)S(1)}, bf16[288,256]{1,0:T(8,128)(2,1)S(1)}, u32[]{:S(2)}, u32[]{:S(2)}) collective-permute-start(bf16[288,256]{1,0:T(8,128)(2,1)S(1)} %get-tuple-element.34), channel_id=1, source_target_pairs={{0,8},{8,0},{16,24},{24,16},{1,9},{9,1},{17,25},{25,17},{2,10},{10... | collective-permute-start | bytes 442376 | tf_op jit(solution)/shard_map/ppermute | solution.py:45
  52.5 3.0 %collective-permute-start.12 = (bf16[288,256]{1,0:T(8,128)(2,1)S(1)}, bf16[288,256]{1,0:T(8,128)(2,1)S(1)}, u32[]{:S(2)}, u32[]{:S(2)}) collective-permute-start(bf16[288,256]{1,0:T(8,128)(2,1)S(1)} %get-tuple-element.36), channel_id=1, source_target_pairs={{0,8},{8,0},{16,24},{24,16},{1,9},{9,1},{17,25},{25,17},{2,10},{10... | collective-permute-start | bytes 442376 | tf_op jit(solution)/shard_map/ppermute | solution.py:45
  53.9 5.2 %collective-permute-start.10 = (bf16[288,256]{1,0:T(8,128)(2,1)S(1)}, bf16[288,256]{1,0:T(8,128)(2,1)S(1)}, u32[]{:S(2)}, u32[]{:S(2)}) collective-permute-start(bf16[288,256]{1,0:T(8,128)(2,1)S(1)} %added.6.first), channel_id=1, source_target_pairs={{0,16},{4,20},{8,12},{12,8},{16,0},{20,4},{24,28},{28,24},{1,17},{... | collective-permute-start | bytes 442376 | tf_op jit(solution)/shard_map/ppermute | solution.py:413
  55.5 5.2 %collective-permute-start.13 = (bf16[288,256]{1,0:T(8,128)(2,1)S(1)}, bf16[288,256]{1,0:T(8,128)(2,1)S(1)}, u32[]{:S(2)}, u32[]{:S(2)}) collective-permute-start(bf16[288,256]{1,0:T(8,128)(2,1)S(1)} %added.9.first), channel_id=1, source_target_pairs={{0,16},{4,20},{8,12},{12,8},{16,0},{20,4},{24,28},{28,24},{1,17},{... | collective-permute-start | bytes 442376 | tf_op jit(solution)/shard_map/ppermute | solution.py:413
  59.1 5.2 %collective-permute-start.11 = (bf16[288,256]{1,0:T(8,128)(2,1)S(1)}, bf16[288,256]{1,0:T(8,128)(2,1)S(1)}, u32[]{:S(2)}, u32[]{:S(2)}) collective-permute-start(bf16[288,256]{1,0:T(8,128)(2,1)S(1)} %added.7.first), channel_id=1, source_target_pairs={{0,4},{4,0},{8,24},{12,28},{16,20},{20,16},{24,8},{28,12},{1,5},{5... | collective-permute-start | bytes 442376 | tf_op jit(solution)/shard_map/ppermute | solution.py:413
  60.8 5.2 %collective-permute-start.14 = (bf16[288,256]{1,0:T(8,128)(2,1)S(1)}, bf16[288,256]{1,0:T(8,128)(2,1)S(1)}, u32[]{:S(2)}, u32[]{:S(2)}) collective-permute-start(bf16[288,256]{1,0:T(8,128)(2,1)S(1)} %added.10.first), channel_id=1, source_target_pairs={{0,4},{4,0},{8,24},{12,28},{16,20},{20,16},{24,8},{28,12},{1,5},{5... | collective-permute-start | bytes 442376 | tf_op jit(solution)/shard_map/ppermute | solution.py:413
  64.4 1.7 %collective-permute-start.15 = (bf16[288,256]{1,0:T(8,128)(2,1)S(1)}, bf16[288,256]{1,0:T(8,128)(2,1)S(1)}, u32[]{:S(2)}, u32[]{:S(2)}) collective-permute-start(bf16[288,256]{1,0:T(8,128)(2,1)S(1)} %added.8.refs_0_), channel_id=1, source_target_pairs={{0,8},{8,0},{16,24},{24,16},{1,9},{9,1},{17,25},{25,17},{2,10},{10... | collective-permute-start | bytes 442376 | tf_op jit(solution)/shard_map/ppermute | solution.py:45
  66.0 1.4 %collective-permute-start.16 = (bf16[288,256]{1,0:T(8,128)(2,1)S(1)}, bf16[288,256]{1,0:T(8,128)(2,1)S(1)}, u32[]{:S(2)}, u32[]{:S(2)}) collective-permute-start(bf16[288,256]{1,0:T(8,128)(2,1)S(1)} %added.11.refs_1_), channel_id=1, source_target_pairs={{0,8},{8,0},{16,24},{24,16},{1,9},{9,1},{17,25},{25,17},{2,10},{10... | collective-permute-start | bytes 442376 | tf_op jit(solution)/shard_map/ppermute | solution.py:45

commit v16 on v14

--- a/solution.py
+++ b/solution.py
@@ -218,9 +218,9 @@
 def pixel_kernel(count, bits, where, places, wanted, cotangent, above, below, mixing, weight,
                  spectra, out, *refs):
     quarters, refs = refs[: len(bits)], refs[len(bits) :]
-    table, scale, sums, near, names, held, sems = refs
+    table, scale, sums, near, names, held, tile, sems = refs
     start, chan = where[0], where[1]
-    tile_rows, half = cotangent.shape[0], table.shape[1]
+    tile_rows, half = tile.shape[0], table.shape[1]
     listed = names.shape[0]
     first_name = pl.multiple_of(start // listed * listed, listed)
     copies = [
@@ -228,7 +228,16 @@
         pltpu.make_async_copy(wanted.at[pl.ds(first_name, listed)], names, sems.at[len(bits) + 1]),
     ]
     parts = quarter_copies(spectra, held, sems, chan, bits)
-    for copy in copies + parts:
+    chunk = tile_rows // 4
+    rows = [
+        pltpu.make_async_copy(
+            cotangent.at[pl.ds(n * chunk, chunk)],
+            tile.at[pl.ds(n * chunk, chunk)],
+            sems.at[len(bits) + 2 + n],
+        )
+        for n in range(4)
+    ]
+    for copy in copies + rows + parts:
         copy.start()
 
     def fill(first, values):
@@ -243,8 +252,10 @@
     scales = [scale[2 * k : 2 * k + 2, :] for k in range(NEIGH)]
     fill(0, above[...])
     fill(HALO + tile_rows, below[...])
-    for first in range(0, tile_rows, 256):
-        fill(HALO + first, cotangent[first : first + 256, :])
+    for n in range(4):
+        rows[n].wait()
+        for first in range(n * chunk, (n + 1) * chunk, 256):
+            fill(HALO + first, tile[first : first + 256, :])
     project_rows(parts, held, weight, quarters)
     for copy in copies:
         copy.wait()
@@ -284,6 +295,7 @@
     depth, rows = spectra.shape[1], spectra.shape[0] // 4
     listed = min(wanted.shape[0], 1024)
     anywhere = pl.BlockSpec(memory_space=pl.ANY)
+    hbm = pl.BlockSpec(memory_space=pltpu.HBM)
     vmem = pl.BlockSpec(memory_space=pltpu.VMEM)
     return pl.pallas_call(
         functools.partial(pixel_kernel, count, bits),
@@ -295,8 +307,9 @@
             pl.BlockSpec(memory_space=pltpu.SMEM),
             anywhere,
             anywhere,
-            *[vmem] * 5,
-            pl.BlockSpec(memory_space=pltpu.HBM),
+            hbm,
+            *[vmem] * 4,
+            hbm,
         ],
         out_specs=(vmem,) * (1 + len(bits)),
         scratch_shapes=[
@@ -306,9 +319,10 @@
             pltpu.SMEM(places.shape, jnp.int32),
             pltpu.SMEM((listed,), jnp.int32),
             pltpu.VMEM((max(len(bits), 1) * rows, depth), jnp.bfloat16),
-            pltpu.SemaphoreType.DMA((len(bits) + 2,)),
+            pltpu.VMEM(cotangent.shape, cotangent.dtype),
+            pltpu.SemaphoreType.DMA((len(bits) + 6,)),
         ],
-        compiler_params=memory(48),
+        compiler_params=memory(LARGE),
         cost_estimate=pl.CostEstimate(
             flops=8 * NEIGH * count * 2048 * width,
             bytes_accessed=4 * tile_rows * width,

time: 68.8 us -> 67.8 us (0.985)
  other arithmetic: 2.86 us -> 1.21 us
    convert_element_type x1, other arithmetic: 1.72 us -> 0.07 us  [shards(): (shared.astype(jnp.float32) + near_first.astype(jnp.float32)).astype(jnp....]
    pallas_call x2, Pallas kernels: 13.4 us -> 14.1 us  [pixel_rows(): pl.pallas_call(functools.partial(pixel_kernel, count, bits), out_shape=(j...]
  transfers between devices with their start and end apart: 17 -> 17, of which waited for: 9 -> 9; matrix products, arithmetic and copies ran while one was open for 2% -> 2% of each run, Pallas kernels for 31% -> 33%
where the time goes in v16:
time: 67.8 us; the launch traced here: 67.6 us
  Pallas kernels  24.7 us (36%)
  waiting for transfers between devices  22.5 us (33%)
  starting transfers between devices  18.8 us (28%)
  other arithmetic  1.21 us (2%)
    ppermute x12, waiting for transfers between devices, swap(): return lax.ppermute(value, axis, [(i, i ^ bit) for i in range(size)])  16 us
    pallas_call x2, Pallas kernels, pixel_rows(): pl.pallas_call(functools.partial(pixel_kernel, count, bits), out_shape=(j...  14.1 us
    ppermute x12, starting transfers between devices, swap(): return lax.ppermute(value, axis, [(i, i ^ bit) for i in range(size)])  13.4 us
    ppermute x4, waiting for transfers between devices, sum_over_panels(): parts = [added(part, lax.ppermute(part, both, perm)) for part in parts]  6.56 us
    ppermute x4, starting transfers between devices, sum_over_panels(): parts = [added(part, lax.ppermute(part, both, perm)) for part in parts]  5.28 us
    pallas_call x2, Pallas kernels, project(): pl.pallas_call(functools.partial(project_kernel, bits), out_shape=(jax.Sh...  4.67 us
    pallas_call x1, Pallas kernels, early_product(): pl.pallas_call(early_kernel, out_shape=(jax.ShapeDtypeStruct((depth, widt...  2.49 us
  transfers between devices with their start and end apart: 17, of which 9 were waited for; matrix products, arithmetic and copies ran while one was open for 2% of the time, Pallas kernels for 33%

profile of v16, /device:TPU:0, one launch (start us, length us, event | category | flops | bytes accessed | tf_op | source)
XLA Modules:
  0.0 67.6 jit_solution(5502463309495975284)
XLA Ops:
  0.0 3.0 %collective-permute-start = (s32[2048]{0:T(1024)}, s32[2048]{0:T(1024)S(1)}, u32[]{:S(2)}, u32[]{:S(2)}) collective-permute-start(s32[2048]{0:T(1024)} %wanted.1), channel_id=1, source_target_pairs={{0,4},{4,0},{1,5},{5,1},{2,6},{6,2},{3,7},{7,3},{8,12},{12,8},{9,1... | collective-permute-start | bytes 24584 | tf_op jit(solution)/shard_map/ppermute | solution.py:45
  3.0 0.9 %slice_select_fusion = bf16[128,256]{1,0:T(8,128)(2,1)S(1)} fusion(bf16[4096,256]{1,0:T(8,128)(2,1)} %cotangent.3, pred[]{:T(512)S(6)} %eq.3), kind=kLoop, calls=%fused_computation.5 | loop fusion | flops 32768 | bytes 196609 | tf_op jit(solution)/shard_map/jit(_where)/select_n | solution.py:22
  4.0 2.7 %project.2 = bf16[512,256]{1,0:T(8,128)(2,1)} custom-call(s32[1]{0:T(128)} %bitcast.1.chan, bf16[2048,1152]{1,0:T(8,128)(2,1)} %spectra.9, bf16[1152,256]{1,0:T(8,128)(2,1)} %weight.7), custom_call_target="tpu_custom_call" | custom-call | flops 301989888 | bytes 2031616 | tf_op jit(solution)/shard_map/project/pallas_call | solution.py:90
  6.7 2.1 %collective-permute-start.2 = (bf16[512,256]{1,0:T(8,128)(2,1)}, bf16[512,256]{1,0:T(8,128)(2,1)S(1)}, u32[]{:S(2)}, u32[]{:S(2)}) collective-permute-start(bf16[512,256]{1,0:T(8,128)(2,1)} %project.2), channel_id=1, source_target_pairs={{0,1},{1,0},{2,3},{3,2},{4,5},{5,4},{6,7},{7,6},{8,9},{9,8},{10,11... | collective-permute-start | bytes 786440 | tf_op jit(solution)/shard_map/ppermute | solution.py:45
  9.1 8.0 %pixel_rows.2 = (bf16[512,256]{1,0:T(8,128)(2,1)S(1)}, bf16[512,256]{1,0:T(8,128)(2,1)S(1)}, bf16[512,256]{1,0:T(8,128)(2,1)S(1)}) custom-call(s32[2]{0:T(128)S(1)} %pad_add_fusion.1.where, s32[16384]{0:T(1024)S(1)} %bitcast.11, s32[2048]{0:T(1024)S(1)} %collective-permute-done.wanted, bf16[4096,256]{1,0:T(8,128)(2,1)} %cotangent.3, ...), custom_call_target="tpu_custom_call" | custom-call | flops 17179869184 | bytes 4194304 | tf_op jit(solution)/shard_map/pixel_rows/pallas_call | solution.py:300
  17.2 0.8 %collective-permute-start.3 = (bf16[512,256]{1,0:T(8,128)(2,1)S(1)}, bf16[512,256]{1,0:T(8,128)(2,1)S(1)}, u32[]{:S(2)}, u32[]{:S(2)}) collective-permute-start(bf16[512,256]{1,0:T(8,128)(2,1)S(1)} %get-tuple-element.27), channel_id=1, source_target_pairs={{0,1},{1,0},{2,3},{3,2},{4,5},{5,4},{6,7},{7,6},{8,9},{9,8},{10,11... | collective-permute-start | bytes 786440 | tf_op jit(solution)/shard_map/ppermute | solution.py:45
  18.0 3.4 %collective-permute-start.4 = (bf16[512,256]{1,0:T(8,128)(2,1)S(1)}, bf16[512,256]{1,0:T(8,128)(2,1)S(1)}, u32[]{:S(2)}, u32[]{:S(2)}) collective-permute-start(bf16[512,256]{1,0:T(8,128)(2,1)S(1)} %add_convert_fusion), channel_id=1, source_target_pairs={{0,3},{1,2},{2,1},{3,0},{4,7},{5,6},{6,5},{7,4},{8,11},{9,10},{10,... | collective-permute-start | bytes 786440 | tf_op jit(solution)/shard_map/ppermute | solution.py:45
  21.3 1.5 %collective-permute-start.5 = (bf16[512,256]{1,0:T(8,128)(2,1)S(1)}, bf16[512,256]{1,0:T(8,128)(2,1)S(1)}, u32[]{:S(2)}, u32[]{:S(2)}) collective-permute-start(bf16[512,256]{1,0:T(8,128)(2,1)S(1)} %get-tuple-element.29), channel_id=1, source_target_pairs={{0,4},{4,0},{1,5},{5,1},{2,6},{6,2},{3,7},{7,3},{8,12},{12,8},{9,1... | collective-permute-start | bytes 786440 | tf_op jit(solution)/shard_map/ppermute | solution.py:45
  22.9 6.1 %pixel_rows.3.mine = bf16[512,256]{1,0:T(8,128)(2,1)S(1)} custom-call(s32[2]{0:T(128)S(1)} %pad_add_fusion.2.where, s32[16384]{0:T(1024)S(1)} %bitcast.12, s32[2048]{0:T(1024)S(1)} %copy-done.3, bf16[4096,256]{1,0:T(8,128)(2,1)} %cotangent.3, bf16[128,256]{1,0:T(8,128)(2,1)S(1)} %collective-permute-done.1.above.below, ...), custom_call_target="tpu_custom_call" | custom-call | flops 17179869184 | bytes 4194304 | tf_op jit(solution)/shard_map/pixel_rows/pallas_call | solution.py:300
  29.1 1.9 %project.3.keep = bf16[512,256]{1,0:T(8,128)(2,1)S(1)} custom-call(s32[1]{0:T(128)} %bitcast.4.chan, bf16[2048,1152]{1,0:T(8,128)(2,1)} %spectra.9, bf16[1152,256]{1,0:T(8,128)(2,1)S(1)} %copy-done), custom_call_target="tpu_custom_call" | custom-call | flops 301989888 | bytes 2031616 | tf_op jit(solution)/shard_map/project/pallas_call | solution.py:90
  31.0 1.2 %collective-permute-done.4.far = bf16[512,256]{1,0:T(8,128)(2,1)S(1)} collective-permute-done((bf16[512,256]{1,0:T(8,128)(2,1)S(1)}, bf16[512,256]{1,0:T(8,128)(2,1)S(1)}, u32[]{:S(2)}, u32[]{:S(2)}) %collective-permute-start.4) | collective-permute-done | bytes 262176 | tf_op jit(solution)/shard_map/ppermute | solution.py:45
  32.2 1.0 %pre_gradient.1.first = bf16[512,256]{1,0:T(8,128)(2,1)S(1)} custom-call(s32[2]{0:T(128)S(1)} %pad_add_fusion.where, bf16[512,256]{1,0:T(8,128)(2,1)S(1)} %project.3.keep, bf16[512,256]{1,0:T(8,128)(2,1)S(1)} %collective-permute-done.3.near, bf16[512,256]{1,0:T(8,128)(2,1)S(1)} %collective-permute-done.4.far, s32[16,128]{1,0:T(8,128)S(1)} %bitcast.13, ...), custom_call_target="tpu_custom_call" | custom-call | tf_op jit(solution)/shard_map/pre_gradient/pallas_call | solution.py:372
  33.2 0.5 collective-permute-start.6
  33.7 1.3 %collective-permute-start.7 = (bf16[512,256]{1,0:T(8,128)(2,1)S(1)}, bf16[512,256]{1,0:T(8,128)(2,1)S(1)}, u32[]{:S(2)}, u32[]{:S(2)}) collective-permute-start(bf16[512,256]{1,0:T(8,128)(2,1)S(1)} %pre_gradient.1.first), channel_id=1, source_target_pairs={{0,1},{1,0},{2,3},{3,2},{4,5},{5,4},{6,7},{7,6},{8,9},{9,8},{10,11... | collective-permute-start | bytes 786440 | tf_op jit(solution)/shard_map/ppermute | solution.py:45
  35.0 9.3 %collective-permute-done.6.second = bf16[512,256]{1,0:T(8,128)(2,1)S(1)} collective-permute-done((bf16[512,256]{1,0:T(8,128)(2,1)S(1)}, bf16[512,256]{1,0:T(8,128)(2,1)S(1)}, u32[]{:S(2)}, u32[]{:S(2)}) %collective-permute-start.6) | collective-permute-done | bytes 262176 | tf_op jit(solution)/shard_map/ppermute | solution.py:45
  44.3 0.2 collective-permute-start.8
  44.5 2.5 %early_product.1 = (f32[1152,256]{1,0:T(8,128)S(1)}, bf16[512,1152]{1,0:T(8,128)(2,1)S(1)}, bf16[512,1152]{1,0:T(8,128)(2,1)S(1)}) custom-call(s32[1]{0:T(128)} %bitcast.1.chan, bf16[2048,1152]{1,0:T(8,128)(2,1)} %spectra.9, bf16[512,256]{1,0:T(8,128)(2,1)S(1)} %pre_gradient.1.first, bf16[512,256]{1,0:T(8,128)(2,1)S(1)} %collective-permute-done.6.second), custom_call_target="tpu_custom_call" | custom-call | flops 603979776 | bytes 5898240 | tf_op jit(solution)/shard_map/early_product/pallas_call | solution.py:137
  47.0 0.1 collective-permute-done.7.rows
  47.2 0.5 more_product.1.before
  47.7 3.2 %collective-permute-done.8.rows = bf16[512,256]{1,0:T(8,128)(2,1)S(1)} collective-permute-done((bf16[512,256]{1,0:T(8,128)(2,1)S(1)}, bf16[512,256]{1,0:T(8,128)(2,1)S(1)}, u32[]{:S(2)}, u32[]{:S(2)}) %collective-permute-start.8) | collective-permute-done | bytes 262176 | tf_op jit(solution)/shard_map/ppermute | solution.py:45
  50.8 0.6 late_product.1
  51.5 0.5 collective-permute-start.12
  52.0 0.9 %collective-permute-done.9.second = bf16[288,256]{1,0:T(8,128)(2,1)S(1)} collective-permute-done((bf16[288,256]{1,0:T(8,128)(2,1)S(1)}, bf16[288,256]{1,0:T(8,128)(2,1)S(1)}, u32[]{:S(2)}, u32[]{:S(2)}) %collective-permute-start.9) | collective-permute-done | bytes 147488 | tf_op jit(solution)/shard_map/ppermute | solution.py:45
  52.9 1.6 %collective-permute-start.10 = (bf16[288,256]{1,0:T(8,128)(2,1)S(1)}, bf16[288,256]{1,0:T(8,128)(2,1)S(1)}, u32[]{:S(2)}, u32[]{:S(2)}) collective-permute-start(bf16[288,256]{1,0:T(8,128)(2,1)S(1)} %added.6.first), channel_id=1, source_target_pairs={{0,16},{4,20},{8,12},{12,8},{16,0},{20,4},{24,28},{28,24},{1,17},{... | collective-permute-start | bytes 442376 | tf_op jit(solution)/shard_map/ppermute | solution.py:427
  54.5 0.6 collective-permute-start.13
  55.1 3.0 %collective-permute-done.10.second = bf16[288,256]{1,0:T(8,128)(2,1)S(1)} collective-permute-done((bf16[288,256]{1,0:T(8,128)(2,1)S(1)}, bf16[288,256]{1,0:T(8,128)(2,1)S(1)}, u32[]{:S(2)}, u32[]{:S(2)}) %collective-permute-start.10) | collective-permute-done | bytes 147488 | tf_op jit(solution)/shard_map/ppermute | solution.py:427
  58.2 1.6 %collective-permute-start.11 = (bf16[288,256]{1,0:T(8,128)(2,1)S(1)}, bf16[288,256]{1,0:T(8,128)(2,1)S(1)}, u32[]{:S(2)}, u32[]{:S(2)}) collective-permute-start(bf16[288,256]{1,0:T(8,128)(2,1)S(1)} %added.7.first), channel_id=1, source_target_pairs={{0,4},{4,0},{8,24},{12,28},{16,20},{20,16},{24,8},{28,12},{1,5},{5... | collective-permute-start | bytes 442376 | tf_op jit(solution)/shard_map/ppermute | solution.py:427
  59.8 1.5 %collective-permute-start.14 = (bf16[288,256]{1,0:T(8,128)(2,1)S(1)}, bf16[288,256]{1,0:T(8,128)(2,1)S(1)}, u32[]{:S(2)}, u32[]{:S(2)}) collective-permute-start(bf16[288,256]{1,0:T(8,128)(2,1)S(1)} %added.10.first), channel_id=1, source_target_pairs={{0,4},{4,0},{8,24},{12,28},{16,20},{20,16},{24,8},{28,12},{1,5},{5... | collective-permute-start | bytes 442376 | tf_op jit(solution)/shard_map/ppermute | solution.py:427
  61.3 2.0 %collective-permute-done.11.second = bf16[288,256]{1,0:T(8,128)(2,1)S(1)} collective-permute-done((bf16[288,256]{1,0:T(8,128)(2,1)S(1)}, bf16[288,256]{1,0:T(8,128)(2,1)S(1)}, u32[]{:S(2)}, u32[]{:S(2)}) %collective-permute-start.11) | collective-permute-done | bytes 147488 | tf_op jit(solution)/shard_map/ppermute | solution.py:427
  63.5 1.5 %collective-permute-done.14.second = bf16[288,256]{1,0:T(8,128)(2,1)S(1)} collective-permute-done((bf16[288,256]{1,0:T(8,128)(2,1)S(1)}, bf16[288,256]{1,0:T(8,128)(2,1)S(1)}, u32[]{:S(2)}, u32[]{:S(2)}) %collective-permute-start.14) | collective-permute-done | bytes 147488 | tf_op jit(solution)/shard_map/ppermute | solution.py:427
  65.1 1.3 %collective-permute-done.16.refs_3_ = bf16[288,256]{1,0:T(8,128)(2,1)S(1)} collective-permute-done((bf16[288,256]{1,0:T(8,128)(2,1)S(1)}, bf16[288,256]{1,0:T(8,128)(2,1)S(1)}, u32[]{:S(2)}, u32[]{:S(2)}) %collective-permute-start.16) | collective-permute-done | bytes 147488 | tf_op jit(solution)/shard_map/ppermute | solution.py:45
  66.5 1.1 %collect.1 = f32[1152,256]{1,0:T(8,128)} custom-call(s32[1]{0:T(128)} %bitcast.core, bf16[288,256]{1,0:T(8,128)(2,1)S(1)} %added.8.refs_0_, bf16[288,256]{1,0:T(8,128)(2,1)S(1)} %added.11.refs_1_, bf16[288,256]{1,0:T(8,128)(2,1)S(1)} %collective-permute-done.15.refs_2_, bf16[288,256]{1,0:T(8,128)(2,1)S(1)} %collective-permute-done.16.refs_3_), custom_call_target="tpu_custom_call" | custom-call | tf_op jit(solution)/shard_map/collect/pallas_call | solution.py:396
  (37 shorter events, 0.9 us)
Async XLA Ops:
  0.0 9.0 %collective-permute-start = (s32[2048]{0:T(1024)}, s32[2048]{0:T(1024)S(1)}, u32[]{:S(2)}, u32[]{:S(2)}) collective-permute-start(s32[2048]{0:T(1024)} %wanted.1), channel_id=1, source_target_pairs={{0,4},{4,0},{1,5},{5,1},{2,6},{6,2},{3,7},{7,3},{8,12},{12,8},{9,1... | collective-permute-start | bytes 24584 | tf_op jit(solution)/shard_map/ppermute | solution.py:45
  3.9 5.2 %collective-permute-start.1 = (bf16[128,256]{1,0:T(8,128)(2,1)S(1)}, bf16[128,256]{1,0:T(8,128)(2,1)S(1)}, u32[]{:S(2)}, u32[]{:S(2)}) collective-permute-start(bf16[128,256]{1,0:T(8,128)(2,1)S(1)} %slice_select_fusion), channel_id=1, source_target_pairs={{0,4},{4,0},{1,5},{5,1},{2,6},{6,2},{3,7},{7,3},{8,12},{12,8},{9,1... | collective-permute-start | bytes 196616 | tf_op jit(solution)/shard_map/ppermute | solution.py:22
  3.9 5.0 %copy-start.5 = (s32[8,4096]{1,0:T(8,128)S(1)}, s32[8,4096]{1,0:T(8,128)}, u32[]{:S(2)}) copy-start(s32[8,4096]{1,0:T(8,128)} %param.14) | copy-start | bytes 393220
  3.9 5.1 %copy-start = (bf16[1152,256]{1,0:T(8,128)(2,1)S(1)}, bf16[1152,256]{1,0:T(8,128)(2,1)}, u32[]{:S(2)}) copy-start(bf16[1152,256]{1,0:T(8,128)(2,1)} %weight.7) | copy-start | bytes 1769476
  4.0 5.1 %copy-start.4 = (f32[8,256]{1,0:T(8,128)S(1)}, f32[8,256]{1,0:T(8,128)}, u32[]{:S(2)}) copy-start(f32[8,256]{1,0:T(8,128)} %mixing.3) | copy-start | bytes 24580
  6.7 10.4 %collective-permute-start.2 = (bf16[512,256]{1,0:T(8,128)(2,1)}, bf16[512,256]{1,0:T(8,128)(2,1)S(1)}, u32[]{:S(2)}, u32[]{:S(2)}) collective-permute-start(bf16[512,256]{1,0:T(8,128)(2,1)} %project.2), channel_id=1, source_target_pairs={{0,1},{1,0},{2,3},{3,2},{4,5},{5,4},{6,7},{7,6},{8,9},{9,8},{10,11... | collective-permute-start | bytes 786440 | tf_op jit(solution)/shard_map/ppermute | solution.py:45
  9.1 13.9 %copy-start.3 = (s32[2048]{0:T(1024)S(1)}, s32[2048]{0:T(1024)}, u32[]{:S(2)}) copy-start(s32[2048]{0:T(1024)} %wanted.1) | copy-start | bytes 24580
  17.2 13.8 %collective-permute-start.3 = (bf16[512,256]{1,0:T(8,128)(2,1)S(1)}, bf16[512,256]{1,0:T(8,128)(2,1)S(1)}, u32[]{:S(2)}, u32[]{:S(2)}) collective-permute-start(bf16[512,256]{1,0:T(8,128)(2,1)S(1)} %get-tuple-element.27), channel_id=1, source_target_pairs={{0,1},{1,0},{2,3},{3,2},{4,5},{5,4},{6,7},{7,6},{8,9},{9,8},{10,11... | collective-permute-start | bytes 786440 | tf_op jit(solution)/shard_map/ppermute | solution.py:45
  18.0 14.2 %collective-permute-start.4 = (bf16[512,256]{1,0:T(8,128)(2,1)S(1)}, bf16[512,256]{1,0:T(8,128)(2,1)S(1)}, u32[]{:S(2)}, u32[]{:S(2)}) collective-permute-start(bf16[512,256]{1,0:T(8,128)(2,1)S(1)} %add_convert_fusion), channel_id=1, source_target_pairs={{0,3},{1,2},{2,1},{3,0},{4,7},{5,6},{6,5},{7,4},{8,11},{9,10},{10,... | collective-permute-start | bytes 786440 | tf_op jit(solution)/shard_map/ppermute | solution.py:45
  21.3 10.8 %collective-permute-start.5 = (bf16[512,256]{1,0:T(8,128)(2,1)S(1)}, bf16[512,256]{1,0:T(8,128)(2,1)S(1)}, u32[]{:S(2)}, u32[]{:S(2)}) collective-permute-start(bf16[512,256]{1,0:T(8,128)(2,1)S(1)} %get-tuple-element.29), channel_id=1, source_target_pairs={{0,4},{4,0},{1,5},{5,1},{2,6},{6,2},{3,7},{7,3},{8,12},{12,8},{9,1... | collective-permute-start | bytes 786440 | tf_op jit(solution)/shard_map/ppermute | solution.py:45
  29.0 3.1 %copy-start.1 = (s32[2048,1]{0,1:T(1,128)S(1)}, s32[2048,1]{0,1:T(1,128)}, u32[]{:S(2)}) copy-start(s32[2048,1]{0,1:T(1,128)} %param.10) | copy-start | bytes 24580
  29.0 3.1 %copy-start.2 = (f32[2048]{0:T(1024)S(1)}, f32[2048]{0:T(1024)}, u32[]{:S(2)}) copy-start(f32[2048]{0:T(1024)} %param.12) | copy-start | bytes 24580
  33.2 11.1 %collective-permute-start.6 = (bf16[512,256]{1,0:T(8,128)(2,1)S(1)}, bf16[512,256]{1,0:T(8,128)(2,1)S(1)}, u32[]{:S(2)}, u32[]{:S(2)}) collective-permute-start(bf16[512,256]{1,0:T(8,128)(2,1)S(1)} %pre_gradient.1.first), channel_id=1, source_target_pairs={{0,3},{1,2},{2,1},{3,0},{4,7},{5,6},{6,5},{7,4},{8,11},{9,10},{10,... | collective-permute-start | bytes 786440 | tf_op jit(solution)/shard_map/ppermute | solution.py:45
  33.7 13.5 %collective-permute-start.7 = (bf16[512,256]{1,0:T(8,128)(2,1)S(1)}, bf16[512,256]{1,0:T(8,128)(2,1)S(1)}, u32[]{:S(2)}, u32[]{:S(2)}) collective-permute-start(bf16[512,256]{1,0:T(8,128)(2,1)S(1)} %pre_gradient.1.first), channel_id=1, source_target_pairs={{0,1},{1,0},{2,3},{3,2},{4,5},{5,4},{6,7},{7,6},{8,9},{9,8},{10,11... | collective-permute-start | bytes 786440 | tf_op jit(solution)/shard_map/ppermute | solution.py:45
  44.3 6.5 %collective-permute-start.8 = (bf16[512,256]{1,0:T(8,128)(2,1)S(1)}, bf16[512,256]{1,0:T(8,128)(2,1)S(1)}, u32[]{:S(2)}, u32[]{:S(2)}) collective-permute-start(bf16[512,256]{1,0:T(8,128)(2,1)S(1)} %collective-permute-done.6.second), channel_id=1, source_target_pairs={{0,1},{1,0},{2,3},{3,2},{4,5},{5,4},{6,7},{7,6},{8,9},{9,8},{10,11... | collective-permute-start | bytes 786440 | tf_op jit(solution)/shard_map/ppermute | solution.py:45
  51.4 1.4 %collective-permute-start.9 = (bf16[288,256]{1,0:T(8,128)(2,1)S(1)}, bf16[288,256]{1,0:T(8,128)(2,1)S(1)}, u32[]{:S(2)}, u32[]{:S(2)}) collective-permute-start(bf16[288,256]{1,0:T(8,128)(2,1)S(1)} %get-tuple-element.34), channel_id=1, source_target_pairs={{0,8},{8,0},{16,24},{24,16},{1,9},{9,1},{17,25},{25,17},{2,10},{10... | collective-permute-start | bytes 442376 | tf_op jit(solution)/shard_map/ppermute | solution.py:45
  51.5 2.9 %collective-permute-start.12 = (bf16[288,256]{1,0:T(8,128)(2,1)S(1)}, bf16[288,256]{1,0:T(8,128)(2,1)S(1)}, u32[]{:S(2)}, u32[]{:S(2)}) collective-permute-start(bf16[288,256]{1,0:T(8,128)(2,1)S(1)} %get-tuple-element.36), channel_id=1, source_target_pairs={{0,8},{8,0},{16,24},{24,16},{1,9},{9,1},{17,25},{25,17},{2,10},{10... | collective-permute-start | bytes 442376 | tf_op jit(solution)/shard_map/ppermute | solution.py:45
  52.9 5.2 %collective-permute-start.10 = (bf16[288,256]{1,0:T(8,128)(2,1)S(1)}, bf16[288,256]{1,0:T(8,128)(2,1)S(1)}, u32[]{:S(2)}, u32[]{:S(2)}) collective-permute-start(bf16[288,256]{1,0:T(8,128)(2,1)S(1)} %added.6.first), channel_id=1, source_target_pairs={{0,16},{4,20},{8,12},{12,8},{16,0},{20,4},{24,28},{28,24},{1,17},{... | collective-permute-start | bytes 442376 | tf_op jit(solution)/shard_map/ppermute | solution.py:427
  54.5 5.2 %collective-permute-start.13 = (bf16[288,256]{1,0:T(8,128)(2,1)S(1)}, bf16[288,256]{1,0:T(8,128)(2,1)S(1)}, u32[]{:S(2)}, u32[]{:S(2)}) collective-permute-start(bf16[288,256]{1,0:T(8,128)(2,1)S(1)} %added.9.first), channel_id=1, source_target_pairs={{0,16},{4,20},{8,12},{12,8},{16,0},{20,4},{24,28},{28,24},{1,17},{... | collective-permute-start | bytes 442376 | tf_op jit(solution)/shard_map/ppermute | solution.py:427
  58.2 5.2 %collective-permute-start.11 = (bf16[288,256]{1,0:T(8,128)(2,1)S(1)}, bf16[288,256]{1,0:T(8,128)(2,1)S(1)}, u32[]{:S(2)}, u32[]{:S(2)}) collective-permute-start(bf16[288,256]{1,0:T(8,128)(2,1)S(1)} %added.7.first), channel_id=1, source_target_pairs={{0,4},{4,0},{8,24},{12,28},{16,20},{20,16},{24,8},{28,12},{1,5},{5... | collective-permute-start | bytes 442376 | tf_op jit(solution)/shard_map/ppermute | solution.py:427
  59.8 5.2 %collective-permute-start.14 = (bf16[288,256]{1,0:T(8,128)(2,1)S(1)}, bf16[288,256]{1,0:T(8,128)(2,1)S(1)}, u32[]{:S(2)}, u32[]{:S(2)}) collective-permute-start(bf16[288,256]{1,0:T(8,128)(2,1)S(1)} %added.10.first), channel_id=1, source_target_pairs={{0,4},{4,0},{8,24},{12,28},{16,20},{20,16},{24,8},{28,12},{1,5},{5... | collective-permute-start | bytes 442376 | tf_op jit(solution)/shard_map/ppermute | solution.py:427
  63.4 1.7 %collective-permute-start.15 = (bf16[288,256]{1,0:T(8,128)(2,1)S(1)}, bf16[288,256]{1,0:T(8,128)(2,1)S(1)}, u32[]{:S(2)}, u32[]{:S(2)}) collective-permute-start(bf16[288,256]{1,0:T(8,128)(2,1)S(1)} %added.8.refs_0_), channel_id=1, source_target_pairs={{0,8},{8,0},{16,24},{24,16},{1,9},{9,1},{17,25},{25,17},{2,10},{10... | collective-permute-start | bytes 442376 | tf_op jit(solution)/shard_map/ppermute | solution.py:45
  65.0 1.4 %collective-permute-start.16 = (bf16[288,256]{1,0:T(8,128)(2,1)S(1)}, bf16[288,256]{1,0:T(8,128)(2,1)S(1)}, u32[]{:S(2)}, u32[]{:S(2)}) collective-permute-start(bf16[288,256]{1,0:T(8,128)(2,1)S(1)} %added.11.refs_1_), channel_id=1, source_target_pairs={{0,8},{8,0},{16,24},{24,16},{1,9},{9,1},{17,25},{25,17},{2,10},{10... | collective-permute-start | bytes 442376 | tf_op jit(solution)/shard_map/ppermute | solution.py:45

commit v17 on v16

--- a/solution.py
+++ b/solution.py
@@ -61,16 +61,12 @@
     ]
 
 
-def project_rows(copies, held, weight, outs):
-    rows = outs[0].shape[0] if outs else 0
-    for turn, (copy, out) in enumerate(zip(copies, outs)):
-        copy.wait()
-        result = jnp.dot(
-            held[turn * rows : (turn + 1) * rows, :],
-            weight[...],
-            preferred_element_type=jnp.float32,
-        )
-        out[...] = result.astype(out.dtype)
+def project_rows(held, weight, turn, out):
+    rows = out.shape[0]
+    result = jnp.dot(
+        held[turn * rows : (turn + 1) * rows, :], weight[...], preferred_element_type=jnp.float32
+    )
+    out[...] = result.astype(out.dtype)
 
 
 def project_kernel(bits, chan, spectra, weight, *refs):
@@ -80,7 +76,9 @@
     for copy in copies:
         copy.start()
     copies[0].wait()
-    project_rows(copies[1:], held, near, outs)
+    for turn, out in enumerate(outs):
+        copies[turn + 1].wait()
+        project_rows(held, near, turn, out)
 
 
 def project(spectra, weight, chan, bits, grant):
@@ -237,7 +235,8 @@
         )
         for n in range(4)
     ]
-    for copy in copies + rows + parts:
+    order = copies + rows[:2] + parts[:1] + rows[2:] + parts[1:]
+    for copy in order:
         copy.start()
 
     def fill(first, values):
@@ -252,11 +251,15 @@
     scales = [scale[2 * k : 2 * k + 2, :] for k in range(NEIGH)]
     fill(0, above[...])
     fill(HALO + tile_rows, below[...])
-    for n in range(4):
-        rows[n].wait()
-        for first in range(n * chunk, (n + 1) * chunk, 256):
+    for n in range(2):
+        rows[2 * n].wait()
+        rows[2 * n + 1].wait()
+        if n < len(parts):
+            parts[n].wait()
+        for first in range(2 * n * chunk, 2 * (n + 1) * chunk, 256):
             fill(HALO + first, tile[first : first + 256, :])
-    project_rows(parts, held, weight, quarters)
+        if n < len(parts):
+            project_rows(held, weight, n, quarters[n])
     for copy in copies:
         copy.wait()
 
@@ -419,6 +422,22 @@
     )(first, second)
 
 
+def hand_on_kernel(value, _, out):
+    out[...] = value[...]
+
+
+def handed_on(value, after):
+    spec = pl.BlockSpec(memory_space=pltpu.VMEM)
+    return pl.pallas_call(
+        hand_on_kernel,
+        out_shape=jax.ShapeDtypeStruct(value.shape, value.dtype),
+        in_specs=[spec, spec],
+        out_specs=spec,
+        compiler_params=memory(16),
+        name="handed_on",
+    )(value, after)
+
+
 def sum_over_panels(core, parts, received):
     both = ("obs", "pix")
     parts = [added(part, other) for part, other in zip(parts, received)]
@@ -457,7 +476,7 @@
     passed_on = (shared.astype(jnp.float32) + near_first.astype(jnp.float32)).astype(jnp.bfloat16)
     passed_on, send, rows, later = lax.optimization_barrier((passed_on, send, rows, chan))
     far = swap(passed_on, "chan", 3)
-    near = swap(send, "chan", 1)
+    near = swap(handed_on(send, passed_on), "chan", 1)
     (keep,) = project(*rest, later, (0,), LARGE)
     if paired:
         answers = swap(rows, "pix", 1)

time: 67.8 us -> 70.1 us (1.034)
  starting transfers between devices: 18.8 us -> 20.1 us
  waiting for transfers between devices: 22.5 us -> 23.6 us
    ppermute x12, starting transfers between devices: 13.4 us -> 14.8 us  [swap(): return lax.ppermute(value, axis, [(i, i ^ bit) for i in range(size)])]
    ppermute x12, waiting for transfers between devices: 16 us -> 17 us  [swap(): return lax.ppermute(value, axis, [(i, i ^ bit) for i in range(size)])]
  transfers between devices with their start and end apart: 17 -> 17, of which waited for: 9 -> 8; matrix products, arithmetic and copies ran while one was open for 2% -> 2% of each run, Pallas kernels for 33% -> 31%
where the time goes in v17:
time: 70.1 us; the launch traced here: 69.9 us
  Pallas kernels  24.6 us (35%)
  waiting for transfers between devices  23.6 us (34%)
  starting transfers between devices  20.1 us (29%)
  other arithmetic  1.21 us (2%)
    ppermute x12, waiting for transfers between devices, swap(): return lax.ppermute(value, axis, [(i, i ^ bit) for i in range(size)])  17 us
    ppermute x12, starting transfers between devices, swap(): return lax.ppermute(value, axis, [(i, i ^ bit) for i in range(size)])  14.8 us
    pallas_call x2, Pallas kernels, pixel_rows(): pl.pallas_call(functools.partial(pixel_kernel, count, bits), out_shape=(j...  14 us
    ppermute x4, waiting for transfers between devices, sum_over_panels(): parts = [added(part, lax.ppermute(part, both, perm)) for part in parts]  6.56 us
    ppermute x4, starting transfers between devices, sum_over_panels(): parts = [added(part, lax.ppermute(part, both, perm)) for part in parts]  5.28 us
    pallas_call x2, Pallas kernels, project(): pl.pallas_call(functools.partial(project_kernel, bits), out_shape=(jax.Sh...  4.67 us
    pallas_call x1, Pallas kernels, early_product(): pl.pallas_call(early_kernel, out_shape=(jax.ShapeDtypeStruct((depth, widt...  2.49 us
  transfers between devices with their start and end apart: 17, of which 8 were waited for; matrix products, arithmetic and copies ran while one was open for 2% of the time, Pallas kernels for 31%

profile of v17, /device:TPU:0, one launch (start us, length us, event | category | flops | bytes accessed | tf_op | source)
XLA Modules:
  0.0 69.9 jit_solution(9933549061974523486)
XLA Ops:
  0.0 3.0 %collective-permute-start = (s32[2048]{0:T(1024)}, s32[2048]{0:T(1024)S(1)}, u32[]{:S(2)}, u32[]{:S(2)}) collective-permute-start(s32[2048]{0:T(1024)} %wanted.1), channel_id=1, source_target_pairs={{0,4},{4,0},{1,5},{5,1},{2,6},{6,2},{3,7},{7,3},{8,12},{12,8},{9,1... | collective-permute-start | bytes 24584 | tf_op jit(solution)/shard_map/ppermute | solution.py:45
  3.0 0.9 %slice_select_fusion = bf16[128,256]{1,0:T(8,128)(2,1)S(1)} fusion(bf16[4096,256]{1,0:T(8,128)(2,1)} %cotangent.3, pred[]{:T(512)S(6)} %eq.3), kind=kLoop, calls=%fused_computation.5 | loop fusion | flops 32768 | bytes 196609 | tf_op jit(solution)/shard_map/jit(_where)/select_n | solution.py:22
  4.0 2.7 %project.2 = bf16[512,256]{1,0:T(8,128)(2,1)} custom-call(s32[1]{0:T(128)} %bitcast.1.chan, bf16[2048,1152]{1,0:T(8,128)(2,1)} %spectra.9, bf16[1152,256]{1,0:T(8,128)(2,1)} %weight.7), custom_call_target="tpu_custom_call" | custom-call | flops 301989888 | bytes 2031616 | tf_op jit(solution)/shard_map/project/pallas_call | solution.py:88
  6.7 2.1 %collective-permute-start.2 = (bf16[512,256]{1,0:T(8,128)(2,1)}, bf16[512,256]{1,0:T(8,128)(2,1)S(1)}, u32[]{:S(2)}, u32[]{:S(2)}) collective-permute-start(bf16[512,256]{1,0:T(8,128)(2,1)} %project.2), channel_id=1, source_target_pairs={{0,1},{1,0},{2,3},{3,2},{4,5},{5,4},{6,7},{7,6},{8,9},{9,8},{10,11... | collective-permute-start | bytes 786440 | tf_op jit(solution)/shard_map/ppermute | solution.py:45
  8.8 0.1 pad_add_fusion.1.where
  8.9 0.1 pad_add_fusion.where
  9.1 7.9 %pixel_rows.2 = (bf16[512,256]{1,0:T(8,128)(2,1)S(1)}, bf16[512,256]{1,0:T(8,128)(2,1)S(1)}, bf16[512,256]{1,0:T(8,128)(2,1)S(1)}) custom-call(s32[2]{0:T(128)S(1)} %pad_add_fusion.1.where, s32[16384]{0:T(1024)S(1)} %bitcast.11, s32[2048]{0:T(1024)S(1)} %collective-permute-done.wanted, bf16[4096,256]{1,0:T(8,128)(2,1)} %cotangent.3, ...), custom_call_target="tpu_custom_call" | custom-call | flops 17179869184 | bytes 4194304 | tf_op jit(solution)/shard_map/pixel_rows/pallas_call | solution.py:303
  17.1 2.8 %collective-permute-start.4 = (bf16[512,256]{1,0:T(8,128)(2,1)S(1)}, bf16[512,256]{1,0:T(8,128)(2,1)S(1)}, u32[]{:S(2)}, u32[]{:S(2)}) collective-permute-start(bf16[512,256]{1,0:T(8,128)(2,1)S(1)} %add_convert_fusion._), channel_id=1, source_target_pairs={{0,3},{1,2},{2,1},{3,0},{4,7},{5,6},{6,5},{7,4},{8,11},{9,10},{10,... | collective-permute-start | bytes 786440 | tf_op jit(solution)/shard_map/ppermute | solution.py:45
  19.9 0.5 collective-permute-start.3
  20.4 1.5 %collective-permute-start.5 = (bf16[512,256]{1,0:T(8,128)(2,1)S(1)}, bf16[512,256]{1,0:T(8,128)(2,1)S(1)}, u32[]{:S(2)}, u32[]{:S(2)}) collective-permute-start(bf16[512,256]{1,0:T(8,128)(2,1)S(1)} %get-tuple-element.29), channel_id=1, source_target_pairs={{0,4},{4,0},{1,5},{5,1},{2,6},{6,2},{3,7},{7,3},{8,12},{12,8},{9,1... | collective-permute-start | bytes 786440 | tf_op jit(solution)/shard_map/ppermute | solution.py:45
  22.0 6.1 %pixel_rows.3.mine = bf16[512,256]{1,0:T(8,128)(2,1)S(1)} custom-call(s32[2]{0:T(128)S(1)} %pad_add_fusion.2.where, s32[16384]{0:T(1024)S(1)} %bitcast.12, s32[2048]{0:T(1024)S(1)} %copy-done.3, bf16[4096,256]{1,0:T(8,128)(2,1)} %cotangent.3, bf16[128,256]{1,0:T(8,128)(2,1)S(1)} %collective-permute-done.1.above.below, ...), custom_call_target="tpu_custom_call" | custom-call | flops 17179869184 | bytes 4194304 | tf_op jit(solution)/shard_map/pixel_rows/pallas_call | solution.py:303
  28.1 1.9 %project.3.keep = bf16[512,256]{1,0:T(8,128)(2,1)S(1)} custom-call(s32[1]{0:T(128)} %bitcast.4.chan, bf16[2048,1152]{1,0:T(8,128)(2,1)} %spectra.9, bf16[1152,256]{1,0:T(8,128)(2,1)S(1)} %copy-done), custom_call_target="tpu_custom_call" | custom-call | flops 301989888 | bytes 2031616 | tf_op jit(solution)/shard_map/project/pallas_call | solution.py:88
  30.1 1.8 %collective-permute-done.3.near = bf16[512,256]{1,0:T(8,128)(2,1)S(1)} collective-permute-done((bf16[512,256]{1,0:T(8,128)(2,1)S(1)}, bf16[512,256]{1,0:T(8,128)(2,1)S(1)}, u32[]{:S(2)}, u32[]{:S(2)}) %collective-permute-start.3) | collective-permute-done | bytes 262176 | tf_op jit(solution)/shard_map/ppermute | solution.py:45
  31.9 1.0 %pre_gradient.1.first = bf16[512,256]{1,0:T(8,128)(2,1)S(1)} custom-call(s32[2]{0:T(128)S(1)} %pad_add_fusion.where, bf16[512,256]{1,0:T(8,128)(2,1)S(1)} %project.3.keep, bf16[512,256]{1,0:T(8,128)(2,1)S(1)} %collective-permute-done.3.near, bf16[512,256]{1,0:T(8,128)(2,1)S(1)} %collective-permute-done.4.far, s32[16,128]{1,0:T(8,128)S(1)} %bitcast.13, ...), custom_call_target="tpu_custom_call" | custom-call | tf_op jit(solution)/shard_map/pre_gradient/pallas_call | solution.py:375
  33.0 1.8 %collective-permute-start.6 = (bf16[512,256]{1,0:T(8,128)(2,1)S(1)}, bf16[512,256]{1,0:T(8,128)(2,1)S(1)}, u32[]{:S(2)}, u32[]{:S(2)}) collective-permute-start(bf16[512,256]{1,0:T(8,128)(2,1)S(1)} %pre_gradient.1.first), channel_id=1, source_target_pairs={{0,3},{1,2},{2,1},{3,0},{4,7},{5,6},{6,5},{7,4},{8,11},{9,10},{10,... | collective-permute-start | bytes 786440 | tf_op jit(solution)/shard_map/ppermute | solution.py:45
  34.8 9.3 %collective-permute-done.6.second = bf16[512,256]{1,0:T(8,128)(2,1)S(1)} collective-permute-done((bf16[512,256]{1,0:T(8,128)(2,1)S(1)}, bf16[512,256]{1,0:T(8,128)(2,1)S(1)}, u32[]{:S(2)}, u32[]{:S(2)}) %collective-permute-start.6) | collective-permute-done | bytes 262176 | tf_op jit(solution)/shard_map/ppermute | solution.py:45
  44.0 2.4 %collective-permute-start.8 = (bf16[512,256]{1,0:T(8,128)(2,1)S(1)}, bf16[512,256]{1,0:T(8,128)(2,1)S(1)}, u32[]{:S(2)}, u32[]{:S(2)}) collective-permute-start(bf16[512,256]{1,0:T(8,128)(2,1)S(1)} %collective-permute-done.6.second), channel_id=1, source_target_pairs={{0,1},{1,0},{2,3},{3,2},{4,5},{5,4},{6,7},{7,6},{8,9},{9,8},{10,11... | collective-permute-start | bytes 786440 | tf_op jit(solution)/shard_map/ppermute | solution.py:45
  46.4 2.5 %early_product.1 = (f32[1152,256]{1,0:T(8,128)S(1)}, bf16[512,1152]{1,0:T(8,128)(2,1)S(1)}, bf16[512,1152]{1,0:T(8,128)(2,1)S(1)}) custom-call(s32[1]{0:T(128)} %bitcast.1.chan, bf16[2048,1152]{1,0:T(8,128)(2,1)} %spectra.9, bf16[512,256]{1,0:T(8,128)(2,1)S(1)} %pre_gradient.1.first, bf16[512,256]{1,0:T(8,128)(2,1)S(1)} %collective-permute-done.6.second), custom_call_target="tpu_custom_call" | custom-call | flops 603979776 | bytes 5898240 | tf_op jit(solution)/shard_map/early_product/pallas_call | solution.py:135
  48.9 0.5 more_product.1.before
  49.4 3.7 %collective-permute-done.8.rows = bf16[512,256]{1,0:T(8,128)(2,1)S(1)} collective-permute-done((bf16[512,256]{1,0:T(8,128)(2,1)S(1)}, bf16[512,256]{1,0:T(8,128)(2,1)S(1)}, u32[]{:S(2)}, u32[]{:S(2)}) %collective-permute-start.8) | collective-permute-done | bytes 262176 | tf_op jit(solution)/shard_map/ppermute | solution.py:45
  53.2 0.6 late_product.1
  53.8 0.5 collective-permute-start.12
  54.3 0.9 %collective-permute-done.9.second = bf16[288,256]{1,0:T(8,128)(2,1)S(1)} collective-permute-done((bf16[288,256]{1,0:T(8,128)(2,1)S(1)}, bf16[288,256]{1,0:T(8,128)(2,1)S(1)}, u32[]{:S(2)}, u32[]{:S(2)}) %collective-permute-start.9) | collective-permute-done | bytes 147488 | tf_op jit(solution)/shard_map/ppermute | solution.py:45
  55.2 1.6 %collective-permute-start.10 = (bf16[288,256]{1,0:T(8,128)(2,1)S(1)}, bf16[288,256]{1,0:T(8,128)(2,1)S(1)}, u32[]{:S(2)}, u32[]{:S(2)}) collective-permute-start(bf16[288,256]{1,0:T(8,128)(2,1)S(1)} %added.6.first), channel_id=1, source_target_pairs={{0,16},{4,20},{8,12},{12,8},{16,0},{20,4},{24,28},{28,24},{1,17},{... | collective-permute-start | bytes 442376 | tf_op jit(solution)/shard_map/ppermute | solution.py:446
  56.8 0.6 collective-permute-start.13
  57.4 3.0 %collective-permute-done.10.second = bf16[288,256]{1,0:T(8,128)(2,1)S(1)} collective-permute-done((bf16[288,256]{1,0:T(8,128)(2,1)S(1)}, bf16[288,256]{1,0:T(8,128)(2,1)S(1)}, u32[]{:S(2)}, u32[]{:S(2)}) %collective-permute-start.10) | collective-permute-done | bytes 147488 | tf_op jit(solution)/shard_map/ppermute | solution.py:446
  60.5 1.6 %collective-permute-start.11 = (bf16[288,256]{1,0:T(8,128)(2,1)S(1)}, bf16[288,256]{1,0:T(8,128)(2,1)S(1)}, u32[]{:S(2)}, u32[]{:S(2)}) collective-permute-start(bf16[288,256]{1,0:T(8,128)(2,1)S(1)} %added.7.first), channel_id=1, source_target_pairs={{0,4},{4,0},{8,24},{12,28},{16,20},{20,16},{24,8},{28,12},{1,5},{5... | collective-permute-start | bytes 442376 | tf_op jit(solution)/shard_map/ppermute | solution.py:446
  62.1 1.5 %collective-permute-start.14 = (bf16[288,256]{1,0:T(8,128)(2,1)S(1)}, bf16[288,256]{1,0:T(8,128)(2,1)S(1)}, u32[]{:S(2)}, u32[]{:S(2)}) collective-permute-start(bf16[288,256]{1,0:T(8,128)(2,1)S(1)} %added.10.first), channel_id=1, source_target_pairs={{0,4},{4,0},{8,24},{12,28},{16,20},{20,16},{24,8},{28,12},{1,5},{5... | collective-permute-start | bytes 442376 | tf_op jit(solution)/shard_map/ppermute | solution.py:446
  63.7 2.0 %collective-permute-done.11.second = bf16[288,256]{1,0:T(8,128)(2,1)S(1)} collective-permute-done((bf16[288,256]{1,0:T(8,128)(2,1)S(1)}, bf16[288,256]{1,0:T(8,128)(2,1)S(1)}, u32[]{:S(2)}, u32[]{:S(2)}) %collective-permute-start.11) | collective-permute-done | bytes 147488 | tf_op jit(solution)/shard_map/ppermute | solution.py:446
  65.8 1.5 %collective-permute-done.14.second = bf16[288,256]{1,0:T(8,128)(2,1)S(1)} collective-permute-done((bf16[288,256]{1,0:T(8,128)(2,1)S(1)}, bf16[288,256]{1,0:T(8,128)(2,1)S(1)}, u32[]{:S(2)}, u32[]{:S(2)}) %collective-permute-start.14) | collective-permute-done | bytes 147488 | tf_op jit(solution)/shard_map/ppermute | solution.py:446
  67.4 1.3 %collective-permute-done.16.refs_3_ = bf16[288,256]{1,0:T(8,128)(2,1)S(1)} collective-permute-done((bf16[288,256]{1,0:T(8,128)(2,1)S(1)}, bf16[288,256]{1,0:T(8,128)(2,1)S(1)}, u32[]{:S(2)}, u32[]{:S(2)}) %collective-permute-start.16) | collective-permute-done | bytes 147488 | tf_op jit(solution)/shard_map/ppermute | solution.py:45
  68.8 1.1 %collect.1 = f32[1152,256]{1,0:T(8,128)} custom-call(s32[1]{0:T(128)} %bitcast.core, bf16[288,256]{1,0:T(8,128)(2,1)S(1)} %added.8.refs_0_, bf16[288,256]{1,0:T(8,128)(2,1)S(1)} %added.11.refs_1_, bf16[288,256]{1,0:T(8,128)(2,1)S(1)} %collective-permute-done.15.refs_2_, bf16[288,256]{1,0:T(8,128)(2,1)S(1)} %collective-permute-done.16.refs_3_), custom_call_target="tpu_custom_call" | custom-call | tf_op jit(solution)/shard_map/collect/pallas_call | solution.py:399
  (38 shorter events, 0.8 us)
Async XLA Ops:
  0.0 9.0 %collective-permute-start = (s32[2048]{0:T(1024)}, s32[2048]{0:T(1024)S(1)}, u32[]{:S(2)}, u32[]{:S(2)}) collective-permute-start(s32[2048]{0:T(1024)} %wanted.1), channel_id=1, source_target_pairs={{0,4},{4,0},{1,5},{5,1},{2,6},{6,2},{3,7},{7,3},{8,12},{12,8},{9,1... | collective-permute-start | bytes 24584 | tf_op jit(solution)/shard_map/ppermute | solution.py:45
  3.9 5.2 %collective-permute-start.1 = (bf16[128,256]{1,0:T(8,128)(2,1)S(1)}, bf16[128,256]{1,0:T(8,128)(2,1)S(1)}, u32[]{:S(2)}, u32[]{:S(2)}) collective-permute-start(bf16[128,256]{1,0:T(8,128)(2,1)S(1)} %slice_select_fusion), channel_id=1, source_target_pairs={{0,4},{4,0},{1,5},{5,1},{2,6},{6,2},{3,7},{7,3},{8,12},{12,8},{9,1... | collective-permute-start | bytes 196616 | tf_op jit(solution)/shard_map/ppermute | solution.py:22
  3.9 5.0 %copy-start.5 = (s32[8,4096]{1,0:T(8,128)S(1)}, s32[8,4096]{1,0:T(8,128)}, u32[]{:S(2)}) copy-start(s32[8,4096]{1,0:T(8,128)} %param.14) | copy-start | bytes 393220
  3.9 5.1 %copy-start = (bf16[1152,256]{1,0:T(8,128)(2,1)S(1)}, bf16[1152,256]{1,0:T(8,128)(2,1)}, u32[]{:S(2)}) copy-start(bf16[1152,256]{1,0:T(8,128)(2,1)} %weight.7) | copy-start | bytes 1769476
  4.0 5.1 %copy-start.4 = (f32[8,256]{1,0:T(8,128)S(1)}, f32[8,256]{1,0:T(8,128)}, u32[]{:S(2)}) copy-start(f32[8,256]{1,0:T(8,128)} %mixing.3) | copy-start | bytes 24580
  6.7 10.3 %collective-permute-start.2 = (bf16[512,256]{1,0:T(8,128)(2,1)}, bf16[512,256]{1,0:T(8,128)(2,1)S(1)}, u32[]{:S(2)}, u32[]{:S(2)}) collective-permute-start(bf16[512,256]{1,0:T(8,128)(2,1)} %project.2), channel_id=1, source_target_pairs={{0,1},{1,0},{2,3},{3,2},{4,5},{5,4},{6,7},{7,6},{8,9},{9,8},{10,11... | collective-permute-start | bytes 786440 | tf_op jit(solution)/shard_map/ppermute | solution.py:45
  17.0 5.0 %copy-start.3 = (s32[2048]{0:T(1024)S(1)}, s32[2048]{0:T(1024)}, u32[]{:S(2)}) copy-start(s32[2048]{0:T(1024)} %wanted.1) | copy-start | bytes 24580
  17.1 14.8 %collective-permute-start.4 = (bf16[512,256]{1,0:T(8,128)(2,1)S(1)}, bf16[512,256]{1,0:T(8,128)(2,1)S(1)}, u32[]{:S(2)}, u32[]{:S(2)}) collective-permute-start(bf16[512,256]{1,0:T(8,128)(2,1)S(1)} %add_convert_fusion._), channel_id=1, source_target_pairs={{0,3},{1,2},{2,1},{3,0},{4,7},{5,6},{6,5},{7,4},{8,11},{9,10},{10,... | collective-permute-start | bytes 786440 | tf_op jit(solution)/shard_map/ppermute | solution.py:45
  19.9 12.0 %collective-permute-start.3 = (bf16[512,256]{1,0:T(8,128)(2,1)S(1)}, bf16[512,256]{1,0:T(8,128)(2,1)S(1)}, u32[]{:S(2)}, u32[]{:S(2)}) collective-permute-start(bf16[512,256]{1,0:T(8,128)(2,1)S(1)} %handed_on.1), channel_id=1, source_target_pairs={{0,1},{1,0},{2,3},{3,2},{4,5},{5,4},{6,7},{7,6},{8,9},{9,8},{10,11... | collective-permute-start | bytes 786440 | tf_op jit(solution)/shard_map/ppermute | solution.py:45
  20.4 11.5 %collective-permute-start.5 = (bf16[512,256]{1,0:T(8,128)(2,1)S(1)}, bf16[512,256]{1,0:T(8,128)(2,1)S(1)}, u32[]{:S(2)}, u32[]{:S(2)}) collective-permute-start(bf16[512,256]{1,0:T(8,128)(2,1)S(1)} %get-tuple-element.29), channel_id=1, source_target_pairs={{0,4},{4,0},{1,5},{5,1},{2,6},{6,2},{3,7},{7,3},{8,12},{12,8},{9,1... | collective-permute-start | bytes 786440 | tf_op jit(solution)/shard_map/ppermute | solution.py:45
  28.1 3.8 %copy-start.1 = (s32[2048,1]{0,1:T(1,128)S(1)}, s32[2048,1]{0,1:T(1,128)}, u32[]{:S(2)}) copy-start(s32[2048,1]{0,1:T(1,128)} %param.10) | copy-start | bytes 24580
  28.1 3.8 %copy-start.2 = (f32[2048]{0:T(1024)S(1)}, f32[2048]{0:T(1024)}, u32[]{:S(2)}) copy-start(f32[2048]{0:T(1024)} %param.12) | copy-start | bytes 24580
  33.0 11.1 %collective-permute-start.6 = (bf16[512,256]{1,0:T(8,128)(2,1)S(1)}, bf16[512,256]{1,0:T(8,128)(2,1)S(1)}, u32[]{:S(2)}, u32[]{:S(2)}) collective-permute-start(bf16[512,256]{1,0:T(8,128)(2,1)S(1)} %pre_gradient.1.first), channel_id=1, source_target_pairs={{0,3},{1,2},{2,1},{3,0},{4,7},{5,6},{6,5},{7,4},{8,11},{9,10},{10,... | collective-permute-start | bytes 786440 | tf_op jit(solution)/shard_map/ppermute | solution.py:45
  34.7 14.2 %collective-permute-start.7 = (bf16[512,256]{1,0:T(8,128)(2,1)S(1)}, bf16[512,256]{1,0:T(8,128)(2,1)S(1)}, u32[]{:S(2)}, u32[]{:S(2)}) collective-permute-start(bf16[512,256]{1,0:T(8,128)(2,1)S(1)} %pre_gradient.1.first), channel_id=1, source_target_pairs={{0,1},{1,0},{2,3},{3,2},{4,5},{5,4},{6,7},{7,6},{8,9},{9,8},{10,11... | collective-permute-start | bytes 786440 | tf_op jit(solution)/shard_map/ppermute | solution.py:45
  44.0 9.1 %collective-permute-start.8 = (bf16[512,256]{1,0:T(8,128)(2,1)S(1)}, bf16[512,256]{1,0:T(8,128)(2,1)S(1)}, u32[]{:S(2)}, u32[]{:S(2)}) collective-permute-start(bf16[512,256]{1,0:T(8,128)(2,1)S(1)} %collective-permute-done.6.second), channel_id=1, source_target_pairs={{0,1},{1,0},{2,3},{3,2},{4,5},{5,4},{6,7},{7,6},{8,9},{9,8},{10,11... | collective-permute-start | bytes 786440 | tf_op jit(solution)/shard_map/ppermute | solution.py:45
  53.8 1.4 %collective-permute-start.9 = (bf16[288,256]{1,0:T(8,128)(2,1)S(1)}, bf16[288,256]{1,0:T(8,128)(2,1)S(1)}, u32[]{:S(2)}, u32[]{:S(2)}) collective-permute-start(bf16[288,256]{1,0:T(8,128)(2,1)S(1)} %get-tuple-element.34), channel_id=1, source_target_pairs={{0,8},{8,0},{16,24},{24,16},{1,9},{9,1},{17,25},{25,17},{2,10},{10... | collective-permute-start | bytes 442376 | tf_op jit(solution)/shard_map/ppermute | solution.py:45
  53.8 2.9 %collective-permute-start.12 = (bf16[288,256]{1,0:T(8,128)(2,1)S(1)}, bf16[288,256]{1,0:T(8,128)(2,1)S(1)}, u32[]{:S(2)}, u32[]{:S(2)}) collective-permute-start(bf16[288,256]{1,0:T(8,128)(2,1)S(1)} %get-tuple-element.36), channel_id=1, source_target_pairs={{0,8},{8,0},{16,24},{24,16},{1,9},{9,1},{17,25},{25,17},{2,10},{10... | collective-permute-start | bytes 442376 | tf_op jit(solution)/shard_map/ppermute | solution.py:45
  55.2 5.2 %collective-permute-start.10 = (bf16[288,256]{1,0:T(8,128)(2,1)S(1)}, bf16[288,256]{1,0:T(8,128)(2,1)S(1)}, u32[]{:S(2)}, u32[]{:S(2)}) collective-permute-start(bf16[288,256]{1,0:T(8,128)(2,1)S(1)} %added.6.first), channel_id=1, source_target_pairs={{0,16},{4,20},{8,12},{12,8},{16,0},{20,4},{24,28},{28,24},{1,17},{... | collective-permute-start | bytes 442376 | tf_op jit(solution)/shard_map/ppermute | solution.py:446
  56.8 5.2 %collective-permute-start.13 = (bf16[288,256]{1,0:T(8,128)(2,1)S(1)}, bf16[288,256]{1,0:T(8,128)(2,1)S(1)}, u32[]{:S(2)}, u32[]{:S(2)}) collective-permute-start(bf16[288,256]{1,0:T(8,128)(2,1)S(1)} %added.9.first), channel_id=1, source_target_pairs={{0,16},{4,20},{8,12},{12,8},{16,0},{20,4},{24,28},{28,24},{1,17},{... | collective-permute-start | bytes 442376 | tf_op jit(solution)/shard_map/ppermute | solution.py:446
  60.5 5.2 %collective-permute-start.11 = (bf16[288,256]{1,0:T(8,128)(2,1)S(1)}, bf16[288,256]{1,0:T(8,128)(2,1)S(1)}, u32[]{:S(2)}, u32[]{:S(2)}) collective-permute-start(bf16[288,256]{1,0:T(8,128)(2,1)S(1)} %added.7.first), channel_id=1, source_target_pairs={{0,4},{4,0},{8,24},{12,28},{16,20},{20,16},{24,8},{28,12},{1,5},{5... | collective-permute-start | bytes 442376 | tf_op jit(solution)/shard_map/ppermute | solution.py:446
  62.1 5.2 %collective-permute-start.14 = (bf16[288,256]{1,0:T(8,128)(2,1)S(1)}, bf16[288,256]{1,0:T(8,128)(2,1)S(1)}, u32[]{:S(2)}, u32[]{:S(2)}) collective-permute-start(bf16[288,256]{1,0:T(8,128)(2,1)S(1)} %added.10.first), channel_id=1, source_target_pairs={{0,4},{4,0},{8,24},{12,28},{16,20},{20,16},{24,8},{28,12},{1,5},{5... | collective-permute-start | bytes 442376 | tf_op jit(solution)/shard_map/ppermute | solution.py:446
  65.7 1.7 %collective-permute-start.15 = (bf16[288,256]{1,0:T(8,128)(2,1)S(1)}, bf16[288,256]{1,0:T(8,128)(2,1)S(1)}, u32[]{:S(2)}, u32[]{:S(2)}) collective-permute-start(bf16[288,256]{1,0:T(8,128)(2,1)S(1)} %added.8.refs_0_), channel_id=1, source_target_pairs={{0,8},{8,0},{16,24},{24,16},{1,9},{9,1},{17,25},{25,17},{2,10},{10... | collective-permute-start | bytes 442376 | tf_op jit(solution)/shard_map/ppermute | solution.py:45
  67.3 1.4 %collective-permute-start.16 = (bf16[288,256]{1,0:T(8,128)(2,1)S(1)}, bf16[288,256]{1,0:T(8,128)(2,1)S(1)}, u32[]{:S(2)}, u32[]{:S(2)}) collective-permute-start(bf16[288,256]{1,0:T(8,128)(2,1)S(1)} %added.11.refs_1_), channel_id=1, source_target_pairs={{0,8},{8,0},{16,24},{24,16},{1,9},{9,1},{17,25},{25,17},{2,10},{10... | collective-permute-start | bytes 442376 | tf_op jit(solution)/shard_map/ppermute | solution.py:45

commit v18 on v17

--- a/solution.py
+++ b/solution.py
@@ -181,31 +181,39 @@
     )(held, before, rows)
 
 
+def chunks(half):
+    first = half * 5 // 8 // 32 * 32
+    return first, half - first
+
+
 def late_kernel(core, held, before, rows, *outs):
     *outs, total = outs
     total[...] = before[...] + turned_product(held[...], rows[...])
-    size = outs[0].shape[0]
+    half = total.shape[0] // 2
     for index, out in enumerate(outs):
-        first = (core[0] ^ (1 - index // 2)) * 2 * size + index % 2 * size
-        here = pl.ds(pl.multiple_of(first, size), size)
+        size = out.shape[0]
+        first = (core[0] ^ (1 - index // 2)) * half + index % 2 * (half - size)
+        here = pl.ds(pl.multiple_of(first, 32), size)
         out[...] = total[here, :].astype(out.dtype)
 
 
 def late_product(core, held, before, rows):
-    size, width = before.shape[0] // 4, before.shape[1]
+    depth, width = before.shape
     spec = pl.BlockSpec(memory_space=pltpu.VMEM)
-    send = jax.ShapeDtypeStruct((size, width), jnp.bfloat16)
-    keep = jax.ShapeDtypeStruct((size, width), jnp.float32)
     outs = pl.pallas_call(
         late_kernel,
-        out_shape=(send, send, keep, keep),
+        out_shape=tuple(
+            jax.ShapeDtypeStruct((size, width), kind)
+            for kind in (jnp.bfloat16, jnp.float32)
+            for size in chunks(depth // 2)
+        ),
         in_specs=[pl.BlockSpec(memory_space=pltpu.SMEM)] + [spec] * 3,
         out_specs=(spec,) * 4,
         scratch_shapes=[pltpu.VMEM(before.shape, jnp.float32)],
         compiler_params=memory(16),
         cost_estimate=pl.CostEstimate(
             flops=2 * held.shape[0] * held.shape[1] * width,
-            bytes_accessed=2 * held.shape[0] * held.shape[1] + 16 * size * width,
+            bytes_accessed=2 * held.shape[0] * held.shape[1] + 8 * depth * width,
             transcendentals=0,
         ),
         name="late_product",
@@ -384,12 +392,12 @@
 
 def collect_kernel(core, *refs):
     *pieces, out = refs
-    half, rows = out.shape[0] // 2, pieces[0].shape[0]
-    count = len(pieces) // 2
+    half = out.shape[0] // 2
     for index, piece in enumerate(pieces):
-        which = core[0] if index < count else 1 - core[0]
-        first = which * half + (index % count) * rows
-        out[pl.ds(pl.multiple_of(first, rows), rows), :] = piece[...].astype(jnp.float32)
+        which = core[0] if index < 2 else 1 - core[0]
+        size = piece.shape[0]
+        first = which * half + index % 2 * (half - size)
+        out[pl.ds(pl.multiple_of(first, 32), size), :] = piece[...].astype(jnp.float32)
 
 
 def collect(core, own, received):
@@ -420,22 +428,6 @@
         compiler_params=memory(16),
         name="added",
     )(first, second)
-
-
-def hand_on_kernel(value, _, out):
-    out[...] = value[...]
-
-
-def handed_on(value, after):
-    spec = pl.BlockSpec(memory_space=pltpu.VMEM)
-    return pl.pallas_call(
-        hand_on_kernel,
-        out_shape=jax.ShapeDtypeStruct(value.shape, value.dtype),
-        in_specs=[spec, spec],
-        out_specs=spec,
-        compiler_params=memory(16),
-        name="handed_on",
-    )(value, after)
 
 
 def sum_over_panels(core, parts, received):
@@ -476,7 +468,7 @@
     passed_on = (shared.astype(jnp.float32) + near_first.astype(jnp.float32)).astype(jnp.bfloat16)
     passed_on, send, rows, later = lax.optimization_barrier((passed_on, send, rows, chan))
     far = swap(passed_on, "chan", 3)
-    near = swap(handed_on(send, passed_on), "chan", 1)
+    near = swap(send, "chan", 1)
     (keep,) = project(*rest, later, (0,), LARGE)
     if paired:
         answers = swap(rows, "pix", 1)

time: 70.1 us -> 72.6 us (1.036)
  waiting for transfers between devices: 23.6 us -> 27.9 us
  starting transfers between devices: 20.1 us -> 18.3 us
    ppermute x4, waiting for transfers between devices: 6.56 us -> 11.5 us  [sum_over_panels(): parts = [added(part, lax.ppermute(part, both, perm)) for part in parts]]
    ppermute x12, starting transfers between devices: 14.8 us -> 12.9 us  [swap(): return lax.ppermute(value, axis, [(i, i ^ bit) for i in range(size)])]
  transfers between devices with their start and end apart: 17 -> 17, of which waited for: 8 -> 9; matrix products, arithmetic and copies ran while one was open for 2% -> 2% of each run, Pallas kernels for 31% -> 30%
where the time goes in v18:
time: 72.6 us; the launch traced here: 72.3 us
  waiting for transfers between devices  27.9 us (38%)
  Pallas kernels  24.6 us (34%)
  starting transfers between devices  18.3 us (25%)
  other arithmetic  1.21 us (2%)
    ppermute x12, waiting for transfers between devices, swap(): return lax.ppermute(value, axis, [(i, i ^ bit) for i in range(size)])  16.5 us
    pallas_call x2, Pallas kernels, pixel_rows(): pl.pallas_call(functools.partial(pixel_kernel, count, bits), out_shape=(j...  14 us
    ppermute x12, starting transfers between devices, swap(): return lax.ppermute(value, axis, [(i, i ^ bit) for i in range(size)])  12.9 us
    ppermute x4, waiting for transfers between devices, sum_over_panels(): parts = [added(part, lax.ppermute(part, both, perm)) for part in parts]  11.5 us
    ppermute x4, starting transfers between devices, sum_over_panels(): parts = [added(part, lax.ppermute(part, both, perm)) for part in parts]  5.26 us
    pallas_call x2, Pallas kernels, project(): pl.pallas_call(functools.partial(project_kernel, bits), out_shape=(jax.Sh...  4.67 us
    pallas_call x1, Pallas kernels, early_product(): pl.pallas_call(early_kernel, out_shape=(jax.ShapeDtypeStruct((depth, widt...  2.49 us
  transfers between devices with their start and end apart: 17, of which 9 were waited for; matrix products, arithmetic and copies ran while one was open for 2% of the time, Pallas kernels for 30%

profile of v18, /device:TPU:0, one launch (start us, length us, event | category | flops | bytes accessed | tf_op | source)
XLA Modules:
  0.0 72.3 jit_solution(9464792154866123348)
XLA Ops:
  0.0 3.0 %collective-permute-start = (s32[2048]{0:T(1024)}, s32[2048]{0:T(1024)S(1)}, u32[]{:S(2)}, u32[]{:S(2)}) collective-permute-start(s32[2048]{0:T(1024)} %wanted.1), channel_id=1, source_target_pairs={{0,4},{4,0},{1,5},{5,1},{2,6},{6,2},{3,7},{7,3},{8,12},{12,8},{9,1... | collective-permute-start | bytes 24584 | tf_op jit(solution)/shard_map/ppermute | solution.py:45
  3.0 0.9 %slice_select_fusion = bf16[128,256]{1,0:T(8,128)(2,1)S(1)} fusion(bf16[4096,256]{1,0:T(8,128)(2,1)} %cotangent.3, pred[]{:T(512)S(6)} %eq.3), kind=kLoop, calls=%fused_computation.5 | loop fusion | flops 32768 | bytes 196609 | tf_op jit(solution)/shard_map/jit(_where)/select_n | solution.py:22
  4.0 2.7 %project.2 = bf16[512,256]{1,0:T(8,128)(2,1)} custom-call(s32[1]{0:T(128)} %bitcast.1.chan, bf16[2048,1152]{1,0:T(8,128)(2,1)} %spectra.9, bf16[1152,256]{1,0:T(8,128)(2,1)} %weight.7), custom_call_target="tpu_custom_call" | custom-call | flops 301989888 | bytes 2031616 | tf_op jit(solution)/shard_map/project/pallas_call | solution.py:88
  6.7 2.1 %collective-permute-start.2 = (bf16[512,256]{1,0:T(8,128)(2,1)}, bf16[512,256]{1,0:T(8,128)(2,1)S(1)}, u32[]{:S(2)}, u32[]{:S(2)}) collective-permute-start(bf16[512,256]{1,0:T(8,128)(2,1)} %project.2), channel_id=1, source_target_pairs={{0,1},{1,0},{2,3},{3,2},{4,5},{5,4},{6,7},{7,6},{8,9},{9,8},{10,11... | collective-permute-start | bytes 786440 | tf_op jit(solution)/shard_map/ppermute | solution.py:45
  8.9 0.1 pad_add_fusion.where
  9.1 7.9 %pixel_rows.2 = (bf16[512,256]{1,0:T(8,128)(2,1)S(1)}, bf16[512,256]{1,0:T(8,128)(2,1)S(1)}, bf16[512,256]{1,0:T(8,128)(2,1)S(1)}) custom-call(s32[2]{0:T(128)S(1)} %pad_add_fusion.1.where, s32[16384]{0:T(1024)S(1)} %bitcast.11, s32[2048]{0:T(1024)S(1)} %collective-permute-done.wanted, bf16[4096,256]{1,0:T(8,128)(2,1)} %cotangent.3, ...), custom_call_target="tpu_custom_call" | custom-call | flops 17179869184 | bytes 4194304 | tf_op jit(solution)/shard_map/pixel_rows/pallas_call | solution.py:311
  17.1 0.8 %collective-permute-start.3 = (bf16[512,256]{1,0:T(8,128)(2,1)S(1)}, bf16[512,256]{1,0:T(8,128)(2,1)S(1)}, u32[]{:S(2)}, u32[]{:S(2)}) collective-permute-start(bf16[512,256]{1,0:T(8,128)(2,1)S(1)} %get-tuple-element.27), channel_id=1, source_target_pairs={{0,1},{1,0},{2,3},{3,2},{4,5},{5,4},{6,7},{7,6},{8,9},{9,8},{10,11... | collective-permute-start | bytes 786440 | tf_op jit(solution)/shard_map/ppermute | solution.py:45
  17.9 3.4 %collective-permute-start.4 = (bf16[512,256]{1,0:T(8,128)(2,1)S(1)}, bf16[512,256]{1,0:T(8,128)(2,1)S(1)}, u32[]{:S(2)}, u32[]{:S(2)}) collective-permute-start(bf16[512,256]{1,0:T(8,128)(2,1)S(1)} %add_convert_fusion), channel_id=1, source_target_pairs={{0,3},{1,2},{2,1},{3,0},{4,7},{5,6},{6,5},{7,4},{8,11},{9,10},{10,... | collective-permute-start | bytes 786440 | tf_op jit(solution)/shard_map/ppermute | solution.py:45
  21.2 1.5 %collective-permute-start.5 = (bf16[512,256]{1,0:T(8,128)(2,1)S(1)}, bf16[512,256]{1,0:T(8,128)(2,1)S(1)}, u32[]{:S(2)}, u32[]{:S(2)}) collective-permute-start(bf16[512,256]{1,0:T(8,128)(2,1)S(1)} %get-tuple-element.29), channel_id=1, source_target_pairs={{0,4},{4,0},{1,5},{5,1},{2,6},{6,2},{3,7},{7,3},{8,12},{12,8},{9,1... | collective-permute-start | bytes 786440 | tf_op jit(solution)/shard_map/ppermute | solution.py:45
  22.8 6.1 %pixel_rows.3.mine = bf16[512,256]{1,0:T(8,128)(2,1)S(1)} custom-call(s32[2]{0:T(128)S(1)} %pad_add_fusion.2.where, s32[16384]{0:T(1024)S(1)} %bitcast.12, s32[2048]{0:T(1024)S(1)} %copy-done.3, bf16[4096,256]{1,0:T(8,128)(2,1)} %cotangent.3, bf16[128,256]{1,0:T(8,128)(2,1)S(1)} %collective-permute-done.1.above.below, ...), custom_call_target="tpu_custom_call" | custom-call | flops 17179869184 | bytes 4194304 | tf_op jit(solution)/shard_map/pixel_rows/pallas_call | solution.py:311
  29.0 1.9 %project.3.keep = bf16[512,256]{1,0:T(8,128)(2,1)S(1)} custom-call(s32[1]{0:T(128)} %bitcast.4.chan, bf16[2048,1152]{1,0:T(8,128)(2,1)} %spectra.9, bf16[1152,256]{1,0:T(8,128)(2,1)S(1)} %copy-done), custom_call_target="tpu_custom_call" | custom-call | flops 301989888 | bytes 2031616 | tf_op jit(solution)/shard_map/project/pallas_call | solution.py:88
  30.9 1.1 %collective-permute-done.4.far = bf16[512,256]{1,0:T(8,128)(2,1)S(1)} collective-permute-done((bf16[512,256]{1,0:T(8,128)(2,1)S(1)}, bf16[512,256]{1,0:T(8,128)(2,1)S(1)}, u32[]{:S(2)}, u32[]{:S(2)}) %collective-permute-start.4) | collective-permute-done | bytes 262176 | tf_op jit(solution)/shard_map/ppermute | solution.py:45
  32.1 1.0 %pre_gradient.1.first = bf16[512,256]{1,0:T(8,128)(2,1)S(1)} custom-call(s32[2]{0:T(128)S(1)} %pad_add_fusion.where, bf16[512,256]{1,0:T(8,128)(2,1)S(1)} %project.3.keep, bf16[512,256]{1,0:T(8,128)(2,1)S(1)} %collective-permute-done.3.near, bf16[512,256]{1,0:T(8,128)(2,1)S(1)} %collective-permute-done.4.far, s32[16,128]{1,0:T(8,128)S(1)} %bitcast.13, ...), custom_call_target="tpu_custom_call" | custom-call | tf_op jit(solution)/shard_map/pre_gradient/pallas_call | solution.py:383
  33.1 0.5 collective-permute-start.6
  33.6 1.3 %collective-permute-start.7 = (bf16[512,256]{1,0:T(8,128)(2,1)S(1)}, bf16[512,256]{1,0:T(8,128)(2,1)S(1)}, u32[]{:S(2)}, u32[]{:S(2)}) collective-permute-start(bf16[512,256]{1,0:T(8,128)(2,1)S(1)} %pre_gradient.1.first), channel_id=1, source_target_pairs={{0,1},{1,0},{2,3},{3,2},{4,5},{5,4},{6,7},{7,6},{8,9},{9,8},{10,11... | collective-permute-start | bytes 786440 | tf_op jit(solution)/shard_map/ppermute | solution.py:45
  34.9 9.3 %collective-permute-done.6.second = bf16[512,256]{1,0:T(8,128)(2,1)S(1)} collective-permute-done((bf16[512,256]{1,0:T(8,128)(2,1)S(1)}, bf16[512,256]{1,0:T(8,128)(2,1)S(1)}, u32[]{:S(2)}, u32[]{:S(2)}) %collective-permute-start.6) | collective-permute-done | bytes 262176 | tf_op jit(solution)/shard_map/ppermute | solution.py:45
  44.2 0.2 collective-permute-start.8
  44.4 2.5 %early_product.1 = (f32[1152,256]{1,0:T(8,128)S(1)}, bf16[512,1152]{1,0:T(8,128)(2,1)S(1)}, bf16[512,1152]{1,0:T(8,128)(2,1)S(1)}) custom-call(s32[1]{0:T(128)} %bitcast.1.chan, bf16[2048,1152]{1,0:T(8,128)(2,1)} %spectra.9, bf16[512,256]{1,0:T(8,128)(2,1)S(1)} %pre_gradient.1.first, bf16[512,256]{1,0:T(8,128)(2,1)S(1)} %collective-permute-done.6.second), custom_call_target="tpu_custom_call" | custom-call | flops 603979776 | bytes 5898240 | tf_op jit(solution)/shard_map/early_product/pallas_call | solution.py:135
  46.9 0.1 collective-permute-done.7.rows
  47.0 0.5 more_product.1.before
  47.6 3.2 %collective-permute-done.8.rows = bf16[512,256]{1,0:T(8,128)(2,1)S(1)} collective-permute-done((bf16[512,256]{1,0:T(8,128)(2,1)S(1)}, bf16[512,256]{1,0:T(8,128)(2,1)S(1)}, u32[]{:S(2)}, u32[]{:S(2)}) %collective-permute-start.8) | collective-permute-done | bytes 262176 | tf_op jit(solution)/shard_map/ppermute | solution.py:45
  50.7 0.6 late_product.1
  51.4 1.4 %collective-permute-done.9.second = bf16[352,256]{1,0:T(8,128)(2,1)S(1)} collective-permute-done((bf16[352,256]{1,0:T(8,128)(2,1)S(1)}, bf16[352,256]{1,0:T(8,128)(2,1)S(1)}, u32[]{:S(2)}, u32[]{:S(2)}) %collective-permute-start.9) | collective-permute-done | bytes 180256 | tf_op jit(solution)/shard_map/ppermute | solution.py:45
  52.9 1.6 %collective-permute-start.10 = (bf16[352,256]{1,0:T(8,128)(2,1)S(1)}, bf16[352,256]{1,0:T(8,128)(2,1)S(1)}, u32[]{:S(2)}, u32[]{:S(2)}) collective-permute-start(bf16[352,256]{1,0:T(8,128)(2,1)S(1)} %added.6.first), channel_id=1, source_target_pairs={{0,16},{4,20},{8,12},{12,8},{16,0},{20,4},{24,28},{28,24},{1,17},{... | collective-permute-start | bytes 540680 | tf_op jit(solution)/shard_map/ppermute | solution.py:438
  54.4 4.0 %collective-permute-done.10.second = bf16[352,256]{1,0:T(8,128)(2,1)S(1)} collective-permute-done((bf16[352,256]{1,0:T(8,128)(2,1)S(1)}, bf16[352,256]{1,0:T(8,128)(2,1)S(1)}, u32[]{:S(2)}, u32[]{:S(2)}) %collective-permute-start.10) | collective-permute-done | bytes 180256 | tf_op jit(solution)/shard_map/ppermute | solution.py:438
  58.5 1.6 %collective-permute-start.11 = (bf16[352,256]{1,0:T(8,128)(2,1)S(1)}, bf16[352,256]{1,0:T(8,128)(2,1)S(1)}, u32[]{:S(2)}, u32[]{:S(2)}) collective-permute-start(bf16[352,256]{1,0:T(8,128)(2,1)S(1)} %added.7.first), channel_id=1, source_target_pairs={{0,4},{4,0},{8,24},{12,28},{16,20},{20,16},{24,8},{28,12},{1,5},{5... | collective-permute-start | bytes 540680 | tf_op jit(solution)/shard_map/ppermute | solution.py:438
  60.1 1.6 %collective-permute-start.13 = (bf16[224,256]{1,0:T(8,128)(2,1)S(1)}, bf16[224,256]{1,0:T(8,128)(2,1)S(1)}, u32[]{:S(2)}, u32[]{:S(2)}) collective-permute-start(bf16[224,256]{1,0:T(8,128)(2,1)S(1)} %added.9.first), channel_id=1, source_target_pairs={{0,16},{4,20},{8,12},{12,8},{16,0},{20,4},{24,28},{28,24},{1,17},{... | collective-permute-start | bytes 344072 | tf_op jit(solution)/shard_map/ppermute | solution.py:438
  61.6 3.3 %collective-permute-done.13.second = bf16[224,256]{1,0:T(8,128)(2,1)S(1)} collective-permute-done((bf16[224,256]{1,0:T(8,128)(2,1)S(1)}, bf16[224,256]{1,0:T(8,128)(2,1)S(1)}, u32[]{:S(2)}, u32[]{:S(2)}) %collective-permute-start.13) | collective-permute-done | bytes 114720 | tf_op jit(solution)/shard_map/ppermute | solution.py:438
  65.0 0.6 collective-permute-start.14
  65.7 4.1 %collective-permute-done.14.second = bf16[224,256]{1,0:T(8,128)(2,1)S(1)} collective-permute-done((bf16[224,256]{1,0:T(8,128)(2,1)S(1)}, bf16[224,256]{1,0:T(8,128)(2,1)S(1)}, u32[]{:S(2)}, u32[]{:S(2)}) %collective-permute-start.14) | collective-permute-done | bytes 114720 | tf_op jit(solution)/shard_map/ppermute | solution.py:438
  69.9 1.3 %collective-permute-done.16.refs_3_ = bf16[224,256]{1,0:T(8,128)(2,1)S(1)} collective-permute-done((bf16[224,256]{1,0:T(8,128)(2,1)S(1)}, bf16[224,256]{1,0:T(8,128)(2,1)S(1)}, u32[]{:S(2)}, u32[]{:S(2)}) %collective-permute-start.16) | collective-permute-done | bytes 114720 | tf_op jit(solution)/shard_map/ppermute | solution.py:45
  71.2 1.1 %collect.1 = f32[1152,256]{1,0:T(8,128)} custom-call(s32[1]{0:T(128)} %bitcast.core, bf16[352,256]{1,0:T(8,128)(2,1)S(1)} %added.8.refs_0_, bf16[224,256]{1,0:T(8,128)(2,1)S(1)} %added.11.refs_1_, bf16[352,256]{1,0:T(8,128)(2,1)S(1)} %collective-permute-done.15.refs_2_, bf16[224,256]{1,0:T(8,128)(2,1)S(1)} %collective-permute-done.16.refs_3_), custom_call_target="tpu_custom_call" | custom-call | tf_op jit(solution)/shard_map/collect/pallas_call | solution.py:407
  (37 shorter events, 0.8 us)
Async XLA Ops:
  0.0 9.0 %collective-permute-start = (s32[2048]{0:T(1024)}, s32[2048]{0:T(1024)S(1)}, u32[]{:S(2)}, u32[]{:S(2)}) collective-permute-start(s32[2048]{0:T(1024)} %wanted.1), channel_id=1, source_target_pairs={{0,4},{4,0},{1,5},{5,1},{2,6},{6,2},{3,7},{7,3},{8,12},{12,8},{9,1... | collective-permute-start | bytes 24584 | tf_op jit(solution)/shard_map/ppermute | solution.py:45
  3.9 5.2 %collective-permute-start.1 = (bf16[128,256]{1,0:T(8,128)(2,1)S(1)}, bf16[128,256]{1,0:T(8,128)(2,1)S(1)}, u32[]{:S(2)}, u32[]{:S(2)}) collective-permute-start(bf16[128,256]{1,0:T(8,128)(2,1)S(1)} %slice_select_fusion), channel_id=1, source_target_pairs={{0,4},{4,0},{1,5},{5,1},{2,6},{6,2},{3,7},{7,3},{8,12},{12,8},{9,1... | collective-permute-start | bytes 196616 | tf_op jit(solution)/shard_map/ppermute | solution.py:22
  3.9 5.0 %copy-start.5 = (s32[8,4096]{1,0:T(8,128)S(1)}, s32[8,4096]{1,0:T(8,128)}, u32[]{:S(2)}) copy-start(s32[8,4096]{1,0:T(8,128)} %param.14) | copy-start | bytes 393220
  3.9 5.1 %copy-start = (bf16[1152,256]{1,0:T(8,128)(2,1)S(1)}, bf16[1152,256]{1,0:T(8,128)(2,1)}, u32[]{:S(2)}) copy-start(bf16[1152,256]{1,0:T(8,128)(2,1)} %weight.7) | copy-start | bytes 1769476
  4.0 5.1 %copy-start.4 = (f32[8,256]{1,0:T(8,128)S(1)}, f32[8,256]{1,0:T(8,128)}, u32[]{:S(2)}) copy-start(f32[8,256]{1,0:T(8,128)} %mixing.3) | copy-start | bytes 24580
  6.7 10.3 %collective-permute-start.2 = (bf16[512,256]{1,0:T(8,128)(2,1)}, bf16[512,256]{1,0:T(8,128)(2,1)S(1)}, u32[]{:S(2)}, u32[]{:S(2)}) collective-permute-start(bf16[512,256]{1,0:T(8,128)(2,1)} %project.2), channel_id=1, source_target_pairs={{0,1},{1,0},{2,3},{3,2},{4,5},{5,4},{6,7},{7,6},{8,9},{9,8},{10,11... | collective-permute-start | bytes 786440 | tf_op jit(solution)/shard_map/ppermute | solution.py:45
  9.1 13.8 %copy-start.3 = (s32[2048]{0:T(1024)S(1)}, s32[2048]{0:T(1024)}, u32[]{:S(2)}) copy-start(s32[2048]{0:T(1024)} %wanted.1) | copy-start | bytes 24580
  17.1 13.8 %collective-permute-start.3 = (bf16[512,256]{1,0:T(8,128)(2,1)S(1)}, bf16[512,256]{1,0:T(8,128)(2,1)S(1)}, u32[]{:S(2)}, u32[]{:S(2)}) collective-permute-start(bf16[512,256]{1,0:T(8,128)(2,1)S(1)} %get-tuple-element.27), channel_id=1, source_target_pairs={{0,1},{1,0},{2,3},{3,2},{4,5},{5,4},{6,7},{7,6},{8,9},{9,8},{10,11... | collective-permute-start | bytes 786440 | tf_op jit(solution)/shard_map/ppermute | solution.py:45
  17.9 14.2 %collective-permute-start.4 = (bf16[512,256]{1,0:T(8,128)(2,1)S(1)}, bf16[512,256]{1,0:T(8,128)(2,1)S(1)}, u32[]{:S(2)}, u32[]{:S(2)}) collective-permute-start(bf16[512,256]{1,0:T(8,128)(2,1)S(1)} %add_convert_fusion), channel_id=1, source_target_pairs={{0,3},{1,2},{2,1},{3,0},{4,7},{5,6},{6,5},{7,4},{8,11},{9,10},{10,... | collective-permute-start | bytes 786440 | tf_op jit(solution)/shard_map/ppermute | solution.py:45
  21.2 10.8 %collective-permute-start.5 = (bf16[512,256]{1,0:T(8,128)(2,1)S(1)}, bf16[512,256]{1,0:T(8,128)(2,1)S(1)}, u32[]{:S(2)}, u32[]{:S(2)}) collective-permute-start(bf16[512,256]{1,0:T(8,128)(2,1)S(1)} %get-tuple-element.29), channel_id=1, source_target_pairs={{0,4},{4,0},{1,5},{5,1},{2,6},{6,2},{3,7},{7,3},{8,12},{12,8},{9,1... | collective-permute-start | bytes 786440 | tf_op jit(solution)/shard_map/ppermute | solution.py:45
  28.9 3.1 %copy-start.1 = (s32[2048,1]{0,1:T(1,128)S(1)}, s32[2048,1]{0,1:T(1,128)}, u32[]{:S(2)}) copy-start(s32[2048,1]{0,1:T(1,128)} %param.10) | copy-start | bytes 24580
  28.9 3.1 %copy-start.2 = (f32[2048]{0:T(1024)S(1)}, f32[2048]{0:T(1024)}, u32[]{:S(2)}) copy-start(f32[2048]{0:T(1024)} %param.12) | copy-start | bytes 24580
  33.1 11.1 %collective-permute-start.6 = (bf16[512,256]{1,0:T(8,128)(2,1)S(1)}, bf16[512,256]{1,0:T(8,128)(2,1)S(1)}, u32[]{:S(2)}, u32[]{:S(2)}) collective-permute-start(bf16[512,256]{1,0:T(8,128)(2,1)S(1)} %pre_gradient.1.first), channel_id=1, source_target_pairs={{0,3},{1,2},{2,1},{3,0},{4,7},{5,6},{6,5},{7,4},{8,11},{9,10},{10,... | collective-permute-start | bytes 786440 | tf_op jit(solution)/shard_map/ppermute | solution.py:45
  33.6 13.5 %collective-permute-start.7 = (bf16[512,256]{1,0:T(8,128)(2,1)S(1)}, bf16[512,256]{1,0:T(8,128)(2,1)S(1)}, u32[]{:S(2)}, u32[]{:S(2)}) collective-permute-start(bf16[512,256]{1,0:T(8,128)(2,1)S(1)} %pre_gradient.1.first), channel_id=1, source_target_pairs={{0,1},{1,0},{2,3},{3,2},{4,5},{5,4},{6,7},{7,6},{8,9},{9,8},{10,11... | collective-permute-start | bytes 786440 | tf_op jit(solution)/shard_map/ppermute | solution.py:45
  44.2 6.5 %collective-permute-start.8 = (bf16[512,256]{1,0:T(8,128)(2,1)S(1)}, bf16[512,256]{1,0:T(8,128)(2,1)S(1)}, u32[]{:S(2)}, u32[]{:S(2)}) collective-permute-start(bf16[512,256]{1,0:T(8,128)(2,1)S(1)} %collective-permute-done.6.second), channel_id=1, source_target_pairs={{0,1},{1,0},{2,3},{3,2},{4,5},{5,4},{6,7},{7,6},{8,9},{9,8},{10,11... | collective-permute-start | bytes 786440 | tf_op jit(solution)/shard_map/ppermute | solution.py:45
  51.3 1.5 %collective-permute-start.9 = (bf16[352,256]{1,0:T(8,128)(2,1)S(1)}, bf16[352,256]{1,0:T(8,128)(2,1)S(1)}, u32[]{:S(2)}, u32[]{:S(2)}) collective-permute-start(bf16[352,256]{1,0:T(8,128)(2,1)S(1)} %get-tuple-element.34), channel_id=1, source_target_pairs={{0,8},{8,0},{16,24},{24,16},{1,9},{9,1},{17,25},{25,17},{2,10},{10... | collective-permute-start | bytes 540680 | tf_op jit(solution)/shard_map/ppermute | solution.py:45
  52.9 5.6 %collective-permute-start.10 = (bf16[352,256]{1,0:T(8,128)(2,1)S(1)}, bf16[352,256]{1,0:T(8,128)(2,1)S(1)}, u32[]{:S(2)}, u32[]{:S(2)}) collective-permute-start(bf16[352,256]{1,0:T(8,128)(2,1)S(1)} %added.6.first), channel_id=1, source_target_pairs={{0,16},{4,20},{8,12},{12,8},{16,0},{20,4},{24,28},{28,24},{1,17},{... | collective-permute-start | bytes 540680 | tf_op jit(solution)/shard_map/ppermute | solution.py:438
  54.4 5.6 %collective-permute-start.12 = (bf16[224,256]{1,0:T(8,128)(2,1)S(1)}, bf16[224,256]{1,0:T(8,128)(2,1)S(1)}, u32[]{:S(2)}, u32[]{:S(2)}) collective-permute-start(bf16[224,256]{1,0:T(8,128)(2,1)S(1)} %get-tuple-element.36), channel_id=1, source_target_pairs={{0,8},{8,0},{16,24},{24,16},{1,9},{9,1},{17,25},{25,17},{2,10},{10... | collective-permute-start | bytes 344072 | tf_op jit(solution)/shard_map/ppermute | solution.py:45
  58.5 7.1 %collective-permute-start.11 = (bf16[352,256]{1,0:T(8,128)(2,1)S(1)}, bf16[352,256]{1,0:T(8,128)(2,1)S(1)}, u32[]{:S(2)}, u32[]{:S(2)}) collective-permute-start(bf16[352,256]{1,0:T(8,128)(2,1)S(1)} %added.7.first), channel_id=1, source_target_pairs={{0,4},{4,0},{8,24},{12,28},{16,20},{20,16},{24,8},{28,12},{1,5},{5... | collective-permute-start | bytes 540680 | tf_op jit(solution)/shard_map/ppermute | solution.py:438
  60.1 4.9 %collective-permute-start.13 = (bf16[224,256]{1,0:T(8,128)(2,1)S(1)}, bf16[224,256]{1,0:T(8,128)(2,1)S(1)}, u32[]{:S(2)}, u32[]{:S(2)}) collective-permute-start(bf16[224,256]{1,0:T(8,128)(2,1)S(1)} %added.9.first), channel_id=1, source_target_pairs={{0,16},{4,20},{8,12},{12,8},{16,0},{20,4},{24,28},{28,24},{1,17},{... | collective-permute-start | bytes 344072 | tf_op jit(solution)/shard_map/ppermute | solution.py:438
  65.0 4.9 %collective-permute-start.14 = (bf16[224,256]{1,0:T(8,128)(2,1)S(1)}, bf16[224,256]{1,0:T(8,128)(2,1)S(1)}, u32[]{:S(2)}, u32[]{:S(2)}) collective-permute-start(bf16[224,256]{1,0:T(8,128)(2,1)S(1)} %added.10.first), channel_id=1, source_target_pairs={{0,4},{4,0},{8,24},{12,28},{16,20},{20,16},{24,8},{28,12},{1,5},{5... | collective-permute-start | bytes 344072 | tf_op jit(solution)/shard_map/ppermute | solution.py:438
  65.6 5.7 %collective-permute-start.15 = (bf16[352,256]{1,0:T(8,128)(2,1)S(1)}, bf16[352,256]{1,0:T(8,128)(2,1)S(1)}, u32[]{:S(2)}, u32[]{:S(2)}) collective-permute-start(bf16[352,256]{1,0:T(8,128)(2,1)S(1)} %added.8.refs_0_), channel_id=1, source_target_pairs={{0,8},{8,0},{16,24},{24,16},{1,9},{9,1},{17,25},{25,17},{2,10},{10... | collective-permute-start | bytes 540680 | tf_op jit(solution)/shard_map/ppermute | solution.py:45
  69.8 1.4 %collective-permute-start.16 = (bf16[224,256]{1,0:T(8,128)(2,1)S(1)}, bf16[224,256]{1,0:T(8,128)(2,1)S(1)}, u32[]{:S(2)}, u32[]{:S(2)}) collective-permute-start(bf16[224,256]{1,0:T(8,128)(2,1)S(1)} %added.11.refs_1_), channel_id=1, source_target_pairs={{0,8},{8,0},{16,24},{24,16},{1,9},{9,1},{17,25},{25,17},{2,10},{10... | collective-permute-start | bytes 344072 | tf_op jit(solution)/shard_map/ppermute | solution.py:45

commit v19 on v17

--- a/solution.py
+++ b/solution.py
@@ -265,17 +265,18 @@
 
     group = 32
     offset = start - first_name
+    pixels = table.reshape(table.shape[0] // 2, 2, half)
 
     def body(turn, carry):
         base = turn * group
         totals = []
         for n in range(group):
             pixel = names[offset + base + n]
-            terms = [table[pl.ds(2 * (pixel + HALO), 2), :]]
+            terms = [pixels[pixel + HALO]]
             for k in range(NEIGH // 2):
                 pair = near[k * tile_rows + pixel]
                 for place, scale in ((pair & 0xFFFF, k), (pair >> 16, k + NEIGH // 2)):
-                    terms.append(table[pl.ds(place, 2), :] * scales[scale])
+                    terms.append(pixels[place] * scales[scale])
             while len(terms) > 1:
                 pairs = [x + y for x, y in zip(terms[::2], terms[1::2])]
                 terms = pairs + terms[len(terms) // 2 * 2 :]
@@ -422,22 +423,6 @@
     )(first, second)
 
 
-def hand_on_kernel(value, _, out):
-    out[...] = value[...]
-
-
-def handed_on(value, after):
-    spec = pl.BlockSpec(memory_space=pltpu.VMEM)
-    return pl.pallas_call(
-        hand_on_kernel,
-        out_shape=jax.ShapeDtypeStruct(value.shape, value.dtype),
-        in_specs=[spec, spec],
-        out_specs=spec,
-        compiler_params=memory(16),
-        name="handed_on",
-    )(value, after)
-
-
 def sum_over_panels(core, parts, received):
     both = ("obs", "pix")
     parts = [added(part, other) for part, other in zip(parts, received)]
@@ -456,7 +441,7 @@
     first_row = chan * quarter
 
     near_first = swap(project(spectra, enc_weight, chan, (2,), LARGE + 4)[0], "chan", 1)
-    places = (adjoint - (tile * tile_rows - HALO)) * 2
+    places = adjoint - (tile * tile_rows - HALO)
     places = (places[: NEIGH // 2] | (places[NEIGH // 2 :] << 16)).reshape(-1)
 
     above, below = edges(cotangent, "pix", HALO)
@@ -476,7 +461,7 @@
     passed_on = (shared.astype(jnp.float32) + near_first.astype(jnp.float32)).astype(jnp.bfloat16)
     passed_on, send, rows, later = lax.optimization_barrier((passed_on, send, rows, chan))
     far = swap(passed_on, "chan", 3)
-    near = swap(handed_on(send, passed_on), "chan", 1)
+    near = swap(send, "chan", 1)
     (keep,) = project(*rest, later, (0,), LARGE)
     if paired:
         answers = swap(rows, "pix", 1)

time: 70.1 us -> 68.9 us (0.983)
  Pallas kernels: 24.6 us -> 26.8 us
  starting transfers between devices: 20.1 us -> 18.4 us
  waiting for transfers between devices: 23.6 us -> 21.9 us
    pallas_call x2, Pallas kernels: 14 us -> 16.3 us  [pixel_rows(): pl.pallas_call(functools.partial(pixel_kernel, count, bits), out_shape=(j...]
    ppermute x12, waiting for transfers between devices: 17 us -> 15.2 us  [swap(): return lax.ppermute(value, axis, [(i, i ^ bit) for i in range(size)])]
    ppermute x12, starting transfers between devices: 14.8 us -> 13.2 us  [swap(): return lax.ppermute(value, axis, [(i, i ^ bit) for i in range(size)])]
  transfers between devices with their start and end apart: 17 -> 17, of which waited for: 8 -> 8; matrix products, arithmetic and copies ran while one was open for 2% -> 2% of each run, Pallas kernels for 31% -> 35%
where the time goes in v19:
time: 68.9 us; the launch traced here: 68.6 us
  Pallas kernels  26.8 us (39%)
  waiting for transfers between devices  21.9 us (32%)
  starting transfers between devices  18.4 us (27%)
  other arithmetic  1.21 us (2%)
    pallas_call x2, Pallas kernels, pixel_rows(): pl.pallas_call(functools.partial(pixel_kernel, count, bits), out_shape=(j...  16.3 us
    ppermute x12, waiting for transfers between devices, swap(): return lax.ppermute(value, axis, [(i, i ^ bit) for i in range(size)])  15.2 us
    ppermute x12, starting transfers between devices, swap(): return lax.ppermute(value, axis, [(i, i ^ bit) for i in range(size)])  13.2 us
    ppermute x4, waiting for transfers between devices, sum_over_panels(): parts = [added(part, lax.ppermute(part, both, perm)) for part in parts]  6.69 us
    ppermute x4, starting transfers between devices, sum_over_panels(): parts = [added(part, lax.ppermute(part, both, perm)) for part in parts]  5.12 us
    pallas_call x2, Pallas kernels, project(): pl.pallas_call(functools.partial(project_kernel, bits), out_shape=(jax.Sh...  4.67 us
    pallas_call x1, Pallas kernels, early_product(): pl.pallas_call(early_kernel, out_shape=(jax.ShapeDtypeStruct((depth, widt...  2.49 us
  transfers between devices with their start and end apart: 17, of which 8 were waited for; matrix products, arithmetic and copies ran while one was open for 2% of the time, Pallas kernels for 35%

profile of v19, /device:TPU:0, one launch (start us, length us, event | category | flops | bytes accessed | tf_op | source)
XLA Modules:
  0.0 68.6 jit_solution(5579684798995586735)
XLA Ops:
  0.0 3.0 %collective-permute-start = (s32[2048]{0:T(1024)}, s32[2048]{0:T(1024)S(1)}, u32[]{:S(2)}, u32[]{:S(2)}) collective-permute-start(s32[2048]{0:T(1024)} %wanted.1), channel_id=1, source_target_pairs={{0,4},{4,0},{1,5},{5,1},{2,6},{6,2},{3,7},{7,3},{8,12},{12,8},{9,1... | collective-permute-start | bytes 24584 | tf_op jit(solution)/shard_map/ppermute | solution.py:45
  3.0 0.9 %slice_select_fusion = bf16[128,256]{1,0:T(8,128)(2,1)S(1)} fusion(bf16[4096,256]{1,0:T(8,128)(2,1)} %cotangent.3, pred[]{:T(512)S(6)} %eq.3), kind=kLoop, calls=%fused_computation.4 | loop fusion | flops 32768 | bytes 196609 | tf_op jit(solution)/shard_map/jit(_where)/select_n | solution.py:22
  4.0 2.7 %project.2 = bf16[512,256]{1,0:T(8,128)(2,1)} custom-call(s32[1]{0:T(128)} %bitcast.1.chan, bf16[2048,1152]{1,0:T(8,128)(2,1)} %spectra.9, bf16[1152,256]{1,0:T(8,128)(2,1)} %weight.7), custom_call_target="tpu_custom_call" | custom-call | flops 301989888 | bytes 2031616 | tf_op jit(solution)/shard_map/project/pallas_call | solution.py:88
  6.7 2.1 %collective-permute-start.2 = (bf16[512,256]{1,0:T(8,128)(2,1)}, bf16[512,256]{1,0:T(8,128)(2,1)S(1)}, u32[]{:S(2)}, u32[]{:S(2)}) collective-permute-start(bf16[512,256]{1,0:T(8,128)(2,1)} %project.2), channel_id=1, source_target_pairs={{0,1},{1,0},{2,3},{3,2},{4,5},{5,4},{6,7},{7,6},{8,9},{9,8},{10,11... | collective-permute-start | bytes 786440 | tf_op jit(solution)/shard_map/ppermute | solution.py:45
  8.8 0.1 pad_add_fusion.1.where
  8.9 0.1 pad_add_fusion.where
  9.1 9.0 %pixel_rows.2 = (bf16[512,256]{1,0:T(8,128)(2,1)S(1)}, bf16[512,256]{1,0:T(8,128)(2,1)S(1)}, bf16[512,256]{1,0:T(8,128)(2,1)S(1)}) custom-call(s32[2]{0:T(128)S(1)} %pad_add_fusion.1.where, s32[16384]{0:T(1024)S(1)} %bitcast.11, s32[2048]{0:T(1024)S(1)} %collective-permute-done.wanted, bf16[4096,256]{1,0:T(8,128)(2,1)} %cotangent.3, ...), custom_call_target="tpu_custom_call" | custom-call | flops 17179869184 | bytes 4194304 | tf_op jit(solution)/shard_map/pixel_rows/pallas_call | solution.py:304
  18.2 0.8 %collective-permute-start.3 = (bf16[512,256]{1,0:T(8,128)(2,1)S(1)}, bf16[512,256]{1,0:T(8,128)(2,1)S(1)}, u32[]{:S(2)}, u32[]{:S(2)}) collective-permute-start(bf16[512,256]{1,0:T(8,128)(2,1)S(1)} %get-tuple-element.27), channel_id=1, source_target_pairs={{0,1},{1,0},{2,3},{3,2},{4,5},{5,4},{6,7},{7,6},{8,9},{9,8},{10,11... | collective-permute-start | bytes 786440 | tf_op jit(solution)/shard_map/ppermute | solution.py:45
  19.0 3.4 %collective-permute-start.4 = (bf16[512,256]{1,0:T(8,128)(2,1)S(1)}, bf16[512,256]{1,0:T(8,128)(2,1)S(1)}, u32[]{:S(2)}, u32[]{:S(2)}) collective-permute-start(bf16[512,256]{1,0:T(8,128)(2,1)S(1)} %add_convert_fusion), channel_id=1, source_target_pairs={{0,3},{1,2},{2,1},{3,0},{4,7},{5,6},{6,5},{7,4},{8,11},{9,10},{10,... | collective-permute-start | bytes 786440 | tf_op jit(solution)/shard_map/ppermute | solution.py:45
  22.3 1.5 %collective-permute-start.5 = (bf16[512,256]{1,0:T(8,128)(2,1)S(1)}, bf16[512,256]{1,0:T(8,128)(2,1)S(1)}, u32[]{:S(2)}, u32[]{:S(2)}) collective-permute-start(bf16[512,256]{1,0:T(8,128)(2,1)S(1)} %get-tuple-element.29), channel_id=1, source_target_pairs={{0,4},{4,0},{1,5},{5,1},{2,6},{6,2},{3,7},{7,3},{8,12},{12,8},{9,1... | collective-permute-start | bytes 786440 | tf_op jit(solution)/shard_map/ppermute | solution.py:45
  23.9 7.2 %pixel_rows.3.mine = bf16[512,256]{1,0:T(8,128)(2,1)S(1)} custom-call(s32[2]{0:T(128)S(1)} %pad_add_fusion.2.where, s32[16384]{0:T(1024)S(1)} %bitcast.12, s32[2048]{0:T(1024)S(1)} %copy-done.3, bf16[4096,256]{1,0:T(8,128)(2,1)} %cotangent.3, bf16[128,256]{1,0:T(8,128)(2,1)S(1)} %collective-permute-done.1.above.below, ...), custom_call_target="tpu_custom_call" | custom-call | flops 17179869184 | bytes 4194304 | tf_op jit(solution)/shard_map/pixel_rows/pallas_call | solution.py:304
  31.2 1.9 %project.3.keep = bf16[512,256]{1,0:T(8,128)(2,1)S(1)} custom-call(s32[1]{0:T(128)} %bitcast.4.chan, bf16[2048,1152]{1,0:T(8,128)(2,1)} %spectra.9, bf16[1152,256]{1,0:T(8,128)(2,1)S(1)} %copy-done), custom_call_target="tpu_custom_call" | custom-call | flops 301989888 | bytes 2031616 | tf_op jit(solution)/shard_map/project/pallas_call | solution.py:88
  33.2 1.0 %pre_gradient.1.first = bf16[512,256]{1,0:T(8,128)(2,1)S(1)} custom-call(s32[2]{0:T(128)S(1)} %pad_add_fusion.where, bf16[512,256]{1,0:T(8,128)(2,1)S(1)} %project.3.keep, bf16[512,256]{1,0:T(8,128)(2,1)S(1)} %collective-permute-done.3.near, bf16[512,256]{1,0:T(8,128)(2,1)S(1)} %collective-permute-done.4.far, s32[16,128]{1,0:T(8,128)S(1)} %bitcast.13, ...), custom_call_target="tpu_custom_call" | custom-call | tf_op jit(solution)/shard_map/pre_gradient/pallas_call | solution.py:376
  34.2 0.5 collective-permute-start.6
  34.7 0.8 %collective-permute-start.7 = (bf16[512,256]{1,0:T(8,128)(2,1)S(1)}, bf16[512,256]{1,0:T(8,128)(2,1)S(1)}, u32[]{:S(2)}, u32[]{:S(2)}) collective-permute-start(bf16[512,256]{1,0:T(8,128)(2,1)S(1)} %pre_gradient.1.first), channel_id=1, source_target_pairs={{0,1},{1,0},{2,3},{3,2},{4,5},{5,4},{6,7},{7,6},{8,9},{9,8},{10,11... | collective-permute-start | bytes 786440 | tf_op jit(solution)/shard_map/ppermute | solution.py:45
  35.5 9.8 %collective-permute-done.6.second = bf16[512,256]{1,0:T(8,128)(2,1)S(1)} collective-permute-done((bf16[512,256]{1,0:T(8,128)(2,1)S(1)}, bf16[512,256]{1,0:T(8,128)(2,1)S(1)}, u32[]{:S(2)}, u32[]{:S(2)}) %collective-permute-start.6) | collective-permute-done | bytes 262176 | tf_op jit(solution)/shard_map/ppermute | solution.py:45
  45.3 0.4 collective-permute-start.8
  45.7 2.5 %early_product.1 = (f32[1152,256]{1,0:T(8,128)S(1)}, bf16[512,1152]{1,0:T(8,128)(2,1)S(1)}, bf16[512,1152]{1,0:T(8,128)(2,1)S(1)}) custom-call(s32[1]{0:T(128)} %bitcast.1.chan, bf16[2048,1152]{1,0:T(8,128)(2,1)} %spectra.9, bf16[512,256]{1,0:T(8,128)(2,1)S(1)} %pre_gradient.1.first, bf16[512,256]{1,0:T(8,128)(2,1)S(1)} %collective-permute-done.6.second), custom_call_target="tpu_custom_call" | custom-call | flops 603979776 | bytes 5898240 | tf_op jit(solution)/shard_map/early_product/pallas_call | solution.py:135
  48.3 0.5 more_product.1.before
  48.8 3.2 %collective-permute-done.8.rows = bf16[512,256]{1,0:T(8,128)(2,1)S(1)} collective-permute-done((bf16[512,256]{1,0:T(8,128)(2,1)S(1)}, bf16[512,256]{1,0:T(8,128)(2,1)S(1)}, u32[]{:S(2)}, u32[]{:S(2)}) %collective-permute-start.8) | collective-permute-done | bytes 262176 | tf_op jit(solution)/shard_map/ppermute | solution.py:45
  51.9 0.6 late_product.1
  52.6 0.5 collective-permute-start.12
  53.1 0.9 %collective-permute-done.9.second = bf16[288,256]{1,0:T(8,128)(2,1)S(1)} collective-permute-done((bf16[288,256]{1,0:T(8,128)(2,1)S(1)}, bf16[288,256]{1,0:T(8,128)(2,1)S(1)}, u32[]{:S(2)}, u32[]{:S(2)}) %collective-permute-start.9) | collective-permute-done | bytes 147488 | tf_op jit(solution)/shard_map/ppermute | solution.py:45
  54.0 1.6 %collective-permute-start.10 = (bf16[288,256]{1,0:T(8,128)(2,1)S(1)}, bf16[288,256]{1,0:T(8,128)(2,1)S(1)}, u32[]{:S(2)}, u32[]{:S(2)}) collective-permute-start(bf16[288,256]{1,0:T(8,128)(2,1)S(1)} %added.6.first), channel_id=1, source_target_pairs={{0,16},{4,20},{8,12},{12,8},{16,0},{20,4},{24,28},{28,24},{1,17},{... | collective-permute-start | bytes 442376 | tf_op jit(solution)/shard_map/ppermute | solution.py:431
  55.6 0.6 collective-permute-start.13
  56.2 3.0 %collective-permute-done.10.second = bf16[288,256]{1,0:T(8,128)(2,1)S(1)} collective-permute-done((bf16[288,256]{1,0:T(8,128)(2,1)S(1)}, bf16[288,256]{1,0:T(8,128)(2,1)S(1)}, u32[]{:S(2)}, u32[]{:S(2)}) %collective-permute-start.10) | collective-permute-done | bytes 147488 | tf_op jit(solution)/shard_map/ppermute | solution.py:431
  59.3 1.5 %collective-permute-start.11 = (bf16[288,256]{1,0:T(8,128)(2,1)S(1)}, bf16[288,256]{1,0:T(8,128)(2,1)S(1)}, u32[]{:S(2)}, u32[]{:S(2)}) collective-permute-start(bf16[288,256]{1,0:T(8,128)(2,1)S(1)} %added.7.first), channel_id=1, source_target_pairs={{0,4},{4,0},{8,24},{12,28},{16,20},{20,16},{24,8},{28,12},{1,5},{5... | collective-permute-start | bytes 442376 | tf_op jit(solution)/shard_map/ppermute | solution.py:431
  60.8 1.5 %collective-permute-start.14 = (bf16[288,256]{1,0:T(8,128)(2,1)S(1)}, bf16[288,256]{1,0:T(8,128)(2,1)S(1)}, u32[]{:S(2)}, u32[]{:S(2)}) collective-permute-start(bf16[288,256]{1,0:T(8,128)(2,1)S(1)} %added.10.first), channel_id=1, source_target_pairs={{0,4},{4,0},{8,24},{12,28},{16,20},{20,16},{24,8},{28,12},{1,5},{5... | collective-permute-start | bytes 442376 | tf_op jit(solution)/shard_map/ppermute | solution.py:431
  62.3 2.1 %collective-permute-done.11.second = bf16[288,256]{1,0:T(8,128)(2,1)S(1)} collective-permute-done((bf16[288,256]{1,0:T(8,128)(2,1)S(1)}, bf16[288,256]{1,0:T(8,128)(2,1)S(1)}, u32[]{:S(2)}, u32[]{:S(2)}) %collective-permute-start.11) | collective-permute-done | bytes 147488 | tf_op jit(solution)/shard_map/ppermute | solution.py:431
  64.6 1.5 %collective-permute-done.14.second = bf16[288,256]{1,0:T(8,128)(2,1)S(1)} collective-permute-done((bf16[288,256]{1,0:T(8,128)(2,1)S(1)}, bf16[288,256]{1,0:T(8,128)(2,1)S(1)}, u32[]{:S(2)}, u32[]{:S(2)}) %collective-permute-start.14) | collective-permute-done | bytes 147488 | tf_op jit(solution)/shard_map/ppermute | solution.py:431
  66.2 1.3 %collective-permute-done.16.refs_3_ = bf16[288,256]{1,0:T(8,128)(2,1)S(1)} collective-permute-done((bf16[288,256]{1,0:T(8,128)(2,1)S(1)}, bf16[288,256]{1,0:T(8,128)(2,1)S(1)}, u32[]{:S(2)}, u32[]{:S(2)}) %collective-permute-start.16) | collective-permute-done | bytes 147488 | tf_op jit(solution)/shard_map/ppermute | solution.py:45
  67.5 1.1 %collect.1 = f32[1152,256]{1,0:T(8,128)} custom-call(s32[1]{0:T(128)} %bitcast.core, bf16[288,256]{1,0:T(8,128)(2,1)S(1)} %added.8.refs_0_, bf16[288,256]{1,0:T(8,128)(2,1)S(1)} %added.11.refs_1_, bf16[288,256]{1,0:T(8,128)(2,1)S(1)} %collective-permute-done.15.refs_2_, bf16[288,256]{1,0:T(8,128)(2,1)S(1)} %collective-permute-done.16.refs_3_), custom_call_target="tpu_custom_call" | custom-call | tf_op jit(solution)/shard_map/collect/pallas_call | solution.py:400
  (37 shorter events, 0.8 us)
Async XLA Ops:
  0.0 9.0 %collective-permute-start = (s32[2048]{0:T(1024)}, s32[2048]{0:T(1024)S(1)}, u32[]{:S(2)}, u32[]{:S(2)}) collective-permute-start(s32[2048]{0:T(1024)} %wanted.1), channel_id=1, source_target_pairs={{0,4},{4,0},{1,5},{5,1},{2,6},{6,2},{3,7},{7,3},{8,12},{12,8},{9,1... | collective-permute-start | bytes 24584 | tf_op jit(solution)/shard_map/ppermute | solution.py:45
  3.9 5.2 %collective-permute-start.1 = (bf16[128,256]{1,0:T(8,128)(2,1)S(1)}, bf16[128,256]{1,0:T(8,128)(2,1)S(1)}, u32[]{:S(2)}, u32[]{:S(2)}) collective-permute-start(bf16[128,256]{1,0:T(8,128)(2,1)S(1)} %slice_select_fusion), channel_id=1, source_target_pairs={{0,4},{4,0},{1,5},{5,1},{2,6},{6,2},{3,7},{7,3},{8,12},{12,8},{9,1... | collective-permute-start | bytes 196616 | tf_op jit(solution)/shard_map/ppermute | solution.py:22
  3.9 5.0 %copy-start.5 = (s32[8,4096]{1,0:T(8,128)S(1)}, s32[8,4096]{1,0:T(8,128)}, u32[]{:S(2)}) copy-start(s32[8,4096]{1,0:T(8,128)} %param.14) | copy-start | bytes 393220
  3.9 5.1 %copy-start = (bf16[1152,256]{1,0:T(8,128)(2,1)S(1)}, bf16[1152,256]{1,0:T(8,128)(2,1)}, u32[]{:S(2)}) copy-start(bf16[1152,256]{1,0:T(8,128)(2,1)} %weight.7) | copy-start | bytes 1769476
  4.0 5.1 %copy-start.4 = (f32[8,256]{1,0:T(8,128)S(1)}, f32[8,256]{1,0:T(8,128)}, u32[]{:S(2)}) copy-start(f32[8,256]{1,0:T(8,128)} %mixing.3) | copy-start | bytes 24580
  6.7 11.4 %collective-permute-start.2 = (bf16[512,256]{1,0:T(8,128)(2,1)}, bf16[512,256]{1,0:T(8,128)(2,1)S(1)}, u32[]{:S(2)}, u32[]{:S(2)}) collective-permute-start(bf16[512,256]{1,0:T(8,128)(2,1)} %project.2), channel_id=1, source_target_pairs={{0,1},{1,0},{2,3},{3,2},{4,5},{5,4},{6,7},{7,6},{8,9},{9,8},{10,11... | collective-permute-start | bytes 786440 | tf_op jit(solution)/shard_map/ppermute | solution.py:45
  9.1 14.9 %copy-start.3 = (s32[2048]{0:T(1024)S(1)}, s32[2048]{0:T(1024)}, u32[]{:S(2)}) copy-start(s32[2048]{0:T(1024)} %wanted.1) | copy-start | bytes 24580
  18.2 14.9 %collective-permute-start.3 = (bf16[512,256]{1,0:T(8,128)(2,1)S(1)}, bf16[512,256]{1,0:T(8,128)(2,1)S(1)}, u32[]{:S(2)}, u32[]{:S(2)}) collective-permute-start(bf16[512,256]{1,0:T(8,128)(2,1)S(1)} %get-tuple-element.27), channel_id=1, source_target_pairs={{0,1},{1,0},{2,3},{3,2},{4,5},{5,4},{6,7},{7,6},{8,9},{9,8},{10,11... | collective-permute-start | bytes 786440 | tf_op jit(solution)/shard_map/ppermute | solution.py:45
  19.0 14.2 %collective-permute-start.4 = (bf16[512,256]{1,0:T(8,128)(2,1)S(1)}, bf16[512,256]{1,0:T(8,128)(2,1)S(1)}, u32[]{:S(2)}, u32[]{:S(2)}) collective-permute-start(bf16[512,256]{1,0:T(8,128)(2,1)S(1)} %add_convert_fusion), channel_id=1, source_target_pairs={{0,3},{1,2},{2,1},{3,0},{4,7},{5,6},{6,5},{7,4},{8,11},{9,10},{10,... | collective-permute-start | bytes 786440 | tf_op jit(solution)/shard_map/ppermute | solution.py:45
  22.3 10.8 %collective-permute-start.5 = (bf16[512,256]{1,0:T(8,128)(2,1)S(1)}, bf16[512,256]{1,0:T(8,128)(2,1)S(1)}, u32[]{:S(2)}, u32[]{:S(2)}) collective-permute-start(bf16[512,256]{1,0:T(8,128)(2,1)S(1)} %get-tuple-element.29), channel_id=1, source_target_pairs={{0,4},{4,0},{1,5},{5,1},{2,6},{6,2},{3,7},{7,3},{8,12},{12,8},{9,1... | collective-permute-start | bytes 786440 | tf_op jit(solution)/shard_map/ppermute | solution.py:45
  31.2 2.0 %copy-start.1 = (s32[2048,1]{0,1:T(1,128)S(1)}, s32[2048,1]{0,1:T(1,128)}, u32[]{:S(2)}) copy-start(s32[2048,1]{0,1:T(1,128)} %param.10) | copy-start | bytes 24580
  31.2 2.0 %copy-start.2 = (f32[2048]{0:T(1024)S(1)}, f32[2048]{0:T(1024)}, u32[]{:S(2)}) copy-start(f32[2048]{0:T(1024)} %param.12) | copy-start | bytes 24580
  34.2 11.1 %collective-permute-start.6 = (bf16[512,256]{1,0:T(8,128)(2,1)S(1)}, bf16[512,256]{1,0:T(8,128)(2,1)S(1)}, u32[]{:S(2)}, u32[]{:S(2)}) collective-permute-start(bf16[512,256]{1,0:T(8,128)(2,1)S(1)} %pre_gradient.1.first), channel_id=1, source_target_pairs={{0,3},{1,2},{2,1},{3,0},{4,7},{5,6},{6,5},{7,4},{8,11},{9,10},{10,... | collective-permute-start | bytes 786440 | tf_op jit(solution)/shard_map/ppermute | solution.py:45
  34.7 13.6 %collective-permute-start.7 = (bf16[512,256]{1,0:T(8,128)(2,1)S(1)}, bf16[512,256]{1,0:T(8,128)(2,1)S(1)}, u32[]{:S(2)}, u32[]{:S(2)}) collective-permute-start(bf16[512,256]{1,0:T(8,128)(2,1)S(1)} %pre_gradient.1.first), channel_id=1, source_target_pairs={{0,1},{1,0},{2,3},{3,2},{4,5},{5,4},{6,7},{7,6},{8,9},{9,8},{10,11... | collective-permute-start | bytes 786440 | tf_op jit(solution)/shard_map/ppermute | solution.py:45
  45.3 6.6 %collective-permute-start.8 = (bf16[512,256]{1,0:T(8,128)(2,1)S(1)}, bf16[512,256]{1,0:T(8,128)(2,1)S(1)}, u32[]{:S(2)}, u32[]{:S(2)}) collective-permute-start(bf16[512,256]{1,0:T(8,128)(2,1)S(1)} %collective-permute-done.6.second), channel_id=1, source_target_pairs={{0,1},{1,0},{2,3},{3,2},{4,5},{5,4},{6,7},{7,6},{8,9},{9,8},{10,11... | collective-permute-start | bytes 786440 | tf_op jit(solution)/shard_map/ppermute | solution.py:45
  52.5 1.4 %collective-permute-start.9 = (bf16[288,256]{1,0:T(8,128)(2,1)S(1)}, bf16[288,256]{1,0:T(8,128)(2,1)S(1)}, u32[]{:S(2)}, u32[]{:S(2)}) collective-permute-start(bf16[288,256]{1,0:T(8,128)(2,1)S(1)} %get-tuple-element.34), channel_id=1, source_target_pairs={{0,8},{8,0},{16,24},{24,16},{1,9},{9,1},{17,25},{25,17},{2,10},{10... | collective-permute-start | bytes 442376 | tf_op jit(solution)/shard_map/ppermute | solution.py:45
  52.6 2.9 %collective-permute-start.12 = (bf16[288,256]{1,0:T(8,128)(2,1)S(1)}, bf16[288,256]{1,0:T(8,128)(2,1)S(1)}, u32[]{:S(2)}, u32[]{:S(2)}) collective-permute-start(bf16[288,256]{1,0:T(8,128)(2,1)S(1)} %get-tuple-element.36), channel_id=1, source_target_pairs={{0,8},{8,0},{16,24},{24,16},{1,9},{9,1},{17,25},{25,17},{2,10},{10... | collective-permute-start | bytes 442376 | tf_op jit(solution)/shard_map/ppermute | solution.py:45
  54.0 5.2 %collective-permute-start.10 = (bf16[288,256]{1,0:T(8,128)(2,1)S(1)}, bf16[288,256]{1,0:T(8,128)(2,1)S(1)}, u32[]{:S(2)}, u32[]{:S(2)}) collective-permute-start(bf16[288,256]{1,0:T(8,128)(2,1)S(1)} %added.6.first), channel_id=1, source_target_pairs={{0,16},{4,20},{8,12},{12,8},{16,0},{20,4},{24,28},{28,24},{1,17},{... | collective-permute-start | bytes 442376 | tf_op jit(solution)/shard_map/ppermute | solution.py:431
  55.6 5.2 %collective-permute-start.13 = (bf16[288,256]{1,0:T(8,128)(2,1)S(1)}, bf16[288,256]{1,0:T(8,128)(2,1)S(1)}, u32[]{:S(2)}, u32[]{:S(2)}) collective-permute-start(bf16[288,256]{1,0:T(8,128)(2,1)S(1)} %added.9.first), channel_id=1, source_target_pairs={{0,16},{4,20},{8,12},{12,8},{16,0},{20,4},{24,28},{28,24},{1,17},{... | collective-permute-start | bytes 442376 | tf_op jit(solution)/shard_map/ppermute | solution.py:431
  59.3 5.2 %collective-permute-start.11 = (bf16[288,256]{1,0:T(8,128)(2,1)S(1)}, bf16[288,256]{1,0:T(8,128)(2,1)S(1)}, u32[]{:S(2)}, u32[]{:S(2)}) collective-permute-start(bf16[288,256]{1,0:T(8,128)(2,1)S(1)} %added.7.first), channel_id=1, source_target_pairs={{0,4},{4,0},{8,24},{12,28},{16,20},{20,16},{24,8},{28,12},{1,5},{5... | collective-permute-start | bytes 442376 | tf_op jit(solution)/shard_map/ppermute | solution.py:431
  60.8 5.2 %collective-permute-start.14 = (bf16[288,256]{1,0:T(8,128)(2,1)S(1)}, bf16[288,256]{1,0:T(8,128)(2,1)S(1)}, u32[]{:S(2)}, u32[]{:S(2)}) collective-permute-start(bf16[288,256]{1,0:T(8,128)(2,1)S(1)} %added.10.first), channel_id=1, source_target_pairs={{0,4},{4,0},{8,24},{12,28},{16,20},{20,16},{24,8},{28,12},{1,5},{5... | collective-permute-start | bytes 442376 | tf_op jit(solution)/shard_map/ppermute | solution.py:431
  64.5 1.7 %collective-permute-start.15 = (bf16[288,256]{1,0:T(8,128)(2,1)S(1)}, bf16[288,256]{1,0:T(8,128)(2,1)S(1)}, u32[]{:S(2)}, u32[]{:S(2)}) collective-permute-start(bf16[288,256]{1,0:T(8,128)(2,1)S(1)} %added.8.refs_0_), channel_id=1, source_target_pairs={{0,8},{8,0},{16,24},{24,16},{1,9},{9,1},{17,25},{25,17},{2,10},{10... | collective-permute-start | bytes 442376 | tf_op jit(solution)/shard_map/ppermute | solution.py:45
  66.1 1.4 %collective-permute-start.16 = (bf16[288,256]{1,0:T(8,128)(2,1)S(1)}, bf16[288,256]{1,0:T(8,128)(2,1)S(1)}, u32[]{:S(2)}, u32[]{:S(2)}) collective-permute-start(bf16[288,256]{1,0:T(8,128)(2,1)S(1)} %added.11.refs_1_), channel_id=1, source_target_pairs={{0,8},{8,0},{16,24},{24,16},{1,9},{9,1},{17,25},{25,17},{2,10},{10... | collective-permute-start | bytes 442376 | tf_op jit(solution)/shard_map/ppermute | solution.py:45

commit v20 on v19

--- a/solution.py
+++ b/solution.py
@@ -265,18 +265,17 @@
 
     group = 32
     offset = start - first_name
-    pixels = table.reshape(table.shape[0] // 2, 2, half)
 
     def body(turn, carry):
         base = turn * group
         totals = []
         for n in range(group):
             pixel = names[offset + base + n]
-            terms = [pixels[pixel + HALO]]
+            terms = [table[pl.ds(2 * (pixel + HALO), 2), :]]
             for k in range(NEIGH // 2):
                 pair = near[k * tile_rows + pixel]
                 for place, scale in ((pair & 0xFFFF, k), (pair >> 16, k + NEIGH // 2)):
-                    terms.append(pixels[place] * scales[scale])
+                    terms.append(table[pl.ds(place, 2), :] * scales[scale])
             while len(terms) > 1:
                 pairs = [x + y for x, y in zip(terms[::2], terms[1::2])]
                 terms = pairs + terms[len(terms) // 2 * 2 :]
@@ -441,7 +440,7 @@
     first_row = chan * quarter
 
     near_first = swap(project(spectra, enc_weight, chan, (2,), LARGE + 4)[0], "chan", 1)
-    places = adjoint - (tile * tile_rows - HALO)
+    places = (adjoint - (tile * tile_rows - HALO)) * 2
     places = (places[: NEIGH // 2] | (places[NEIGH // 2 :] << 16)).reshape(-1)
 
     above, below = edges(cotangent, "pix", HALO)
@@ -462,11 +461,11 @@
     passed_on, send, rows, later = lax.optimization_barrier((passed_on, send, rows, chan))
     far = swap(passed_on, "chan", 3)
     near = swap(send, "chan", 1)
-    (keep,) = project(*rest, later, (0,), LARGE)
     if paired:
         answers = swap(rows, "pix", 1)
-        (mine,) = pixel_rows(*pixels, pix_local, later * quarter, count, *rest, later, ())
+        mine, keep = pixel_rows(*pixels, pix_local, later * quarter, count, *rest, later, (0,))
     else:
+        (keep,) = project(*rest, later, (0,), LARGE)
         answers = lax.all_to_all(
             rows.reshape(tile_count, capacity, -1), "pix", split_axis=0, concat_axis=0, tiled=True
         )

time: 68.9 us -> 67.6 us (0.981)
  Pallas kernels: 26.8 us -> 23.4 us
  starting transfers between devices: 18.4 us -> 19.6 us
  waiting for transfers between devices: 21.9 us -> 23 us
    pallas_call x2 -> x1, Pallas kernels: 4.67 us -> 2.74 us  [project(): pl.pallas_call(functools.partial(project_kernel, bits), out_shape=(jax.Sh...]
    pallas_call x2, Pallas kernels: 16.3 us -> 14.7 us  [pixel_rows(): pl.pallas_call(functools.partial(pixel_kernel, count, bits), out_shape=(j...]
    ppermute x12, waiting for transfers between devices: 15.2 us -> 16.4 us  [swap(): return lax.ppermute(value, axis, [(i, i ^ bit) for i in range(size)])]
    ppermute x12, starting transfers between devices: 13.2 us -> 14.2 us  [swap(): return lax.ppermute(value, axis, [(i, i ^ bit) for i in range(size)])]
  transfers between devices with their start and end apart: 17 -> 17, of which waited for: 8 -> 9; matrix products, arithmetic and copies ran while one was open for 2% -> 2% of each run, Pallas kernels for 35% -> 31%
where the time goes in v20:
time: 67.6 us; the launch traced here: 67.4 us
  Pallas kernels  23.4 us (35%)
  waiting for transfers between devices  23 us (34%)
  starting transfers between devices  19.6 us (29%)
  other arithmetic  1.21 us (2%)
    ppermute x12, waiting for transfers between devices, swap(): return lax.ppermute(value, axis, [(i, i ^ bit) for i in range(size)])  16.4 us
    pallas_call x2, Pallas kernels, pixel_rows(): pl.pallas_call(functools.partial(pixel_kernel, count, bits), out_shape=(j...  14.7 us
    ppermute x12, starting transfers between devices, swap(): return lax.ppermute(value, axis, [(i, i ^ bit) for i in range(size)])  14.2 us
    ppermute x4, waiting for transfers between devices, sum_over_panels(): parts = [added(part, lax.ppermute(part, both, perm)) for part in parts]  6.56 us
    ppermute x4, starting transfers between devices, sum_over_panels(): parts = [added(part, lax.ppermute(part, both, perm)) for part in parts]  5.28 us
    pallas_call x1, Pallas kernels, project(): pl.pallas_call(functools.partial(project_kernel, bits), out_shape=(jax.Sh...  2.74 us
    pallas_call x1, Pallas kernels, early_product(): pl.pallas_call(early_kernel, out_shape=(jax.ShapeDtypeStruct((depth, widt...  2.49 us
  transfers between devices with their start and end apart: 17, of which 9 were waited for; matrix products, arithmetic and copies ran while one was open for 2% of the time, Pallas kernels for 31%

profile of v20, /device:TPU:0, one launch (start us, length us, event | category | flops | bytes accessed | tf_op | source)
XLA Modules:
  0.0 67.4 jit_solution(8585151390531864172)
XLA Ops:
  0.0 3.0 %collective-permute-start = (s32[2048]{0:T(1024)}, s32[2048]{0:T(1024)S(1)}, u32[]{:S(2)}, u32[]{:S(2)}) collective-permute-start(s32[2048]{0:T(1024)} %wanted.1), channel_id=1, source_target_pairs={{0,4},{4,0},{1,5},{5,1},{2,6},{6,2},{3,7},{7,3},{8,12},{12,8},{9,1... | collective-permute-start | bytes 24584 | tf_op jit(solution)/shard_map/ppermute | solution.py:45
  3.0 0.9 %slice_select_fusion = bf16[128,256]{1,0:T(8,128)(2,1)S(1)} fusion(bf16[4096,256]{1,0:T(8,128)(2,1)} %cotangent.3, pred[]{:T(512)S(6)} %eq.3), kind=kLoop, calls=%fused_computation.5 | loop fusion | flops 32768 | bytes 196609 | tf_op jit(solution)/shard_map/jit(_where)/select_n | solution.py:22
  4.0 2.7 %project.1 = bf16[512,256]{1,0:T(8,128)(2,1)} custom-call(s32[1]{0:T(128)} %bitcast.1.chan, bf16[2048,1152]{1,0:T(8,128)(2,1)} %spectra.7, bf16[1152,256]{1,0:T(8,128)(2,1)} %weight.5), custom_call_target="tpu_custom_call" | custom-call | flops 301989888 | bytes 2031616 | tf_op jit(solution)/shard_map/project/pallas_call | solution.py:88
  6.7 2.1 %collective-permute-start.2 = (bf16[512,256]{1,0:T(8,128)(2,1)}, bf16[512,256]{1,0:T(8,128)(2,1)S(1)}, u32[]{:S(2)}, u32[]{:S(2)}) collective-permute-start(bf16[512,256]{1,0:T(8,128)(2,1)} %project.1), channel_id=1, source_target_pairs={{0,1},{1,0},{2,3},{3,2},{4,5},{5,4},{6,7},{7,6},{8,9},{9,8},{10,11... | collective-permute-start | bytes 786440 | tf_op jit(solution)/shard_map/ppermute | solution.py:45
  8.9 0.1 pad_add_fusion.where
  9.1 7.9 %pixel_rows.2 = (bf16[512,256]{1,0:T(8,128)(2,1)S(1)}, bf16[512,256]{1,0:T(8,128)(2,1)S(1)}, bf16[512,256]{1,0:T(8,128)(2,1)S(1)}) custom-call(s32[2]{0:T(128)S(1)} %pad_add_fusion.1.where, s32[16384]{0:T(1024)S(1)} %bitcast.11, s32[2048]{0:T(1024)S(1)} %collective-permute-done.wanted, bf16[4096,256]{1,0:T(8,128)(2,1)} %cotangent.3, ...), custom_call_target="tpu_custom_call" | custom-call | flops 17179869184 | bytes 4194304 | tf_op jit(solution)/shard_map/pixel_rows/pallas_call | solution.py:303
  17.1 0.8 %collective-permute-start.3 = (bf16[512,256]{1,0:T(8,128)(2,1)S(1)}, bf16[512,256]{1,0:T(8,128)(2,1)S(1)}, u32[]{:S(2)}, u32[]{:S(2)}) collective-permute-start(bf16[512,256]{1,0:T(8,128)(2,1)S(1)} %get-tuple-element.30), channel_id=1, source_target_pairs={{0,1},{1,0},{2,3},{3,2},{4,5},{5,4},{6,7},{7,6},{8,9},{9,8},{10,11... | collective-permute-start | bytes 786440 | tf_op jit(solution)/shard_map/ppermute | solution.py:45
  17.9 3.4 %collective-permute-start.4 = (bf16[512,256]{1,0:T(8,128)(2,1)S(1)}, bf16[512,256]{1,0:T(8,128)(2,1)S(1)}, u32[]{:S(2)}, u32[]{:S(2)}) collective-permute-start(bf16[512,256]{1,0:T(8,128)(2,1)S(1)} %add_convert_fusion), channel_id=1, source_target_pairs={{0,3},{1,2},{2,1},{3,0},{4,7},{5,6},{6,5},{7,4},{8,11},{9,10},{10,... | collective-permute-start | bytes 786440 | tf_op jit(solution)/shard_map/ppermute | solution.py:45
  21.2 1.5 %collective-permute-start.5 = (bf16[512,256]{1,0:T(8,128)(2,1)S(1)}, bf16[512,256]{1,0:T(8,128)(2,1)S(1)}, u32[]{:S(2)}, u32[]{:S(2)}) collective-permute-start(bf16[512,256]{1,0:T(8,128)(2,1)S(1)} %get-tuple-element.33), channel_id=1, source_target_pairs={{0,4},{4,0},{1,5},{5,1},{2,6},{6,2},{3,7},{7,3},{8,12},{12,8},{9,1... | collective-permute-start | bytes 786440 | tf_op jit(solution)/shard_map/ppermute | solution.py:45
  22.8 6.8 %pixel_rows.3 = (bf16[512,256]{1,0:T(8,128)(2,1)S(1)}, bf16[512,256]{1,0:T(8,128)(2,1)S(1)}) custom-call(s32[2]{0:T(128)S(1)} %pad_add_fusion.2.where, s32[16384]{0:T(1024)S(1)} %bitcast.12, s32[2048]{0:T(1024)S(1)} %copy-done.3, bf16[4096,256]{1,0:T(8,128)(2,1)} %cotangent.3, bf16[128,256]{1,0:T(8,128)(2,1)S(1)} %collective-permute-done.1.above.below, ...), custom_call_target="tpu_custom_call" | custom-call | flops 17179869184 | bytes 4194304 | tf_op jit(solution)/shard_map/pixel_rows/pallas_call | solution.py:303
  29.7 2.5 %collective-permute-done.4.far = bf16[512,256]{1,0:T(8,128)(2,1)S(1)} collective-permute-done((bf16[512,256]{1,0:T(8,128)(2,1)S(1)}, bf16[512,256]{1,0:T(8,128)(2,1)S(1)}, u32[]{:S(2)}, u32[]{:S(2)}) %collective-permute-start.4) | collective-permute-done | bytes 262176 | tf_op jit(solution)/shard_map/ppermute | solution.py:45
  32.1 1.0 %pre_gradient.1.first = bf16[512,256]{1,0:T(8,128)(2,1)S(1)} custom-call(s32[2]{0:T(128)S(1)} %pad_add_fusion.where, bf16[512,256]{1,0:T(8,128)(2,1)S(1)} %get-tuple-element.29.keep, bf16[512,256]{1,0:T(8,128)(2,1)S(1)} %collective-permute-done.3.near, bf16[512,256]{1,0:T(8,128)(2,1)S(1)} %collective-permute-done.4.far, s32[16,128]{1,0:T(8,128)S(1)} %bitcast.13, ...), custom_call_target="tpu_custom_call" | custom-call | tf_op jit(solution)/shard_map/pre_gradient/pallas_call | solution.py:375
  33.2 0.4 collective-permute-start.6
  33.6 2.2 %collective-permute-start.7 = (bf16[512,256]{1,0:T(8,128)(2,1)S(1)}, bf16[512,256]{1,0:T(8,128)(2,1)S(1)}, u32[]{:S(2)}, u32[]{:S(2)}) collective-permute-start(bf16[512,256]{1,0:T(8,128)(2,1)S(1)} %pre_gradient.1.first), channel_id=1, source_target_pairs={{0,1},{1,0},{2,3},{3,2},{4,5},{5,4},{6,7},{7,6},{8,9},{9,8},{10,11... | collective-permute-start | bytes 786440 | tf_op jit(solution)/shard_map/ppermute | solution.py:45
  35.8 8.5 %collective-permute-done.6.second = bf16[512,256]{1,0:T(8,128)(2,1)S(1)} collective-permute-done((bf16[512,256]{1,0:T(8,128)(2,1)S(1)}, bf16[512,256]{1,0:T(8,128)(2,1)S(1)}, u32[]{:S(2)}, u32[]{:S(2)}) %collective-permute-start.6) | collective-permute-done | bytes 262176 | tf_op jit(solution)/shard_map/ppermute | solution.py:45
  44.3 0.1 collective-permute-start.8
  44.4 2.5 %early_product.1 = (f32[1152,256]{1,0:T(8,128)S(1)}, bf16[512,1152]{1,0:T(8,128)(2,1)S(1)}, bf16[512,1152]{1,0:T(8,128)(2,1)S(1)}) custom-call(s32[1]{0:T(128)} %bitcast.1.chan, bf16[2048,1152]{1,0:T(8,128)(2,1)} %spectra.7, bf16[512,256]{1,0:T(8,128)(2,1)S(1)} %pre_gradient.1.first, bf16[512,256]{1,0:T(8,128)(2,1)S(1)} %collective-permute-done.6.second), custom_call_target="tpu_custom_call" | custom-call | flops 603979776 | bytes 5898240 | tf_op jit(solution)/shard_map/early_product/pallas_call | solution.py:135
  46.9 0.1 collective-permute-done.7.rows
  47.0 0.5 more_product.1.before
  47.6 3.2 %collective-permute-done.8.rows = bf16[512,256]{1,0:T(8,128)(2,1)S(1)} collective-permute-done((bf16[512,256]{1,0:T(8,128)(2,1)S(1)}, bf16[512,256]{1,0:T(8,128)(2,1)S(1)}, u32[]{:S(2)}, u32[]{:S(2)}) %collective-permute-start.8) | collective-permute-done | bytes 262176 | tf_op jit(solution)/shard_map/ppermute | solution.py:45
  50.7 0.6 late_product.1
  51.4 0.5 collective-permute-start.12
  51.9 0.9 %collective-permute-done.9.second = bf16[288,256]{1,0:T(8,128)(2,1)S(1)} collective-permute-done((bf16[288,256]{1,0:T(8,128)(2,1)S(1)}, bf16[288,256]{1,0:T(8,128)(2,1)S(1)}, u32[]{:S(2)}, u32[]{:S(2)}) %collective-permute-start.9) | collective-permute-done | bytes 147488 | tf_op jit(solution)/shard_map/ppermute | solution.py:45
  52.8 1.6 %collective-permute-start.10 = (bf16[288,256]{1,0:T(8,128)(2,1)S(1)}, bf16[288,256]{1,0:T(8,128)(2,1)S(1)}, u32[]{:S(2)}, u32[]{:S(2)}) collective-permute-start(bf16[288,256]{1,0:T(8,128)(2,1)S(1)} %added.6.first), channel_id=1, source_target_pairs={{0,16},{4,20},{8,12},{12,8},{16,0},{20,4},{24,28},{28,24},{1,17},{... | collective-permute-start | bytes 442376 | tf_op jit(solution)/shard_map/ppermute | solution.py:430
  54.4 0.6 collective-permute-start.13
  55.0 3.0 %collective-permute-done.10.second = bf16[288,256]{1,0:T(8,128)(2,1)S(1)} collective-permute-done((bf16[288,256]{1,0:T(8,128)(2,1)S(1)}, bf16[288,256]{1,0:T(8,128)(2,1)S(1)}, u32[]{:S(2)}, u32[]{:S(2)}) %collective-permute-start.10) | collective-permute-done | bytes 147488 | tf_op jit(solution)/shard_map/ppermute | solution.py:430
  58.0 1.6 %collective-permute-start.11 = (bf16[288,256]{1,0:T(8,128)(2,1)S(1)}, bf16[288,256]{1,0:T(8,128)(2,1)S(1)}, u32[]{:S(2)}, u32[]{:S(2)}) collective-permute-start(bf16[288,256]{1,0:T(8,128)(2,1)S(1)} %added.7.first), channel_id=1, source_target_pairs={{0,4},{4,0},{8,24},{12,28},{16,20},{20,16},{24,8},{28,12},{1,5},{5... | collective-permute-start | bytes 442376 | tf_op jit(solution)/shard_map/ppermute | solution.py:430
  59.7 1.6 %collective-permute-start.14 = (bf16[288,256]{1,0:T(8,128)(2,1)S(1)}, bf16[288,256]{1,0:T(8,128)(2,1)S(1)}, u32[]{:S(2)}, u32[]{:S(2)}) collective-permute-start(bf16[288,256]{1,0:T(8,128)(2,1)S(1)} %added.10.first), channel_id=1, source_target_pairs={{0,4},{4,0},{8,24},{12,28},{16,20},{20,16},{24,8},{28,12},{1,5},{5... | collective-permute-start | bytes 442376 | tf_op jit(solution)/shard_map/ppermute | solution.py:430
  61.2 2.0 %collective-permute-done.11.second = bf16[288,256]{1,0:T(8,128)(2,1)S(1)} collective-permute-done((bf16[288,256]{1,0:T(8,128)(2,1)S(1)}, bf16[288,256]{1,0:T(8,128)(2,1)S(1)}, u32[]{:S(2)}, u32[]{:S(2)}) %collective-permute-start.11) | collective-permute-done | bytes 147488 | tf_op jit(solution)/shard_map/ppermute | solution.py:430
  63.4 1.5 %collective-permute-done.14.second = bf16[288,256]{1,0:T(8,128)(2,1)S(1)} collective-permute-done((bf16[288,256]{1,0:T(8,128)(2,1)S(1)}, bf16[288,256]{1,0:T(8,128)(2,1)S(1)}, u32[]{:S(2)}, u32[]{:S(2)}) %collective-permute-start.14) | collective-permute-done | bytes 147488 | tf_op jit(solution)/shard_map/ppermute | solution.py:430
  65.0 1.3 %collective-permute-done.16.refs_3_ = bf16[288,256]{1,0:T(8,128)(2,1)S(1)} collective-permute-done((bf16[288,256]{1,0:T(8,128)(2,1)S(1)}, bf16[288,256]{1,0:T(8,128)(2,1)S(1)}, u32[]{:S(2)}, u32[]{:S(2)}) %collective-permute-start.16) | collective-permute-done | bytes 147488 | tf_op jit(solution)/shard_map/ppermute | solution.py:45
  66.4 1.1 %collect.1 = f32[1152,256]{1,0:T(8,128)} custom-call(s32[1]{0:T(128)} %bitcast.core, bf16[288,256]{1,0:T(8,128)(2,1)S(1)} %added.8.refs_0_, bf16[288,256]{1,0:T(8,128)(2,1)S(1)} %added.11.refs_1_, bf16[288,256]{1,0:T(8,128)(2,1)S(1)} %collective-permute-done.15.refs_2_, bf16[288,256]{1,0:T(8,128)(2,1)S(1)} %collective-permute-done.16.refs_3_), custom_call_target="tpu_custom_call" | custom-call | tf_op jit(solution)/shard_map/collect/pallas_call | solution.py:399
  (36 shorter events, 0.8 us)
Async XLA Ops:
  0.0 9.0 %collective-permute-start = (s32[2048]{0:T(1024)}, s32[2048]{0:T(1024)S(1)}, u32[]{:S(2)}, u32[]{:S(2)}) collective-permute-start(s32[2048]{0:T(1024)} %wanted.1), channel_id=1, source_target_pairs={{0,4},{4,0},{1,5},{5,1},{2,6},{6,2},{3,7},{7,3},{8,12},{12,8},{9,1... | collective-permute-start | bytes 24584 | tf_op jit(solution)/shard_map/ppermute | solution.py:45
  3.9 5.2 %collective-permute-start.1 = (bf16[128,256]{1,0:T(8,128)(2,1)S(1)}, bf16[128,256]{1,0:T(8,128)(2,1)S(1)}, u32[]{:S(2)}, u32[]{:S(2)}) collective-permute-start(bf16[128,256]{1,0:T(8,128)(2,1)S(1)} %slice_select_fusion), channel_id=1, source_target_pairs={{0,4},{4,0},{1,5},{5,1},{2,6},{6,2},{3,7},{7,3},{8,12},{12,8},{9,1... | collective-permute-start | bytes 196616 | tf_op jit(solution)/shard_map/ppermute | solution.py:22
  3.9 5.0 %copy-start.5 = (s32[8,4096]{1,0:T(8,128)S(1)}, s32[8,4096]{1,0:T(8,128)}, u32[]{:S(2)}) copy-start(s32[8,4096]{1,0:T(8,128)} %param.14) | copy-start | bytes 393220
  3.9 5.1 %copy-start = (bf16[1152,256]{1,0:T(8,128)(2,1)S(1)}, bf16[1152,256]{1,0:T(8,128)(2,1)}, u32[]{:S(2)}) copy-start(bf16[1152,256]{1,0:T(8,128)(2,1)} %weight.5) | copy-start | bytes 1769476
  4.0 5.1 %copy-start.4 = (f32[8,256]{1,0:T(8,128)S(1)}, f32[8,256]{1,0:T(8,128)}, u32[]{:S(2)}) copy-start(f32[8,256]{1,0:T(8,128)} %mixing.3) | copy-start | bytes 24580
  6.7 10.3 %collective-permute-start.2 = (bf16[512,256]{1,0:T(8,128)(2,1)}, bf16[512,256]{1,0:T(8,128)(2,1)S(1)}, u32[]{:S(2)}, u32[]{:S(2)}) collective-permute-start(bf16[512,256]{1,0:T(8,128)(2,1)} %project.1), channel_id=1, source_target_pairs={{0,1},{1,0},{2,3},{3,2},{4,5},{5,4},{6,7},{7,6},{8,9},{9,8},{10,11... | collective-permute-start | bytes 786440 | tf_op jit(solution)/shard_map/ppermute | solution.py:45
  9.1 13.8 %copy-start.3 = (s32[2048]{0:T(1024)S(1)}, s32[2048]{0:T(1024)}, u32[]{:S(2)}) copy-start(s32[2048]{0:T(1024)} %wanted.1) | copy-start | bytes 24580
  17.1 12.5 %collective-permute-start.3 = (bf16[512,256]{1,0:T(8,128)(2,1)S(1)}, bf16[512,256]{1,0:T(8,128)(2,1)S(1)}, u32[]{:S(2)}, u32[]{:S(2)}) collective-permute-start(bf16[512,256]{1,0:T(8,128)(2,1)S(1)} %get-tuple-element.30), channel_id=1, source_target_pairs={{0,1},{1,0},{2,3},{3,2},{4,5},{5,4},{6,7},{7,6},{8,9},{9,8},{10,11... | collective-permute-start | bytes 786440 | tf_op jit(solution)/shard_map/ppermute | solution.py:45
  17.9 14.3 %collective-permute-start.4 = (bf16[512,256]{1,0:T(8,128)(2,1)S(1)}, bf16[512,256]{1,0:T(8,128)(2,1)S(1)}, u32[]{:S(2)}, u32[]{:S(2)}) collective-permute-start(bf16[512,256]{1,0:T(8,128)(2,1)S(1)} %add_convert_fusion), channel_id=1, source_target_pairs={{0,3},{1,2},{2,1},{3,0},{4,7},{5,6},{6,5},{7,4},{8,11},{9,10},{10,... | collective-permute-start | bytes 786440 | tf_op jit(solution)/shard_map/ppermute | solution.py:45
  21.2 10.9 %collective-permute-start.5 = (bf16[512,256]{1,0:T(8,128)(2,1)S(1)}, bf16[512,256]{1,0:T(8,128)(2,1)S(1)}, u32[]{:S(2)}, u32[]{:S(2)}) collective-permute-start(bf16[512,256]{1,0:T(8,128)(2,1)S(1)} %get-tuple-element.33), channel_id=1, source_target_pairs={{0,4},{4,0},{1,5},{5,1},{2,6},{6,2},{3,7},{7,3},{8,12},{12,8},{9,1... | collective-permute-start | bytes 786440 | tf_op jit(solution)/shard_map/ppermute | solution.py:45
  22.8 9.3 %copy-start.1 = (s32[2048,1]{0,1:T(1,128)S(1)}, s32[2048,1]{0,1:T(1,128)}, u32[]{:S(2)}) copy-start(s32[2048,1]{0,1:T(1,128)} %param.10) | copy-start | bytes 24580
  22.8 9.3 %copy-start.2 = (f32[2048]{0:T(1024)S(1)}, f32[2048]{0:T(1024)}, u32[]{:S(2)}) copy-start(f32[2048]{0:T(1024)} %param.12) | copy-start | bytes 24580
  33.2 11.1 %collective-permute-start.6 = (bf16[512,256]{1,0:T(8,128)(2,1)S(1)}, bf16[512,256]{1,0:T(8,128)(2,1)S(1)}, u32[]{:S(2)}, u32[]{:S(2)}) collective-permute-start(bf16[512,256]{1,0:T(8,128)(2,1)S(1)} %pre_gradient.1.first), channel_id=1, source_target_pairs={{0,3},{1,2},{2,1},{3,0},{4,7},{5,6},{6,5},{7,4},{8,11},{9,10},{10,... | collective-permute-start | bytes 786440 | tf_op jit(solution)/shard_map/ppermute | solution.py:45
  33.6 13.4 %collective-permute-start.7 = (bf16[512,256]{1,0:T(8,128)(2,1)S(1)}, bf16[512,256]{1,0:T(8,128)(2,1)S(1)}, u32[]{:S(2)}, u32[]{:S(2)}) collective-permute-start(bf16[512,256]{1,0:T(8,128)(2,1)S(1)} %pre_gradient.1.first), channel_id=1, source_target_pairs={{0,1},{1,0},{2,3},{3,2},{4,5},{5,4},{6,7},{7,6},{8,9},{9,8},{10,11... | collective-permute-start | bytes 786440 | tf_op jit(solution)/shard_map/ppermute | solution.py:45
  44.3 6.5 %collective-permute-start.8 = (bf16[512,256]{1,0:T(8,128)(2,1)S(1)}, bf16[512,256]{1,0:T(8,128)(2,1)S(1)}, u32[]{:S(2)}, u32[]{:S(2)}) collective-permute-start(bf16[512,256]{1,0:T(8,128)(2,1)S(1)} %collective-permute-done.6.second), channel_id=1, source_target_pairs={{0,1},{1,0},{2,3},{3,2},{4,5},{5,4},{6,7},{7,6},{8,9},{9,8},{10,11... | collective-permute-start | bytes 786440 | tf_op jit(solution)/shard_map/ppermute | solution.py:45
  51.3 1.4 %collective-permute-start.9 = (bf16[288,256]{1,0:T(8,128)(2,1)S(1)}, bf16[288,256]{1,0:T(8,128)(2,1)S(1)}, u32[]{:S(2)}, u32[]{:S(2)}) collective-permute-start(bf16[288,256]{1,0:T(8,128)(2,1)S(1)} %get-tuple-element.38), channel_id=1, source_target_pairs={{0,8},{8,0},{16,24},{24,16},{1,9},{9,1},{17,25},{25,17},{2,10},{10... | collective-permute-start | bytes 442376 | tf_op jit(solution)/shard_map/ppermute | solution.py:45
  51.4 2.9 %collective-permute-start.12 = (bf16[288,256]{1,0:T(8,128)(2,1)S(1)}, bf16[288,256]{1,0:T(8,128)(2,1)S(1)}, u32[]{:S(2)}, u32[]{:S(2)}) collective-permute-start(bf16[288,256]{1,0:T(8,128)(2,1)S(1)} %get-tuple-element.40), channel_id=1, source_target_pairs={{0,8},{8,0},{16,24},{24,16},{1,9},{9,1},{17,25},{25,17},{2,10},{10... | collective-permute-start | bytes 442376 | tf_op jit(solution)/shard_map/ppermute | solution.py:45
  52.8 5.2 %collective-permute-start.10 = (bf16[288,256]{1,0:T(8,128)(2,1)S(1)}, bf16[288,256]{1,0:T(8,128)(2,1)S(1)}, u32[]{:S(2)}, u32[]{:S(2)}) collective-permute-start(bf16[288,256]{1,0:T(8,128)(2,1)S(1)} %added.6.first), channel_id=1, source_target_pairs={{0,16},{4,20},{8,12},{12,8},{16,0},{20,4},{24,28},{28,24},{1,17},{... | collective-permute-start | bytes 442376 | tf_op jit(solution)/shard_map/ppermute | solution.py:430
  54.4 5.2 %collective-permute-start.13 = (bf16[288,256]{1,0:T(8,128)(2,1)S(1)}, bf16[288,256]{1,0:T(8,128)(2,1)S(1)}, u32[]{:S(2)}, u32[]{:S(2)}) collective-permute-start(bf16[288,256]{1,0:T(8,128)(2,1)S(1)} %added.9.first), channel_id=1, source_target_pairs={{0,16},{4,20},{8,12},{12,8},{16,0},{20,4},{24,28},{28,24},{1,17},{... | collective-permute-start | bytes 442376 | tf_op jit(solution)/shard_map/ppermute | solution.py:430
  58.0 5.2 %collective-permute-start.11 = (bf16[288,256]{1,0:T(8,128)(2,1)S(1)}, bf16[288,256]{1,0:T(8,128)(2,1)S(1)}, u32[]{:S(2)}, u32[]{:S(2)}) collective-permute-start(bf16[288,256]{1,0:T(8,128)(2,1)S(1)} %added.7.first), channel_id=1, source_target_pairs={{0,4},{4,0},{8,24},{12,28},{16,20},{20,16},{24,8},{28,12},{1,5},{5... | collective-permute-start | bytes 442376 | tf_op jit(solution)/shard_map/ppermute | solution.py:430
  59.7 5.2 %collective-permute-start.14 = (bf16[288,256]{1,0:T(8,128)(2,1)S(1)}, bf16[288,256]{1,0:T(8,128)(2,1)S(1)}, u32[]{:S(2)}, u32[]{:S(2)}) collective-permute-start(bf16[288,256]{1,0:T(8,128)(2,1)S(1)} %added.10.first), channel_id=1, source_target_pairs={{0,4},{4,0},{8,24},{12,28},{16,20},{20,16},{24,8},{28,12},{1,5},{5... | collective-permute-start | bytes 442376 | tf_op jit(solution)/shard_map/ppermute | solution.py:430
  63.3 1.7 %collective-permute-start.15 = (bf16[288,256]{1,0:T(8,128)(2,1)S(1)}, bf16[288,256]{1,0:T(8,128)(2,1)S(1)}, u32[]{:S(2)}, u32[]{:S(2)}) collective-permute-start(bf16[288,256]{1,0:T(8,128)(2,1)S(1)} %added.8.refs_0_), channel_id=1, source_target_pairs={{0,8},{8,0},{16,24},{24,16},{1,9},{9,1},{17,25},{25,17},{2,10},{10... | collective-permute-start | bytes 442376 | tf_op jit(solution)/shard_map/ppermute | solution.py:45
  64.9 1.4 %collective-permute-start.16 = (bf16[288,256]{1,0:T(8,128)(2,1)S(1)}, bf16[288,256]{1,0:T(8,128)(2,1)S(1)}, u32[]{:S(2)}, u32[]{:S(2)}) collective-permute-start(bf16[288,256]{1,0:T(8,128)(2,1)S(1)} %added.11.refs_1_), channel_id=1, source_target_pairs={{0,8},{8,0},{16,24},{24,16},{1,9},{9,1},{17,25},{25,17},{2,10},{10... | collective-permute-start | bytes 442376 | tf_op jit(solution)/shard_map/ppermute | solution.py:45

commit v21 on v20

--- a/solution.py
+++ b/solution.py
@@ -337,17 +337,17 @@
     )
 
 
-def gradient_kernel(where, keep, near, far, tiles, weights, mine, answers, out):
+def gradient_kernel(where, first, second, third, fourth, tiles, weights, mine, answers, out):
     tile, chan = where[0], where[1]
     rows = out.shape[0]
     size = tiles.shape[1]
     count = rows // size
     group = 8 // count
     wide = jnp.float32
-    first = pl.multiple_of(chan // group * 8, 8)
+    start = pl.multiple_of(chan // group * 8, 8)
 
     def columns(values):
-        turned = values[pl.ds(first, 8), :].T
+        turned = values[pl.ds(start, 8), :].T
         places = [turned[:, n * count : (n + 1) * count] for n in range(group)]
         picked = places[0]
         for n in range(1, group):
@@ -358,7 +358,8 @@
     factors = columns(weights)
     for n in range(count):
         here = slice(n * size, (n + 1) * size)
-        pre = keep[here, :].astype(wide) + near[here, :].astype(wide) + far[here, :].astype(wide)
+        pre = first[here, :].astype(wide) + second[here, :].astype(wide)
+        pre = pre + third[here, :].astype(wide) + fourth[here, :].astype(wide)
         sigma = jax.nn.sigmoid(pre)
         deriv = sigma * (1.0 + pre * (1.0 - sigma))
         fetched = jnp.where(
@@ -369,17 +370,17 @@
         out[here, :] = (factors[:, n : n + 1] * deriv * fetched).astype(out.dtype)
 
 
-def pre_gradient(tile, chan, keep, near, far, tiles, weights, mine, answers):
+def pre_gradient(tile, chan, parts, tiles, weights, mine, answers):
     spec = pl.BlockSpec(memory_space=pltpu.VMEM)
     tiles, weights = tiles.reshape(-1, 128), weights.reshape(-1, 128)
     return pl.pallas_call(
         gradient_kernel,
-        out_shape=jax.ShapeDtypeStruct(far.shape, jnp.bfloat16),
-        in_specs=[pl.BlockSpec(memory_space=pltpu.SMEM)] + [spec] * 7,
+        out_shape=jax.ShapeDtypeStruct(mine.shape, jnp.bfloat16),
+        in_specs=[pl.BlockSpec(memory_space=pltpu.SMEM)] + [spec] * 8,
         out_specs=spec,
         compiler_params=memory(16),
         name="pre_gradient",
-    )(jnp.stack([tile, chan]), keep, near, far, tiles, weights, mine, answers)
+    )(jnp.stack([tile, chan]), *parts, tiles, weights, mine, answers)
 
 
 def collect_kernel(core, *refs):
@@ -439,7 +440,8 @@
     chan = lax.axis_index("chan")
     first_row = chan * quarter
 
-    near_first = swap(project(spectra, enc_weight, chan, (2,), LARGE + 4)[0], "chan", 1)
+    across, beyond = project(spectra, enc_weight, chan, (2, 3), LARGE + 4)
+    parts = [swap(across, "chan", 2), swap(beyond, "chan", 3)]
     places = (adjoint - (tile * tile_rows - HALO)) * 2
     places = (places[: NEIGH // 2] | (places[NEIGH // 2 :] << 16)).reshape(-1)
 
@@ -455,12 +457,9 @@
         local_ids = lax.dynamic_slice_in_dim(pix_local, first_row, quarter, 0)
         slot_index, wanted = requests(tile_ids, local_ids, capacity)
         start, count = 0 * chan, wanted.shape[0]
-    rows, shared, send = pixel_rows(*pixels, wanted, start, count, *rest, chan, (3, 1))
-    near_first, rows = lax.optimization_barrier((near_first, rows))
-    passed_on = (shared.astype(jnp.float32) + near_first.astype(jnp.float32)).astype(jnp.bfloat16)
-    passed_on, send, rows, later = lax.optimization_barrier((passed_on, send, rows, chan))
-    far = swap(passed_on, "chan", 3)
-    near = swap(send, "chan", 1)
+    rows, send = pixel_rows(*pixels, wanted, start, count, *rest, chan, (1,))
+    rows, send, later = lax.optimization_barrier((rows, send, chan))
+    parts.append(swap(send, "chan", 1))
     if paired:
         answers = swap(rows, "pix", 1)
         mine, keep = pixel_rows(*pixels, pix_local, later * quarter, count, *rest, later, (0,))
@@ -470,11 +469,12 @@
             rows.reshape(tile_count, capacity, -1), "pix", split_axis=0, concat_axis=0, tiled=True
         )
         mine = answers = jnp.take(answers.reshape(tile_count * capacity, -1), slot_index, axis=0)
-    grads = pre_gradient(tile, chan, keep, near, far, pix_tile, foot_weight, mine, answers)
-
+    parts.append(keep)
+    grads = pre_gradient(tile, chan, parts, pix_tile, foot_weight, mine, answers)
+
+    last = swap(grads, "chan", 2)
     across = swap(grads, "chan", 3)
     beside = swap(grads, "chan", 1)
-    last = swap(across, "chan", 1)
     early, held, held_last = early_product(spectra, chan, grads, across)
     early = more_product(held, early, beside)
     core = lax.axis_index("obs") & 1

time: 67.6 us -> 77.9 us (1.15)
  waiting for transfers between devices: 23 us -> 33 us
    ppermute x12, waiting for transfers between devices: 16.4 us -> 26.5 us  [swap(): return lax.ppermute(value, axis, [(i, i ^ bit) for i in range(size)])]
    pallas_call x1, Pallas kernels: 2.74 us -> 3.89 us  [project(): pl.pallas_call(functools.partial(project_kernel, bits), out_shape=(jax.Sh...]
    pallas_call x2, Pallas kernels: 14.7 us -> 13.7 us  [pixel_rows(): pl.pallas_call(functools.partial(pixel_kernel, count, bits), out_shape=(j...]
  transfers between devices with their start and end apart: 17 -> 17, of which waited for: 9 -> 10; matrix products, arithmetic and copies ran while one was open for 2% -> 1% of each run, Pallas kernels for 31% -> 27%
where the time goes in v21:
time: 77.9 us; the launch traced here: 77.7 us
  waiting for transfers between devices  33 us (42%)
  Pallas kernels  23.5 us (30%)
  starting transfers between devices  19.8 us (25%)
  other arithmetic  1.14 us (1%)
    ppermute x12, waiting for transfers between devices, swap(): return lax.ppermute(value, axis, [(i, i ^ bit) for i in range(size)])  26.5 us
    ppermute x12, starting transfers between devices, swap(): return lax.ppermute(value, axis, [(i, i ^ bit) for i in range(size)])  14.4 us
    pallas_call x2, Pallas kernels, pixel_rows(): pl.pallas_call(functools.partial(pixel_kernel, count, bits), out_shape=(j...  13.7 us
    ppermute x4, waiting for transfers between devices, sum_over_panels(): parts = [added(part, lax.ppermute(part, both, perm)) for part in parts]  6.56 us
    ppermute x4, starting transfers between devices, sum_over_panels(): parts = [added(part, lax.ppermute(part, both, perm)) for part in parts]  5.29 us
    pallas_call x1, Pallas kernels, project(): pl.pallas_call(functools.partial(project_kernel, bits), out_shape=(jax.Sh...  3.89 us
    pallas_call x1, Pallas kernels, early_product(): pl.pallas_call(early_kernel, out_shape=(jax.ShapeDtypeStruct((depth, widt...  2.49 us
  transfers between devices with their start and end apart: 17, of which 10 were waited for; matrix products, arithmetic and copies ran while one was open for 1% of the time, Pallas kernels for 27%

profile of v21, /device:TPU:0, one launch (start us, length us, event | category | flops | bytes accessed | tf_op | source)
XLA Modules:
  0.0 77.7 jit_solution(7592590074330228032)
XLA Ops:
  0.0 3.0 %collective-permute-start.2 = (s32[2048]{0:T(1024)}, s32[2048]{0:T(1024)S(1)}, u32[]{:S(2)}, u32[]{:S(2)}) collective-permute-start(s32[2048]{0:T(1024)} %wanted.1), channel_id=1, source_target_pairs={{0,4},{4,0},{1,5},{5,1},{2,6},{6,2},{3,7},{7,3},{8,12},{12,8},{9,1... | collective-permute-start | bytes 24584 | tf_op jit(solution)/shard_map/ppermute | solution.py:45
  3.0 0.9 %slice_select_fusion = bf16[128,256]{1,0:T(8,128)(2,1)S(1)} fusion(bf16[4096,256]{1,0:T(8,128)(2,1)} %cotangent.3, pred[]{:T(512)S(6)} %eq.3), kind=kLoop, calls=%fused_computation.4 | loop fusion | flops 32768 | bytes 196609 | tf_op jit(solution)/shard_map/jit(_where)/select_n | solution.py:22
  4.0 3.9 %project.1 = (bf16[512,256]{1,0:T(8,128)(2,1)}, bf16[512,256]{1,0:T(8,128)(2,1)}) custom-call(s32[1]{0:T(128)} %bitcast.1.chan, bf16[2048,1152]{1,0:T(8,128)(2,1)} %spectra.7, bf16[1152,256]{1,0:T(8,128)(2,1)} %weight.5), custom_call_target="tpu_custom_call" | custom-call | flops 603979776 | bytes 3473408 | tf_op jit(solution)/shard_map/project/pallas_call | solution.py:88
  7.9 3.1 %collective-permute-start = (bf16[512,256]{1,0:T(8,128)(2,1)}, bf16[512,256]{1,0:T(8,128)(2,1)S(1)}, u32[]{:S(2)}, u32[]{:S(2)}) collective-permute-start(bf16[512,256]{1,0:T(8,128)(2,1)} %get-tuple-element.21), channel_id=1, source_target_pairs={{0,2},{1,3},{2,0},{3,1},{4,6},{5,7},{6,4},{7,5},{8,10},{9,11},{10,... | collective-permute-start | bytes 786440 | tf_op jit(solution)/shard_map/ppermute | solution.py:45
  11.0 1.3 %collective-permute-start.1 = (bf16[512,256]{1,0:T(8,128)(2,1)}, bf16[512,256]{1,0:T(8,128)(2,1)S(1)}, u32[]{:S(2)}, u32[]{:S(2)}) collective-permute-start(bf16[512,256]{1,0:T(8,128)(2,1)} %get-tuple-element.22), channel_id=1, source_target_pairs={{0,3},{1,2},{2,1},{3,0},{4,7},{5,6},{6,5},{7,4},{8,11},{9,10},{10,... | collective-permute-start | bytes 786440 | tf_op jit(solution)/shard_map/ppermute | solution.py:45
  12.5 0.1 pad_add_fusion.where
  12.6 6.8 %pixel_rows.2 = (bf16[512,256]{1,0:T(8,128)(2,1)S(1)}, bf16[512,256]{1,0:T(8,128)(2,1)S(1)}) custom-call(s32[2]{0:T(128)S(1)} %pad_add_fusion.1.where, s32[16384]{0:T(1024)S(1)} %bitcast.11, s32[2048]{0:T(1024)S(1)} %collective-permute-done.2.wanted, bf16[4096,256]{1,0:T(8,128)(2,1)} %cotangent.3, bf16[128,256]{1,0:T(8,128)(2,1)S(1)} %collective-permute-done.3.above.below, ...), custom_call_target="tpu_custom_call" | custom-call | flops 17179869184 | bytes 4194304 | tf_op jit(solution)/shard_map/pixel_rows/pallas_call | solution.py:303
  19.4 0.3 collective-permute-start.4
  19.7 1.5 %collective-permute-start.5 = (bf16[512,256]{1,0:T(8,128)(2,1)S(1)}, bf16[512,256]{1,0:T(8,128)(2,1)S(1)}, u32[]{:S(2)}, u32[]{:S(2)}) collective-permute-start(bf16[512,256]{1,0:T(8,128)(2,1)S(1)} %get-tuple-element.29), channel_id=1, source_target_pairs={{0,4},{4,0},{1,5},{5,1},{2,6},{6,2},{3,7},{7,3},{8,12},{12,8},{9,1... | collective-permute-start | bytes 786440 | tf_op jit(solution)/shard_map/ppermute | solution.py:45
  21.3 6.8 %pixel_rows.3 = (bf16[512,256]{1,0:T(8,128)(2,1)S(1)}, bf16[512,256]{1,0:T(8,128)(2,1)S(1)}) custom-call(s32[2]{0:T(128)S(1)} %pad_add_fusion.2.where, s32[16384]{0:T(1024)S(1)} %bitcast.12, s32[2048]{0:T(1024)S(1)} %copy-done.3, bf16[4096,256]{1,0:T(8,128)(2,1)} %cotangent.3, bf16[128,256]{1,0:T(8,128)(2,1)S(1)} %collective-permute-done.3.above.below, ...), custom_call_target="tpu_custom_call" | custom-call | flops 17179869184 | bytes 4194304 | tf_op jit(solution)/shard_map/pixel_rows/pallas_call | solution.py:303
  28.2 1.3 %collective-permute-done.first = bf16[512,256]{1,0:T(8,128)(2,1)S(1)} collective-permute-done((bf16[512,256]{1,0:T(8,128)(2,1)}, bf16[512,256]{1,0:T(8,128)(2,1)S(1)}, u32[]{:S(2)}, u32[]{:S(2)}) %collective-permute-start) | collective-permute-done | bytes 262176 | tf_op jit(solution)/shard_map/ppermute | solution.py:45
  29.4 4.4 %collective-permute-done.4.third = bf16[512,256]{1,0:T(8,128)(2,1)S(1)} collective-permute-done((bf16[512,256]{1,0:T(8,128)(2,1)S(1)}, bf16[512,256]{1,0:T(8,128)(2,1)S(1)}, u32[]{:S(2)}, u32[]{:S(2)}) %collective-permute-start.4) | collective-permute-done | bytes 262176 | tf_op jit(solution)/shard_map/ppermute | solution.py:45
  33.8 1.1 %pre_gradient.1.first = bf16[512,256]{1,0:T(8,128)(2,1)S(1)} custom-call(s32[2]{0:T(128)S(1)} %pad_add_fusion.where, bf16[512,256]{1,0:T(8,128)(2,1)S(1)} %collective-permute-done.first, bf16[512,256]{1,0:T(8,128)(2,1)S(1)} %collective-permute-done.1.second, bf16[512,256]{1,0:T(8,128)(2,1)S(1)} %collective-permute-done.4.third, ...), custom_call_target="tpu_custom_call" | custom-call | tf_op jit(solution)/shard_map/pre_gradient/pallas_call | solution.py:376
  34.9 3.6 %collective-permute-start.6 = (bf16[512,256]{1,0:T(8,128)(2,1)S(1)}, bf16[512,256]{1,0:T(8,128)(2,1)S(1)}, u32[]{:S(2)}, u32[]{:S(2)}) collective-permute-start(bf16[512,256]{1,0:T(8,128)(2,1)S(1)} %pre_gradient.1.first), channel_id=1, source_target_pairs={{0,3},{1,2},{2,1},{3,0},{4,7},{5,6},{6,5},{7,4},{8,11},{9,10},{10,... | collective-permute-start | bytes 786440 | tf_op jit(solution)/shard_map/ppermute | solution.py:45
  38.5 0.8 %collective-permute-start.8 = (bf16[512,256]{1,0:T(8,128)(2,1)S(1)}, bf16[512,256]{1,0:T(8,128)(2,1)S(1)}, u32[]{:S(2)}, u32[]{:S(2)}) collective-permute-start(bf16[512,256]{1,0:T(8,128)(2,1)S(1)} %pre_gradient.1.first), channel_id=1, source_target_pairs={{0,2},{1,3},{2,0},{3,1},{4,6},{5,7},{6,4},{7,5},{8,10},{9,11},{10,... | collective-permute-start | bytes 786440 | tf_op jit(solution)/shard_map/ppermute | solution.py:45
  39.3 6.7 %collective-permute-done.6.second = bf16[512,256]{1,0:T(8,128)(2,1)S(1)} collective-permute-done((bf16[512,256]{1,0:T(8,128)(2,1)S(1)}, bf16[512,256]{1,0:T(8,128)(2,1)S(1)}, u32[]{:S(2)}, u32[]{:S(2)}) %collective-permute-start.6) | collective-permute-done | bytes 262176 | tf_op jit(solution)/shard_map/ppermute | solution.py:45
  46.0 2.5 %early_product.1 = (f32[1152,256]{1,0:T(8,128)S(1)}, bf16[512,1152]{1,0:T(8,128)(2,1)S(1)}, bf16[512,1152]{1,0:T(8,128)(2,1)S(1)}) custom-call(s32[1]{0:T(128)} %bitcast.1.chan, bf16[2048,1152]{1,0:T(8,128)(2,1)} %spectra.7, bf16[512,256]{1,0:T(8,128)(2,1)S(1)} %pre_gradient.1.first, bf16[512,256]{1,0:T(8,128)(2,1)S(1)} %collective-permute-done.6.second), custom_call_target="tpu_custom_call" | custom-call | flops 603979776 | bytes 5898240 | tf_op jit(solution)/shard_map/early_product/pallas_call | solution.py:135
  48.5 3.1 %collective-permute-done.7.rows = bf16[512,256]{1,0:T(8,128)(2,1)S(1)} collective-permute-done((bf16[512,256]{1,0:T(8,128)(2,1)S(1)}, bf16[512,256]{1,0:T(8,128)(2,1)S(1)}, u32[]{:S(2)}, u32[]{:S(2)}) %collective-permute-start.7) | collective-permute-done | bytes 262176 | tf_op jit(solution)/shard_map/ppermute | solution.py:45
  51.6 0.5 more_product.1.before
  52.1 8.8 %collective-permute-done.8.rows = bf16[512,256]{1,0:T(8,128)(2,1)S(1)} collective-permute-done((bf16[512,256]{1,0:T(8,128)(2,1)S(1)}, bf16[512,256]{1,0:T(8,128)(2,1)S(1)}, u32[]{:S(2)}, u32[]{:S(2)}) %collective-permute-start.8) | collective-permute-done | bytes 262176 | tf_op jit(solution)/shard_map/ppermute | solution.py:45
  61.0 0.6 late_product.1
  61.6 0.5 collective-permute-start.12
  62.1 0.9 %collective-permute-done.9.second = bf16[288,256]{1,0:T(8,128)(2,1)S(1)} collective-permute-done((bf16[288,256]{1,0:T(8,128)(2,1)S(1)}, bf16[288,256]{1,0:T(8,128)(2,1)S(1)}, u32[]{:S(2)}, u32[]{:S(2)}) %collective-permute-start.9) | collective-permute-done | bytes 147488 | tf_op jit(solution)/shard_map/ppermute | solution.py:45
  63.0 1.6 %collective-permute-start.10 = (bf16[288,256]{1,0:T(8,128)(2,1)S(1)}, bf16[288,256]{1,0:T(8,128)(2,1)S(1)}, u32[]{:S(2)}, u32[]{:S(2)}) collective-permute-start(bf16[288,256]{1,0:T(8,128)(2,1)S(1)} %added.6.first), channel_id=1, source_target_pairs={{0,16},{4,20},{8,12},{12,8},{16,0},{20,4},{24,28},{28,24},{1,17},{... | collective-permute-start | bytes 442376 | tf_op jit(solution)/shard_map/ppermute | solution.py:431
  64.6 0.6 collective-permute-start.13
  65.2 3.0 %collective-permute-done.10.second = bf16[288,256]{1,0:T(8,128)(2,1)S(1)} collective-permute-done((bf16[288,256]{1,0:T(8,128)(2,1)S(1)}, bf16[288,256]{1,0:T(8,128)(2,1)S(1)}, u32[]{:S(2)}, u32[]{:S(2)}) %collective-permute-start.10) | collective-permute-done | bytes 147488 | tf_op jit(solution)/shard_map/ppermute | solution.py:431
  68.3 1.6 %collective-permute-start.11 = (bf16[288,256]{1,0:T(8,128)(2,1)S(1)}, bf16[288,256]{1,0:T(8,128)(2,1)S(1)}, u32[]{:S(2)}, u32[]{:S(2)}) collective-permute-start(bf16[288,256]{1,0:T(8,128)(2,1)S(1)} %added.7.first), channel_id=1, source_target_pairs={{0,4},{4,0},{8,24},{12,28},{16,20},{20,16},{24,8},{28,12},{1,5},{5... | collective-permute-start | bytes 442376 | tf_op jit(solution)/shard_map/ppermute | solution.py:431
  69.9 1.5 %collective-permute-start.14 = (bf16[288,256]{1,0:T(8,128)(2,1)S(1)}, bf16[288,256]{1,0:T(8,128)(2,1)S(1)}, u32[]{:S(2)}, u32[]{:S(2)}) collective-permute-start(bf16[288,256]{1,0:T(8,128)(2,1)S(1)} %added.10.first), channel_id=1, source_target_pairs={{0,4},{4,0},{8,24},{12,28},{16,20},{20,16},{24,8},{28,12},{1,5},{5... | collective-permute-start | bytes 442376 | tf_op jit(solution)/shard_map/ppermute | solution.py:431
  71.5 2.0 %collective-permute-done.11.second = bf16[288,256]{1,0:T(8,128)(2,1)S(1)} collective-permute-done((bf16[288,256]{1,0:T(8,128)(2,1)S(1)}, bf16[288,256]{1,0:T(8,128)(2,1)S(1)}, u32[]{:S(2)}, u32[]{:S(2)}) %collective-permute-start.11) | collective-permute-done | bytes 147488 | tf_op jit(solution)/shard_map/ppermute | solution.py:431
  73.6 1.5 %collective-permute-done.14.second = bf16[288,256]{1,0:T(8,128)(2,1)S(1)} collective-permute-done((bf16[288,256]{1,0:T(8,128)(2,1)S(1)}, bf16[288,256]{1,0:T(8,128)(2,1)S(1)}, u32[]{:S(2)}, u32[]{:S(2)}) %collective-permute-start.14) | collective-permute-done | bytes 147488 | tf_op jit(solution)/shard_map/ppermute | solution.py:431
  75.2 1.3 %collective-permute-done.16.refs_3_ = bf16[288,256]{1,0:T(8,128)(2,1)S(1)} collective-permute-done((bf16[288,256]{1,0:T(8,128)(2,1)S(1)}, bf16[288,256]{1,0:T(8,128)(2,1)S(1)}, u32[]{:S(2)}, u32[]{:S(2)}) %collective-permute-start.16) | collective-permute-done | bytes 147488 | tf_op jit(solution)/shard_map/ppermute | solution.py:45
  76.6 1.1 %collect.1 = f32[1152,256]{1,0:T(8,128)} custom-call(s32[1]{0:T(128)} %bitcast.core, bf16[288,256]{1,0:T(8,128)(2,1)S(1)} %added.8.refs_0_, bf16[288,256]{1,0:T(8,128)(2,1)S(1)} %added.11.refs_1_, bf16[288,256]{1,0:T(8,128)(2,1)S(1)} %collective-permute-done.15.refs_2_, bf16[288,256]{1,0:T(8,128)(2,1)S(1)} %collective-permute-done.16.refs_3_), custom_call_target="tpu_custom_call" | custom-call | tf_op jit(solution)/shard_map/collect/pallas_call | solution.py:400
  (35 shorter events, 0.7 us)
Async XLA Ops:
  0.0 12.5 %collective-permute-start.2 = (s32[2048]{0:T(1024)}, s32[2048]{0:T(1024)S(1)}, u32[]{:S(2)}, u32[]{:S(2)}) collective-permute-start(s32[2048]{0:T(1024)} %wanted.1), channel_id=1, source_target_pairs={{0,4},{4,0},{1,5},{5,1},{2,6},{6,2},{3,7},{7,3},{8,12},{12,8},{9,1... | collective-permute-start | bytes 24584 | tf_op jit(solution)/shard_map/ppermute | solution.py:45
  3.9 8.7 %collective-permute-start.3 = (bf16[128,256]{1,0:T(8,128)(2,1)S(1)}, bf16[128,256]{1,0:T(8,128)(2,1)S(1)}, u32[]{:S(2)}, u32[]{:S(2)}) collective-permute-start(bf16[128,256]{1,0:T(8,128)(2,1)S(1)} %slice_select_fusion), channel_id=1, source_target_pairs={{0,4},{4,0},{1,5},{5,1},{2,6},{6,2},{3,7},{7,3},{8,12},{12,8},{9,1... | collective-permute-start | bytes 196616 | tf_op jit(solution)/shard_map/ppermute | solution.py:22
  3.9 8.5 %copy-start.5 = (s32[8,4096]{1,0:T(8,128)S(1)}, s32[8,4096]{1,0:T(8,128)}, u32[]{:S(2)}) copy-start(s32[8,4096]{1,0:T(8,128)} %param.14) | copy-start | bytes 393220
  3.9 8.6 %copy-start = (bf16[1152,256]{1,0:T(8,128)(2,1)S(1)}, bf16[1152,256]{1,0:T(8,128)(2,1)}, u32[]{:S(2)}) copy-start(bf16[1152,256]{1,0:T(8,128)(2,1)} %weight.5) | copy-start | bytes 1769476
  4.0 8.6 %copy-start.4 = (f32[8,256]{1,0:T(8,128)S(1)}, f32[8,256]{1,0:T(8,128)}, u32[]{:S(2)}) copy-start(f32[8,256]{1,0:T(8,128)} %mixing.3) | copy-start | bytes 24580
  7.9 21.6 %collective-permute-start = (bf16[512,256]{1,0:T(8,128)(2,1)}, bf16[512,256]{1,0:T(8,128)(2,1)S(1)}, u32[]{:S(2)}, u32[]{:S(2)}) collective-permute-start(bf16[512,256]{1,0:T(8,128)(2,1)} %get-tuple-element.21), channel_id=1, source_target_pairs={{0,2},{1,3},{2,0},{3,1},{4,6},{5,7},{6,4},{7,5},{8,10},{9,11},{10,... | collective-permute-start | bytes 786440 | tf_op jit(solution)/shard_map/ppermute | solution.py:45
  11.0 18.5 %collective-permute-start.1 = (bf16[512,256]{1,0:T(8,128)(2,1)}, bf16[512,256]{1,0:T(8,128)(2,1)S(1)}, u32[]{:S(2)}, u32[]{:S(2)}) collective-permute-start(bf16[512,256]{1,0:T(8,128)(2,1)} %get-tuple-element.22), channel_id=1, source_target_pairs={{0,3},{1,2},{2,1},{3,0},{4,7},{5,6},{6,5},{7,4},{8,11},{9,10},{10,... | collective-permute-start | bytes 786440 | tf_op jit(solution)/shard_map/ppermute | solution.py:45
  12.6 8.7 %copy-start.3 = (s32[2048]{0:T(1024)S(1)}, s32[2048]{0:T(1024)}, u32[]{:S(2)}) copy-start(s32[2048]{0:T(1024)} %wanted.1) | copy-start | bytes 24580
  19.4 14.4 %collective-permute-start.4 = (bf16[512,256]{1,0:T(8,128)(2,1)S(1)}, bf16[512,256]{1,0:T(8,128)(2,1)S(1)}, u32[]{:S(2)}, u32[]{:S(2)}) collective-permute-start(bf16[512,256]{1,0:T(8,128)(2,1)S(1)} %get-tuple-element.25), channel_id=1, source_target_pairs={{0,1},{1,0},{2,3},{3,2},{4,5},{5,4},{6,7},{7,6},{8,9},{9,8},{10,11... | collective-permute-start | bytes 786440 | tf_op jit(solution)/shard_map/ppermute | solution.py:45
  19.7 14.1 %collective-permute-start.5 = (bf16[512,256]{1,0:T(8,128)(2,1)S(1)}, bf16[512,256]{1,0:T(8,128)(2,1)S(1)}, u32[]{:S(2)}, u32[]{:S(2)}) collective-permute-start(bf16[512,256]{1,0:T(8,128)(2,1)S(1)} %get-tuple-element.29), channel_id=1, source_target_pairs={{0,4},{4,0},{1,5},{5,1},{2,6},{6,2},{3,7},{7,3},{8,12},{12,8},{9,1... | collective-permute-start | bytes 786440 | tf_op jit(solution)/shard_map/ppermute | solution.py:45
  21.3 12.5 %copy-start.1 = (s32[2048,1]{0,1:T(1,128)S(1)}, s32[2048,1]{0,1:T(1,128)}, u32[]{:S(2)}) copy-start(s32[2048,1]{0,1:T(1,128)} %param.10) | copy-start | bytes 24580
  21.3 12.5 %copy-start.2 = (f32[2048]{0:T(1024)S(1)}, f32[2048]{0:T(1024)}, u32[]{:S(2)}) copy-start(f32[2048]{0:T(1024)} %param.12) | copy-start | bytes 24580
  34.9 11.1 %collective-permute-start.6 = (bf16[512,256]{1,0:T(8,128)(2,1)S(1)}, bf16[512,256]{1,0:T(8,128)(2,1)S(1)}, u32[]{:S(2)}, u32[]{:S(2)}) collective-permute-start(bf16[512,256]{1,0:T(8,128)(2,1)S(1)} %pre_gradient.1.first), channel_id=1, source_target_pairs={{0,3},{1,2},{2,1},{3,0},{4,7},{5,6},{6,5},{7,4},{8,11},{9,10},{10,... | collective-permute-start | bytes 786440 | tf_op jit(solution)/shard_map/ppermute | solution.py:45
  38.5 13.1 %collective-permute-start.7 = (bf16[512,256]{1,0:T(8,128)(2,1)S(1)}, bf16[512,256]{1,0:T(8,128)(2,1)S(1)}, u32[]{:S(2)}, u32[]{:S(2)}) collective-permute-start(bf16[512,256]{1,0:T(8,128)(2,1)S(1)} %pre_gradient.1.first), channel_id=1, source_target_pairs={{0,1},{1,0},{2,3},{3,2},{4,5},{5,4},{6,7},{7,6},{8,9},{9,8},{10,11... | collective-permute-start | bytes 786440 | tf_op jit(solution)/shard_map/ppermute | solution.py:45
  38.5 22.5 %collective-permute-start.8 = (bf16[512,256]{1,0:T(8,128)(2,1)S(1)}, bf16[512,256]{1,0:T(8,128)(2,1)S(1)}, u32[]{:S(2)}, u32[]{:S(2)}) collective-permute-start(bf16[512,256]{1,0:T(8,128)(2,1)S(1)} %pre_gradient.1.first), channel_id=1, source_target_pairs={{0,2},{1,3},{2,0},{3,1},{4,6},{5,7},{6,4},{7,5},{8,10},{9,11},{10,... | collective-permute-start | bytes 786440 | tf_op jit(solution)/shard_map/ppermute | solution.py:45
  61.6 1.4 %collective-permute-start.9 = (bf16[288,256]{1,0:T(8,128)(2,1)S(1)}, bf16[288,256]{1,0:T(8,128)(2,1)S(1)}, u32[]{:S(2)}, u32[]{:S(2)}) collective-permute-start(bf16[288,256]{1,0:T(8,128)(2,1)S(1)} %get-tuple-element.34), channel_id=1, source_target_pairs={{0,8},{8,0},{16,24},{24,16},{1,9},{9,1},{17,25},{25,17},{2,10},{10... | collective-permute-start | bytes 442376 | tf_op jit(solution)/shard_map/ppermute | solution.py:45
  61.6 2.9 %collective-permute-start.12 = (bf16[288,256]{1,0:T(8,128)(2,1)S(1)}, bf16[288,256]{1,0:T(8,128)(2,1)S(1)}, u32[]{:S(2)}, u32[]{:S(2)}) collective-permute-start(bf16[288,256]{1,0:T(8,128)(2,1)S(1)} %get-tuple-element.36), channel_id=1, source_target_pairs={{0,8},{8,0},{16,24},{24,16},{1,9},{9,1},{17,25},{25,17},{2,10},{10... | collective-permute-start | bytes 442376 | tf_op jit(solution)/shard_map/ppermute | solution.py:45
  63.0 5.2 %collective-permute-start.10 = (bf16[288,256]{1,0:T(8,128)(2,1)S(1)}, bf16[288,256]{1,0:T(8,128)(2,1)S(1)}, u32[]{:S(2)}, u32[]{:S(2)}) collective-permute-start(bf16[288,256]{1,0:T(8,128)(2,1)S(1)} %added.6.first), channel_id=1, source_target_pairs={{0,16},{4,20},{8,12},{12,8},{16,0},{20,4},{24,28},{28,24},{1,17},{... | collective-permute-start | bytes 442376 | tf_op jit(solution)/shard_map/ppermute | solution.py:431
  64.6 5.2 %collective-permute-start.13 = (bf16[288,256]{1,0:T(8,128)(2,1)S(1)}, bf16[288,256]{1,0:T(8,128)(2,1)S(1)}, u32[]{:S(2)}, u32[]{:S(2)}) collective-permute-start(bf16[288,256]{1,0:T(8,128)(2,1)S(1)} %added.9.first), channel_id=1, source_target_pairs={{0,16},{4,20},{8,12},{12,8},{16,0},{20,4},{24,28},{28,24},{1,17},{... | collective-permute-start | bytes 442376 | tf_op jit(solution)/shard_map/ppermute | solution.py:431
  68.3 5.2 %collective-permute-start.11 = (bf16[288,256]{1,0:T(8,128)(2,1)S(1)}, bf16[288,256]{1,0:T(8,128)(2,1)S(1)}, u32[]{:S(2)}, u32[]{:S(2)}) collective-permute-start(bf16[288,256]{1,0:T(8,128)(2,1)S(1)} %added.7.first), channel_id=1, source_target_pairs={{0,4},{4,0},{8,24},{12,28},{16,20},{20,16},{24,8},{28,12},{1,5},{5... | collective-permute-start | bytes 442376 | tf_op jit(solution)/shard_map/ppermute | solution.py:431
  69.9 5.2 %collective-permute-start.14 = (bf16[288,256]{1,0:T(8,128)(2,1)S(1)}, bf16[288,256]{1,0:T(8,128)(2,1)S(1)}, u32[]{:S(2)}, u32[]{:S(2)}) collective-permute-start(bf16[288,256]{1,0:T(8,128)(2,1)S(1)} %added.10.first), channel_id=1, source_target_pairs={{0,4},{4,0},{8,24},{12,28},{16,20},{20,16},{24,8},{28,12},{1,5},{5... | collective-permute-start | bytes 442376 | tf_op jit(solution)/shard_map/ppermute | solution.py:431
  73.5 1.7 %collective-permute-start.15 = (bf16[288,256]{1,0:T(8,128)(2,1)S(1)}, bf16[288,256]{1,0:T(8,128)(2,1)S(1)}, u32[]{:S(2)}, u32[]{:S(2)}) collective-permute-start(bf16[288,256]{1,0:T(8,128)(2,1)S(1)} %added.8.refs_0_), channel_id=1, source_target_pairs={{0,8},{8,0},{16,24},{24,16},{1,9},{9,1},{17,25},{25,17},{2,10},{10... | collective-permute-start | bytes 442376 | tf_op jit(solution)/shard_map/ppermute | solution.py:45
  75.2 1.4 %collective-permute-start.16 = (bf16[288,256]{1,0:T(8,128)(2,1)S(1)}, bf16[288,256]{1,0:T(8,128)(2,1)S(1)}, u32[]{:S(2)}, u32[]{:S(2)}) collective-permute-start(bf16[288,256]{1,0:T(8,128)(2,1)S(1)} %added.11.refs_1_), channel_id=1, source_target_pairs={{0,8},{8,0},{16,24},{24,16},{1,9},{9,1},{17,25},{25,17},{2,10},{10... | collective-permute-start | bytes 442376 | tf_op jit(solution)/shard_map/ppermute | solution.py:45

commit v22 on v20

--- a/solution.py
+++ b/solution.py
@@ -213,11 +213,12 @@
     return outs[:2], outs[2:]
 
 
-def pixel_kernel(count, bits, where, places, wanted, cotangent, above, below, mixing, weight,
+def pixel_kernel(count, bits, stride, where, places, wanted, cotangent, above, below, mixing, weight,
                  spectra, out, *refs):
     quarters, refs = refs[: len(bits)], refs[len(bits) :]
     table, scale, sums, near, names, held, tile, sems = refs
-    start, chan = where[0], where[1]
+    chan = where[0]
+    start = chan * stride
     tile_rows, half = tile.shape[0], table.shape[1]
     listed = names.shape[0]
     first_name = pl.multiple_of(start // listed * listed, listed)
@@ -292,7 +293,7 @@
 
 
 def pixel_rows(
-    cotangent, above, below, places, mixing, wanted, start, count, spectra, weight, chan, bits
+    cotangent, above, below, places, mixing, wanted, stride, count, spectra, weight, chan, bits
 ):
     tile_rows, width = cotangent.shape
     depth, rows = spectra.shape[1], spectra.shape[0] // 4
@@ -301,7 +302,7 @@
     hbm = pl.BlockSpec(memory_space=pltpu.HBM)
     vmem = pl.BlockSpec(memory_space=pltpu.VMEM)
     return pl.pallas_call(
-        functools.partial(pixel_kernel, count, bits),
+        functools.partial(pixel_kernel, count, bits, stride),
         out_shape=(
             jax.ShapeDtypeStruct((count, width), jnp.bfloat16),
             *[jax.ShapeDtypeStruct((rows, width), jnp.bfloat16)] * len(bits),
@@ -333,12 +334,12 @@
         ),
         name="pixel_rows",
     )(
-        jnp.stack([start, chan]), places, wanted, cotangent, above, below, mixing, weight, spectra
+        chan.reshape(1), places, wanted, cotangent, above, below, mixing, weight, spectra
     )
 
 
-def gradient_kernel(where, keep, near, far, tiles, weights, mine, answers, out):
-    tile, chan = where[0], where[1]
+def gradient_kernel(tile_at, chan_at, keep, near, far, tiles, weights, mine, answers, out):
+    tile, chan = tile_at[0], chan_at[0]
     rows = out.shape[0]
     size = tiles.shape[1]
     count = rows // size
@@ -375,35 +376,49 @@
     return pl.pallas_call(
         gradient_kernel,
         out_shape=jax.ShapeDtypeStruct(far.shape, jnp.bfloat16),
-        in_specs=[pl.BlockSpec(memory_space=pltpu.SMEM)] + [spec] * 7,
+        in_specs=[pl.BlockSpec(memory_space=pltpu.SMEM)] * 2 + [spec] * 7,
         out_specs=spec,
         compiler_params=memory(16),
         name="pre_gradient",
-    )(jnp.stack([tile, chan]), keep, near, far, tiles, weights, mine, answers)
-
-
-def collect_kernel(core, *refs):
-    *pieces, out = refs
-    half, rows = out.shape[0] // 2, pieces[0].shape[0]
-    count = len(pieces) // 2
-    for index, piece in enumerate(pieces):
-        which = core[0] if index < count else 1 - core[0]
-        first = which * half + (index % count) * rows
-        out[pl.ds(pl.multiple_of(first, rows), rows), :] = piece[...].astype(jnp.float32)
+    )(tile.reshape(1), chan.reshape(1), keep, near, far, tiles, weights, mine, answers)
+
+
+def write_kernel(other, core, *refs):
+    *pieces, out, first, second, sems = refs
+    half, rows = out.shape[0] // 2, first.shape[0]
+    copies = []
+    for index, (piece, held) in enumerate(zip(pieces[-2:], (first, second))):
+        held[...] = piece[...].astype(jnp.float32)
+        place = (core[0] ^ other) * half + index * rows
+        here = out.at[pl.ds(pl.multiple_of(place, rows), rows)]
+        copies.append(pltpu.make_async_copy(held, here, sems.at[index]))
+        copies[-1].start()
+    for copy in copies:
+        copy.wait()
+
+
+def written(other, core, pieces, before=()):
+    rows, width = pieces[0].shape
+    spec = pl.BlockSpec(memory_space=pltpu.VMEM)
+    hbm = pl.BlockSpec(memory_space=pltpu.HBM)
+    return pl.pallas_call(
+        functools.partial(write_kernel, other),
+        out_shape=jax.ShapeDtypeStruct((4 * rows, width), jnp.float32),
+        in_specs=[pl.BlockSpec(memory_space=pltpu.SMEM)] + [hbm] * len(before) + [spec] * 2,
+        out_specs=hbm,
+        input_output_aliases={1: 0} if before else {},
+        scratch_shapes=[
+            pltpu.VMEM((rows, width), jnp.float32),
+            pltpu.VMEM((rows, width), jnp.float32),
+            pltpu.SemaphoreType.DMA((2,)),
+        ],
+        compiler_params=memory(16),
+        name="written",
+    )(core.reshape(1), *before, *pieces)
 
 
 def collect(core, own, received):
-    spec = pl.BlockSpec(memory_space=pltpu.VMEM)
-    pieces = [*own, *received]
-    rows, width = sum(piece.shape[0] for piece in pieces), own[0].shape[1]
-    return pl.pallas_call(
-        collect_kernel,
-        out_shape=jax.ShapeDtypeStruct((rows, width), jnp.float32),
-        in_specs=[pl.BlockSpec(memory_space=pltpu.SMEM)] + [spec] * len(pieces),
-        out_specs=spec,
-        compiler_params=memory(16),
-        name="collect",
-    )(core.reshape(1), *pieces)
+    return written(1, core, received, (written(0, core, own),))
 
 
 def add_kernel(first, second, out):
@@ -449,13 +464,13 @@
     rest = (spectra, enc_weight)
     paired = capacity >= quarter and tile_count == 2
     if paired:
-        wanted, start, count = swap(pix_local, "pix", 1), first_row, quarter
+        wanted, stride, count = swap(pix_local, "pix", 1), quarter, quarter
     else:
         tile_ids = lax.dynamic_slice_in_dim(pix_tile[:, 0], first_row, quarter, 0)
         local_ids = lax.dynamic_slice_in_dim(pix_local, first_row, quarter, 0)
         slot_index, wanted = requests(tile_ids, local_ids, capacity)
-        start, count = 0 * chan, wanted.shape[0]
-    rows, shared, send = pixel_rows(*pixels, wanted, start, count, *rest, chan, (3, 1))
+        stride, count = 0, wanted.shape[0]
+    rows, shared, send = pixel_rows(*pixels, wanted, stride, count, *rest, chan, (3, 1))
     near_first, rows = lax.optimization_barrier((near_first, rows))
     passed_on = (shared.astype(jnp.float32) + near_first.astype(jnp.float32)).astype(jnp.bfloat16)
     passed_on, send, rows, later = lax.optimization_barrier((passed_on, send, rows, chan))
@@ -463,7 +478,7 @@
     near = swap(send, "chan", 1)
     if paired:
         answers = swap(rows, "pix", 1)
-        mine, keep = pixel_rows(*pixels, pix_local, later * quarter, count, *rest, later, (0,))
+        mine, keep = pixel_rows(*pixels, pix_local, stride, count, *rest, later, (0,))
     else:
         (keep,) = project(*rest, later, (0,), LARGE)
         answers = lax.all_to_all(

time: 67.6 us -> 66.2 us (0.979)
  Pallas kernels: 23.4 us -> 22.4 us
    pallas_call x3 -> x4, Pallas kernels: 15.8 us -> 15.4 us  [the longest x2 13.7 us: pixel_rows(): pl.pallas_call(functools.partial(pixel_kernel, count, bits, stride), out_...]
  transfers between devices with their start and end apart: 17 -> 17, of which waited for: 9 -> 9; matrix products, arithmetic and copies ran while one was open for 2% -> 1% of each run, Pallas kernels for 31% -> 31%
where the time goes in v22:
time: 66.2 us; the launch traced here: 66 us
  waiting for transfers between devices  22.7 us (34%)
  Pallas kernels  22.4 us (34%)
  starting transfers between devices  19.6 us (30%)
  other arithmetic  0.98 us (1%)
    ppermute x12, waiting for transfers between devices, swap(): return lax.ppermute(value, axis, [(i, i ^ bit) for i in range(size)])  16.1 us
    ppermute x12, starting transfers between devices, swap(): return lax.ppermute(value, axis, [(i, i ^ bit) for i in range(size)])  14.2 us
    pallas_call x2, Pallas kernels, pixel_rows(): pl.pallas_call(functools.partial(pixel_kernel, count, bits, stride), out_...  13.7 us
    ppermute x4, waiting for transfers between devices, sum_over_panels(): parts = [added(part, lax.ppermute(part, both, perm)) for part in parts]  6.57 us
    ppermute x4, starting transfers between devices, sum_over_panels(): parts = [added(part, lax.ppermute(part, both, perm)) for part in parts]  5.33 us
    pallas_call x1, Pallas kernels, project(): pl.pallas_call(functools.partial(project_kernel, bits), out_shape=(jax.Sh...  2.74 us
    pallas_call x1, Pallas kernels, early_product(): pl.pallas_call(early_kernel, out_shape=(jax.ShapeDtypeStruct((depth, widt...  2.49 us
    pallas_call x2, Pallas kernels, written(): pl.pallas_call(functools.partial(write_kernel, other), out_shape=jax.Shap...  1.7 us
  transfers between devices with their start and end apart: 17, of which 9 were waited for; matrix products, arithmetic and copies ran while one was open for 1% of the time, Pallas kernels for 31%

profile of v22, /device:TPU:0, one launch (start us, length us, event | category | flops | bytes accessed | tf_op | source)
XLA Modules:
  0.0 66.0 jit_solution(8568417796945250445)
XLA Ops:
  0.0 3.0 %collective-permute-start = (s32[2048]{0:T(1024)}, s32[2048]{0:T(1024)S(1)}, u32[]{:S(2)}, u32[]{:S(2)}) collective-permute-start(s32[2048]{0:T(1024)} %wanted.1), channel_id=1, source_target_pairs={{0,4},{4,0},{1,5},{5,1},{2,6},{6,2},{3,7},{7,3},{8,12},{12,8},{9,1... | collective-permute-start | bytes 24584 | tf_op jit(solution)/shard_map/ppermute | solution.py:45
  3.0 0.9 %slice_select_fusion = bf16[128,256]{1,0:T(8,128)(2,1)S(1)} fusion(bf16[4096,256]{1,0:T(8,128)(2,1)} %cotangent.3, pred[]{:T(512)S(6)} %eq.3), kind=kLoop, calls=%fused_computation.5 | loop fusion | flops 32768 | bytes 196609 | tf_op jit(solution)/shard_map/jit(_where)/select_n | solution.py:22
  4.0 2.7 %project.1 = bf16[512,256]{1,0:T(8,128)(2,1)} custom-call(s32[1]{0:T(128)} %bitcast.1.where.chan.chan_at, bf16[2048,1152]{1,0:T(8,128)(2,1)} %spectra.7, bf16[1152,256]{1,0:T(8,128)(2,1)} %weight.5), custom_call_target="tpu_custom_call" | custom-call | flops 301989888 | bytes 2031616 | tf_op jit(solution)/shard_map/project/pallas_call | solution.py:88
  6.7 2.1 %collective-permute-start.2 = (bf16[512,256]{1,0:T(8,128)(2,1)}, bf16[512,256]{1,0:T(8,128)(2,1)S(1)}, u32[]{:S(2)}, u32[]{:S(2)}) collective-permute-start(bf16[512,256]{1,0:T(8,128)(2,1)} %project.1), channel_id=1, source_target_pairs={{0,1},{1,0},{2,3},{3,2},{4,5},{5,4},{6,7},{7,6},{8,9},{9,8},{10,11... | collective-permute-start | bytes 786440 | tf_op jit(solution)/shard_map/ppermute | solution.py:45
  8.9 7.4 %pixel_rows.2 = (bf16[512,256]{1,0:T(8,128)(2,1)S(1)}, bf16[512,256]{1,0:T(8,128)(2,1)S(1)}, bf16[512,256]{1,0:T(8,128)(2,1)S(1)}) custom-call(s32[1]{0:T(128)} %bitcast.1.where.chan.chan_at, s32[16384]{0:T(1024)S(1)} %bitcast.9, s32[2048]{0:T(1024)S(1)} %collective-permute-done.wanted, bf16[4096,256]{1,0:T(8,128)(2,1)} %cotangent.3, ...), custom_call_target="tpu_custom_call" | custom-call | flops 17179869184 | bytes 4194304 | tf_op jit(solution)/shard_map/pixel_rows/pallas_call | solution.py:304
  16.4 0.9 %collective-permute-start.3 = (bf16[512,256]{1,0:T(8,128)(2,1)S(1)}, bf16[512,256]{1,0:T(8,128)(2,1)S(1)}, u32[]{:S(2)}, u32[]{:S(2)}) collective-permute-start(bf16[512,256]{1,0:T(8,128)(2,1)S(1)} %get-tuple-element.30), channel_id=1, source_target_pairs={{0,1},{1,0},{2,3},{3,2},{4,5},{5,4},{6,7},{7,6},{8,9},{9,8},{10,11... | collective-permute-start | bytes 786440 | tf_op jit(solution)/shard_map/ppermute | solution.py:45
  17.3 3.2 %collective-permute-start.4 = (bf16[512,256]{1,0:T(8,128)(2,1)S(1)}, bf16[512,256]{1,0:T(8,128)(2,1)S(1)}, u32[]{:S(2)}, u32[]{:S(2)}) collective-permute-start(bf16[512,256]{1,0:T(8,128)(2,1)S(1)} %add_convert_fusion), channel_id=1, source_target_pairs={{0,3},{1,2},{2,1},{3,0},{4,7},{5,6},{6,5},{7,4},{8,11},{9,10},{10,... | collective-permute-start | bytes 786440 | tf_op jit(solution)/shard_map/ppermute | solution.py:45
  20.5 1.5 %collective-permute-start.5 = (bf16[512,256]{1,0:T(8,128)(2,1)S(1)}, bf16[512,256]{1,0:T(8,128)(2,1)S(1)}, u32[]{:S(2)}, u32[]{:S(2)}) collective-permute-start(bf16[512,256]{1,0:T(8,128)(2,1)S(1)} %get-tuple-element.33), channel_id=1, source_target_pairs={{0,4},{4,0},{1,5},{5,1},{2,6},{6,2},{3,7},{7,3},{8,12},{12,8},{9,1... | collective-permute-start | bytes 786440 | tf_op jit(solution)/shard_map/ppermute | solution.py:45
  22.1 6.3 %pixel_rows.3 = (bf16[512,256]{1,0:T(8,128)(2,1)S(1)}, bf16[512,256]{1,0:T(8,128)(2,1)S(1)}) custom-call(s32[1]{0:T(128)} %bitcast.3.where, s32[16384]{0:T(1024)S(1)} %bitcast.10, s32[2048]{0:T(1024)S(1)} %copy-done.3, bf16[4096,256]{1,0:T(8,128)(2,1)} %cotangent.3, bf16[128,256]{1,0:T(8,128)(2,1)S(1)} %collective-permute-done.1.above.below, ...), custom_call_target="tpu_custom_call" | custom-call | flops 17179869184 | bytes 4194304 | tf_op jit(solution)/shard_map/pixel_rows/pallas_call | solution.py:304
  28.4 3.1 %collective-permute-done.4.far = bf16[512,256]{1,0:T(8,128)(2,1)S(1)} collective-permute-done((bf16[512,256]{1,0:T(8,128)(2,1)S(1)}, bf16[512,256]{1,0:T(8,128)(2,1)S(1)}, u32[]{:S(2)}, u32[]{:S(2)}) %collective-permute-start.4) | collective-permute-done | bytes 262176 | tf_op jit(solution)/shard_map/ppermute | solution.py:45
  31.5 0.5 pre_gradient.1.first
  32.0 0.4 collective-permute-start.6
  32.4 2.3 %collective-permute-start.7 = (bf16[512,256]{1,0:T(8,128)(2,1)S(1)}, bf16[512,256]{1,0:T(8,128)(2,1)S(1)}, u32[]{:S(2)}, u32[]{:S(2)}) collective-permute-start(bf16[512,256]{1,0:T(8,128)(2,1)S(1)} %pre_gradient.1.first), channel_id=1, source_target_pairs={{0,1},{1,0},{2,3},{3,2},{4,5},{5,4},{6,7},{7,6},{8,9},{9,8},{10,11... | collective-permute-start | bytes 786440 | tf_op jit(solution)/shard_map/ppermute | solution.py:45
  34.7 8.4 %collective-permute-done.6.second = bf16[512,256]{1,0:T(8,128)(2,1)S(1)} collective-permute-done((bf16[512,256]{1,0:T(8,128)(2,1)S(1)}, bf16[512,256]{1,0:T(8,128)(2,1)S(1)}, u32[]{:S(2)}, u32[]{:S(2)}) %collective-permute-start.6) | collective-permute-done | bytes 262176 | tf_op jit(solution)/shard_map/ppermute | solution.py:45
  43.1 0.1 collective-permute-start.8
  43.2 2.5 %early_product.1 = (f32[1152,256]{1,0:T(8,128)S(1)}, bf16[512,1152]{1,0:T(8,128)(2,1)S(1)}, bf16[512,1152]{1,0:T(8,128)(2,1)S(1)}) custom-call(s32[1]{0:T(128)} %bitcast.1.where.chan.chan_at, bf16[2048,1152]{1,0:T(8,128)(2,1)} %spectra.7, bf16[512,256]{1,0:T(8,128)(2,1)S(1)} %pre_gradient.1.first, bf16[512,256]{1,0:T(8,128)(2,1)S(1)} %collective-permute-done.6.second), custom_call_target="tpu_custom_call" | custom-call | flops 603979776 | bytes 5898240 | tf_op jit(solution)/shard_map/early_product/pallas_call | solution.py:135
  45.7 0.1 collective-permute-done.7.rows
  45.8 0.5 more_product.1.before
  46.4 3.2 %collective-permute-done.8.rows = bf16[512,256]{1,0:T(8,128)(2,1)S(1)} collective-permute-done((bf16[512,256]{1,0:T(8,128)(2,1)S(1)}, bf16[512,256]{1,0:T(8,128)(2,1)S(1)}, u32[]{:S(2)}, u32[]{:S(2)}) %collective-permute-start.8) | collective-permute-done | bytes 262176 | tf_op jit(solution)/shard_map/ppermute | solution.py:45
  49.5 0.6 late_product.1
  50.2 0.5 collective-permute-start.12
  50.7 0.9 %collective-permute-done.9.second = bf16[288,256]{1,0:T(8,128)(2,1)S(1)} collective-permute-done((bf16[288,256]{1,0:T(8,128)(2,1)S(1)}, bf16[288,256]{1,0:T(8,128)(2,1)S(1)}, u32[]{:S(2)}, u32[]{:S(2)}) %collective-permute-start.9) | collective-permute-done | bytes 147488 | tf_op jit(solution)/shard_map/ppermute | solution.py:45
  51.6 1.6 %collective-permute-start.10 = (bf16[288,256]{1,0:T(8,128)(2,1)S(1)}, bf16[288,256]{1,0:T(8,128)(2,1)S(1)}, u32[]{:S(2)}, u32[]{:S(2)}) collective-permute-start(bf16[288,256]{1,0:T(8,128)(2,1)S(1)} %added.6.first), channel_id=1, source_target_pairs={{0,16},{4,20},{8,12},{12,8},{16,0},{20,4},{24,28},{28,24},{1,17},{... | collective-permute-start | bytes 442376 | tf_op jit(solution)/shard_map/ppermute | solution.py:445
  53.2 0.6 collective-permute-start.13
  53.8 3.0 %collective-permute-done.10.second = bf16[288,256]{1,0:T(8,128)(2,1)S(1)} collective-permute-done((bf16[288,256]{1,0:T(8,128)(2,1)S(1)}, bf16[288,256]{1,0:T(8,128)(2,1)S(1)}, u32[]{:S(2)}, u32[]{:S(2)}) %collective-permute-start.10) | collective-permute-done | bytes 147488 | tf_op jit(solution)/shard_map/ppermute | solution.py:445
  56.8 1.6 %collective-permute-start.11 = (bf16[288,256]{1,0:T(8,128)(2,1)S(1)}, bf16[288,256]{1,0:T(8,128)(2,1)S(1)}, u32[]{:S(2)}, u32[]{:S(2)}) collective-permute-start(bf16[288,256]{1,0:T(8,128)(2,1)S(1)} %added.7.first), channel_id=1, source_target_pairs={{0,4},{4,0},{8,24},{12,28},{16,20},{20,16},{24,8},{28,12},{1,5},{5... | collective-permute-start | bytes 442376 | tf_op jit(solution)/shard_map/ppermute | solution.py:445
  58.5 1.5 %collective-permute-start.14 = (bf16[288,256]{1,0:T(8,128)(2,1)S(1)}, bf16[288,256]{1,0:T(8,128)(2,1)S(1)}, u32[]{:S(2)}, u32[]{:S(2)}) collective-permute-start(bf16[288,256]{1,0:T(8,128)(2,1)S(1)} %added.10.first), channel_id=1, source_target_pairs={{0,4},{4,0},{8,24},{12,28},{16,20},{20,16},{24,8},{28,12},{1,5},{5... | collective-permute-start | bytes 442376 | tf_op jit(solution)/shard_map/ppermute | solution.py:445
  60.0 2.0 %collective-permute-done.11.second = bf16[288,256]{1,0:T(8,128)(2,1)S(1)} collective-permute-done((bf16[288,256]{1,0:T(8,128)(2,1)S(1)}, bf16[288,256]{1,0:T(8,128)(2,1)S(1)}, u32[]{:S(2)}, u32[]{:S(2)}) %collective-permute-start.11) | collective-permute-done | bytes 147488 | tf_op jit(solution)/shard_map/ppermute | solution.py:445
  62.2 1.6 %collective-permute-done.14.second = bf16[288,256]{1,0:T(8,128)(2,1)S(1)} collective-permute-done((bf16[288,256]{1,0:T(8,128)(2,1)S(1)}, bf16[288,256]{1,0:T(8,128)(2,1)S(1)}, u32[]{:S(2)}, u32[]{:S(2)}) %collective-permute-start.14) | collective-permute-done | bytes 147488 | tf_op jit(solution)/shard_map/ppermute | solution.py:445
  63.8 0.9 %written.2.refs_0_ = f32[1152,256]{1,0:T(8,128)} custom-call(s32[1]{0:T(128)} %bitcast.core, bf16[288,256]{1,0:T(8,128)(2,1)S(1)} %added.8.refs_0_, bf16[288,256]{1,0:T(8,128)(2,1)S(1)} %added.11.refs_1_), custom_call_target="tpu_custom_call" | custom-call | tf_op jit(solution)/shard_map/written/pallas_call | solution.py:404
  64.7 0.5 collective-permute-done.16.refs_2_
  65.2 0.8 %written.3 = f32[1152,256]{1,0:T(8,128)} custom-call(s32[1]{0:T(128)} %bitcast.core, f32[1152,256]{1,0:T(8,128)} %written.2.refs_0_, bf16[288,256]{1,0:T(8,128)(2,1)S(1)} %collective-permute-done.15.refs_1_, bf16[288,256]{1,0:T(8,128)(2,1)S(1)} %collective-permute-done.16.refs_2_), custom_call_target="tpu_custom_call", output_to_operand_aliasing={{}: (1, {})} | custom-call | tf_op jit(solution)/shard_map/written/pallas_call | solution.py:404
  (34 shorter events, 0.6 us)
Async XLA Ops:
  0.0 8.9 %collective-permute-start = (s32[2048]{0:T(1024)}, s32[2048]{0:T(1024)S(1)}, u32[]{:S(2)}, u32[]{:S(2)}) collective-permute-start(s32[2048]{0:T(1024)} %wanted.1), channel_id=1, source_target_pairs={{0,4},{4,0},{1,5},{5,1},{2,6},{6,2},{3,7},{7,3},{8,12},{12,8},{9,1... | collective-permute-start | bytes 24584 | tf_op jit(solution)/shard_map/ppermute | solution.py:45
  3.9 5.0 %collective-permute-start.1 = (bf16[128,256]{1,0:T(8,128)(2,1)S(1)}, bf16[128,256]{1,0:T(8,128)(2,1)S(1)}, u32[]{:S(2)}, u32[]{:S(2)}) collective-permute-start(bf16[128,256]{1,0:T(8,128)(2,1)S(1)} %slice_select_fusion), channel_id=1, source_target_pairs={{0,4},{4,0},{1,5},{5,1},{2,6},{6,2},{3,7},{7,3},{8,12},{12,8},{9,1... | collective-permute-start | bytes 196616 | tf_op jit(solution)/shard_map/ppermute | solution.py:22
  3.9 4.9 %copy-start.5 = (s32[8,4096]{1,0:T(8,128)S(1)}, s32[8,4096]{1,0:T(8,128)}, u32[]{:S(2)}) copy-start(s32[8,4096]{1,0:T(8,128)} %param.14) | copy-start | bytes 393220
  3.9 5.0 %copy-start = (bf16[1152,256]{1,0:T(8,128)(2,1)S(1)}, bf16[1152,256]{1,0:T(8,128)(2,1)}, u32[]{:S(2)}) copy-start(bf16[1152,256]{1,0:T(8,128)(2,1)} %weight.5) | copy-start | bytes 1769476
  4.0 5.0 %copy-start.4 = (f32[8,256]{1,0:T(8,128)S(1)}, f32[8,256]{1,0:T(8,128)}, u32[]{:S(2)}) copy-start(f32[8,256]{1,0:T(8,128)} %mixing.3) | copy-start | bytes 24580
  6.7 9.6 %collective-permute-start.2 = (bf16[512,256]{1,0:T(8,128)(2,1)}, bf16[512,256]{1,0:T(8,128)(2,1)S(1)}, u32[]{:S(2)}, u32[]{:S(2)}) collective-permute-start(bf16[512,256]{1,0:T(8,128)(2,1)} %project.1), channel_id=1, source_target_pairs={{0,1},{1,0},{2,3},{3,2},{4,5},{5,4},{6,7},{7,6},{8,9},{9,8},{10,11... | collective-permute-start | bytes 786440 | tf_op jit(solution)/shard_map/ppermute | solution.py:45
  8.9 13.1 %copy-start.3 = (s32[2048]{0:T(1024)S(1)}, s32[2048]{0:T(1024)}, u32[]{:S(2)}) copy-start(s32[2048]{0:T(1024)} %wanted.1) | copy-start | bytes 24580
  16.4 11.9 %collective-permute-start.3 = (bf16[512,256]{1,0:T(8,128)(2,1)S(1)}, bf16[512,256]{1,0:T(8,128)(2,1)S(1)}, u32[]{:S(2)}, u32[]{:S(2)}) collective-permute-start(bf16[512,256]{1,0:T(8,128)(2,1)S(1)} %get-tuple-element.30), channel_id=1, source_target_pairs={{0,1},{1,0},{2,3},{3,2},{4,5},{5,4},{6,7},{7,6},{8,9},{9,8},{10,11... | collective-permute-start | bytes 786440 | tf_op jit(solution)/shard_map/ppermute | solution.py:45
  17.3 14.1 %collective-permute-start.4 = (bf16[512,256]{1,0:T(8,128)(2,1)S(1)}, bf16[512,256]{1,0:T(8,128)(2,1)S(1)}, u32[]{:S(2)}, u32[]{:S(2)}) collective-permute-start(bf16[512,256]{1,0:T(8,128)(2,1)S(1)} %add_convert_fusion), channel_id=1, source_target_pairs={{0,3},{1,2},{2,1},{3,0},{4,7},{5,6},{6,5},{7,4},{8,11},{9,10},{10,... | collective-permute-start | bytes 786440 | tf_op jit(solution)/shard_map/ppermute | solution.py:45
  20.5 10.9 %collective-permute-start.5 = (bf16[512,256]{1,0:T(8,128)(2,1)S(1)}, bf16[512,256]{1,0:T(8,128)(2,1)S(1)}, u32[]{:S(2)}, u32[]{:S(2)}) collective-permute-start(bf16[512,256]{1,0:T(8,128)(2,1)S(1)} %get-tuple-element.33), channel_id=1, source_target_pairs={{0,4},{4,0},{1,5},{5,1},{2,6},{6,2},{3,7},{7,3},{8,12},{12,8},{9,1... | collective-permute-start | bytes 786440 | tf_op jit(solution)/shard_map/ppermute | solution.py:45
  22.1 9.4 %copy-start.1 = (s32[2048,1]{0,1:T(1,128)S(1)}, s32[2048,1]{0,1:T(1,128)}, u32[]{:S(2)}) copy-start(s32[2048,1]{0,1:T(1,128)} %param.10) | copy-start | bytes 24580
  22.1 9.4 %copy-start.2 = (f32[2048]{0:T(1024)S(1)}, f32[2048]{0:T(1024)}, u32[]{:S(2)}) copy-start(f32[2048]{0:T(1024)} %param.12) | copy-start | bytes 24580
  32.0 11.1 %collective-permute-start.6 = (bf16[512,256]{1,0:T(8,128)(2,1)S(1)}, bf16[512,256]{1,0:T(8,128)(2,1)S(1)}, u32[]{:S(2)}, u32[]{:S(2)}) collective-permute-start(bf16[512,256]{1,0:T(8,128)(2,1)S(1)} %pre_gradient.1.first), channel_id=1, source_target_pairs={{0,3},{1,2},{2,1},{3,0},{4,7},{5,6},{6,5},{7,4},{8,11},{9,10},{10,... | collective-permute-start | bytes 786440 | tf_op jit(solution)/shard_map/ppermute | solution.py:45
  32.4 13.4 %collective-permute-start.7 = (bf16[512,256]{1,0:T(8,128)(2,1)S(1)}, bf16[512,256]{1,0:T(8,128)(2,1)S(1)}, u32[]{:S(2)}, u32[]{:S(2)}) collective-permute-start(bf16[512,256]{1,0:T(8,128)(2,1)S(1)} %pre_gradient.1.first), channel_id=1, source_target_pairs={{0,1},{1,0},{2,3},{3,2},{4,5},{5,4},{6,7},{7,6},{8,9},{9,8},{10,11... | collective-permute-start | bytes 786440 | tf_op jit(solution)/shard_map/ppermute | solution.py:45
  43.1 6.5 %collective-permute-start.8 = (bf16[512,256]{1,0:T(8,128)(2,1)S(1)}, bf16[512,256]{1,0:T(8,128)(2,1)S(1)}, u32[]{:S(2)}, u32[]{:S(2)}) collective-permute-start(bf16[512,256]{1,0:T(8,128)(2,1)S(1)} %collective-permute-done.6.second), channel_id=1, source_target_pairs={{0,1},{1,0},{2,3},{3,2},{4,5},{5,4},{6,7},{7,6},{8,9},{9,8},{10,11... | collective-permute-start | bytes 786440 | tf_op jit(solution)/shard_map/ppermute | solution.py:45
  50.1 1.4 %collective-permute-start.9 = (bf16[288,256]{1,0:T(8,128)(2,1)S(1)}, bf16[288,256]{1,0:T(8,128)(2,1)S(1)}, u32[]{:S(2)}, u32[]{:S(2)}) collective-permute-start(bf16[288,256]{1,0:T(8,128)(2,1)S(1)} %get-tuple-element.38), channel_id=1, source_target_pairs={{0,8},{8,0},{16,24},{24,16},{1,9},{9,1},{17,25},{25,17},{2,10},{10... | collective-permute-start | bytes 442376 | tf_op jit(solution)/shard_map/ppermute | solution.py:45
  50.2 2.9 %collective-permute-start.12 = (bf16[288,256]{1,0:T(8,128)(2,1)S(1)}, bf16[288,256]{1,0:T(8,128)(2,1)S(1)}, u32[]{:S(2)}, u32[]{:S(2)}) collective-permute-start(bf16[288,256]{1,0:T(8,128)(2,1)S(1)} %get-tuple-element.40), channel_id=1, source_target_pairs={{0,8},{8,0},{16,24},{24,16},{1,9},{9,1},{17,25},{25,17},{2,10},{10... | collective-permute-start | bytes 442376 | tf_op jit(solution)/shard_map/ppermute | solution.py:45
  51.6 5.2 %collective-permute-start.10 = (bf16[288,256]{1,0:T(8,128)(2,1)S(1)}, bf16[288,256]{1,0:T(8,128)(2,1)S(1)}, u32[]{:S(2)}, u32[]{:S(2)}) collective-permute-start(bf16[288,256]{1,0:T(8,128)(2,1)S(1)} %added.6.first), channel_id=1, source_target_pairs={{0,16},{4,20},{8,12},{12,8},{16,0},{20,4},{24,28},{28,24},{1,17},{... | collective-permute-start | bytes 442376 | tf_op jit(solution)/shard_map/ppermute | solution.py:445
  53.2 5.3 %collective-permute-start.13 = (bf16[288,256]{1,0:T(8,128)(2,1)S(1)}, bf16[288,256]{1,0:T(8,128)(2,1)S(1)}, u32[]{:S(2)}, u32[]{:S(2)}) collective-permute-start(bf16[288,256]{1,0:T(8,128)(2,1)S(1)} %added.9.first), channel_id=1, source_target_pairs={{0,16},{4,20},{8,12},{12,8},{16,0},{20,4},{24,28},{28,24},{1,17},{... | collective-permute-start | bytes 442376 | tf_op jit(solution)/shard_map/ppermute | solution.py:445
  56.8 5.2 %collective-permute-start.11 = (bf16[288,256]{1,0:T(8,128)(2,1)S(1)}, bf16[288,256]{1,0:T(8,128)(2,1)S(1)}, u32[]{:S(2)}, u32[]{:S(2)}) collective-permute-start(bf16[288,256]{1,0:T(8,128)(2,1)S(1)} %added.7.first), channel_id=1, source_target_pairs={{0,4},{4,0},{8,24},{12,28},{16,20},{20,16},{24,8},{28,12},{1,5},{5... | collective-permute-start | bytes 442376 | tf_op jit(solution)/shard_map/ppermute | solution.py:445
  58.5 5.2 %collective-permute-start.14 = (bf16[288,256]{1,0:T(8,128)(2,1)S(1)}, bf16[288,256]{1,0:T(8,128)(2,1)S(1)}, u32[]{:S(2)}, u32[]{:S(2)}) collective-permute-start(bf16[288,256]{1,0:T(8,128)(2,1)S(1)} %added.10.first), channel_id=1, source_target_pairs={{0,4},{4,0},{8,24},{12,28},{16,20},{20,16},{24,8},{28,12},{1,5},{5... | collective-permute-start | bytes 442376 | tf_op jit(solution)/shard_map/ppermute | solution.py:445
  62.1 2.6 %collective-permute-start.15 = (bf16[288,256]{1,0:T(8,128)(2,1)S(1)}, bf16[288,256]{1,0:T(8,128)(2,1)S(1)}, u32[]{:S(2)}, u32[]{:S(2)}) collective-permute-start(bf16[288,256]{1,0:T(8,128)(2,1)S(1)} %added.8.refs_0_), channel_id=1, source_target_pairs={{0,8},{8,0},{16,24},{24,16},{1,9},{9,1},{17,25},{25,17},{2,10},{10... | collective-permute-start | bytes 442376 | tf_op jit(solution)/shard_map/ppermute | solution.py:45
  63.8 1.4 %collective-permute-start.16 = (bf16[288,256]{1,0:T(8,128)(2,1)S(1)}, bf16[288,256]{1,0:T(8,128)(2,1)S(1)}, u32[]{:S(2)}, u32[]{:S(2)}) collective-permute-start(bf16[288,256]{1,0:T(8,128)(2,1)S(1)} %added.11.refs_1_), channel_id=1, source_target_pairs={{0,8},{8,0},{16,24},{24,16},{1,9},{9,1},{17,25},{25,17},{2,10},{10... | collective-permute-start | bytes 442376 | tf_op jit(solution)/shard_map/ppermute | solution.py:45

commit v23 on v22

--- a/solution.py
+++ b/solution.py
@@ -13,14 +13,36 @@
 LARGE = 52
 
 
+def edge_kernel(tile, value, out, sem):
+    first = (1 - tile[0]) * (value.shape[0] - out.shape[0])
+    rows = value.at[pl.ds(pl.multiple_of(first, out.shape[0]), out.shape[0])]
+    copy = pltpu.make_async_copy(rows, out, sem)
+    copy.start()
+    copy.wait()
+
+
+def edge(tile, value, width):
+    return pl.pallas_call(
+        edge_kernel,
+        out_shape=jax.ShapeDtypeStruct((width, value.shape[1]), value.dtype),
+        in_specs=[
+            pl.BlockSpec(memory_space=pltpu.SMEM),
+            pl.BlockSpec(memory_space=pltpu.HBM),
+        ],
+        out_specs=pl.BlockSpec(memory_space=pltpu.VMEM),
+        scratch_shapes=[pltpu.SemaphoreType.DMA],
+        compiler_params=memory(LARGE),
+        name="edge",
+    )(tile.reshape(1), value)
+
+
 def edges(value, axis, width):
     size, length = lax.axis_size(axis), value.shape[0]
+    if size == 2:
+        other = swap(edge(lax.axis_index(axis), value, width), axis, 1)
+        return other, other
     last = lax.slice_in_dim(value, length - width, length, axis=0)
     first = lax.slice_in_dim(value, 0, width, axis=0)
-    if size == 2:
-        index = lax.axis_index(axis)
-        other = lax.ppermute(jnp.where(index == 0, last, first), axis, [(0, 1), (1, 0)])
-        return other, other
     up = [(i, i + 1) for i in range(size - 1)]
     return lax.ppermute(last, axis, up), lax.ppermute(first, axis, [(j, i) for i, j in up])
 
@@ -383,42 +405,41 @@
     )(tile.reshape(1), chan.reshape(1), keep, near, far, tiles, weights, mine, answers)
 
 
-def write_kernel(other, core, *refs):
-    *pieces, out, first, second, sems = refs
-    half, rows = out.shape[0] // 2, first.shape[0]
-    copies = []
-    for index, (piece, held) in enumerate(zip(pieces[-2:], (first, second))):
-        held[...] = piece[...].astype(jnp.float32)
-        place = (core[0] ^ other) * half + index * rows
-        here = out.at[pl.ds(pl.multiple_of(place, rows), rows)]
-        copies.append(pltpu.make_async_copy(held, here, sems.at[index]))
-        copies[-1].start()
-    for copy in copies:
-        copy.wait()
-
-
-def written(other, core, pieces, before=()):
-    rows, width = pieces[0].shape
-    spec = pl.BlockSpec(memory_space=pltpu.VMEM)
+def write_kernel(other, index, core, *refs):
+    piece, out, held, sem = refs[-4:]
+    rows = held.shape[0]
+    held[...] = piece[...].astype(jnp.float32)
+    first = ((core[0] ^ other) * 2 + index) * rows
+    copy = pltpu.make_async_copy(held, out.at[pl.ds(pl.multiple_of(first, rows), rows)], sem)
+    copy.start()
+    copy.wait()
+
+
+def written(other, index, core, piece, before=()):
+    rows, width = piece.shape
     hbm = pl.BlockSpec(memory_space=pltpu.HBM)
     return pl.pallas_call(
-        functools.partial(write_kernel, other),
+        functools.partial(write_kernel, other, index),
         out_shape=jax.ShapeDtypeStruct((4 * rows, width), jnp.float32),
-        in_specs=[pl.BlockSpec(memory_space=pltpu.SMEM)] + [hbm] * len(before) + [spec] * 2,
+        in_specs=[
+            pl.BlockSpec(memory_space=pltpu.SMEM),
+            *[hbm] * len(before),
+            pl.BlockSpec(memory_space=pltpu.VMEM),
+        ],
         out_specs=hbm,
         input_output_aliases={1: 0} if before else {},
-        scratch_shapes=[
-            pltpu.VMEM((rows, width), jnp.float32),
-            pltpu.VMEM((rows, width), jnp.float32),
-            pltpu.SemaphoreType.DMA((2,)),
-        ],
+        scratch_shapes=[pltpu.VMEM((rows, width), jnp.float32), pltpu.SemaphoreType.DMA],
         compiler_params=memory(16),
         name="written",
-    )(core.reshape(1), *before, *pieces)
+    )(core.reshape(1), *before, piece)
 
 
 def collect(core, own, received):
-    return written(1, core, received, (written(0, core, own),))
+    result = ()
+    for index in range(2):
+        for other, pieces in enumerate((own, received)):
+            result = (written(other, index, core, pieces[index], result),)
+    return result[0]
 
 
 def add_kernel(first, second, out):

time: 66.2 us -> 67.1 us (1.014)
  Pallas kernels: 22.4 us -> 24.6 us
  other arithmetic: 0.98 us -> 0.1 us
    pallas_call x2 -> x5, Pallas kernels: 1.7 us -> 3.83 us  [the longest x4 2.98 us: written(): pl.pallas_call(functools.partial(write_kernel, other, index), out_shape=j...]
    select_n x1 -> x0, other arithmetic: 0.88 us -> none  [edges(): jnp.where(index == 0, last, first)]
    ppermute x12 -> x13, waiting for transfers between devices: 16.1 us -> 15.7 us  [swap(): return lax.ppermute(value, axis, [(i, i ^ bit) for i in range(size)])]
    ppermute x12 -> x13, starting transfers between devices: 14.2 us -> 14.3 us  [swap(): return lax.ppermute(value, axis, [(i, i ^ bit) for i in range(size)])]
  transfers between devices with their start and end apart: 17 -> 17, of which waited for: 9 -> 8; matrix products, arithmetic and copies ran while one was open for 1% -> 0% of each run, Pallas kernels for 31% -> 34%
where the time goes in v23:
time: 67.1 us; the launch traced here: 66.8 us
  Pallas kernels  24.6 us (37%)
  waiting for transfers between devices  22.2 us (33%)
  starting transfers between devices  19.6 us (29%)
    ppermute x13, waiting for transfers between devices, swap(): return lax.ppermute(value, axis, [(i, i ^ bit) for i in range(size)])  15.7 us
    ppermute x13, starting transfers between devices, swap(): return lax.ppermute(value, axis, [(i, i ^ bit) for i in range(size)])  14.3 us
    pallas_call x2, Pallas kernels, pixel_rows(): pl.pallas_call(functools.partial(pixel_kernel, count, bits, stride), out_...  13.7 us
    ppermute x4, waiting for transfers between devices, sum_over_panels(): parts = [added(part, lax.ppermute(part, both, perm)) for part in parts]  6.55 us
    ppermute x4, starting transfers between devices, sum_over_panels(): parts = [added(part, lax.ppermute(part, both, perm)) for part in parts]  5.34 us
    pallas_call x4, Pallas kernels, written(): pl.pallas_call(functools.partial(write_kernel, other, index), out_shape=j...  2.98 us
    pallas_call x1, Pallas kernels, project(): pl.pallas_call(functools.partial(project_kernel, bits), out_shape=(jax.Sh...  2.74 us
    pallas_call x1, Pallas kernels, early_product(): pl.pallas_call(early_kernel, out_shape=(jax.ShapeDtypeStruct((depth, widt...  2.49 us
  transfers between devices with their start and end apart: 17, of which 8 were waited for; matrix products, arithmetic and copies ran while one was open for 0% of the time, Pallas kernels for 34%

profile of v23, /device:TPU:0, one launch (start us, length us, event | category | flops | bytes accessed | tf_op | source)
XLA Modules:
  0.0 66.8 jit_solution(8274566099818013166)
XLA Ops:
  0.0 3.0 %collective-permute-start = (s32[2048]{0:T(1024)}, s32[2048]{0:T(1024)S(1)}, u32[]{:S(2)}, u32[]{:S(2)}) collective-permute-start(s32[2048]{0:T(1024)} %wanted.1), channel_id=1, source_target_pairs={{0,4},{4,0},{1,5},{5,1},{2,6},{6,2},{3,7},{7,3},{8,12},{12,8},{9,1... | collective-permute-start | bytes 24584 | tf_op jit(solution)/shard_map/ppermute | solution.py:67
  3.0 0.8 %edge.1 = bf16[128,256]{1,0:T(8,128)(2,1)S(1)} custom-call(s32[1]{0:T(128)} %bitcast.2.tile.tile_at, bf16[4096,256]{1,0:T(8,128)(2,1)} %cotangent.3), custom_call_target="tpu_custom_call" | custom-call | tf_op jit(solution)/shard_map/edge/pallas_call | solution.py:25
  3.9 2.7 %project.1 = bf16[512,256]{1,0:T(8,128)(2,1)} custom-call(s32[1]{0:T(128)} %bitcast.1.where.chan.chan_at, bf16[2048,1152]{1,0:T(8,128)(2,1)} %spectra.7, bf16[1152,256]{1,0:T(8,128)(2,1)} %weight.5), custom_call_target="tpu_custom_call" | custom-call | flops 301989888 | bytes 2031616 | tf_op jit(solution)/shard_map/project/pallas_call | solution.py:110
  6.7 2.1 %collective-permute-start.2 = (bf16[512,256]{1,0:T(8,128)(2,1)}, bf16[512,256]{1,0:T(8,128)(2,1)S(1)}, u32[]{:S(2)}, u32[]{:S(2)}) collective-permute-start(bf16[512,256]{1,0:T(8,128)(2,1)} %project.1), channel_id=1, source_target_pairs={{0,1},{1,0},{2,3},{3,2},{4,5},{5,4},{6,7},{7,6},{8,9},{9,8},{10,11... | collective-permute-start | bytes 786440 | tf_op jit(solution)/shard_map/ppermute | solution.py:67
  8.9 7.4 %pixel_rows.2 = (bf16[512,256]{1,0:T(8,128)(2,1)S(1)}, bf16[512,256]{1,0:T(8,128)(2,1)S(1)}, bf16[512,256]{1,0:T(8,128)(2,1)S(1)}) custom-call(s32[1]{0:T(128)} %bitcast.1.where.chan.chan_at, s32[16384]{0:T(1024)S(1)} %bitcast.9, s32[2048]{0:T(1024)S(1)} %collective-permute-done.wanted, bf16[4096,256]{1,0:T(8,128)(2,1)} %cotangent.3, ...), custom_call_target="tpu_custom_call" | custom-call | flops 17179869184 | bytes 4194304 | tf_op jit(solution)/shard_map/pixel_rows/pallas_call | solution.py:326
  16.4 0.9 %collective-permute-start.3 = (bf16[512,256]{1,0:T(8,128)(2,1)S(1)}, bf16[512,256]{1,0:T(8,128)(2,1)S(1)}, u32[]{:S(2)}, u32[]{:S(2)}) collective-permute-start(bf16[512,256]{1,0:T(8,128)(2,1)S(1)} %get-tuple-element.30), channel_id=1, source_target_pairs={{0,1},{1,0},{2,3},{3,2},{4,5},{5,4},{6,7},{7,6},{8,9},{9,8},{10,11... | collective-permute-start | bytes 786440 | tf_op jit(solution)/shard_map/ppermute | solution.py:67
  17.3 3.2 %collective-permute-start.4 = (bf16[512,256]{1,0:T(8,128)(2,1)S(1)}, bf16[512,256]{1,0:T(8,128)(2,1)S(1)}, u32[]{:S(2)}, u32[]{:S(2)}) collective-permute-start(bf16[512,256]{1,0:T(8,128)(2,1)S(1)} %add_convert_fusion), channel_id=1, source_target_pairs={{0,3},{1,2},{2,1},{3,0},{4,7},{5,6},{6,5},{7,4},{8,11},{9,10},{10,... | collective-permute-start | bytes 786440 | tf_op jit(solution)/shard_map/ppermute | solution.py:67
  20.5 1.5 %collective-permute-start.5 = (bf16[512,256]{1,0:T(8,128)(2,1)S(1)}, bf16[512,256]{1,0:T(8,128)(2,1)S(1)}, u32[]{:S(2)}, u32[]{:S(2)}) collective-permute-start(bf16[512,256]{1,0:T(8,128)(2,1)S(1)} %get-tuple-element.33), channel_id=1, source_target_pairs={{0,4},{4,0},{1,5},{5,1},{2,6},{6,2},{3,7},{7,3},{8,12},{12,8},{9,1... | collective-permute-start | bytes 786440 | tf_op jit(solution)/shard_map/ppermute | solution.py:67
  22.0 6.3 %pixel_rows.3 = (bf16[512,256]{1,0:T(8,128)(2,1)S(1)}, bf16[512,256]{1,0:T(8,128)(2,1)S(1)}) custom-call(s32[1]{0:T(128)} %bitcast.3.where, s32[16384]{0:T(1024)S(1)} %bitcast.10, s32[2048]{0:T(1024)S(1)} %copy-done.3, bf16[4096,256]{1,0:T(8,128)(2,1)} %cotangent.3, bf16[128,256]{1,0:T(8,128)(2,1)S(1)} %collective-permute-done.1.above.below, ...), custom_call_target="tpu_custom_call" | custom-call | flops 17179869184 | bytes 4194304 | tf_op jit(solution)/shard_map/pixel_rows/pallas_call | solution.py:326
  28.4 3.1 %collective-permute-done.4.far = bf16[512,256]{1,0:T(8,128)(2,1)S(1)} collective-permute-done((bf16[512,256]{1,0:T(8,128)(2,1)S(1)}, bf16[512,256]{1,0:T(8,128)(2,1)S(1)}, u32[]{:S(2)}, u32[]{:S(2)}) %collective-permute-start.4) | collective-permute-done | bytes 262176 | tf_op jit(solution)/shard_map/ppermute | solution.py:67
  31.4 0.5 pre_gradient.1.first
  31.9 0.4 collective-permute-start.6
  32.4 2.3 %collective-permute-start.7 = (bf16[512,256]{1,0:T(8,128)(2,1)S(1)}, bf16[512,256]{1,0:T(8,128)(2,1)S(1)}, u32[]{:S(2)}, u32[]{:S(2)}) collective-permute-start(bf16[512,256]{1,0:T(8,128)(2,1)S(1)} %pre_gradient.1.first), channel_id=1, source_target_pairs={{0,1},{1,0},{2,3},{3,2},{4,5},{5,4},{6,7},{7,6},{8,9},{9,8},{10,11... | collective-permute-start | bytes 786440 | tf_op jit(solution)/shard_map/ppermute | solution.py:67
  34.6 8.4 %collective-permute-done.6.second = bf16[512,256]{1,0:T(8,128)(2,1)S(1)} collective-permute-done((bf16[512,256]{1,0:T(8,128)(2,1)S(1)}, bf16[512,256]{1,0:T(8,128)(2,1)S(1)}, u32[]{:S(2)}, u32[]{:S(2)}) %collective-permute-start.6) | collective-permute-done | bytes 262176 | tf_op jit(solution)/shard_map/ppermute | solution.py:67
  43.0 0.1 collective-permute-start.8
  43.2 2.5 %early_product.1 = (f32[1152,256]{1,0:T(8,128)S(1)}, bf16[512,1152]{1,0:T(8,128)(2,1)S(1)}, bf16[512,1152]{1,0:T(8,128)(2,1)S(1)}) custom-call(s32[1]{0:T(128)} %bitcast.1.where.chan.chan_at, bf16[2048,1152]{1,0:T(8,128)(2,1)} %spectra.7, bf16[512,256]{1,0:T(8,128)(2,1)S(1)} %pre_gradient.1.first, bf16[512,256]{1,0:T(8,128)(2,1)S(1)} %collective-permute-done.6.second), custom_call_target="tpu_custom_call" | custom-call | flops 603979776 | bytes 5898240 | tf_op jit(solution)/shard_map/early_product/pallas_call | solution.py:157
  45.8 0.5 more_product.1.before
  46.3 3.2 %collective-permute-done.8.rows = bf16[512,256]{1,0:T(8,128)(2,1)S(1)} collective-permute-done((bf16[512,256]{1,0:T(8,128)(2,1)S(1)}, bf16[512,256]{1,0:T(8,128)(2,1)S(1)}, u32[]{:S(2)}, u32[]{:S(2)}) %collective-permute-start.8) | collective-permute-done | bytes 262176 | tf_op jit(solution)/shard_map/ppermute | solution.py:67
  49.5 0.6 late_product.1
  50.2 0.5 collective-permute-start.13
  50.7 0.9 %collective-permute-done.9.second = bf16[288,256]{1,0:T(8,128)(2,1)S(1)} collective-permute-done((bf16[288,256]{1,0:T(8,128)(2,1)S(1)}, bf16[288,256]{1,0:T(8,128)(2,1)S(1)}, u32[]{:S(2)}, u32[]{:S(2)}) %collective-permute-start.9) | collective-permute-done | bytes 147488 | tf_op jit(solution)/shard_map/ppermute | solution.py:67
  51.6 1.6 %collective-permute-start.10 = (bf16[288,256]{1,0:T(8,128)(2,1)S(1)}, bf16[288,256]{1,0:T(8,128)(2,1)S(1)}, u32[]{:S(2)}, u32[]{:S(2)}) collective-permute-start(bf16[288,256]{1,0:T(8,128)(2,1)S(1)} %added.6.first), channel_id=1, source_target_pairs={{0,16},{4,20},{8,12},{12,8},{16,0},{20,4},{24,28},{28,24},{1,17},{... | collective-permute-start | bytes 442376 | tf_op jit(solution)/shard_map/ppermute | solution.py:466
  53.1 0.6 collective-permute-start.14
  53.7 3.0 %collective-permute-done.10.second = bf16[288,256]{1,0:T(8,128)(2,1)S(1)} collective-permute-done((bf16[288,256]{1,0:T(8,128)(2,1)S(1)}, bf16[288,256]{1,0:T(8,128)(2,1)S(1)}, u32[]{:S(2)}, u32[]{:S(2)}) %collective-permute-start.10) | collective-permute-done | bytes 147488 | tf_op jit(solution)/shard_map/ppermute | solution.py:466
  56.8 1.6 %collective-permute-start.11 = (bf16[288,256]{1,0:T(8,128)(2,1)S(1)}, bf16[288,256]{1,0:T(8,128)(2,1)S(1)}, u32[]{:S(2)}, u32[]{:S(2)}) collective-permute-start(bf16[288,256]{1,0:T(8,128)(2,1)S(1)} %added.7.first), channel_id=1, source_target_pairs={{0,4},{4,0},{8,24},{12,28},{16,20},{20,16},{24,8},{28,12},{1,5},{5... | collective-permute-start | bytes 442376 | tf_op jit(solution)/shard_map/ppermute | solution.py:466
  58.5 1.6 %collective-permute-start.15 = (bf16[288,256]{1,0:T(8,128)(2,1)S(1)}, bf16[288,256]{1,0:T(8,128)(2,1)S(1)}, u32[]{:S(2)}, u32[]{:S(2)}) collective-permute-start(bf16[288,256]{1,0:T(8,128)(2,1)S(1)} %added.10.first), channel_id=1, source_target_pairs={{0,4},{4,0},{8,24},{12,28},{16,20},{20,16},{24,8},{28,12},{1,5},{5... | collective-permute-start | bytes 442376 | tf_op jit(solution)/shard_map/ppermute | solution.py:466
  60.0 2.0 %collective-permute-done.11.second = bf16[288,256]{1,0:T(8,128)(2,1)S(1)} collective-permute-done((bf16[288,256]{1,0:T(8,128)(2,1)S(1)}, bf16[288,256]{1,0:T(8,128)(2,1)S(1)}, u32[]{:S(2)}, u32[]{:S(2)}) %collective-permute-start.11) | collective-permute-done | bytes 147488 | tf_op jit(solution)/shard_map/ppermute | solution.py:466
  62.1 1.5 %collective-permute-done.15.second = bf16[288,256]{1,0:T(8,128)(2,1)S(1)} collective-permute-done((bf16[288,256]{1,0:T(8,128)(2,1)S(1)}, bf16[288,256]{1,0:T(8,128)(2,1)S(1)}, u32[]{:S(2)}, u32[]{:S(2)}) %collective-permute-start.15) | collective-permute-done | bytes 147488 | tf_op jit(solution)/shard_map/ppermute | solution.py:466
  63.8 0.7 %written.4.refs_0_ = f32[1152,256]{1,0:T(8,128)} custom-call(s32[1]{0:T(128)} %bitcast.core, bf16[288,256]{1,0:T(8,128)(2,1)S(1)} %added.8.refs_0_), custom_call_target="tpu_custom_call" | custom-call | tf_op jit(solution)/shard_map/written/pallas_call | solution.py:421
  64.6 0.7 %written.5.refs_0_ = f32[1152,256]{1,0:T(8,128)} custom-call(s32[1]{0:T(128)} %bitcast.core, f32[1152,256]{1,0:T(8,128)} %written.4.refs_0_, bf16[288,256]{1,0:T(8,128)(2,1)S(1)} %collective-permute-done.12.refs_1_), custom_call_target="tpu_custom_call", output_to_operand_aliasing={{}: (1, {})} | custom-call | tf_op jit(solution)/shard_map/written/pallas_call | solution.py:421
  65.3 0.7 %written.6.refs_0_ = f32[1152,256]{1,0:T(8,128)} custom-call(s32[1]{0:T(128)} %bitcast.core, f32[1152,256]{1,0:T(8,128)} %written.5.refs_0_, bf16[288,256]{1,0:T(8,128)(2,1)S(1)} %added.11.refs_1_), custom_call_target="tpu_custom_call", output_to_operand_aliasing={{}: (1, {})} | custom-call | tf_op jit(solution)/shard_map/written/pallas_call | solution.py:421
  66.1 0.7 %written.7 = f32[1152,256]{1,0:T(8,128)} custom-call(s32[1]{0:T(128)} %bitcast.core, f32[1152,256]{1,0:T(8,128)} %written.6.refs_0_, bf16[288,256]{1,0:T(8,128)(2,1)S(1)} %collective-permute-done.16.refs_1_), custom_call_target="tpu_custom_call", output_to_operand_aliasing={{}: (1, {})} | custom-call | tf_op jit(solution)/shard_map/written/pallas_call | solution.py:421
  (36 shorter events, 0.8 us)
Async XLA Ops:
  0.0 8.9 %collective-permute-start = (s32[2048]{0:T(1024)}, s32[2048]{0:T(1024)S(1)}, u32[]{:S(2)}, u32[]{:S(2)}) collective-permute-start(s32[2048]{0:T(1024)} %wanted.1), channel_id=1, source_target_pairs={{0,4},{4,0},{1,5},{5,1},{2,6},{6,2},{3,7},{7,3},{8,12},{12,8},{9,1... | collective-permute-start | bytes 24584 | tf_op jit(solution)/shard_map/ppermute | solution.py:67
  3.8 5.0 %collective-permute-start.1 = (bf16[128,256]{1,0:T(8,128)(2,1)S(1)}, bf16[128,256]{1,0:T(8,128)(2,1)S(1)}, u32[]{:S(2)}, u32[]{:S(2)}) collective-permute-start(bf16[128,256]{1,0:T(8,128)(2,1)S(1)} %edge.1), channel_id=1, source_target_pairs={{0,4},{4,0},{1,5},{5,1},{2,6},{6,2},{3,7},{7,3},{8,12},{12,8},{9,1... | collective-permute-start | bytes 196616 | tf_op jit(solution)/shard_map/ppermute | solution.py:67
  3.9 4.9 %copy-start.5 = (s32[8,4096]{1,0:T(8,128)S(1)}, s32[8,4096]{1,0:T(8,128)}, u32[]{:S(2)}) copy-start(s32[8,4096]{1,0:T(8,128)} %param.14) | copy-start | bytes 393220
  3.9 5.0 %copy-start = (bf16[1152,256]{1,0:T(8,128)(2,1)S(1)}, bf16[1152,256]{1,0:T(8,128)(2,1)}, u32[]{:S(2)}) copy-start(bf16[1152,256]{1,0:T(8,128)(2,1)} %weight.5) | copy-start | bytes 1769476
  3.9 5.0 %copy-start.4 = (f32[8,256]{1,0:T(8,128)S(1)}, f32[8,256]{1,0:T(8,128)}, u32[]{:S(2)}) copy-start(f32[8,256]{1,0:T(8,128)} %mixing.3) | copy-start | bytes 24580
  6.7 9.6 %collective-permute-start.2 = (bf16[512,256]{1,0:T(8,128)(2,1)}, bf16[512,256]{1,0:T(8,128)(2,1)S(1)}, u32[]{:S(2)}, u32[]{:S(2)}) collective-permute-start(bf16[512,256]{1,0:T(8,128)(2,1)} %project.1), channel_id=1, source_target_pairs={{0,1},{1,0},{2,3},{3,2},{4,5},{5,4},{6,7},{7,6},{8,9},{9,8},{10,11... | collective-permute-start | bytes 786440 | tf_op jit(solution)/shard_map/ppermute | solution.py:67
  8.9 13.1 %copy-start.3 = (s32[2048]{0:T(1024)S(1)}, s32[2048]{0:T(1024)}, u32[]{:S(2)}) copy-start(s32[2048]{0:T(1024)} %wanted.1) | copy-start | bytes 24580
  16.4 11.9 %collective-permute-start.3 = (bf16[512,256]{1,0:T(8,128)(2,1)S(1)}, bf16[512,256]{1,0:T(8,128)(2,1)S(1)}, u32[]{:S(2)}, u32[]{:S(2)}) collective-permute-start(bf16[512,256]{1,0:T(8,128)(2,1)S(1)} %get-tuple-element.30), channel_id=1, source_target_pairs={{0,1},{1,0},{2,3},{3,2},{4,5},{5,4},{6,7},{7,6},{8,9},{9,8},{10,11... | collective-permute-start | bytes 786440 | tf_op jit(solution)/shard_map/ppermute | solution.py:67
  17.3 14.1 %collective-permute-start.4 = (bf16[512,256]{1,0:T(8,128)(2,1)S(1)}, bf16[512,256]{1,0:T(8,128)(2,1)S(1)}, u32[]{:S(2)}, u32[]{:S(2)}) collective-permute-start(bf16[512,256]{1,0:T(8,128)(2,1)S(1)} %add_convert_fusion), channel_id=1, source_target_pairs={{0,3},{1,2},{2,1},{3,0},{4,7},{5,6},{6,5},{7,4},{8,11},{9,10},{10,... | collective-permute-start | bytes 786440 | tf_op jit(solution)/shard_map/ppermute | solution.py:67
  20.5 10.9 %collective-permute-start.5 = (bf16[512,256]{1,0:T(8,128)(2,1)S(1)}, bf16[512,256]{1,0:T(8,128)(2,1)S(1)}, u32[]{:S(2)}, u32[]{:S(2)}) collective-permute-start(bf16[512,256]{1,0:T(8,128)(2,1)S(1)} %get-tuple-element.33), channel_id=1, source_target_pairs={{0,4},{4,0},{1,5},{5,1},{2,6},{6,2},{3,7},{7,3},{8,12},{12,8},{9,1... | collective-permute-start | bytes 786440 | tf_op jit(solution)/shard_map/ppermute | solution.py:67
  22.0 9.4 %copy-start.1 = (s32[2048,1]{0,1:T(1,128)S(1)}, s32[2048,1]{0,1:T(1,128)}, u32[]{:S(2)}) copy-start(s32[2048,1]{0,1:T(1,128)} %param.10) | copy-start | bytes 24580
  22.0 9.4 %copy-start.2 = (f32[2048]{0:T(1024)S(1)}, f32[2048]{0:T(1024)}, u32[]{:S(2)}) copy-start(f32[2048]{0:T(1024)} %param.12) | copy-start | bytes 24580
  31.9 11.1 %collective-permute-start.6 = (bf16[512,256]{1,0:T(8,128)(2,1)S(1)}, bf16[512,256]{1,0:T(8,128)(2,1)S(1)}, u32[]{:S(2)}, u32[]{:S(2)}) collective-permute-start(bf16[512,256]{1,0:T(8,128)(2,1)S(1)} %pre_gradient.1.first), channel_id=1, source_target_pairs={{0,3},{1,2},{2,1},{3,0},{4,7},{5,6},{6,5},{7,4},{8,11},{9,10},{10,... | collective-permute-start | bytes 786440 | tf_op jit(solution)/shard_map/ppermute | solution.py:67
  32.4 13.4 %collective-permute-start.7 = (bf16[512,256]{1,0:T(8,128)(2,1)S(1)}, bf16[512,256]{1,0:T(8,128)(2,1)S(1)}, u32[]{:S(2)}, u32[]{:S(2)}) collective-permute-start(bf16[512,256]{1,0:T(8,128)(2,1)S(1)} %pre_gradient.1.first), channel_id=1, source_target_pairs={{0,1},{1,0},{2,3},{3,2},{4,5},{5,4},{6,7},{7,6},{8,9},{9,8},{10,11... | collective-permute-start | bytes 786440 | tf_op jit(solution)/shard_map/ppermute | solution.py:67
  43.0 6.4 %collective-permute-start.8 = (bf16[512,256]{1,0:T(8,128)(2,1)S(1)}, bf16[512,256]{1,0:T(8,128)(2,1)S(1)}, u32[]{:S(2)}, u32[]{:S(2)}) collective-permute-start(bf16[512,256]{1,0:T(8,128)(2,1)S(1)} %collective-permute-done.6.second), channel_id=1, source_target_pairs={{0,1},{1,0},{2,3},{3,2},{4,5},{5,4},{6,7},{7,6},{8,9},{9,8},{10,11... | collective-permute-start | bytes 786440 | tf_op jit(solution)/shard_map/ppermute | solution.py:67
  50.1 1.4 %collective-permute-start.9 = (bf16[288,256]{1,0:T(8,128)(2,1)S(1)}, bf16[288,256]{1,0:T(8,128)(2,1)S(1)}, u32[]{:S(2)}, u32[]{:S(2)}) collective-permute-start(bf16[288,256]{1,0:T(8,128)(2,1)S(1)} %get-tuple-element.38), channel_id=1, source_target_pairs={{0,8},{8,0},{16,24},{24,16},{1,9},{9,1},{17,25},{25,17},{2,10},{10... | collective-permute-start | bytes 442376 | tf_op jit(solution)/shard_map/ppermute | solution.py:67
  50.2 2.9 %collective-permute-start.13 = (bf16[288,256]{1,0:T(8,128)(2,1)S(1)}, bf16[288,256]{1,0:T(8,128)(2,1)S(1)}, u32[]{:S(2)}, u32[]{:S(2)}) collective-permute-start(bf16[288,256]{1,0:T(8,128)(2,1)S(1)} %get-tuple-element.40), channel_id=1, source_target_pairs={{0,8},{8,0},{16,24},{24,16},{1,9},{9,1},{17,25},{25,17},{2,10},{10... | collective-permute-start | bytes 442376 | tf_op jit(solution)/shard_map/ppermute | solution.py:67
  51.6 5.2 %collective-permute-start.10 = (bf16[288,256]{1,0:T(8,128)(2,1)S(1)}, bf16[288,256]{1,0:T(8,128)(2,1)S(1)}, u32[]{:S(2)}, u32[]{:S(2)}) collective-permute-start(bf16[288,256]{1,0:T(8,128)(2,1)S(1)} %added.6.first), channel_id=1, source_target_pairs={{0,16},{4,20},{8,12},{12,8},{16,0},{20,4},{24,28},{28,24},{1,17},{... | collective-permute-start | bytes 442376 | tf_op jit(solution)/shard_map/ppermute | solution.py:466
  53.1 5.3 %collective-permute-start.14 = (bf16[288,256]{1,0:T(8,128)(2,1)S(1)}, bf16[288,256]{1,0:T(8,128)(2,1)S(1)}, u32[]{:S(2)}, u32[]{:S(2)}) collective-permute-start(bf16[288,256]{1,0:T(8,128)(2,1)S(1)} %added.9.first), channel_id=1, source_target_pairs={{0,16},{4,20},{8,12},{12,8},{16,0},{20,4},{24,28},{28,24},{1,17},{... | collective-permute-start | bytes 442376 | tf_op jit(solution)/shard_map/ppermute | solution.py:466
  56.8 5.2 %collective-permute-start.11 = (bf16[288,256]{1,0:T(8,128)(2,1)S(1)}, bf16[288,256]{1,0:T(8,128)(2,1)S(1)}, u32[]{:S(2)}, u32[]{:S(2)}) collective-permute-start(bf16[288,256]{1,0:T(8,128)(2,1)S(1)} %added.7.first), channel_id=1, source_target_pairs={{0,4},{4,0},{8,24},{12,28},{16,20},{20,16},{24,8},{28,12},{1,5},{5... | collective-permute-start | bytes 442376 | tf_op jit(solution)/shard_map/ppermute | solution.py:466
  58.5 5.2 %collective-permute-start.15 = (bf16[288,256]{1,0:T(8,128)(2,1)S(1)}, bf16[288,256]{1,0:T(8,128)(2,1)S(1)}, u32[]{:S(2)}, u32[]{:S(2)}) collective-permute-start(bf16[288,256]{1,0:T(8,128)(2,1)S(1)} %added.10.first), channel_id=1, source_target_pairs={{0,4},{4,0},{8,24},{12,28},{16,20},{20,16},{24,8},{28,12},{1,5},{5... | collective-permute-start | bytes 442376 | tf_op jit(solution)/shard_map/ppermute | solution.py:466
  62.0 2.5 %collective-permute-start.12 = (bf16[288,256]{1,0:T(8,128)(2,1)S(1)}, bf16[288,256]{1,0:T(8,128)(2,1)S(1)}, u32[]{:S(2)}, u32[]{:S(2)}) collective-permute-start(bf16[288,256]{1,0:T(8,128)(2,1)S(1)} %added.8.refs_0_), channel_id=1, source_target_pairs={{0,8},{8,0},{16,24},{24,16},{1,9},{9,1},{17,25},{25,17},{2,10},{10... | collective-permute-start | bytes 442376 | tf_op jit(solution)/shard_map/ppermute | solution.py:67
  63.7 2.4 %collective-permute-start.16 = (bf16[288,256]{1,0:T(8,128)(2,1)S(1)}, bf16[288,256]{1,0:T(8,128)(2,1)S(1)}, u32[]{:S(2)}, u32[]{:S(2)}) collective-permute-start(bf16[288,256]{1,0:T(8,128)(2,1)S(1)} %added.11.refs_1_), channel_id=1, source_target_pairs={{0,8},{8,0},{16,24},{24,16},{1,9},{9,1},{17,25},{25,17},{2,10},{10... | collective-permute-start | bytes 442376 | tf_op jit(solution)/shard_map/ppermute | solution.py:67

commit v24 on v22

--- a/solution.py
+++ b/solution.py
@@ -213,12 +213,12 @@
     return outs[:2], outs[2:]
 
 
-def pixel_kernel(count, bits, stride, where, places, wanted, cotangent, above, below, mixing, weight,
+def pixel_kernel(count, bits, stride, skip, where, places, wanted, cotangent, above, below, mixing, weight,
                  spectra, out, *refs):
     quarters, refs = refs[: len(bits)], refs[len(bits) :]
     table, scale, sums, near, names, held, tile, sems = refs
     chan = where[0]
-    start = chan * stride
+    start = chan * stride + skip
     tile_rows, half = tile.shape[0], table.shape[1]
     listed = names.shape[0]
     first_name = pl.multiple_of(start // listed * listed, listed)
@@ -293,7 +293,7 @@
 
 
 def pixel_rows(
-    cotangent, above, below, places, mixing, wanted, stride, count, spectra, weight, chan, bits
+    cotangent, above, below, places, mixing, wanted, stride, count, spectra, weight, chan, bits, skip=0
 ):
     tile_rows, width = cotangent.shape
     depth, rows = spectra.shape[1], spectra.shape[0] // 4
@@ -302,7 +302,7 @@
     hbm = pl.BlockSpec(memory_space=pltpu.HBM)
     vmem = pl.BlockSpec(memory_space=pltpu.VMEM)
     return pl.pallas_call(
-        functools.partial(pixel_kernel, count, bits, stride),
+        functools.partial(pixel_kernel, count, bits, stride, skip),
         out_shape=(
             jax.ShapeDtypeStruct((count, width), jnp.bfloat16),
             *[jax.ShapeDtypeStruct((rows, width), jnp.bfloat16)] * len(bits),
@@ -470,12 +470,16 @@
         local_ids = lax.dynamic_slice_in_dim(pix_local, first_row, quarter, 0)
         slot_index, wanted = requests(tile_ids, local_ids, capacity)
         stride, count = 0, wanted.shape[0]
-    rows, shared, send = pixel_rows(*pixels, wanted, stride, count, *rest, chan, (3, 1))
+    part = count // 2
+    rows, shared, send = pixel_rows(*pixels, wanted, stride, part, *rest, chan, (3, 1))
     near_first, rows = lax.optimization_barrier((near_first, rows))
     passed_on = (shared.astype(jnp.float32) + near_first.astype(jnp.float32)).astype(jnp.bfloat16)
     passed_on, send, rows, later = lax.optimization_barrier((passed_on, send, rows, chan))
     far = swap(passed_on, "chan", 3)
     near = swap(send, "chan", 1)
+    (more,) = pixel_rows(*pixels, wanted, stride, count - part, *rest, later, (), part)
+    rows = jnp.concatenate([rows, more])
+    rows, later = lax.optimization_barrier((rows, later))
     if paired:
         answers = swap(rows, "pix", 1)
         mine, keep = pixel_rows(*pixels, pix_local, stride, count, *rest, later, (0,))

time: 66.2 us -> 69 us (1.042)
  starting transfers between devices: 19.6 us -> 23.8 us
  waiting for transfers between devices: 22.7 us -> 19.5 us
  Pallas kernels: 22.4 us -> 24.2 us
    ppermute x12, starting transfers between devices: 14.2 us -> 20.3 us  [swap(): return lax.ppermute(value, axis, [(i, i ^ bit) for i in range(size)])]
    ppermute x12, waiting for transfers between devices: 16.1 us -> 11.1 us  [swap(): return lax.ppermute(value, axis, [(i, i ^ bit) for i in range(size)])]
    ppermute x4, starting transfers between devices: 5.33 us -> 3.34 us  [sum_over_panels(): parts = [added(part, lax.ppermute(part, both, perm)) for part in parts]]
    ppermute x4, waiting for transfers between devices: 6.57 us -> 8.47 us  [sum_over_panels(): parts = [added(part, lax.ppermute(part, both, perm)) for part in parts]]
    pallas_call x2 -> x3, Pallas kernels: 13.7 us -> 15.4 us  [pixel_rows(): pl.pallas_call(functools.partial(pixel_kernel, count, bits, stride, skip)...]
  transfers between devices with their start and end apart: 17 -> 17, of which waited for: 9 -> 10; matrix products, arithmetic and copies ran while one was open for 1% -> 1% of each run, Pallas kernels for 31% -> 27%
where the time goes in v24:
time: 69 us; the launch traced here: 68.7 us
  Pallas kernels  24.2 us (35%)
  starting transfers between devices  23.8 us (34%)
  waiting for transfers between devices  19.5 us (28%)
  other arithmetic  1 us (1%)
    ppermute x12, starting transfers between devices, swap(): return lax.ppermute(value, axis, [(i, i ^ bit) for i in range(size)])  20.3 us
    pallas_call x3, Pallas kernels, pixel_rows(): pl.pallas_call(functools.partial(pixel_kernel, count, bits, stride, skip)...  15.4 us
    ppermute x12, waiting for transfers between devices, swap(): return lax.ppermute(value, axis, [(i, i ^ bit) for i in range(size)])  11.1 us
    ppermute x4, waiting for transfers between devices, sum_over_panels(): parts = [added(part, lax.ppermute(part, both, perm)) for part in parts]  8.47 us
    ppermute x4, starting transfers between devices, sum_over_panels(): parts = [added(part, lax.ppermute(part, both, perm)) for part in parts]  3.34 us
    pallas_call x1, Pallas kernels, project(): pl.pallas_call(functools.partial(project_kernel, bits), out_shape=(jax.Sh...  2.74 us
    pallas_call x1, Pallas kernels, early_product(): pl.pallas_call(early_kernel, out_shape=(jax.ShapeDtypeStruct((depth, widt...  2.49 us
    pallas_call x2, Pallas kernels, written(): pl.pallas_call(functools.partial(write_kernel, other), out_shape=jax.Shap...  1.7 us
  transfers between devices with their start and end apart: 17, of which 10 were waited for; matrix products, arithmetic and copies ran while one was open for 1% of the time, Pallas kernels for 27%

profile of v24, /device:TPU:0, one launch (start us, length us, event | category | flops | bytes accessed | tf_op | source)
XLA Modules:
  0.0 68.7 jit_solution(7283408939086462428)
XLA Ops:
  0.0 3.0 %collective-permute-start = (s32[2048]{0:T(1024)}, s32[2048]{0:T(1024)S(1)}, u32[]{:S(2)}, u32[]{:S(2)}) collective-permute-start(s32[2048]{0:T(1024)} %wanted.1), channel_id=1, source_target_pairs={{0,4},{4,0},{1,5},{5,1},{2,6},{6,2},{3,7},{7,3},{8,12},{12,8},{9,1... | collective-permute-start | bytes 24584 | tf_op jit(solution)/shard_map/ppermute | solution.py:45
  3.0 0.9 %slice_select_fusion = bf16[128,256]{1,0:T(8,128)(2,1)S(1)} fusion(bf16[4096,256]{1,0:T(8,128)(2,1)} %cotangent.5, pred[]{:T(512)S(6)} %eq.3), kind=kLoop, calls=%fused_computation.6 | loop fusion | flops 32768 | bytes 196609 | tf_op jit(solution)/shard_map/jit(_where)/select_n | solution.py:22
  4.0 2.7 %project.1 = bf16[512,256]{1,0:T(8,128)(2,1)} custom-call(s32[1]{0:T(128)} %bitcast.1.where.chan.chan_at, bf16[2048,1152]{1,0:T(8,128)(2,1)} %spectra.9, bf16[1152,256]{1,0:T(8,128)(2,1)} %weight.7), custom_call_target="tpu_custom_call" | custom-call | flops 301989888 | bytes 2031616 | tf_op jit(solution)/shard_map/project/pallas_call | solution.py:88
  6.7 2.1 %collective-permute-start.2 = (bf16[512,256]{1,0:T(8,128)(2,1)}, bf16[512,256]{1,0:T(8,128)(2,1)S(1)}, u32[]{:S(2)}, u32[]{:S(2)}) collective-permute-start(bf16[512,256]{1,0:T(8,128)(2,1)} %project.1), channel_id=1, source_target_pairs={{0,1},{1,0},{2,3},{3,2},{4,5},{5,4},{6,7},{7,6},{8,9},{9,8},{10,11... | collective-permute-start | bytes 786440 | tf_op jit(solution)/shard_map/ppermute | solution.py:45
  8.9 5.5 %pixel_rows.3 = (bf16[256,256]{1,0:T(8,128)(2,1)S(1)}, bf16[512,256]{1,0:T(8,128)(2,1)S(1)}, bf16[512,256]{1,0:T(8,128)(2,1)S(1)}) custom-call(s32[1]{0:T(128)} %bitcast.1.where.chan.chan_at, s32[16384]{0:T(1024)S(1)} %bitcast.10, s32[2048]{0:T(1024)S(1)} %collective-permute-done.wanted, bf16[4096,256]{1,0:T(8,128)(2,1)} %cotangent.5, ...), custom_call_target="tpu_custom_call" | custom-call | flops 8589934592 | bytes 4194304 | tf_op jit(solution)/shard_map/pixel_rows/pallas_call | solution.py:304
  14.9 3.7 %pixel_rows.4 = bf16[256,256]{1,0:T(8,128)(2,1)S(1)} custom-call(s32[1]{0:T(128)} %bitcast.3.where, s32[16384]{0:T(1024)S(1)} %bitcast.11, s32[2048]{0:T(1024)S(1)} %collective-permute-done.wanted, bf16[4096,256]{1,0:T(8,128)(2,1)} %cotangent.5, bf16[128,256]{1,0:T(8,128)(2,1)S(1)} %collective-permute-done.1.above.below, ...), custom_call_target="tpu_custom_call" | custom-call | flops 8589934592 | bytes 4194304 | tf_op jit(solution)/shard_map/pixel_rows/pallas_call | solution.py:304
  18.6 1.7 %collective-permute-start.5 = (bf16[512,256]{1,0:T(8,128)(2,1)S(1)}, bf16[512,256]{1,0:T(8,128)(2,1)S(1)}, u32[]{:S(2)}, u32[]{:S(2)}) collective-permute-start(bf16[512,256]{1,0:T(8,128)(2,1)S(1)} %pad_maximum_fusion), channel_id=1, source_target_pairs={{0,4},{4,0},{1,5},{5,1},{2,6},{6,2},{3,7},{7,3},{8,12},{12,8},{9,1... | collective-permute-start | bytes 786440 | tf_op jit(solution)/shard_map/ppermute | solution.py:45
  20.3 1.6 %collective-permute-start.3 = (bf16[512,256]{1,0:T(8,128)(2,1)S(1)}, bf16[512,256]{1,0:T(8,128)(2,1)S(1)}, u32[]{:S(2)}, u32[]{:S(2)}) collective-permute-start(bf16[512,256]{1,0:T(8,128)(2,1)S(1)} %get-tuple-element.34), channel_id=1, source_target_pairs={{0,1},{1,0},{2,3},{3,2},{4,5},{5,4},{6,7},{7,6},{8,9},{9,8},{10,11... | collective-permute-start | bytes 786440 | tf_op jit(solution)/shard_map/ppermute | solution.py:45
  21.9 2.5 %collective-permute-start.4 = (bf16[512,256]{1,0:T(8,128)(2,1)S(1)}, bf16[512,256]{1,0:T(8,128)(2,1)S(1)}, u32[]{:S(2)}, u32[]{:S(2)}) collective-permute-start(bf16[512,256]{1,0:T(8,128)(2,1)S(1)} %add_convert_fusion), channel_id=1, source_target_pairs={{0,3},{1,2},{2,1},{3,0},{4,7},{5,6},{6,5},{7,4},{8,11},{9,10},{10,... | collective-permute-start | bytes 786440 | tf_op jit(solution)/shard_map/ppermute | solution.py:45
  24.4 6.3 %pixel_rows.5 = (bf16[512,256]{1,0:T(8,128)(2,1)S(1)}, bf16[512,256]{1,0:T(8,128)(2,1)S(1)}) custom-call(s32[1]{0:T(128)} %bitcast.4.where, s32[16384]{0:T(1024)S(1)} %bitcast.12, s32[2048]{0:T(1024)S(1)} %copy-done.3, bf16[4096,256]{1,0:T(8,128)(2,1)} %cotangent.5, bf16[128,256]{1,0:T(8,128)(2,1)S(1)} %collective-permute-done.1.above.below, ...), custom_call_target="tpu_custom_call" | custom-call | flops 17179869184 | bytes 4194304 | tf_op jit(solution)/shard_map/pixel_rows/pallas_call | solution.py:304
  30.7 3.8 %collective-permute-done.4.far = bf16[512,256]{1,0:T(8,128)(2,1)S(1)} collective-permute-done((bf16[512,256]{1,0:T(8,128)(2,1)S(1)}, bf16[512,256]{1,0:T(8,128)(2,1)S(1)}, u32[]{:S(2)}, u32[]{:S(2)}) %collective-permute-start.4) | collective-permute-done | bytes 262176 | tf_op jit(solution)/shard_map/ppermute | solution.py:45
  35.0 1.4 %collective-permute-start.6 = (bf16[512,256]{1,0:T(8,128)(2,1)S(1)}, bf16[512,256]{1,0:T(8,128)(2,1)S(1)}, u32[]{:S(2)}, u32[]{:S(2)}) collective-permute-start(bf16[512,256]{1,0:T(8,128)(2,1)S(1)} %pre_gradient.1.first), channel_id=1, source_target_pairs={{0,3},{1,2},{2,1},{3,0},{4,7},{5,6},{6,5},{7,4},{8,11},{9,10},{10,... | collective-permute-start | bytes 786440 | tf_op jit(solution)/shard_map/ppermute | solution.py:45
  36.4 4.9 %collective-permute-start.7 = (bf16[512,256]{1,0:T(8,128)(2,1)S(1)}, bf16[512,256]{1,0:T(8,128)(2,1)S(1)}, u32[]{:S(2)}, u32[]{:S(2)}) collective-permute-start(bf16[512,256]{1,0:T(8,128)(2,1)S(1)} %pre_gradient.1.first), channel_id=1, source_target_pairs={{0,1},{1,0},{2,3},{3,2},{4,5},{5,4},{6,7},{7,6},{8,9},{9,8},{10,11... | collective-permute-start | bytes 786440 | tf_op jit(solution)/shard_map/ppermute | solution.py:45
  41.3 3.8 %collective-permute-done.6.second = bf16[512,256]{1,0:T(8,128)(2,1)S(1)} collective-permute-done((bf16[512,256]{1,0:T(8,128)(2,1)S(1)}, bf16[512,256]{1,0:T(8,128)(2,1)S(1)}, u32[]{:S(2)}, u32[]{:S(2)}) %collective-permute-start.6) | collective-permute-done | bytes 262176 | tf_op jit(solution)/shard_map/ppermute | solution.py:45
  45.2 2.4 %collective-permute-start.8 = (bf16[512,256]{1,0:T(8,128)(2,1)S(1)}, bf16[512,256]{1,0:T(8,128)(2,1)S(1)}, u32[]{:S(2)}, u32[]{:S(2)}) collective-permute-start(bf16[512,256]{1,0:T(8,128)(2,1)S(1)} %collective-permute-done.6.second), channel_id=1, source_target_pairs={{0,1},{1,0},{2,3},{3,2},{4,5},{5,4},{6,7},{7,6},{8,9},{9,8},{10,11... | collective-permute-start | bytes 786440 | tf_op jit(solution)/shard_map/ppermute | solution.py:45
  47.6 2.5 %early_product.1 = (f32[1152,256]{1,0:T(8,128)S(1)}, bf16[512,1152]{1,0:T(8,128)(2,1)S(1)}, bf16[512,1152]{1,0:T(8,128)(2,1)S(1)}) custom-call(s32[1]{0:T(128)} %bitcast.1.where.chan.chan_at, bf16[2048,1152]{1,0:T(8,128)(2,1)} %spectra.9, bf16[512,256]{1,0:T(8,128)(2,1)S(1)} %pre_gradient.1.first, bf16[512,256]{1,0:T(8,128)(2,1)S(1)} %collective-permute-done.6.second), custom_call_target="tpu_custom_call" | custom-call | flops 603979776 | bytes 5898240 | tf_op jit(solution)/shard_map/early_product/pallas_call | solution.py:135
  50.1 0.5 more_product.1.before
  50.6 1.7 %collective-permute-done.8.rows = bf16[512,256]{1,0:T(8,128)(2,1)S(1)} collective-permute-done((bf16[512,256]{1,0:T(8,128)(2,1)S(1)}, bf16[512,256]{1,0:T(8,128)(2,1)S(1)}, u32[]{:S(2)}, u32[]{:S(2)}) %collective-permute-start.8) | collective-permute-done | bytes 262176 | tf_op jit(solution)/shard_map/ppermute | solution.py:45
  52.3 0.6 late_product.1
  53.0 0.5 collective-permute-start.12
  53.5 0.9 %collective-permute-done.9.second = bf16[288,256]{1,0:T(8,128)(2,1)S(1)} collective-permute-done((bf16[288,256]{1,0:T(8,128)(2,1)S(1)}, bf16[288,256]{1,0:T(8,128)(2,1)S(1)}, u32[]{:S(2)}, u32[]{:S(2)}) %collective-permute-start.9) | collective-permute-done | bytes 147488 | tf_op jit(solution)/shard_map/ppermute | solution.py:45
  54.4 1.6 %collective-permute-start.10 = (bf16[288,256]{1,0:T(8,128)(2,1)S(1)}, bf16[288,256]{1,0:T(8,128)(2,1)S(1)}, u32[]{:S(2)}, u32[]{:S(2)}) collective-permute-start(bf16[288,256]{1,0:T(8,128)(2,1)S(1)} %added.6.first), channel_id=1, source_target_pairs={{0,16},{4,20},{8,12},{12,8},{16,0},{20,4},{24,28},{28,24},{1,17},{... | collective-permute-start | bytes 442376 | tf_op jit(solution)/shard_map/ppermute | solution.py:445
  56.0 0.6 collective-permute-start.13
  56.6 3.0 %collective-permute-done.10.second = bf16[288,256]{1,0:T(8,128)(2,1)S(1)} collective-permute-done((bf16[288,256]{1,0:T(8,128)(2,1)S(1)}, bf16[288,256]{1,0:T(8,128)(2,1)S(1)}, u32[]{:S(2)}, u32[]{:S(2)}) %collective-permute-start.10) | collective-permute-done | bytes 147488 | tf_op jit(solution)/shard_map/ppermute | solution.py:445
  59.6 0.6 collective-permute-start.11
  60.2 1.0 %collective-permute-done.13.second = bf16[288,256]{1,0:T(8,128)(2,1)S(1)} collective-permute-done((bf16[288,256]{1,0:T(8,128)(2,1)S(1)}, bf16[288,256]{1,0:T(8,128)(2,1)S(1)}, u32[]{:S(2)}, u32[]{:S(2)}) %collective-permute-start.13) | collective-permute-done | bytes 147488 | tf_op jit(solution)/shard_map/ppermute | solution.py:445
  61.2 0.6 collective-permute-start.14
  61.8 3.0 %collective-permute-done.11.second = bf16[288,256]{1,0:T(8,128)(2,1)S(1)} collective-permute-done((bf16[288,256]{1,0:T(8,128)(2,1)S(1)}, bf16[288,256]{1,0:T(8,128)(2,1)S(1)}, u32[]{:S(2)}, u32[]{:S(2)}) %collective-permute-start.11) | collective-permute-done | bytes 147488 | tf_op jit(solution)/shard_map/ppermute | solution.py:445
  64.9 1.5 %collective-permute-done.14.second = bf16[288,256]{1,0:T(8,128)(2,1)S(1)} collective-permute-done((bf16[288,256]{1,0:T(8,128)(2,1)S(1)}, bf16[288,256]{1,0:T(8,128)(2,1)S(1)}, u32[]{:S(2)}, u32[]{:S(2)}) %collective-permute-start.14) | collective-permute-done | bytes 147488 | tf_op jit(solution)/shard_map/ppermute | solution.py:445
  66.5 0.9 %written.2.refs_0_ = f32[1152,256]{1,0:T(8,128)} custom-call(s32[1]{0:T(128)} %bitcast.core, bf16[288,256]{1,0:T(8,128)(2,1)S(1)} %added.8.refs_0_, bf16[288,256]{1,0:T(8,128)(2,1)S(1)} %added.11.refs_1_), custom_call_target="tpu_custom_call" | custom-call | tf_op jit(solution)/shard_map/written/pallas_call | solution.py:404
  67.4 0.5 collective-permute-done.16.refs_2_
  67.9 0.8 %written.3 = f32[1152,256]{1,0:T(8,128)} custom-call(s32[1]{0:T(128)} %bitcast.core, f32[1152,256]{1,0:T(8,128)} %written.2.refs_0_, bf16[288,256]{1,0:T(8,128)(2,1)S(1)} %collective-permute-done.15.refs_1_, bf16[288,256]{1,0:T(8,128)(2,1)S(1)} %collective-permute-done.16.refs_2_), custom_call_target="tpu_custom_call", output_to_operand_aliasing={{}: (1, {})} | custom-call | tf_op jit(solution)/shard_map/written/pallas_call | solution.py:404
  (36 shorter events, 1.5 us)
Async XLA Ops:
  0.0 8.9 %collective-permute-start = (s32[2048]{0:T(1024)}, s32[2048]{0:T(1024)S(1)}, u32[]{:S(2)}, u32[]{:S(2)}) collective-permute-start(s32[2048]{0:T(1024)} %wanted.1), channel_id=1, source_target_pairs={{0,4},{4,0},{1,5},{5,1},{2,6},{6,2},{3,7},{7,3},{8,12},{12,8},{9,1... | collective-permute-start | bytes 24584 | tf_op jit(solution)/shard_map/ppermute | solution.py:45
  3.9 5.0 %collective-permute-start.1 = (bf16[128,256]{1,0:T(8,128)(2,1)S(1)}, bf16[128,256]{1,0:T(8,128)(2,1)S(1)}, u32[]{:S(2)}, u32[]{:S(2)}) collective-permute-start(bf16[128,256]{1,0:T(8,128)(2,1)S(1)} %slice_select_fusion), channel_id=1, source_target_pairs={{0,4},{4,0},{1,5},{5,1},{2,6},{6,2},{3,7},{7,3},{8,12},{12,8},{9,1... | collective-permute-start | bytes 196616 | tf_op jit(solution)/shard_map/ppermute | solution.py:22
  3.9 4.9 %copy-start.5 = (s32[8,4096]{1,0:T(8,128)S(1)}, s32[8,4096]{1,0:T(8,128)}, u32[]{:S(2)}) copy-start(s32[8,4096]{1,0:T(8,128)} %param.14) | copy-start | bytes 393220
  3.9 5.0 %copy-start = (bf16[1152,256]{1,0:T(8,128)(2,1)S(1)}, bf16[1152,256]{1,0:T(8,128)(2,1)}, u32[]{:S(2)}) copy-start(bf16[1152,256]{1,0:T(8,128)(2,1)} %weight.7) | copy-start | bytes 1769476
  4.0 5.0 %copy-start.4 = (f32[8,256]{1,0:T(8,128)S(1)}, f32[8,256]{1,0:T(8,128)}, u32[]{:S(2)}) copy-start(f32[8,256]{1,0:T(8,128)} %mixing.5) | copy-start | bytes 24580
  6.7 8.1 %collective-permute-start.2 = (bf16[512,256]{1,0:T(8,128)(2,1)}, bf16[512,256]{1,0:T(8,128)(2,1)S(1)}, u32[]{:S(2)}, u32[]{:S(2)}) collective-permute-start(bf16[512,256]{1,0:T(8,128)(2,1)} %project.1), channel_id=1, source_target_pairs={{0,1},{1,0},{2,3},{3,2},{4,5},{5,4},{6,7},{7,6},{8,9},{9,8},{10,11... | collective-permute-start | bytes 786440 | tf_op jit(solution)/shard_map/ppermute | solution.py:45
  14.8 9.5 %copy-start.3 = (s32[2048]{0:T(1024)S(1)}, s32[2048]{0:T(1024)}, u32[]{:S(2)}) copy-start(s32[2048]{0:T(1024)} %wanted.1) | copy-start | bytes 24580
  18.6 12.1 %collective-permute-start.5 = (bf16[512,256]{1,0:T(8,128)(2,1)S(1)}, bf16[512,256]{1,0:T(8,128)(2,1)S(1)}, u32[]{:S(2)}, u32[]{:S(2)}) collective-permute-start(bf16[512,256]{1,0:T(8,128)(2,1)S(1)} %pad_maximum_fusion), channel_id=1, source_target_pairs={{0,4},{4,0},{1,5},{5,1},{2,6},{6,2},{3,7},{7,3},{8,12},{12,8},{9,1... | collective-permute-start | bytes 786440 | tf_op jit(solution)/shard_map/ppermute | solution.py:45
  20.3 10.4 %collective-permute-start.3 = (bf16[512,256]{1,0:T(8,128)(2,1)S(1)}, bf16[512,256]{1,0:T(8,128)(2,1)S(1)}, u32[]{:S(2)}, u32[]{:S(2)}) collective-permute-start(bf16[512,256]{1,0:T(8,128)(2,1)S(1)} %get-tuple-element.34), channel_id=1, source_target_pairs={{0,1},{1,0},{2,3},{3,2},{4,5},{5,4},{6,7},{7,6},{8,9},{9,8},{10,11... | collective-permute-start | bytes 786440 | tf_op jit(solution)/shard_map/ppermute | solution.py:45
  21.9 12.6 %collective-permute-start.4 = (bf16[512,256]{1,0:T(8,128)(2,1)S(1)}, bf16[512,256]{1,0:T(8,128)(2,1)S(1)}, u32[]{:S(2)}, u32[]{:S(2)}) collective-permute-start(bf16[512,256]{1,0:T(8,128)(2,1)S(1)} %add_convert_fusion), channel_id=1, source_target_pairs={{0,3},{1,2},{2,1},{3,0},{4,7},{5,6},{6,5},{7,4},{8,11},{9,10},{10,... | collective-permute-start | bytes 786440 | tf_op jit(solution)/shard_map/ppermute | solution.py:45
  24.4 10.1 %copy-start.1 = (s32[2048,1]{0,1:T(1,128)S(1)}, s32[2048,1]{0,1:T(1,128)}, u32[]{:S(2)}) copy-start(s32[2048,1]{0,1:T(1,128)} %param.10) | copy-start | bytes 24580
  24.4 10.1 %copy-start.2 = (f32[2048]{0:T(1024)S(1)}, f32[2048]{0:T(1024)}, u32[]{:S(2)}) copy-start(f32[2048]{0:T(1024)} %param.12) | copy-start | bytes 24580
  35.0 10.2 %collective-permute-start.6 = (bf16[512,256]{1,0:T(8,128)(2,1)S(1)}, bf16[512,256]{1,0:T(8,128)(2,1)S(1)}, u32[]{:S(2)}, u32[]{:S(2)}) collective-permute-start(bf16[512,256]{1,0:T(8,128)(2,1)S(1)} %pre_gradient.1.first), channel_id=1, source_target_pairs={{0,3},{1,2},{2,1},{3,0},{4,7},{5,6},{6,5},{7,4},{8,11},{9,10},{10,... | collective-permute-start | bytes 786440 | tf_op jit(solution)/shard_map/ppermute | solution.py:45
  36.4 13.7 %collective-permute-start.7 = (bf16[512,256]{1,0:T(8,128)(2,1)S(1)}, bf16[512,256]{1,0:T(8,128)(2,1)S(1)}, u32[]{:S(2)}, u32[]{:S(2)}) collective-permute-start(bf16[512,256]{1,0:T(8,128)(2,1)S(1)} %pre_gradient.1.first), channel_id=1, source_target_pairs={{0,1},{1,0},{2,3},{3,2},{4,5},{5,4},{6,7},{7,6},{8,9},{9,8},{10,11... | collective-permute-start | bytes 786440 | tf_op jit(solution)/shard_map/ppermute | solution.py:45
  45.2 7.2 %collective-permute-start.8 = (bf16[512,256]{1,0:T(8,128)(2,1)S(1)}, bf16[512,256]{1,0:T(8,128)(2,1)S(1)}, u32[]{:S(2)}, u32[]{:S(2)}) collective-permute-start(bf16[512,256]{1,0:T(8,128)(2,1)S(1)} %collective-permute-done.6.second), channel_id=1, source_target_pairs={{0,1},{1,0},{2,3},{3,2},{4,5},{5,4},{6,7},{7,6},{8,9},{9,8},{10,11... | collective-permute-start | bytes 786440 | tf_op jit(solution)/shard_map/ppermute | solution.py:45
  52.9 1.4 %collective-permute-start.9 = (bf16[288,256]{1,0:T(8,128)(2,1)S(1)}, bf16[288,256]{1,0:T(8,128)(2,1)S(1)}, u32[]{:S(2)}, u32[]{:S(2)}) collective-permute-start(bf16[288,256]{1,0:T(8,128)(2,1)S(1)} %get-tuple-element.42), channel_id=1, source_target_pairs={{0,8},{8,0},{16,24},{24,16},{1,9},{9,1},{17,25},{25,17},{2,10},{10... | collective-permute-start | bytes 442376 | tf_op jit(solution)/shard_map/ppermute | solution.py:45
  53.0 2.9 %collective-permute-start.12 = (bf16[288,256]{1,0:T(8,128)(2,1)S(1)}, bf16[288,256]{1,0:T(8,128)(2,1)S(1)}, u32[]{:S(2)}, u32[]{:S(2)}) collective-permute-start(bf16[288,256]{1,0:T(8,128)(2,1)S(1)} %get-tuple-element.44), channel_id=1, source_target_pairs={{0,8},{8,0},{16,24},{24,16},{1,9},{9,1},{17,25},{25,17},{2,10},{10... | collective-permute-start | bytes 442376 | tf_op jit(solution)/shard_map/ppermute | solution.py:45
  54.4 5.2 %collective-permute-start.10 = (bf16[288,256]{1,0:T(8,128)(2,1)S(1)}, bf16[288,256]{1,0:T(8,128)(2,1)S(1)}, u32[]{:S(2)}, u32[]{:S(2)}) collective-permute-start(bf16[288,256]{1,0:T(8,128)(2,1)S(1)} %added.6.first), channel_id=1, source_target_pairs={{0,16},{4,20},{8,12},{12,8},{16,0},{20,4},{24,28},{28,24},{1,17},{... | collective-permute-start | bytes 442376 | tf_op jit(solution)/shard_map/ppermute | solution.py:445
  56.0 5.2 %collective-permute-start.13 = (bf16[288,256]{1,0:T(8,128)(2,1)S(1)}, bf16[288,256]{1,0:T(8,128)(2,1)S(1)}, u32[]{:S(2)}, u32[]{:S(2)}) collective-permute-start(bf16[288,256]{1,0:T(8,128)(2,1)S(1)} %added.9.first), channel_id=1, source_target_pairs={{0,16},{4,20},{8,12},{12,8},{16,0},{20,4},{24,28},{28,24},{1,17},{... | collective-permute-start | bytes 442376 | tf_op jit(solution)/shard_map/ppermute | solution.py:445
  59.6 5.2 %collective-permute-start.11 = (bf16[288,256]{1,0:T(8,128)(2,1)S(1)}, bf16[288,256]{1,0:T(8,128)(2,1)S(1)}, u32[]{:S(2)}, u32[]{:S(2)}) collective-permute-start(bf16[288,256]{1,0:T(8,128)(2,1)S(1)} %added.7.first), channel_id=1, source_target_pairs={{0,4},{4,0},{8,24},{12,28},{16,20},{20,16},{24,8},{28,12},{1,5},{5... | collective-permute-start | bytes 442376 | tf_op jit(solution)/shard_map/ppermute | solution.py:445
  61.2 5.2 %collective-permute-start.14 = (bf16[288,256]{1,0:T(8,128)(2,1)S(1)}, bf16[288,256]{1,0:T(8,128)(2,1)S(1)}, u32[]{:S(2)}, u32[]{:S(2)}) collective-permute-start(bf16[288,256]{1,0:T(8,128)(2,1)S(1)} %added.10.first), channel_id=1, source_target_pairs={{0,4},{4,0},{8,24},{12,28},{16,20},{20,16},{24,8},{28,12},{1,5},{5... | collective-permute-start | bytes 442376 | tf_op jit(solution)/shard_map/ppermute | solution.py:445
  64.9 2.5 %collective-permute-start.15 = (bf16[288,256]{1,0:T(8,128)(2,1)S(1)}, bf16[288,256]{1,0:T(8,128)(2,1)S(1)}, u32[]{:S(2)}, u32[]{:S(2)}) collective-permute-start(bf16[288,256]{1,0:T(8,128)(2,1)S(1)} %added.8.refs_0_), channel_id=1, source_target_pairs={{0,8},{8,0},{16,24},{24,16},{1,9},{9,1},{17,25},{25,17},{2,10},{10... | collective-permute-start | bytes 442376 | tf_op jit(solution)/shard_map/ppermute | solution.py:45
  66.5 1.4 %collective-permute-start.16 = (bf16[288,256]{1,0:T(8,128)(2,1)S(1)}, bf16[288,256]{1,0:T(8,128)(2,1)S(1)}, u32[]{:S(2)}, u32[]{:S(2)}) collective-permute-start(bf16[288,256]{1,0:T(8,128)(2,1)S(1)} %added.11.refs_1_), channel_id=1, source_target_pairs={{0,8},{8,0},{16,24},{24,16},{1,9},{9,1},{17,25},{25,17},{2,10},{10... | collective-permute-start | bytes 442376 | tf_op jit(solution)/shard_map/ppermute | solution.py:45

commit v25 on v22

--- a/solution.py
+++ b/solution.py
@@ -11,6 +11,7 @@
 HALO = 128
 MIB = 1024 * 1024
 LARGE = 52
+CHUNKS = 3
 
 
 def edges(value, axis, width):
@@ -186,21 +187,21 @@
     total[...] = before[...] + turned_product(held[...], rows[...])
     size = outs[0].shape[0]
     for index, out in enumerate(outs):
-        first = (core[0] ^ (1 - index // 2)) * 2 * size + index % 2 * size
+        first = (core[0] ^ (1 - index // CHUNKS)) * CHUNKS * size + index % CHUNKS * size
         here = pl.ds(pl.multiple_of(first, size), size)
         out[...] = total[here, :].astype(out.dtype)
 
 
 def late_product(core, held, before, rows):
-    size, width = before.shape[0] // 4, before.shape[1]
+    size, width = before.shape[0] // (2 * CHUNKS), before.shape[1]
     spec = pl.BlockSpec(memory_space=pltpu.VMEM)
     send = jax.ShapeDtypeStruct((size, width), jnp.bfloat16)
     keep = jax.ShapeDtypeStruct((size, width), jnp.float32)
     outs = pl.pallas_call(
         late_kernel,
-        out_shape=(send, send, keep, keep),
+        out_shape=(send,) * CHUNKS + (keep,) * CHUNKS,
         in_specs=[pl.BlockSpec(memory_space=pltpu.SMEM)] + [spec] * 3,
-        out_specs=(spec,) * 4,
+        out_specs=(spec,) * (2 * CHUNKS),
         scratch_shapes=[pltpu.VMEM(before.shape, jnp.float32)],
         compiler_params=memory(16),
         cost_estimate=pl.CostEstimate(
@@ -210,7 +211,7 @@
         ),
         name="late_product",
     )(core.reshape(1), held, before, rows)
-    return outs[:2], outs[2:]
+    return outs[:CHUNKS], outs[CHUNKS:]
 
 
 def pixel_kernel(count, bits, stride, where, places, wanted, cotangent, above, below, mixing, weight,
@@ -384,10 +385,11 @@
 
 
 def write_kernel(other, core, *refs):
-    *pieces, out, first, second, sems = refs
-    half, rows = out.shape[0] // 2, first.shape[0]
+    out, holds, sems = refs[-CHUNKS - 2], refs[-CHUNKS - 1 : -1], refs[-1]
+    pieces = refs[-2 * CHUNKS - 2 : -CHUNKS - 2]
+    half, rows = out.shape[0] // 2, holds[0].shape[0]
     copies = []
-    for index, (piece, held) in enumerate(zip(pieces[-2:], (first, second))):
+    for index, (piece, held) in enumerate(zip(pieces, holds)):
         held[...] = piece[...].astype(jnp.float32)
         place = (core[0] ^ other) * half + index * rows
         here = out.at[pl.ds(pl.multiple_of(place, rows), rows)]
@@ -403,14 +405,13 @@
     hbm = pl.BlockSpec(memory_space=pltpu.HBM)
     return pl.pallas_call(
         functools.partial(write_kernel, other),
-        out_shape=jax.ShapeDtypeStruct((4 * rows, width), jnp.float32),
-        in_specs=[pl.BlockSpec(memory_space=pltpu.SMEM)] + [hbm] * len(before) + [spec] * 2,
+        out_shape=jax.ShapeDtypeStruct((2 * CHUNKS * rows, width), jnp.float32),
+        in_specs=[pl.BlockSpec(memory_space=pltpu.SMEM)] + [hbm] * len(before) + [spec] * CHUNKS,
         out_specs=hbm,
         input_output_aliases={1: 0} if before else {},
         scratch_shapes=[
-            pltpu.VMEM((rows, width), jnp.float32),
-            pltpu.VMEM((rows, width), jnp.float32),
-            pltpu.SemaphoreType.DMA((2,)),
+            *[pltpu.VMEM((rows, width), jnp.float32)] * CHUNKS,
+            pltpu.SemaphoreType.DMA((CHUNKS,)),
         ],
         compiler_params=memory(16),
         name="written",

time: 66.2 us -> 66.6 us (level)
  starting transfers between devices: 19.6 us -> 22.9 us
  waiting for transfers between devices: 22.7 us -> 19.7 us
    ppermute x4 -> x6, starting transfers between devices: 5.33 us -> 8.48 us  [sum_over_panels(): parts = [added(part, lax.ppermute(part, both, perm)) for part in parts]]
    ppermute x4 -> x6, waiting for transfers between devices: 6.57 us -> 3.79 us  [sum_over_panels(): parts = [added(part, lax.ppermute(part, both, perm)) for part in parts]]
    ppermute x12 -> x14, waiting for transfers between devices: 16.1 us -> 15.9 us  [swap(): return lax.ppermute(value, axis, [(i, i ^ bit) for i in range(size)])]
    ppermute x12 -> x14, starting transfers between devices: 14.2 us -> 14.4 us  [swap(): return lax.ppermute(value, axis, [(i, i ^ bit) for i in range(size)])]
  transfers between devices with their start and end apart: 17 -> 21, of which waited for: 9 -> 9; matrix products, arithmetic and copies ran while one was open for 1% -> 1% of each run, Pallas kernels for 31% -> 31%
where the time goes in v25:
time: 66.6 us; the launch traced here: 66.4 us
  starting transfers between devices  22.9 us (34%)
  Pallas kernels  22.4 us (34%)
  waiting for transfers between devices  19.7 us (30%)
  other arithmetic  0.98 us (1%)
    ppermute x14, waiting for transfers between devices, swap(): return lax.ppermute(value, axis, [(i, i ^ bit) for i in range(size)])  15.9 us
    ppermute x14, starting transfers between devices, swap(): return lax.ppermute(value, axis, [(i, i ^ bit) for i in range(size)])  14.4 us
    pallas_call x2, Pallas kernels, pixel_rows(): pl.pallas_call(functools.partial(pixel_kernel, count, bits, stride), out_...  13.7 us
    ppermute x6, starting transfers between devices, sum_over_panels(): parts = [added(part, lax.ppermute(part, both, perm)) for part in parts]  8.48 us
    ppermute x6, waiting for transfers between devices, sum_over_panels(): parts = [added(part, lax.ppermute(part, both, perm)) for part in parts]  3.79 us
    pallas_call x1, Pallas kernels, project(): pl.pallas_call(functools.partial(project_kernel, bits), out_shape=(jax.Sh...  2.74 us
    pallas_call x1, Pallas kernels, early_product(): pl.pallas_call(early_kernel, out_shape=(jax.ShapeDtypeStruct((depth, widt...  2.49 us
    pallas_call x2, Pallas kernels, written(): pl.pallas_call(functools.partial(write_kernel, other), out_shape=jax.Shap...  1.69 us
  transfers between devices with their start and end apart: 21, of which 9 were waited for; matrix products, arithmetic and copies ran while one was open for 1% of the time, Pallas kernels for 31%

profile of v25, /device:TPU:0, one launch (start us, length us, event | category | flops | bytes accessed | tf_op | source)
XLA Modules:
  0.0 66.4 jit_solution(12320555131361500675)
XLA Ops:
  0.0 3.0 %collective-permute-start = (s32[2048]{0:T(1024)}, s32[2048]{0:T(1024)S(1)}, u32[]{:S(2)}, u32[]{:S(2)}) collective-permute-start(s32[2048]{0:T(1024)} %wanted.1), channel_id=1, source_target_pairs={{0,4},{4,0},{1,5},{5,1},{2,6},{6,2},{3,7},{7,3},{8,12},{12,8},{9,1... | collective-permute-start | bytes 24584 | tf_op jit(solution)/shard_map/ppermute | solution.py:46
  3.0 0.9 %slice_select_fusion = bf16[128,256]{1,0:T(8,128)(2,1)S(1)} fusion(bf16[4096,256]{1,0:T(8,128)(2,1)} %cotangent.3, pred[]{:T(512)S(6)} %eq.3), kind=kLoop, calls=%fused_computation.5 | loop fusion | flops 32768 | bytes 196609 | tf_op jit(solution)/shard_map/jit(_where)/select_n | solution.py:23
  4.0 2.7 %project.1 = bf16[512,256]{1,0:T(8,128)(2,1)} custom-call(s32[1]{0:T(128)} %bitcast.1.where.chan.chan_at, bf16[2048,1152]{1,0:T(8,128)(2,1)} %spectra.7, bf16[1152,256]{1,0:T(8,128)(2,1)} %weight.5), custom_call_target="tpu_custom_call" | custom-call | flops 301989888 | bytes 2031616 | tf_op jit(solution)/shard_map/project/pallas_call | solution.py:89
  6.7 2.1 %collective-permute-start.2 = (bf16[512,256]{1,0:T(8,128)(2,1)}, bf16[512,256]{1,0:T(8,128)(2,1)S(1)}, u32[]{:S(2)}, u32[]{:S(2)}) collective-permute-start(bf16[512,256]{1,0:T(8,128)(2,1)} %project.1), channel_id=1, source_target_pairs={{0,1},{1,0},{2,3},{3,2},{4,5},{5,4},{6,7},{7,6},{8,9},{9,8},{10,11... | collective-permute-start | bytes 786440 | tf_op jit(solution)/shard_map/ppermute | solution.py:46
  8.9 7.4 %pixel_rows.2 = (bf16[512,256]{1,0:T(8,128)(2,1)S(1)}, bf16[512,256]{1,0:T(8,128)(2,1)S(1)}, bf16[512,256]{1,0:T(8,128)(2,1)S(1)}) custom-call(s32[1]{0:T(128)} %bitcast.1.where.chan.chan_at, s32[16384]{0:T(1024)S(1)} %bitcast.9, s32[2048]{0:T(1024)S(1)} %collective-permute-done.wanted, bf16[4096,256]{1,0:T(8,128)(2,1)} %cotangent.3, ...), custom_call_target="tpu_custom_call" | custom-call | flops 17179869184 | bytes 4194304 | tf_op jit(solution)/shard_map/pixel_rows/pallas_call | solution.py:305
  16.4 0.9 %collective-permute-start.3 = (bf16[512,256]{1,0:T(8,128)(2,1)S(1)}, bf16[512,256]{1,0:T(8,128)(2,1)S(1)}, u32[]{:S(2)}, u32[]{:S(2)}) collective-permute-start(bf16[512,256]{1,0:T(8,128)(2,1)S(1)} %get-tuple-element.32), channel_id=1, source_target_pairs={{0,1},{1,0},{2,3},{3,2},{4,5},{5,4},{6,7},{7,6},{8,9},{9,8},{10,11... | collective-permute-start | bytes 786440 | tf_op jit(solution)/shard_map/ppermute | solution.py:46
  17.3 3.2 %collective-permute-start.4 = (bf16[512,256]{1,0:T(8,128)(2,1)S(1)}, bf16[512,256]{1,0:T(8,128)(2,1)S(1)}, u32[]{:S(2)}, u32[]{:S(2)}) collective-permute-start(bf16[512,256]{1,0:T(8,128)(2,1)S(1)} %add_convert_fusion), channel_id=1, source_target_pairs={{0,3},{1,2},{2,1},{3,0},{4,7},{5,6},{6,5},{7,4},{8,11},{9,10},{10,... | collective-permute-start | bytes 786440 | tf_op jit(solution)/shard_map/ppermute | solution.py:46
  20.5 1.5 %collective-permute-start.5 = (bf16[512,256]{1,0:T(8,128)(2,1)S(1)}, bf16[512,256]{1,0:T(8,128)(2,1)S(1)}, u32[]{:S(2)}, u32[]{:S(2)}) collective-permute-start(bf16[512,256]{1,0:T(8,128)(2,1)S(1)} %get-tuple-element.35), channel_id=1, source_target_pairs={{0,4},{4,0},{1,5},{5,1},{2,6},{6,2},{3,7},{7,3},{8,12},{12,8},{9,1... | collective-permute-start | bytes 786440 | tf_op jit(solution)/shard_map/ppermute | solution.py:46
  22.1 6.3 %pixel_rows.3 = (bf16[512,256]{1,0:T(8,128)(2,1)S(1)}, bf16[512,256]{1,0:T(8,128)(2,1)S(1)}) custom-call(s32[1]{0:T(128)} %bitcast.3.where, s32[16384]{0:T(1024)S(1)} %bitcast.10, s32[2048]{0:T(1024)S(1)} %copy-done.3, bf16[4096,256]{1,0:T(8,128)(2,1)} %cotangent.3, bf16[128,256]{1,0:T(8,128)(2,1)S(1)} %collective-permute-done.1.above.below, ...), custom_call_target="tpu_custom_call" | custom-call | flops 17179869184 | bytes 4194304 | tf_op jit(solution)/shard_map/pixel_rows/pallas_call | solution.py:305
  28.4 3.1 %collective-permute-done.4.far = bf16[512,256]{1,0:T(8,128)(2,1)S(1)} collective-permute-done((bf16[512,256]{1,0:T(8,128)(2,1)S(1)}, bf16[512,256]{1,0:T(8,128)(2,1)S(1)}, u32[]{:S(2)}, u32[]{:S(2)}) %collective-permute-start.4) | collective-permute-done | bytes 262176 | tf_op jit(solution)/shard_map/ppermute | solution.py:46
  31.5 0.5 pre_gradient.1.first
  32.0 0.4 collective-permute-start.6
  32.4 2.3 %collective-permute-start.7 = (bf16[512,256]{1,0:T(8,128)(2,1)S(1)}, bf16[512,256]{1,0:T(8,128)(2,1)S(1)}, u32[]{:S(2)}, u32[]{:S(2)}) collective-permute-start(bf16[512,256]{1,0:T(8,128)(2,1)S(1)} %pre_gradient.1.first), channel_id=1, source_target_pairs={{0,1},{1,0},{2,3},{3,2},{4,5},{5,4},{6,7},{7,6},{8,9},{9,8},{10,11... | collective-permute-start | bytes 786440 | tf_op jit(solution)/shard_map/ppermute | solution.py:46
  34.7 8.4 %collective-permute-done.6.second = bf16[512,256]{1,0:T(8,128)(2,1)S(1)} collective-permute-done((bf16[512,256]{1,0:T(8,128)(2,1)S(1)}, bf16[512,256]{1,0:T(8,128)(2,1)S(1)}, u32[]{:S(2)}, u32[]{:S(2)}) %collective-permute-start.6) | collective-permute-done | bytes 262176 | tf_op jit(solution)/shard_map/ppermute | solution.py:46
  43.2 2.5 %early_product.1 = (f32[1152,256]{1,0:T(8,128)S(1)}, bf16[512,1152]{1,0:T(8,128)(2,1)S(1)}, bf16[512,1152]{1,0:T(8,128)(2,1)S(1)}) custom-call(s32[1]{0:T(128)} %bitcast.1.where.chan.chan_at, bf16[2048,1152]{1,0:T(8,128)(2,1)} %spectra.7, bf16[512,256]{1,0:T(8,128)(2,1)S(1)} %pre_gradient.1.first, bf16[512,256]{1,0:T(8,128)(2,1)S(1)} %collective-permute-done.6.second), custom_call_target="tpu_custom_call" | custom-call | flops 603979776 | bytes 5898240 | tf_op jit(solution)/shard_map/early_product/pallas_call | solution.py:136
  45.8 0.5 more_product.1.before
  46.4 3.2 %collective-permute-done.8.rows = bf16[512,256]{1,0:T(8,128)(2,1)S(1)} collective-permute-done((bf16[512,256]{1,0:T(8,128)(2,1)S(1)}, bf16[512,256]{1,0:T(8,128)(2,1)S(1)}, u32[]{:S(2)}, u32[]{:S(2)}) %collective-permute-start.8) | collective-permute-done | bytes 262176 | tf_op jit(solution)/shard_map/ppermute | solution.py:46
  49.5 0.6 late_product.1
  50.2 0.5 collective-permute-start.12
  50.8 0.7 %collective-permute-done.9.second = bf16[192,256]{1,0:T(8,128)(2,1)S(1)} collective-permute-done((bf16[192,256]{1,0:T(8,128)(2,1)S(1)}, bf16[192,256]{1,0:T(8,128)(2,1)S(1)}, u32[]{:S(2)}, u32[]{:S(2)}) %collective-permute-start.9) | collective-permute-done | bytes 98336 | tf_op jit(solution)/shard_map/ppermute | solution.py:46
  51.5 1.6 %collective-permute-start.10 = (bf16[192,256]{1,0:T(8,128)(2,1)S(1)}, bf16[192,256]{1,0:T(8,128)(2,1)S(1)}, u32[]{:S(2)}, u32[]{:S(2)}) collective-permute-start(bf16[192,256]{1,0:T(8,128)(2,1)S(1)} %added.9.first), channel_id=1, source_target_pairs={{0,16},{4,20},{8,12},{12,8},{16,0},{20,4},{24,28},{28,24},{1,17},{... | collective-permute-start | bytes 294920 | tf_op jit(solution)/shard_map/ppermute | solution.py:446
  53.1 0.6 collective-permute-start.13
  53.7 1.6 %collective-permute-start.16 = (bf16[192,256]{1,0:T(8,128)(2,1)S(1)}, bf16[192,256]{1,0:T(8,128)(2,1)S(1)}, u32[]{:S(2)}, u32[]{:S(2)}) collective-permute-start(bf16[192,256]{1,0:T(8,128)(2,1)S(1)} %added.15.first), channel_id=1, source_target_pairs={{0,16},{4,20},{8,12},{12,8},{16,0},{20,4},{24,28},{28,24},{1,17},{... | collective-permute-start | bytes 294920 | tf_op jit(solution)/shard_map/ppermute | solution.py:446
  55.3 0.9 %collective-permute-done.10.second = bf16[192,256]{1,0:T(8,128)(2,1)S(1)} collective-permute-done((bf16[192,256]{1,0:T(8,128)(2,1)S(1)}, bf16[192,256]{1,0:T(8,128)(2,1)S(1)}, u32[]{:S(2)}, u32[]{:S(2)}) %collective-permute-start.10) | collective-permute-done | bytes 98336 | tf_op jit(solution)/shard_map/ppermute | solution.py:446
  56.2 1.6 %collective-permute-start.11 = (bf16[192,256]{1,0:T(8,128)(2,1)S(1)}, bf16[192,256]{1,0:T(8,128)(2,1)S(1)}, u32[]{:S(2)}, u32[]{:S(2)}) collective-permute-start(bf16[192,256]{1,0:T(8,128)(2,1)S(1)} %added.10.first), channel_id=1, source_target_pairs={{0,4},{4,0},{8,24},{12,28},{16,20},{20,16},{24,8},{28,12},{1,5},{5... | collective-permute-start | bytes 294920 | tf_op jit(solution)/shard_map/ppermute | solution.py:446
  57.9 1.5 %collective-permute-start.14 = (bf16[192,256]{1,0:T(8,128)(2,1)S(1)}, bf16[192,256]{1,0:T(8,128)(2,1)S(1)}, u32[]{:S(2)}, u32[]{:S(2)}) collective-permute-start(bf16[192,256]{1,0:T(8,128)(2,1)S(1)} %added.13.first), channel_id=1, source_target_pairs={{0,4},{4,0},{8,24},{12,28},{16,20},{20,16},{24,8},{28,12},{1,5},{5... | collective-permute-start | bytes 294920 | tf_op jit(solution)/shard_map/ppermute | solution.py:446
  59.5 1.6 %collective-permute-start.17 = (bf16[192,256]{1,0:T(8,128)(2,1)S(1)}, bf16[192,256]{1,0:T(8,128)(2,1)S(1)}, u32[]{:S(2)}, u32[]{:S(2)}) collective-permute-start(bf16[192,256]{1,0:T(8,128)(2,1)S(1)} %added.16.first), channel_id=1, source_target_pairs={{0,4},{4,0},{8,24},{12,28},{16,20},{20,16},{24,8},{28,12},{1,5},{5... | collective-permute-start | bytes 294920 | tf_op jit(solution)/shard_map/ppermute | solution.py:446
  61.2 1.4 %collective-permute-done.14.second = bf16[192,256]{1,0:T(8,128)(2,1)S(1)} collective-permute-done((bf16[192,256]{1,0:T(8,128)(2,1)S(1)}, bf16[192,256]{1,0:T(8,128)(2,1)S(1)}, u32[]{:S(2)}, u32[]{:S(2)}) %collective-permute-start.14) | collective-permute-done | bytes 98336 | tf_op jit(solution)/shard_map/ppermute | solution.py:446
  62.7 1.5 %collective-permute-done.17.second = bf16[192,256]{1,0:T(8,128)(2,1)S(1)} collective-permute-done((bf16[192,256]{1,0:T(8,128)(2,1)S(1)}, bf16[192,256]{1,0:T(8,128)(2,1)S(1)}, u32[]{:S(2)}, u32[]{:S(2)}) %collective-permute-start.17) | collective-permute-done | bytes 98336 | tf_op jit(solution)/shard_map/ppermute | solution.py:446
  64.2 0.8 %written.2.refs_0_ = f32[1152,256]{1,0:T(8,128)} custom-call(s32[1]{0:T(128)} %bitcast.core, bf16[192,256]{1,0:T(8,128)(2,1)S(1)} %added.11.refs_0_, bf16[192,256]{1,0:T(8,128)(2,1)S(1)} %added.14.refs_1_, bf16[192,256]{1,0:T(8,128)(2,1)S(1)} %added.17.refs_2_), custom_call_target="tpu_custom_call" | custom-call | tf_op jit(solution)/shard_map/written/pallas_call | solution.py:406
  65.1 0.4 collective-permute-done.20.refs_3_
  65.5 0.8 %written.3 = f32[1152,256]{1,0:T(8,128)} custom-call(s32[1]{0:T(128)} %bitcast.core, f32[1152,256]{1,0:T(8,128)} %written.2.refs_0_, bf16[192,256]{1,0:T(8,128)(2,1)S(1)} %collective-permute-done.18.refs_1_, bf16[192,256]{1,0:T(8,128)(2,1)S(1)} %collective-permute-done.19.refs_2_, ...), custom_call_target="tpu_custom_call", output_to_operand_aliasing={{}: (1, {})} | custom-call | tf_op jit(solution)/shard_map/written/pallas_call | solution.py:406
  (45 shorter events, 1.1 us)
Async XLA Ops:
  0.0 8.9 %collective-permute-start = (s32[2048]{0:T(1024)}, s32[2048]{0:T(1024)S(1)}, u32[]{:S(2)}, u32[]{:S(2)}) collective-permute-start(s32[2048]{0:T(1024)} %wanted.1), channel_id=1, source_target_pairs={{0,4},{4,0},{1,5},{5,1},{2,6},{6,2},{3,7},{7,3},{8,12},{12,8},{9,1... | collective-permute-start | bytes 24584 | tf_op jit(solution)/shard_map/ppermute | solution.py:46
  3.9 5.0 %collective-permute-start.1 = (bf16[128,256]{1,0:T(8,128)(2,1)S(1)}, bf16[128,256]{1,0:T(8,128)(2,1)S(1)}, u32[]{:S(2)}, u32[]{:S(2)}) collective-permute-start(bf16[128,256]{1,0:T(8,128)(2,1)S(1)} %slice_select_fusion), channel_id=1, source_target_pairs={{0,4},{4,0},{1,5},{5,1},{2,6},{6,2},{3,7},{7,3},{8,12},{12,8},{9,1... | collective-permute-start | bytes 196616 | tf_op jit(solution)/shard_map/ppermute | solution.py:23
  3.9 4.9 %copy-start.5 = (s32[8,4096]{1,0:T(8,128)S(1)}, s32[8,4096]{1,0:T(8,128)}, u32[]{:S(2)}) copy-start(s32[8,4096]{1,0:T(8,128)} %param.14) | copy-start | bytes 393220
  3.9 5.0 %copy-start = (bf16[1152,256]{1,0:T(8,128)(2,1)S(1)}, bf16[1152,256]{1,0:T(8,128)(2,1)}, u32[]{:S(2)}) copy-start(bf16[1152,256]{1,0:T(8,128)(2,1)} %weight.5) | copy-start | bytes 1769476
  4.0 5.0 %copy-start.4 = (f32[8,256]{1,0:T(8,128)S(1)}, f32[8,256]{1,0:T(8,128)}, u32[]{:S(2)}) copy-start(f32[8,256]{1,0:T(8,128)} %mixing.3) | copy-start | bytes 24580
  6.7 9.6 %collective-permute-start.2 = (bf16[512,256]{1,0:T(8,128)(2,1)}, bf16[512,256]{1,0:T(8,128)(2,1)S(1)}, u32[]{:S(2)}, u32[]{:S(2)}) collective-permute-start(bf16[512,256]{1,0:T(8,128)(2,1)} %project.1), channel_id=1, source_target_pairs={{0,1},{1,0},{2,3},{3,2},{4,5},{5,4},{6,7},{7,6},{8,9},{9,8},{10,11... | collective-permute-start | bytes 786440 | tf_op jit(solution)/shard_map/ppermute | solution.py:46
  8.9 13.1 %copy-start.3 = (s32[2048]{0:T(1024)S(1)}, s32[2048]{0:T(1024)}, u32[]{:S(2)}) copy-start(s32[2048]{0:T(1024)} %wanted.1) | copy-start | bytes 24580
  16.4 11.9 %collective-permute-start.3 = (bf16[512,256]{1,0:T(8,128)(2,1)S(1)}, bf16[512,256]{1,0:T(8,128)(2,1)S(1)}, u32[]{:S(2)}, u32[]{:S(2)}) collective-permute-start(bf16[512,256]{1,0:T(8,128)(2,1)S(1)} %get-tuple-element.32), channel_id=1, source_target_pairs={{0,1},{1,0},{2,3},{3,2},{4,5},{5,4},{6,7},{7,6},{8,9},{9,8},{10,11... | collective-permute-start | bytes 786440 | tf_op jit(solution)/shard_map/ppermute | solution.py:46
  17.3 14.1 %collective-permute-start.4 = (bf16[512,256]{1,0:T(8,128)(2,1)S(1)}, bf16[512,256]{1,0:T(8,128)(2,1)S(1)}, u32[]{:S(2)}, u32[]{:S(2)}) collective-permute-start(bf16[512,256]{1,0:T(8,128)(2,1)S(1)} %add_convert_fusion), channel_id=1, source_target_pairs={{0,3},{1,2},{2,1},{3,0},{4,7},{5,6},{6,5},{7,4},{8,11},{9,10},{10,... | collective-permute-start | bytes 786440 | tf_op jit(solution)/shard_map/ppermute | solution.py:46
  20.5 10.9 %collective-permute-start.5 = (bf16[512,256]{1,0:T(8,128)(2,1)S(1)}, bf16[512,256]{1,0:T(8,128)(2,1)S(1)}, u32[]{:S(2)}, u32[]{:S(2)}) collective-permute-start(bf16[512,256]{1,0:T(8,128)(2,1)S(1)} %get-tuple-element.35), channel_id=1, source_target_pairs={{0,4},{4,0},{1,5},{5,1},{2,6},{6,2},{3,7},{7,3},{8,12},{12,8},{9,1... | collective-permute-start | bytes 786440 | tf_op jit(solution)/shard_map/ppermute | solution.py:46
  22.1 9.4 %copy-start.1 = (s32[2048,1]{0,1:T(1,128)S(1)}, s32[2048,1]{0,1:T(1,128)}, u32[]{:S(2)}) copy-start(s32[2048,1]{0,1:T(1,128)} %param.10) | copy-start | bytes 24580
  22.1 9.4 %copy-start.2 = (f32[2048]{0:T(1024)S(1)}, f32[2048]{0:T(1024)}, u32[]{:S(2)}) copy-start(f32[2048]{0:T(1024)} %param.12) | copy-start | bytes 24580
  32.0 11.1 %collective-permute-start.6 = (bf16[512,256]{1,0:T(8,128)(2,1)S(1)}, bf16[512,256]{1,0:T(8,128)(2,1)S(1)}, u32[]{:S(2)}, u32[]{:S(2)}) collective-permute-start(bf16[512,256]{1,0:T(8,128)(2,1)S(1)} %pre_gradient.1.first), channel_id=1, source_target_pairs={{0,3},{1,2},{2,1},{3,0},{4,7},{5,6},{6,5},{7,4},{8,11},{9,10},{10,... | collective-permute-start | bytes 786440 | tf_op jit(solution)/shard_map/ppermute | solution.py:46
  32.4 13.4 %collective-permute-start.7 = (bf16[512,256]{1,0:T(8,128)(2,1)S(1)}, bf16[512,256]{1,0:T(8,128)(2,1)S(1)}, u32[]{:S(2)}, u32[]{:S(2)}) collective-permute-start(bf16[512,256]{1,0:T(8,128)(2,1)S(1)} %pre_gradient.1.first), channel_id=1, source_target_pairs={{0,1},{1,0},{2,3},{3,2},{4,5},{5,4},{6,7},{7,6},{8,9},{9,8},{10,11... | collective-permute-start | bytes 786440 | tf_op jit(solution)/shard_map/ppermute | solution.py:46
  43.1 6.5 %collective-permute-start.8 = (bf16[512,256]{1,0:T(8,128)(2,1)S(1)}, bf16[512,256]{1,0:T(8,128)(2,1)S(1)}, u32[]{:S(2)}, u32[]{:S(2)}) collective-permute-start(bf16[512,256]{1,0:T(8,128)(2,1)S(1)} %collective-permute-done.6.second), channel_id=1, source_target_pairs={{0,1},{1,0},{2,3},{3,2},{4,5},{5,4},{6,7},{7,6},{8,9},{9,8},{10,11... | collective-permute-start | bytes 786440 | tf_op jit(solution)/shard_map/ppermute | solution.py:46
  50.1 1.4 %collective-permute-start.9 = (bf16[192,256]{1,0:T(8,128)(2,1)S(1)}, bf16[192,256]{1,0:T(8,128)(2,1)S(1)}, u32[]{:S(2)}, u32[]{:S(2)}) collective-permute-start(bf16[192,256]{1,0:T(8,128)(2,1)S(1)} %get-tuple-element.40), channel_id=1, source_target_pairs={{0,8},{8,0},{16,24},{24,16},{1,9},{9,1},{17,25},{25,17},{2,10},{10... | collective-permute-start | bytes 294920 | tf_op jit(solution)/shard_map/ppermute | solution.py:46
  50.2 2.9 %collective-permute-start.12 = (bf16[192,256]{1,0:T(8,128)(2,1)S(1)}, bf16[192,256]{1,0:T(8,128)(2,1)S(1)}, u32[]{:S(2)}, u32[]{:S(2)}) collective-permute-start(bf16[192,256]{1,0:T(8,128)(2,1)S(1)} %get-tuple-element.42), channel_id=1, source_target_pairs={{0,8},{8,0},{16,24},{24,16},{1,9},{9,1},{17,25},{25,17},{2,10},{10... | collective-permute-start | bytes 294920 | tf_op jit(solution)/shard_map/ppermute | solution.py:46
  50.7 3.0 %collective-permute-start.15 = (bf16[192,256]{1,0:T(8,128)(2,1)S(1)}, bf16[192,256]{1,0:T(8,128)(2,1)S(1)}, u32[]{:S(2)}, u32[]{:S(2)}) collective-permute-start(bf16[192,256]{1,0:T(8,128)(2,1)S(1)} %get-tuple-element.44), channel_id=1, source_target_pairs={{0,8},{8,0},{16,24},{24,16},{1,9},{9,1},{17,25},{25,17},{2,10},{10... | collective-permute-start | bytes 294920 | tf_op jit(solution)/shard_map/ppermute | solution.py:46
  51.5 4.7 %collective-permute-start.10 = (bf16[192,256]{1,0:T(8,128)(2,1)S(1)}, bf16[192,256]{1,0:T(8,128)(2,1)S(1)}, u32[]{:S(2)}, u32[]{:S(2)}) collective-permute-start(bf16[192,256]{1,0:T(8,128)(2,1)S(1)} %added.9.first), channel_id=1, source_target_pairs={{0,16},{4,20},{8,12},{12,8},{16,0},{20,4},{24,28},{28,24},{1,17},{... | collective-permute-start | bytes 294920 | tf_op jit(solution)/shard_map/ppermute | solution.py:446
  53.1 4.8 %collective-permute-start.13 = (bf16[192,256]{1,0:T(8,128)(2,1)S(1)}, bf16[192,256]{1,0:T(8,128)(2,1)S(1)}, u32[]{:S(2)}, u32[]{:S(2)}) collective-permute-start(bf16[192,256]{1,0:T(8,128)(2,1)S(1)} %added.12.first), channel_id=1, source_target_pairs={{0,16},{4,20},{8,12},{12,8},{16,0},{20,4},{24,28},{28,24},{1,17},{... | collective-permute-start | bytes 294920 | tf_op jit(solution)/shard_map/ppermute | solution.py:446
  53.7 5.7 %collective-permute-start.16 = (bf16[192,256]{1,0:T(8,128)(2,1)S(1)}, bf16[192,256]{1,0:T(8,128)(2,1)S(1)}, u32[]{:S(2)}, u32[]{:S(2)}) collective-permute-start(bf16[192,256]{1,0:T(8,128)(2,1)S(1)} %added.15.first), channel_id=1, source_target_pairs={{0,16},{4,20},{8,12},{12,8},{16,0},{20,4},{24,28},{28,24},{1,17},{... | collective-permute-start | bytes 294920 | tf_op jit(solution)/shard_map/ppermute | solution.py:446
  56.2 4.8 %collective-permute-start.11 = (bf16[192,256]{1,0:T(8,128)(2,1)S(1)}, bf16[192,256]{1,0:T(8,128)(2,1)S(1)}, u32[]{:S(2)}, u32[]{:S(2)}) collective-permute-start(bf16[192,256]{1,0:T(8,128)(2,1)S(1)} %added.10.first), channel_id=1, source_target_pairs={{0,4},{4,0},{8,24},{12,28},{16,20},{20,16},{24,8},{28,12},{1,5},{5... | collective-permute-start | bytes 294920 | tf_op jit(solution)/shard_map/ppermute | solution.py:446
  57.9 4.7 %collective-permute-start.14 = (bf16[192,256]{1,0:T(8,128)(2,1)S(1)}, bf16[192,256]{1,0:T(8,128)(2,1)S(1)}, u32[]{:S(2)}, u32[]{:S(2)}) collective-permute-start(bf16[192,256]{1,0:T(8,128)(2,1)S(1)} %added.13.first), channel_id=1, source_target_pairs={{0,4},{4,0},{8,24},{12,28},{16,20},{20,16},{24,8},{28,12},{1,5},{5... | collective-permute-start | bytes 294920 | tf_op jit(solution)/shard_map/ppermute | solution.py:446
  59.5 4.7 %collective-permute-start.17 = (bf16[192,256]{1,0:T(8,128)(2,1)S(1)}, bf16[192,256]{1,0:T(8,128)(2,1)S(1)}, u32[]{:S(2)}, u32[]{:S(2)}) collective-permute-start(bf16[192,256]{1,0:T(8,128)(2,1)S(1)} %added.16.first), channel_id=1, source_target_pairs={{0,4},{4,0},{8,24},{12,28},{16,20},{20,16},{24,8},{28,12},{1,5},{5... | collective-permute-start | bytes 294920 | tf_op jit(solution)/shard_map/ppermute | solution.py:446
  61.1 4.0 %collective-permute-start.18 = (bf16[192,256]{1,0:T(8,128)(2,1)S(1)}, bf16[192,256]{1,0:T(8,128)(2,1)S(1)}, u32[]{:S(2)}, u32[]{:S(2)}) collective-permute-start(bf16[192,256]{1,0:T(8,128)(2,1)S(1)} %added.11.refs_0_), channel_id=1, source_target_pairs={{0,8},{8,0},{16,24},{24,16},{1,9},{9,1},{17,25},{25,17},{2,10},{10... | collective-permute-start | bytes 294920 | tf_op jit(solution)/shard_map/ppermute | solution.py:46
  62.6 2.5 %collective-permute-start.19 = (bf16[192,256]{1,0:T(8,128)(2,1)S(1)}, bf16[192,256]{1,0:T(8,128)(2,1)S(1)}, u32[]{:S(2)}, u32[]{:S(2)}) collective-permute-start(bf16[192,256]{1,0:T(8,128)(2,1)S(1)} %added.14.refs_1_), channel_id=1, source_target_pairs={{0,8},{8,0},{16,24},{24,16},{1,9},{9,1},{17,25},{25,17},{2,10},{10... | collective-permute-start | bytes 294920 | tf_op jit(solution)/shard_map/ppermute | solution.py:46
  64.2 1.4 %collective-permute-start.20 = (bf16[192,256]{1,0:T(8,128)(2,1)S(1)}, bf16[192,256]{1,0:T(8,128)(2,1)S(1)}, u32[]{:S(2)}, u32[]{:S(2)}) collective-permute-start(bf16[192,256]{1,0:T(8,128)(2,1)S(1)} %added.17.refs_2_), channel_id=1, source_target_pairs={{0,8},{8,0},{16,24},{24,16},{1,9},{9,1},{17,25},{25,17},{2,10},{10... | collective-permute-start | bytes 294920 | tf_op jit(solution)/shard_map/ppermute | solution.py:46

commit v26 on v22

--- a/solution.py
+++ b/solution.py
@@ -435,6 +435,22 @@
         compiler_params=memory(16),
         name="added",
     )(first, second)
+
+
+def hand_on_kernel(value, out):
+    out[...] = value[...]
+
+
+def handed_on(value):
+    spec = pl.BlockSpec(memory_space=pltpu.VMEM)
+    return pl.pallas_call(
+        hand_on_kernel,
+        out_shape=jax.ShapeDtypeStruct(value.shape, value.dtype),
+        in_specs=[spec],
+        out_specs=spec,
+        compiler_params=memory(16),
+        name="handed_on",
+    )(value)
 
 
 def sum_over_panels(core, parts, received):
@@ -487,7 +503,7 @@
         mine = answers = jnp.take(answers.reshape(tile_count * capacity, -1), slot_index, axis=0)
     grads = pre_gradient(tile, chan, keep, near, far, pix_tile, foot_weight, mine, answers)
 
-    across = swap(grads, "chan", 3)
+    across = swap(handed_on(grads), "chan", 3)
     beside = swap(grads, "chan", 1)
     last = swap(across, "chan", 1)
     early, held, held_last = early_product(spectra, chan, grads, across)

time: 66.2 us -> 66.3 us (level)
  no operation moved by 1% of the time
where the time goes in v26:
time: 66.3 us; the launch traced here: 66.1 us
  waiting for transfers between devices  22.7 us (34%)
  Pallas kernels  22.4 us (34%)
  starting transfers between devices  19.6 us (30%)
  other arithmetic  0.98 us (1%)
    ppermute x12, waiting for transfers between devices, swap(): return lax.ppermute(value, axis, [(i, i ^ bit) for i in range(size)])  16.1 us
    ppermute x12, starting transfers between devices, swap(): return lax.ppermute(value, axis, [(i, i ^ bit) for i in range(size)])  14.2 us
    pallas_call x2, Pallas kernels, pixel_rows(): pl.pallas_call(functools.partial(pixel_kernel, count, bits, stride), out_...  13.7 us
    ppermute x4, waiting for transfers between devices, sum_over_panels(): parts = [added(part, lax.ppermute(part, both, perm)) for part in parts]  6.56 us
    ppermute x4, starting transfers between devices, sum_over_panels(): parts = [added(part, lax.ppermute(part, both, perm)) for part in parts]  5.33 us
    pallas_call x1, Pallas kernels, project(): pl.pallas_call(functools.partial(project_kernel, bits), out_shape=(jax.Sh...  2.74 us
    pallas_call x1, Pallas kernels, early_product(): pl.pallas_call(early_kernel, out_shape=(jax.ShapeDtypeStruct((depth, widt...  2.49 us
    pallas_call x2, Pallas kernels, written(): pl.pallas_call(functools.partial(write_kernel, other), out_shape=jax.Shap...  1.7 us
  transfers between devices with their start and end apart: 17, of which 9 were waited for; matrix products, arithmetic and copies ran while one was open for 1% of the time, Pallas kernels for 31%

profile of v26, /device:TPU:0, one launch (start us, length us, event | category | flops | bytes accessed | tf_op | source)
XLA Modules:
  0.0 66.1 jit_solution(1127906324402030427)
XLA Ops:
  0.0 3.0 %collective-permute-start = (s32[2048]{0:T(1024)}, s32[2048]{0:T(1024)S(1)}, u32[]{:S(2)}, u32[]{:S(2)}) collective-permute-start(s32[2048]{0:T(1024)} %wanted.1), channel_id=1, source_target_pairs={{0,4},{4,0},{1,5},{5,1},{2,6},{6,2},{3,7},{7,3},{8,12},{12,8},{9,1... | collective-permute-start | bytes 24584 | tf_op jit(solution)/shard_map/ppermute | solution.py:45
  3.0 0.9 %slice_select_fusion = bf16[128,256]{1,0:T(8,128)(2,1)S(1)} fusion(bf16[4096,256]{1,0:T(8,128)(2,1)} %cotangent.3, pred[]{:T(512)S(6)} %eq.3), kind=kLoop, calls=%fused_computation.5 | loop fusion | flops 32768 | bytes 196609 | tf_op jit(solution)/shard_map/jit(_where)/select_n | solution.py:22
  4.0 2.7 %project.1 = bf16[512,256]{1,0:T(8,128)(2,1)} custom-call(s32[1]{0:T(128)} %bitcast.1.where.chan.chan_at, bf16[2048,1152]{1,0:T(8,128)(2,1)} %spectra.7, bf16[1152,256]{1,0:T(8,128)(2,1)} %weight.5), custom_call_target="tpu_custom_call" | custom-call | flops 301989888 | bytes 2031616 | tf_op jit(solution)/shard_map/project/pallas_call | solution.py:88
  6.7 2.1 %collective-permute-start.2 = (bf16[512,256]{1,0:T(8,128)(2,1)}, bf16[512,256]{1,0:T(8,128)(2,1)S(1)}, u32[]{:S(2)}, u32[]{:S(2)}) collective-permute-start(bf16[512,256]{1,0:T(8,128)(2,1)} %project.1), channel_id=1, source_target_pairs={{0,1},{1,0},{2,3},{3,2},{4,5},{5,4},{6,7},{7,6},{8,9},{9,8},{10,11... | collective-permute-start | bytes 786440 | tf_op jit(solution)/shard_map/ppermute | solution.py:45
  8.9 7.4 %pixel_rows.2 = (bf16[512,256]{1,0:T(8,128)(2,1)S(1)}, bf16[512,256]{1,0:T(8,128)(2,1)S(1)}, bf16[512,256]{1,0:T(8,128)(2,1)S(1)}) custom-call(s32[1]{0:T(128)} %bitcast.1.where.chan.chan_at, s32[16384]{0:T(1024)S(1)} %bitcast.9, s32[2048]{0:T(1024)S(1)} %collective-permute-done.wanted, bf16[4096,256]{1,0:T(8,128)(2,1)} %cotangent.3, ...), custom_call_target="tpu_custom_call" | custom-call | flops 17179869184 | bytes 4194304 | tf_op jit(solution)/shard_map/pixel_rows/pallas_call | solution.py:304
  16.4 0.9 %collective-permute-start.3 = (bf16[512,256]{1,0:T(8,128)(2,1)S(1)}, bf16[512,256]{1,0:T(8,128)(2,1)S(1)}, u32[]{:S(2)}, u32[]{:S(2)}) collective-permute-start(bf16[512,256]{1,0:T(8,128)(2,1)S(1)} %get-tuple-element.30), channel_id=1, source_target_pairs={{0,1},{1,0},{2,3},{3,2},{4,5},{5,4},{6,7},{7,6},{8,9},{9,8},{10,11... | collective-permute-start | bytes 786440 | tf_op jit(solution)/shard_map/ppermute | solution.py:45
  17.3 3.2 %collective-permute-start.4 = (bf16[512,256]{1,0:T(8,128)(2,1)S(1)}, bf16[512,256]{1,0:T(8,128)(2,1)S(1)}, u32[]{:S(2)}, u32[]{:S(2)}) collective-permute-start(bf16[512,256]{1,0:T(8,128)(2,1)S(1)} %add_convert_fusion), channel_id=1, source_target_pairs={{0,3},{1,2},{2,1},{3,0},{4,7},{5,6},{6,5},{7,4},{8,11},{9,10},{10,... | collective-permute-start | bytes 786440 | tf_op jit(solution)/shard_map/ppermute | solution.py:45
  20.5 1.5 %collective-permute-start.5 = (bf16[512,256]{1,0:T(8,128)(2,1)S(1)}, bf16[512,256]{1,0:T(8,128)(2,1)S(1)}, u32[]{:S(2)}, u32[]{:S(2)}) collective-permute-start(bf16[512,256]{1,0:T(8,128)(2,1)S(1)} %get-tuple-element.33), channel_id=1, source_target_pairs={{0,4},{4,0},{1,5},{5,1},{2,6},{6,2},{3,7},{7,3},{8,12},{12,8},{9,1... | collective-permute-start | bytes 786440 | tf_op jit(solution)/shard_map/ppermute | solution.py:45
  22.1 6.3 %pixel_rows.3 = (bf16[512,256]{1,0:T(8,128)(2,1)S(1)}, bf16[512,256]{1,0:T(8,128)(2,1)S(1)}) custom-call(s32[1]{0:T(128)} %bitcast.3.where, s32[16384]{0:T(1024)S(1)} %bitcast.10, s32[2048]{0:T(1024)S(1)} %copy-done.3, bf16[4096,256]{1,0:T(8,128)(2,1)} %cotangent.3, bf16[128,256]{1,0:T(8,128)(2,1)S(1)} %collective-permute-done.1.above.below, ...), custom_call_target="tpu_custom_call" | custom-call | flops 17179869184 | bytes 4194304 | tf_op jit(solution)/shard_map/pixel_rows/pallas_call | solution.py:304
  28.4 3.1 %collective-permute-done.4.far = bf16[512,256]{1,0:T(8,128)(2,1)S(1)} collective-permute-done((bf16[512,256]{1,0:T(8,128)(2,1)S(1)}, bf16[512,256]{1,0:T(8,128)(2,1)S(1)}, u32[]{:S(2)}, u32[]{:S(2)}) %collective-permute-start.4) | collective-permute-done | bytes 262176 | tf_op jit(solution)/shard_map/ppermute | solution.py:45
  31.5 0.5 pre_gradient.1.value.first
  32.0 0.4 collective-permute-start.6
  32.4 2.3 %collective-permute-start.7 = (bf16[512,256]{1,0:T(8,128)(2,1)S(1)}, bf16[512,256]{1,0:T(8,128)(2,1)S(1)}, u32[]{:S(2)}, u32[]{:S(2)}) collective-permute-start(bf16[512,256]{1,0:T(8,128)(2,1)S(1)} %pre_gradient.1.value.first), channel_id=1, source_target_pairs={{0,1},{1,0},{2,3},{3,2},{4,5},{5,4},{6,7},{7,6},{8,9},{9,8},{10,11... | collective-permute-start | bytes 786440 | tf_op jit(solution)/shard_map/ppermute | solution.py:45
  34.7 8.4 %collective-permute-done.6.second = bf16[512,256]{1,0:T(8,128)(2,1)S(1)} collective-permute-done((bf16[512,256]{1,0:T(8,128)(2,1)S(1)}, bf16[512,256]{1,0:T(8,128)(2,1)S(1)}, u32[]{:S(2)}, u32[]{:S(2)}) %collective-permute-start.6) | collective-permute-done | bytes 262176 | tf_op jit(solution)/shard_map/ppermute | solution.py:45
  43.1 0.1 collective-permute-start.8
  43.2 2.5 %early_product.1 = (f32[1152,256]{1,0:T(8,128)S(1)}, bf16[512,1152]{1,0:T(8,128)(2,1)S(1)}, bf16[512,1152]{1,0:T(8,128)(2,1)S(1)}) custom-call(s32[1]{0:T(128)} %bitcast.1.where.chan.chan_at, bf16[2048,1152]{1,0:T(8,128)(2,1)} %spectra.7, bf16[512,256]{1,0:T(8,128)(2,1)S(1)} %pre_gradient.1.value.first, bf16[512,256]{1,0:T(8,128)(2,1)S(1)} %collective-permute-done.6.second), custom_call_target="tpu_custom_call" | custom-call | flops 603979776 | bytes 5898240 | tf_op jit(solution)/shard_map/early_product/pallas_call | solution.py:135
  45.7 0.1 collective-permute-done.7.rows
  45.9 0.5 more_product.1.before
  46.4 3.2 %collective-permute-done.8.rows = bf16[512,256]{1,0:T(8,128)(2,1)S(1)} collective-permute-done((bf16[512,256]{1,0:T(8,128)(2,1)S(1)}, bf16[512,256]{1,0:T(8,128)(2,1)S(1)}, u32[]{:S(2)}, u32[]{:S(2)}) %collective-permute-start.8) | collective-permute-done | bytes 262176 | tf_op jit(solution)/shard_map/ppermute | solution.py:45
  49.6 0.6 late_product.1
  50.2 0.5 collective-permute-start.12
  50.7 0.9 %collective-permute-done.9.second = bf16[288,256]{1,0:T(8,128)(2,1)S(1)} collective-permute-done((bf16[288,256]{1,0:T(8,128)(2,1)S(1)}, bf16[288,256]{1,0:T(8,128)(2,1)S(1)}, u32[]{:S(2)}, u32[]{:S(2)}) %collective-permute-start.9) | collective-permute-done | bytes 147488 | tf_op jit(solution)/shard_map/ppermute | solution.py:45
  51.6 1.6 %collective-permute-start.10 = (bf16[288,256]{1,0:T(8,128)(2,1)S(1)}, bf16[288,256]{1,0:T(8,128)(2,1)S(1)}, u32[]{:S(2)}, u32[]{:S(2)}) collective-permute-start(bf16[288,256]{1,0:T(8,128)(2,1)S(1)} %added.6.first), channel_id=1, source_target_pairs={{0,16},{4,20},{8,12},{12,8},{16,0},{20,4},{24,28},{28,24},{1,17},{... | collective-permute-start | bytes 442376 | tf_op jit(solution)/shard_map/ppermute | solution.py:461
  53.2 0.6 collective-permute-start.13
  53.8 3.0 %collective-permute-done.10.second = bf16[288,256]{1,0:T(8,128)(2,1)S(1)} collective-permute-done((bf16[288,256]{1,0:T(8,128)(2,1)S(1)}, bf16[288,256]{1,0:T(8,128)(2,1)S(1)}, u32[]{:S(2)}, u32[]{:S(2)}) %collective-permute-start.10) | collective-permute-done | bytes 147488 | tf_op jit(solution)/shard_map/ppermute | solution.py:461
  56.9 1.6 %collective-permute-start.11 = (bf16[288,256]{1,0:T(8,128)(2,1)S(1)}, bf16[288,256]{1,0:T(8,128)(2,1)S(1)}, u32[]{:S(2)}, u32[]{:S(2)}) collective-permute-start(bf16[288,256]{1,0:T(8,128)(2,1)S(1)} %added.7.first), channel_id=1, source_target_pairs={{0,4},{4,0},{8,24},{12,28},{16,20},{20,16},{24,8},{28,12},{1,5},{5... | collective-permute-start | bytes 442376 | tf_op jit(solution)/shard_map/ppermute | solution.py:461
  58.5 1.5 %collective-permute-start.14 = (bf16[288,256]{1,0:T(8,128)(2,1)S(1)}, bf16[288,256]{1,0:T(8,128)(2,1)S(1)}, u32[]{:S(2)}, u32[]{:S(2)}) collective-permute-start(bf16[288,256]{1,0:T(8,128)(2,1)S(1)} %added.10.first), channel_id=1, source_target_pairs={{0,4},{4,0},{8,24},{12,28},{16,20},{20,16},{24,8},{28,12},{1,5},{5... | collective-permute-start | bytes 442376 | tf_op jit(solution)/shard_map/ppermute | solution.py:461
  60.1 2.0 %collective-permute-done.11.second = bf16[288,256]{1,0:T(8,128)(2,1)S(1)} collective-permute-done((bf16[288,256]{1,0:T(8,128)(2,1)S(1)}, bf16[288,256]{1,0:T(8,128)(2,1)S(1)}, u32[]{:S(2)}, u32[]{:S(2)}) %collective-permute-start.11) | collective-permute-done | bytes 147488 | tf_op jit(solution)/shard_map/ppermute | solution.py:461
  62.2 1.6 %collective-permute-done.14.second = bf16[288,256]{1,0:T(8,128)(2,1)S(1)} collective-permute-done((bf16[288,256]{1,0:T(8,128)(2,1)S(1)}, bf16[288,256]{1,0:T(8,128)(2,1)S(1)}, u32[]{:S(2)}, u32[]{:S(2)}) %collective-permute-start.14) | collective-permute-done | bytes 147488 | tf_op jit(solution)/shard_map/ppermute | solution.py:461
  63.9 0.9 %written.2.refs_0_ = f32[1152,256]{1,0:T(8,128)} custom-call(s32[1]{0:T(128)} %bitcast.core, bf16[288,256]{1,0:T(8,128)(2,1)S(1)} %added.8.refs_0_, bf16[288,256]{1,0:T(8,128)(2,1)S(1)} %added.11.refs_1_), custom_call_target="tpu_custom_call" | custom-call | tf_op jit(solution)/shard_map/written/pallas_call | solution.py:404
  64.7 0.5 collective-permute-done.16.refs_2_
  65.2 0.8 %written.3 = f32[1152,256]{1,0:T(8,128)} custom-call(s32[1]{0:T(128)} %bitcast.core, f32[1152,256]{1,0:T(8,128)} %written.2.refs_0_, bf16[288,256]{1,0:T(8,128)(2,1)S(1)} %collective-permute-done.15.refs_1_, bf16[288,256]{1,0:T(8,128)(2,1)S(1)} %collective-permute-done.16.refs_2_), custom_call_target="tpu_custom_call", output_to_operand_aliasing={{}: (1, {})} | custom-call | tf_op jit(solution)/shard_map/written/pallas_call | solution.py:404
  (35 shorter events, 0.7 us)
Async XLA Ops:
  0.0 8.9 %collective-permute-start = (s32[2048]{0:T(1024)}, s32[2048]{0:T(1024)S(1)}, u32[]{:S(2)}, u32[]{:S(2)}) collective-permute-start(s32[2048]{0:T(1024)} %wanted.1), channel_id=1, source_target_pairs={{0,4},{4,0},{1,5},{5,1},{2,6},{6,2},{3,7},{7,3},{8,12},{12,8},{9,1... | collective-permute-start | bytes 24584 | tf_op jit(solution)/shard_map/ppermute | solution.py:45
  3.9 5.0 %collective-permute-start.1 = (bf16[128,256]{1,0:T(8,128)(2,1)S(1)}, bf16[128,256]{1,0:T(8,128)(2,1)S(1)}, u32[]{:S(2)}, u32[]{:S(2)}) collective-permute-start(bf16[128,256]{1,0:T(8,128)(2,1)S(1)} %slice_select_fusion), channel_id=1, source_target_pairs={{0,4},{4,0},{1,5},{5,1},{2,6},{6,2},{3,7},{7,3},{8,12},{12,8},{9,1... | collective-permute-start | bytes 196616 | tf_op jit(solution)/shard_map/ppermute | solution.py:22
  3.9 4.9 %copy-start.5 = (s32[8,4096]{1,0:T(8,128)S(1)}, s32[8,4096]{1,0:T(8,128)}, u32[]{:S(2)}) copy-start(s32[8,4096]{1,0:T(8,128)} %param.14) | copy-start | bytes 393220
  3.9 5.0 %copy-start = (bf16[1152,256]{1,0:T(8,128)(2,1)S(1)}, bf16[1152,256]{1,0:T(8,128)(2,1)}, u32[]{:S(2)}) copy-start(bf16[1152,256]{1,0:T(8,128)(2,1)} %weight.5) | copy-start | bytes 1769476
  4.0 5.0 %copy-start.4 = (f32[8,256]{1,0:T(8,128)S(1)}, f32[8,256]{1,0:T(8,128)}, u32[]{:S(2)}) copy-start(f32[8,256]{1,0:T(8,128)} %mixing.3) | copy-start | bytes 24580
  6.7 9.6 %collective-permute-start.2 = (bf16[512,256]{1,0:T(8,128)(2,1)}, bf16[512,256]{1,0:T(8,128)(2,1)S(1)}, u32[]{:S(2)}, u32[]{:S(2)}) collective-permute-start(bf16[512,256]{1,0:T(8,128)(2,1)} %project.1), channel_id=1, source_target_pairs={{0,1},{1,0},{2,3},{3,2},{4,5},{5,4},{6,7},{7,6},{8,9},{9,8},{10,11... | collective-permute-start | bytes 786440 | tf_op jit(solution)/shard_map/ppermute | solution.py:45
  8.9 13.1 %copy-start.3 = (s32[2048]{0:T(1024)S(1)}, s32[2048]{0:T(1024)}, u32[]{:S(2)}) copy-start(s32[2048]{0:T(1024)} %wanted.1) | copy-start | bytes 24580
  16.4 11.9 %collective-permute-start.3 = (bf16[512,256]{1,0:T(8,128)(2,1)S(1)}, bf16[512,256]{1,0:T(8,128)(2,1)S(1)}, u32[]{:S(2)}, u32[]{:S(2)}) collective-permute-start(bf16[512,256]{1,0:T(8,128)(2,1)S(1)} %get-tuple-element.30), channel_id=1, source_target_pairs={{0,1},{1,0},{2,3},{3,2},{4,5},{5,4},{6,7},{7,6},{8,9},{9,8},{10,11... | collective-permute-start | bytes 786440 | tf_op jit(solution)/shard_map/ppermute | solution.py:45
  17.3 14.1 %collective-permute-start.4 = (bf16[512,256]{1,0:T(8,128)(2,1)S(1)}, bf16[512,256]{1,0:T(8,128)(2,1)S(1)}, u32[]{:S(2)}, u32[]{:S(2)}) collective-permute-start(bf16[512,256]{1,0:T(8,128)(2,1)S(1)} %add_convert_fusion), channel_id=1, source_target_pairs={{0,3},{1,2},{2,1},{3,0},{4,7},{5,6},{6,5},{7,4},{8,11},{9,10},{10,... | collective-permute-start | bytes 786440 | tf_op jit(solution)/shard_map/ppermute | solution.py:45
  20.5 10.9 %collective-permute-start.5 = (bf16[512,256]{1,0:T(8,128)(2,1)S(1)}, bf16[512,256]{1,0:T(8,128)(2,1)S(1)}, u32[]{:S(2)}, u32[]{:S(2)}) collective-permute-start(bf16[512,256]{1,0:T(8,128)(2,1)S(1)} %get-tuple-element.33), channel_id=1, source_target_pairs={{0,4},{4,0},{1,5},{5,1},{2,6},{6,2},{3,7},{7,3},{8,12},{12,8},{9,1... | collective-permute-start | bytes 786440 | tf_op jit(solution)/shard_map/ppermute | solution.py:45
  22.1 9.4 %copy-start.1 = (s32[2048,1]{0,1:T(1,128)S(1)}, s32[2048,1]{0,1:T(1,128)}, u32[]{:S(2)}) copy-start(s32[2048,1]{0,1:T(1,128)} %param.10) | copy-start | bytes 24580
  22.1 9.4 %copy-start.2 = (f32[2048]{0:T(1024)S(1)}, f32[2048]{0:T(1024)}, u32[]{:S(2)}) copy-start(f32[2048]{0:T(1024)} %param.12) | copy-start | bytes 24580
  32.0 11.1 %collective-permute-start.6 = (bf16[512,256]{1,0:T(8,128)(2,1)S(1)}, bf16[512,256]{1,0:T(8,128)(2,1)S(1)}, u32[]{:S(2)}, u32[]{:S(2)}) collective-permute-start(bf16[512,256]{1,0:T(8,128)(2,1)S(1)} %handed_on.1), channel_id=1, source_target_pairs={{0,3},{1,2},{2,1},{3,0},{4,7},{5,6},{6,5},{7,4},{8,11},{9,10},{10,... | collective-permute-start | bytes 786440 | tf_op jit(solution)/shard_map/ppermute | solution.py:45
  32.4 13.4 %collective-permute-start.7 = (bf16[512,256]{1,0:T(8,128)(2,1)S(1)}, bf16[512,256]{1,0:T(8,128)(2,1)S(1)}, u32[]{:S(2)}, u32[]{:S(2)}) collective-permute-start(bf16[512,256]{1,0:T(8,128)(2,1)S(1)} %pre_gradient.1.value.first), channel_id=1, source_target_pairs={{0,1},{1,0},{2,3},{3,2},{4,5},{5,4},{6,7},{7,6},{8,9},{9,8},{10,11... | collective-permute-start | bytes 786440 | tf_op jit(solution)/shard_map/ppermute | solution.py:45
  43.1 6.5 %collective-permute-start.8 = (bf16[512,256]{1,0:T(8,128)(2,1)S(1)}, bf16[512,256]{1,0:T(8,128)(2,1)S(1)}, u32[]{:S(2)}, u32[]{:S(2)}) collective-permute-start(bf16[512,256]{1,0:T(8,128)(2,1)S(1)} %collective-permute-done.6.second), channel_id=1, source_target_pairs={{0,1},{1,0},{2,3},{3,2},{4,5},{5,4},{6,7},{7,6},{8,9},{9,8},{10,11... | collective-permute-start | bytes 786440 | tf_op jit(solution)/shard_map/ppermute | solution.py:45
  50.1 1.4 %collective-permute-start.9 = (bf16[288,256]{1,0:T(8,128)(2,1)S(1)}, bf16[288,256]{1,0:T(8,128)(2,1)S(1)}, u32[]{:S(2)}, u32[]{:S(2)}) collective-permute-start(bf16[288,256]{1,0:T(8,128)(2,1)S(1)} %get-tuple-element.38), channel_id=1, source_target_pairs={{0,8},{8,0},{16,24},{24,16},{1,9},{9,1},{17,25},{25,17},{2,10},{10... | collective-permute-start | bytes 442376 | tf_op jit(solution)/shard_map/ppermute | solution.py:45
  50.2 2.9 %collective-permute-start.12 = (bf16[288,256]{1,0:T(8,128)(2,1)S(1)}, bf16[288,256]{1,0:T(8,128)(2,1)S(1)}, u32[]{:S(2)}, u32[]{:S(2)}) collective-permute-start(bf16[288,256]{1,0:T(8,128)(2,1)S(1)} %get-tuple-element.40), channel_id=1, source_target_pairs={{0,8},{8,0},{16,24},{24,16},{1,9},{9,1},{17,25},{25,17},{2,10},{10... | collective-permute-start | bytes 442376 | tf_op jit(solution)/shard_map/ppermute | solution.py:45
  51.6 5.2 %collective-permute-start.10 = (bf16[288,256]{1,0:T(8,128)(2,1)S(1)}, bf16[288,256]{1,0:T(8,128)(2,1)S(1)}, u32[]{:S(2)}, u32[]{:S(2)}) collective-permute-start(bf16[288,256]{1,0:T(8,128)(2,1)S(1)} %added.6.first), channel_id=1, source_target_pairs={{0,16},{4,20},{8,12},{12,8},{16,0},{20,4},{24,28},{28,24},{1,17},{... | collective-permute-start | bytes 442376 | tf_op jit(solution)/shard_map/ppermute | solution.py:461
  53.2 5.3 %collective-permute-start.13 = (bf16[288,256]{1,0:T(8,128)(2,1)S(1)}, bf16[288,256]{1,0:T(8,128)(2,1)S(1)}, u32[]{:S(2)}, u32[]{:S(2)}) collective-permute-start(bf16[288,256]{1,0:T(8,128)(2,1)S(1)} %added.9.first), channel_id=1, source_target_pairs={{0,16},{4,20},{8,12},{12,8},{16,0},{20,4},{24,28},{28,24},{1,17},{... | collective-permute-start | bytes 442376 | tf_op jit(solution)/shard_map/ppermute | solution.py:461
  56.9 5.2 %collective-permute-start.11 = (bf16[288,256]{1,0:T(8,128)(2,1)S(1)}, bf16[288,256]{1,0:T(8,128)(2,1)S(1)}, u32[]{:S(2)}, u32[]{:S(2)}) collective-permute-start(bf16[288,256]{1,0:T(8,128)(2,1)S(1)} %added.7.first), channel_id=1, source_target_pairs={{0,4},{4,0},{8,24},{12,28},{16,20},{20,16},{24,8},{28,12},{1,5},{5... | collective-permute-start | bytes 442376 | tf_op jit(solution)/shard_map/ppermute | solution.py:461
  58.5 5.2 %collective-permute-start.14 = (bf16[288,256]{1,0:T(8,128)(2,1)S(1)}, bf16[288,256]{1,0:T(8,128)(2,1)S(1)}, u32[]{:S(2)}, u32[]{:S(2)}) collective-permute-start(bf16[288,256]{1,0:T(8,128)(2,1)S(1)} %added.10.first), channel_id=1, source_target_pairs={{0,4},{4,0},{8,24},{12,28},{16,20},{20,16},{24,8},{28,12},{1,5},{5... | collective-permute-start | bytes 442376 | tf_op jit(solution)/shard_map/ppermute | solution.py:461
  62.1 2.6 %collective-permute-start.15 = (bf16[288,256]{1,0:T(8,128)(2,1)S(1)}, bf16[288,256]{1,0:T(8,128)(2,1)S(1)}, u32[]{:S(2)}, u32[]{:S(2)}) collective-permute-start(bf16[288,256]{1,0:T(8,128)(2,1)S(1)} %added.8.refs_0_), channel_id=1, source_target_pairs={{0,8},{8,0},{16,24},{24,16},{1,9},{9,1},{17,25},{25,17},{2,10},{10... | collective-permute-start | bytes 442376 | tf_op jit(solution)/shard_map/ppermute | solution.py:45
  63.8 1.4 %collective-permute-start.16 = (bf16[288,256]{1,0:T(8,128)(2,1)S(1)}, bf16[288,256]{1,0:T(8,128)(2,1)S(1)}, u32[]{:S(2)}, u32[]{:S(2)}) collective-permute-start(bf16[288,256]{1,0:T(8,128)(2,1)S(1)} %added.11.refs_1_), channel_id=1, source_target_pairs={{0,8},{8,0},{16,24},{24,16},{1,9},{9,1},{17,25},{25,17},{2,10},{10... | collective-permute-start | bytes 442376 | tf_op jit(solution)/shard_map/ppermute | solution.py:45

commit v27 on v25

--- a/solution.py
+++ b/solution.py
@@ -11,7 +11,7 @@
 HALO = 128
 MIB = 1024 * 1024
 LARGE = 52
-CHUNKS = 3
+CHUNKS = 4
 
 
 def edges(value, axis, width):

time: 66.6 us -> 67.4 us (1.012)
  starting transfers between devices: 22.9 us -> 25.9 us
  waiting for transfers between devices: 19.7 us -> 17.5 us
    ppermute x6 -> x8, starting transfers between devices: 8.48 us -> 10.5 us  [sum_over_panels(): parts = [added(part, lax.ppermute(part, both, perm)) for part in parts]]
    ppermute x6 -> x8, waiting for transfers between devices: 3.79 us -> 2.1 us  [sum_over_panels(): parts = [added(part, lax.ppermute(part, both, perm)) for part in parts]]
    ppermute x14 -> x16, starting transfers between devices: 14.4 us -> 15.4 us  [swap(): return lax.ppermute(value, axis, [(i, i ^ bit) for i in range(size)])]
    ppermute x14 -> x16, waiting for transfers between devices: 15.9 us -> 15.4 us  [swap(): return lax.ppermute(value, axis, [(i, i ^ bit) for i in range(size)])]
  transfers between devices with their start and end apart: 21 -> 25, of which waited for: 9 -> 8; matrix products, arithmetic and copies ran while one was open for 1% -> 1% of each run, Pallas kernels for 31% -> 31%
where the time goes in v27:
time: 67.4 us; the launch traced here: 67.2 us
  starting transfers between devices  25.9 us (38%)
  Pallas kernels  22.5 us (33%)
  waiting for transfers between devices  17.5 us (26%)
  other arithmetic  0.98 us (1%)
    ppermute x16, waiting for transfers between devices, swap(): return lax.ppermute(value, axis, [(i, i ^ bit) for i in range(size)])  15.4 us
    ppermute x16, starting transfers between devices, swap(): return lax.ppermute(value, axis, [(i, i ^ bit) for i in range(size)])  15.4 us
    pallas_call x2, Pallas kernels, pixel_rows(): pl.pallas_call(functools.partial(pixel_kernel, count, bits, stride), out_...  13.7 us
    ppermute x8, starting transfers between devices, sum_over_panels(): parts = [added(part, lax.ppermute(part, both, perm)) for part in parts]  10.5 us
    pallas_call x1, Pallas kernels, project(): pl.pallas_call(functools.partial(project_kernel, bits), out_shape=(jax.Sh...  2.74 us
    pallas_call x1, Pallas kernels, early_product(): pl.pallas_call(early_kernel, out_shape=(jax.ShapeDtypeStruct((depth, widt...  2.49 us
    ppermute x8, waiting for transfers between devices, sum_over_panels(): parts = [added(part, lax.ppermute(part, both, perm)) for part in parts]  2.1 us
    pallas_call x2, Pallas kernels, written(): pl.pallas_call(functools.partial(write_kernel, other), out_shape=jax.Shap...  1.71 us
  transfers between devices with their start and end apart: 25, of which 8 were waited for; matrix products, arithmetic and copies ran while one was open for 1% of the time, Pallas kernels for 31%

profile of v27, /device:TPU:0, one launch (start us, length us, event | category | flops | bytes accessed | tf_op | source)
XLA Modules:
  0.0 67.2 jit_solution(1136301155764697646)
XLA Ops:
  0.0 3.0 %collective-permute-start = (s32[2048]{0:T(1024)}, s32[2048]{0:T(1024)S(1)}, u32[]{:S(2)}, u32[]{:S(2)}) collective-permute-start(s32[2048]{0:T(1024)} %wanted.1), channel_id=1, source_target_pairs={{0,4},{4,0},{1,5},{5,1},{2,6},{6,2},{3,7},{7,3},{8,12},{12,8},{9,1... | collective-permute-start | bytes 24584 | tf_op jit(solution)/shard_map/ppermute | solution.py:46
  3.0 0.9 %slice_select_fusion = bf16[128,256]{1,0:T(8,128)(2,1)S(1)} fusion(bf16[4096,256]{1,0:T(8,128)(2,1)} %cotangent.3, pred[]{:T(512)S(6)} %eq.3), kind=kLoop, calls=%fused_computation.5 | loop fusion | flops 32768 | bytes 196609 | tf_op jit(solution)/shard_map/jit(_where)/select_n | solution.py:23
  4.0 2.7 %project.1 = bf16[512,256]{1,0:T(8,128)(2,1)} custom-call(s32[1]{0:T(128)} %bitcast.1.where.chan.chan_at, bf16[2048,1152]{1,0:T(8,128)(2,1)} %spectra.7, bf16[1152,256]{1,0:T(8,128)(2,1)} %weight.5), custom_call_target="tpu_custom_call" | custom-call | flops 301989888 | bytes 2031616 | tf_op jit(solution)/shard_map/project/pallas_call | solution.py:89
  6.7 2.1 %collective-permute-start.2 = (bf16[512,256]{1,0:T(8,128)(2,1)}, bf16[512,256]{1,0:T(8,128)(2,1)S(1)}, u32[]{:S(2)}, u32[]{:S(2)}) collective-permute-start(bf16[512,256]{1,0:T(8,128)(2,1)} %project.1), channel_id=1, source_target_pairs={{0,1},{1,0},{2,3},{3,2},{4,5},{5,4},{6,7},{7,6},{8,9},{9,8},{10,11... | collective-permute-start | bytes 786440 | tf_op jit(solution)/shard_map/ppermute | solution.py:46
  8.9 7.4 %pixel_rows.2 = (bf16[512,256]{1,0:T(8,128)(2,1)S(1)}, bf16[512,256]{1,0:T(8,128)(2,1)S(1)}, bf16[512,256]{1,0:T(8,128)(2,1)S(1)}) custom-call(s32[1]{0:T(128)} %bitcast.1.where.chan.chan_at, s32[16384]{0:T(1024)S(1)} %bitcast.9, s32[2048]{0:T(1024)S(1)} %collective-permute-done.wanted, bf16[4096,256]{1,0:T(8,128)(2,1)} %cotangent.3, ...), custom_call_target="tpu_custom_call" | custom-call | flops 17179869184 | bytes 4194304 | tf_op jit(solution)/shard_map/pixel_rows/pallas_call | solution.py:305
  16.4 0.9 %collective-permute-start.3 = (bf16[512,256]{1,0:T(8,128)(2,1)S(1)}, bf16[512,256]{1,0:T(8,128)(2,1)S(1)}, u32[]{:S(2)}, u32[]{:S(2)}) collective-permute-start(bf16[512,256]{1,0:T(8,128)(2,1)S(1)} %get-tuple-element.34), channel_id=1, source_target_pairs={{0,1},{1,0},{2,3},{3,2},{4,5},{5,4},{6,7},{7,6},{8,9},{9,8},{10,11... | collective-permute-start | bytes 786440 | tf_op jit(solution)/shard_map/ppermute | solution.py:46
  17.3 3.2 %collective-permute-start.4 = (bf16[512,256]{1,0:T(8,128)(2,1)S(1)}, bf16[512,256]{1,0:T(8,128)(2,1)S(1)}, u32[]{:S(2)}, u32[]{:S(2)}) collective-permute-start(bf16[512,256]{1,0:T(8,128)(2,1)S(1)} %add_convert_fusion), channel_id=1, source_target_pairs={{0,3},{1,2},{2,1},{3,0},{4,7},{5,6},{6,5},{7,4},{8,11},{9,10},{10,... | collective-permute-start | bytes 786440 | tf_op jit(solution)/shard_map/ppermute | solution.py:46
  20.5 1.5 %collective-permute-start.5 = (bf16[512,256]{1,0:T(8,128)(2,1)S(1)}, bf16[512,256]{1,0:T(8,128)(2,1)S(1)}, u32[]{:S(2)}, u32[]{:S(2)}) collective-permute-start(bf16[512,256]{1,0:T(8,128)(2,1)S(1)} %get-tuple-element.37), channel_id=1, source_target_pairs={{0,4},{4,0},{1,5},{5,1},{2,6},{6,2},{3,7},{7,3},{8,12},{12,8},{9,1... | collective-permute-start | bytes 786440 | tf_op jit(solution)/shard_map/ppermute | solution.py:46
  22.1 6.3 %pixel_rows.3 = (bf16[512,256]{1,0:T(8,128)(2,1)S(1)}, bf16[512,256]{1,0:T(8,128)(2,1)S(1)}) custom-call(s32[1]{0:T(128)} %bitcast.3.where, s32[16384]{0:T(1024)S(1)} %bitcast.10, s32[2048]{0:T(1024)S(1)} %copy-done.3, bf16[4096,256]{1,0:T(8,128)(2,1)} %cotangent.3, bf16[128,256]{1,0:T(8,128)(2,1)S(1)} %collective-permute-done.1.above.below, ...), custom_call_target="tpu_custom_call" | custom-call | flops 17179869184 | bytes 4194304 | tf_op jit(solution)/shard_map/pixel_rows/pallas_call | solution.py:305
  28.4 3.1 %collective-permute-done.4.far = bf16[512,256]{1,0:T(8,128)(2,1)S(1)} collective-permute-done((bf16[512,256]{1,0:T(8,128)(2,1)S(1)}, bf16[512,256]{1,0:T(8,128)(2,1)S(1)}, u32[]{:S(2)}, u32[]{:S(2)}) %collective-permute-start.4) | collective-permute-done | bytes 262176 | tf_op jit(solution)/shard_map/ppermute | solution.py:46
  31.5 0.5 pre_gradient.1.first
  32.4 2.3 %collective-permute-start.7 = (bf16[512,256]{1,0:T(8,128)(2,1)S(1)}, bf16[512,256]{1,0:T(8,128)(2,1)S(1)}, u32[]{:S(2)}, u32[]{:S(2)}) collective-permute-start(bf16[512,256]{1,0:T(8,128)(2,1)S(1)} %pre_gradient.1.first), channel_id=1, source_target_pairs={{0,1},{1,0},{2,3},{3,2},{4,5},{5,4},{6,7},{7,6},{8,9},{9,8},{10,11... | collective-permute-start | bytes 786440 | tf_op jit(solution)/shard_map/ppermute | solution.py:46
  34.7 8.4 %collective-permute-done.6.second = bf16[512,256]{1,0:T(8,128)(2,1)S(1)} collective-permute-done((bf16[512,256]{1,0:T(8,128)(2,1)S(1)}, bf16[512,256]{1,0:T(8,128)(2,1)S(1)}, u32[]{:S(2)}, u32[]{:S(2)}) %collective-permute-start.6) | collective-permute-done | bytes 262176 | tf_op jit(solution)/shard_map/ppermute | solution.py:46
  43.2 2.5 %early_product.1 = (f32[1152,256]{1,0:T(8,128)S(1)}, bf16[512,1152]{1,0:T(8,128)(2,1)S(1)}, bf16[512,1152]{1,0:T(8,128)(2,1)S(1)}) custom-call(s32[1]{0:T(128)} %bitcast.1.where.chan.chan_at, bf16[2048,1152]{1,0:T(8,128)(2,1)} %spectra.7, bf16[512,256]{1,0:T(8,128)(2,1)S(1)} %pre_gradient.1.first, bf16[512,256]{1,0:T(8,128)(2,1)S(1)} %collective-permute-done.6.second), custom_call_target="tpu_custom_call" | custom-call | flops 603979776 | bytes 5898240 | tf_op jit(solution)/shard_map/early_product/pallas_call | solution.py:136
  45.8 0.5 more_product.1.before
  46.4 3.2 %collective-permute-done.8.rows = bf16[512,256]{1,0:T(8,128)(2,1)S(1)} collective-permute-done((bf16[512,256]{1,0:T(8,128)(2,1)S(1)}, bf16[512,256]{1,0:T(8,128)(2,1)S(1)}, u32[]{:S(2)}, u32[]{:S(2)}) %collective-permute-start.8) | collective-permute-done | bytes 262176 | tf_op jit(solution)/shard_map/ppermute | solution.py:46
  49.5 0.6 late_product.1
  50.2 0.5 collective-permute-start.12
  50.8 0.4 collective-permute-start.18
  51.5 1.6 %collective-permute-start.10 = (bf16[144,256]{1,0:T(8,128)(2,1)S(1)}, bf16[144,256]{1,0:T(8,128)(2,1)S(1)}, u32[]{:S(2)}, u32[]{:S(2)}) collective-permute-start(bf16[144,256]{1,0:T(8,128)(2,1)S(1)} %added.12.first), channel_id=1, source_target_pairs={{0,16},{4,20},{8,12},{12,8},{16,0},{20,4},{24,28},{28,24},{1,17},{... | collective-permute-start | bytes 221192 | tf_op jit(solution)/shard_map/ppermute | solution.py:446
  53.0 0.6 collective-permute-start.13
  53.7 1.6 %collective-permute-start.16 = (bf16[144,256]{1,0:T(8,128)(2,1)S(1)}, bf16[144,256]{1,0:T(8,128)(2,1)S(1)}, u32[]{:S(2)}, u32[]{:S(2)}) collective-permute-start(bf16[144,256]{1,0:T(8,128)(2,1)S(1)} %added.18.first), channel_id=1, source_target_pairs={{0,16},{4,20},{8,12},{12,8},{16,0},{20,4},{24,28},{28,24},{1,17},{... | collective-permute-start | bytes 221192 | tf_op jit(solution)/shard_map/ppermute | solution.py:446
  55.3 0.6 collective-permute-start.19
  55.9 1.6 %collective-permute-start.11 = (bf16[144,256]{1,0:T(8,128)(2,1)S(1)}, bf16[144,256]{1,0:T(8,128)(2,1)S(1)}, u32[]{:S(2)}, u32[]{:S(2)}) collective-permute-start(bf16[144,256]{1,0:T(8,128)(2,1)S(1)} %added.13.first), channel_id=1, source_target_pairs={{0,4},{4,0},{8,24},{12,28},{16,20},{20,16},{24,8},{28,12},{1,5},{5... | collective-permute-start | bytes 221192 | tf_op jit(solution)/shard_map/ppermute | solution.py:446
  57.6 1.5 %collective-permute-start.14 = (bf16[144,256]{1,0:T(8,128)(2,1)S(1)}, bf16[144,256]{1,0:T(8,128)(2,1)S(1)}, u32[]{:S(2)}, u32[]{:S(2)}) collective-permute-start(bf16[144,256]{1,0:T(8,128)(2,1)S(1)} %added.16.first), channel_id=1, source_target_pairs={{0,4},{4,0},{8,24},{12,28},{16,20},{20,16},{24,8},{28,12},{1,5},{5... | collective-permute-start | bytes 221192 | tf_op jit(solution)/shard_map/ppermute | solution.py:446
  59.1 1.4 %collective-permute-start.17 = (bf16[144,256]{1,0:T(8,128)(2,1)S(1)}, bf16[144,256]{1,0:T(8,128)(2,1)S(1)}, u32[]{:S(2)}, u32[]{:S(2)}) collective-permute-start(bf16[144,256]{1,0:T(8,128)(2,1)S(1)} %added.19.first), channel_id=1, source_target_pairs={{0,4},{4,0},{8,24},{12,28},{16,20},{20,16},{24,8},{28,12},{1,5},{5... | collective-permute-start | bytes 221192 | tf_op jit(solution)/shard_map/ppermute | solution.py:446
  60.6 1.6 %collective-permute-start.20 = (bf16[144,256]{1,0:T(8,128)(2,1)S(1)}, bf16[144,256]{1,0:T(8,128)(2,1)S(1)}, u32[]{:S(2)}, u32[]{:S(2)}) collective-permute-start(bf16[144,256]{1,0:T(8,128)(2,1)S(1)} %added.22.first), channel_id=1, source_target_pairs={{0,4},{4,0},{8,24},{12,28},{16,20},{20,16},{24,8},{28,12},{1,5},{5... | collective-permute-start | bytes 221192 | tf_op jit(solution)/shard_map/ppermute | solution.py:446
  62.3 0.5 collective-permute-start.22
  62.9 0.7 %collective-permute-done.17.second = bf16[144,256]{1,0:T(8,128)(2,1)S(1)} collective-permute-done((bf16[144,256]{1,0:T(8,128)(2,1)S(1)}, bf16[144,256]{1,0:T(8,128)(2,1)S(1)}, u32[]{:S(2)}, u32[]{:S(2)}) %collective-permute-start.17) | collective-permute-done | bytes 73760 | tf_op jit(solution)/shard_map/ppermute | solution.py:446
  63.7 1.4 %collective-permute-done.20.second = bf16[144,256]{1,0:T(8,128)(2,1)S(1)} collective-permute-done((bf16[144,256]{1,0:T(8,128)(2,1)S(1)}, bf16[144,256]{1,0:T(8,128)(2,1)S(1)}, u32[]{:S(2)}, u32[]{:S(2)}) %collective-permute-start.20) | collective-permute-done | bytes 73760 | tf_op jit(solution)/shard_map/ppermute | solution.py:446
  65.1 0.9 %written.2.refs_0_ = f32[1152,256]{1,0:T(8,128)} custom-call(s32[1]{0:T(128)} %bitcast.core, bf16[144,256]{1,0:T(8,128)(2,1)S(1)} %added.14.refs_0_, bf16[144,256]{1,0:T(8,128)(2,1)S(1)} %added.17.refs_1_, bf16[144,256]{1,0:T(8,128)(2,1)S(1)} %added.20.refs_2_, bf16[144,256]{1,0:T(8,128)(2,1)S(1)} %added.23.refs_3_), custom_call_target="tpu_custom_call" | custom-call | tf_op jit(solution)/shard_map/written/pallas_call | solution.py:406
  66.4 0.9 %written.3 = f32[1152,256]{1,0:T(8,128)} custom-call(s32[1]{0:T(128)} %bitcast.core, f32[1152,256]{1,0:T(8,128)} %written.2.refs_0_, bf16[144,256]{1,0:T(8,128)(2,1)S(1)} %collective-permute-done.21.refs_1_, bf16[144,256]{1,0:T(8,128)(2,1)S(1)} %collective-permute-done.22.refs_2_, ...), custom_call_target="tpu_custom_call", output_to_operand_aliasing={{}: (1, {})} | custom-call | tf_op jit(solution)/shard_map/written/pallas_call | solution.py:406
  (56 shorter events, 2.2 us)
Async XLA Ops:
  0.0 8.9 %collective-permute-start = (s32[2048]{0:T(1024)}, s32[2048]{0:T(1024)S(1)}, u32[]{:S(2)}, u32[]{:S(2)}) collective-permute-start(s32[2048]{0:T(1024)} %wanted.1), channel_id=1, source_target_pairs={{0,4},{4,0},{1,5},{5,1},{2,6},{6,2},{3,7},{7,3},{8,12},{12,8},{9,1... | collective-permute-start | bytes 24584 | tf_op jit(solution)/shard_map/ppermute | solution.py:46
  3.9 5.0 %collective-permute-start.1 = (bf16[128,256]{1,0:T(8,128)(2,1)S(1)}, bf16[128,256]{1,0:T(8,128)(2,1)S(1)}, u32[]{:S(2)}, u32[]{:S(2)}) collective-permute-start(bf16[128,256]{1,0:T(8,128)(2,1)S(1)} %slice_select_fusion), channel_id=1, source_target_pairs={{0,4},{4,0},{1,5},{5,1},{2,6},{6,2},{3,7},{7,3},{8,12},{12,8},{9,1... | collective-permute-start | bytes 196616 | tf_op jit(solution)/shard_map/ppermute | solution.py:23
  3.9 4.9 %copy-start.5 = (s32[8,4096]{1,0:T(8,128)S(1)}, s32[8,4096]{1,0:T(8,128)}, u32[]{:S(2)}) copy-start(s32[8,4096]{1,0:T(8,128)} %param.14) | copy-start | bytes 393220
  3.9 5.0 %copy-start = (bf16[1152,256]{1,0:T(8,128)(2,1)S(1)}, bf16[1152,256]{1,0:T(8,128)(2,1)}, u32[]{:S(2)}) copy-start(bf16[1152,256]{1,0:T(8,128)(2,1)} %weight.5) | copy-start | bytes 1769476
  4.0 5.0 %copy-start.4 = (f32[8,256]{1,0:T(8,128)S(1)}, f32[8,256]{1,0:T(8,128)}, u32[]{:S(2)}) copy-start(f32[8,256]{1,0:T(8,128)} %mixing.3) | copy-start | bytes 24580
  6.7 9.6 %collective-permute-start.2 = (bf16[512,256]{1,0:T(8,128)(2,1)}, bf16[512,256]{1,0:T(8,128)(2,1)S(1)}, u32[]{:S(2)}, u32[]{:S(2)}) collective-permute-start(bf16[512,256]{1,0:T(8,128)(2,1)} %project.1), channel_id=1, source_target_pairs={{0,1},{1,0},{2,3},{3,2},{4,5},{5,4},{6,7},{7,6},{8,9},{9,8},{10,11... | collective-permute-start | bytes 786440 | tf_op jit(solution)/shard_map/ppermute | solution.py:46
  8.9 13.1 %copy-start.3 = (s32[2048]{0:T(1024)S(1)}, s32[2048]{0:T(1024)}, u32[]{:S(2)}) copy-start(s32[2048]{0:T(1024)} %wanted.1) | copy-start | bytes 24580
  16.4 11.9 %collective-permute-start.3 = (bf16[512,256]{1,0:T(8,128)(2,1)S(1)}, bf16[512,256]{1,0:T(8,128)(2,1)S(1)}, u32[]{:S(2)}, u32[]{:S(2)}) collective-permute-start(bf16[512,256]{1,0:T(8,128)(2,1)S(1)} %get-tuple-element.34), channel_id=1, source_target_pairs={{0,1},{1,0},{2,3},{3,2},{4,5},{5,4},{6,7},{7,6},{8,9},{9,8},{10,11... | collective-permute-start | bytes 786440 | tf_op jit(solution)/shard_map/ppermute | solution.py:46
  17.3 14.1 %collective-permute-start.4 = (bf16[512,256]{1,0:T(8,128)(2,1)S(1)}, bf16[512,256]{1,0:T(8,128)(2,1)S(1)}, u32[]{:S(2)}, u32[]{:S(2)}) collective-permute-start(bf16[512,256]{1,0:T(8,128)(2,1)S(1)} %add_convert_fusion), channel_id=1, source_target_pairs={{0,3},{1,2},{2,1},{3,0},{4,7},{5,6},{6,5},{7,4},{8,11},{9,10},{10,... | collective-permute-start | bytes 786440 | tf_op jit(solution)/shard_map/ppermute | solution.py:46
  20.5 10.9 %collective-permute-start.5 = (bf16[512,256]{1,0:T(8,128)(2,1)S(1)}, bf16[512,256]{1,0:T(8,128)(2,1)S(1)}, u32[]{:S(2)}, u32[]{:S(2)}) collective-permute-start(bf16[512,256]{1,0:T(8,128)(2,1)S(1)} %get-tuple-element.37), channel_id=1, source_target_pairs={{0,4},{4,0},{1,5},{5,1},{2,6},{6,2},{3,7},{7,3},{8,12},{12,8},{9,1... | collective-permute-start | bytes 786440 | tf_op jit(solution)/shard_map/ppermute | solution.py:46
  22.1 9.4 %copy-start.1 = (s32[2048,1]{0,1:T(1,128)S(1)}, s32[2048,1]{0,1:T(1,128)}, u32[]{:S(2)}) copy-start(s32[2048,1]{0,1:T(1,128)} %param.10) | copy-start | bytes 24580
  22.1 9.4 %copy-start.2 = (f32[2048]{0:T(1024)S(1)}, f32[2048]{0:T(1024)}, u32[]{:S(2)}) copy-start(f32[2048]{0:T(1024)} %param.12) | copy-start | bytes 24580
  32.0 11.1 %collective-permute-start.6 = (bf16[512,256]{1,0:T(8,128)(2,1)S(1)}, bf16[512,256]{1,0:T(8,128)(2,1)S(1)}, u32[]{:S(2)}, u32[]{:S(2)}) collective-permute-start(bf16[512,256]{1,0:T(8,128)(2,1)S(1)} %pre_gradient.1.first), channel_id=1, source_target_pairs={{0,3},{1,2},{2,1},{3,0},{4,7},{5,6},{6,5},{7,4},{8,11},{9,10},{10,... | collective-permute-start | bytes 786440 | tf_op jit(solution)/shard_map/ppermute | solution.py:46
  32.4 13.4 %collective-permute-start.7 = (bf16[512,256]{1,0:T(8,128)(2,1)S(1)}, bf16[512,256]{1,0:T(8,128)(2,1)S(1)}, u32[]{:S(2)}, u32[]{:S(2)}) collective-permute-start(bf16[512,256]{1,0:T(8,128)(2,1)S(1)} %pre_gradient.1.first), channel_id=1, source_target_pairs={{0,1},{1,0},{2,3},{3,2},{4,5},{5,4},{6,7},{7,6},{8,9},{9,8},{10,11... | collective-permute-start | bytes 786440 | tf_op jit(solution)/shard_map/ppermute | solution.py:46
  43.1 6.5 %collective-permute-start.8 = (bf16[512,256]{1,0:T(8,128)(2,1)S(1)}, bf16[512,256]{1,0:T(8,128)(2,1)S(1)}, u32[]{:S(2)}, u32[]{:S(2)}) collective-permute-start(bf16[512,256]{1,0:T(8,128)(2,1)S(1)} %collective-permute-done.6.second), channel_id=1, source_target_pairs={{0,1},{1,0},{2,3},{3,2},{4,5},{5,4},{6,7},{7,6},{8,9},{9,8},{10,11... | collective-permute-start | bytes 786440 | tf_op jit(solution)/shard_map/ppermute | solution.py:46
  50.1 1.3 %collective-permute-start.9 = (bf16[144,256]{1,0:T(8,128)(2,1)S(1)}, bf16[144,256]{1,0:T(8,128)(2,1)S(1)}, u32[]{:S(2)}, u32[]{:S(2)}) collective-permute-start(bf16[144,256]{1,0:T(8,128)(2,1)S(1)} %get-tuple-element.42), channel_id=1, source_target_pairs={{0,8},{8,0},{16,24},{24,16},{1,9},{9,1},{17,25},{25,17},{2,10},{10... | collective-permute-start | bytes 221192 | tf_op jit(solution)/shard_map/ppermute | solution.py:46
  50.2 2.8 %collective-permute-start.12 = (bf16[144,256]{1,0:T(8,128)(2,1)S(1)}, bf16[144,256]{1,0:T(8,128)(2,1)S(1)}, u32[]{:S(2)}, u32[]{:S(2)}) collective-permute-start(bf16[144,256]{1,0:T(8,128)(2,1)S(1)} %get-tuple-element.44), channel_id=1, source_target_pairs={{0,8},{8,0},{16,24},{24,16},{1,9},{9,1},{17,25},{25,17},{2,10},{10... | collective-permute-start | bytes 221192 | tf_op jit(solution)/shard_map/ppermute | solution.py:46
  50.7 3.0 %collective-permute-start.15 = (bf16[144,256]{1,0:T(8,128)(2,1)S(1)}, bf16[144,256]{1,0:T(8,128)(2,1)S(1)}, u32[]{:S(2)}, u32[]{:S(2)}) collective-permute-start(bf16[144,256]{1,0:T(8,128)(2,1)S(1)} %get-tuple-element.46), channel_id=1, source_target_pairs={{0,8},{8,0},{16,24},{24,16},{1,9},{9,1},{17,25},{25,17},{2,10},{10... | collective-permute-start | bytes 221192 | tf_op jit(solution)/shard_map/ppermute | solution.py:46
  50.8 4.5 %collective-permute-start.18 = (bf16[144,256]{1,0:T(8,128)(2,1)S(1)}, bf16[144,256]{1,0:T(8,128)(2,1)S(1)}, u32[]{:S(2)}, u32[]{:S(2)}) collective-permute-start(bf16[144,256]{1,0:T(8,128)(2,1)S(1)} %get-tuple-element.48), channel_id=1, source_target_pairs={{0,8},{8,0},{16,24},{24,16},{1,9},{9,1},{17,25},{25,17},{2,10},{10... | collective-permute-start | bytes 221192 | tf_op jit(solution)/shard_map/ppermute | solution.py:46
  51.5 4.4 %collective-permute-start.10 = (bf16[144,256]{1,0:T(8,128)(2,1)S(1)}, bf16[144,256]{1,0:T(8,128)(2,1)S(1)}, u32[]{:S(2)}, u32[]{:S(2)}) collective-permute-start(bf16[144,256]{1,0:T(8,128)(2,1)S(1)} %added.12.first), channel_id=1, source_target_pairs={{0,16},{4,20},{8,12},{12,8},{16,0},{20,4},{24,28},{28,24},{1,17},{... | collective-permute-start | bytes 221192 | tf_op jit(solution)/shard_map/ppermute | solution.py:446
  53.0 4.5 %collective-permute-start.13 = (bf16[144,256]{1,0:T(8,128)(2,1)S(1)}, bf16[144,256]{1,0:T(8,128)(2,1)S(1)}, u32[]{:S(2)}, u32[]{:S(2)}) collective-permute-start(bf16[144,256]{1,0:T(8,128)(2,1)S(1)} %added.15.first), channel_id=1, source_target_pairs={{0,16},{4,20},{8,12},{12,8},{16,0},{20,4},{24,28},{28,24},{1,17},{... | collective-permute-start | bytes 221192 | tf_op jit(solution)/shard_map/ppermute | solution.py:446
  53.7 5.4 %collective-permute-start.16 = (bf16[144,256]{1,0:T(8,128)(2,1)S(1)}, bf16[144,256]{1,0:T(8,128)(2,1)S(1)}, u32[]{:S(2)}, u32[]{:S(2)}) collective-permute-start(bf16[144,256]{1,0:T(8,128)(2,1)S(1)} %added.18.first), channel_id=1, source_target_pairs={{0,16},{4,20},{8,12},{12,8},{16,0},{20,4},{24,28},{28,24},{1,17},{... | collective-permute-start | bytes 221192 | tf_op jit(solution)/shard_map/ppermute | solution.py:446
  55.3 5.3 %collective-permute-start.19 = (bf16[144,256]{1,0:T(8,128)(2,1)S(1)}, bf16[144,256]{1,0:T(8,128)(2,1)S(1)}, u32[]{:S(2)}, u32[]{:S(2)}) collective-permute-start(bf16[144,256]{1,0:T(8,128)(2,1)S(1)} %added.21.first), channel_id=1, source_target_pairs={{0,16},{4,20},{8,12},{12,8},{16,0},{20,4},{24,28},{28,24},{1,17},{... | collective-permute-start | bytes 221192 | tf_op jit(solution)/shard_map/ppermute | solution.py:446
  55.9 6.3 %collective-permute-start.11 = (bf16[144,256]{1,0:T(8,128)(2,1)S(1)}, bf16[144,256]{1,0:T(8,128)(2,1)S(1)}, u32[]{:S(2)}, u32[]{:S(2)}) collective-permute-start(bf16[144,256]{1,0:T(8,128)(2,1)S(1)} %added.13.first), channel_id=1, source_target_pairs={{0,4},{4,0},{8,24},{12,28},{16,20},{20,16},{24,8},{28,12},{1,5},{5... | collective-permute-start | bytes 221192 | tf_op jit(solution)/shard_map/ppermute | solution.py:446
  57.6 4.7 %collective-permute-start.14 = (bf16[144,256]{1,0:T(8,128)(2,1)S(1)}, bf16[144,256]{1,0:T(8,128)(2,1)S(1)}, u32[]{:S(2)}, u32[]{:S(2)}) collective-permute-start(bf16[144,256]{1,0:T(8,128)(2,1)S(1)} %added.16.first), channel_id=1, source_target_pairs={{0,4},{4,0},{8,24},{12,28},{16,20},{20,16},{24,8},{28,12},{1,5},{5... | collective-permute-start | bytes 221192 | tf_op jit(solution)/shard_map/ppermute | solution.py:446
  59.1 4.4 %collective-permute-start.17 = (bf16[144,256]{1,0:T(8,128)(2,1)S(1)}, bf16[144,256]{1,0:T(8,128)(2,1)S(1)}, u32[]{:S(2)}, u32[]{:S(2)}) collective-permute-start(bf16[144,256]{1,0:T(8,128)(2,1)S(1)} %added.19.first), channel_id=1, source_target_pairs={{0,4},{4,0},{8,24},{12,28},{16,20},{20,16},{24,8},{28,12},{1,5},{5... | collective-permute-start | bytes 221192 | tf_op jit(solution)/shard_map/ppermute | solution.py:446
  60.6 4.4 %collective-permute-start.20 = (bf16[144,256]{1,0:T(8,128)(2,1)S(1)}, bf16[144,256]{1,0:T(8,128)(2,1)S(1)}, u32[]{:S(2)}, u32[]{:S(2)}) collective-permute-start(bf16[144,256]{1,0:T(8,128)(2,1)S(1)} %added.22.first), channel_id=1, source_target_pairs={{0,4},{4,0},{8,24},{12,28},{16,20},{20,16},{24,8},{28,12},{1,5},{5... | collective-permute-start | bytes 221192 | tf_op jit(solution)/shard_map/ppermute | solution.py:446
  62.2 3.8 %collective-permute-start.21 = (bf16[144,256]{1,0:T(8,128)(2,1)S(1)}, bf16[144,256]{1,0:T(8,128)(2,1)S(1)}, u32[]{:S(2)}, u32[]{:S(2)}) collective-permute-start(bf16[144,256]{1,0:T(8,128)(2,1)S(1)} %added.14.refs_0_), channel_id=1, source_target_pairs={{0,8},{8,0},{16,24},{24,16},{1,9},{9,1},{17,25},{25,17},{2,10},{10... | collective-permute-start | bytes 221192 | tf_op jit(solution)/shard_map/ppermute | solution.py:46
  62.3 3.7 %collective-permute-start.22 = (bf16[144,256]{1,0:T(8,128)(2,1)S(1)}, bf16[144,256]{1,0:T(8,128)(2,1)S(1)}, u32[]{:S(2)}, u32[]{:S(2)}) collective-permute-start(bf16[144,256]{1,0:T(8,128)(2,1)S(1)} %added.17.refs_1_), channel_id=1, source_target_pairs={{0,8},{8,0},{16,24},{24,16},{1,9},{9,1},{17,25},{25,17},{2,10},{10... | collective-permute-start | bytes 221192 | tf_op jit(solution)/shard_map/ppermute | solution.py:46
  63.6 2.4 %collective-permute-start.23 = (bf16[144,256]{1,0:T(8,128)(2,1)S(1)}, bf16[144,256]{1,0:T(8,128)(2,1)S(1)}, u32[]{:S(2)}, u32[]{:S(2)}) collective-permute-start(bf16[144,256]{1,0:T(8,128)(2,1)S(1)} %added.20.refs_2_), channel_id=1, source_target_pairs={{0,8},{8,0},{16,24},{24,16},{1,9},{9,1},{17,25},{25,17},{2,10},{10... | collective-permute-start | bytes 221192 | tf_op jit(solution)/shard_map/ppermute | solution.py:46
  65.1 1.3 %collective-permute-start.24 = (bf16[144,256]{1,0:T(8,128)(2,1)S(1)}, bf16[144,256]{1,0:T(8,128)(2,1)S(1)}, u32[]{:S(2)}, u32[]{:S(2)}) collective-permute-start(bf16[144,256]{1,0:T(8,128)(2,1)S(1)} %added.23.refs_3_), channel_id=1, source_target_pairs={{0,8},{8,0},{16,24},{24,16},{1,9},{9,1},{17,25},{25,17},{2,10},{10... | collective-permute-start | bytes 221192 | tf_op jit(solution)/shard_map/ppermute | solution.py:46
